TPU v7x, 32 devices: a whole 2x2x4 slice. The times are simulated.
32 devices in a mesh: row: 2 (over x), col: 4 (over z), layer: 4 (over y, core).
Axes of the slice: x: 2, y: 2, z: 4, core: 2. Of those that a mesh axis runs over, the one named last changes fastest.
Arguments:
- sign_start: bfloat16 [32, 12, 128, 128], P(('row', 'col', 'layer')), as said below
- neighbors: int32 [32, 12], replicated, may hold values from 0 to 31, as said below
- atom_size: int32 [32], replicated, may hold values from 64 to 128
- basis_proj: bfloat16 [32, 6, 128], replicated, may hold values from -6 to 6
- pair_extent: int32 [32, 12], P(('row', 'col', 'layer')), may hold values from 3 to 6
- atom_x: int32 [32], replicated, may hold values from 6 to 9
- atom_y: int32 [32], replicated, may hold values from 6 to 9
- atom_z: int32 [32], replicated, may hold values from 62 to 65
Outputs:
- sign_next: bfloat16 [32, 12, 128, 128], P(('row', 'col', 'layer'))
- density: float32 [32, 64, 512], P('row', 'col', 'layer')
Inputs may be any that keep to these rules, and one draw needn't show every extreme that they name: `neighbors`: atom a belongs to index a of row+col+layer. Row a lists 12 distinct atoms, a among them; b is in row a exactly when a is in row b; every listed atom lies on the same row and col indices as a or on one of the eight around them (with wrap), and exactly 3 entries of a row lie on each layer index. sign_start is symmetric: the block of atom b in row a is the transpose of the block of atom a in row b.
All inputs are finite; a program needn't handle non-finite values.
Results may differ from a plain program's by a relative error of at most 0.017.
Values may be sent and summed in bfloat16 or wider, within the bound.
No kernel may reach another device: no remote copies, remote signals or barrier semaphores. Data moves between devices by JAX's collectives and lax.ppermute only.
A program may use at most 64 MiB of HBM per device.

v0:
```python
import jax
import jax.numpy as jnp
from jax import lax
from jax.sharding import PartitionSpec as P

EXT = 6
DRIFT = 2
BX = 16
BY = 16
BZ = 128


def extended(x, sides, width):
    for axis, dim in sides:
        count, length = (lax.axis_size(axis), x.shape[dim])
        up = [(i, (i + 1) % count) for i in range(count)]
        down = [(j, i) for i, j in up]
        last = lax.slice_in_dim(x, length - width, length, axis=dim)
        first = lax.slice_in_dim(x, 0, width, axis=dim)
        before = lax.ppermute(last, axis, up)
        after = lax.ppermute(first, axis, down)
        x = jnp.concatenate([before, x, after], axis=dim)
    return x


def profile(coords, centers, extent, rates):
    offset = coords[None, :] - centers[:, None]
    inside = (jnp.abs(offset) <= extent[:, None]).astype(jnp.float32)
    return (
        jnp.exp(-rates[:, :, :, None] * (offset * offset)[:, None, None, :])
        * inside[:, None, None, :]
    )


def collocate(coeffs, cent_x, cent_y, cent_z, extent, grid_x, grid_height, grid_z):
    shells_count = coeffs.shape[1]
    shells = jnp.arange(1, shells_count + 1).astype(jnp.float32)
    inverse = (shells_count / extent[:, None]) ** 2 / shells[None, :] ** 2
    rates = inverse[:, :, None] + inverse[:, None, :]
    along_x = profile(grid_x, cent_x, extent, rates)
    along_y = profile(grid_height, cent_y, extent, rates)
    along_z = profile(grid_z, cent_z, extent, rates) * coeffs[:, :, :, None]
    groups = coeffs.shape[0] // 4
    terms_count = 4 * shells_count * shells_count
    pieces = (
        along_x.reshape(groups, terms_count, grid_x.shape[0]),
        along_y.reshape(groups, terms_count, grid_height.shape[0]),
        along_z.reshape(groups, terms_count, grid_z.shape[0]),
    )

    def accumulate(running, piece):
        outer_rows = (piece[0][:, :, None] * piece[1][:, None, :]).reshape(terms_count, -1)
        added = jnp.einsum("kp,kz->pz", outer_rows, piece[2], precision=lax.Precision.HIGHEST)
        return (running + added, None)

    start = jnp.zeros((grid_x.shape[0] * grid_height.shape[0], grid_z.shape[0]), jnp.float32)
    running = lax.scan(accumulate, start, pieces)[0]
    return running.reshape(grid_x.shape[0], grid_height.shape[0], grid_z.shape[0])


def local(sign_start, neighbors, atom_size, basis_proj, pair_extent, atom_x, atom_y, atom_z):
    n_row = lax.axis_size("row")
    n_col = lax.axis_size("col")
    n_lay = lax.axis_size("layer")
    my_row = lax.axis_index("row")
    my_col = lax.axis_index("col")
    my_lay = lax.axis_index("layer")
    slots = sign_start.shape[1]
    block_size = sign_start.shape[2]
    per_layer = slots // n_lay
    tile_base = (my_row * n_col + my_col) * n_lay
    my_atom = tile_base + my_lay
    lane_ids = jnp.arange(block_size)
    size_mask = lane_ids[None, :] < atom_size[:, None]
    listed = lax.dynamic_index_in_dim(neighbors, my_atom, 0, keepdims=False)
    own_mask = lax.dynamic_index_in_dim(size_mask, my_atom, 0, keepdims=False)
    col_mask = jnp.take(size_mask, listed, axis=0)
    keeping = (own_mask[None, :, None] & col_mask[:, None, :]).astype(jnp.bfloat16)
    masked = sign_start[0] * keeping
    tile_atoms = tile_base + jnp.arange(n_lay)
    tile_lists = jnp.take(neighbors, tile_atoms, axis=0)
    in_layer = (tile_lists % n_lay == my_lay).astype(jnp.int32)
    rank_ids = jnp.cumsum(in_layer, axis=1) - 1
    chosen = in_layer[:, None, :] * (
        rank_ids[:, None, :] == jnp.arange(per_layer)[None, :, None]
    ).astype(jnp.int32)
    places = jnp.arange(slots)
    term_atoms = jnp.sum(chosen * tile_lists[:, None, :], axis=2)
    term_slots = jnp.sum(chosen * places[None, None, :], axis=2)
    term_row = term_atoms // (n_lay * n_col)
    term_col = term_atoms // n_lay % n_col
    tile_slot = (term_row - my_row + 1) % n_row * 3 + (term_col - my_col + 1) % n_col
    term_index_lists = jnp.take(neighbors, term_atoms, axis=0)
    at_own = jnp.sum(jnp.where(term_index_lists == tile_atoms[:, None, None], places, 0), axis=2)
    matches = term_index_lists[:, :, None, :] == tile_lists[:, None, :, None]
    present = jnp.any(matches, axis=3)
    at_pair = jnp.sum(jnp.where(matches, places, 0), axis=3)
    left_index = tile_slot * slots + at_own
    right_index = tile_slot[:, :, None] * slots + at_pair
    beside_all = extended(masked[None, None], (("row", 0), ("col", 1)), 1)
    around_flat = beside_all.reshape(9 * slots, block_size, block_size)
    left_x = jnp.take(around_flat, left_index, axis=0)
    right_x = jnp.where(
        present[:, :, :, None, None],
        jnp.take(around_flat, right_index, axis=0),
        jnp.zeros((), jnp.bfloat16),
    )
    first_terms = jnp.einsum(
        "imab,imwac->iwbc", left_x, right_x, preferred_element_type=jnp.float32
    )
    square_row = lax.psum_scatter(
        first_terms.astype(jnp.bfloat16), "layer", scatter_dimension=0, tiled=True
    )
    tile_square = lax.all_gather(square_row, "layer", axis=0, tiled=True)
    left_square = tile_square[jnp.arange(n_lay)[:, None], term_slots]
    second_terms = jnp.einsum(
        "imab,imwbc->iwac", left_square, right_x, preferred_element_type=jnp.float32
    )
    cubed = lax.psum_scatter(
        second_terms.astype(jnp.bfloat16), "layer", scatter_dimension=0, tiled=True
    ).astype(jnp.float32)[0]
    sign_full = 1.5 * masked.astype(jnp.float32) - 0.5 * cubed
    is_self = listed == my_atom
    own_float = own_mask.astype(jnp.float32)
    dmat = 0.5 * (jnp.where(is_self[:, None, None], jnp.diag(own_float)[None], 0.0) - sign_full)
    own_basis = lax.dynamic_index_in_dim(basis_proj, my_atom, 0, keepdims=False).astype(jnp.float32)
    pair_basis = jnp.take(basis_proj, listed, axis=0).astype(jnp.float32)
    halfway = jnp.einsum("sa,wab->wsb", own_basis, dmat, precision=lax.Precision.HIGHEST)
    coeffs = jnp.einsum("wsb,wtb->wst", halfway, pair_basis, precision=lax.Precision.HIGHEST)
    pair_row = listed // (n_lay * n_col)
    pair_col = listed // n_lay % n_col
    pair_layer = listed % n_lay
    step_row = ((pair_row - my_row + 1) % n_row - 1).astype(jnp.float32)
    step_col = ((pair_col - my_col + 1) % n_col - 1).astype(jnp.float32)
    step_lay = jnp.minimum((pair_layer - my_lay + 1) % n_lay - 1, 1).astype(jnp.float32)
    own_x = lax.dynamic_index_in_dim(atom_x, my_atom, 0, keepdims=False).astype(jnp.float32)
    own_y = lax.dynamic_index_in_dim(atom_y, my_atom, 0, keepdims=False).astype(jnp.float32)
    own_z = lax.dynamic_index_in_dim(atom_z, my_atom, 0, keepdims=False).astype(jnp.float32)
    cent_x = 0.5 * (own_x + jnp.take(atom_x, listed).astype(jnp.float32) + BX * step_row)
    cent_y = 0.5 * (own_y + jnp.take(atom_y, listed).astype(jnp.float32) + BY * step_col)
    cent_z = 0.5 * (own_z + jnp.take(atom_z, listed).astype(jnp.float32) + BZ * step_lay)
    extent = pair_extent[0].astype(jnp.float32)
    margin = DRIFT + EXT
    grid_x = jnp.arange(BX + 2 * margin).astype(jnp.float32) - margin
    grid_height = jnp.arange(BY + 2 * margin).astype(jnp.float32) - margin
    grid_z = jnp.arange(BZ + 2 * margin).astype(jnp.float32) - margin
    padded = collocate(coeffs, cent_x, cent_y, cent_z, extent, grid_x, grid_height, grid_z)
    widened = extended(
        padded.astype(jnp.bfloat16), (("row", 0), ("col", 1), ("layer", 2)), margin
    ).astype(padded.dtype)
    span_x = BX + 2 * margin
    span_y = BY + 2 * margin
    span_z = BZ + 2 * margin
    core_x = widened[2 * margin : 2 * margin + BX]
    core_x = core_x.at[:margin].add(widened[:margin])
    core_x = core_x.at[BX - margin :].add(widened[span_x + margin :])
    core_y = core_x[:, 2 * margin : 2 * margin + BY]
    core_y = core_y.at[:, :margin].add(core_x[:, :margin])
    core_y = core_y.at[:, BY - margin :].add(core_x[:, span_y + margin :])
    core = core_y[:, :, 2 * margin : 2 * margin + BZ]
    core = core.at[:, :, :margin].add(core_y[:, :, :margin])
    core = core.at[:, :, BZ - margin :].add(core_y[:, :, span_z + margin :])
    return (sign_full.astype(jnp.bfloat16)[None], core)


def solution(mesh):
    in_specs = (
        P(("row", "col", "layer"), None, None, None),
        P(),
        P(),
        P(),
        P(("row", "col", "layer"), None),
        P(),
        P(),
        P(),
    )
    out_specs = (P(("row", "col", "layer"), None, None, None), P("row", "col", "layer"))
    return jax.shard_map(local, mesh=mesh, in_specs=in_specs, out_specs=out_specs, check_vma=False)
```

profile of v0, /device:TPU:0, one launch (start us, length us, event | category | flops | bytes accessed | tf_op | source)
XLA Modules:
  0.0 238.1 jit_solution(4312216820353229128)
XLA Ops:
  7.2 0.9 dynamic-slice_reduce_fusion
  8.1 0.7 iota_compare_fusion.2
  8.9 0.6 gather_fusion
  9.6 1.2 and_select_fusion
  10.8 3.0 %collective-permute-start.1 = (bf16[1,1,12,128,128]{4,3,2,1,0:T(8,128)(2,1)S(1)}, bf16[1,1,12,128,128]{4,3,2,1,0:T(8,128)(2,1)S(1)}, u32[]{:S(2)}, u32[]{:S(2)}) collective-permute-start(bf16[1,1,12,128,128]{4,3,2,1,0:T(8,128)(2,1)S(1)} %and_select_fusion), channel_id=1, source_target_pairs={{16,0},{0,16},{17,1},{1,17},{18,2},{2,18},{19,3},{3,19},{20,4},{4,... | collective-permute-start | bytes 1179656 | tf_op jit(solution)/shard_map/ppermute | solution.py:21
  13.8 0.8 copy.94
  14.6 0.6 gather_fusion.1
  16.0 0.6 gather_fusion.2
  16.7 7.0 %collective-permute-done.1 = bf16[1,1,12,128,128]{4,3,2,1,0:T(8,128)(2,1)S(1)} collective-permute-done((bf16[1,1,12,128,128]{4,3,2,1,0:T(8,128)(2,1)S(1)}, bf16[1,1,12,128,128]{4,3,2,1,0:T(8,128)(2,1)S(1)}, u32[]{:S(2)}, u32[]{:S(2)}) %collective-permute-start.1) | collective-permute-done | bytes 393248 | tf_op jit(solution)/shard_map/ppermute | solution.py:21
  23.7 7.6 %collective-permute-done = bf16[1,1,12,128,128]{4,3,2,1,0:T(8,128)(2,1)S(1)} collective-permute-done((bf16[1,1,12,128,128]{4,3,2,1,0:T(8,128)(2,1)S(1)}, bf16[1,1,12,128,128]{4,3,2,1,0:T(8,128)(2,1)S(1)}, u32[]{:S(2)}, u32[]{:S(2)}) %collective-permute-start) | collective-permute-done | bytes 393248 | tf_op jit(solution)/shard_map/ppermute | solution.py:20
  31.3 1.1 pad_maximum_fusion.1
  32.4 3.9 %collective-permute-start.3 = (bf16[3,1,12,128,128]{4,3,2,1,0:T(8,128)(2,1)}, bf16[3,1,12,128,128]{4,3,2,1,0:T(8,128)(2,1)S(1)}, u32[]{:S(2)}, u32[]{:S(2)}) collective-permute-start(bf16[3,1,12,128,128]{4,3,2,1,0:T(8,128)(2,1)} %pad_maximum_fusion.1), channel_id=1, source_target_pairs={{4,0},{8,4},{12,8},{0,12},{5,1},{9,5},{13,9},{1,13},{6,2},{10,6},{... | collective-permute-start | bytes 3538952 | tf_op jit(solution)/shard_map/ppermute | solution.py:21
  36.5 0.8 fusion.31
  37.6 0.8 compare_reduce_fusion
  38.8 24.2 %collective-permute-done.3 = bf16[3,1,12,128,128]{4,3,2,1,0:T(8,128)(2,1)S(1)} collective-permute-done((bf16[3,1,12,128,128]{4,3,2,1,0:T(8,128)(2,1)}, bf16[3,1,12,128,128]{4,3,2,1,0:T(8,128)(2,1)S(1)}, u32[]{:S(2)}, u32[]{:S(2)}) %collective-permute-start.3) | collective-permute-done | bytes 1179680 | tf_op jit(solution)/shard_map/ppermute | solution.py:21
  63.0 24.1 %collective-permute-done.2 = bf16[3,1,12,128,128]{4,3,2,1,0:T(8,128)(2,1)} collective-permute-done((bf16[3,1,12,128,128]{4,3,2,1,0:T(8,128)(2,1)}, bf16[3,1,12,128,128]{4,3,2,1,0:T(8,128)(2,1)}, u32[]{:S(2)}, u32[]{:S(2)}) %collective-permute-start.2) | collective-permute-done | bytes 1179680 | tf_op jit(solution)/shard_map/ppermute | solution.py:20
  87.2 3.1 %pad_maximum_fusion = bf16[3,3,12,128,128]{4,3,2,1,0:T(8,128)(2,1)} fusion(bf16[3,1,12,128,128]{4,3,2,1,0:T(8,128)(2,1)S(1)} %collective-permute-done.3, bf16[1,1,12,128,128]{4,3,2,1,0:T(8,128)(2,1)S(1)} %collective-permute-done.1, bf16[1,1,12,128,128]{4,3,2,1,0:T(8,128)(2,1)S(1)} %and_select_fusion, ...), kind=kLoop, calls=%fused_computation.20 | loop fusion | flops 7077888 | bytes 7077888 | tf_op jit(solution)/shard_map/concatenate | solution.py:22
  90.2 9.5 %gather_fusion.3 = bf16[144,128,128]{2,1,0:T(8,128)(2,1)} fusion(bf16[108,128,128]{2,1,0:T(8,128)(2,1)} %bitcast.118, s32[1024]{0:T(1024)S(1)} %pad_clamp_fusion.2), kind=kCustom, calls=%fused_computation.6 | custom fusion | bytes 9437760 | tf_op jit(solution)/shard_map/jit(_take)/gather | solution.py:105
  99.8 2.6 %gather_fusion.4 = bf16[12,128,128]{2,1,0:T(8,128)(2,1)S(1)} fusion(bf16[108,128,128]{2,1,0:T(8,128)(2,1)} %bitcast.119, s32[1024]{0:T(1024)S(1)} %pad_clamp_fusion.1), kind=kCustom, calls=%fused_computation.7 | custom fusion | bytes 786480 | tf_op jit(solution)/shard_map/jit(_take)/gather | solution.py:102
  102.4 5.6 %fusion.9 = bf16[4,12,128,128]{2,3,1,0:T(8,128)(2,1)} fusion(bf16[4,3,12,128,128]{4,3,2,1,0:T(8,128)(2,1)} %bitcast.123, pred[4,3,12]{2,1,0:T(4,128)(4,1)S(1)} %copy.104, pred[4,3,12]{2,1,0:T(4,128)(4,1)S(1)} %copy.103, bf16[4,3,128,128]{3,2,1,0:T(8,128)(2,1)S(1)} %bitcast.126, pred[4,3]{1,0:T(4,128)(4,1)S(1)} %copy.106), kind=kOutput, calls=%fused_computation.27 | convolution fusion | flops 609681408 | bytes 6684972 | tf_op jit(solution)/shard_map/imab,imwac->iwbc/dot_general | solution.py:108
  108.1 27.7 %reduce-scatter.3.cloned.1.call-done = bf16[1,12,128,128]{2,3,1,0:T(8,128)(2,1)} async-done(((bf16[4,12,128,128]{2,3,1,0:T(8,128)(2,1)}), bf16[1,12,128,128]{2,3,1,0:T(8,128)(2,1)}) %reduce-scatter.3.cloned.1.call-update) | async-done | bytes 393232 | tf_op jit(solution)/shard_map/reduce_scatter | solution.py:111
  135.8 1.9 copy.109
  137.7 0.2 reduce-scatter.5.cloned.1.call-start
  137.9 0.2 copy.93
  138.2 0.7 dynamic_slice.37
  138.9 0.7 gather_fusion.9
  139.5 0.7 gather_fusion.7
  140.2 0.6 dynamic_slice.35
  140.8 0.7 gather_fusion.8
  141.4 0.6 dynamic_slice.36
  144.1 13.6 %all-gather.2.cloned.1.call-done = bf16[4,12,128,128]{3,2,1,0:T(8,128)(2,1)} async-done(((bf16[1,12,128,128]{3,2,1,0:T(8,128)(2,1)}), bf16[4,12,128,128]{3,2,1,0:T(8,128)(2,1)}) %all-gather.2.cloned.1.call-update) | async-done | bytes 1572880 | tf_op jit(solution)/shard_map/all_gather | solution.py:114
  157.7 2.1 gather_fusion.5
  159.8 5.6 %fusion.10 = bf16[4,12,128,128]{2,3,1,0:T(8,128)(2,1)} fusion(bf16[4,3,128,128,1]{3,2,4,1,0:T(8,128)(2,1)S(1)} %bitcast.125, bf16[4,3,12,128,128]{4,3,2,1,0:T(8,128)(2,1)} %bitcast.124, pred[4,3,12]{2,1,0:T(4,128)(4,1)S(1)} %copy.104, pred[4,3,12]{2,1,0:T(4,128)(4,1)S(1)} %copy.103), kind=kOutput, calls=%fused_computation.28 | convolution fusion | flops 609484800 | bytes 6684960 | tf_op jit(solution)/shard_map/imab,imwbc->iwac/dot_general | solution.py:116
  167.0 0.6 gather_fusion.6
  167.8 25.9 %reduce-scatter.5.cloned.1.call-done = bf16[1,12,128,128]{2,3,1,0:T(8,128)(2,1)} async-done(((bf16[4,12,128,128]{2,3,1,0:T(8,128)(2,1)}), bf16[1,12,128,128]{2,3,1,0:T(8,128)(2,1)}) %reduce-scatter.5.cloned.1.call-update) | async-done | bytes 393232 | tf_op jit(solution)/shard_map/reduce_scatter | solution.py:119
  193.7 1.8 fusion.11
  195.5 0.2 fusion.35
  196.0 4.8 %while.17 = (s32[]{:T(128)}, f32[1024,144]{0,1:T(8,128)S(1)}, f32[3,144,32]{1,2,0:T(8,128)S(1)}, f32[3,144,32]{1,2,0:T(8,128)S(1)}, f32[3,144,144]{2,1,0:T(8,128)S(1)}, /*index=5*/s32[]{:T(128)}, s32[]{:T(128)}) while((s32[]{:T(128)}, f32[1024,144]{0,1:T(8,128)S(1)}, f32[3,144,32]{1,2,0:T(8,128)S(1)}, ...), condition=%wide.region_9.11_spmd.clone, body=%wide.region_8.10_spmd.clone.sunk | while | flops 255246336 | bytes 3076199 | solution.py:57
  196.2 1.4 convolution_add_fusion.2
  197.8 1.4 convolution_add_fusion.2
  199.4 1.4 convolution_add_fusion.2
  200.8 0.2 copy.117
  201.1 1.5 collective-permute-start.5
  202.6 0.6 collective-permute-start.4
  203.2 4.4 %collective-permute-done.5 = bf16[8,32,144]{2,1,0:T(8,128)(2,1)S(1)} collective-permute-done((bf16[8,32,144]{2,1,0:T(8,128)(2,1)S(1)}, bf16[8,32,144]{2,1,0:T(8,128)(2,1)S(1)}, u32[]{:S(2)}, u32[]{:S(2)}) %collective-permute-start.5) | collective-permute-done | bytes 73760 | tf_op jit(solution)/shard_map/ppermute | solution.py:21
  207.5 1.6 collective-permute-done.4
  209.2 3.4 %collective-permute-start.7 = (bf16[48,8,144]{2,1,0:T(8,128)(2,1)S(1)}, bf16[48,8,144]{2,1,0:T(8,128)(2,1)S(1)}, u32[]{:S(2)}, u32[]{:S(2)}) collective-permute-start(bf16[48,8,144]{2,1,0:T(8,128)(2,1)S(1)} %get-tuple-element.183), channel_id=1, source_target_pairs={{4,0},{8,4},{12,8},{0,12},{5,1},{9,5},{13,9},{1,13},{6,2},{10,6},{... | collective-permute-start | bytes 331784 | tf_op jit(solution)/shard_map/ppermute | solution.py:21
  212.6 5.4 %collective-permute-done.7 = bf16[48,8,144]{2,1,0:T(8,128)(2,1)S(1)} collective-permute-done((bf16[48,8,144]{2,1,0:T(8,128)(2,1)S(1)}, bf16[48,8,144]{2,1,0:T(8,128)(2,1)S(1)}, u32[]{:S(2)}, u32[]{:S(2)}) %collective-permute-start.7) | collective-permute-done | bytes 110624 | tf_op jit(solution)/shard_map/ppermute | solution.py:21
  218.0 3.1 %collective-permute-done.6 = bf16[48,8,144]{2,1,0:T(8,128)(2,1)S(1)} collective-permute-done((bf16[48,8,144]{2,1,0:T(8,128)(2,1)S(1)}, bf16[48,8,144]{2,1,0:T(8,128)(2,1)S(1)}, u32[]{:S(2)}, u32[]{:S(2)}) %collective-permute-start.6) | collective-permute-done | bytes 110624 | tf_op jit(solution)/shard_map/ppermute | solution.py:20
  221.1 0.2 pad_maximum_fusion.2
  221.4 0.3 fusion.114
  221.7 0.2 copy.119
  221.9 0.2 copy.118
  222.2 0.5 collective-permute-start.8
  222.7 0.3 fusion.16
  223.0 0.9 copy.122
  223.9 0.9 collective-permute-done.9
  224.9 0.3 copy.121
  225.2 1.1 collective-permute-done.8
  226.2 0.3 copy.120
  226.5 0.8 maximum_convert_fusion
  227.9 0.4 scatter-add.26
  228.4 2.5 %scatter-add.29 = f32[16,16,128]{2,1,0:T(8,128)S(1)} dynamic-update-slice(f32[16,16,128]{2,1,0:T(8,128)S(1)} %scatter-add.26, f32[16,16,8]{2,1,0:T(8,128)S(1)} %slice_add_fusion.2, s32[]{:T(128)} %constant.424.clone.1, s32[]{:T(128)} %constant.424.clone.1, s32[]{:T(128)} %constant.448.clone.1) | dynamic-update-slice | bytes 16388 | tf_op jit(solution)/shard_map/scatter-add | solution.py:162
  230.9 0.6 copy-done.5
  (118 shorter events, 5.4 us)
Async XLA Ops:
  7.2 159.9 %copy-start = (bf16[32,6,128]{2,0,1:T(8,128)(2,1)S(1)}, bf16[32,6,128]{2,0,1:T(8,128)(2,1)}, u32[]{:S(2)}) copy-start(bf16[32,6,128]{2,0,1:T(8,128)(2,1)} %param.27) | copy-start | bytes 147460
  7.2 128.6 %reduce-scatter.3.cloned.1.call-start = ((), (), s32[]{:S(2)}) async-start(), calls=%async_computation.2 | async-start | bytes 1966080 | tf_op jit(solution)/shard_map/reduce_scatter | solution.py:111
  10.8 12.9 %collective-permute-start.1 = (bf16[1,1,12,128,128]{4,3,2,1,0:T(8,128)(2,1)S(1)}, bf16[1,1,12,128,128]{4,3,2,1,0:T(8,128)(2,1)S(1)}, u32[]{:S(2)}, u32[]{:S(2)}) collective-permute-start(bf16[1,1,12,128,128]{4,3,2,1,0:T(8,128)(2,1)S(1)} %and_select_fusion), channel_id=1, source_target_pairs={{16,0},{0,16},{17,1},{1,17},{18,2},{2,18},{19,3},{3,19},{20,4},{4,... | collective-permute-start | bytes 1179656 | tf_op jit(solution)/shard_map/ppermute | solution.py:21
  13.8 17.5 %collective-permute-start = (bf16[1,1,12,128,128]{4,3,2,1,0:T(8,128)(2,1)S(1)}, bf16[1,1,12,128,128]{4,3,2,1,0:T(8,128)(2,1)S(1)}, u32[]{:S(2)}, u32[]{:S(2)}) collective-permute-start(bf16[1,1,12,128,128]{4,3,2,1,0:T(8,128)(2,1)S(1)} %and_select_fusion), channel_id=1, source_target_pairs={{0,16},{16,0},{1,17},{17,1},{2,18},{18,2},{3,19},{19,3},{4,20},{20... | collective-permute-start | bytes 1179656 | tf_op jit(solution)/shard_map/ppermute | solution.py:20
  32.4 30.6 %collective-permute-start.3 = (bf16[3,1,12,128,128]{4,3,2,1,0:T(8,128)(2,1)}, bf16[3,1,12,128,128]{4,3,2,1,0:T(8,128)(2,1)S(1)}, u32[]{:S(2)}, u32[]{:S(2)}) collective-permute-start(bf16[3,1,12,128,128]{4,3,2,1,0:T(8,128)(2,1)} %pad_maximum_fusion.1), channel_id=1, source_target_pairs={{4,0},{8,4},{12,8},{0,12},{5,1},{9,5},{13,9},{1,13},{6,2},{10,6},{... | collective-permute-start | bytes 3538952 | tf_op jit(solution)/shard_map/ppermute | solution.py:21
  36.3 50.9 %collective-permute-start.2 = (bf16[3,1,12,128,128]{4,3,2,1,0:T(8,128)(2,1)}, bf16[3,1,12,128,128]{4,3,2,1,0:T(8,128)(2,1)}, u32[]{:S(2)}, u32[]{:S(2)}) collective-permute-start(bf16[3,1,12,128,128]{4,3,2,1,0:T(8,128)(2,1)} %pad_maximum_fusion.1), channel_id=1, source_target_pairs={{0,4},{4,8},{8,12},{12,0},{1,5},{5,9},{9,13},{13,1},{2,6},{6,10},{... | collective-permute-start | bytes 3538952 | tf_op jit(solution)/shard_map/ppermute | solution.py:20
  108.0 29.9 %copy-start.4 = (bf16[1,12,128,128]{3,2,1,0:T(8,128)(2,1)S(1)}, bf16[1,12,128,128]{3,2,1,0:T(8,128)(2,1)}, u32[]{:S(2)}) copy-start(bf16[1,12,128,128]{3,2,1,0:T(8,128)(2,1)} %param.24) | copy-start | bytes 1179652
  108.0 30.2 %copy-start.1 = (s32[32]{0:T(128)S(1)}, s32[32]{0:T(128)}, u32[]{:S(2)}) copy-start(s32[32]{0:T(128)} %param.31) | copy-start | bytes 388
  108.0 31.5 %copy-start.2 = (s32[32]{0:T(128)S(1)}, s32[32]{0:T(128)}, u32[]{:S(2)}) copy-start(s32[32]{0:T(128)} %param.29) | copy-start | bytes 388
  108.0 32.8 %copy-start.3 = (s32[32]{0:T(128)S(1)}, s32[32]{0:T(128)}, u32[]{:S(2)}) copy-start(s32[32]{0:T(128)} %param.30) | copy-start | bytes 388
  108.0 49.6 %all-gather.2.cloned.1.call-start = ((), (), s32[]{:S(2)}) async-start(), calls=%async_computation.3 | async-start | bytes 1966080 | tf_op jit(solution)/shard_map/all_gather | solution.py:114
  137.7 56.0 %reduce-scatter.5.cloned.1.call-start = ((), (), s32[]{:S(2)}) async-start(), calls=%async_computation.4 | async-start | bytes 1966080 | tf_op jit(solution)/shard_map/reduce_scatter | solution.py:119
  159.8 5.7 %copy-start.7 = (s32[1,12]{1,0:T(1,128)S(1)}, s32[1,12]{1,0:T(1,128)}, u32[]{:S(2)}) copy-start(s32[1,12]{1,0:T(1,128)} %param.28) | copy-start | bytes 148
  201.1 6.5 %collective-permute-start.5 = (bf16[8,32,144]{2,1,0:T(8,128)(2,1)S(1)}, bf16[8,32,144]{2,1,0:T(8,128)(2,1)S(1)}, u32[]{:S(2)}, u32[]{:S(2)}) collective-permute-start(bf16[8,32,144]{2,1,0:T(8,128)(2,1)S(1)} %bitcast.128), channel_id=1, source_target_pairs={{16,0},{0,16},{17,1},{1,17},{18,2},{2,18},{19,3},{3,19},{20,4},{4,... | collective-permute-start | bytes 221192 | tf_op jit(solution)/shard_map/ppermute | solution.py:21
  202.6 6.6 %collective-permute-start.4 = (bf16[8,32,144]{2,1,0:T(8,128)(2,1)S(1)}, bf16[8,32,144]{2,1,0:T(8,128)(2,1)S(1)}, u32[]{:S(2)}, u32[]{:S(2)}) collective-permute-start(bf16[8,32,144]{2,1,0:T(8,128)(2,1)S(1)} %bitcast.127), channel_id=1, source_target_pairs={{0,16},{16,0},{1,17},{17,1},{2,18},{18,2},{3,19},{19,3},{4,20},{20... | collective-permute-start | bytes 221192 | tf_op jit(solution)/shard_map/ppermute | solution.py:20
  209.2 8.7 %collective-permute-start.7 = (bf16[48,8,144]{2,1,0:T(8,128)(2,1)S(1)}, bf16[48,8,144]{2,1,0:T(8,128)(2,1)S(1)}, u32[]{:S(2)}, u32[]{:S(2)}) collective-permute-start(bf16[48,8,144]{2,1,0:T(8,128)(2,1)S(1)} %get-tuple-element.183), channel_id=1, source_target_pairs={{4,0},{8,4},{12,8},{0,12},{5,1},{9,5},{13,9},{1,13},{6,2},{10,6},{... | collective-permute-start | bytes 331784 | tf_op jit(solution)/shard_map/ppermute | solution.py:21
  212.6 8.5 %collective-permute-start.6 = (bf16[48,8,144]{2,1,0:T(8,128)(2,1)S(1)}, bf16[48,8,144]{2,1,0:T(8,128)(2,1)S(1)}, u32[]{:S(2)}, u32[]{:S(2)}) collective-permute-start(bf16[48,8,144]{2,1,0:T(8,128)(2,1)S(1)} %get-tuple-element.182), channel_id=1, source_target_pairs={{0,4},{4,8},{8,12},{12,0},{1,5},{5,9},{9,13},{13,1},{2,6},{6,10},{... | collective-permute-start | bytes 331784 | tf_op jit(solution)/shard_map/ppermute | solution.py:20
  221.4 1.3 copy-start.6
  221.9 3.0 %collective-permute-start.9 = (bf16[48,48,8]{1,2,0:T(8,128)(2,1)S(1)}, bf16[48,48,8]{1,2,0:T(8,128)(2,1)S(1)}, u32[]{:S(2)}, u32[]{:S(2)}) collective-permute-start(bf16[48,48,8]{1,2,0:T(8,128)(2,1)S(1)} %copy.119), channel_id=1, source_target_pairs={{1,0},{2,1},{3,2},{0,3},{5,4},{6,5},{7,6},{4,7},{9,8},{10,9},{11,1... | collective-permute-start | bytes 110600 | tf_op jit(solution)/shard_map/ppermute | solution.py:21
  222.2 4.1 %collective-permute-start.8 = (bf16[48,48,8]{1,2,0:T(8,128)(2,1)S(1)}, bf16[48,48,8]{1,2,0:T(8,128)(2,1)S(1)}, u32[]{:S(2)}, u32[]{:S(2)}) collective-permute-start(bf16[48,48,8]{1,2,0:T(8,128)(2,1)S(1)} %copy.118), channel_id=1, source_target_pairs={{0,1},{1,2},{2,3},{3,0},{4,5},{5,6},{6,7},{7,4},{8,9},{9,10},{10,1... | collective-permute-start | bytes 110600 | tf_op jit(solution)/shard_map/ppermute | solution.py:20
  230.9 0.7 copy-start.5
Sparse Core Ops, SparseCore 0:
  108.2 27.5 reduce-scatter.2
  138.0 19.6 all-gather.1
  165.5 28.1 reduce-scatter.4
where the time goes:
time: 239 us; the launch traced here: 238 us
  waiting for transfers between devices  147 us (62%)
  local copies, waits for them, and re-layouts  32.9 us (14%)
  matrix products  17.5 us (7%)
  between operations  16.1 us (7%)
  starting transfers between devices  13.3 us (6%)
  other arithmetic  11.4 us (5%)
    ppermute x5, waiting for transfers between devices, extended(): after = lax.ppermute(first, axis, down)  41.9 us
    ppermute x5, waiting for transfers between devices, extended(): before = lax.ppermute(last, axis, up)  37.6 us
    reduce_scatter x1, waiting for transfers between devices, local(): lax.psum_scatter(first_terms.astype(jnp.bfloat16), 'layer', scatter_dimen...  27.7 us
    reduce_scatter x1, waiting for transfers between devices, local(): lax.psum_scatter(second_terms.astype(jnp.bfloat16), 'layer', scatter_dime...  25.9 us
    all_gather x1, waiting for transfers between devices, local(): tile_square = lax.all_gather(square_row, 'layer', axis=0, tiled=True)  13.6 us
    ppermute x5, starting transfers between devices, extended(): after = lax.ppermute(first, axis, down)  11.8 us
    gather x1, local copies, waits for them, and re-layouts, local(): jnp.take(around_flat, right_index, axis=0)  9.53 us
    dot_general x1, matrix products, local(): jnp.einsum('imab,imwbc->iwac', left_square, right_x, preferred_element_ty...  5.62 us
  transfers between devices with their start and end apart: 13, of which 13 were waited for; matrix products, arithmetic and copies ran while one was open for 6% of the time, Pallas kernels for 0%

commit v1 on v0

v1 whole, which is shorter than its diff:
```python
import functools

import jax
import jax.numpy as jnp
from jax import lax
from jax.experimental import pallas as pl
from jax.experimental.pallas import tpu as pltpu
from jax.sharding import PartitionSpec as P

DRIFT = 2
BX = 16
BY = 16
BZ = 128
LANES = 128
VMEM = pl.BlockSpec(memory_space=pltpu.VMEM)
SMEM = pl.BlockSpec(memory_space=pltpu.SMEM)
ANY = pl.BlockSpec(memory_space=pl.ANY)


def from_offset(x, axis, step):
    count = lax.axis_size(axis)
    return lax.ppermute(x, axis, [((i + step) % count, i) for i in range(count)])


def from_layer(x, flip):
    count = lax.axis_size("layer")
    return lax.ppermute(x, "layer", [(i ^ flip, i) for i in range(count)])


def column_targets(n_row, row):
    same = [(0, 0), (0, 1), (0, 2)]
    if n_row == 2:
        return same + [(1, row), (1, row + 1)]
    return same + [(1, 0), (1, 1), (1, 2), (1, 3)]


def pick_kernel(n_row, n_col, n_lay, listed_ref, sign_ref, out_ref, sems):
    row = lax.axis_index("row")
    col = lax.axis_index("col")
    lay = lax.axis_index("layer")
    slots = sign_ref.shape[0]
    copies = []
    for i, (step_row, step_lay) in enumerate(column_targets(n_row, row)):
        target = (lax.rem(row + step_row, n_row) * n_col + col) * n_lay + lax.rem(lay + step_lay, n_lay)
        place = jnp.int32(0)
        for u in range(slots):
            place = jnp.where(listed_ref[u] == target, u, place)
        copy = pltpu.make_async_copy(sign_ref.at[place], out_ref.at[i], sems.at[i])
        copy.start()
        copies.append(copy)
    for copy in copies:
        copy.wait()


def step_kernel(offsets, lengths, pairs, n_pool, *refs):
    tab_ref, info_ref, basis_ref, spread_ref, sign_ref = refs[:5]
    piece_refs = refs[5 : 5 + len(offsets)]
    next_ref, coef_ref, pool, gram, own, square, sems = refs[5 + len(offsets) :]
    slots, size = sign_ref.shape[0], sign_ref.shape[1]
    copies = []
    for i, piece in enumerate(piece_refs):
        copy = pltpu.make_async_copy(piece, pool.at[pl.ds(offsets[i], lengths[i])], sems.at[i])
        copy.start()
        copies.append(copy)
    pool[n_pool] = jnp.zeros((size, size), pool.dtype)
    rows = lax.broadcasted_iota(jnp.int32, (size, size), 0)
    lanes = lax.broadcasted_iota(jnp.int32, (size, size), 1)
    own_size = info_ref[slots]
    self_slot = info_ref[slots + 1]
    for w in range(slots):
        kept = (rows < own_size) & (lanes < info_ref[w])
        block = jnp.where(kept, sign_ref[w].astype(jnp.float32), 0.0)
        own[:, w * size : (w + 1) * size] = block.astype(own.dtype)
    for copy in copies:
        copy.wait()

    def place(i, carry):
        p = pl.multiple_of(tab_ref[i] * size, size)
        q = pl.multiple_of(tab_ref[pairs + i] * size, size)
        block = pool[tab_ref[2 * pairs + i]]
        gram[pl.ds(p, size), pl.ds(q, size)] = block
        gram[pl.ds(q, size), pl.ds(p, size)] = block.T
        return carry

    lax.fori_loop(0, pairs, place, 0)
    wide = 2 * size
    wide_lanes = lax.broadcasted_iota(jnp.int32, (size, wide), 1)
    wide_rows = lax.broadcasted_iota(jnp.int32, (size, wide), 0)

    def column_kept(n):
        first = info_ref[2 * n]
        second = info_ref[2 * n + 1]
        return (wide_lanes < first) | ((wide_lanes >= size) & (wide_lanes < size + second))

    for n in range(slots // 2):
        part = jnp.dot(own[...], gram[:, n * wide : (n + 1) * wide], preferred_element_type=jnp.float32)
        square[:, n * wide : (n + 1) * wide] = jnp.where(column_kept(n), part, 0.0).astype(square.dtype)
    coef = jnp.zeros((basis_ref.shape[0], LANES), jnp.float32)
    for n in range(slots // 2):
        part = jnp.dot(square[...], gram[:, n * wide : (n + 1) * wide], preferred_element_type=jnp.float32)
        cube = jnp.where(column_kept(n), part, 0.0)
        full = 1.5 * own[:, n * wide : (n + 1) * wide].astype(jnp.float32) - 0.5 * cube
        next_ref[2 * n] = full[:, :size].astype(next_ref.dtype)
        next_ref[2 * n + 1] = full[:, size:].astype(next_ref.dtype)
        shift = (self_slot - 2 * n) * size
        is_self = (self_slot >= 2 * n) & (self_slot < 2 * n + 2)
        diag = (wide_lanes == wide_rows + shift) & (wide_rows < own_size) & is_self
        dmat = 0.5 * (jnp.where(diag, 1.0, 0.0) - full)
        high = dmat.astype(jnp.bfloat16)
        low = (dmat - high.astype(jnp.float32)).astype(jnp.bfloat16)
        half = jnp.dot(basis_ref[...], high, preferred_element_type=jnp.float32) + jnp.dot(
            basis_ref[...], low, preferred_element_type=jnp.float32
        )
        half_high = half.astype(jnp.bfloat16)
        half_low = (half - half_high.astype(jnp.float32)).astype(jnp.bfloat16)
        spread = spread_ref[n * wide : (n + 1) * wide]
        coef = coef + jnp.dot(half_high, spread, preferred_element_type=jnp.float32)
        coef = coef + jnp.dot(half_low, spread, preferred_element_type=jnp.float32)
    coef_ref[...] = coef[: coef_ref.shape[0]]


def profile_kernel(periods, lane_ref, sub_ref, plane_ref, line_ref):
    shells = plane_ref.shape[1]
    cells = plane_ref.shape[2]
    cell = lax.broadcasted_iota(jnp.int32, (cells, LANES), 0)
    grid_x = (cell // BY).astype(jnp.float32)
    grid_y = (cell % BY).astype(jnp.float32)
    grid_z = lax.broadcasted_iota(jnp.int32, (LANES, BZ), 1).astype(jnp.float32)

    def nearest(offset, period):
        return offset - period * jnp.floor(offset * (1.0 / period) + 0.5)

    for o in range(lane_ref.shape[0]):
        row = lane_ref[o]
        d_x = nearest(grid_x - row[0:1], periods[0])
        d_y = nearest(grid_y - row[1:2], periods[1])
        inside = (jnp.abs(d_x) <= row[3:4]) & (jnp.abs(d_y) <= row[3:4])
        squared = d_x * d_x + d_y * d_y
        sub = sub_ref[o]
        d_z = nearest(grid_z - sub[:, 2:3], periods[2])
        inside_z = jnp.abs(d_z) <= sub[:, 3:4]
        squared_z = d_z * d_z
        for s in range(shells):
            part = 1.0 / ((s + 1) * (s + 1))
            rate = row[5:6] * part + row[4:5]
            plane_ref[o, s] = jnp.where(inside, jnp.exp(-rate * squared), 0.0).astype(plane_ref.dtype)
            rate_z = sub[:, 5:6] * part + sub[:, 4:5]
            line_ref[o, s] = jnp.where(inside_z, jnp.exp(-rate_z * squared_z), 0.0).astype(line_ref.dtype)


def density_kernel(tiles, *refs):
    tile_refs = refs[:tiles]
    plane_ref, line_ref, out_ref, terms = refs[tiles:]
    shells = plane_ref.shape[1]
    for o in range(tiles):
        for s in range(shells):
            scaled = plane_ref[o, s].astype(jnp.float32) * tile_refs[o][s : s + 1, :]
            at = (o * shells + s) * LANES
            terms[:, at : at + LANES] = scaled.astype(terms.dtype)
    out_ref[...] = jnp.dot(terms[...], line_ref[...], preferred_element_type=jnp.float32)


def local(sign_start, neighbors, atom_size, basis_proj, pair_extent, atom_x, atom_y, atom_z):
    n_row = lax.axis_size("row")
    n_col = lax.axis_size("col")
    n_lay = lax.axis_size("layer")
    assert n_lay == 4 and n_col >= 4 and (n_row == 2 or n_row >= 4)
    row = lax.axis_index("row")
    col = lax.axis_index("col")
    lay = lax.axis_index("layer")
    atoms, slots = neighbors.shape
    size = sign_start.shape[2]
    shells = basis_proj.shape[1]
    me = (row * n_col + col) * n_lay + lay
    steps = [0, 1] if n_row == 2 else [0, 1, -1]
    count = len(steps)
    own = sign_start[0]
    listed = lax.dynamic_index_in_dim(neighbors, me, 0, keepdims=False)

    n_pick = len(column_targets(n_row, 0))
    picked = pl.pallas_call(
        functools.partial(pick_kernel, n_row, n_col, n_lay),
        out_shape=jax.ShapeDtypeStruct((n_pick, size, size), own.dtype),
        in_specs=[SMEM, ANY],
        out_specs=ANY,
        scratch_shapes=[pltpu.SemaphoreType.DMA((n_pick,))],
        name="pick_column_blocks",
    )(listed, own)
    half = slots // 2
    first, second = own[:half], own[half:]
    pieces = {}

    def give(name, di, flip, value, start, width):
        pieces[(name, di, flip)] = (value, start, width)

    a_parts, b_parts, up_parts, down_parts = {}, {}, {}, {}
    a_parts[0, 0], b_parts[0, 0] = first, second
    for di in range(1, count):
        a_parts[di, 0] = from_offset(first, "row", steps[di])
    b_parts[0, 2] = from_layer(second, 2)
    up_parts[0, 0] = from_offset(picked, "col", 1)
    down_parts[0, 0] = from_offset(picked, "col", -1)
    for di in range(count):
        a_parts[di, 2] = from_layer(a_parts[di, 0], 2)
    for di in range(1, count):
        for flip in (0, 2):
            b_parts[di, flip] = from_offset(b_parts[0, flip], "row", steps[di])
    for di in range(1, count):
        up_parts[di, 0] = from_offset(up_parts[0, 0], "row", steps[di])
    down_parts[0, 2] = from_layer(down_parts[0, 0], 2)
    for di in range(count):
        up_parts[di, 2] = from_layer(up_parts[di, 0], 2)
    for di in range(1, count):
        for flip in (0, 2):
            down_parts[di, flip] = from_offset(down_parts[0, flip], "row", steps[di])
    values, starts, widths = [], [], []

    def add(value, start):
        values.append(value)
        starts.append(start)
        widths.append(value.shape[0])

    column_base = count * 4 * slots
    for di in range(count):
        for flip in (0, 2):
            place = (di * 4 + flip) * slots
            mate = (di * 4 + flip + 1) * slots
            if di == 0 and flip == 0:
                add(own, place)
                add(from_layer(own, 1), mate)
            else:
                add(a_parts[di, flip], place)
                add(b_parts[di, flip], place + half)
                add(from_layer(a_parts[di, flip], 1), mate)
                add(from_layer(b_parts[di, flip], 1), mate + half)
            for side, parts in enumerate((up_parts, down_parts)):
                base = column_base + ((side * count + di) * 4 + flip) * n_pick
                add(parts[di, flip], base)
                add(from_layer(parts[di, flip], 1), base + n_pick)
    n_pool = column_base + 2 * count * 4 * n_pick

    atom_ids = jnp.arange(atoms, dtype=jnp.int32)
    l_row = listed // (n_lay * n_col)
    l_col = listed // n_lay % n_col
    l_lay = listed % n_lay
    step_row = (l_row - row) % n_row
    row_place = jnp.where(step_row == 0, 0, jnp.where(step_row == 1, 1, 2))
    step_col = (l_col - col) % n_col
    in_column = step_col == 0
    side = jnp.where(step_col == 1, 0, 1)
    line = row_place * 4 + (l_lay ^ lay)
    listings = jnp.take(neighbors, listed, axis=0)
    match = listings[:, None, :] == listed[None, :, None]
    present = jnp.any(match, axis=2)
    slot = jnp.sum(jnp.where(match, jnp.arange(slots, dtype=jnp.int32), 0), axis=2)
    d_row = (l_row[None, :] - l_row[:, None]) % n_row
    d_lay = (l_lay[None, :] - l_lay[:, None]) % n_lay
    if n_row == 2:
        lead = d_lay - l_row[:, None]
        across = jnp.where((lead >= 0) & (lead < 2), 3 + lead, -1)
    else:
        across = 3 + d_lay
    target = jnp.where(d_row == 0, jnp.where(d_lay < 3, d_lay, -1), jnp.where(d_row == 1, across, -1))
    beside = ~in_column[:, None] & (step_col[:, None] == step_col[None, :]) & (target >= 0)
    direct = present & (in_column[:, None] | beside)
    located = jnp.where(
        in_column[:, None],
        line[:, None] * slots + slot,
        column_base + (side[:, None] * count * 4 + line[:, None]) * n_pick + target,
    )
    upper = [(v, w) for v in range(slots) for w in range(v, slots)]
    pairs = len(upper)
    idx = jnp.arange(slots, dtype=jnp.int32)
    forward = direct
    backward = direct.T & ~direct
    from_p = jnp.where(backward, idx[None, :], idx[:, None])
    from_q = jnp.where(backward, idx[:, None], idx[None, :])
    source = jnp.where(forward, located, jnp.where(backward, located.T, n_pool))
    table = jnp.concatenate(
        [part[v, v:] for part in (from_p, from_q, source) for v in range(slots)]
    ).astype(jnp.int32)
    sizes = jnp.take(atom_size, listed)
    own_size = lax.dynamic_index_in_dim(atom_size, me, 0, keepdims=True)
    self_slot = jnp.sum(jnp.where(listed == me, idx, 0), keepdims=True)
    info = jnp.concatenate([sizes, own_size, self_slot]).astype(jnp.int32)

    layer_step = (neighbors % n_lay - atom_ids[:, None] % n_lay) % n_lay
    earlier = (layer_step[:, :, None] == layer_step[:, None, :]) & (idx[None, None, :] < idx[None, :, None])
    rank = 3 * layer_step + jnp.sum(earlier.astype(jnp.int32), axis=2)
    own_rank = lax.dynamic_index_in_dim(rank, me, 0, keepdims=False)
    lane = jnp.arange(LANES, dtype=jnp.int32)
    wanted = jnp.where(lane[None, :] // shells == own_rank[:, None], listed[:, None] * shells + lane[None, :] % shells, -1)
    one_hot = (wanted[:, :, None] == jnp.arange(atoms * shells, dtype=jnp.int32)).astype(jnp.bfloat16)
    spread = jnp.einsum(
        "wln,nb->wbl", one_hot, basis_proj.reshape(atoms * shells, size), preferred_element_type=jnp.float32
    ).astype(jnp.bfloat16).reshape(slots * size, LANES)
    own_basis = lax.dynamic_index_in_dim(basis_proj, me, 0, keepdims=False)
    own_basis = jnp.pad(own_basis, ((0, 16 - shells), (0, 0)))

    extents = lax.all_gather(pair_extent, ("row", "col", "layer"), axis=0, tiled=True)
    tile_steps = [(dr, dc) for dr in steps for dc in (0, 1, -1)]
    tiles = len(tile_steps)
    tile_rows = jnp.stack([(row + dr) % n_row for dr, _ in tile_steps])
    tile_cols = jnp.stack([(col + dc) % n_col for _, dc in tile_steps])
    order = [(0, k) for k in range(12)] + [(-1, k) for k in range(3, 9)] + [(1, k) for k in range(9, 12)]
    lane_layer = jnp.array([d for d, _ in order], dtype=jnp.int32)
    lane_rank = jnp.array([k for _, k in order], dtype=jnp.int32)
    pair_lay = (lay + lane_layer) % n_lay
    pair_atom = (tile_rows * n_col + tile_cols)[:, None] * n_lay + pair_lay[None, :]
    at_rank = jnp.take(rank, pair_atom, axis=0) == lane_rank[None, :, None]
    pair_other = jnp.sum(jnp.where(at_rank, jnp.take(neighbors, pair_atom, axis=0), 0), axis=2)
    pair_ext = jnp.sum(jnp.where(at_rank, jnp.take(extents, pair_atom, axis=0), 0), axis=2)
    coords = jnp.stack([atom_x, atom_y, atom_z], axis=1)
    total = (jnp.take(coords, pair_atom, axis=0) + jnp.take(coords, pair_other, axis=0)).astype(jnp.float32)
    o_row = pair_other // (n_lay * n_col)
    o_col = pair_other // n_lay % n_col
    o_lay = pair_other % n_lay
    go_row = (o_row - tile_rows[:, None] + 1) % n_row - 1
    go_col = (o_col - tile_cols[:, None] + 1) % n_col - 1
    go_lay = jnp.minimum((o_lay - pair_lay[None, :] + 1) % n_lay - 1, 1)
    base_row = jnp.array([dr for dr, _ in tile_steps], dtype=jnp.float32)[:, None] * BX
    base_col = jnp.array([dc for _, dc in tile_steps], dtype=jnp.float32)[:, None] * BY
    base_lay = lane_layer[None, :].astype(jnp.float32) * BZ
    cent_x = base_row + 0.5 * (total[..., 0] + BX * go_row.astype(jnp.float32))
    cent_y = base_col + 0.5 * (total[..., 1] + BY * go_col.astype(jnp.float32))
    cent_z = base_lay + 0.5 * (total[..., 2] + BZ * go_lay.astype(jnp.float32))
    ext = pair_ext.astype(jnp.float32)
    inverse = (shells / ext) ** 2
    shell = jnp.arange(1, shells + 1).astype(jnp.float32)
    packed = jnp.stack([cent_x, cent_y, cent_z, ext, inverse, inverse], axis=1)
    packed = jnp.broadcast_to(packed[..., None], packed.shape + (shells,))
    divided = jnp.concatenate(
        [jnp.ones((4, shells)), (1.0 / (shell * shell))[None], jnp.ones((1, shells))]
    ).astype(jnp.float32)
    packed = (packed * divided[None, :, None, :]).reshape(tiles, 6, len(order) * shells)
    spare = LANES - len(order) * shells
    lane_geo = jnp.pad(packed, ((0, 0), (0, 2), (0, spare)), constant_values=-1.0)
    sub_geo = lane_geo.transpose(0, 2, 1)
    periods = (float(BX * n_row), float(BY * n_col), float(BZ * n_lay))
    plane, line_z = pl.pallas_call(
        functools.partial(profile_kernel, periods),
        out_shape=(
            jax.ShapeDtypeStruct((tiles, shells, BX * BY, LANES), jnp.bfloat16),
            jax.ShapeDtypeStruct((tiles, shells, LANES, BZ), jnp.bfloat16),
        ),
        in_specs=[VMEM, VMEM],
        out_specs=(VMEM, VMEM),
        compiler_params=pltpu.CompilerParams(vmem_limit_bytes=32 << 20),
        cost_estimate=pl.CostEstimate(flops=30_000_000, bytes_accessed=4_000_000, transcendentals=2_000_000),
        name="profiles",
    )(lane_geo, sub_geo)

    sign_next, coef = pl.pallas_call(
        functools.partial(step_kernel, tuple(starts), tuple(widths), pairs, n_pool),
        out_shape=(
            jax.ShapeDtypeStruct((slots, size, size), jnp.bfloat16),
            jax.ShapeDtypeStruct((8, LANES), jnp.float32),
        ),
        in_specs=[SMEM, SMEM, VMEM, VMEM, VMEM] + [ANY] * len(values),
        out_specs=(VMEM, VMEM),
        scratch_shapes=[
            pltpu.VMEM((n_pool + 1, size, size), jnp.bfloat16),
            pltpu.VMEM((slots * size, slots * size), jnp.bfloat16),
            pltpu.VMEM((size, slots * size), jnp.bfloat16),
            pltpu.VMEM((size, slots * size), jnp.bfloat16),
            pltpu.SemaphoreType.DMA((len(values),)),
        ],
        compiler_params=pltpu.CompilerParams(vmem_limit_bytes=40 << 20),
        cost_estimate=pl.CostEstimate(flops=1_300_000_000, bytes_accessed=8_000_000, transcendentals=0),
        name="square_cube_coefficients",
    )(table, info, own_basis, spread, own, *values)

    per_class = 3 * shells
    below = from_offset(coef, "layer", -1)
    above = from_offset(coef, "layer", 1)
    merged = jnp.concatenate(
        [
            coef[:, : 4 * per_class],
            below[:, per_class : 3 * per_class],
            above[:, 3 * per_class : 4 * per_class],
            jnp.zeros((8, spare), jnp.float32),
        ],
        axis=1,
    )
    received = []
    for dr, dc in tile_steps:
        if dr == 0 and dc == 0:
            received.append(merged)
        elif dr == 0:
            received.append(from_offset(merged, "col", dc))
        elif dc == 0:
            received.append(from_offset(merged, "row", dr))
        else:
            moves = [
                (((i + dr) % n_row) * n_col + (j + dc) % n_col, i * n_col + j)
                for i in range(n_row)
                for j in range(n_col)
            ]
            received.append(lax.ppermute(merged, ("row", "col"), moves))
    density = pl.pallas_call(
        functools.partial(density_kernel, tiles),
        out_shape=jax.ShapeDtypeStruct((BX * BY, BZ), jnp.float32),
        in_specs=[VMEM] * (tiles + 2),
        out_specs=VMEM,
        scratch_shapes=[pltpu.VMEM((BX * BY, tiles * shells * LANES), jnp.bfloat16)],
        compiler_params=pltpu.CompilerParams(vmem_limit_bytes=32 << 20),
        cost_estimate=pl.CostEstimate(flops=310_000_000, bytes_accessed=4_000_000, transcendentals=0),
        name="density",
    )(*received, plane, line_z.reshape(tiles * shells * LANES, BZ))
    return sign_next[None], density.reshape(BX, BY, BZ)


def solution(mesh):
    rows = P(("row", "col", "layer"), None, None, None)
    in_specs = (rows, P(), P(), P(), P(("row", "col", "layer"), None), P(), P(), P())
    out_specs = (rows, P("row", "col", "layer"))
    return jax.shard_map(local, mesh=mesh, in_specs=in_specs, out_specs=out_specs, check_vma=False)
```

time: 239 us -> 177 us (0.74)
  waiting for transfers between devices: 147 us -> 12.3 us
  blocking collectives: 0 us -> 40.9 us
  Pallas kernels: 0 us -> 29.2 us
  local copies, waits for them, and re-layouts: 32.9 us -> 53.6 us
  matrix products: 17.5 us -> 0.38 us
  starting transfers between devices: 13.3 us -> 29.8 us
  between operations: 16.1 us -> 1.33 us
  other arithmetic: 11.4 us -> 8.36 us
    ppermute x10 -> x36, waiting for transfers between devices: 79.5 us -> 12.3 us  [the longest x13 9.84 us: from_offset(): lax.ppermute(x, axis, [((i + step) % count, i) for i in range(count)])]
    reduce_scatter x2 -> x0, waiting for transfers between devices: 53.6 us -> none  [the longest x1 27.7 us: local(): lax.psum_scatter(first_terms.astype(jnp.bfloat16), 'layer', scatter_dimen...]
    all_gather x0 -> x1, blocking collectives: none -> 40.9 us  [local(): lax.all_gather(pair_extent, ('row', 'col', 'layer'), axis=0, tiled=True)]
    pallas_call x0 -> x4, Pallas kernels: none -> 29.2 us  [the longest x1 18 us: local(): pl.pallas_call(functools.partial(step_kernel, tuple(starts), tuple(widths...]
    dot_general x7 -> x1, matrix products: 17.5 us -> 0.38 us  [local(): jnp.einsum('wln,nb->wbl', one_hot, basis_proj.reshape(atoms * shells, siz...]
    ppermute x10 -> x36, starting transfers between devices: 13 us -> 29.8 us  [the longest x13 17.7 us: from_offset(): lax.ppermute(x, axis, [((i + step) % count, i) for i in range(count)])]
    squeeze x0 -> x23, local copies, waits for them, and re-layouts: none -> 14.9 us  [the longest x22 13.6 us: local(): part[v, v:]]
    unnamed x21 -> x85, local copies, waits for them, and re-layouts: 2.9 us -> 16.5 us
  transfers between devices with their start and end apart: 13 -> 36, of which waited for: 13 -> 9; matrix products, arithmetic and copies ran while one was open for 6% -> 25% of each run, Pallas kernels for 0% -> 2%
where the time goes in v1:
time: 177 us; the launch traced here: 176 us
  local copies, waits for them, and re-layouts  53.6 us (30%)
  blocking collectives  40.9 us (23%)
  starting transfers between devices  29.8 us (17%)
  Pallas kernels  29.2 us (16%)
  waiting for transfers between devices  12.3 us (7%)
  other arithmetic  8.36 us (5%)
    all_gather x1, blocking collectives, local(): lax.all_gather(pair_extent, ('row', 'col', 'layer'), axis=0, tiled=True)  40.9 us
    pallas_call x1, Pallas kernels, local(): pl.pallas_call(functools.partial(step_kernel, tuple(starts), tuple(widths...  18 us
    ppermute x13, starting transfers between devices, from_offset(): lax.ppermute(x, axis, [((i + step) % count, i) for i in range(count)])  17.7 us
    unnamed x85, local copies, waits for them, and re-layouts  16.5 us
    squeeze x22, local copies, waits for them, and re-layouts, local(): part[v, v:]  13.6 us
    ppermute x13, waiting for transfers between devices, from_offset(): lax.ppermute(x, axis, [((i + step) % count, i) for i in range(count)])  9.84 us
    ppermute x21, starting transfers between devices, from_layer(): return lax.ppermute(x, 'layer', [(i ^ flip, i) for i in range(count)])  9.16 us
    pallas_call x1, Pallas kernels, local(): pl.pallas_call(functools.partial(pick_kernel, n_row, n_col, n_lay), out_s...  6.93 us
  transfers between devices with their start and end apart: 36, of which 9 were waited for; matrix products, arithmetic and copies ran while one was open for 25% of the time, Pallas kernels for 2%

profile of v1, /device:TPU:0, one launch (start us, length us, event | category | flops | bytes accessed | tf_op | source)
XLA Modules:
  0.0 175.8 jit_solution(1791263798526843093)
XLA Ops:
  0.7 1.5 fusion.11
  2.1 6.9 %pick_column_blocks.1 = bf16[5,128,128]{2,1,0:T(8,128)(2,1)} custom-call(s32[12]{0:T(128)} %get-tuple-element.17.listed_ref, bf16[12,128,128]{2,1,0:T(8,128)(2,1)} %bitcast.126), custom_call_target="tpu_custom_call" | custom-call | tf_op jit(solution)/shard_map/pick_column_blocks/pallas_call | solution.py:181
  9.1 5.1 %collective-permute-start.1 = (bf16[5,128,128]{2,1,0:T(8,128)(2,1)}, bf16[5,128,128]{2,1,0:T(8,128)(2,1)S(1)}, u32[]{:S(2)}, u32[]{:S(2)}) collective-permute-start(bf16[5,128,128]{2,1,0:T(8,128)(2,1)} %pick_column_blocks.1), channel_id=1, source_target_pairs={{4,0},{8,4},{12,8},{0,12},{5,1},{9,5},{13,9},{1,13},{6,2},{10,6},{... | collective-permute-start | bytes 491528 | tf_op jit(solution)/shard_map/ppermute | solution.py:22
  14.2 1.0 slice_bitcast_fusion
  15.2 1.6 collective-permute-start.5
  16.8 1.5 collective-permute-start.13
  19.5 0.7 gather_fusion.1
  20.2 1.3 broadcast_multiply_fusion.1
  23.8 0.7 slice_bitcast_fusion.21
  27.6 0.7 slice_bitcast_fusion.15
  28.8 0.7 slice_bitcast_fusion.13
  31.9 0.7 slice_bitcast_fusion.8
  36.2 40.9 %all-gather = s32[32,1,12]{2,1,0:T(1,128)S(1)} all-gather(s32[1,1,12]{2,1,0:T(1,128)S(1)} %bitcast.136), channel_id=1, replica_groups=mesh['row'=2,'col'=4,'layer'=4] {'row','col','layer'}, dimensions={0}, use_global_device_ids=true | all-gather | bytes 1584 | tf_op jit(solution)/shard_map/all_gather | solution.py:300
  81.7 0.7 multiply_add_fusion.1
  83.3 1.5 collective-permute-start.14
  86.0 4.3 %collective-permute-done.14.refs_20_ = bf16[6,128,128]{2,1,0:T(8,128)(2,1)S(1)} collective-permute-done((bf16[6,128,128]{2,1,0:T(8,128)(2,1)S(1)}, bf16[6,128,128]{2,1,0:T(8,128)(2,1)S(1)}, u32[]{:S(2)}, u32[]{:S(2)}) %collective-permute-start.14) | collective-permute-done | bytes 196640 | tf_op jit(solution)/shard_map/ppermute | solution.py:22
  90.3 0.7 copy-done.5
  91.0 1.5 collective-permute-start.17
  92.5 0.7 copy-done.1
  93.1 0.7 copy-done.9
  94.3 0.7 copy-done.3
  96.3 1.1 collective-permute-done.17.refs_23_
  97.4 2.0 %collective-permute-start.21 = (bf16[6,128,128]{2,1,0:T(8,128)(2,1)S(1)}, bf16[6,128,128]{2,1,0:T(8,128)(2,1)S(1)}, u32[]{:S(2)}, u32[]{:S(2)}) collective-permute-start(bf16[6,128,128]{2,1,0:T(8,128)(2,1)S(1)} %collective-permute-done.13.refs_19_), channel_id=1, source_target_pairs={{2,0},{3,1},{0,2},{1,3},{6,4},{7,5},{4,6},{5,7},{10,8},{11,9},{8,1... | collective-permute-start | bytes 589832 | tf_op jit(solution)/shard_map/ppermute | solution.py:27
  99.4 0.7 collective-permute-done.19.refs_25_
  100.1 1.5 collective-permute-start.22
  102.7 1.7 collective-permute-start.25
  105.1 0.7 collective-permute-start.27
  105.8 0.7 copy-done.11
  106.5 0.9 collective-permute-done.22.refs_28_
  108.8 0.7 copy-done.19
  109.9 0.7 copy-done.17
  110.6 0.7 copy-done.15
  112.2 1.3 dynamic-slice_bitcast_fusion
  113.5 1.3 slice.209
  115.4 1.3 slice.233
  117.3 1.3 stack.60
  118.6 1.7 broadcast_in_dim.173
  120.3 1.8 %broadcast_in_dim.174 = f32[6,6,126]{2,1,0:T(8,128)} reshape(f32[6,6,21,6]{3,2,1,0:T(8,128)} %broadcast_in_dim.173) | data formatting | bytes 36288 | tf_op jit(solution)/shard_map/broadcast_in_dim | solution.py:331
  122.1 1.7 copy.140
  124.5 1.0 mul.191
  125.4 0.7 copy.139
  126.2 2.2 %concatenate.20.refs_0_ = s32[234]{0:T(256)S(1)} concatenate(s32[12]{0:T(128)} %get-tuple-element.73, s32[11]{0:T(128)} %get-tuple-element.71, s32[10]{0:T(128)} %get-tuple-element.69, s32[9]{0:T(128)} %get-tuple-element.67, s32[8]{0:T(128)} %get-tuple-element.65, s32[7]{0:T(128)} %get-tuple-element.63, s32[6]{0:T(128)} %get-tuple-element.61, s32[5]{0:T(128)} %get-tuple-element.59, ...), dimensions={0} | concatenate | bytes 1872 | tf_op jit(solution)/shard_map/concatenate | solution.py:279
  128.4 2.0 %pad_add_fusion.1.refs_1_ = s32[14]{0:T(128)S(1)} fusion(s32[1]{0:T(128)} %bitcast.39, s32[1]{0:T(128)} %dynamic_slice.16, s32[12]{0:T(128)} %get-tuple-element.46), kind=kLoop, calls=%fused_computation.236 | loop fusion | flops 28 | bytes 112 | tf_op jit(solution)/shard_map/concatenate | solution.py:285
  130.4 0.9 copy-done.2
  131.3 0.9 copy-done.4
  132.2 0.9 copy-done.6
  133.1 0.9 copy-done.8
  134.0 0.9 copy-done.10
  134.9 0.9 copy-done.12
  135.9 0.9 copy-done.14
  136.8 0.9 copy-done.16
  137.7 0.9 copy-done.18
  138.6 0.9 copy-done.20
  139.5 18.0 %square_cube_coefficients.1 = (bf16[12,128,128]{2,1,0:T(8,128)(2,1)}, f32[8,128]{1,0:T(8,128)S(1)}) custom-call(s32[234]{0:T(256)S(1)} %concatenate.20.refs_0_, s32[14]{0:T(128)S(1)} %pad_add_fusion.1.refs_1_, bf16[16,128]{1,0:T(8,128)(2,1)S(1)} %pad.8.refs_2_, bf16[1536,128]{1,0:T(8,128)(2,1)S(1)} %bitcast.131, bf16[12,128,128]{2,1,0:T(8,128)(2,1)S(1)} %bitcast.128, ...), custom_call_target="tpu_custom_call" | custom-call | flops 1300000000 | bytes 8000000 | tf_op jit(solution)/shard_map/square_cube_coefficients/pallas_call | solution.py:353
  157.5 2.0 %collective-permute-start.30 = (f32[8,128]{1,0:T(8,128)S(1)}, f32[8,128]{1,0:T(8,128)S(1)}, u32[]{:S(2)}, u32[]{:S(2)}) collective-permute-start(f32[8,128]{1,0:T(8,128)S(1)} %get-tuple-element.9), channel_id=1, source_target_pairs={{1,0},{2,1},{3,2},{0,3},{5,4},{6,5},{7,6},{4,7},{9,8},{10,9},{11,1... | collective-permute-start | bytes 12296 | tf_op jit(solution)/shard_map/ppermute | solution.py:22
  159.6 1.2 collective-permute-done.30
  160.9 1.6 collective-permute-done.29
  162.7 2.0 %collective-permute-start.32 = (f32[8,128]{1,0:T(8,128)S(1)}, f32[8,128]{1,0:T(8,128)S(1)}, u32[]{:S(2)}, u32[]{:S(2)}) collective-permute-start(f32[8,128]{1,0:T(8,128)S(1)} %maximum_maximum_fusion.refs_0_), channel_id=1, source_target_pairs={{12,0},{0,4},{4,8},{8,12},{13,1},{1,5},{5,9},{9,13},{14,2},{2,6},{... | collective-permute-start | bytes 12296 | tf_op jit(solution)/shard_map/ppermute | solution.py:22
  164.7 1.4 collective-permute-start.33
  166.1 1.9 %collective-permute-start.34 = (f32[8,128]{1,0:T(8,128)S(1)}, f32[8,128]{1,0:T(8,128)S(1)}, u32[]{:S(2)}, u32[]{:S(2)}) collective-permute-start(f32[8,128]{1,0:T(8,128)S(1)} %maximum_maximum_fusion.refs_0_), channel_id=1, source_target_pairs={{20,0},{24,4},{28,8},{16,12},{4,16},{8,20},{12,24},{0,28},{21,1},{... | collective-permute-start | bytes 12296 | tf_op jit(solution)/shard_map/ppermute | solution.py:399
  168.0 1.0 collective-permute-start.35
  169.2 2.8 %profiles.1 = (bf16[6,6,256,128]{3,2,1,0:T(8,128)(2,1)S(1)}, bf16[6,6,128,128]{3,2,1,0:T(8,128)(2,1)S(1)}) custom-call(f32[6,8,128]{2,1,0:T(8,128)S(1)} %pad.9.clone.lane_ref, f32[6,128,8]{2,1,0:T(8,128)S(1)} %pad_bitcast_fusion.sub_ref), custom_call_target="tpu_custom_call" | custom-call | flops 30000000 | bytes 4000000 | tf_op jit(solution)/shard_map/profiles/pallas_call | solution.py:340
  172.0 2.3 %collective-permute-done.35.refs_5_ = f32[8,128]{1,0:T(8,128)S(1)} collective-permute-done((f32[8,128]{1,0:T(8,128)S(1)}, f32[8,128]{1,0:T(8,128)S(1)}, u32[]{:S(2)}, u32[]{:S(2)}) %collective-permute-start.35) | collective-permute-done | bytes 4128 | tf_op jit(solution)/shard_map/ppermute | solution.py:399
  174.3 1.5 density.1
  (212 shorter events, 28.4 us)
Async XLA Ops:
  0.6 33.3 %copy-start.40 = (s32[21]{0:T(128)S(1)}, s32[21]{0:T(128)}, u32[]{:S(2)}) copy-start(s32[21]{0:T(128)} %constant.342.clone) | copy-start | bytes 256
  0.6 18.2 %copy-start.26 = (s32[32,12]{0,1:T(8,128)S(1)}, s32[32,12]{0,1:T(8,128)}, u32[]{:S(2)}) copy-start(s32[32,12]{0,1:T(8,128)} %param.17) | copy-start | bytes 4612
  0.7 18.8 %copy-start.21 = (s32[32]{0:T(128)S(1)}, s32[32]{0:T(128)}, u32[]{:S(2)}) copy-start(s32[32]{0:T(128)} %param.18) | copy-start | bytes 388
  2.1 16.8 %copy-start.29 = (s32[12]{0:T(128)S(1)}, s32[12]{0:T(128)}, u32[]{:S(2)}) copy-start(s32[12]{0:T(128)} %get-tuple-element.17.listed_ref) | copy-start | bytes 148
  9.1 73.9 %collective-permute-start.1 = (bf16[5,128,128]{2,1,0:T(8,128)(2,1)}, bf16[5,128,128]{2,1,0:T(8,128)(2,1)S(1)}, u32[]{:S(2)}, u32[]{:S(2)}) collective-permute-start(bf16[5,128,128]{2,1,0:T(8,128)(2,1)} %pick_column_blocks.1), channel_id=1, source_target_pairs={{4,0},{8,4},{12,8},{0,12},{5,1},{9,5},{13,9},{1,13},{6,2},{10,6},{... | collective-permute-start | bytes 491528 | tf_op jit(solution)/shard_map/ppermute | solution.py:22
  14.2 69.1 %collective-permute-start.3 = (bf16[5,128,128]{2,1,0:T(8,128)(2,1)}, bf16[5,128,128]{2,1,0:T(8,128)(2,1)S(1)}, u32[]{:S(2)}, u32[]{:S(2)}) collective-permute-start(bf16[5,128,128]{2,1,0:T(8,128)(2,1)} %pick_column_blocks.1), channel_id=1, source_target_pairs={{12,0},{0,4},{4,8},{8,12},{13,1},{1,5},{5,9},{9,13},{14,2},{2,6},{... | collective-permute-start | bytes 491528 | tf_op jit(solution)/shard_map/ppermute | solution.py:22
  15.2 69.5 %collective-permute-start.5 = (bf16[6,128,128]{2,1,0:T(8,128)(2,1)S(1)}, bf16[6,128,128]{2,1,0:T(8,128)(2,1)S(1)}, u32[]{:S(2)}, u32[]{:S(2)}) collective-permute-start(bf16[6,128,128]{2,1,0:T(8,128)(2,1)S(1)} %get-tuple-element.30), channel_id=1, source_target_pairs={{2,0},{3,1},{0,2},{1,3},{6,4},{7,5},{4,6},{5,7},{10,8},{11,9},{8,1... | collective-permute-start | bytes 589832 | tf_op jit(solution)/shard_map/ppermute | solution.py:27
  16.8 68.1 %collective-permute-start.13 = (bf16[6,128,128]{2,1,0:T(8,128)(2,1)S(1)}, bf16[6,128,128]{2,1,0:T(8,128)(2,1)S(1)}, u32[]{:S(2)}, u32[]{:S(2)}) collective-permute-start(bf16[6,128,128]{2,1,0:T(8,128)(2,1)S(1)} %get-tuple-element.30), channel_id=1, source_target_pairs={{16,0},{0,16},{17,1},{1,17},{18,2},{2,18},{19,3},{3,19},{20,4},{4,... | collective-permute-start | bytes 589832 | tf_op jit(solution)/shard_map/ppermute | solution.py:22
  18.3 66.5 %collective-permute-start.6 = (bf16[6,128,128]{2,1,0:T(8,128)(2,1)S(1)}, bf16[6,128,128]{2,1,0:T(8,128)(2,1)S(1)}, u32[]{:S(2)}, u32[]{:S(2)}) collective-permute-start(bf16[6,128,128]{2,1,0:T(8,128)(2,1)S(1)} %get-tuple-element.29), channel_id=1, source_target_pairs={{2,0},{3,1},{0,2},{1,3},{6,4},{7,5},{4,6},{5,7},{10,8},{11,9},{8,1... | collective-permute-start | bytes 589832 | tf_op jit(solution)/shard_map/ppermute | solution.py:27
  19.5 16.7 %copy-start.36 = (s32[1,12]{1,0:T(1,128)S(1)}, s32[1,12]{1,0:T(1,128)}, u32[]{:S(2)}) copy-start(s32[1,12]{1,0:T(1,128)} %param.20) | copy-start | bytes 148
  22.6 79.2 %copy-start.30 = (s32[12,12]{1,0:T(8,128)}, s32[12,12]{1,0:T(8,128)S(1)}, u32[]{:S(2)}) copy-start(s32[12,12]{1,0:T(8,128)S(1)} %get-tuple-element.22) | copy-start | bytes 1732
  22.6 11.6 %copy-start.27 = (s32[12,12]{1,0:T(8,128)}, s32[12,12]{1,0:T(8,128)S(1)}, u32[]{:S(2)}) copy-start(s32[12,12]{1,0:T(8,128)S(1)} %get-tuple-element.38) | copy-start | bytes 1732
  34.8 43.3 %copy-start.35 = (s32[21]{0:T(128)S(1)}, s32[21]{0:T(128)}, u32[]{:S(2)}) copy-start(s32[21]{0:T(128)} %constant.343.clone) | copy-start | bytes 256
  34.9 43.4 %copy-start.25 = (bf16[32,6,128]{2,0,1:T(8,128)(2,1)S(1)}, bf16[32,6,128]{2,0,1:T(8,128)(2,1)}, u32[]{:S(2)}) copy-start(bf16[32,6,128]{2,0,1:T(8,128)(2,1)} %param.19) | copy-start | bytes 147460
  35.5 42.9 %copy-start.37 = (s32[32]{0:T(128)S(1)}, s32[32]{0:T(128)}, u32[]{:S(2)}) copy-start(s32[32]{0:T(128)} %param.23) | copy-start | bytes 388
  35.5 42.9 %copy-start.38 = (s32[32]{0:T(128)S(1)}, s32[32]{0:T(128)}, u32[]{:S(2)}) copy-start(s32[32]{0:T(128)} %param.22) | copy-start | bytes 388
  35.5 42.9 %copy-start.39 = (s32[32]{0:T(128)S(1)}, s32[32]{0:T(128)}, u32[]{:S(2)}) copy-start(s32[32]{0:T(128)} %param.21) | copy-start | bytes 388
  78.3 3.3 %copy-start.32 = (f32[21]{0:T(128)S(1)}, f32[21]{0:T(128)}, u32[]{:S(2)}) copy-start(f32[21]{0:T(128)} %constant.355) | copy-start | bytes 256
  78.3 3.3 %copy-start.33 = (f32[6]{0:T(128)S(1)}, f32[6]{0:T(128)}, u32[]{:S(2)}) copy-start(f32[6]{0:T(128)} %constant.353) | copy-start | bytes 76
  78.3 3.3 %copy-start.34 = (f32[6]{0:T(128)S(1)}, f32[6]{0:T(128)}, u32[]{:S(2)}) copy-start(f32[6]{0:T(128)} %constant.352) | copy-start | bytes 76
  78.4 4.6 %copy-start = (bf16[1,12,128,128]{3,2,1,0:T(8,128)(2,1)S(1)}, bf16[1,12,128,128]{3,2,1,0:T(8,128)(2,1)}, u32[]{:S(2)}) copy-start(bf16[1,12,128,128]{3,2,1,0:T(8,128)(2,1)} %param.16) | copy-start | bytes 1179652
  83.0 17.1 %collective-permute-start = (bf16[12,128,128]{2,1,0:T(8,128)(2,1)S(1)}, bf16[12,128,128]{2,1,0:T(8,128)(2,1)S(1)}, u32[]{:S(2)}, u32[]{:S(2)}) collective-permute-start(bf16[12,128,128]{2,1,0:T(8,128)(2,1)S(1)} %bitcast.127), channel_id=1, source_target_pairs={{1,0},{0,1},{3,2},{2,3},{5,4},{4,5},{7,6},{6,7},{9,8},{8,9},{11,10... | collective-permute-start | bytes 1179656 | tf_op jit(solution)/shard_map/ppermute | solution.py:27
  83.3 7.0 %collective-permute-start.14 = (bf16[6,128,128]{2,1,0:T(8,128)(2,1)S(1)}, bf16[6,128,128]{2,1,0:T(8,128)(2,1)S(1)}, u32[]{:S(2)}, u32[]{:S(2)}) collective-permute-start(bf16[6,128,128]{2,1,0:T(8,128)(2,1)S(1)} %get-tuple-element.29), channel_id=1, source_target_pairs={{16,0},{0,16},{17,1},{1,17},{18,2},{2,18},{19,3},{3,19},{20,4},{4,... | collective-permute-start | bytes 589832 | tf_op jit(solution)/shard_map/ppermute | solution.py:22
  84.8 5.5 %collective-permute-start.2 = (bf16[5,128,128]{2,1,0:T(8,128)(2,1)S(1)}, bf16[5,128,128]{2,1,0:T(8,128)(2,1)S(1)}, u32[]{:S(2)}, u32[]{:S(2)}) collective-permute-start(bf16[5,128,128]{2,1,0:T(8,128)(2,1)S(1)} %collective-permute-done.1.refs_7_), channel_id=1, source_target_pairs={{1,0},{0,1},{3,2},{2,3},{5,4},{4,5},{7,6},{6,7},{9,8},{8,9},{11,10... | collective-permute-start | bytes 491528 | tf_op jit(solution)/shard_map/ppermute | solution.py:27
  84.8 10.2 %collective-permute-start.9 = (bf16[5,128,128]{2,1,0:T(8,128)(2,1)S(1)}, bf16[5,128,128]{2,1,0:T(8,128)(2,1)S(1)}, u32[]{:S(2)}, u32[]{:S(2)}) collective-permute-start(bf16[5,128,128]{2,1,0:T(8,128)(2,1)S(1)} %collective-permute-done.1.refs_7_), channel_id=1, source_target_pairs={{2,0},{3,1},{0,2},{1,3},{6,4},{7,5},{4,6},{5,7},{10,8},{11,9},{8,1... | collective-permute-start | bytes 491528 | tf_op jit(solution)/shard_map/ppermute | solution.py:27
  84.9 8.2 %collective-permute-start.4 = (bf16[5,128,128]{2,1,0:T(8,128)(2,1)S(1)}, bf16[5,128,128]{2,1,0:T(8,128)(2,1)S(1)}, u32[]{:S(2)}, u32[]{:S(2)}) collective-permute-start(bf16[5,128,128]{2,1,0:T(8,128)(2,1)S(1)} %collective-permute-done.3.refs_9_), channel_id=1, source_target_pairs={{1,0},{0,1},{3,2},{2,3},{5,4},{4,5},{7,6},{6,7},{9,8},{8,9},{11,10... | collective-permute-start | bytes 491528 | tf_op jit(solution)/shard_map/ppermute | solution.py:27
  90.3 5.5 %collective-permute-start.11 = (bf16[5,128,128]{2,1,0:T(8,128)(2,1)S(1)}, bf16[5,128,128]{2,1,0:T(8,128)(2,1)S(1)}, u32[]{:S(2)}, u32[]{:S(2)}) collective-permute-start(bf16[5,128,128]{2,1,0:T(8,128)(2,1)S(1)} %collective-permute-done.3.refs_9_), channel_id=1, source_target_pairs={{2,0},{3,1},{0,2},{1,3},{6,4},{7,5},{4,6},{5,7},{10,8},{11,9},{8,1... | collective-permute-start | bytes 491528 | tf_op jit(solution)/shard_map/ppermute | solution.py:27
  91.0 6.4 %collective-permute-start.17 = (bf16[5,128,128]{2,1,0:T(8,128)(2,1)S(1)}, bf16[5,128,128]{2,1,0:T(8,128)(2,1)S(1)}, u32[]{:S(2)}, u32[]{:S(2)}) collective-permute-start(bf16[5,128,128]{2,1,0:T(8,128)(2,1)S(1)} %collective-permute-done.1.refs_7_), channel_id=1, source_target_pairs={{16,0},{0,16},{17,1},{1,17},{18,2},{2,18},{19,3},{3,19},{20,4},{4,... | collective-permute-start | bytes 491528 | tf_op jit(solution)/shard_map/ppermute | solution.py:22
  93.8 6.3 %collective-permute-start.19 = (bf16[5,128,128]{2,1,0:T(8,128)(2,1)S(1)}, bf16[5,128,128]{2,1,0:T(8,128)(2,1)}, u32[]{:S(2)}, u32[]{:S(2)}) collective-permute-start(bf16[5,128,128]{2,1,0:T(8,128)(2,1)S(1)} %collective-permute-done.3.refs_9_), channel_id=1, source_target_pairs={{16,0},{0,16},{17,1},{1,17},{18,2},{2,18},{19,3},{3,19},{20,4},{4,... | collective-permute-start | bytes 491528 | tf_op jit(solution)/shard_map/ppermute | solution.py:22
  95.0 6.6 %collective-permute-start.7 = (bf16[6,128,128]{2,1,0:T(8,128)(2,1)S(1)}, bf16[6,128,128]{2,1,0:T(8,128)(2,1)S(1)}, u32[]{:S(2)}, u32[]{:S(2)}) collective-permute-start(bf16[6,128,128]{2,1,0:T(8,128)(2,1)S(1)} %collective-permute-done.5.refs_11_), channel_id=1, source_target_pairs={{1,0},{0,1},{3,2},{2,3},{5,4},{4,5},{7,6},{6,7},{9,8},{8,9},{11,10... | collective-permute-start | bytes 589832 | tf_op jit(solution)/shard_map/ppermute | solution.py:27
  95.8 6.9 %collective-permute-start.15 = (bf16[6,128,128]{2,1,0:T(8,128)(2,1)S(1)}, bf16[6,128,128]{2,1,0:T(8,128)(2,1)S(1)}, u32[]{:S(2)}, u32[]{:S(2)}) collective-permute-start(bf16[6,128,128]{2,1,0:T(8,128)(2,1)S(1)} %collective-permute-done.13.refs_19_), channel_id=1, source_target_pairs={{1,0},{0,1},{3,2},{2,3},{5,4},{4,5},{7,6},{6,7},{9,8},{8,9},{11,10... | collective-permute-start | bytes 589832 | tf_op jit(solution)/shard_map/ppermute | solution.py:27
  97.4 7.7 %collective-permute-start.21 = (bf16[6,128,128]{2,1,0:T(8,128)(2,1)S(1)}, bf16[6,128,128]{2,1,0:T(8,128)(2,1)S(1)}, u32[]{:S(2)}, u32[]{:S(2)}) collective-permute-start(bf16[6,128,128]{2,1,0:T(8,128)(2,1)S(1)} %collective-permute-done.13.refs_19_), channel_id=1, source_target_pairs={{2,0},{3,1},{0,2},{1,3},{6,4},{7,5},{4,6},{5,7},{10,8},{11,9},{8,1... | collective-permute-start | bytes 589832 | tf_op jit(solution)/shard_map/ppermute | solution.py:27
  100.1 2.3 %collective-permute-start.8 = (bf16[6,128,128]{2,1,0:T(8,128)(2,1)S(1)}, bf16[6,128,128]{2,1,0:T(8,128)(2,1)S(1)}, u32[]{:S(2)}, u32[]{:S(2)}) collective-permute-start(bf16[6,128,128]{2,1,0:T(8,128)(2,1)S(1)} %collective-permute-done.6.refs_12_), channel_id=1, source_target_pairs={{1,0},{0,1},{3,2},{2,3},{5,4},{4,5},{7,6},{6,7},{9,8},{8,9},{11,10... | collective-permute-start | bytes 589832 | tf_op jit(solution)/shard_map/ppermute | solution.py:27
  100.1 7.3 %collective-permute-start.22 = (bf16[6,128,128]{2,1,0:T(8,128)(2,1)S(1)}, bf16[6,128,128]{2,1,0:T(8,128)(2,1)S(1)}, u32[]{:S(2)}, u32[]{:S(2)}) collective-permute-start(bf16[6,128,128]{2,1,0:T(8,128)(2,1)S(1)} %collective-permute-done.6.refs_12_), channel_id=1, source_target_pairs={{16,0},{0,16},{17,1},{1,17},{18,2},{2,18},{19,3},{3,19},{20,4},{4,... | collective-permute-start | bytes 589832 | tf_op jit(solution)/shard_map/ppermute | solution.py:22
  101.6 3.5 %collective-permute-start.16 = (bf16[6,128,128]{2,1,0:T(8,128)(2,1)S(1)}, bf16[6,128,128]{2,1,0:T(8,128)(2,1)S(1)}, u32[]{:S(2)}, u32[]{:S(2)}) collective-permute-start(bf16[6,128,128]{2,1,0:T(8,128)(2,1)S(1)} %collective-permute-done.14.refs_20_), channel_id=1, source_target_pairs={{1,0},{0,1},{3,2},{2,3},{5,4},{4,5},{7,6},{6,7},{9,8},{8,9},{11,10... | collective-permute-start | bytes 589832 | tf_op jit(solution)/shard_map/ppermute | solution.py:27
  102.4 8.2 %collective-permute-start.18 = (bf16[5,128,128]{2,1,0:T(8,128)(2,1)S(1)}, bf16[5,128,128]{2,1,0:T(8,128)(2,1)S(1)}, u32[]{:S(2)}, u32[]{:S(2)}) collective-permute-start(bf16[5,128,128]{2,1,0:T(8,128)(2,1)S(1)} %collective-permute-done.17.refs_23_), channel_id=1, source_target_pairs={{1,0},{0,1},{3,2},{2,3},{5,4},{4,5},{7,6},{6,7},{9,8},{8,9},{11,10... | collective-permute-start | bytes 491528 | tf_op jit(solution)/shard_map/ppermute | solution.py:27
  102.7 9.0 %collective-permute-start.25 = (bf16[5,128,128]{2,1,0:T(8,128)(2,1)S(1)}, bf16[5,128,128]{2,1,0:T(8,128)(2,1)}, u32[]{:S(2)}, u32[]{:S(2)}) collective-permute-start(bf16[5,128,128]{2,1,0:T(8,128)(2,1)S(1)} %collective-permute-done.17.refs_23_), channel_id=1, source_target_pairs={{2,0},{3,1},{0,2},{1,3},{6,4},{7,5},{4,6},{5,7},{10,8},{11,9},{8,1... | collective-permute-start | bytes 491528 | tf_op jit(solution)/shard_map/ppermute | solution.py:27
  105.1 4.8 %collective-permute-start.12 = (bf16[5,128,128]{2,1,0:T(8,128)(2,1)S(1)}, bf16[5,128,128]{2,1,0:T(8,128)(2,1)S(1)}, u32[]{:S(2)}, u32[]{:S(2)}) collective-permute-start(bf16[5,128,128]{2,1,0:T(8,128)(2,1)S(1)} %collective-permute-done.11.refs_17_), channel_id=1, source_target_pairs={{1,0},{0,1},{3,2},{2,3},{5,4},{4,5},{7,6},{6,7},{9,8},{8,9},{11,10... | collective-permute-start | bytes 491528 | tf_op jit(solution)/shard_map/ppermute | solution.py:27
  105.1 6.7 %collective-permute-start.27 = (bf16[5,128,128]{2,1,0:T(8,128)(2,1)S(1)}, bf16[5,128,128]{2,1,0:T(8,128)(2,1)}, u32[]{:S(2)}, u32[]{:S(2)}) collective-permute-start(bf16[5,128,128]{2,1,0:T(8,128)(2,1)S(1)} %collective-permute-done.11.refs_17_), channel_id=1, source_target_pairs={{16,0},{0,16},{17,1},{1,17},{18,2},{2,18},{19,3},{3,19},{20,4},{4,... | collective-permute-start | bytes 491528 | tf_op jit(solution)/shard_map/ppermute | solution.py:22
  107.4 1.4 collective-permute-start.10
  109.4 20.9 %collective-permute-start.20 = (bf16[5,128,128]{2,1,0:T(8,128)(2,1)}, bf16[5,128,128]{2,1,0:T(8,128)(2,1)}, u32[]{:S(2)}, u32[]{:S(2)}) collective-permute-start(bf16[5,128,128]{2,1,0:T(8,128)(2,1)} %collective-permute-done.19.refs_25_), channel_id=1, source_target_pairs={{1,0},{0,1},{3,2},{2,3},{5,4},{4,5},{7,6},{6,7},{9,8},{8,9},{11,10... | collective-permute-start | bytes 491528 | tf_op jit(solution)/shard_map/ppermute | solution.py:27
  110.5 19.8 %collective-permute-start.23 = (bf16[6,128,128]{2,1,0:T(8,128)(2,1)S(1)}, bf16[6,128,128]{2,1,0:T(8,128)(2,1)S(1)}, u32[]{:S(2)}, u32[]{:S(2)}) collective-permute-start(bf16[6,128,128]{2,1,0:T(8,128)(2,1)S(1)} %collective-permute-done.21.refs_27_), channel_id=1, source_target_pairs={{1,0},{0,1},{3,2},{2,3},{5,4},{4,5},{7,6},{6,7},{9,8},{8,9},{11,10... | collective-permute-start | bytes 589832 | tf_op jit(solution)/shard_map/ppermute | solution.py:27
  111.3 19.0 %collective-permute-start.24 = (bf16[6,128,128]{2,1,0:T(8,128)(2,1)S(1)}, bf16[6,128,128]{2,1,0:T(8,128)(2,1)S(1)}, u32[]{:S(2)}, u32[]{:S(2)}) collective-permute-start(bf16[6,128,128]{2,1,0:T(8,128)(2,1)S(1)} %collective-permute-done.22.refs_28_), channel_id=1, source_target_pairs={{1,0},{0,1},{3,2},{2,3},{5,4},{4,5},{7,6},{6,7},{9,8},{8,9},{11,10... | collective-permute-start | bytes 589832 | tf_op jit(solution)/shard_map/ppermute | solution.py:27
  111.7 18.6 %collective-permute-start.26 = (bf16[5,128,128]{2,1,0:T(8,128)(2,1)}, bf16[5,128,128]{2,1,0:T(8,128)(2,1)}, u32[]{:S(2)}, u32[]{:S(2)}) collective-permute-start(bf16[5,128,128]{2,1,0:T(8,128)(2,1)} %collective-permute-done.25.refs_31_), channel_id=1, source_target_pairs={{1,0},{0,1},{3,2},{2,3},{5,4},{4,5},{7,6},{6,7},{9,8},{8,9},{11,10... | collective-permute-start | bytes 491528 | tf_op jit(solution)/shard_map/ppermute | solution.py:27
  111.8 18.5 %collective-permute-start.28 = (bf16[5,128,128]{2,1,0:T(8,128)(2,1)}, bf16[5,128,128]{2,1,0:T(8,128)(2,1)}, u32[]{:S(2)}, u32[]{:S(2)}) collective-permute-start(bf16[5,128,128]{2,1,0:T(8,128)(2,1)} %collective-permute-done.27.refs_33_), channel_id=1, source_target_pairs={{1,0},{0,1},{3,2},{2,3},{5,4},{4,5},{7,6},{6,7},{9,8},{8,9},{11,10... | collective-permute-start | bytes 491528 | tf_op jit(solution)/shard_map/ppermute | solution.py:27
  115.4 8.4 %copy-start.28 = (f32[6,6]{1,0:T(8,128)S(1)}, f32[6,6]{1,0:T(8,128)}, u32[]{:S(2)}) copy-start(f32[6,6]{1,0:T(8,128)} %pad_maximum_fusion) | copy-start | bytes 436
  115.4 10.8 %copy-start.31 = (bf16[6,128]{1,0:T(8,128)(2,1)S(1)}, bf16[6,128]{1,0:T(8,128)(2,1)}, u32[]{:S(2)}) copy-start(bf16[6,128]{1,0:T(8,128)(2,1)} %dynamic-slice_bitcast_fusion) | copy-start | bytes 4612
  130.3 0.9 copy-start.2
  131.3 0.9 copy-start.4
  132.2 0.9 copy-start.6
  133.1 0.9 copy-start.8
  134.0 0.9 copy-start.10
  134.9 0.9 copy-start.12
  136.8 0.9 copy-start.16
  137.7 0.9 copy-start.18
  139.5 20.0 %copy-start.22 = (f32[6,6,126]{1,2,0:T(8,128)S(1)}, f32[6,6,126]{1,2,0:T(8,128)}, u32[]{:S(2)}) copy-start(f32[6,6,126]{1,2,0:T(8,128)} %copy.140) | copy-start | bytes 54436
  139.5 20.0 %copy-start.24 = (f32[6,126]{0,1:T(8,128)S(1)}, f32[6,126]{0,1:T(8,128)}, u32[]{:S(2)}) copy-start(f32[6,126]{0,1:T(8,128)} %copy.139) | copy-start | bytes 9076
  157.5 3.3 %collective-permute-start.30 = (f32[8,128]{1,0:T(8,128)S(1)}, f32[8,128]{1,0:T(8,128)S(1)}, u32[]{:S(2)}, u32[]{:S(2)}) collective-permute-start(f32[8,128]{1,0:T(8,128)S(1)} %get-tuple-element.9), channel_id=1, source_target_pairs={{1,0},{2,1},{3,2},{0,3},{5,4},{6,5},{7,6},{4,7},{9,8},{10,9},{11,1... | collective-permute-start | bytes 12296 | tf_op jit(solution)/shard_map/ppermute | solution.py:22
  159.5 3.0 %collective-permute-start.29 = (f32[8,128]{1,0:T(8,128)S(1)}, f32[8,128]{1,0:T(8,128)S(1)}, u32[]{:S(2)}, u32[]{:S(2)}) collective-permute-start(f32[8,128]{1,0:T(8,128)S(1)} %get-tuple-element.9), channel_id=1, source_target_pairs={{3,0},{0,1},{1,2},{2,3},{7,4},{4,5},{5,6},{6,7},{11,8},{8,9},{9,10... | collective-permute-start | bytes 12296 | tf_op jit(solution)/shard_map/ppermute | solution.py:22
  162.7 9.3 %collective-permute-start.31 = (f32[8,128]{1,0:T(8,128)S(1)}, f32[8,128]{1,0:T(8,128)S(1)}, u32[]{:S(2)}, u32[]{:S(2)}) collective-permute-start(f32[8,128]{1,0:T(8,128)S(1)} %maximum_maximum_fusion.refs_0_), channel_id=1, source_target_pairs={{4,0},{8,4},{12,8},{0,12},{5,1},{9,5},{13,9},{1,13},{6,2},{10,6},{... | collective-permute-start | bytes 12296 | tf_op jit(solution)/shard_map/ppermute | solution.py:22
  162.7 9.3 %collective-permute-start.32 = (f32[8,128]{1,0:T(8,128)S(1)}, f32[8,128]{1,0:T(8,128)S(1)}, u32[]{:S(2)}, u32[]{:S(2)}) collective-permute-start(f32[8,128]{1,0:T(8,128)S(1)} %maximum_maximum_fusion.refs_0_), channel_id=1, source_target_pairs={{12,0},{0,4},{4,8},{8,12},{13,1},{1,5},{5,9},{9,13},{14,2},{2,6},{... | collective-permute-start | bytes 12296 | tf_op jit(solution)/shard_map/ppermute | solution.py:22
  164.7 7.3 %collective-permute-start.33 = (f32[8,128]{1,0:T(8,128)S(1)}, f32[8,128]{1,0:T(8,128)S(1)}, u32[]{:S(2)}, u32[]{:S(2)}) collective-permute-start(f32[8,128]{1,0:T(8,128)S(1)} %maximum_maximum_fusion.refs_0_), channel_id=1, source_target_pairs={{16,0},{0,16},{17,1},{1,17},{18,2},{2,18},{19,3},{3,19},{20,4},{4,... | collective-permute-start | bytes 12296 | tf_op jit(solution)/shard_map/ppermute | solution.py:22
  166.1 6.0 %collective-permute-start.34 = (f32[8,128]{1,0:T(8,128)S(1)}, f32[8,128]{1,0:T(8,128)S(1)}, u32[]{:S(2)}, u32[]{:S(2)}) collective-permute-start(f32[8,128]{1,0:T(8,128)S(1)} %maximum_maximum_fusion.refs_0_), channel_id=1, source_target_pairs={{20,0},{24,4},{28,8},{16,12},{4,16},{8,20},{12,24},{0,28},{21,1},{... | collective-permute-start | bytes 12296 | tf_op jit(solution)/shard_map/ppermute | solution.py:399
  168.0 6.3 %collective-permute-start.35 = (f32[8,128]{1,0:T(8,128)S(1)}, f32[8,128]{1,0:T(8,128)S(1)}, u32[]{:S(2)}, u32[]{:S(2)}) collective-permute-start(f32[8,128]{1,0:T(8,128)S(1)} %maximum_maximum_fusion.refs_0_), channel_id=1, source_target_pairs={{28,0},{16,4},{20,8},{24,12},{12,16},{0,20},{4,24},{8,28},{29,1},{... | collective-permute-start | bytes 12296 | tf_op jit(solution)/shard_map/ppermute | solution.py:399
  (13 other events, 9.1 us)

commit v2 on v1

v2 whole, which is shorter than its diff:
```python
import functools

import jax
import jax.numpy as jnp
from jax import lax
from jax.experimental import pallas as pl
from jax.experimental.pallas import tpu as pltpu
from jax.sharding import PartitionSpec as P

BX = 16
BY = 16
BZ = 128
LANES = 128
UNROLL = 4
VMEM = pl.BlockSpec(memory_space=pltpu.VMEM)
SMEM = pl.BlockSpec(memory_space=pltpu.SMEM)
ANY = pl.BlockSpec(memory_space=pl.ANY)


def from_offset(x, axis, step):
    count = lax.axis_size(axis)
    return lax.ppermute(x, axis, [((i + step) % count, i) for i in range(count)])


def from_layer(x, flip):
    count = lax.axis_size("layer")
    return lax.ppermute(x, "layer", [(i ^ flip, i) for i in range(count)])


def column_targets(n_row):
    return 5 if n_row == 2 else 7


def target_place(n_row, step_row, step_lay, row):
    same = jnp.where(step_lay < 3, step_lay, -1)
    if n_row == 2:
        lead = step_lay - row
        across = jnp.where((lead >= 0) & (lead < 2), 3 + lead, -1)
    else:
        across = 3 + step_lay
    return jnp.where(step_row == 0, same, jnp.where(step_row == 1, across, -1))


class Places:
    def __init__(self, n_row, n_col, n_lay):
        self.n_row, self.n_col, self.n_lay = n_row, n_col, n_lay
        self.lay_bits = n_lay.bit_length() - 1
        self.col_bits = n_col.bit_length() - 1
        self.row = lax.axis_index("row")
        self.col = lax.axis_index("col")
        self.lay = lax.axis_index("layer")
        self.me = (((self.row << self.col_bits) + self.col) << self.lay_bits) + self.lay

    def split(self, atom):
        return (
            atom >> (self.lay_bits + self.col_bits),
            (atom >> self.lay_bits) & (self.n_col - 1),
            atom & (self.n_lay - 1),
        )


def pick_kernel(axes, neighbors_ref, sign_ref, out_ref, place_ref):
    at = Places(*axes)
    for i in range(out_ref.shape[0] + 1):
        place_ref[i] = 0
    for u in range(sign_ref.shape[0]):
        row, col, lay = at.split(neighbors_ref[at.me, u])
        place = target_place(at.n_row, (row - at.row) & (at.n_row - 1), (lay - at.lay) & (at.n_lay - 1), at.row)
        place = jnp.where((col == at.col) & (place >= 0), place, out_ref.shape[0])
        place_ref[place] = u
    for i in range(out_ref.shape[0]):
        out_ref[i] = sign_ref[place_ref[i]]


def prepare_kernel(axes, count, n_pick, *refs):
    neighbors_ref, extent_ref, size_ref, x_ref, y_ref, z_ref, basis_ref = refs[:7]
    table_ref, info_ref, geo_ref, spread_ref, own_basis_ref, known, inverse = refs[7:]
    at = Places(*axes)
    slots = extent_ref.shape[1]
    shells = 6
    column_base = count * at.n_lay * slots
    sub = lax.broadcasted_iota(jnp.int32, (8, LANES), 0)
    lane_pair = lax.broadcasted_iota(jnp.int32, (8, LANES), 1) // shells
    hot_row = lax.broadcasted_iota(jnp.int32, (LANES, 16), 0)
    hot_shell = lax.broadcasted_iota(jnp.int32, (LANES, 16), 1)
    geo = jnp.zeros((8, LANES), jnp.int32)
    seen = [jnp.int32(0)] * at.n_lay
    self_slot = jnp.int32(0)
    for w in range(slots):
        atom = neighbors_ref[at.me, w]
        row, col, lay = at.split(atom)
        step_row = (row - at.row) & (at.n_row - 1)
        step_col = (col - at.col) & (at.n_col - 1)
        step_lay = (lay - at.lay) & (at.n_lay - 1)
        rank = jnp.int32(0)
        for k in range(at.n_lay):
            rank = jnp.where(step_lay == k, 3 * k + seen[k], rank)
            seen[k] = seen[k] + (step_lay == k).astype(jnp.int32)
        go_row = ((step_row + 1) & (at.n_row - 1)) - 1
        go_col = ((step_col + 1) & (at.n_col - 1)) - 1
        go_lay = jnp.minimum(((step_lay + 1) & (at.n_lay - 1)) - 1, 1)
        twice_x = x_ref[at.me] + x_ref[atom] + BX * go_row
        twice_y = y_ref[at.me] + y_ref[atom] + BY * go_col
        twice_z = z_ref[at.me] + z_ref[atom] + BZ * go_lay
        values = jnp.where(sub == 0, twice_x, jnp.where(sub == 1, twice_y, jnp.where(sub == 2, twice_z, 2 * extent_ref[0, w])))
        geo = jnp.where(lane_pair == rank, values, geo)
        self_slot = jnp.where(atom == at.me, w, self_slot)
        info_ref[w] = size_ref[atom]
        hot = (hot_row == rank * shells + hot_shell) & (hot_shell < shells)
        spread_ref[w] = jnp.dot(
            hot.astype(jnp.bfloat16), basis_ref[atom], preferred_element_type=jnp.float32
        ).astype(spread_ref.dtype)
        known[0, w] = atom
        known[1, w] = jnp.where(step_col == 0, 0, jnp.where(step_col == 1, 1, 2))
        known[2, w] = jnp.where(step_row == 0, 0, jnp.where(step_row == 1, 1, 2)) * at.n_lay + (lay ^ at.lay)
        inverse[atom] = -1
    geo_ref[...] = 0.5 * geo.astype(jnp.float32)
    own_basis_ref[...] = basis_ref[at.me]
    info_ref[slots] = size_ref[at.me]
    info_ref[slots + 1] = self_slot

    def row_of_pairs(v, total):
        atom = known[0, v]
        side = known[1, v]
        line = known[2, v]
        row, _, lay = at.split(atom)
        for u in range(slots):
            inverse[neighbors_ref[atom, u]] = v * 16 + u
        column_line = column_base + ((side - 1) * count * at.n_lay + line) * n_pick
        for w in range(slots):
            other = known[0, w]
            other_side = known[1, w]
            mark = inverse[other]
            o_row, _, o_lay = at.split(other)
            there = target_place(at.n_row, (o_row - row) & (at.n_row - 1), (o_lay - lay) & (at.n_lay - 1), row)
            back = target_place(at.n_row, (row - o_row) & (at.n_row - 1), (lay - o_lay) & (at.n_lay - 1), o_row)
            from_row = (other_side != 0) | (v <= w)
            from_column = (side == other_side) & (there >= 0) & ((back < 0) | (v <= w))
            chosen = ((mark >> 4) == v) & jnp.where(side == 0, from_row, from_column)
            table_ref[3 * total + 1] = v
            table_ref[3 * total + 2] = w
            table_ref[3 * total + 3] = jnp.where(side == 0, line * slots + (mark & 15), column_line + there)
            total = total + chosen.astype(jnp.int32)
        return total

    total = lax.fori_loop(0, slots, row_of_pairs, jnp.int32(0))
    table_ref[0] = (total + UNROLL - 1) // UNROLL
    for i in range(UNROLL - 1):
        for k in range(3):
            table_ref[3 * (total + i) + 1 + k] = table_ref[3 * (total - 1) + 1 + k]


def step_kernel(offsets, lengths, *refs):
    tab_ref, info_ref, basis_ref, spread_ref, sign_ref = refs[:5]
    piece_refs = refs[5 : 5 + len(offsets)]
    next_ref, coef_ref, pool, gram, own, square, sems = refs[5 + len(offsets) :]
    slots, size = sign_ref.shape[0], sign_ref.shape[1]
    copies = []
    for i, piece in enumerate(piece_refs):
        copy = pltpu.make_async_copy(piece, pool.at[pl.ds(offsets[i], lengths[i])], sems.at[i])
        copy.start()
        copies.append(copy)
    for v in range(slots):
        gram[v * size : (v + 1) * size] = jnp.zeros((size, slots * size), gram.dtype)
    rows = lax.broadcasted_iota(jnp.int32, (size, size), 0)
    lanes = lax.broadcasted_iota(jnp.int32, (size, size), 1)
    own_size = info_ref[slots]
    self_slot = info_ref[slots + 1]
    for w in range(slots):
        kept = (rows < own_size) & (lanes < info_ref[w])
        block = jnp.where(kept, sign_ref[w].astype(jnp.float32), 0.0)
        own[:, w * size : (w + 1) * size] = block.astype(own.dtype)
    for copy in copies:
        copy.wait()

    def place(i, carry):
        for k in range(UNROLL):
            entry = 3 * (i * UNROLL + k)
            p = pl.multiple_of(tab_ref[entry + 1] * size, size)
            q = pl.multiple_of(tab_ref[entry + 2] * size, size)
            block = pool[tab_ref[entry + 3]]
            gram[pl.ds(p, size), pl.ds(q, size)] = block
            gram[pl.ds(q, size), pl.ds(p, size)] = block.T
        return carry

    lax.fori_loop(0, tab_ref[0], place, 0)
    wide = 2 * size
    wide_lanes = lax.broadcasted_iota(jnp.int32, (size, wide), 1)
    wide_rows = lax.broadcasted_iota(jnp.int32, (size, wide), 0)

    def column_kept(n):
        first = info_ref[2 * n]
        second = info_ref[2 * n + 1]
        return (wide_lanes < first) | ((wide_lanes >= size) & (wide_lanes < size + second))

    for n in range(slots // 2):
        part = jnp.dot(own[...], gram[:, n * wide : (n + 1) * wide], preferred_element_type=jnp.float32)
        square[:, n * wide : (n + 1) * wide] = jnp.where(column_kept(n), part, 0.0).astype(square.dtype)
    coef = jnp.zeros((basis_ref.shape[0], LANES), jnp.float32)
    across = (((1,), (1,)), ((), ()))
    for n in range(slots // 2):
        part = jnp.dot(square[...], gram[:, n * wide : (n + 1) * wide], preferred_element_type=jnp.float32)
        cube = jnp.where(column_kept(n), part, 0.0)
        full = 1.5 * own[:, n * wide : (n + 1) * wide].astype(jnp.float32) - 0.5 * cube
        next_ref[2 * n] = full[:, :size].astype(next_ref.dtype)
        next_ref[2 * n + 1] = full[:, size:].astype(next_ref.dtype)
        shift = (self_slot - 2 * n) * size
        is_self = (self_slot >= 2 * n) & (self_slot < 2 * n + 2)
        diag = (wide_lanes == wide_rows + shift) & (wide_rows < own_size) & is_self
        dmat = 0.5 * (jnp.where(diag, 1.0, 0.0) - full)
        high = dmat.astype(jnp.bfloat16)
        low = (dmat - high.astype(jnp.float32)).astype(jnp.bfloat16)
        half = jnp.dot(basis_ref[...], high, preferred_element_type=jnp.float32) + jnp.dot(
            basis_ref[...], low, preferred_element_type=jnp.float32
        )
        half_high = half.astype(jnp.bfloat16)
        half_low = (half - half_high.astype(jnp.float32)).astype(jnp.bfloat16)
        for k in range(2):
            spread = spread_ref[2 * n + k]
            for part in (half_high, half_low):
                coef = coef + lax.dot_general(
                    part[:, k * size : (k + 1) * size], spread, across, preferred_element_type=jnp.float32
                )
    coef_ref[...] = coef[: coef_ref.shape[0]]


def profile_kernel(periods, tile_steps, *refs):
    tiles = len(tile_steps)
    geo_refs = refs[:tiles]
    plane_ref, line_ref = refs[tiles:]
    shells = plane_ref.shape[1]
    cells = plane_ref.shape[2]
    cell = lax.broadcasted_iota(jnp.int32, (cells, LANES), 0)
    grid_x = (cell // BY).astype(jnp.float32)
    grid_y = (cell % BY).astype(jnp.float32)
    grid_z = lax.broadcasted_iota(jnp.int32, (LANES, BZ), 1).astype(jnp.float32)
    lane = lax.broadcasted_iota(jnp.int32, (1, LANES), 1)
    shell = (lane % shells + 1).astype(jnp.float32)
    valid = lane < 21 * shells

    def nearest(offset, period):
        return offset - period * jnp.floor(offset * (1.0 / period) + 0.5)

    for o, (step_row, step_col) in enumerate(tile_steps):
        geo = geo_refs[o][...]
        extent = jnp.where(valid, geo[3:4], 1.0)
        inverse = (shells / extent) * (shells / extent)
        reach = jnp.where(valid, extent, -1.0)
        rate_t = inverse / (shell * shell)
        packed = jnp.concatenate([geo[2:3], reach, rate_t, inverse, jnp.zeros((4, LANES), jnp.float32)], axis=0)
        sub = packed.T
        d_x = nearest(grid_x - (geo[0:1] + float(BX * step_row)), periods[0])
        d_y = nearest(grid_y - (geo[1:2] + float(BY * step_col)), periods[1])
        inside = (jnp.abs(d_x) <= reach) & (jnp.abs(d_y) <= reach)
        squared = d_x * d_x + d_y * d_y
        d_z = nearest(grid_z - sub[:, 0:1], periods[2])
        inside_z = jnp.abs(d_z) <= sub[:, 1:2]
        squared_z = d_z * d_z
        for s in range(shells):
            part = 1.0 / ((s + 1) * (s + 1))
            rate = inverse * part + rate_t
            plane_ref[o, s] = jnp.where(inside, jnp.exp(-rate * squared), 0.0).astype(plane_ref.dtype)
            rate_z = sub[:, 3:4] * part + sub[:, 2:3]
            line_ref[o, s] = jnp.where(inside_z, jnp.exp(-rate_z * squared_z), 0.0).astype(line_ref.dtype)


def density_kernel(tiles, *refs):
    tile_refs = refs[:tiles]
    plane_ref, line_ref, out_ref, terms = refs[tiles:]
    shells = plane_ref.shape[1]
    for o in range(tiles):
        for s in range(shells):
            scaled = plane_ref[o, s].astype(jnp.float32) * tile_refs[o][s : s + 1, :]
            at = (o * shells + s) * LANES
            terms[:, at : at + LANES] = scaled.astype(terms.dtype)
    out_ref[...] = jnp.dot(terms[...], line_ref[...], preferred_element_type=jnp.float32)


def to_tiles(tile, shift, tile_steps, n_row, n_col):
    shells = 6
    span = 3 * shells
    below = from_offset(tile, "layer", -1)
    above = from_offset(tile, "layer", 1)
    merged = jnp.concatenate(
        [
            tile[:, : 4 * span],
            below[:, span : 3 * span],
            above[:, 3 * span : 4 * span],
            jnp.zeros((8, LANES - 7 * span), jnp.float32),
        ],
        axis=1,
    )
    if shift is not None:
        merged = merged + shift
    received = []
    for dr, dc in tile_steps:
        if dr == 0 and dc == 0:
            received.append(merged)
        elif dr == 0:
            received.append(from_offset(merged, "col", dc))
        elif dc == 0:
            received.append(from_offset(merged, "row", dr))
        else:
            moves = [
                (((i + dr) % n_row) * n_col + (j + dc) % n_col, i * n_col + j)
                for i in range(n_row)
                for j in range(n_col)
            ]
            received.append(lax.ppermute(merged, ("row", "col"), moves))
    return received


def local(sign_start, neighbors, atom_size, basis_proj, pair_extent, atom_x, atom_y, atom_z):
    n_row = lax.axis_size("row")
    n_col = lax.axis_size("col")
    n_lay = lax.axis_size("layer")
    assert n_lay == 4 and n_col >= 4 and (n_row == 2 or n_row >= 4)
    assert n_row & (n_row - 1) == 0 and n_col & (n_col - 1) == 0
    axes = (n_row, n_col, n_lay)
    atoms, slots = neighbors.shape
    size = sign_start.shape[2]
    shells = basis_proj.shape[1]
    steps = [0, 1] if n_row == 2 else [0, 1, -1]
    count = len(steps)
    own = sign_start[0]
    half = slots // 2

    rows, tops, ends, ups, downs = {}, {}, {}, {}, {}
    for di in range(1, count):
        rows[di, 0] = from_offset(own, "row", steps[di])
    rows[0, 2] = from_layer(own, 2)
    n_pick = column_targets(n_row)
    picked = pl.pallas_call(
        functools.partial(pick_kernel, axes),
        out_shape=jax.ShapeDtypeStruct((n_pick, size, size), own.dtype),
        in_specs=[SMEM, VMEM],
        out_specs=VMEM,
        scratch_shapes=[pltpu.SMEM((n_pick + 1,), jnp.int32)],
        name="pick_column_blocks",
    )(neighbors, own)
    ups[0, 0] = from_offset(picked, "col", 1)
    downs[0, 0] = from_offset(picked, "col", -1)
    for di in range(1, count):
        tops[di, 2] = from_layer(rows[di, 0][:half], 2)
        ends[di, 2] = from_offset(rows[0, 2][half:], "row", steps[di])
    for di in range(1, count):
        ups[di, 0] = from_offset(ups[0, 0], "row", steps[di])
    downs[0, 2] = from_layer(downs[0, 0], 2)
    for di in range(count):
        ups[di, 2] = from_layer(ups[di, 0], 2)
    for di in range(1, count):
        downs[di, 0] = from_offset(downs[0, 0], "row", steps[di])
        downs[di, 2] = from_offset(downs[0, 2], "row", steps[di])
    values, starts, widths = [], [], []

    def add(value, start, mate):
        for piece, place in ((value, start), (from_layer(value, 1), mate)):
            values.append(piece)
            starts.append(place)
            widths.append(piece.shape[0])

    column_base = count * n_lay * slots
    add(own, 0, slots)
    add(rows[0, 2], 2 * slots, 3 * slots)
    for di in range(1, count):
        base = di * n_lay * slots
        add(rows[di, 0], base, base + slots)
        add(tops[di, 2], base + 2 * slots, base + 3 * slots)
        add(ends[di, 2], base + 2 * slots + half, base + 3 * slots + half)
    for side, parts in enumerate((ups, downs)):
        for di in range(count):
            for flip in (0, 2):
                base = column_base + ((side * count + di) * n_lay + flip) * n_pick
                add(parts[di, flip], base, base + n_pick)
    n_pool = column_base + 2 * count * n_lay * n_pick

    basis = jnp.pad(basis_proj, ((0, 0), (0, 16 - shells), (0, 0)))
    pairs = slots * (slots + 1) // 2
    table, info, geo, spread, own_basis = pl.pallas_call(
        functools.partial(prepare_kernel, axes, count, n_pick),
        out_shape=(
            jax.ShapeDtypeStruct((3 * (pairs + UNROLL) + 1,), jnp.int32),
            jax.ShapeDtypeStruct((slots + 2,), jnp.int32),
            jax.ShapeDtypeStruct((8, LANES), jnp.float32),
            jax.ShapeDtypeStruct((slots, LANES, size), jnp.bfloat16),
            jax.ShapeDtypeStruct((16, size), jnp.bfloat16),
        ),
        in_specs=[SMEM] * 6 + [VMEM],
        out_specs=(SMEM, SMEM, VMEM, VMEM, VMEM),
        scratch_shapes=[pltpu.SMEM((3, slots), jnp.int32), pltpu.SMEM((atoms,), jnp.int32)],
        cost_estimate=pl.CostEstimate(flops=10_000_000, bytes_accessed=1_000_000, transcendentals=0),
        name="prepare",
    )(neighbors, pair_extent, atom_size, atom_x, atom_y, atom_z, basis)

    tile_steps = [(dr, dc) for dr in steps for dc in (0, 1, -1)]
    tiles = len(tile_steps)
    lane = jnp.arange(LANES)
    shift_z = jnp.where(lane < 12 * shells, 0.0, jnp.where(lane < 18 * shells, -float(BZ), float(BZ)))
    shift = jnp.where(jnp.arange(8)[:, None] == 2, shift_z[None, :], 0.0).astype(jnp.float32)
    geos = to_tiles(geo, shift, tile_steps, n_row, n_col)
    periods = (float(BX * n_row), float(BY * n_col), float(BZ * n_lay))
    plane, line = pl.pallas_call(
        functools.partial(profile_kernel, periods, tile_steps),
        out_shape=(
            jax.ShapeDtypeStruct((tiles, shells, BX * BY, LANES), jnp.bfloat16),
            jax.ShapeDtypeStruct((tiles, shells, LANES, BZ), jnp.bfloat16),
        ),
        in_specs=[VMEM] * tiles,
        out_specs=(VMEM, VMEM),
        compiler_params=pltpu.CompilerParams(vmem_limit_bytes=12 << 20),
        cost_estimate=pl.CostEstimate(flops=30_000_000, bytes_accessed=4_000_000, transcendentals=2_000_000),
        name="profiles",
    )(*geos)

    sign_next, coef = pl.pallas_call(
        functools.partial(step_kernel, tuple(starts), tuple(widths)),
        out_shape=(
            jax.ShapeDtypeStruct((slots, size, size), jnp.bfloat16),
            jax.ShapeDtypeStruct((8, LANES), jnp.float32),
        ),
        in_specs=[SMEM, SMEM, VMEM, VMEM, VMEM] + [ANY] * len(values),
        out_specs=(VMEM, VMEM),
        scratch_shapes=[
            pltpu.VMEM((n_pool, size, size), jnp.bfloat16),
            pltpu.VMEM((slots * size, slots * size), jnp.bfloat16),
            pltpu.VMEM((size, slots * size), jnp.bfloat16),
            pltpu.VMEM((size, slots * size), jnp.bfloat16),
            pltpu.SemaphoreType.DMA((len(values),)),
        ],
        compiler_params=pltpu.CompilerParams(vmem_limit_bytes=(10 << 20) + n_pool * size * size * 2),
        cost_estimate=pl.CostEstimate(flops=1_300_000_000, bytes_accessed=8_000_000, transcendentals=0),
        name="square_cube_coefficients",
    )(table, info, own_basis, spread, own, *values)

    received = to_tiles(coef, None, tile_steps, n_row, n_col)
    density = pl.pallas_call(
        functools.partial(density_kernel, tiles),
        out_shape=jax.ShapeDtypeStruct((BX * BY, BZ), jnp.float32),
        in_specs=[VMEM] * (tiles + 2),
        out_specs=VMEM,
        scratch_shapes=[pltpu.VMEM((BX * BY, tiles * shells * LANES), jnp.bfloat16)],
        compiler_params=pltpu.CompilerParams(vmem_limit_bytes=16 << 20),
        cost_estimate=pl.CostEstimate(flops=310_000_000, bytes_accessed=4_000_000, transcendentals=0),
        name="density",
    )(*received, plane, line.reshape(tiles * shells * LANES, BZ))
    return sign_next[None], density.reshape(BX, BY, BZ)


def solution(mesh):
    rows = P(("row", "col", "layer"), None, None, None)
    in_specs = (rows, P(), P(), P(), P(("row", "col", "layer"), None), P(), P(), P())
    out_specs = (rows, P("row", "col", "layer"))
    return jax.shard_map(local, mesh=mesh, in_specs=in_specs, out_specs=out_specs, check_vma=False)
```

time: 177 us -> 113 us (0.64)
  blocking collectives: 40.9 us -> 0 us
  local copies, waits for them, and re-layouts: 53.6 us -> 20.3 us
  waiting for transfers between devices: 12.3 us -> 25 us
  starting transfers between devices: 29.8 us -> 42.3 us
  other arithmetic: 8.36 us -> 0.09 us
  Pallas kernels: 29.2 us -> 23.2 us
    all_gather x1 -> x0, blocking collectives: 40.9 us -> none  [local(): lax.all_gather(pair_extent, ('row', 'col', 'layer'), axis=0, tiled=True)]
    squeeze x23 -> x0, local copies, waits for them, and re-layouts: 14.9 us -> none  [the longest x22 13.6 us: local(): part[v, v:]]
    ppermute x13 -> x17, starting transfers between devices: 17.7 us -> 25.3 us  [from_offset(): lax.ppermute(x, axis, [((i + step) % count, i) for i in range(count)])]
    ppermute x21 -> x18, waiting for transfers between devices: 0.22 us -> 7.09 us  [from_layer(): return lax.ppermute(x, 'layer', [(i ^ flip, i) for i in range(count)])]
    pallas_call x1, Pallas kernels: 18 us -> 11.9 us  [local(): pl.pallas_call(functools.partial(step_kernel, tuple(starts), tuple(widths...]
    ppermute x2 -> x4, starting transfers between devices: 2.93 us -> 8.48 us  [to_tiles(): received.append(lax.ppermute(merged, ('row', 'col'), moves))]
    broadcast_in_dim x5 -> x0, local copies, waits for them, and re-layouts: 5.35 us -> none  [the longest x3 5.2 us: local(): packed = jnp.broadcast_to(packed[..., None], packed.shape + (shells,))]
    gather x17 -> x0, local copies, waits for them, and re-layouts: 5.2 us -> none  [the longest x3 0.81 us: local(): at_rank = jnp.take(rank, pair_atom, axis=0) == lane_rank[None, :, None]]
  transfers between devices with their start and end apart: 36 -> 39, of which waited for: 9 -> 10; matrix products, arithmetic and copies ran while one was open for 25% -> 2% of each run, Pallas kernels for 2% -> 18%
where the time goes in v2:
time: 113 us; the launch traced here: 112 us
  starting transfers between devices  42.3 us (37%)
  waiting for transfers between devices  25 us (22%)
  Pallas kernels  23.2 us (21%)
  local copies, waits for them, and re-layouts  20.3 us (18%)
    ppermute x17, starting transfers between devices, from_offset(): lax.ppermute(x, axis, [((i + step) % count, i) for i in range(count)])  25.3 us
    unnamed x54, local copies, waits for them, and re-layouts  19.3 us
    ppermute x17, waiting for transfers between devices, from_offset(): lax.ppermute(x, axis, [((i + step) % count, i) for i in range(count)])  14.4 us
    pallas_call x1, Pallas kernels, local(): pl.pallas_call(functools.partial(step_kernel, tuple(starts), tuple(widths...  11.9 us
    ppermute x18, starting transfers between devices, from_layer(): return lax.ppermute(x, 'layer', [(i ^ flip, i) for i in range(count)])  8.53 us
    ppermute x4, starting transfers between devices, to_tiles(): received.append(lax.ppermute(merged, ('row', 'col'), moves))  8.48 us
    ppermute x18, waiting for transfers between devices, from_layer(): return lax.ppermute(x, 'layer', [(i ^ flip, i) for i in range(count)])  7.09 us
    pallas_call x1, Pallas kernels, local(): pl.pallas_call(functools.partial(prepare_kernel, axes, count, n_pick), ou...  5.24 us
  transfers between devices with their start and end apart: 39, of which 10 were waited for; matrix products, arithmetic and copies ran while one was open for 2% of the time, Pallas kernels for 18%

profile of v2, /device:TPU:0, one launch (start us, length us, event | category | flops | bytes accessed | tf_op | source)
XLA Modules:
  0.0 111.8 jit_solution(10981478236784667318)
XLA Ops:
  0.6 1.4 %copy.11.refs_0_.neighbors_ref = s32[32,12]{1,0:T(8,128)} copy(s32[32,12]{0,1:T(8,128)} %param.9) | data formatting | bytes 3072 | tf_op args[1]
  2.0 1.8 %pick_column_blocks.1 = bf16[5,128,128]{2,1,0:T(8,128)(2,1)} custom-call(s32[32,12]{1,0:T(8,128)} %copy.11.refs_0_.neighbors_ref, bf16[12,128,128]{2,1,0:T(8,128)(2,1)} %bitcast.6), custom_call_target="tpu_custom_call" | custom-call | tf_op jit(solution)/shard_map/pick_column_blocks/pallas_call | solution.py:333
  3.8 5.0 %collective-permute-start.9 = (bf16[5,128,128]{2,1,0:T(8,128)(2,1)}, bf16[5,128,128]{2,1,0:T(8,128)(2,1)S(1)}, u32[]{:S(2)}, u32[]{:S(2)}) collective-permute-start(bf16[5,128,128]{2,1,0:T(8,128)(2,1)} %pick_column_blocks.1), channel_id=1, source_target_pairs={{4,0},{8,4},{12,8},{0,12},{5,1},{9,5},{13,9},{1,13},{6,2},{10,6},{... | collective-permute-start | bytes 491528 | tf_op jit(solution)/shard_map/ppermute | solution.py:22
  8.8 4.9 %collective-permute-done.9.refs_15_ = bf16[5,128,128]{2,1,0:T(8,128)(2,1)S(1)} collective-permute-done((bf16[5,128,128]{2,1,0:T(8,128)(2,1)}, bf16[5,128,128]{2,1,0:T(8,128)(2,1)S(1)}, u32[]{:S(2)}, u32[]{:S(2)}) %collective-permute-start.9) | collective-permute-done | bytes 163872 | tf_op jit(solution)/shard_map/ppermute | solution.py:22
  13.8 1.5 %collective-permute-start.13 = (bf16[5,128,128]{2,1,0:T(8,128)(2,1)S(1)}, bf16[5,128,128]{2,1,0:T(8,128)(2,1)S(1)}, u32[]{:S(2)}, u32[]{:S(2)}) collective-permute-start(bf16[5,128,128]{2,1,0:T(8,128)(2,1)S(1)} %collective-permute-done.9.refs_15_), channel_id=1, source_target_pairs={{16,0},{0,16},{17,1},{1,17},{18,2},{2,18},{19,3},{3,19},{20,4},{4,... | collective-permute-start | bytes 491528 | tf_op jit(solution)/shard_map/ppermute | solution.py:22
  15.3 1.7 %collective-permute-done.17.refs_23_ = bf16[5,128,128]{2,1,0:T(8,128)(2,1)S(1)} collective-permute-done((bf16[5,128,128]{2,1,0:T(8,128)(2,1)}, bf16[5,128,128]{2,1,0:T(8,128)(2,1)S(1)}, u32[]{:S(2)}, u32[]{:S(2)}) %collective-permute-start.17) | collective-permute-done | bytes 163872 | tf_op jit(solution)/shard_map/ppermute | solution.py:22
  16.9 1.5 %collective-permute-start.19 = (bf16[5,128,128]{2,1,0:T(8,128)(2,1)S(1)}, bf16[5,128,128]{2,1,0:T(8,128)(2,1)S(1)}, u32[]{:S(2)}, u32[]{:S(2)}) collective-permute-start(bf16[5,128,128]{2,1,0:T(8,128)(2,1)S(1)} %collective-permute-done.17.refs_23_), channel_id=1, source_target_pairs={{2,0},{3,1},{0,2},{1,3},{6,4},{7,5},{4,6},{5,7},{10,8},{11,9},{8,1... | collective-permute-start | bytes 491528 | tf_op jit(solution)/shard_map/ppermute | solution.py:27
  18.5 0.5 collective-permute-start.11
  19.0 1.5 %collective-permute-start.3 = (bf16[12,128,128]{2,1,0:T(8,128)(2,1)}, bf16[12,128,128]{2,1,0:T(8,128)(2,1)S(1)}, u32[]{:S(2)}, u32[]{:S(2)}) collective-permute-start(bf16[12,128,128]{2,1,0:T(8,128)(2,1)} %bitcast.7), channel_id=1, source_target_pairs={{16,0},{0,16},{17,1},{1,17},{18,2},{2,18},{19,3},{3,19},{20,4},{4,... | collective-permute-start | bytes 1179656 | tf_op jit(solution)/shard_map/ppermute | solution.py:22
  20.4 1.5 %collective-permute-start.1 = (bf16[12,128,128]{2,1,0:T(8,128)(2,1)}, bf16[12,128,128]{2,1,0:T(8,128)(2,1)S(1)}, u32[]{:S(2)}, u32[]{:S(2)}) collective-permute-start(bf16[12,128,128]{2,1,0:T(8,128)(2,1)} %bitcast.8), channel_id=1, source_target_pairs={{2,0},{3,1},{0,2},{1,3},{6,4},{7,5},{4,6},{5,7},{10,8},{11,9},{8,1... | collective-permute-start | bytes 1179656 | tf_op jit(solution)/shard_map/ppermute | solution.py:27
  22.0 2.1 %collective-permute-done.19.refs_25_ = bf16[5,128,128]{2,1,0:T(8,128)(2,1)S(1)} collective-permute-done((bf16[5,128,128]{2,1,0:T(8,128)(2,1)S(1)}, bf16[5,128,128]{2,1,0:T(8,128)(2,1)S(1)}, u32[]{:S(2)}, u32[]{:S(2)}) %collective-permute-start.19) | collective-permute-done | bytes 163872 | tf_op jit(solution)/shard_map/ppermute | solution.py:27
  24.1 1.5 %collective-permute-start.21 = (bf16[5,128,128]{2,1,0:T(8,128)(2,1)S(1)}, bf16[5,128,128]{2,1,0:T(8,128)(2,1)S(1)}, u32[]{:S(2)}, u32[]{:S(2)}) collective-permute-start(bf16[5,128,128]{2,1,0:T(8,128)(2,1)S(1)} %collective-permute-done.17.refs_23_), channel_id=1, source_target_pairs={{16,0},{0,16},{17,1},{1,17},{18,2},{2,18},{19,3},{3,19},{20,4},{4,... | collective-permute-start | bytes 491528 | tf_op jit(solution)/shard_map/ppermute | solution.py:22
  25.6 2.0 %collective-permute-done.11.refs_17_ = bf16[5,128,128]{2,1,0:T(8,128)(2,1)S(1)} collective-permute-done((bf16[5,128,128]{2,1,0:T(8,128)(2,1)S(1)}, bf16[5,128,128]{2,1,0:T(8,128)(2,1)S(1)}, u32[]{:S(2)}, u32[]{:S(2)}) %collective-permute-start.11) | collective-permute-done | bytes 163872 | tf_op jit(solution)/shard_map/ppermute | solution.py:27
  27.6 4.6 %collective-permute-done.21.refs_27_ = bf16[5,128,128]{2,1,0:T(8,128)(2,1)S(1)} collective-permute-done((bf16[5,128,128]{2,1,0:T(8,128)(2,1)S(1)}, bf16[5,128,128]{2,1,0:T(8,128)(2,1)S(1)}, u32[]{:S(2)}, u32[]{:S(2)}) %collective-permute-start.21) | collective-permute-done | bytes 163872 | tf_op jit(solution)/shard_map/ppermute | solution.py:22
  32.2 1.6 %collective-permute-start.15 = (bf16[5,128,128]{2,1,0:T(8,128)(2,1)S(1)}, bf16[5,128,128]{2,1,0:T(8,128)(2,1)S(1)}, u32[]{:S(2)}, u32[]{:S(2)}) collective-permute-start(bf16[5,128,128]{2,1,0:T(8,128)(2,1)S(1)} %collective-permute-done.13.refs_19_), channel_id=1, source_target_pairs={{2,0},{3,1},{0,2},{1,3},{6,4},{7,5},{4,6},{5,7},{10,8},{11,9},{8,1... | collective-permute-start | bytes 491528 | tf_op jit(solution)/shard_map/ppermute | solution.py:27
  33.8 1.5 %collective-permute-start.23 = (bf16[5,128,128]{2,1,0:T(8,128)(2,1)S(1)}, bf16[5,128,128]{2,1,0:T(8,128)(2,1)}, u32[]{:S(2)}, u32[]{:S(2)}) collective-permute-start(bf16[5,128,128]{2,1,0:T(8,128)(2,1)S(1)} %collective-permute-done.19.refs_25_), channel_id=1, source_target_pairs={{16,0},{0,16},{17,1},{1,17},{18,2},{2,18},{19,3},{3,19},{20,4},{4,... | collective-permute-start | bytes 491528 | tf_op jit(solution)/shard_map/ppermute | solution.py:22
  35.3 0.5 collective-permute-start.20
  35.9 2.9 %collective-permute-done.15.refs_21_ = bf16[5,128,128]{2,1,0:T(8,128)(2,1)S(1)} collective-permute-done((bf16[5,128,128]{2,1,0:T(8,128)(2,1)S(1)}, bf16[5,128,128]{2,1,0:T(8,128)(2,1)S(1)}, u32[]{:S(2)}, u32[]{:S(2)}) %collective-permute-start.15) | collective-permute-done | bytes 163872 | tf_op jit(solution)/shard_map/ppermute | solution.py:27
  38.9 1.3 %collective-permute-done.23.refs_29_ = bf16[5,128,128]{2,1,0:T(8,128)(2,1)} collective-permute-done((bf16[5,128,128]{2,1,0:T(8,128)(2,1)S(1)}, bf16[5,128,128]{2,1,0:T(8,128)(2,1)}, u32[]{:S(2)}, u32[]{:S(2)}) %collective-permute-start.23) | collective-permute-done | bytes 163872 | tf_op jit(solution)/shard_map/ppermute | solution.py:22
  40.2 1.3 %collective-permute-start.5 = (bf16[6,128,128]{2,1,0:T(8,128)(2,1)S(1)}, bf16[6,128,128]{2,1,0:T(8,128)(2,1)S(1)}, u32[]{:S(2)}, u32[]{:S(2)}) collective-permute-start(bf16[6,128,128]{2,1,0:T(8,128)(2,1)S(1)} %slice.32), channel_id=1, source_target_pairs={{2,0},{3,1},{0,2},{1,3},{6,4},{7,5},{4,6},{5,7},{10,8},{11,9},{8,1... | collective-permute-start | bytes 589832 | tf_op jit(solution)/shard_map/ppermute | solution.py:27
  41.5 0.7 copy-done.12
  42.1 1.5 %collective-permute-start.7 = (bf16[6,128,128]{2,1,0:T(8,128)(2,1)S(1)}, bf16[6,128,128]{2,1,0:T(8,128)(2,1)S(1)}, u32[]{:S(2)}, u32[]{:S(2)}) collective-permute-start(bf16[6,128,128]{2,1,0:T(8,128)(2,1)S(1)} %slice.33), channel_id=1, source_target_pairs={{16,0},{0,16},{17,1},{1,17},{18,2},{2,18},{19,3},{3,19},{20,4},{4,... | collective-permute-start | bytes 589832 | tf_op jit(solution)/shard_map/ppermute | solution.py:22
  43.6 0.7 copy-done.14
  44.3 0.6 copy-done.16
  45.0 0.5 collective-permute-start.4
  45.5 0.7 copy-done.18
  46.2 0.7 copy-done.10
  46.8 0.5 collective-permute-start.6
  47.3 0.9 collective-permute-done.7.refs_13_
  48.2 0.7 copy-done.20
  48.9 0.5 collective-permute-start.24
  49.4 0.8 copy.10
  50.2 0.7 pad.4.refs_6_
  50.9 5.2 %prepare.1 = (s32[247]{0:T(256)}, s32[14]{0:T(128)}, f32[8,128]{1,0:T(8,128)}, bf16[12,128,128]{2,1,0:T(8,128)(2,1)}, bf16[16,128]{1,0:T(8,128)(2,1)}) custom-call(s32[32,12]{1,0:T(8,128)} %copy.11.refs_0_.neighbors_ref, s32[1,12]{1,0:T(1,128)} %refs_1_.1, s32[32]{0:T(128)} %refs_2_.1, s32[32]{0:T(128)} %refs_3_.1, s32[32]{0:T(128)} %refs_4_.1, s32[32]{0:T(128)} %refs_5_.1, ...), custom_call_target="tpu_custom_call" | custom-call | flops 10000000 | bytes 1000000 | tf_op jit(solution)/shard_map/prepare/pallas_call | solution.py:379
  56.2 1.7 %collective-permute-start.33 = (f32[8,128]{1,0:T(8,128)}, f32[8,128]{1,0:T(8,128)S(1)}, u32[]{:S(2)}, u32[]{:S(2)}) collective-permute-start(f32[8,128]{1,0:T(8,128)} %get-tuple-element.17), channel_id=1, source_target_pairs={{1,0},{2,1},{3,2},{0,3},{5,4},{6,5},{7,6},{4,7},{9,8},{10,9},{11,1... | collective-permute-start | bytes 12296 | tf_op jit(solution)/shard_map/ppermute | solution.py:22
  58.0 1.0 copy-done
  59.0 1.0 copy-done.1
  59.9 0.9 copy-done.3
  60.9 0.9 copy-done.5
  61.8 0.9 copy-done.7
  62.7 0.9 copy-done.9
  63.6 0.9 copy-done.11
  64.5 0.9 copy-done.13
  65.4 0.9 copy-done.15
  66.4 0.9 copy-done.17
  67.3 0.9 copy-done.19
  68.2 0.9 copy-done.21
  69.1 0.7 copy-done.22
  69.8 0.7 copy-done.23
  70.5 0.6 copy-done.24
  71.1 11.9 %square_cube_coefficients.1 = (bf16[12,128,128]{2,1,0:T(8,128)(2,1)}, f32[8,128]{1,0:T(8,128)S(1)}) custom-call(s32[247]{0:T(256)S(1)} %copy-done.23, s32[14]{0:T(128)S(1)} %copy-done.24, bf16[16,128]{1,0:T(8,128)(2,1)S(1)} %copy-done.22, bf16[12,128,128]{2,1,0:T(8,128)(2,1)S(1)} %copy-done.1, bf16[12,128,128]{2,1,0:T(8,128)(2,1)S(1)} %bitcast.10, ...), custom_call_target="tpu_custom_call" | custom-call | flops 1300000000 | bytes 8000000 | tf_op jit(solution)/shard_map/square_cube_coefficients/pallas_call | solution.py:415
  83.1 1.7 %collective-permute-start.26 = (f32[8,128]{1,0:T(8,128)S(1)}, f32[8,128]{1,0:T(8,128)S(1)}, u32[]{:S(2)}, u32[]{:S(2)}) collective-permute-start(f32[8,128]{1,0:T(8,128)S(1)} %get-tuple-element.16), channel_id=1, source_target_pairs={{1,0},{2,1},{3,2},{0,3},{5,4},{6,5},{7,6},{4,7},{9,8},{10,9},{11,1... | collective-permute-start | bytes 12296 | tf_op jit(solution)/shard_map/ppermute | solution.py:22
  84.8 0.1 pad.12.clone
  85.0 1.1 collective-permute-done.25
  86.2 0.1 maximum_add_fusion
  86.3 2.8 %collective-permute-start.34 = (f32[8,128]{1,0:T(8,128)S(1)}, f32[8,128]{1,0:T(8,128)S(1)}, u32[]{:S(2)}, u32[]{:S(2)}) collective-permute-start(f32[8,128]{1,0:T(8,128)S(1)} %get-tuple-element.20.refs_0_), channel_id=1, source_target_pairs={{4,0},{8,4},{12,8},{0,12},{5,1},{9,5},{13,9},{1,13},{6,2},{10,6},{... | collective-permute-start | bytes 12296 | tf_op jit(solution)/shard_map/ppermute | solution.py:22
  89.2 1.0 collective-permute-start.36
  90.2 4.3 %collective-permute-start.37 = (f32[8,128]{1,0:T(8,128)S(1)}, f32[8,128]{1,0:T(8,128)S(1)}, u32[]{:S(2)}, u32[]{:S(2)}) collective-permute-start(f32[8,128]{1,0:T(8,128)S(1)} %get-tuple-element.20.refs_0_), channel_id=1, source_target_pairs={{20,0},{24,4},{28,8},{16,12},{4,16},{8,20},{12,24},{0,28},{21,1},{... | collective-permute-start | bytes 12296 | tf_op jit(solution)/shard_map/ppermute | solution.py:309
  94.5 4.3 %collective-permute-start.27 = (f32[8,128]{1,0:T(8,128)S(1)}, f32[8,128]{1,0:T(8,128)S(1)}, u32[]{:S(2)}, u32[]{:S(2)}) collective-permute-start(f32[8,128]{1,0:T(8,128)S(1)} %get-tuple-element.21.refs_0_), channel_id=1, source_target_pairs={{4,0},{8,4},{12,8},{0,12},{5,1},{9,5},{13,9},{1,13},{6,2},{10,6},{... | collective-permute-start | bytes 12296 | tf_op jit(solution)/shard_map/ppermute | solution.py:22
  98.7 1.1 collective-permute-start.29
  99.8 4.2 %collective-permute-start.30 = (f32[8,128]{1,0:T(8,128)S(1)}, f32[8,128]{1,0:T(8,128)S(1)}, u32[]{:S(2)}, u32[]{:S(2)}) collective-permute-start(f32[8,128]{1,0:T(8,128)S(1)} %get-tuple-element.21.refs_0_), channel_id=1, source_target_pairs={{20,0},{24,4},{28,8},{16,12},{4,16},{8,20},{12,24},{0,28},{21,1},{... | collective-permute-start | bytes 12296 | tf_op jit(solution)/shard_map/ppermute | solution.py:309
  104.0 2.8 %profiles.1 = (bf16[6,6,256,128]{3,2,1,0:T(8,128)(2,1)S(1)}, bf16[6,6,128,128]{3,2,1,0:T(8,128)(2,1)S(1)}) custom-call(f32[8,128]{1,0:T(8,128)S(1)} %get-tuple-element.20.refs_0_, f32[8,128]{1,0:T(8,128)S(1)} %collective-permute-done.34.refs_1_, f32[8,128]{1,0:T(8,128)S(1)} %collective-permute-done.35.refs_2_, f32[8,128]{1,0:T(8,128)S(1)} %collective-permute-done.36.refs_3_, ...), custom_call_target="tpu_custom_call" | custom-call | flops 30000000 | bytes 4000000 | tf_op jit(solution)/shard_map/profiles/pallas_call | solution.py:402
  106.9 3.5 %collective-permute-done.31.refs_5_ = f32[8,128]{1,0:T(8,128)S(1)} collective-permute-done((f32[8,128]{1,0:T(8,128)S(1)}, f32[8,128]{1,0:T(8,128)S(1)}, u32[]{:S(2)}, u32[]{:S(2)}) %collective-permute-start.31) | collective-permute-done | bytes 4128 | tf_op jit(solution)/shard_map/ppermute | solution.py:309
  110.3 1.5 %density.1 = f32[256,128]{1,0:T(8,128)} custom-call(f32[8,128]{1,0:T(8,128)S(1)} %get-tuple-element.21.refs_0_, f32[8,128]{1,0:T(8,128)S(1)} %collective-permute-done.27.refs_1_, f32[8,128]{1,0:T(8,128)S(1)} %collective-permute-done.28.refs_2_, f32[8,128]{1,0:T(8,128)S(1)} %collective-permute-done.29.refs_3_, f32[8,128]{1,0:T(8,128)S(1)} %collective-permute-done.30.refs_4_, ...), custom_call_target="tpu_custom_call" | custom-call | flops 310000000 | bytes 4000000 | tf_op jit(solution)/shard_map/density/pallas_call | solution.py:436
  (85 shorter events, 0.7 us)
Async XLA Ops:
  3.8 10.0 %collective-permute-start.9 = (bf16[5,128,128]{2,1,0:T(8,128)(2,1)}, bf16[5,128,128]{2,1,0:T(8,128)(2,1)S(1)}, u32[]{:S(2)}, u32[]{:S(2)}) collective-permute-start(bf16[5,128,128]{2,1,0:T(8,128)(2,1)} %pick_column_blocks.1), channel_id=1, source_target_pairs={{4,0},{8,4},{12,8},{0,12},{5,1},{9,5},{13,9},{1,13},{6,2},{10,6},{... | collective-permute-start | bytes 491528 | tf_op jit(solution)/shard_map/ppermute | solution.py:22
  8.8 8.1 %collective-permute-start.17 = (bf16[5,128,128]{2,1,0:T(8,128)(2,1)}, bf16[5,128,128]{2,1,0:T(8,128)(2,1)S(1)}, u32[]{:S(2)}, u32[]{:S(2)}) collective-permute-start(bf16[5,128,128]{2,1,0:T(8,128)(2,1)} %pick_column_blocks.1), channel_id=1, source_target_pairs={{12,0},{0,4},{4,8},{8,12},{13,1},{1,5},{5,9},{9,13},{14,2},{2,6},{... | collective-permute-start | bytes 491528 | tf_op jit(solution)/shard_map/ppermute | solution.py:22
  13.8 8.2 %collective-permute-start.13 = (bf16[5,128,128]{2,1,0:T(8,128)(2,1)S(1)}, bf16[5,128,128]{2,1,0:T(8,128)(2,1)S(1)}, u32[]{:S(2)}, u32[]{:S(2)}) collective-permute-start(bf16[5,128,128]{2,1,0:T(8,128)(2,1)S(1)} %collective-permute-done.9.refs_15_), channel_id=1, source_target_pairs={{16,0},{0,16},{17,1},{1,17},{18,2},{2,18},{19,3},{3,19},{20,4},{4,... | collective-permute-start | bytes 491528 | tf_op jit(solution)/shard_map/ppermute | solution.py:22
  16.9 7.1 %collective-permute-start.19 = (bf16[5,128,128]{2,1,0:T(8,128)(2,1)S(1)}, bf16[5,128,128]{2,1,0:T(8,128)(2,1)S(1)}, u32[]{:S(2)}, u32[]{:S(2)}) collective-permute-start(bf16[5,128,128]{2,1,0:T(8,128)(2,1)S(1)} %collective-permute-done.17.refs_23_), channel_id=1, source_target_pairs={{2,0},{3,1},{0,2},{1,3},{6,4},{7,5},{4,6},{5,7},{10,8},{11,9},{8,1... | collective-permute-start | bytes 491528 | tf_op jit(solution)/shard_map/ppermute | solution.py:27
  18.5 9.1 %collective-permute-start.11 = (bf16[5,128,128]{2,1,0:T(8,128)(2,1)S(1)}, bf16[5,128,128]{2,1,0:T(8,128)(2,1)S(1)}, u32[]{:S(2)}, u32[]{:S(2)}) collective-permute-start(bf16[5,128,128]{2,1,0:T(8,128)(2,1)S(1)} %collective-permute-done.9.refs_15_), channel_id=1, source_target_pairs={{2,0},{3,1},{0,2},{1,3},{6,4},{7,5},{4,6},{5,7},{10,8},{11,9},{8,1... | collective-permute-start | bytes 491528 | tf_op jit(solution)/shard_map/ppermute | solution.py:27
  19.0 16.3 %collective-permute-start.3 = (bf16[12,128,128]{2,1,0:T(8,128)(2,1)}, bf16[12,128,128]{2,1,0:T(8,128)(2,1)S(1)}, u32[]{:S(2)}, u32[]{:S(2)}) collective-permute-start(bf16[12,128,128]{2,1,0:T(8,128)(2,1)} %bitcast.7), channel_id=1, source_target_pairs={{16,0},{0,16},{17,1},{1,17},{18,2},{2,18},{19,3},{3,19},{20,4},{4,... | collective-permute-start | bytes 1179656 | tf_op jit(solution)/shard_map/ppermute | solution.py:22
  20.4 14.9 %collective-permute-start.1 = (bf16[12,128,128]{2,1,0:T(8,128)(2,1)}, bf16[12,128,128]{2,1,0:T(8,128)(2,1)S(1)}, u32[]{:S(2)}, u32[]{:S(2)}) collective-permute-start(bf16[12,128,128]{2,1,0:T(8,128)(2,1)} %bitcast.8), channel_id=1, source_target_pairs={{2,0},{3,1},{0,2},{1,3},{6,4},{7,5},{4,6},{5,7},{10,8},{11,9},{8,1... | collective-permute-start | bytes 1179656 | tf_op jit(solution)/shard_map/ppermute | solution.py:27
  22.0 13.8 %collective-permute-start = (bf16[12,128,128]{2,1,0:T(8,128)(2,1)}, bf16[12,128,128]{2,1,0:T(8,128)(2,1)S(1)}, u32[]{:S(2)}, u32[]{:S(2)}) collective-permute-start(bf16[12,128,128]{2,1,0:T(8,128)(2,1)} %bitcast.9), channel_id=1, source_target_pairs={{1,0},{0,1},{3,2},{2,3},{5,4},{4,5},{7,6},{6,7},{9,8},{8,9},{11,10... | collective-permute-start | bytes 1179656 | tf_op jit(solution)/shard_map/ppermute | solution.py:27
  24.1 8.1 %collective-permute-start.21 = (bf16[5,128,128]{2,1,0:T(8,128)(2,1)S(1)}, bf16[5,128,128]{2,1,0:T(8,128)(2,1)S(1)}, u32[]{:S(2)}, u32[]{:S(2)}) collective-permute-start(bf16[5,128,128]{2,1,0:T(8,128)(2,1)S(1)} %collective-permute-done.17.refs_23_), channel_id=1, source_target_pairs={{16,0},{0,16},{17,1},{1,17},{18,2},{2,18},{19,3},{3,19},{20,4},{4,... | collective-permute-start | bytes 491528 | tf_op jit(solution)/shard_map/ppermute | solution.py:22
  27.6 16.7 %copy-start.2 = (bf16[5,128,128]{2,1,0:T(8,128)(2,1)}, bf16[5,128,128]{2,1,0:T(8,128)(2,1)S(1)}, u32[]{:S(2)}) copy-start(bf16[5,128,128]{2,1,0:T(8,128)(2,1)S(1)} %collective-permute-done.11.refs_17_) | copy-start | bytes 491524
  27.6 4.6 %collective-permute-start.10 = (bf16[5,128,128]{2,1,0:T(8,128)(2,1)S(1)}, bf16[5,128,128]{2,1,0:T(8,128)(2,1)S(1)}, u32[]{:S(2)}, u32[]{:S(2)}) collective-permute-start(bf16[5,128,128]{2,1,0:T(8,128)(2,1)S(1)} %collective-permute-done.9.refs_15_), channel_id=1, source_target_pairs={{1,0},{0,1},{3,2},{2,3},{5,4},{4,5},{7,6},{6,7},{9,8},{8,9},{11,10... | collective-permute-start | bytes 491528 | tf_op jit(solution)/shard_map/ppermute | solution.py:27
  32.2 13.9 %copy-start.4 = (bf16[5,128,128]{2,1,0:T(8,128)(2,1)}, bf16[5,128,128]{2,1,0:T(8,128)(2,1)S(1)}, u32[]{:S(2)}) copy-start(bf16[5,128,128]{2,1,0:T(8,128)(2,1)S(1)} %collective-permute-done.21.refs_27_) | copy-start | bytes 491524
  32.2 1.6 %collective-permute-start.18 = (bf16[5,128,128]{2,1,0:T(8,128)(2,1)S(1)}, bf16[5,128,128]{2,1,0:T(8,128)(2,1)S(1)}, u32[]{:S(2)}, u32[]{:S(2)}) collective-permute-start(bf16[5,128,128]{2,1,0:T(8,128)(2,1)S(1)} %collective-permute-done.17.refs_23_), channel_id=1, source_target_pairs={{1,0},{0,1},{3,2},{2,3},{5,4},{4,5},{7,6},{6,7},{9,8},{8,9},{11,10... | collective-permute-start | bytes 491528 | tf_op jit(solution)/shard_map/ppermute | solution.py:27
  32.2 13.9 %copy-start.6 = (bf16[5,128,128]{2,1,0:T(8,128)(2,1)}, bf16[5,128,128]{2,1,0:T(8,128)(2,1)S(1)}, u32[]{:S(2)}) copy-start(bf16[5,128,128]{2,1,0:T(8,128)(2,1)S(1)} %collective-permute-done.10.refs_16_) | copy-start | bytes 491524
  32.2 6.6 %collective-permute-start.15 = (bf16[5,128,128]{2,1,0:T(8,128)(2,1)S(1)}, bf16[5,128,128]{2,1,0:T(8,128)(2,1)S(1)}, u32[]{:S(2)}, u32[]{:S(2)}) collective-permute-start(bf16[5,128,128]{2,1,0:T(8,128)(2,1)S(1)} %collective-permute-done.13.refs_19_), channel_id=1, source_target_pairs={{2,0},{3,1},{0,2},{1,3},{6,4},{7,5},{4,6},{5,7},{10,8},{11,9},{8,1... | collective-permute-start | bytes 491528 | tf_op jit(solution)/shard_map/ppermute | solution.py:27
  33.8 9.8 %copy-start.8 = (bf16[5,128,128]{2,1,0:T(8,128)(2,1)}, bf16[5,128,128]{2,1,0:T(8,128)(2,1)S(1)}, u32[]{:S(2)}) copy-start(bf16[5,128,128]{2,1,0:T(8,128)(2,1)S(1)} %collective-permute-done.18.refs_24_) | copy-start | bytes 491524
  33.8 6.4 %collective-permute-start.23 = (bf16[5,128,128]{2,1,0:T(8,128)(2,1)S(1)}, bf16[5,128,128]{2,1,0:T(8,128)(2,1)}, u32[]{:S(2)}, u32[]{:S(2)}) collective-permute-start(bf16[5,128,128]{2,1,0:T(8,128)(2,1)S(1)} %collective-permute-done.19.refs_25_), channel_id=1, source_target_pairs={{16,0},{0,16},{17,1},{1,17},{18,2},{2,18},{19,3},{3,19},{20,4},{4,... | collective-permute-start | bytes 491528 | tf_op jit(solution)/shard_map/ppermute | solution.py:22
  35.3 6.2 %collective-permute-start.14 = (bf16[5,128,128]{2,1,0:T(8,128)(2,1)S(1)}, bf16[5,128,128]{2,1,0:T(8,128)(2,1)S(1)}, u32[]{:S(2)}, u32[]{:S(2)}) collective-permute-start(bf16[5,128,128]{2,1,0:T(8,128)(2,1)S(1)} %collective-permute-done.13.refs_19_), channel_id=1, source_target_pairs={{1,0},{0,1},{3,2},{2,3},{5,4},{4,5},{7,6},{6,7},{9,8},{8,9},{11,10... | collective-permute-start | bytes 491528 | tf_op jit(solution)/shard_map/ppermute | solution.py:27
  35.3 8.3 %collective-permute-start.20 = (bf16[5,128,128]{2,1,0:T(8,128)(2,1)S(1)}, bf16[5,128,128]{2,1,0:T(8,128)(2,1)S(1)}, u32[]{:S(2)}, u32[]{:S(2)}) collective-permute-start(bf16[5,128,128]{2,1,0:T(8,128)(2,1)S(1)} %collective-permute-done.19.refs_25_), channel_id=1, source_target_pairs={{1,0},{0,1},{3,2},{2,3},{5,4},{4,5},{7,6},{6,7},{9,8},{8,9},{11,10... | collective-permute-start | bytes 491528 | tf_op jit(solution)/shard_map/ppermute | solution.py:27
  35.8 8.5 %collective-permute-start.12 = (bf16[5,128,128]{2,1,0:T(8,128)(2,1)S(1)}, bf16[5,128,128]{2,1,0:T(8,128)(2,1)S(1)}, u32[]{:S(2)}, u32[]{:S(2)}) collective-permute-start(bf16[5,128,128]{2,1,0:T(8,128)(2,1)S(1)} %collective-permute-done.11.refs_17_), channel_id=1, source_target_pairs={{1,0},{0,1},{3,2},{2,3},{5,4},{4,5},{7,6},{6,7},{9,8},{8,9},{11,10... | collective-permute-start | bytes 491528 | tf_op jit(solution)/shard_map/ppermute | solution.py:27
  38.8 6.6 %collective-permute-start.22 = (bf16[5,128,128]{2,1,0:T(8,128)(2,1)S(1)}, bf16[5,128,128]{2,1,0:T(8,128)(2,1)S(1)}, u32[]{:S(2)}, u32[]{:S(2)}) collective-permute-start(bf16[5,128,128]{2,1,0:T(8,128)(2,1)S(1)} %collective-permute-done.21.refs_27_), channel_id=1, source_target_pairs={{1,0},{0,1},{3,2},{2,3},{5,4},{4,5},{7,6},{6,7},{9,8},{8,9},{11,10... | collective-permute-start | bytes 491528 | tf_op jit(solution)/shard_map/ppermute | solution.py:27
  40.2 6.6 %collective-permute-start.5 = (bf16[6,128,128]{2,1,0:T(8,128)(2,1)S(1)}, bf16[6,128,128]{2,1,0:T(8,128)(2,1)S(1)}, u32[]{:S(2)}, u32[]{:S(2)}) collective-permute-start(bf16[6,128,128]{2,1,0:T(8,128)(2,1)S(1)} %slice.32), channel_id=1, source_target_pairs={{2,0},{3,1},{0,2},{1,3},{6,4},{7,5},{4,6},{5,7},{10,8},{11,9},{8,1... | collective-permute-start | bytes 589832 | tf_op jit(solution)/shard_map/ppermute | solution.py:27
  41.5 0.7 copy-start.12
  42.1 6.0 %collective-permute-start.7 = (bf16[6,128,128]{2,1,0:T(8,128)(2,1)S(1)}, bf16[6,128,128]{2,1,0:T(8,128)(2,1)S(1)}, u32[]{:S(2)}, u32[]{:S(2)}) collective-permute-start(bf16[6,128,128]{2,1,0:T(8,128)(2,1)S(1)} %slice.33), channel_id=1, source_target_pairs={{16,0},{0,16},{17,1},{1,17},{18,2},{2,18},{19,3},{3,19},{20,4},{4,... | collective-permute-start | bytes 589832 | tf_op jit(solution)/shard_map/ppermute | solution.py:22
  43.6 0.7 copy-start.14
  44.3 13.6 %collective-permute-start.2 = (bf16[12,128,128]{2,1,0:T(8,128)(2,1)S(1)}, bf16[12,128,128]{2,1,0:T(8,128)(2,1)S(1)}, u32[]{:S(2)}, u32[]{:S(2)}) collective-permute-start(bf16[12,128,128]{2,1,0:T(8,128)(2,1)S(1)} %collective-permute-done.1.refs_7_), channel_id=1, source_target_pairs={{1,0},{0,1},{3,2},{2,3},{5,4},{4,5},{7,6},{6,7},{9,8},{8,9},{11,10... | collective-permute-start | bytes 1179656 | tf_op jit(solution)/shard_map/ppermute | solution.py:27
  44.3 0.7 copy-start.16
  45.0 13.0 %collective-permute-start.4 = (bf16[12,128,128]{2,1,0:T(8,128)(2,1)S(1)}, bf16[12,128,128]{2,1,0:T(8,128)(2,1)S(1)}, u32[]{:S(2)}, u32[]{:S(2)}) collective-permute-start(bf16[12,128,128]{2,1,0:T(8,128)(2,1)S(1)} %collective-permute-done.3.refs_9_), channel_id=1, source_target_pairs={{1,0},{0,1},{3,2},{2,3},{5,4},{4,5},{7,6},{6,7},{9,8},{8,9},{11,10... | collective-permute-start | bytes 1179656 | tf_op jit(solution)/shard_map/ppermute | solution.py:27
  45.5 0.7 copy-start.18
  46.1 2.1 %collective-permute-start.16 = (bf16[5,128,128]{2,1,0:T(8,128)(2,1)S(1)}, bf16[5,128,128]{2,1,0:T(8,128)(2,1)S(1)}, u32[]{:S(2)}, u32[]{:S(2)}) collective-permute-start(bf16[5,128,128]{2,1,0:T(8,128)(2,1)S(1)} %collective-permute-done.15.refs_21_), channel_id=1, source_target_pairs={{1,0},{0,1},{3,2},{2,3},{5,4},{4,5},{7,6},{6,7},{9,8},{8,9},{11,10... | collective-permute-start | bytes 491528 | tf_op jit(solution)/shard_map/ppermute | solution.py:27
  46.1 0.7 copy-start.10
  46.8 9.4 %collective-permute-start.6 = (bf16[6,128,128]{2,1,0:T(8,128)(2,1)S(1)}, bf16[6,128,128]{2,1,0:T(8,128)(2,1)S(1)}, u32[]{:S(2)}, u32[]{:S(2)}) collective-permute-start(bf16[6,128,128]{2,1,0:T(8,128)(2,1)S(1)} %collective-permute-done.5.refs_11_), channel_id=1, source_target_pairs={{1,0},{0,1},{3,2},{2,3},{5,4},{4,5},{7,6},{6,7},{9,8},{8,9},{11,10... | collective-permute-start | bytes 589832 | tf_op jit(solution)/shard_map/ppermute | solution.py:27
  48.2 9.8 %collective-permute-start.8 = (bf16[6,128,128]{2,1,0:T(8,128)(2,1)S(1)}, bf16[6,128,128]{2,1,0:T(8,128)(2,1)S(1)}, u32[]{:S(2)}, u32[]{:S(2)}) collective-permute-start(bf16[6,128,128]{2,1,0:T(8,128)(2,1)S(1)} %collective-permute-done.7.refs_13_), channel_id=1, source_target_pairs={{1,0},{0,1},{3,2},{2,3},{5,4},{4,5},{7,6},{6,7},{9,8},{8,9},{11,10... | collective-permute-start | bytes 589832 | tf_op jit(solution)/shard_map/ppermute | solution.py:27
  48.2 0.7 copy-start.20
  48.9 7.3 %collective-permute-start.24 = (bf16[5,128,128]{2,1,0:T(8,128)(2,1)}, bf16[5,128,128]{2,1,0:T(8,128)(2,1)}, u32[]{:S(2)}, u32[]{:S(2)}) collective-permute-start(bf16[5,128,128]{2,1,0:T(8,128)(2,1)} %collective-permute-done.23.refs_29_), channel_id=1, source_target_pairs={{1,0},{0,1},{3,2},{2,3},{5,4},{4,5},{7,6},{6,7},{9,8},{8,9},{11,10... | collective-permute-start | bytes 491528 | tf_op jit(solution)/shard_map/ppermute | solution.py:27
  56.1 28.8 %collective-permute-start.32 = (f32[8,128]{1,0:T(8,128)}, f32[8,128]{1,0:T(8,128)S(1)}, u32[]{:S(2)}, u32[]{:S(2)}) collective-permute-start(f32[8,128]{1,0:T(8,128)} %get-tuple-element.17), channel_id=1, source_target_pairs={{3,0},{0,1},{1,2},{2,3},{7,4},{4,5},{5,6},{6,7},{11,8},{8,9},{9,10... | collective-permute-start | bytes 12296 | tf_op jit(solution)/shard_map/ppermute | solution.py:22
  56.2 28.8 %collective-permute-start.33 = (f32[8,128]{1,0:T(8,128)}, f32[8,128]{1,0:T(8,128)S(1)}, u32[]{:S(2)}, u32[]{:S(2)}) collective-permute-start(f32[8,128]{1,0:T(8,128)} %get-tuple-element.17), channel_id=1, source_target_pairs={{1,0},{2,1},{3,2},{0,3},{5,4},{6,5},{7,6},{4,7},{9,8},{10,9},{11,1... | collective-permute-start | bytes 12296 | tf_op jit(solution)/shard_map/ppermute | solution.py:22
  58.0 1.0 copy-start
  59.0 1.0 copy-start.1
  59.9 0.9 copy-start.3
  60.9 0.9 copy-start.5
  61.8 0.9 copy-start.7
  62.7 0.9 copy-start.9
  63.6 0.9 copy-start.11
  64.5 0.9 copy-start.13
  65.4 0.9 copy-start.15
  66.4 0.9 copy-start.17
  67.3 0.9 copy-start.19
  68.2 0.9 copy-start.21
  69.1 0.7 copy-start.22
  69.8 0.7 copy-start.23
  71.1 15.2 %copy-start.25 = (f32[8,128]{1,0:T(8,128)S(1)}, f32[8,128]{1,0:T(8,128)}, u32[]{:S(2)}) copy-start(f32[8,128]{1,0:T(8,128)} %get-tuple-element.17) | copy-start | bytes 12292
  83.0 3.1 %collective-permute-start.25 = (f32[8,128]{1,0:T(8,128)S(1)}, f32[8,128]{1,0:T(8,128)S(1)}, u32[]{:S(2)}, u32[]{:S(2)}) collective-permute-start(f32[8,128]{1,0:T(8,128)S(1)} %get-tuple-element.16), channel_id=1, source_target_pairs={{3,0},{0,1},{1,2},{2,3},{7,4},{4,5},{5,6},{6,7},{11,8},{8,9},{9,10... | collective-permute-start | bytes 12296 | tf_op jit(solution)/shard_map/ppermute | solution.py:22
  83.1 3.1 %collective-permute-start.26 = (f32[8,128]{1,0:T(8,128)S(1)}, f32[8,128]{1,0:T(8,128)S(1)}, u32[]{:S(2)}, u32[]{:S(2)}) collective-permute-start(f32[8,128]{1,0:T(8,128)S(1)} %get-tuple-element.16), channel_id=1, source_target_pairs={{1,0},{2,1},{3,2},{0,3},{5,4},{6,5},{7,6},{4,7},{9,8},{10,9},{11,1... | collective-permute-start | bytes 12296 | tf_op jit(solution)/shard_map/ppermute | solution.py:22
  86.3 8.1 %collective-permute-start.34 = (f32[8,128]{1,0:T(8,128)S(1)}, f32[8,128]{1,0:T(8,128)S(1)}, u32[]{:S(2)}, u32[]{:S(2)}) collective-permute-start(f32[8,128]{1,0:T(8,128)S(1)} %get-tuple-element.20.refs_0_), channel_id=1, source_target_pairs={{4,0},{8,4},{12,8},{0,12},{5,1},{9,5},{13,9},{1,13},{6,2},{10,6},{... | collective-permute-start | bytes 12296 | tf_op jit(solution)/shard_map/ppermute | solution.py:22
  89.2 9.6 %collective-permute-start.35 = (f32[8,128]{1,0:T(8,128)S(1)}, f32[8,128]{1,0:T(8,128)S(1)}, u32[]{:S(2)}, u32[]{:S(2)}) collective-permute-start(f32[8,128]{1,0:T(8,128)S(1)} %get-tuple-element.20.refs_0_), channel_id=1, source_target_pairs={{12,0},{0,4},{4,8},{8,12},{13,1},{1,5},{5,9},{9,13},{14,2},{2,6},{... | collective-permute-start | bytes 12296 | tf_op jit(solution)/shard_map/ppermute | solution.py:22
  89.2 9.6 %collective-permute-start.36 = (f32[8,128]{1,0:T(8,128)S(1)}, f32[8,128]{1,0:T(8,128)S(1)}, u32[]{:S(2)}, u32[]{:S(2)}) collective-permute-start(f32[8,128]{1,0:T(8,128)S(1)} %get-tuple-element.20.refs_0_), channel_id=1, source_target_pairs={{16,0},{0,16},{17,1},{1,17},{18,2},{2,18},{19,3},{3,19},{20,4},{4,... | collective-permute-start | bytes 12296 | tf_op jit(solution)/shard_map/ppermute | solution.py:22
  90.2 9.7 %collective-permute-start.37 = (f32[8,128]{1,0:T(8,128)S(1)}, f32[8,128]{1,0:T(8,128)S(1)}, u32[]{:S(2)}, u32[]{:S(2)}) collective-permute-start(f32[8,128]{1,0:T(8,128)S(1)} %get-tuple-element.20.refs_0_), channel_id=1, source_target_pairs={{20,0},{24,4},{28,8},{16,12},{4,16},{8,20},{12,24},{0,28},{21,1},{... | collective-permute-start | bytes 12296 | tf_op jit(solution)/shard_map/ppermute | solution.py:309
  94.4 9.6 %collective-permute-start.38 = (f32[8,128]{1,0:T(8,128)S(1)}, f32[8,128]{1,0:T(8,128)S(1)}, u32[]{:S(2)}, u32[]{:S(2)}) collective-permute-start(f32[8,128]{1,0:T(8,128)S(1)} %get-tuple-element.20.refs_0_), channel_id=1, source_target_pairs={{28,0},{16,4},{20,8},{24,12},{12,16},{0,20},{4,24},{8,28},{29,1},{... | collective-permute-start | bytes 12296 | tf_op jit(solution)/shard_map/ppermute | solution.py:309
  94.5 12.4 %collective-permute-start.27 = (f32[8,128]{1,0:T(8,128)S(1)}, f32[8,128]{1,0:T(8,128)S(1)}, u32[]{:S(2)}, u32[]{:S(2)}) collective-permute-start(f32[8,128]{1,0:T(8,128)S(1)} %get-tuple-element.21.refs_0_), channel_id=1, source_target_pairs={{4,0},{8,4},{12,8},{0,12},{5,1},{9,5},{13,9},{1,13},{6,2},{10,6},{... | collective-permute-start | bytes 12296 | tf_op jit(solution)/shard_map/ppermute | solution.py:22
  98.7 8.1 %collective-permute-start.28 = (f32[8,128]{1,0:T(8,128)S(1)}, f32[8,128]{1,0:T(8,128)S(1)}, u32[]{:S(2)}, u32[]{:S(2)}) collective-permute-start(f32[8,128]{1,0:T(8,128)S(1)} %get-tuple-element.21.refs_0_), channel_id=1, source_target_pairs={{12,0},{0,4},{4,8},{8,12},{13,1},{1,5},{5,9},{9,13},{14,2},{2,6},{... | collective-permute-start | bytes 12296 | tf_op jit(solution)/shard_map/ppermute | solution.py:22
  98.7 8.1 %collective-permute-start.29 = (f32[8,128]{1,0:T(8,128)S(1)}, f32[8,128]{1,0:T(8,128)S(1)}, u32[]{:S(2)}, u32[]{:S(2)}) collective-permute-start(f32[8,128]{1,0:T(8,128)S(1)} %get-tuple-element.21.refs_0_), channel_id=1, source_target_pairs={{16,0},{0,16},{17,1},{1,17},{18,2},{2,18},{19,3},{3,19},{20,4},{4,... | collective-permute-start | bytes 12296 | tf_op jit(solution)/shard_map/ppermute | solution.py:22
  99.8 7.0 %collective-permute-start.30 = (f32[8,128]{1,0:T(8,128)S(1)}, f32[8,128]{1,0:T(8,128)S(1)}, u32[]{:S(2)}, u32[]{:S(2)}) collective-permute-start(f32[8,128]{1,0:T(8,128)S(1)} %get-tuple-element.21.refs_0_), channel_id=1, source_target_pairs={{20,0},{24,4},{28,8},{16,12},{4,16},{8,20},{12,24},{0,28},{21,1},{... | collective-permute-start | bytes 12296 | tf_op jit(solution)/shard_map/ppermute | solution.py:309
  104.0 6.3 %collective-permute-start.31 = (f32[8,128]{1,0:T(8,128)S(1)}, f32[8,128]{1,0:T(8,128)S(1)}, u32[]{:S(2)}, u32[]{:S(2)}) collective-permute-start(f32[8,128]{1,0:T(8,128)S(1)} %get-tuple-element.21.refs_0_), channel_id=1, source_target_pairs={{28,0},{16,4},{20,8},{24,12},{12,16},{0,20},{4,24},{8,28},{29,1},{... | collective-permute-start | bytes 12296 | tf_op jit(solution)/shard_map/ppermute | solution.py:309
  (1 other events, 0.6 us)

commit v3 on v2

v3 whole, which is shorter than its diff:
```python
import functools

import jax
import jax.numpy as jnp
from jax import lax
from jax.experimental import pallas as pl
from jax.experimental.pallas import tpu as pltpu
from jax.sharding import PartitionSpec as P

BX = 16
BY = 16
BZ = 128
LANES = 128
UNROLL = 4
SHELLS = 6
SPAN = 3 * SHELLS
GEO = 16
VMEM = pl.BlockSpec(memory_space=pltpu.VMEM)
SMEM = pl.BlockSpec(memory_space=pltpu.SMEM)
ANY = pl.BlockSpec(memory_space=pl.ANY)


def from_offset(x, axis, step):
    count = lax.axis_size(axis)
    return lax.ppermute(x, axis, [((i + step) % count, i) for i in range(count)])


def from_layer(x, flip):
    count = lax.axis_size("layer")
    return lax.ppermute(x, "layer", [(i ^ flip, i) for i in range(count)])


def column_targets(n_row):
    return 5 if n_row == 2 else 7


def target_place(n_row, step_row, step_lay, row):
    same = jnp.where(step_lay < 3, step_lay, -1)
    if n_row == 2:
        lead = step_lay - row
        across = jnp.where((lead >= 0) & (lead < 2), 3 + lead, -1)
    else:
        across = 3 + step_lay
    return jnp.where(step_row == 0, same, jnp.where(step_row == 1, across, -1))


class Places:
    def __init__(self, n_row, n_col, n_lay):
        self.n_row, self.n_col, self.n_lay = n_row, n_col, n_lay
        self.lay_bits = n_lay.bit_length() - 1
        self.col_bits = n_col.bit_length() - 1
        self.row = lax.axis_index("row")
        self.col = lax.axis_index("col")
        self.lay = lax.axis_index("layer")
        self.me = (((self.row << self.col_bits) + self.col) << self.lay_bits) + self.lay

    def split(self, atom):
        return (
            atom >> (self.lay_bits + self.col_bits),
            (atom >> self.lay_bits) & (self.n_col - 1),
            atom & (self.n_lay - 1),
        )


def own_ranks(at, neighbors_ref):
    seen = [jnp.int32(0)] * at.n_lay
    listed = []
    for w in range(neighbors_ref.shape[0]):
        atom = neighbors_ref[w, at.me]
        step_lay = (atom - at.lay) & (at.n_lay - 1)
        rank = jnp.int32(0)
        for k in range(at.n_lay):
            rank = jnp.where(step_lay == k, 3 * k + seen[k], rank)
            seen[k] = seen[k] + (step_lay == k).astype(jnp.int32)
        listed.append((atom, rank))
    return listed


def pick_kernel(axes, *refs):
    neighbors_ref, extent_ref, x_ref, y_ref, z_ref, sign_ref, out_ref, geo_ref, place_ref = refs
    at = Places(*axes)
    n_pick = place_ref.shape[0] - 1
    size = sign_ref.shape[1]
    sub = lax.broadcasted_iota(jnp.int32, (GEO, LANES), 0)
    lane_pair = lax.broadcasted_iota(jnp.int32, (GEO, LANES), 1) // SHELLS
    geo = jnp.zeros((GEO, LANES), jnp.int32)
    for i in range(n_pick + 1):
        place_ref[i] = 0
    for w, (atom, rank) in enumerate(own_ranks(at, neighbors_ref)):
        row, col, lay = at.split(atom)
        step_row = (row - at.row) & (at.n_row - 1)
        step_col = (col - at.col) & (at.n_col - 1)
        step_lay = (lay - at.lay) & (at.n_lay - 1)
        place = target_place(at.n_row, step_row, step_lay, at.row)
        place_ref[jnp.where((step_col == 0) & (place >= 0), place, n_pick)] = w
        go_row = ((step_row + 1) & (at.n_row - 1)) - 1
        go_col = ((step_col + 1) & (at.n_col - 1)) - 1
        go_lay = jnp.minimum(((step_lay + 1) & (at.n_lay - 1)) - 1, 1)
        twice_x = x_ref[at.me] + x_ref[atom] + BX * go_row
        twice_y = y_ref[at.me] + y_ref[atom] + BY * go_col
        twice_z = z_ref[at.me] + z_ref[atom] + BZ * go_lay - BZ
        values = jnp.where(sub == 0, twice_x, jnp.where(sub == 1, twice_y, jnp.where(sub == 2, twice_z, extent_ref[0, w])))
        geo = jnp.where(lane_pair == rank, values, geo)
    geo = geo.astype(jnp.float32).astype(geo_ref.dtype)
    geo_ref[...] = geo
    out_ref[n_pick * size : n_pick * size + GEO] = geo
    for i in range(n_pick):
        out_ref[i * size : (i + 1) * size] = sign_ref[place_ref[i]]


def prepare_kernel(axes, count, late_from, *refs):
    neighbors_ref, size_ref, layout_ref, basis_ref = refs[:4]
    early_ref, late_ref, info_ref, spread_ref, own_basis_ref, known, inverse = refs[4:]
    at = Places(*axes)
    slots = neighbors_ref.shape[0]
    atoms = neighbors_ref.shape[1]
    bits = atoms.bit_length() - 1
    lines = count * at.n_lay

    def hot(rows, atom, first):
        sub = lax.broadcasted_iota(jnp.int32, (rows, SHELLS * atoms), 0)
        lane = lax.broadcasted_iota(jnp.int32, (rows, SHELLS * atoms), 1)
        return ((lane & (atoms - 1)) == atom) & (sub == first + (lane >> bits))

    def rows_of(chosen):
        picked = jnp.where(chosen, 1.0, 0.0).astype(jnp.bfloat16)
        return jnp.dot(picked, basis_ref[...], preferred_element_type=jnp.float32).astype(jnp.bfloat16)

    self_slot = jnp.int32(0)
    for w, (atom, rank) in enumerate(own_ranks(at, neighbors_ref)):
        row, col, lay = at.split(atom)
        step_row = (row - at.row) & (at.n_row - 1)
        step_col = (col - at.col) & (at.n_col - 1)
        self_slot = jnp.where(atom == at.me, w, self_slot)
        info_ref[w] = size_ref[atom]
        spread_ref[w] = rows_of(hot(LANES, atom, rank * SHELLS))
        flip = lay ^ at.lay
        known[0, w] = atom
        known[1, w] = jnp.where(step_col == 0, 0, jnp.where(step_col == 1, 1, 2))
        known[2, w] = jnp.where(step_row == 0, 0, jnp.where(step_row == 1, 1, 2)) * at.n_lay + flip
        known[3, w] = jnp.where((step_row != 0) & (flip == 3), 16 + w, w)
        inverse[atom] = -1
    own_basis_ref[...] = rows_of(hot(16, at.me, 0))
    info_ref[slots] = size_ref[at.me]
    info_ref[slots + 1] = self_slot

    def row_of_pairs(v, totals):
        early, late = totals
        atom = known[0, v]
        side = known[1, v]
        line = known[2, v]
        turn = known[3, v]
        row, _, lay = at.split(atom)
        for u in range(slots):
            inverse[neighbors_ref[u, atom]] = v * 16 + u
        top = layout_ref[line]
        end = layout_ref[lines + line]
        beside = layout_ref[(side + 1) * lines + line]
        half = slots // 2
        for w in range(slots):
            other = known[0, w]
            other_side = known[1, w]
            mark = inverse[other]
            slot = mark & 15
            o_row, _, o_lay = at.split(other)
            there = target_place(at.n_row, (o_row - row) & (at.n_row - 1), (o_lay - lay) & (at.n_lay - 1), row)
            back = target_place(at.n_row, (row - o_row) & (at.n_row - 1), (lay - o_lay) & (at.n_lay - 1), o_row)
            from_row = (other_side != 0) | (turn <= known[3, w])
            from_column = (side == other_side) & (there >= 0) & ((back < 0) | (v <= w))
            chosen = ((mark >> 4) == v) & jnp.where(side == 0, from_row, from_column)
            in_row = jnp.where(slot < half, top + slot * LANES, end + (slot - half) * LANES)
            where = jnp.where(side == 0, in_row, beside + there * LANES)
            is_late = where >= late_from
            for ref, total in ((early_ref, early), (late_ref, late)):
                ref[3 * total + 1] = v
                ref[3 * total + 2] = w
                ref[3 * total + 3] = where
            late_ref[3 * late + 3] = where - late_from
            early = early + (chosen & ~is_late).astype(jnp.int32)
            late = late + (chosen & is_late).astype(jnp.int32)
        return early, late

    totals = lax.fori_loop(0, slots, row_of_pairs, (jnp.int32(0), jnp.int32(0)))
    for ref, total in zip((early_ref, late_ref), totals):
        ref[0] = (total + UNROLL - 1) // UNROLL
        last = 3 * jnp.maximum(total - 1, 0) + 1
        for i in range(UNROLL - 1):
            for k in range(3):
                ref[3 * (total + i) + 1 + k] = ref[last + k]


def pack_kernel(moves, inputs, outputs, *refs):
    sems = refs[-1]
    copies = []
    for k, (source, start, rows, target, place) in enumerate(moves):
        copy = pltpu.make_async_copy(
            refs[source].at[pl.ds(start, rows)], refs[inputs + target].at[pl.ds(place, rows)], sems.at[k]
        )
        copy.start()
        copies.append(copy)
    for copy in copies:
        copy.wait()


def pack(values, plans, extra, name):
    moves, shapes = [], []
    for target, plan in enumerate(plans):
        place = 0
        for source, start, rows in plan:
            moves.append((source, start, rows, target, place))
            place += rows
        shapes.append(jax.ShapeDtypeStruct((place, LANES), values[0].dtype))
    inputs = len(values) + len(extra)
    return pl.pallas_call(
        functools.partial(pack_kernel, tuple(moves), inputs, len(plans)),
        out_shape=tuple(shapes),
        in_specs=[ANY] * inputs,
        out_specs=tuple([ANY] * len(plans)),
        scratch_shapes=[pltpu.SemaphoreType.DMA((len(moves),))],
        compiler_params=pltpu.CompilerParams(vmem_limit_bytes=1 << 20),
        cost_estimate=pl.CostEstimate(flops=0, bytes_accessed=3_000_000, transcendentals=0),
        name=name,
    )(*values, *extra)


def fill(piece_refs, pool, sems):
    copies = []
    place = 0
    for i, piece in enumerate(piece_refs):
        rows = piece.shape[0]
        copy = pltpu.make_async_copy(piece, pool.at[pl.ds(place, rows)], sems.at[i])
        copy.start()
        copies.append(copy)
        place += rows
    return copies


def place_pairs(table_ref, pool, gram, size):
    def place(i, carry):
        for k in range(UNROLL):
            entry = 3 * (i * UNROLL + k)
            p = pl.multiple_of(table_ref[entry + 1] * size, size)
            q = pl.multiple_of(table_ref[entry + 2] * size, size)
            block = pool[pl.ds(pl.multiple_of(table_ref[entry + 3], 16), size)]
            gram[pl.ds(p, size), pl.ds(q, size)] = block
            gram[pl.ds(q, size), pl.ds(p, size)] = block.T
        return carry

    lax.fori_loop(0, table_ref[0], place, 0)


def gram_kernel(pieces, *refs):
    table_ref = refs[0]
    piece_refs = refs[1 : 1 + pieces]
    gram, pool, sems = refs[-3:]
    size = LANES
    copies = fill(piece_refs, pool, sems)
    for v in range(gram.shape[0] // size):
        gram[v * size : (v + 1) * size] = jnp.zeros((size, gram.shape[1]), gram.dtype)
    for copy in copies:
        copy.wait()
    place_pairs(table_ref, pool, gram, size)


def step_kernel(pieces, *refs):
    table_ref, info_ref, basis_ref, spread_ref, sign_ref, early_ref = refs[:6]
    piece_refs = refs[6 : 6 + pieces]
    next_ref, coef_ref, pool, gram, own, square, sems = refs[6 + pieces :]
    slots, size = sign_ref.shape[0], sign_ref.shape[1]
    copies = fill(piece_refs, pool, sems)
    for v in range(slots):
        gram[v * size : (v + 1) * size] = early_ref[v * size : (v + 1) * size]
    rows = lax.broadcasted_iota(jnp.int32, (size, size), 0)
    lanes = lax.broadcasted_iota(jnp.int32, (size, size), 1)
    own_size = info_ref[slots]
    self_slot = info_ref[slots + 1]
    for w in range(slots):
        kept = (rows < own_size) & (lanes < info_ref[w])
        block = jnp.where(kept, sign_ref[w].astype(jnp.float32), 0.0)
        own[:, w * size : (w + 1) * size] = block.astype(own.dtype)
    for copy in copies:
        copy.wait()
    place_pairs(table_ref, pool, gram, size)
    wide = 2 * size
    wide_lanes = lax.broadcasted_iota(jnp.int32, (size, wide), 1)
    wide_rows = lax.broadcasted_iota(jnp.int32, (size, wide), 0)

    def column_kept(n):
        first = info_ref[2 * n]
        second = info_ref[2 * n + 1]
        return (wide_lanes < first) | ((wide_lanes >= size) & (wide_lanes < size + second))

    for n in range(slots // 2):
        part = jnp.dot(own[...], gram[:, n * wide : (n + 1) * wide], preferred_element_type=jnp.float32)
        square[:, n * wide : (n + 1) * wide] = jnp.where(column_kept(n), part, 0.0).astype(square.dtype)
    coef = jnp.zeros((basis_ref.shape[0], LANES), jnp.float32)
    across = (((1,), (1,)), ((), ()))
    for n in range(slots // 2):
        part = jnp.dot(square[...], gram[:, n * wide : (n + 1) * wide], preferred_element_type=jnp.float32)
        cube = jnp.where(column_kept(n), part, 0.0)
        full = 1.5 * own[:, n * wide : (n + 1) * wide].astype(jnp.float32) - 0.5 * cube
        next_ref[2 * n] = full[:, :size].astype(next_ref.dtype)
        next_ref[2 * n + 1] = full[:, size:].astype(next_ref.dtype)
        shift = (self_slot - 2 * n) * size
        is_self = (self_slot >= 2 * n) & (self_slot < 2 * n + 2)
        diag = (wide_lanes == wide_rows + shift) & (wide_rows < own_size) & is_self
        dmat = 0.5 * (jnp.where(diag, 1.0, 0.0) - full)
        high = dmat.astype(jnp.bfloat16)
        low = (dmat - high.astype(jnp.float32)).astype(jnp.bfloat16)
        half = jnp.dot(basis_ref[...], high, preferred_element_type=jnp.float32) + jnp.dot(
            basis_ref[...], low, preferred_element_type=jnp.float32
        )
        half_high = half.astype(jnp.bfloat16)
        half_low = (half - half_high.astype(jnp.float32)).astype(jnp.bfloat16)
        for k in range(2):
            spread = spread_ref[2 * n + k]
            for part in (half_high, half_low):
                coef = coef + lax.dot_general(
                    part[:, k * size : (k + 1) * size], spread, across, preferred_element_type=jnp.float32
                )
    coef_ref[...] = coef[: coef_ref.shape[0]]


def profile_kernel(periods, steps, sources, inputs, *refs):
    plane_ref, line_ref, geos, sems = refs[inputs:]
    odd = (lax.axis_index("layer") & 1) == 1
    copies = []
    for o, source in enumerate(sources):
        for k, (buffer, start) in enumerate(source):
            copy = pltpu.make_async_copy(refs[buffer].at[pl.ds(start, GEO)], geos.at[3 * o + k], sems.at[3 * o + k])
            copy.start()
            copies.append(copy)
    cells = plane_ref.shape[2]
    cell = lax.broadcasted_iota(jnp.int32, (cells, LANES), 0)
    grid_x = (cell // BY).astype(jnp.float32)
    grid_y = (cell % BY).astype(jnp.float32)
    grid_z = lax.broadcasted_iota(jnp.int32, (LANES, BZ), 1).astype(jnp.float32)
    lane = lax.broadcasted_iota(jnp.int32, (1, LANES), 1)
    shell = (lane % SHELLS + 1).astype(jnp.float32)
    valid = lane < 7 * SPAN
    from_own = lane < 4 * SPAN
    from_below = lane < 6 * SPAN
    lift = jnp.where(from_own, 0.0, jnp.where(from_below, -float(BZ), float(BZ))) + 0.5 * BZ

    def nearest(offset, period):
        return offset - period * jnp.floor(offset * (1.0 / period) + 0.5)

    for copy in copies:
        copy.wait()
    for o, (step_row, step_col) in enumerate(steps):
        own, first, third = (geos[3 * o + k].astype(jnp.float32) for k in range(3))
        below = jnp.where(odd, first, third)
        above = jnp.where(odd, third, first)
        moved = jnp.where(from_below, pltpu.roll(below, 3 * SPAN, axis=1), pltpu.roll(above, 3 * SPAN, axis=1))
        geo = jnp.where(from_own, own, moved)
        extent = jnp.where(valid, geo[3:4], 1.0)
        inverse = (SHELLS / extent) * (SHELLS / extent)
        reach = jnp.where(valid, extent, -1.0)
        rate_t = inverse / (shell * shell)
        packed = jnp.concatenate(
            [0.5 * geo[2:3] + lift, reach, rate_t, inverse, jnp.zeros((4, LANES), jnp.float32)], axis=0
        )
        sub = packed.T
        d_x = nearest(grid_x - (0.5 * geo[0:1] + float(BX * step_row)), periods[0])
        d_y = nearest(grid_y - (0.5 * geo[1:2] + float(BY * step_col)), periods[1])
        inside = (jnp.abs(d_x) <= reach) & (jnp.abs(d_y) <= reach)
        squared = d_x * d_x + d_y * d_y
        d_z = nearest(grid_z - sub[:, 0:1], periods[2])
        inside_z = jnp.abs(d_z) <= sub[:, 1:2]
        squared_z = d_z * d_z
        for s in range(SHELLS):
            part = 1.0 / ((s + 1) * (s + 1))
            rate = inverse * part + rate_t
            plane_ref[o, s] = jnp.where(inside, jnp.exp(-rate * squared), 0.0).astype(plane_ref.dtype)
            rate_z = sub[:, 3:4] * part + sub[:, 2:3]
            line_ref[o, s] = jnp.where(inside_z, jnp.exp(-rate_z * squared_z), 0.0).astype(line_ref.dtype)


def density_kernel(column_steps, *refs):
    coef_refs = refs[:column_steps]
    plane_ref, line_ref, out_ref, terms = refs[column_steps:]
    for o in range(plane_ref.shape[0]):
        coef = coef_refs[o % column_steps]
        first = 8 * (o // column_steps)
        for s in range(SHELLS):
            scaled = plane_ref[o, s].astype(jnp.float32) * coef[first + s : first + s + 1, :]
            at = (o * SHELLS + s) * LANES
            terms[:, at : at + LANES] = scaled.astype(terms.dtype)
    out_ref[...] = jnp.dot(terms[...], line_ref[...], preferred_element_type=jnp.float32)


def local(sign_start, neighbors, atom_size, basis_proj, pair_extent, atom_x, atom_y, atom_z):
    n_row = lax.axis_size("row")
    n_col = lax.axis_size("col")
    n_lay = lax.axis_size("layer")
    assert n_lay == 4 and n_col >= 4 and (n_row == 2 or n_row >= 4)
    assert n_row & (n_row - 1) == 0 and n_col & (n_col - 1) == 0
    axes = (n_row, n_col, n_lay)
    atoms, slots = neighbors.shape
    size = sign_start.shape[2]
    steps = [0, 1] if n_row == 2 else [0, 1, -1]
    count = len(steps)
    others = range(1, count)
    own = sign_start[0]
    flat = own.reshape(slots * size, size)
    listings = neighbors.T
    full = slots * size
    half = full // 2
    n_pick = column_targets(n_row)
    part = n_pick * size + GEO

    def on_row(value, di):
        return from_offset(value, "row", steps[di])

    x_row = {di: on_row(flat, di) for di in others}
    y_row = from_layer(flat, 2)
    m_row = from_layer(flat, 1)
    picked, geo = pl.pallas_call(
        functools.partial(pick_kernel, axes),
        out_shape=(
            jax.ShapeDtypeStruct((part, size), own.dtype),
            jax.ShapeDtypeStruct((GEO, LANES), own.dtype),
        ),
        in_specs=[SMEM] * 5 + [VMEM],
        out_specs=(VMEM, VMEM),
        scratch_shapes=[pltpu.SMEM((n_pick + 1,), jnp.int32)],
        compiler_params=pltpu.CompilerParams(vmem_limit_bytes=2 << 20),
        name="pick_column_blocks",
    )(listings, pair_extent, atom_x, atom_y, atom_z, own)
    up = from_offset(picked, "col", 1)
    down = from_offset(picked, "col", -1)

    at = {}
    buffers = {}

    def note(name, value, contents):
        buffers[name] = value
        start = 0
        for what, rows in contents:
            if what is not None:
                at[what] = (name, start)
            start += rows

    def row_of(di, flip):
        return [(("top", di, flip), half), (("end", di, flip), half)]

    def side_of(kind, di, flip):
        return [((kind, di, flip), part - GEO), ((kind + " geo", di, flip), GEO)]

    note("own", flat, row_of(0, 0))
    note("mate", m_row, row_of(0, 1))
    note("far", y_row, row_of(0, 2))
    note("up", up, side_of("up", 0, 0))
    note("down", down, side_of("down", 0, 0))
    note("geo", geo, [(("geo", 0, 0), GEO)])
    for di in others:
        note(("x", di), x_row[di], row_of(di, 0))

    names = ["up", "down", "geo", "far"] + [("x", di) for di in others]
    place = {name: i for i, name in enumerate(names)}
    xs = [place["x", di] for di in others]
    plans = [
        [(place["far"], half, half), (0, 0, part), (2, 0, GEO)],
        [(x, 0, half) for x in xs] + [(1, 0, part), (2, 0, GEO)],
        [(x, 0, full) for x in xs] + [(place["far"], 0, full), (0, 0, part), (1, 0, part), (2, 0, GEO)],
    ]

    early_order = ["own", "mate", "far", "up", "down", "geo"] + [("x", di) for di in others]
    early_order += [("two x", di) for di in others] + ["two y", "two m"]
    late_order = [("three x", di) for di in others] + ["three y", "three m"]
    late_order += [("four x", di) for di in others] + ["four y"]

    contents = {}
    for di in others:
        contents["two x", di] = [(("end", di, 2), half)] + side_of("up", di, 0) + [(("geo", di, 0), GEO)]
    contents["two y"] = [(("top", di, 2), half) for di in others] + side_of("down", 0, 2) + [(("geo", 0, 2), GEO)]
    contents["two m"] = sum([row_of(di, 1) for di in others], []) + row_of(0, 3)
    contents["two m"] += side_of("up", 0, 1) + side_of("down", 0, 1) + [(("geo", 0, 1), GEO)]
    for di in others:
        contents["three x", di] = side_of("down", di, 0) + side_of("down", di, 2) + [(("geo", di, 2), GEO)]
    contents["three y"] = side_of("up", 0, 2) + sum([side_of("up", di, 2) for di in others], [])
    contents["three m"] = []
    for di in others:
        contents["three m"] += [(("end", di, 3), half)] + side_of("up", di, 1) + [(("geo", di, 1), GEO)]
    contents["three m"] += [(("top", di, 3), half) for di in others] + side_of("down", 0, 3) + [(("geo", 0, 3), GEO)]
    for di in others:
        contents["four x", di] = side_of("down", di, 1) + side_of("down", di, 3) + [(("geo", di, 3), GEO)]
    contents["four y"] = side_of("up", 0, 3) + sum([side_of("up", di, 3) for di in others], [])
    lengths = {name: sum(rows for _, rows in content) for name, content in contents.items()}
    for name in early_order:
        if name in buffers:
            lengths[name] = buffers[name].shape[0]
    base = {}
    total = 0
    for name in early_order + late_order:
        base[name] = total
        total += lengths[name]
        if name == early_order[-1]:
            late_from = total
    located = dict(at)
    for name, content in contents.items():
        start = 0
        for what, rows in content:
            located[what] = (name, start)
            start += rows
    layout = [
        base[located[kind, di, flip][0]] + located[kind, di, flip][1]
        for kind in ("top", "end", "up", "down")
        for di in range(count)
        for flip in range(n_lay)
    ]
    pairs = slots * (slots + 1) // 2
    entries = 3 * (pairs + UNROLL) + 1
    early_table, late_table, info, spread, own_basis = pl.pallas_call(
        functools.partial(prepare_kernel, axes, count, late_from),
        out_shape=(
            jax.ShapeDtypeStruct((entries,), jnp.int32),
            jax.ShapeDtypeStruct((entries,), jnp.int32),
            jax.ShapeDtypeStruct((slots + 2,), jnp.int32),
            jax.ShapeDtypeStruct((slots, LANES, size), jnp.bfloat16),
            jax.ShapeDtypeStruct((16, size), jnp.bfloat16),
        ),
        in_specs=[SMEM] * 3 + [VMEM],
        out_specs=(SMEM, SMEM, SMEM, VMEM, VMEM),
        scratch_shapes=[pltpu.SMEM((4, slots), jnp.int32), pltpu.SMEM((atoms,), jnp.int32)],
        compiler_params=pltpu.CompilerParams(vmem_limit_bytes=(2 << 20) + atoms * 16384),
        cost_estimate=pl.CostEstimate(flops=1_000_000_000, bytes_accessed=8_000_000, transcendentals=0),
        name="prepare",
    )(
        listings,
        atom_size,
        jnp.array(layout, dtype=jnp.int32),
        basis_proj.transpose(1, 0, 2).reshape(SHELLS * atoms, size),
    )

    two_x, two_y, two_m = pack([buffers[name] for name in names], plans, [own_basis], "pack_two")
    for di in others:
        note(("two x", di), on_row(two_x, di), contents["two x", di])
    note("two y", from_layer(two_y, 2), contents["two y"])
    note("two m", from_layer(two_m, 1), contents["two m"])

    names = ["up", "down", "two y"] + [("two x", di) for di in others]
    place = {name: i for i, name in enumerate(names)}
    y_down = at["down", 0, 2][1]
    x_up = at["up", 1, 0][1]
    xs = [place["two x", di] for di in others]
    plans = [
        [(1, 0, part), (2, y_down, part + GEO)],
        [(0, 0, part)] + [(x, x_up, part) for x in xs],
        [(x, 0, lengths["two x", 1]) for x in xs] + [(2, 0, lengths["two y"])],
    ]
    three_x, three_y, three_m = pack([buffers[name] for name in names], plans, [], "pack_three")
    for di in others:
        note(("three x", di), on_row(three_x, di), contents["three x", di])
    note("three y", from_layer(three_y, 2), contents["three y"])
    note("three m", from_layer(three_m, 1), contents["three m"])

    early_values = [buffers[name] for name in early_order]
    gram = pl.pallas_call(
        functools.partial(gram_kernel, len(early_values)),
        out_shape=jax.ShapeDtypeStruct((full, full), jnp.bfloat16),
        in_specs=[SMEM] + [ANY] * (len(early_values) + 1),
        out_specs=VMEM,
        scratch_shapes=[
            pltpu.VMEM((late_from, LANES), jnp.bfloat16),
            pltpu.SemaphoreType.DMA((len(early_values),)),
        ],
        compiler_params=pltpu.CompilerParams(vmem_limit_bytes=(6 << 20) + late_from * LANES * 2),
        cost_estimate=pl.CostEstimate(flops=1_000_000_000, bytes_accessed=20_000_000, transcendentals=0),
        name="gram_early",
    )(early_table, *early_values, three_x)

    for di in others:
        note(("four x", di), from_layer(buffers["three x", di], 1), contents["four x", di])
    note("four y", from_layer(buffers["three y"], 1), contents["four y"])

    late_values = [buffers[name] for name in late_order]
    sign_next, coef = pl.pallas_call(
        functools.partial(step_kernel, len(late_values)),
        out_shape=(
            jax.ShapeDtypeStruct((slots, size, size), jnp.bfloat16),
            jax.ShapeDtypeStruct((8, LANES), jnp.float32),
        ),
        in_specs=[SMEM, SMEM, VMEM, VMEM, VMEM, VMEM] + [ANY] * len(late_values),
        out_specs=(VMEM, VMEM),
        scratch_shapes=[
            pltpu.VMEM((total - late_from, LANES), jnp.bfloat16),
            pltpu.VMEM((full, full), jnp.bfloat16),
            pltpu.VMEM((size, full), jnp.bfloat16),
            pltpu.VMEM((size, full), jnp.bfloat16),
            pltpu.SemaphoreType.DMA((len(late_values),)),
        ],
        compiler_params=pltpu.CompilerParams(vmem_limit_bytes=(15 << 20) + (total - late_from) * LANES * 2),
        cost_estimate=pl.CostEstimate(flops=1_300_000_000, bytes_accessed=8_000_000, transcendentals=0),
        name="square_cube_coefficients",
    )(late_table, info, own_basis, spread, own, gram, *late_values)

    below = from_offset(coef, "layer", -1)
    above = from_offset(coef, "layer", 1)
    merged = jnp.concatenate(
        [
            coef[:, : 4 * SPAN],
            below[:, SPAN : 3 * SPAN],
            above[:, 3 * SPAN : 4 * SPAN],
            jnp.zeros((8, LANES - 7 * SPAN), jnp.float32),
        ],
        axis=1,
    )
    stacked = jnp.concatenate([merged] + [on_row(merged, di) for di in others], axis=0)
    column_steps = (0, 1, -1)
    received = [stacked] + [from_offset(stacked, "col", dc) for dc in column_steps[1:]]

    tile_steps = [(dr, dc) for dr in steps for dc in column_steps]
    tiles = len(tile_steps)
    used, sources = [], []
    for di in range(count):
        for kind in ("geo", "up geo", "down geo"):
            source = []
            for flip in (0, 1, 3):
                name, start = at[kind, di, flip]
                if name not in used:
                    used.append(name)
                source.append((used.index(name), start))
            sources.append(tuple(source))
    periods = (float(BX * n_row), float(BY * n_col), float(BZ * n_lay))
    plane, line = pl.pallas_call(
        functools.partial(profile_kernel, periods, tile_steps, tuple(sources), len(used)),
        out_shape=(
            jax.ShapeDtypeStruct((tiles, SHELLS, BX * BY, LANES), jnp.bfloat16),
            jax.ShapeDtypeStruct((tiles, SHELLS, LANES, BZ), jnp.bfloat16),
        ),
        in_specs=[ANY] * len(used),
        out_specs=(VMEM, VMEM),
        scratch_shapes=[
            pltpu.VMEM((3 * tiles, GEO, LANES), jnp.bfloat16),
            pltpu.SemaphoreType.DMA((3 * tiles,)),
        ],
        compiler_params=pltpu.CompilerParams(vmem_limit_bytes=10 << 20),
        cost_estimate=pl.CostEstimate(flops=30_000_000, bytes_accessed=4_000_000, transcendentals=2_000_000),
        name="profiles",
    )(*[buffers[name] for name in used])

    density = pl.pallas_call(
        functools.partial(density_kernel, len(column_steps)),
        out_shape=jax.ShapeDtypeStruct((BX * BY, BZ), jnp.float32),
        in_specs=[VMEM] * (len(column_steps) + 2),
        out_specs=VMEM,
        scratch_shapes=[pltpu.VMEM((BX * BY, tiles * SHELLS * LANES), jnp.bfloat16)],
        compiler_params=pltpu.CompilerParams(vmem_limit_bytes=16 << 20),
        cost_estimate=pl.CostEstimate(flops=310_000_000, bytes_accessed=4_000_000, transcendentals=0),
        name="density",
    )(*received, plane, line.reshape(tiles * SHELLS * LANES, BZ))
    return sign_next[None], density.reshape(BX, BY, BZ)


def solution(mesh):
    rows = P(("row", "col", "layer"), None, None, None)
    in_specs = (rows, P(), P(), P(), P(("row", "col", "layer"), None), P(), P(), P())
    out_specs = (rows, P("row", "col", "layer"))
    return jax.shard_map(local, mesh=mesh, in_specs=in_specs, out_specs=out_specs, check_vma=False)
```

time: 113 us -> 77 us (0.68)
  starting transfers between devices: 42.3 us -> 16.3 us
  local copies, waits for them, and re-layouts: 20.3 us -> 7.3 us
  waiting for transfers between devices: 25 us -> 27.5 us
  Pallas kernels: 23.2 us -> 24.5 us
    ppermute x17 -> x10, starting transfers between devices: 25.3 us -> 12.1 us  [from_offset(): lax.ppermute(x, axis, [((i + step) % count, i) for i in range(count)])]
    unnamed x54 -> x22, local copies, waits for them, and re-layouts: 19.3 us -> 7.15 us
    ppermute x17 -> x10, waiting for transfers between devices: 14.4 us -> 26.1 us  [from_offset(): lax.ppermute(x, axis, [((i + step) % count, i) for i in range(count)])]
    ppermute x4 -> x0, starting transfers between devices: 8.48 us -> none  [to_tiles(): received.append(lax.ppermute(merged, ('row', 'col'), moves))]
    ppermute x18 -> x8, waiting for transfers between devices: 7.09 us -> 1.39 us  [from_layer(): return lax.ppermute(x, 'layer', [(i ^ flip, i) for i in range(count)])]
    ppermute x18 -> x8, starting transfers between devices: 8.53 us -> 4.2 us  [from_layer(): return lax.ppermute(x, 'layer', [(i ^ flip, i) for i in range(count)])]
    ppermute x4 -> x0, waiting for transfers between devices: 3.47 us -> none  [to_tiles(): received.append(lax.ppermute(merged, ('row', 'col'), moves))]
    pallas_call x5 -> x8, Pallas kernels: 23.2 us -> 24.5 us  [the longest x1 5.92 us: local(): pl.pallas_call(functools.partial(prepare_kernel, axes, count, late_from),...]
  transfers between devices with their start and end apart: 39 -> 18, of which waited for: 10 -> 8; matrix products, arithmetic and copies ran while one was open for 2% -> 0% of each run, Pallas kernels for 18% -> 20%
where the time goes in v3:
time: 77 us; the launch traced here: 76.6 us
  waiting for transfers between devices  27.5 us (36%)
  Pallas kernels  24.5 us (32%)
  starting transfers between devices  16.3 us (21%)
  local copies, waits for them, and re-layouts  7.3 us (9%)
  between operations  0.8 us (1%)
    ppermute x10, waiting for transfers between devices, from_offset(): lax.ppermute(x, axis, [((i + step) % count, i) for i in range(count)])  26.1 us
    ppermute x10, starting transfers between devices, from_offset(): lax.ppermute(x, axis, [((i + step) % count, i) for i in range(count)])  12.1 us
    unnamed x22, local copies, waits for them, and re-layouts  7.15 us
    pallas_call x1, Pallas kernels, local(): pl.pallas_call(functools.partial(prepare_kernel, axes, count, late_from),...  5.92 us
    pallas_call x1, Pallas kernels, local(): pl.pallas_call(functools.partial(step_kernel, len(late_values)), out_shap...  5.75 us
    ppermute x8, starting transfers between devices, from_layer(): return lax.ppermute(x, 'layer', [(i ^ flip, i) for i in range(count)])  4.2 us
    pallas_call x1, Pallas kernels, local(): pl.pallas_call(functools.partial(profile_kernel, periods, tile_steps, tup...  3.67 us
    pallas_call x1, Pallas kernels, local(): pl.pallas_call(functools.partial(gram_kernel, len(early_values)), out_sha...  3.63 us
  transfers between devices with their start and end apart: 18, of which 8 were waited for; matrix products, arithmetic and copies ran while one was open for 0% of the time, Pallas kernels for 20%

profile of v3, /device:TPU:0, one launch (start us, length us, event | category | flops | bytes accessed | tf_op | source)
XLA Modules:
  0.0 76.6 jit_solution(14262169226254454284)
XLA Ops:
  0.6 3.0 %collective-permute-start.1 = (bf16[1536,128]{1,0:T(8,128)(2,1)}, bf16[1536,128]{1,0:T(8,128)(2,1)S(1)}, u32[]{:S(2)}, u32[]{:S(2)}) collective-permute-start(bf16[1536,128]{1,0:T(8,128)(2,1)} %bitcast.10), channel_id=1, source_target_pairs={{2,0},{3,1},{0,2},{1,3},{6,4},{7,5},{4,6},{5,7},{10,8},{11,9},{8,1... | collective-permute-start | bytes 1179656 | tf_op jit(solution)/shard_map/ppermute | solution.py:30
  3.7 1.5 %collective-permute-start.4 = (bf16[1536,128]{1,0:T(8,128)(2,1)}, bf16[1536,128]{1,0:T(8,128)(2,1)S(1)}, u32[]{:S(2)}, u32[]{:S(2)}) collective-permute-start(bf16[1536,128]{1,0:T(8,128)(2,1)} %bitcast.11), channel_id=1, source_target_pairs={{16,0},{0,16},{17,1},{1,17},{18,2},{2,18},{19,3},{3,19},{20,4},{4,... | collective-permute-start | bytes 1179656 | tf_op jit(solution)/shard_map/ppermute | solution.py:25
  5.2 0.0 copy-start
  5.2 1.0 %copy-done = bf16[1,12,128,128]{3,2,1,0:T(8,128)(2,1)S(1)} copy-done((bf16[1,12,128,128]{3,2,1,0:T(8,128)(2,1)S(1)}, bf16[1,12,128,128]{3,2,1,0:T(8,128)(2,1)}, u32[]{:S(2)}) %copy-start) | copy-done | bytes 393240
  6.2 0.0 copy-start.2
  6.2 0.7 copy-done.2
  6.9 0.0 copy-start.4
  6.9 0.7 copy-done.4
  7.5 0.0 copy-start.5
  7.5 0.7 copy-done.5
  8.2 0.7 copy-done.6
  8.9 0.7 copy-done.7
  9.5 1.0 %pick_column_blocks.1 = (bf16[656,128]{1,0:T(8,128)(2,1)S(1)}, bf16[16,128]{1,0:T(8,128)(2,1)S(1)}) custom-call(s32[12,32]{1,0:T(8,128)S(1)} %bitcast.19, s32[1,12]{1,0:T(1,128)S(1)} %copy-done.4, s32[32]{0:T(128)S(1)} %copy-done.5, s32[32]{0:T(128)S(1)} %copy-done.6, s32[32]{0:T(128)S(1)} %copy-done.7, bf16[12,128,128]{2,1,0:T(8,128)(2,1)S(1)} %bitcast.12), custom_call_target="tpu_custom_call" | custom-call | tf_op jit(solution)/shard_map/pick_column_blocks/pallas_call | solution.py:418
  10.5 3.7 %collective-permute-start.2 = (bf16[656,128]{1,0:T(8,128)(2,1)S(1)}, bf16[656,128]{1,0:T(8,128)(2,1)S(1)}, u32[]{:S(2)}, u32[]{:S(2)}) collective-permute-start(bf16[656,128]{1,0:T(8,128)(2,1)S(1)} %get-tuple-element.24), channel_id=1, source_target_pairs={{4,0},{8,4},{12,8},{0,12},{5,1},{9,5},{13,9},{1,13},{6,2},{10,6},{... | collective-permute-start | bytes 503816 | tf_op jit(solution)/shard_map/ppermute | solution.py:25
  14.2 0.0 collective-permute-start.3
  14.2 0.7 copy-done.3
  14.9 0.8 %copy-done.8 = bf16[32,6,128]{2,0,1:T(8,128)(2,1)S(1)} copy-done((bf16[32,6,128]{2,0,1:T(8,128)(2,1)S(1)}, bf16[32,6,128]{2,0,1:T(8,128)(2,1)}, u32[]{:S(2)}) %copy-start.8) | copy-done | bytes 49176
  15.7 0.7 copy-done.9
  16.3 0.7 copy-done.10
  17.0 5.9 %prepare.1 = (s32[247]{0:T(256)S(1)}, s32[247]{0:T(256)S(1)}, s32[14]{0:T(128)S(1)}, bf16[12,128,128]{2,1,0:T(8,128)(2,1)S(1)}, bf16[16,128]{1,0:T(8,128)(2,1)S(1)}) custom-call(s32[12,32]{1,0:T(8,128)S(1)} %bitcast.20, s32[32]{0:T(128)S(1)} %copy-done.9, s32[32]{0:T(128)S(1)} %copy-done.10, bf16[192,128]{1,0:T(8,128)(2,1)S(1)} %bitcast.21), custom_call_target="tpu_custom_call" | custom-call | flops 1000000000 | bytes 8000000 | tf_op jit(solution)/shard_map/prepare/pallas_call | solution.py:514
  22.9 0.0 copy-start.1
  22.9 0.0 collective-permute-done.2.refs_0_.refs_4_.refs_3_
  22.9 0.0 collective-permute-done.3.refs_1_.refs_5_
  22.9 0.0 collective-permute-done.1.refs_3_
  23.0 0.0 collective-permute-done.4.refs_4_.refs_7_
  23.0 1.9 %pack_two.1 = (bf16[1440,128]{1,0:T(8,128)(2,1)S(1)}, bf16[1440,128]{1,0:T(8,128)(2,1)S(1)}, bf16[4400,128]{1,0:T(8,128)(2,1)S(1)}) custom-call(bf16[656,128]{1,0:T(8,128)(2,1)S(1)} %collective-permute-done.2.refs_0_.refs_4_.refs_3_, bf16[656,128]{1,0:T(8,128)(2,1)S(1)} %collective-permute-done.3.refs_1_.refs_5_, ...), custom_call_target="tpu_custom_call" | custom-call | bytes 3000000 | tf_op jit(solution)/shard_map/pack_two/pallas_call | solution.py:214
  24.9 0.1 collective-permute-start.7
  24.9 0.6 collective-permute-start.5
  25.5 0.5 collective-permute-start.6
  26.0 9.9 %collective-permute-done.5.refs_3_.refs_8_.refs_6_ = bf16[1440,128]{1,0:T(8,128)(2,1)S(1)} collective-permute-done((bf16[1440,128]{1,0:T(8,128)(2,1)S(1)}, bf16[1440,128]{1,0:T(8,128)(2,1)S(1)}, u32[]{:S(2)}, u32[]{:S(2)}) %collective-permute-start.5) | collective-permute-done | bytes 368672 | tf_op jit(solution)/shard_map/ppermute | solution.py:25
  35.9 0.3 collective-permute-done.6.refs_2_.refs_9_
  36.2 1.2 %pack_three.1 = (bf16[1328,128]{1,0:T(8,128)(2,1)S(1)}, bf16[1312,128]{1,0:T(8,128)(2,1)S(1)}, bf16[2880,128]{1,0:T(8,128)(2,1)S(1)}) custom-call(bf16[656,128]{1,0:T(8,128)(2,1)S(1)} %collective-permute-done.2.refs_0_.refs_4_.refs_3_, bf16[656,128]{1,0:T(8,128)(2,1)S(1)} %collective-permute-done.3.refs_1_.refs_5_, ...), custom_call_target="tpu_custom_call" | custom-call | bytes 3000000 | tf_op jit(solution)/shard_map/pack_three/pallas_call | solution.py:214
  37.4 0.1 collective-permute-start.10
  37.5 1.6 %collective-permute-start.8 = (bf16[1328,128]{1,0:T(8,128)(2,1)S(1)}, bf16[1328,128]{1,0:T(8,128)(2,1)S(1)}, u32[]{:S(2)}, u32[]{:S(2)}) collective-permute-start(bf16[1328,128]{1,0:T(8,128)(2,1)S(1)} %get-tuple-element.29.refs_11_), channel_id=1, source_target_pairs={{16,0},{0,16},{17,1},{1,17},{18,2},{2,18},{19,3},{3,19},{20,4},{4,... | collective-permute-start | bytes 1019912 | tf_op jit(solution)/shard_map/ppermute | solution.py:25
  39.0 0.5 collective-permute-start.9
  39.6 0.0 copy-done.1
  39.6 0.0 collective-permute-start
  39.6 8.3 %collective-permute-done.8.refs_6_.refs_8_ = bf16[1328,128]{1,0:T(8,128)(2,1)S(1)} collective-permute-done((bf16[1328,128]{1,0:T(8,128)(2,1)S(1)}, bf16[1328,128]{1,0:T(8,128)(2,1)S(1)}, u32[]{:S(2)}, u32[]{:S(2)}) %collective-permute-start.8) | collective-permute-done | bytes 340000 | tf_op jit(solution)/shard_map/ppermute | solution.py:25
  47.9 0.0 collective-permute-start.11
  47.9 1.1 %collective-permute-done.9.refs_7_ = bf16[1312,128]{1,0:T(8,128)(2,1)S(1)} collective-permute-done((bf16[1312,128]{1,0:T(8,128)(2,1)S(1)}, bf16[1312,128]{1,0:T(8,128)(2,1)S(1)}, u32[]{:S(2)}, u32[]{:S(2)}) %collective-permute-start.9) | collective-permute-done | bytes 335904 | tf_op jit(solution)/shard_map/ppermute | solution.py:30
  49.0 0.0 collective-permute-start.12
  49.0 0.0 collective-permute-done.refs_2_
  49.0 0.0 collective-permute-done.7.refs_10_.refs_1_
  49.0 3.6 %gram_early.1.refs_5_ = bf16[1536,1536]{1,0:T(8,128)(2,1)S(1)} custom-call(s32[247]{0:T(256)S(1)} %get-tuple-element.23.refs_0_, bf16[1536,128]{1,0:T(8,128)(2,1)S(1)} %bitcast.14, bf16[1536,128]{1,0:T(8,128)(2,1)S(1)} %collective-permute-done.refs_2_, bf16[1536,128]{1,0:T(8,128)(2,1)S(1)} %collective-permute-done.1.refs_3_, ...), custom_call_target="tpu_custom_call" | custom-call | flops 1000000000 | bytes 20000000 | tf_op jit(solution)/shard_map/gram_early/pallas_call | solution.py:559
  52.7 0.0 collective-permute-done.12.refs_10_.refs_4_
  52.7 0.0 collective-permute-done.11.refs_9_.refs_7_
  52.7 0.0 collective-permute-done.10.refs_8_.refs_2_
  52.7 5.7 %square_cube_coefficients.1 = (bf16[12,128,128]{2,1,0:T(8,128)(2,1)}, f32[8,128]{1,0:T(8,128)S(1)}) custom-call(s32[247]{0:T(256)S(1)} %get-tuple-element.19.refs_0_, s32[14]{0:T(128)S(1)} %get-tuple-element.20.refs_1_, bf16[16,128]{1,0:T(8,128)(2,1)S(1)} %get-tuple-element.21.refs_5_.refs_2_, bf16[12,128,128]{2,1,0:T(8,128)(2,1)S(1)} %get-tuple-element.22.refs_3_, ...), custom_call_target="tpu_custom_call" | custom-call | flops 1300000000 | bytes 8000000 | tf_op jit(solution)/shard_map/square_cube_coefficients/pallas_call | solution.py:578
  58.4 0.7 collective-permute-start.14
  59.1 0.0 collective-permute-start.13
  59.1 1.3 %collective-permute-done.14 = f32[8,128]{1,0:T(8,128)S(1)} collective-permute-done((f32[8,128]{1,0:T(8,128)S(1)}, f32[8,128]{1,0:T(8,128)S(1)}, u32[]{:S(2)}, u32[]{:S(2)}) %collective-permute-start.14) | collective-permute-done | bytes 4128 | tf_op jit(solution)/shard_map/ppermute | solution.py:25
  60.4 0.1 slice.11
  60.5 1.6 %collective-permute-done.13 = f32[8,128]{1,0:T(8,128)S(1)} collective-permute-done((f32[8,128]{1,0:T(8,128)S(1)}, f32[8,128]{1,0:T(8,128)S(1)}, u32[]{:S(2)}, u32[]{:S(2)}) %collective-permute-start.13) | collective-permute-done | bytes 4128 | tf_op jit(solution)/shard_map/ppermute | solution.py:25
  62.1 0.1 slice.10
  62.2 0.1 pad_maximum_fusion.1
  62.3 0.4 collective-permute-start.15
  62.7 3.2 %collective-permute-done.15 = f32[8,128]{1,0:T(8,128)S(1)} collective-permute-done((f32[8,128]{1,0:T(8,128)S(1)}, f32[8,128]{1,0:T(8,128)S(1)}, u32[]{:S(2)}, u32[]{:S(2)}) %collective-permute-start.15) | collective-permute-done | bytes 4128 | tf_op jit(solution)/shard_map/ppermute | solution.py:25
  65.9 0.1 pad_maximum_fusion.refs_0_
  66.0 3.7 %collective-permute-start.16 = (f32[16,128]{1,0:T(8,128)S(1)}, f32[16,128]{1,0:T(8,128)S(1)}, u32[]{:S(2)}, u32[]{:S(2)}) collective-permute-start(f32[16,128]{1,0:T(8,128)S(1)} %pad_maximum_fusion.refs_0_), channel_id=1, source_target_pairs={{4,0},{8,4},{12,8},{0,12},{5,1},{9,5},{13,9},{1,13},{6,2},{10,6},{... | collective-permute-start | bytes 24584 | tf_op jit(solution)/shard_map/ppermute | solution.py:25
  69.7 0.0 collective-permute-start.17
  69.7 3.7 %profiles.1 = (bf16[6,6,256,128]{3,2,1,0:T(8,128)(2,1)S(1)}, bf16[6,6,128,128]{3,2,1,0:T(8,128)(2,1)S(1)}) custom-call(bf16[16,128]{1,0:T(8,128)(2,1)S(1)} %get-tuple-element.25.refs_2_.refs_6_.refs_0_, bf16[4400,128]{1,0:T(8,128)(2,1)S(1)} %collective-permute-done.7.refs_10_.refs_1_, bf16[2880,128]{1,0:T(8,128)(2,1)S(1)} %collective-permute-done.10.refs_8_.refs_2_, ...), custom_call_target="tpu_custom_call" | custom-call | flops 30000000 | bytes 4000000 | tf_op jit(solution)/shard_map/profiles/pallas_call | solution.py:626
  73.4 0.0 collective-permute-done.16.refs_1_
  73.4 1.8 %collective-permute-done.17.refs_2_ = f32[16,128]{1,0:T(8,128)S(1)} collective-permute-done((f32[16,128]{1,0:T(8,128)S(1)}, f32[16,128]{1,0:T(8,128)S(1)}, u32[]{:S(2)}, u32[]{:S(2)}) %collective-permute-start.17) | collective-permute-done | bytes 8224 | tf_op jit(solution)/shard_map/ppermute | solution.py:25
  75.2 1.5 %density.1 = f32[256,128]{1,0:T(8,128)} custom-call(f32[16,128]{1,0:T(8,128)S(1)} %pad_maximum_fusion.refs_0_, f32[16,128]{1,0:T(8,128)S(1)} %collective-permute-done.16.refs_1_, f32[16,128]{1,0:T(8,128)S(1)} %collective-permute-done.17.refs_2_, bf16[6,6,256,128]{3,2,1,0:T(8,128)(2,1)S(1)} %get-tuple-element.34.refs_3_, bf16[4608,128]{1,0:T(8,128)(2,1)S(1)} %bitcast.16), custom_call_target="tpu_custom_call" | custom-call | flops 310000000 | bytes 4000000 | tf_op jit(solution)/shard_map/density/pallas_call | solution.py:643
  (7 shorter events, 0.0 us)
Async XLA Ops:
  0.6 22.3 %collective-permute-start.1 = (bf16[1536,128]{1,0:T(8,128)(2,1)}, bf16[1536,128]{1,0:T(8,128)(2,1)S(1)}, u32[]{:S(2)}, u32[]{:S(2)}) collective-permute-start(bf16[1536,128]{1,0:T(8,128)(2,1)} %bitcast.10), channel_id=1, source_target_pairs={{2,0},{3,1},{0,2},{1,3},{6,4},{7,5},{4,6},{5,7},{10,8},{11,9},{8,1... | collective-permute-start | bytes 1179656 | tf_op jit(solution)/shard_map/ppermute | solution.py:30
  3.7 19.3 %collective-permute-start.4 = (bf16[1536,128]{1,0:T(8,128)(2,1)}, bf16[1536,128]{1,0:T(8,128)(2,1)S(1)}, u32[]{:S(2)}, u32[]{:S(2)}) collective-permute-start(bf16[1536,128]{1,0:T(8,128)(2,1)} %bitcast.11), channel_id=1, source_target_pairs={{16,0},{0,16},{17,1},{1,17},{18,2},{2,18},{19,3},{3,19},{20,4},{4,... | collective-permute-start | bytes 1179656 | tf_op jit(solution)/shard_map/ppermute | solution.py:25
  5.2 1.0 %copy-start = (bf16[1,12,128,128]{3,2,1,0:T(8,128)(2,1)S(1)}, bf16[1,12,128,128]{3,2,1,0:T(8,128)(2,1)}, u32[]{:S(2)}) copy-start(bf16[1,12,128,128]{3,2,1,0:T(8,128)(2,1)} %param.9) | copy-start | bytes 1179652
  6.2 0.7 copy-start.2
  6.9 0.7 copy-start.4
  7.5 0.7 copy-start.5
  8.2 0.7 copy-start.6
  8.8 0.7 copy-start.7
  10.5 12.4 %collective-permute-start.2 = (bf16[656,128]{1,0:T(8,128)(2,1)S(1)}, bf16[656,128]{1,0:T(8,128)(2,1)S(1)}, u32[]{:S(2)}, u32[]{:S(2)}) collective-permute-start(bf16[656,128]{1,0:T(8,128)(2,1)S(1)} %get-tuple-element.24), channel_id=1, source_target_pairs={{4,0},{8,4},{12,8},{0,12},{5,1},{9,5},{13,9},{1,13},{6,2},{10,6},{... | collective-permute-start | bytes 503816 | tf_op jit(solution)/shard_map/ppermute | solution.py:25
  14.2 8.8 %collective-permute-start.3 = (bf16[656,128]{1,0:T(8,128)(2,1)S(1)}, bf16[656,128]{1,0:T(8,128)(2,1)S(1)}, u32[]{:S(2)}, u32[]{:S(2)}) collective-permute-start(bf16[656,128]{1,0:T(8,128)(2,1)S(1)} %get-tuple-element.24), channel_id=1, source_target_pairs={{12,0},{0,4},{4,8},{8,12},{13,1},{1,5},{5,9},{9,13},{14,2},{2,6},{... | collective-permute-start | bytes 503816 | tf_op jit(solution)/shard_map/ppermute | solution.py:25
  14.2 0.7 copy-start.3
  14.9 0.8 %copy-start.8 = (bf16[32,6,128]{2,0,1:T(8,128)(2,1)S(1)}, bf16[32,6,128]{2,0,1:T(8,128)(2,1)}, u32[]{:S(2)}) copy-start(bf16[32,6,128]{2,0,1:T(8,128)(2,1)} %param.12) | copy-start | bytes 147460
  15.7 0.7 copy-start.9
  16.3 0.7 copy-start.10
  22.9 16.6 %copy-start.1 = (bf16[1,12,128,128]{3,2,1,0:T(8,128)(2,1)S(1)}, bf16[1,12,128,128]{3,2,1,0:T(8,128)(2,1)}, u32[]{:S(2)}) copy-start(bf16[1,12,128,128]{3,2,1,0:T(8,128)(2,1)} %param.9) | copy-start | bytes 1179652
  24.9 24.2 %collective-permute-start.7 = (bf16[4400,128]{1,0:T(8,128)(2,1)S(1)}, bf16[4400,128]{1,0:T(8,128)(2,1)S(1)}, u32[]{:S(2)}, u32[]{:S(2)}) collective-permute-start(bf16[4400,128]{1,0:T(8,128)(2,1)S(1)} %get-tuple-element.28), channel_id=1, source_target_pairs={{1,0},{0,1},{3,2},{2,3},{5,4},{4,5},{7,6},{6,7},{9,8},{8,9},{11,10... | collective-permute-start | bytes 3379208 | tf_op jit(solution)/shard_map/ppermute | solution.py:30
  24.9 11.0 %collective-permute-start.5 = (bf16[1440,128]{1,0:T(8,128)(2,1)S(1)}, bf16[1440,128]{1,0:T(8,128)(2,1)S(1)}, u32[]{:S(2)}, u32[]{:S(2)}) collective-permute-start(bf16[1440,128]{1,0:T(8,128)(2,1)S(1)} %get-tuple-element.26), channel_id=1, source_target_pairs={{16,0},{0,16},{17,1},{1,17},{18,2},{2,18},{19,3},{3,19},{20,4},{4,... | collective-permute-start | bytes 1105928 | tf_op jit(solution)/shard_map/ppermute | solution.py:25
  25.5 10.7 %collective-permute-start.6 = (bf16[1440,128]{1,0:T(8,128)(2,1)S(1)}, bf16[1440,128]{1,0:T(8,128)(2,1)S(1)}, u32[]{:S(2)}, u32[]{:S(2)}) collective-permute-start(bf16[1440,128]{1,0:T(8,128)(2,1)S(1)} %get-tuple-element.27), channel_id=1, source_target_pairs={{2,0},{3,1},{0,2},{1,3},{6,4},{7,5},{4,6},{5,7},{10,8},{11,9},{8,1... | collective-permute-start | bytes 1105928 | tf_op jit(solution)/shard_map/ppermute | solution.py:30
  37.4 15.3 %collective-permute-start.10 = (bf16[2880,128]{1,0:T(8,128)(2,1)S(1)}, bf16[2880,128]{1,0:T(8,128)(2,1)S(1)}, u32[]{:S(2)}, u32[]{:S(2)}) collective-permute-start(bf16[2880,128]{1,0:T(8,128)(2,1)S(1)} %get-tuple-element.31), channel_id=1, source_target_pairs={{1,0},{0,1},{3,2},{2,3},{5,4},{4,5},{7,6},{6,7},{9,8},{8,9},{11,10... | collective-permute-start | bytes 2211848 | tf_op jit(solution)/shard_map/ppermute | solution.py:30
  37.5 10.4 %collective-permute-start.8 = (bf16[1328,128]{1,0:T(8,128)(2,1)S(1)}, bf16[1328,128]{1,0:T(8,128)(2,1)S(1)}, u32[]{:S(2)}, u32[]{:S(2)}) collective-permute-start(bf16[1328,128]{1,0:T(8,128)(2,1)S(1)} %get-tuple-element.29.refs_11_), channel_id=1, source_target_pairs={{16,0},{0,16},{17,1},{1,17},{18,2},{2,18},{19,3},{3,19},{20,4},{4,... | collective-permute-start | bytes 1019912 | tf_op jit(solution)/shard_map/ppermute | solution.py:25
  39.0 10.0 %collective-permute-start.9 = (bf16[1312,128]{1,0:T(8,128)(2,1)S(1)}, bf16[1312,128]{1,0:T(8,128)(2,1)S(1)}, u32[]{:S(2)}, u32[]{:S(2)}) collective-permute-start(bf16[1312,128]{1,0:T(8,128)(2,1)S(1)} %get-tuple-element.30), channel_id=1, source_target_pairs={{2,0},{3,1},{0,2},{1,3},{6,4},{7,5},{4,6},{5,7},{10,8},{11,9},{8,1... | collective-permute-start | bytes 1007624 | tf_op jit(solution)/shard_map/ppermute | solution.py:30
  39.6 9.5 %collective-permute-start = (bf16[1536,128]{1,0:T(8,128)(2,1)S(1)}, bf16[1536,128]{1,0:T(8,128)(2,1)S(1)}, u32[]{:S(2)}, u32[]{:S(2)}) collective-permute-start(bf16[1536,128]{1,0:T(8,128)(2,1)S(1)} %bitcast.13), channel_id=1, source_target_pairs={{1,0},{0,1},{3,2},{2,3},{5,4},{4,5},{7,6},{6,7},{9,8},{8,9},{11,10... | collective-permute-start | bytes 1179656 | tf_op jit(solution)/shard_map/ppermute | solution.py:30
  47.9 4.8 %collective-permute-start.11 = (bf16[1328,128]{1,0:T(8,128)(2,1)S(1)}, bf16[1328,128]{1,0:T(8,128)(2,1)S(1)}, u32[]{:S(2)}, u32[]{:S(2)}) collective-permute-start(bf16[1328,128]{1,0:T(8,128)(2,1)S(1)} %collective-permute-done.8.refs_6_.refs_8_), channel_id=1, source_target_pairs={{1,0},{0,1},{3,2},{2,3},{5,4},{4,5},{7,6},{6,7},{9,8},{8,9},{11,10... | collective-permute-start | bytes 1019912 | tf_op jit(solution)/shard_map/ppermute | solution.py:30
  49.0 3.6 %collective-permute-start.12 = (bf16[1312,128]{1,0:T(8,128)(2,1)S(1)}, bf16[1312,128]{1,0:T(8,128)(2,1)S(1)}, u32[]{:S(2)}, u32[]{:S(2)}) collective-permute-start(bf16[1312,128]{1,0:T(8,128)(2,1)S(1)} %collective-permute-done.9.refs_7_), channel_id=1, source_target_pairs={{1,0},{0,1},{3,2},{2,3},{5,4},{4,5},{7,6},{6,7},{9,8},{8,9},{11,10... | collective-permute-start | bytes 1007624 | tf_op jit(solution)/shard_map/ppermute | solution.py:30
  58.4 2.0 %collective-permute-start.14 = (f32[8,128]{1,0:T(8,128)S(1)}, f32[8,128]{1,0:T(8,128)S(1)}, u32[]{:S(2)}, u32[]{:S(2)}) collective-permute-start(f32[8,128]{1,0:T(8,128)S(1)} %get-tuple-element.33), channel_id=1, source_target_pairs={{1,0},{2,1},{3,2},{0,3},{5,4},{6,5},{7,6},{4,7},{9,8},{10,9},{11,1... | collective-permute-start | bytes 12296 | tf_op jit(solution)/shard_map/ppermute | solution.py:25
  59.1 3.0 %collective-permute-start.13 = (f32[8,128]{1,0:T(8,128)S(1)}, f32[8,128]{1,0:T(8,128)S(1)}, u32[]{:S(2)}, u32[]{:S(2)}) collective-permute-start(f32[8,128]{1,0:T(8,128)S(1)} %get-tuple-element.33), channel_id=1, source_target_pairs={{3,0},{0,1},{1,2},{2,3},{7,4},{4,5},{5,6},{6,7},{11,8},{8,9},{9,10... | collective-permute-start | bytes 12296 | tf_op jit(solution)/shard_map/ppermute | solution.py:25
  62.3 3.6 %collective-permute-start.15 = (f32[8,128]{1,0:T(8,128)S(1)}, f32[8,128]{1,0:T(8,128)S(1)}, u32[]{:S(2)}, u32[]{:S(2)}) collective-permute-start(f32[8,128]{1,0:T(8,128)S(1)} %pad_maximum_fusion.1), channel_id=1, source_target_pairs={{16,0},{0,16},{17,1},{1,17},{18,2},{2,18},{19,3},{3,19},{20,4},{4,... | collective-permute-start | bytes 12296 | tf_op jit(solution)/shard_map/ppermute | solution.py:25
  66.0 7.4 %collective-permute-start.16 = (f32[16,128]{1,0:T(8,128)S(1)}, f32[16,128]{1,0:T(8,128)S(1)}, u32[]{:S(2)}, u32[]{:S(2)}) collective-permute-start(f32[16,128]{1,0:T(8,128)S(1)} %pad_maximum_fusion.refs_0_), channel_id=1, source_target_pairs={{4,0},{8,4},{12,8},{0,12},{5,1},{9,5},{13,9},{1,13},{6,2},{10,6},{... | collective-permute-start | bytes 24584 | tf_op jit(solution)/shard_map/ppermute | solution.py:25
  69.7 5.4 %collective-permute-start.17 = (f32[16,128]{1,0:T(8,128)S(1)}, f32[16,128]{1,0:T(8,128)S(1)}, u32[]{:S(2)}, u32[]{:S(2)}) collective-permute-start(f32[16,128]{1,0:T(8,128)S(1)} %pad_maximum_fusion.refs_0_), channel_id=1, source_target_pairs={{12,0},{0,4},{4,8},{8,12},{13,1},{1,5},{5,9},{9,13},{14,2},{2,6},{... | collective-permute-start | bytes 24584 | tf_op jit(solution)/shard_map/ppermute | solution.py:25

commit v4 on v3

--- a/solution.py
+++ b/solution.py
@@ -18,6 +18,7 @@
 VMEM = pl.BlockSpec(memory_space=pltpu.VMEM)
 SMEM = pl.BlockSpec(memory_space=pltpu.SMEM)
 ANY = pl.BlockSpec(memory_space=pl.ANY)
+HBM = pl.BlockSpec(memory_space=pltpu.HBM)
 
 
 def from_offset(x, axis, step):
@@ -62,11 +63,11 @@
         )
 
 
-def own_ranks(at, neighbors_ref):
+def own_ranks(at, ints_ref):
     seen = [jnp.int32(0)] * at.n_lay
     listed = []
-    for w in range(neighbors_ref.shape[0]):
-        atom = neighbors_ref[w, at.me]
+    for w in range(ints_ref.shape[0] - 5):
+        atom = ints_ref[w, at.me]
         step_lay = (atom - at.lay) & (at.n_lay - 1)
         rank = jnp.int32(0)
         for k in range(at.n_lay):
@@ -76,44 +77,52 @@
     return listed
 
 
-def pick_kernel(axes, *refs):
-    neighbors_ref, extent_ref, x_ref, y_ref, z_ref, sign_ref, out_ref, geo_ref, place_ref = refs
+def pick_kernel(axes, ints_ref, sign_ref, out_ref, geo_ref, place_ref, sems):
     at = Places(*axes)
+    slots = sign_ref.shape[0]
     n_pick = place_ref.shape[0] - 1
     size = sign_ref.shape[1]
+    for i in range(n_pick + 1):
+        place_ref[i] = 0
+    ranks = own_ranks(at, ints_ref)
+    for w, (atom, _) in enumerate(ranks):
+        row, col, lay = at.split(atom)
+        place = target_place(at.n_row, (row - at.row) & (at.n_row - 1), (lay - at.lay) & (at.n_lay - 1), at.row)
+        place_ref[jnp.where((col == at.col) & (place >= 0), place, n_pick)] = w
+    copies = []
+    for i in range(n_pick):
+        copy = pltpu.make_async_copy(sign_ref.at[place_ref[i]], out_ref.at[pl.ds(i * size, size)], sems.at[i])
+        copy.start()
+        copies.append(copy)
     sub = lax.broadcasted_iota(jnp.int32, (GEO, LANES), 0)
     lane_pair = lax.broadcasted_iota(jnp.int32, (GEO, LANES), 1) // SHELLS
     geo = jnp.zeros((GEO, LANES), jnp.int32)
-    for i in range(n_pick + 1):
-        place_ref[i] = 0
-    for w, (atom, rank) in enumerate(own_ranks(at, neighbors_ref)):
+    for w, (atom, rank) in enumerate(ranks):
         row, col, lay = at.split(atom)
-        step_row = (row - at.row) & (at.n_row - 1)
-        step_col = (col - at.col) & (at.n_col - 1)
-        step_lay = (lay - at.lay) & (at.n_lay - 1)
-        place = target_place(at.n_row, step_row, step_lay, at.row)
-        place_ref[jnp.where((step_col == 0) & (place >= 0), place, n_pick)] = w
-        go_row = ((step_row + 1) & (at.n_row - 1)) - 1
-        go_col = ((step_col + 1) & (at.n_col - 1)) - 1
-        go_lay = jnp.minimum(((step_lay + 1) & (at.n_lay - 1)) - 1, 1)
-        twice_x = x_ref[at.me] + x_ref[atom] + BX * go_row
-        twice_y = y_ref[at.me] + y_ref[atom] + BY * go_col
-        twice_z = z_ref[at.me] + z_ref[atom] + BZ * go_lay - BZ
-        values = jnp.where(sub == 0, twice_x, jnp.where(sub == 1, twice_y, jnp.where(sub == 2, twice_z, extent_ref[0, w])))
+        go_row = ((row - at.row + 1) & (at.n_row - 1)) - 1
+        go_col = ((col - at.col + 1) & (at.n_col - 1)) - 1
+        go_lay = jnp.minimum(((lay - at.lay + 1) & (at.n_lay - 1)) - 1, 1)
+        twice_x = ints_ref[slots + 1, at.me] + ints_ref[slots + 1, atom] + BX * go_row
+        twice_y = ints_ref[slots + 2, at.me] + ints_ref[slots + 2, atom] + BY * go_col
+        twice_z = ints_ref[slots + 3, at.me] + ints_ref[slots + 3, atom] + BZ * go_lay - BZ
+        extent = ints_ref[slots + 4, w]
+        values = jnp.where(sub == 0, twice_x, jnp.where(sub == 1, twice_y, jnp.where(sub == 2, twice_z, extent)))
         geo = jnp.where(lane_pair == rank, values, geo)
     geo = geo.astype(jnp.float32).astype(geo_ref.dtype)
     geo_ref[...] = geo
     out_ref[n_pick * size : n_pick * size + GEO] = geo
-    for i in range(n_pick):
-        out_ref[i * size : (i + 1) * size] = sign_ref[place_ref[i]]
-
-
-def prepare_kernel(axes, count, late_from, *refs):
-    neighbors_ref, size_ref, layout_ref, basis_ref = refs[:4]
-    early_ref, late_ref, info_ref, spread_ref, own_basis_ref, known, inverse = refs[4:]
+    for copy in copies:
+        copy.wait()
+
+
+def prepare_kernel(axes, count, layout, late_from, *refs):
+    ints_ref, basis_ref = refs[:2]
+    early_ref, late_ref, info_ref, spread_ref, own_basis_ref, known, inverse, layout_ref = refs[-8:]
     at = Places(*axes)
-    slots = neighbors_ref.shape[0]
-    atoms = neighbors_ref.shape[1]
+    slots = ints_ref.shape[0] - 5
+    atoms = ints_ref.shape[1]
+    for i, value in enumerate(layout):
+        layout_ref[i] = value
     bits = atoms.bit_length() - 1
     lines = count * at.n_lay
 
@@ -127,12 +136,12 @@
         return jnp.dot(picked, basis_ref[...], preferred_element_type=jnp.float32).astype(jnp.bfloat16)
 
     self_slot = jnp.int32(0)
-    for w, (atom, rank) in enumerate(own_ranks(at, neighbors_ref)):
+    for w, (atom, rank) in enumerate(own_ranks(at, ints_ref)):
         row, col, lay = at.split(atom)
         step_row = (row - at.row) & (at.n_row - 1)
         step_col = (col - at.col) & (at.n_col - 1)
         self_slot = jnp.where(atom == at.me, w, self_slot)
-        info_ref[w] = size_ref[atom]
+        info_ref[w] = ints_ref[slots, atom]
         spread_ref[w] = rows_of(hot(LANES, atom, rank * SHELLS))
         flip = lay ^ at.lay
         known[0, w] = atom
@@ -141,7 +150,7 @@
         known[3, w] = jnp.where((step_row != 0) & (flip == 3), 16 + w, w)
         inverse[atom] = -1
     own_basis_ref[...] = rows_of(hot(16, at.me, 0))
-    info_ref[slots] = size_ref[at.me]
+    info_ref[slots] = ints_ref[slots, at.me]
     info_ref[slots + 1] = self_slot
 
     def row_of_pairs(v, totals):
@@ -152,7 +161,7 @@
         turn = known[3, v]
         row, _, lay = at.split(atom)
         for u in range(slots):
-            inverse[neighbors_ref[u, atom]] = v * 16 + u
+            inverse[ints_ref[u, atom]] = v * 16 + u
         top = layout_ref[line]
         end = layout_ref[lines + line]
         beside = layout_ref[(side + 1) * lines + line]
@@ -265,7 +274,7 @@
 def step_kernel(pieces, *refs):
     table_ref, info_ref, basis_ref, spread_ref, sign_ref, early_ref = refs[:6]
     piece_refs = refs[6 : 6 + pieces]
-    next_ref, coef_ref, pool, gram, own, square, sems = refs[6 + pieces :]
+    next_ref, coef_ref, pool, gram, own, square, sems = refs[-7:]
     slots, size = sign_ref.shape[0], sign_ref.shape[1]
     copies = fill(piece_refs, pool, sems)
     for v in range(slots):
@@ -321,15 +330,16 @@
     coef_ref[...] = coef[: coef_ref.shape[0]]
 
 
-def profile_kernel(periods, steps, sources, inputs, *refs):
-    plane_ref, line_ref, geos, sems = refs[inputs:]
+def profile_kernel(periods, steps, mate_from, *refs):
+    own_ref, mate_ref, third_ref = refs[:3]
+    plane_ref, line_ref, geos, sems = refs[-4:]
     odd = (lax.axis_index("layer") & 1) == 1
+    rows = len(steps) * GEO
     copies = []
-    for o, source in enumerate(sources):
-        for k, (buffer, start) in enumerate(source):
-            copy = pltpu.make_async_copy(refs[buffer].at[pl.ds(start, GEO)], geos.at[3 * o + k], sems.at[3 * o + k])
-            copy.start()
-            copies.append(copy)
+    for k, source in enumerate((own_ref, mate_ref.at[pl.ds(mate_from, rows)], third_ref)):
+        copy = pltpu.make_async_copy(source, geos.at[k], sems.at[k])
+        copy.start()
+        copies.append(copy)
     cells = plane_ref.shape[2]
     cell = lax.broadcasted_iota(jnp.int32, (cells, LANES), 0)
     grid_x = (cell // BY).astype(jnp.float32)
@@ -348,7 +358,7 @@
     for copy in copies:
         copy.wait()
     for o, (step_row, step_col) in enumerate(steps):
-        own, first, third = (geos[3 * o + k].astype(jnp.float32) for k in range(3))
+        own, first, third = (geos[k, o * GEO : (o + 1) * GEO].astype(jnp.float32) for k in range(3))
         below = jnp.where(odd, first, third)
         above = jnp.where(odd, third, first)
         moved = jnp.where(from_below, pltpu.roll(below, 3 * SPAN, axis=1), pltpu.roll(above, 3 * SPAN, axis=1))
@@ -403,7 +413,17 @@
     others = range(1, count)
     own = sign_start[0]
     flat = own.reshape(slots * size, size)
-    listings = neighbors.T
+    ints = jnp.concatenate(
+        [
+            neighbors.T,
+            atom_size[None],
+            atom_x[None],
+            atom_y[None],
+            atom_z[None],
+            jnp.pad(pair_extent, ((0, 0), (0, atoms - slots))),
+        ],
+        axis=0,
+    )
     full = slots * size
     half = full // 2
     n_pick = column_targets(n_row)
@@ -421,12 +441,12 @@
             jax.ShapeDtypeStruct((part, size), own.dtype),
             jax.ShapeDtypeStruct((GEO, LANES), own.dtype),
         ),
-        in_specs=[SMEM] * 5 + [VMEM],
+        in_specs=[SMEM, HBM],
         out_specs=(VMEM, VMEM),
-        scratch_shapes=[pltpu.SMEM((n_pick + 1,), jnp.int32)],
+        scratch_shapes=[pltpu.SMEM((n_pick + 1,), jnp.int32), pltpu.SemaphoreType.DMA((n_pick,))],
         compiler_params=pltpu.CompilerParams(vmem_limit_bytes=2 << 20),
         name="pick_column_blocks",
-    )(listings, pair_extent, atom_x, atom_y, atom_z, own)
+    )(ints, own)
     up = from_offset(picked, "col", 1)
     down = from_offset(picked, "col", -1)
 
@@ -460,10 +480,12 @@
     place = {name: i for i, name in enumerate(names)}
     xs = [place["x", di] for di in others]
     plans = [
-        [(place["far"], half, half), (0, 0, part), (2, 0, GEO)],
-        [(x, 0, half) for x in xs] + [(1, 0, part), (2, 0, GEO)],
-        [(x, 0, full) for x in xs] + [(place["far"], 0, full), (0, 0, part), (1, 0, part), (2, 0, GEO)],
+        [(place["far"], half, half), (0, 0, part), (2, 0, GEO), (1, part - GEO, GEO)],
+        [(x, 0, half) for x in xs] + [(1, 0, part)],
+        [(x, 0, full) for x in xs] + [(place["far"], 0, full), (0, 0, part), (1, 0, part)],
     ]
+
+    two_x, two_y, two_m = pack([buffers[name] for name in names], plans, [], "pack_two")
 
     early_order = ["own", "mate", "far", "up", "down", "geo"] + [("x", di) for di in others]
     early_order += [("two x", di) for di in others] + ["two y", "two m"]
@@ -472,19 +494,21 @@
 
     contents = {}
     for di in others:
-        contents["two x", di] = [(("end", di, 2), half)] + side_of("up", di, 0) + [(("geo", di, 0), GEO)]
-    contents["two y"] = [(("top", di, 2), half) for di in others] + side_of("down", 0, 2) + [(("geo", 0, 2), GEO)]
+        contents["two x", di] = [(("end", di, 2), half)] + side_of("up", di, 0)
+        contents["two x", di] += [(("geo", di, 0), GEO), (("down geo", di, 0), GEO)]
+    contents["two y"] = [(("top", di, 2), half) for di in others] + side_of("down", 0, 2)
     contents["two m"] = sum([row_of(di, 1) for di in others], []) + row_of(0, 3)
-    contents["two m"] += side_of("up", 0, 1) + side_of("down", 0, 1) + [(("geo", 0, 1), GEO)]
-    for di in others:
-        contents["three x", di] = side_of("down", di, 0) + side_of("down", di, 2) + [(("geo", di, 2), GEO)]
+    contents["two m"] += side_of("up", 0, 1) + side_of("down", 0, 1)
+    for di in others:
+        contents["three x", di] = side_of("down", di, 0) + side_of("down", di, 2)
     contents["three y"] = side_of("up", 0, 2) + sum([side_of("up", di, 2) for di in others], [])
     contents["three m"] = []
     for di in others:
-        contents["three m"] += [(("end", di, 3), half)] + side_of("up", di, 1) + [(("geo", di, 1), GEO)]
-    contents["three m"] += [(("top", di, 3), half) for di in others] + side_of("down", 0, 3) + [(("geo", 0, 3), GEO)]
-    for di in others:
-        contents["four x", di] = side_of("down", di, 1) + side_of("down", di, 3) + [(("geo", di, 3), GEO)]
+        contents["three m"] += [(("end", di, 3), half)] + side_of("up", di, 1) + [(None, 2 * GEO)]
+    contents["three m"] += [(("top", di, 3), half) for di in others] + side_of("down", 0, 3)
+    contents["three m"] += [("geos", count * 3 * GEO)]
+    for di in others:
+        contents["four x", di] = side_of("down", di, 1) + side_of("down", di, 3)
     contents["four y"] = side_of("up", 0, 3) + sum([side_of("up", di, 3) for di in others], [])
     lengths = {name: sum(rows for _, rows in content) for name, content in contents.items()}
     for name in early_order:
@@ -512,7 +536,7 @@
     pairs = slots * (slots + 1) // 2
     entries = 3 * (pairs + UNROLL) + 1
     early_table, late_table, info, spread, own_basis = pl.pallas_call(
-        functools.partial(prepare_kernel, axes, count, late_from),
+        functools.partial(prepare_kernel, axes, count, tuple(layout), late_from),
         out_shape=(
             jax.ShapeDtypeStruct((entries,), jnp.int32),
             jax.ShapeDtypeStruct((entries,), jnp.int32),
@@ -520,40 +544,45 @@
             jax.ShapeDtypeStruct((slots, LANES, size), jnp.bfloat16),
             jax.ShapeDtypeStruct((16, size), jnp.bfloat16),
         ),
-        in_specs=[SMEM] * 3 + [VMEM],
+        in_specs=[SMEM, VMEM, ANY],
         out_specs=(SMEM, SMEM, SMEM, VMEM, VMEM),
-        scratch_shapes=[pltpu.SMEM((4, slots), jnp.int32), pltpu.SMEM((atoms,), jnp.int32)],
+        scratch_shapes=[
+            pltpu.SMEM((4, slots), jnp.int32),
+            pltpu.SMEM((atoms,), jnp.int32),
+            pltpu.SMEM((len(layout),), jnp.int32),
+        ],
         compiler_params=pltpu.CompilerParams(vmem_limit_bytes=(2 << 20) + atoms * 16384),
-        cost_estimate=pl.CostEstimate(flops=1_000_000_000, bytes_accessed=8_000_000, transcendentals=0),
+        cost_estimate=pl.CostEstimate(flops=6_000_000_000, bytes_accessed=8_000_000, transcendentals=0),
         name="prepare",
-    )(
-        listings,
-        atom_size,
-        jnp.array(layout, dtype=jnp.int32),
-        basis_proj.transpose(1, 0, 2).reshape(SHELLS * atoms, size),
-    )
-
-    two_x, two_y, two_m = pack([buffers[name] for name in names], plans, [own_basis], "pack_two")
+    )(ints, basis_proj.transpose(1, 0, 2).reshape(SHELLS * atoms, size), two_x)
+
     for di in others:
         note(("two x", di), on_row(two_x, di), contents["two x", di])
     note("two y", from_layer(two_y, 2), contents["two y"])
     note("two m", from_layer(two_m, 1), contents["two m"])
 
-    names = ["up", "down", "two y"] + [("two x", di) for di in others]
+    names = ["up", "down", "two y", "geo"] + [("two x", di) for di in others]
     place = {name: i for i, name in enumerate(names)}
     y_down = at["down", 0, 2][1]
     x_up = at["up", 1, 0][1]
+    gather = []
+    for di in range(count):
+        for kind in ("geo", "up geo", "down geo"):
+            name, start = at[kind, di, 0]
+            gather.append((place[name], start, GEO))
     xs = [place["two x", di] for di in others]
     plans = [
-        [(1, 0, part), (2, y_down, part + GEO)],
+        [(1, 0, part), (2, y_down, part)],
         [(0, 0, part)] + [(x, x_up, part) for x in xs],
-        [(x, 0, lengths["two x", 1]) for x in xs] + [(2, 0, lengths["two y"])],
+        [(x, 0, lengths["two x", 1]) for x in xs] + [(2, 0, lengths["two y"])] + gather,
+        gather,
     ]
-    three_x, three_y, three_m = pack([buffers[name] for name in names], plans, [], "pack_three")
+    three_x, three_y, three_m, geos = pack([buffers[name] for name in names], plans, [own_basis], "pack_three")
     for di in others:
         note(("three x", di), on_row(three_x, di), contents["three x", di])
     note("three y", from_layer(three_y, 2), contents["three y"])
     note("three m", from_layer(three_m, 1), contents["three m"])
+    third_geos = from_layer(geos, 3)
 
     early_values = [buffers[name] for name in early_order]
     gram = pl.pallas_call(
@@ -574,6 +603,27 @@
         note(("four x", di), from_layer(buffers["three x", di], 1), contents["four x", di])
     note("four y", from_layer(buffers["three y"], 1), contents["four y"])
 
+    column_steps = (0, 1, -1)
+    tile_steps = [(dr, dc) for dr in steps for dc in column_steps]
+    tiles = len(tile_steps)
+    periods = (float(BX * n_row), float(BY * n_col), float(BZ * n_lay))
+    plane, line = pl.pallas_call(
+        functools.partial(profile_kernel, periods, tile_steps, at["geos"][1]),
+        out_shape=(
+            jax.ShapeDtypeStruct((tiles, SHELLS, BX * BY, LANES), jnp.bfloat16),
+            jax.ShapeDtypeStruct((tiles, SHELLS, LANES, BZ), jnp.bfloat16),
+        ),
+        in_specs=[ANY] * 4,
+        out_specs=(VMEM, VMEM),
+        scratch_shapes=[
+            pltpu.VMEM((3, tiles * GEO, LANES), jnp.bfloat16),
+            pltpu.SemaphoreType.DMA((3,)),
+        ],
+        compiler_params=pltpu.CompilerParams(vmem_limit_bytes=10 << 20),
+        cost_estimate=pl.CostEstimate(flops=5_000_000_000, bytes_accessed=4_000_000, transcendentals=2_000_000),
+        name="profiles",
+    )(geos, buffers["three m"], third_geos, gram)
+
     late_values = [buffers[name] for name in late_order]
     sign_next, coef = pl.pallas_call(
         functools.partial(step_kernel, len(late_values)),
@@ -581,7 +631,7 @@
             jax.ShapeDtypeStruct((slots, size, size), jnp.bfloat16),
             jax.ShapeDtypeStruct((8, LANES), jnp.float32),
         ),
-        in_specs=[SMEM, SMEM, VMEM, VMEM, VMEM, VMEM] + [ANY] * len(late_values),
+        in_specs=[SMEM, SMEM, VMEM, VMEM, VMEM, VMEM] + [ANY] * (len(late_values) + 1),
         out_specs=(VMEM, VMEM),
         scratch_shapes=[
             pltpu.VMEM((total - late_from, LANES), jnp.bfloat16),
@@ -593,7 +643,7 @@
         compiler_params=pltpu.CompilerParams(vmem_limit_bytes=(15 << 20) + (total - late_from) * LANES * 2),
         cost_estimate=pl.CostEstimate(flops=1_300_000_000, bytes_accessed=8_000_000, transcendentals=0),
         name="square_cube_coefficients",
-    )(late_table, info, own_basis, spread, own, gram, *late_values)
+    )(late_table, info, own_basis, spread, own, gram, *late_values, line)
 
     below = from_offset(coef, "layer", -1)
     above = from_offset(coef, "layer", 1)
@@ -607,38 +657,7 @@
         axis=1,
     )
     stacked = jnp.concatenate([merged] + [on_row(merged, di) for di in others], axis=0)
-    column_steps = (0, 1, -1)
     received = [stacked] + [from_offset(stacked, "col", dc) for dc in column_steps[1:]]
-
-    tile_steps = [(dr, dc) for dr in steps for dc in column_steps]
-    tiles = len(tile_steps)
-    used, sources = [], []
-    for di in range(count):
-        for kind in ("geo", "up geo", "down geo"):
-            source = []
-            for flip in (0, 1, 3):
-                name, start = at[kind, di, flip]
-                if name not in used:
-                    used.append(name)
-                source.append((used.index(name), start))
-            sources.append(tuple(source))
-    periods = (float(BX * n_row), float(BY * n_col), float(BZ * n_lay))
-    plane, line = pl.pallas_call(
-        functools.partial(profile_kernel, periods, tile_steps, tuple(sources), len(used)),
-        out_shape=(
-            jax.ShapeDtypeStruct((tiles, SHELLS, BX * BY, LANES), jnp.bfloat16),
-            jax.ShapeDtypeStruct((tiles, SHELLS, LANES, BZ), jnp.bfloat16),
-        ),
-        in_specs=[ANY] * len(used),
-        out_specs=(VMEM, VMEM),
-        scratch_shapes=[
-            pltpu.VMEM((3 * tiles, GEO, LANES), jnp.bfloat16),
-            pltpu.SemaphoreType.DMA((3 * tiles,)),
-        ],
-        compiler_params=pltpu.CompilerParams(vmem_limit_bytes=10 << 20),
-        cost_estimate=pl.CostEstimate(flops=30_000_000, bytes_accessed=4_000_000, transcendentals=2_000_000),
-        name="profiles",
-    )(*[buffers[name] for name in used])
 
     density = pl.pallas_call(
         functools.partial(density_kernel, len(column_steps)),

time: 77 us -> 72.9 us (0.947)
  local copies, waits for them, and re-layouts: 7.3 us -> 3.24 us
    unnamed x22 -> x6, local copies, waits for them, and re-layouts: 7.15 us -> 1 us
    ppermute x10, waiting for transfers between devices: 26.1 us -> 23 us  [from_offset(): lax.ppermute(x, axis, [((i + step) % count, i) for i in range(count)])]
    ppermute x8 -> x9, waiting for transfers between devices: 1.39 us -> 3.95 us  [from_layer(): return lax.ppermute(x, 'layer', [(i ^ flip, i) for i in range(count)])]
    concatenate x0 -> x1, local copies, waits for them, and re-layouts: none -> 1.43 us  [local(): jnp.concatenate([neighbors.T, atom_size[None], atom_x[None], atom_y[None]...]
    ppermute x8 -> x9, starting transfers between devices: 4.2 us -> 4.97 us  [from_layer(): return lax.ppermute(x, 'layer', [(i ^ flip, i) for i in range(count)])]
  transfers between devices with their start and end apart: 18 -> 19, of which waited for: 8 -> 10; matrix products, arithmetic and copies ran while one was open for 0% -> 3% of each run, Pallas kernels for 20% -> 22%
where the time goes in v4:
time: 72.9 us; the launch traced here: 72.7 us
  waiting for transfers between devices  27 us (37%)
  Pallas kernels  25 us (34%)
  starting transfers between devices  16.6 us (23%)
  local copies, waits for them, and re-layouts  3.24 us (4%)
  between operations  0.76 us (1%)
    ppermute x10, waiting for transfers between devices, from_offset(): lax.ppermute(x, axis, [((i + step) % count, i) for i in range(count)])  23 us
    ppermute x10, starting transfers between devices, from_offset(): lax.ppermute(x, axis, [((i + step) % count, i) for i in range(count)])  11.6 us
    pallas_call x1, Pallas kernels, local(): pl.pallas_call(functools.partial(prepare_kernel, axes, count, tuple(layou...  6.01 us
    pallas_call x1, Pallas kernels, local(): pl.pallas_call(functools.partial(step_kernel, len(late_values)), out_shap...  5.77 us
    ppermute x9, starting transfers between devices, from_layer(): return lax.ppermute(x, 'layer', [(i ^ flip, i) for i in range(count)])  4.97 us
    ppermute x9, waiting for transfers between devices, from_layer(): return lax.ppermute(x, 'layer', [(i ^ flip, i) for i in range(count)])  3.95 us
    pallas_call x1, Pallas kernels, local(): pl.pallas_call(functools.partial(profile_kernel, periods, tile_steps, at[...  3.53 us
    pallas_call x1, Pallas kernels, local(): pl.pallas_call(functools.partial(gram_kernel, len(early_values)), out_sha...  3.52 us
  transfers between devices with their start and end apart: 19, of which 10 were waited for; matrix products, arithmetic and copies ran while one was open for 3% of the time, Pallas kernels for 22%

profile of v4, /device:TPU:0, one launch (start us, length us, event | category | flops | bytes accessed | tf_op | source)
XLA Modules:
  0.0 72.7 jit_solution(18406166032513367492)
XLA Ops:
  0.6 3.0 %collective-permute-start.2 = (bf16[1536,128]{1,0:T(8,128)(2,1)}, bf16[1536,128]{1,0:T(8,128)(2,1)S(1)}, u32[]{:S(2)}, u32[]{:S(2)}) collective-permute-start(bf16[1536,128]{1,0:T(8,128)(2,1)} %bitcast.15), channel_id=1, source_target_pairs={{2,0},{3,1},{0,2},{1,3},{6,4},{7,5},{4,6},{5,7},{10,8},{11,9},{8,1... | collective-permute-start | bytes 1179656 | tf_op jit(solution)/shard_map/ppermute | solution.py:31
  3.7 1.5 %collective-permute-start.3 = (bf16[1536,128]{1,0:T(8,128)(2,1)}, bf16[1536,128]{1,0:T(8,128)(2,1)S(1)}, u32[]{:S(2)}, u32[]{:S(2)}) collective-permute-start(bf16[1536,128]{1,0:T(8,128)(2,1)} %bitcast.16), channel_id=1, source_target_pairs={{16,0},{0,16},{17,1},{1,17},{18,2},{2,18},{19,3},{3,19},{20,4},{4,... | collective-permute-start | bytes 1179656 | tf_op jit(solution)/shard_map/ppermute | solution.py:26
  5.2 0.7 pad.4
  5.8 1.4 %concatenate.9.ints_ref.refs_0_ = s32[17,32]{1,0:T(8,128)S(1)} concatenate(s32[12,32]{1,0:T(8,128)} %bitcast.25, s32[1,32]{1,0:T(1,128)} %bitcast.26, s32[1,32]{1,0:T(1,128)} %bitcast.27, s32[1,32]{1,0:T(1,128)} %bitcast.28, s32[1,32]{1,0:T(1,128)} %bitcast.29, s32[1,32]{1,0:T(1,128)S(1)} %pad.4), dimensions={0} | concatenate | bytes 4352 | tf_op jit(solution)/shard_map/concatenate | solution.py:416
  7.2 0.0 copy-start
  7.2 1.0 %copy-done = bf16[1,12,128,128]{3,2,1,0:T(8,128)(2,1)S(1)} copy-done((bf16[1,12,128,128]{3,2,1,0:T(8,128)(2,1)S(1)}, bf16[1,12,128,128]{3,2,1,0:T(8,128)(2,1)}, u32[]{:S(2)}) %copy-start) | copy-done | bytes 393240
  8.2 0.0 copy-start.2
  8.2 1.4 %pick_column_blocks.1 = (bf16[656,128]{1,0:T(8,128)(2,1)S(1)}, bf16[16,128]{1,0:T(8,128)(2,1)S(1)}) custom-call(s32[17,32]{1,0:T(8,128)S(1)} %concatenate.9.ints_ref.refs_0_, bf16[12,128,128]{2,1,0:T(8,128)(2,1)S(1)} %bitcast.17), custom_call_target="tpu_custom_call" | custom-call | tf_op jit(solution)/shard_map/pick_column_blocks/pallas_call | solution.py:438
  9.7 3.7 %collective-permute-start = (bf16[656,128]{1,0:T(8,128)(2,1)S(1)}, bf16[656,128]{1,0:T(8,128)(2,1)S(1)}, u32[]{:S(2)}, u32[]{:S(2)}) collective-permute-start(bf16[656,128]{1,0:T(8,128)(2,1)S(1)} %get-tuple-element.20), channel_id=1, source_target_pairs={{4,0},{8,4},{12,8},{0,12},{5,1},{9,5},{13,9},{1,13},{6,2},{10,6},{... | collective-permute-start | bytes 503816 | tf_op jit(solution)/shard_map/ppermute | solution.py:26
  13.3 0.0 collective-permute-start.1
  13.3 4.7 %collective-permute-done.refs_0_.refs_4_ = bf16[656,128]{1,0:T(8,128)(2,1)S(1)} collective-permute-done((bf16[656,128]{1,0:T(8,128)(2,1)S(1)}, bf16[656,128]{1,0:T(8,128)(2,1)S(1)}, u32[]{:S(2)}, u32[]{:S(2)}) %collective-permute-start) | collective-permute-done | bytes 167968 | tf_op jit(solution)/shard_map/ppermute | solution.py:26
  18.1 2.7 %collective-permute-done.1.refs_1_.refs_5_ = bf16[656,128]{1,0:T(8,128)(2,1)S(1)} collective-permute-done((bf16[656,128]{1,0:T(8,128)(2,1)S(1)}, bf16[656,128]{1,0:T(8,128)(2,1)S(1)}, u32[]{:S(2)}, u32[]{:S(2)}) %collective-permute-start.1) | collective-permute-done | bytes 167968 | tf_op jit(solution)/shard_map/ppermute | solution.py:26
  20.8 0.0 collective-permute-done.2.refs_3_
  20.8 0.0 collective-permute-done.3.refs_4_.refs_7_
  20.8 1.9 %pack_two.1 = (bf16[1456,128]{1,0:T(8,128)(2,1)S(1)}, bf16[1424,128]{1,0:T(8,128)(2,1)S(1)}, bf16[4384,128]{1,0:T(8,128)(2,1)S(1)}) custom-call(bf16[656,128]{1,0:T(8,128)(2,1)S(1)} %collective-permute-done.refs_0_.refs_4_, bf16[656,128]{1,0:T(8,128)(2,1)S(1)} %collective-permute-done.1.refs_1_.refs_5_, ...), custom_call_target="tpu_custom_call" | custom-call | bytes 3000000 | tf_op jit(solution)/shard_map/pack_two/pallas_call | solution.py:223
  22.7 0.6 collective-permute-start.5
  23.3 0.5 collective-permute-start.6
  23.8 0.0 collective-permute-start.7
  23.8 0.0 copy-done.2
  23.8 0.0 copy-start.1
  23.8 6.0 %prepare.1 = (s32[247]{0:T(256)S(1)}, s32[247]{0:T(256)S(1)}, s32[14]{0:T(128)S(1)}, bf16[12,128,128]{2,1,0:T(8,128)(2,1)S(1)}, bf16[16,128]{1,0:T(8,128)(2,1)S(1)}) custom-call(s32[17,32]{1,0:T(8,128)S(1)} %concatenate.9.ints_ref.refs_0_, bf16[192,128]{1,0:T(8,128)(2,1)S(1)} %bitcast.23, bf16[1456,128]{1,0:T(8,128)(2,1)S(1)} %get-tuple-element.22.refs_2_), custom_call_target="tpu_custom_call" | custom-call | flops 6000000000 | bytes 8000000 | tf_op jit(solution)/shard_map/prepare/pallas_call | solution.py:538
  29.8 2.2 %collective-permute-done.6.refs_2_.refs_9_ = bf16[1424,128]{1,0:T(8,128)(2,1)S(1)} collective-permute-done((bf16[1424,128]{1,0:T(8,128)(2,1)S(1)}, bf16[1424,128]{1,0:T(8,128)(2,1)S(1)}, u32[]{:S(2)}, u32[]{:S(2)}) %collective-permute-start.6) | collective-permute-done | bytes 364576 | tf_op jit(solution)/shard_map/ppermute | solution.py:31
  32.0 0.0 collective-permute-done.5.refs_4_.refs_8_
  32.0 1.4 %pack_three.1 = (bf16[1312,128]{1,0:T(8,128)(2,1)S(1)}, bf16[1312,128]{1,0:T(8,128)(2,1)S(1)}, bf16[2976,128]{1,0:T(8,128)(2,1)S(1)}, bf16[96,128]{1,0:T(8,128)(2,1)S(1)}) custom-call(bf16[656,128]{1,0:T(8,128)(2,1)S(1)} %collective-permute-done.refs_0_.refs_4_, bf16[656,128]{1,0:T(8,128)(2,1)S(1)} %collective-permute-done.1.refs_1_.refs_5_, ...), custom_call_target="tpu_custom_call" | custom-call | bytes 3000000 | tf_op jit(solution)/shard_map/pack_three/pallas_call | solution.py:223
  33.4 0.1 collective-permute-start.10
  33.5 0.0 copy-done.1
  33.5 0.5 collective-permute-start.4
  34.0 1.5 %collective-permute-start.8 = (bf16[1312,128]{1,0:T(8,128)(2,1)S(1)}, bf16[1312,128]{1,0:T(8,128)(2,1)S(1)}, u32[]{:S(2)}, u32[]{:S(2)}) collective-permute-start(bf16[1312,128]{1,0:T(8,128)(2,1)S(1)} %get-tuple-element.30.refs_11_), channel_id=1, source_target_pairs={{16,0},{0,16},{17,1},{1,17},{18,2},{2,18},{19,3},{3,19},{20,4},{4,... | collective-permute-start | bytes 1007624 | tf_op jit(solution)/shard_map/ppermute | solution.py:26
  35.5 0.5 collective-permute-start.9
  36.0 0.3 collective-permute-done.4.refs_2_
  36.3 0.4 collective-permute-start.13
  36.6 7.2 %collective-permute-done.8.refs_6_ = bf16[1312,128]{1,0:T(8,128)(2,1)S(1)} collective-permute-done((bf16[1312,128]{1,0:T(8,128)(2,1)S(1)}, bf16[1312,128]{1,0:T(8,128)(2,1)S(1)}, u32[]{:S(2)}, u32[]{:S(2)}) %collective-permute-start.8) | collective-permute-done | bytes 335904 | tf_op jit(solution)/shard_map/ppermute | solution.py:26
  43.9 0.0 collective-permute-start.11
  43.9 1.5 %collective-permute-done.9.refs_7_ = bf16[1312,128]{1,0:T(8,128)(2,1)S(1)} collective-permute-done((bf16[1312,128]{1,0:T(8,128)(2,1)S(1)}, bf16[1312,128]{1,0:T(8,128)(2,1)S(1)}, u32[]{:S(2)}, u32[]{:S(2)}) %collective-permute-start.9) | collective-permute-done | bytes 335904 | tf_op jit(solution)/shard_map/ppermute | solution.py:31
  45.3 0.0 collective-permute-start.12
  45.3 0.0 collective-permute-done.7.refs_10_
  45.3 3.5 %gram_early.1.refs_3_.refs_5_ = bf16[1536,1536]{1,0:T(8,128)(2,1)S(1)} custom-call(s32[247]{0:T(256)S(1)} %get-tuple-element.27.refs_0_, bf16[1536,128]{1,0:T(8,128)(2,1)S(1)} %bitcast.19, bf16[1536,128]{1,0:T(8,128)(2,1)S(1)} %collective-permute-done.4.refs_2_, bf16[1536,128]{1,0:T(8,128)(2,1)S(1)} %collective-permute-done.2.refs_3_, ...), custom_call_target="tpu_custom_call" | custom-call | flops 1000000000 | bytes 20000000 | tf_op jit(solution)/shard_map/gram_early/pallas_call | solution.py:588
  48.9 0.0 collective-permute-done.13.refs_2_
  48.9 0.0 collective-permute-done.10.refs_1_.refs_8_
  48.9 3.5 %profiles.1 = (bf16[6,6,256,128]{3,2,1,0:T(8,128)(2,1)S(1)}, bf16[6,6,128,128]{3,2,1,0:T(8,128)(2,1)S(1)}) custom-call(bf16[96,128]{1,0:T(8,128)(2,1)S(1)} %get-tuple-element.33.refs_0_, bf16[2976,128]{1,0:T(8,128)(2,1)S(1)} %collective-permute-done.10.refs_1_.refs_8_, bf16[96,128]{1,0:T(8,128)(2,1)S(1)} %collective-permute-done.13.refs_2_, ...), custom_call_target="tpu_custom_call" | custom-call | flops 5000000000 | bytes 4000000 | tf_op jit(solution)/shard_map/profiles/pallas_call | solution.py:610
  52.4 0.0 collective-permute-done.11.refs_9_
  52.4 0.0 collective-permute-done.12.refs_10_
  52.4 5.8 %square_cube_coefficients.1 = (bf16[12,128,128]{2,1,0:T(8,128)(2,1)}, f32[8,128]{1,0:T(8,128)S(1)}) custom-call(s32[247]{0:T(256)S(1)} %get-tuple-element.23.refs_0_, s32[14]{0:T(128)S(1)} %get-tuple-element.24.refs_1_, bf16[16,128]{1,0:T(8,128)(2,1)S(1)} %get-tuple-element.25.refs_5_.refs_2_, bf16[12,128,128]{2,1,0:T(8,128)(2,1)S(1)} %get-tuple-element.26.refs_3_, ...), custom_call_target="tpu_custom_call" | custom-call | flops 1300000000 | bytes 8000000 | tf_op jit(solution)/shard_map/square_cube_coefficients/pallas_call | solution.py:628
  58.2 0.7 collective-permute-start.14
  58.9 1.1 %collective-permute-start.15 = (f32[8,128]{1,0:T(8,128)S(1)}, f32[8,128]{1,0:T(8,128)S(1)}, u32[]{:S(2)}, u32[]{:S(2)}) collective-permute-start(f32[8,128]{1,0:T(8,128)S(1)} %get-tuple-element.36), channel_id=1, source_target_pairs={{1,0},{2,1},{3,2},{0,3},{5,4},{6,5},{7,6},{4,7},{9,8},{10,9},{11,1... | collective-permute-start | bytes 12296 | tf_op jit(solution)/shard_map/ppermute | solution.py:26
  60.0 1.3 %collective-permute-done.14 = f32[8,128]{1,0:T(8,128)S(1)} collective-permute-done((f32[8,128]{1,0:T(8,128)S(1)}, f32[8,128]{1,0:T(8,128)S(1)}, u32[]{:S(2)}, u32[]{:S(2)}) %collective-permute-start.14) | collective-permute-done | bytes 4128 | tf_op jit(solution)/shard_map/ppermute | solution.py:26
  61.3 0.1 slice.10
  61.4 0.0 collective-permute-done.15
  61.4 0.1 slice.11
  61.5 0.1 pad_maximum_fusion.1
  61.5 0.5 collective-permute-start.16
  62.1 3.1 %collective-permute-done.16 = f32[8,128]{1,0:T(8,128)S(1)} collective-permute-done((f32[8,128]{1,0:T(8,128)S(1)}, f32[8,128]{1,0:T(8,128)S(1)}, u32[]{:S(2)}, u32[]{:S(2)}) %collective-permute-start.16) | collective-permute-done | bytes 4128 | tf_op jit(solution)/shard_map/ppermute | solution.py:26
  65.1 0.1 pad_maximum_fusion.refs_0_
  65.2 0.5 collective-permute-start.17
  65.7 1.5 %collective-permute-start.18 = (f32[16,128]{1,0:T(8,128)S(1)}, f32[16,128]{1,0:T(8,128)S(1)}, u32[]{:S(2)}, u32[]{:S(2)}) collective-permute-start(f32[16,128]{1,0:T(8,128)S(1)} %pad_maximum_fusion.refs_0_), channel_id=1, source_target_pairs={{12,0},{0,4},{4,8},{8,12},{13,1},{1,5},{5,9},{9,13},{14,2},{2,6},{... | collective-permute-start | bytes 24584 | tf_op jit(solution)/shard_map/ppermute | solution.py:26
  67.2 1.6 %collective-permute-done.17.refs_1_ = f32[16,128]{1,0:T(8,128)S(1)} collective-permute-done((f32[16,128]{1,0:T(8,128)S(1)}, f32[16,128]{1,0:T(8,128)S(1)}, u32[]{:S(2)}, u32[]{:S(2)}) %collective-permute-start.17) | collective-permute-done | bytes 8224 | tf_op jit(solution)/shard_map/ppermute | solution.py:26
  68.9 2.3 %collective-permute-done.18.refs_2_ = f32[16,128]{1,0:T(8,128)S(1)} collective-permute-done((f32[16,128]{1,0:T(8,128)S(1)}, f32[16,128]{1,0:T(8,128)S(1)}, u32[]{:S(2)}, u32[]{:S(2)}) %collective-permute-start.18) | collective-permute-done | bytes 8224 | tf_op jit(solution)/shard_map/ppermute | solution.py:26
  71.2 1.5 %density.1 = f32[256,128]{1,0:T(8,128)} custom-call(f32[16,128]{1,0:T(8,128)S(1)} %pad_maximum_fusion.refs_0_, f32[16,128]{1,0:T(8,128)S(1)} %collective-permute-done.17.refs_1_, f32[16,128]{1,0:T(8,128)S(1)} %collective-permute-done.18.refs_2_, bf16[6,6,256,128]{3,2,1,0:T(8,128)(2,1)S(1)} %get-tuple-element.37.refs_3_, bf16[4608,128]{1,0:T(8,128)(2,1)S(1)} %bitcast.14), custom_call_target="tpu_custom_call" | custom-call | flops 310000000 | bytes 4000000 | tf_op jit(solution)/shard_map/density/pallas_call | solution.py:662
  (1 shorter events, 0.0 us)
Async XLA Ops:
  0.6 20.2 %collective-permute-start.2 = (bf16[1536,128]{1,0:T(8,128)(2,1)}, bf16[1536,128]{1,0:T(8,128)(2,1)S(1)}, u32[]{:S(2)}, u32[]{:S(2)}) collective-permute-start(bf16[1536,128]{1,0:T(8,128)(2,1)} %bitcast.15), channel_id=1, source_target_pairs={{2,0},{3,1},{0,2},{1,3},{6,4},{7,5},{4,6},{5,7},{10,8},{11,9},{8,1... | collective-permute-start | bytes 1179656 | tf_op jit(solution)/shard_map/ppermute | solution.py:31
  3.7 17.1 %collective-permute-start.3 = (bf16[1536,128]{1,0:T(8,128)(2,1)}, bf16[1536,128]{1,0:T(8,128)(2,1)S(1)}, u32[]{:S(2)}, u32[]{:S(2)}) collective-permute-start(bf16[1536,128]{1,0:T(8,128)(2,1)} %bitcast.16), channel_id=1, source_target_pairs={{16,0},{0,16},{17,1},{1,17},{18,2},{2,18},{19,3},{3,19},{20,4},{4,... | collective-permute-start | bytes 1179656 | tf_op jit(solution)/shard_map/ppermute | solution.py:26
  7.2 1.0 %copy-start = (bf16[1,12,128,128]{3,2,1,0:T(8,128)(2,1)S(1)}, bf16[1,12,128,128]{3,2,1,0:T(8,128)(2,1)}, u32[]{:S(2)}) copy-start(bf16[1,12,128,128]{3,2,1,0:T(8,128)(2,1)} %param.8) | copy-start | bytes 1179652
  8.2 15.5 %copy-start.2 = (bf16[32,6,128]{2,0,1:T(8,128)(2,1)S(1)}, bf16[32,6,128]{2,0,1:T(8,128)(2,1)}, u32[]{:S(2)}) copy-start(bf16[32,6,128]{2,0,1:T(8,128)(2,1)} %param.11) | copy-start | bytes 147460
  9.7 8.4 %collective-permute-start = (bf16[656,128]{1,0:T(8,128)(2,1)S(1)}, bf16[656,128]{1,0:T(8,128)(2,1)S(1)}, u32[]{:S(2)}, u32[]{:S(2)}) collective-permute-start(bf16[656,128]{1,0:T(8,128)(2,1)S(1)} %get-tuple-element.20), channel_id=1, source_target_pairs={{4,0},{8,4},{12,8},{0,12},{5,1},{9,5},{13,9},{1,13},{6,2},{10,6},{... | collective-permute-start | bytes 503816 | tf_op jit(solution)/shard_map/ppermute | solution.py:26
  13.3 7.5 %collective-permute-start.1 = (bf16[656,128]{1,0:T(8,128)(2,1)S(1)}, bf16[656,128]{1,0:T(8,128)(2,1)S(1)}, u32[]{:S(2)}, u32[]{:S(2)}) collective-permute-start(bf16[656,128]{1,0:T(8,128)(2,1)S(1)} %get-tuple-element.20), channel_id=1, source_target_pairs={{12,0},{0,4},{4,8},{8,12},{13,1},{1,5},{5,9},{9,13},{14,2},{2,6},{... | collective-permute-start | bytes 503816 | tf_op jit(solution)/shard_map/ppermute | solution.py:26
  22.7 9.3 %collective-permute-start.5 = (bf16[1456,128]{1,0:T(8,128)(2,1)S(1)}, bf16[1456,128]{1,0:T(8,128)(2,1)S(1)}, u32[]{:S(2)}, u32[]{:S(2)}) collective-permute-start(bf16[1456,128]{1,0:T(8,128)(2,1)S(1)} %get-tuple-element.22.refs_2_), channel_id=1, source_target_pairs={{16,0},{0,16},{17,1},{1,17},{18,2},{2,18},{19,3},{3,19},{20,4},{4,... | collective-permute-start | bytes 1118216 | tf_op jit(solution)/shard_map/ppermute | solution.py:26
  23.3 8.7 %collective-permute-start.6 = (bf16[1424,128]{1,0:T(8,128)(2,1)S(1)}, bf16[1424,128]{1,0:T(8,128)(2,1)S(1)}, u32[]{:S(2)}, u32[]{:S(2)}) collective-permute-start(bf16[1424,128]{1,0:T(8,128)(2,1)S(1)} %get-tuple-element.28), channel_id=1, source_target_pairs={{2,0},{3,1},{0,2},{1,3},{6,4},{7,5},{4,6},{5,7},{10,8},{11,9},{8,1... | collective-permute-start | bytes 1093640 | tf_op jit(solution)/shard_map/ppermute | solution.py:31
  23.8 21.6 %collective-permute-start.7 = (bf16[4384,128]{1,0:T(8,128)(2,1)S(1)}, bf16[4384,128]{1,0:T(8,128)(2,1)S(1)}, u32[]{:S(2)}, u32[]{:S(2)}) collective-permute-start(bf16[4384,128]{1,0:T(8,128)(2,1)S(1)} %get-tuple-element.29), channel_id=1, source_target_pairs={{1,0},{0,1},{3,2},{2,3},{5,4},{4,5},{7,6},{6,7},{9,8},{8,9},{11,10... | collective-permute-start | bytes 3366920 | tf_op jit(solution)/shard_map/ppermute | solution.py:31
  23.8 9.7 %copy-start.1 = (bf16[1,12,128,128]{3,2,1,0:T(8,128)(2,1)S(1)}, bf16[1,12,128,128]{3,2,1,0:T(8,128)(2,1)}, u32[]{:S(2)}) copy-start(bf16[1,12,128,128]{3,2,1,0:T(8,128)(2,1)} %param.8) | copy-start | bytes 1179652
  33.4 15.5 %collective-permute-start.10 = (bf16[2976,128]{1,0:T(8,128)(2,1)S(1)}, bf16[2976,128]{1,0:T(8,128)(2,1)S(1)}, u32[]{:S(2)}, u32[]{:S(2)}) collective-permute-start(bf16[2976,128]{1,0:T(8,128)(2,1)S(1)} %get-tuple-element.32), channel_id=1, source_target_pairs={{1,0},{0,1},{3,2},{2,3},{5,4},{4,5},{7,6},{6,7},{9,8},{8,9},{11,10... | collective-permute-start | bytes 2285576 | tf_op jit(solution)/shard_map/ppermute | solution.py:31
  33.5 2.8 %collective-permute-start.4 = (bf16[1536,128]{1,0:T(8,128)(2,1)S(1)}, bf16[1536,128]{1,0:T(8,128)(2,1)S(1)}, u32[]{:S(2)}, u32[]{:S(2)}) collective-permute-start(bf16[1536,128]{1,0:T(8,128)(2,1)S(1)} %bitcast.18), channel_id=1, source_target_pairs={{1,0},{0,1},{3,2},{2,3},{5,4},{4,5},{7,6},{6,7},{9,8},{8,9},{11,10... | collective-permute-start | bytes 1179656 | tf_op jit(solution)/shard_map/ppermute | solution.py:31
  34.0 9.9 %collective-permute-start.8 = (bf16[1312,128]{1,0:T(8,128)(2,1)S(1)}, bf16[1312,128]{1,0:T(8,128)(2,1)S(1)}, u32[]{:S(2)}, u32[]{:S(2)}) collective-permute-start(bf16[1312,128]{1,0:T(8,128)(2,1)S(1)} %get-tuple-element.30.refs_11_), channel_id=1, source_target_pairs={{16,0},{0,16},{17,1},{1,17},{18,2},{2,18},{19,3},{3,19},{20,4},{4,... | collective-permute-start | bytes 1007624 | tf_op jit(solution)/shard_map/ppermute | solution.py:26
  35.5 9.9 %collective-permute-start.9 = (bf16[1312,128]{1,0:T(8,128)(2,1)S(1)}, bf16[1312,128]{1,0:T(8,128)(2,1)S(1)}, u32[]{:S(2)}, u32[]{:S(2)}) collective-permute-start(bf16[1312,128]{1,0:T(8,128)(2,1)S(1)} %get-tuple-element.31), channel_id=1, source_target_pairs={{2,0},{3,1},{0,2},{1,3},{6,4},{7,5},{4,6},{5,7},{10,8},{11,9},{8,1... | collective-permute-start | bytes 1007624 | tf_op jit(solution)/shard_map/ppermute | solution.py:31
  36.3 12.6 %collective-permute-start.13 = (bf16[96,128]{1,0:T(8,128)(2,1)S(1)}, bf16[96,128]{1,0:T(8,128)(2,1)S(1)}, u32[]{:S(2)}, u32[]{:S(2)}) collective-permute-start(bf16[96,128]{1,0:T(8,128)(2,1)S(1)} %get-tuple-element.33.refs_0_), channel_id=1, source_target_pairs={{3,0},{2,1},{1,2},{0,3},{7,4},{6,5},{5,6},{4,7},{11,8},{10,9},{9,1... | collective-permute-start | bytes 73736 | tf_op jit(solution)/shard_map/ppermute | solution.py:31
  43.9 8.6 %collective-permute-start.11 = (bf16[1312,128]{1,0:T(8,128)(2,1)S(1)}, bf16[1312,128]{1,0:T(8,128)(2,1)S(1)}, u32[]{:S(2)}, u32[]{:S(2)}) collective-permute-start(bf16[1312,128]{1,0:T(8,128)(2,1)S(1)} %collective-permute-done.8.refs_6_), channel_id=1, source_target_pairs={{1,0},{0,1},{3,2},{2,3},{5,4},{4,5},{7,6},{6,7},{9,8},{8,9},{11,10... | collective-permute-start | bytes 1007624 | tf_op jit(solution)/shard_map/ppermute | solution.py:31
  45.3 7.1 %collective-permute-start.12 = (bf16[1312,128]{1,0:T(8,128)(2,1)S(1)}, bf16[1312,128]{1,0:T(8,128)(2,1)S(1)}, u32[]{:S(2)}, u32[]{:S(2)}) collective-permute-start(bf16[1312,128]{1,0:T(8,128)(2,1)S(1)} %collective-permute-done.9.refs_7_), channel_id=1, source_target_pairs={{1,0},{0,1},{3,2},{2,3},{5,4},{4,5},{7,6},{6,7},{9,8},{8,9},{11,10... | collective-permute-start | bytes 1007624 | tf_op jit(solution)/shard_map/ppermute | solution.py:31
  58.2 3.1 %collective-permute-start.14 = (f32[8,128]{1,0:T(8,128)S(1)}, f32[8,128]{1,0:T(8,128)S(1)}, u32[]{:S(2)}, u32[]{:S(2)}) collective-permute-start(f32[8,128]{1,0:T(8,128)S(1)} %get-tuple-element.36), channel_id=1, source_target_pairs={{3,0},{0,1},{1,2},{2,3},{7,4},{4,5},{5,6},{6,7},{11,8},{8,9},{9,10... | collective-permute-start | bytes 12296 | tf_op jit(solution)/shard_map/ppermute | solution.py:26
  58.9 2.5 %collective-permute-start.15 = (f32[8,128]{1,0:T(8,128)S(1)}, f32[8,128]{1,0:T(8,128)S(1)}, u32[]{:S(2)}, u32[]{:S(2)}) collective-permute-start(f32[8,128]{1,0:T(8,128)S(1)} %get-tuple-element.36), channel_id=1, source_target_pairs={{1,0},{2,1},{3,2},{0,3},{5,4},{6,5},{7,6},{4,7},{9,8},{10,9},{11,1... | collective-permute-start | bytes 12296 | tf_op jit(solution)/shard_map/ppermute | solution.py:26
  61.5 3.6 %collective-permute-start.16 = (f32[8,128]{1,0:T(8,128)S(1)}, f32[8,128]{1,0:T(8,128)S(1)}, u32[]{:S(2)}, u32[]{:S(2)}) collective-permute-start(f32[8,128]{1,0:T(8,128)S(1)} %pad_maximum_fusion.1), channel_id=1, source_target_pairs={{16,0},{0,16},{17,1},{1,17},{18,2},{2,18},{19,3},{3,19},{20,4},{4,... | collective-permute-start | bytes 12296 | tf_op jit(solution)/shard_map/ppermute | solution.py:26
  65.2 3.7 %collective-permute-start.17 = (f32[16,128]{1,0:T(8,128)S(1)}, f32[16,128]{1,0:T(8,128)S(1)}, u32[]{:S(2)}, u32[]{:S(2)}) collective-permute-start(f32[16,128]{1,0:T(8,128)S(1)} %pad_maximum_fusion.refs_0_), channel_id=1, source_target_pairs={{4,0},{8,4},{12,8},{0,12},{5,1},{9,5},{13,9},{1,13},{6,2},{10,6},{... | collective-permute-start | bytes 24584 | tf_op jit(solution)/shard_map/ppermute | solution.py:26
  65.7 5.4 %collective-permute-start.18 = (f32[16,128]{1,0:T(8,128)S(1)}, f32[16,128]{1,0:T(8,128)S(1)}, u32[]{:S(2)}, u32[]{:S(2)}) collective-permute-start(f32[16,128]{1,0:T(8,128)S(1)} %pad_maximum_fusion.refs_0_), channel_id=1, source_target_pairs={{12,0},{0,4},{4,8},{8,12},{13,1},{1,5},{5,9},{9,13},{14,2},{2,6},{... | collective-permute-start | bytes 24584 | tf_op jit(solution)/shard_map/ppermute | solution.py:26

commit v5 on v4

--- a/solution.py
+++ b/solution.py
@@ -26,6 +26,14 @@
     return lax.ppermute(x, axis, [((i + step) % count, i) for i in range(count)])
 
 
+def from_row_layer(x, step, mover):
+    rows, layers = lax.axis_size("row"), lax.axis_size("layer")
+    moves = [
+        (((i + step) % rows) * layers + mover(j) % layers, i * layers + j) for i in range(rows) for j in range(layers)
+    ]
+    return lax.ppermute(x, ("row", "layer"), moves)
+
+
 def from_layer(x, flip):
     count = lax.axis_size("layer")
     return lax.ppermute(x, "layer", [(i ^ flip, i) for i in range(count)])
@@ -63,11 +71,19 @@
         )
 
 
-def own_ranks(at, ints_ref):
+def load(sources, targets, sems):
+    copies = [pltpu.make_async_copy(a, b, sems.at[i]) for i, (a, b) in enumerate(zip(sources, targets))]
+    for copy in copies:
+        copy.start()
+    for copy in copies:
+        copy.wait()
+
+
+def own_ranks(at, neighbors_ref):
     seen = [jnp.int32(0)] * at.n_lay
     listed = []
-    for w in range(ints_ref.shape[0] - 5):
-        atom = ints_ref[w, at.me]
+    for w in range(neighbors_ref.shape[0]):
+        atom = neighbors_ref[w, at.me]
         step_lay = (atom - at.lay) & (at.n_lay - 1)
         rank = jnp.int32(0)
         for k in range(at.n_lay):
@@ -77,14 +93,16 @@
     return listed
 
 
-def pick_kernel(axes, ints_ref, sign_ref, out_ref, geo_ref, place_ref, sems):
+def pick_kernel(axes, *refs):
+    sign_ref, out_ref, geo_ref, neighbors_ref, extent_ref, x_ref, y_ref, z_ref, place_ref, loads, sems = refs[5:]
     at = Places(*axes)
     slots = sign_ref.shape[0]
     n_pick = place_ref.shape[0] - 1
     size = sign_ref.shape[1]
     for i in range(n_pick + 1):
         place_ref[i] = 0
-    ranks = own_ranks(at, ints_ref)
+    load(refs[:5], (neighbors_ref, extent_ref, x_ref, y_ref, z_ref), loads)
+    ranks = own_ranks(at, neighbors_ref)
     for w, (atom, _) in enumerate(ranks):
         row, col, lay = at.split(atom)
         place = target_place(at.n_row, (row - at.row) & (at.n_row - 1), (lay - at.lay) & (at.n_lay - 1), at.row)
@@ -102,28 +120,29 @@
         go_row = ((row - at.row + 1) & (at.n_row - 1)) - 1
         go_col = ((col - at.col + 1) & (at.n_col - 1)) - 1
         go_lay = jnp.minimum(((lay - at.lay + 1) & (at.n_lay - 1)) - 1, 1)
-        twice_x = ints_ref[slots + 1, at.me] + ints_ref[slots + 1, atom] + BX * go_row
-        twice_y = ints_ref[slots + 2, at.me] + ints_ref[slots + 2, atom] + BY * go_col
-        twice_z = ints_ref[slots + 3, at.me] + ints_ref[slots + 3, atom] + BZ * go_lay - BZ
-        extent = ints_ref[slots + 4, w]
+        twice_x = x_ref[at.me] + x_ref[atom] + BX * go_row
+        twice_y = y_ref[at.me] + y_ref[atom] + BY * go_col
+        twice_z = z_ref[at.me] + z_ref[atom] + BZ * go_lay - BZ
+        extent = extent_ref[0, w]
         values = jnp.where(sub == 0, twice_x, jnp.where(sub == 1, twice_y, jnp.where(sub == 2, twice_z, extent)))
         geo = jnp.where(lane_pair == rank, values, geo)
     geo = geo.astype(jnp.float32).astype(geo_ref.dtype)
     geo_ref[...] = geo
-    out_ref[n_pick * size : n_pick * size + GEO] = geo
+    out_ref[n_pick * size :] = geo
     for copy in copies:
         copy.wait()
 
 
 def prepare_kernel(axes, count, layout, late_from, *refs):
-    ints_ref, basis_ref = refs[:2]
-    early_ref, late_ref, info_ref, spread_ref, own_basis_ref, known, inverse, layout_ref = refs[-8:]
+    basis_ref = refs[2]
+    early_ref, late_ref, info_ref, spread_ref, own_basis_ref = refs[-11:-6]
+    neighbors_ref, size_ref, known, inverse, layout_ref, loads = refs[-6:]
     at = Places(*axes)
-    slots = ints_ref.shape[0] - 5
-    atoms = ints_ref.shape[1]
+    load(refs[:2], (neighbors_ref, size_ref), loads)
+    slots, atoms = neighbors_ref.shape
+    bits = atoms.bit_length() - 1
     for i, value in enumerate(layout):
         layout_ref[i] = value
-    bits = atoms.bit_length() - 1
     lines = count * at.n_lay
 
     def hot(rows, atom, first):
@@ -136,21 +155,20 @@
         return jnp.dot(picked, basis_ref[...], preferred_element_type=jnp.float32).astype(jnp.bfloat16)
 
     self_slot = jnp.int32(0)
-    for w, (atom, rank) in enumerate(own_ranks(at, ints_ref)):
+    for w, (atom, rank) in enumerate(own_ranks(at, neighbors_ref)):
         row, col, lay = at.split(atom)
         step_row = (row - at.row) & (at.n_row - 1)
         step_col = (col - at.col) & (at.n_col - 1)
         self_slot = jnp.where(atom == at.me, w, self_slot)
-        info_ref[w] = ints_ref[slots, atom]
-        spread_ref[w] = rows_of(hot(LANES, atom, rank * SHELLS))
+        info_ref[w] = size_ref[atom]
+        spread_ref[:, w * LANES : (w + 1) * LANES] = rows_of(hot(LANES, atom, rank * SHELLS))
         flip = lay ^ at.lay
         known[0, w] = atom
         known[1, w] = jnp.where(step_col == 0, 0, jnp.where(step_col == 1, 1, 2))
         known[2, w] = jnp.where(step_row == 0, 0, jnp.where(step_row == 1, 1, 2)) * at.n_lay + flip
-        known[3, w] = jnp.where((step_row != 0) & (flip == 3), 16 + w, w)
         inverse[atom] = -1
     own_basis_ref[...] = rows_of(hot(16, at.me, 0))
-    info_ref[slots] = ints_ref[slots, at.me]
+    info_ref[slots] = size_ref[at.me]
     info_ref[slots + 1] = self_slot
 
     def row_of_pairs(v, totals):
@@ -158,10 +176,9 @@
         atom = known[0, v]
         side = known[1, v]
         line = known[2, v]
-        turn = known[3, v]
         row, _, lay = at.split(atom)
         for u in range(slots):
-            inverse[ints_ref[u, atom]] = v * 16 + u
+            inverse[neighbors_ref[u, atom]] = v * 16 + u
         top = layout_ref[line]
         end = layout_ref[lines + line]
         beside = layout_ref[(side + 1) * lines + line]
@@ -174,7 +191,7 @@
             o_row, _, o_lay = at.split(other)
             there = target_place(at.n_row, (o_row - row) & (at.n_row - 1), (o_lay - lay) & (at.n_lay - 1), row)
             back = target_place(at.n_row, (row - o_row) & (at.n_row - 1), (lay - o_lay) & (at.n_lay - 1), o_row)
-            from_row = (other_side != 0) | (turn <= known[3, w])
+            from_row = (other_side != 0) | (v <= w)
             from_column = (side == other_side) & (there >= 0) & ((back < 0) | (v <= w))
             chosen = ((mark >> 4) == v) & jnp.where(side == 0, from_row, from_column)
             in_row = jnp.where(slot < half, top + slot * LANES, end + (slot - half) * LANES)
@@ -302,7 +319,8 @@
     for n in range(slots // 2):
         part = jnp.dot(own[...], gram[:, n * wide : (n + 1) * wide], preferred_element_type=jnp.float32)
         square[:, n * wide : (n + 1) * wide] = jnp.where(column_kept(n), part, 0.0).astype(square.dtype)
-    coef = jnp.zeros((basis_ref.shape[0], LANES), jnp.float32)
+    basis = jnp.concatenate([basis_ref[...], basis_ref[...]], axis=1)
+    coef = jnp.zeros((2 * basis_ref.shape[0], LANES), jnp.float32)
     across = (((1,), (1,)), ((), ()))
     for n in range(slots // 2):
         part = jnp.dot(square[...], gram[:, n * wide : (n + 1) * wide], preferred_element_type=jnp.float32)
@@ -316,28 +334,25 @@
         dmat = 0.5 * (jnp.where(diag, 1.0, 0.0) - full)
         high = dmat.astype(jnp.bfloat16)
         low = (dmat - high.astype(jnp.float32)).astype(jnp.bfloat16)
-        half = jnp.dot(basis_ref[...], high, preferred_element_type=jnp.float32) + jnp.dot(
-            basis_ref[...], low, preferred_element_type=jnp.float32
-        )
+        half = jnp.dot(basis, jnp.concatenate([high, low], axis=0), preferred_element_type=jnp.float32)
         half_high = half.astype(jnp.bfloat16)
         half_low = (half - half_high.astype(jnp.float32)).astype(jnp.bfloat16)
-        for k in range(2):
-            spread = spread_ref[2 * n + k]
-            for part in (half_high, half_low):
-                coef = coef + lax.dot_general(
-                    part[:, k * size : (k + 1) * size], spread, across, preferred_element_type=jnp.float32
-                )
+        coef = coef + lax.dot_general(
+            jnp.concatenate([half_high, half_low], axis=0),
+            spread_ref[:, n * wide : (n + 1) * wide],
+            across,
+            preferred_element_type=jnp.float32,
+        )
+    coef = coef[: basis_ref.shape[0]] + coef[basis_ref.shape[0] :]
     coef_ref[...] = coef[: coef_ref.shape[0]]
 
 
-def profile_kernel(periods, steps, mate_from, *refs):
-    own_ref, mate_ref, third_ref = refs[:3]
+def profile_kernel(periods, steps, *refs):
     plane_ref, line_ref, geos, sems = refs[-4:]
     odd = (lax.axis_index("layer") & 1) == 1
-    rows = len(steps) * GEO
     copies = []
-    for k, source in enumerate((own_ref, mate_ref.at[pl.ds(mate_from, rows)], third_ref)):
-        copy = pltpu.make_async_copy(source, geos.at[k], sems.at[k])
+    for k in range(3):
+        copy = pltpu.make_async_copy(refs[k], geos.at[k], sems.at[k])
         copy.start()
         copies.append(copy)
     cells = plane_ref.shape[2]
@@ -357,8 +372,8 @@
 
     for copy in copies:
         copy.wait()
-    for o, (step_row, step_col) in enumerate(steps):
-        own, first, third = (geos[k, o * GEO : (o + 1) * GEO].astype(jnp.float32) for k in range(3))
+    for o, (place, step_row, step_col) in enumerate(steps):
+        own, first, third = (geos[k, place * GEO : (place + 1) * GEO].astype(jnp.float32) for k in range(3))
         below = jnp.where(odd, first, third)
         above = jnp.where(odd, third, first)
         moved = jnp.where(from_below, pltpu.roll(below, 3 * SPAN, axis=1), pltpu.roll(above, 3 * SPAN, axis=1))
@@ -386,17 +401,22 @@
             line_ref[o, s] = jnp.where(inside_z, jnp.exp(-rate_z * squared_z), 0.0).astype(line_ref.dtype)
 
 
-def density_kernel(column_steps, *refs):
-    coef_refs = refs[:column_steps]
-    plane_ref, line_ref, out_ref, terms = refs[column_steps:]
-    for o in range(plane_ref.shape[0]):
-        coef = coef_refs[o % column_steps]
-        first = 8 * (o // column_steps)
+def density_kernel(tiles, inputs, *refs):
+    coef_refs = refs[: inputs - 2]
+    plane_ref, line_ref = refs[inputs - 2 : inputs]
+    out_ref, terms = refs[-2:]
+    for i, (o, source, first) in enumerate(tiles):
         for s in range(SHELLS):
-            scaled = plane_ref[o, s].astype(jnp.float32) * coef[first + s : first + s + 1, :]
-            at = (o * SHELLS + s) * LANES
+            scaled = plane_ref[o, s].astype(jnp.float32) * coef_refs[source][first + s : first + s + 1, :]
+            at = (i * SHELLS + s) * LANES
             terms[:, at : at + LANES] = scaled.astype(terms.dtype)
-    out_ref[...] = jnp.dot(terms[...], line_ref[...], preferred_element_type=jnp.float32)
+    start = tiles[0][0] * SHELLS * LANES
+    summed = jnp.dot(
+        terms[...], line_ref[start : start + len(tiles) * SHELLS * LANES], preferred_element_type=jnp.float32
+    )
+    if len(refs) > inputs + 2:
+        summed = summed + refs[inputs][...]
+    out_ref[...] = summed
 
 
 def local(sign_start, neighbors, atom_size, basis_proj, pair_extent, atom_x, atom_y, atom_z):
@@ -413,126 +433,104 @@
     others = range(1, count)
     own = sign_start[0]
     flat = own.reshape(slots * size, size)
-    ints = jnp.concatenate(
-        [
-            neighbors.T,
-            atom_size[None],
-            atom_x[None],
-            atom_y[None],
-            atom_z[None],
-            jnp.pad(pair_extent, ((0, 0), (0, atoms - slots))),
-        ],
-        axis=0,
-    )
+    listings = neighbors.T
     full = slots * size
     half = full // 2
     n_pick = column_targets(n_row)
-    part = n_pick * size + GEO
+    picks = n_pick * size
+    part = picks + GEO
+    kinds = ("geo", "up geo", "down geo")
 
     def on_row(value, di):
         return from_offset(value, "row", steps[di])
 
-    x_row = {di: on_row(flat, di) for di in others}
-    y_row = from_layer(flat, 2)
-    m_row = from_layer(flat, 1)
     picked, geo = pl.pallas_call(
         functools.partial(pick_kernel, axes),
         out_shape=(
             jax.ShapeDtypeStruct((part, size), own.dtype),
             jax.ShapeDtypeStruct((GEO, LANES), own.dtype),
         ),
-        in_specs=[SMEM, HBM],
+        in_specs=[HBM] * 6,
         out_specs=(VMEM, VMEM),
-        scratch_shapes=[pltpu.SMEM((n_pick + 1,), jnp.int32), pltpu.SemaphoreType.DMA((n_pick,))],
+        scratch_shapes=[
+            pltpu.SMEM((slots, atoms), jnp.int32),
+            pltpu.SMEM((1, slots), jnp.int32),
+            pltpu.SMEM((atoms,), jnp.int32),
+            pltpu.SMEM((atoms,), jnp.int32),
+            pltpu.SMEM((atoms,), jnp.int32),
+            pltpu.SMEM((n_pick + 1,), jnp.int32),
+            pltpu.SemaphoreType.DMA((5,)),
+            pltpu.SemaphoreType.DMA((n_pick,)),
+        ],
         compiler_params=pltpu.CompilerParams(vmem_limit_bytes=2 << 20),
         name="pick_column_blocks",
-    )(ints, own)
+    )(listings, pair_extent, atom_x, atom_y, atom_z, own)
+    x_row = {di: on_row(flat, di) for di in others}
+    far = from_layer(flat, 2)
     up = from_offset(picked, "col", 1)
     down = from_offset(picked, "col", -1)
-
-    at = {}
-    buffers = {}
-
-    def note(name, value, contents):
-        buffers[name] = value
-        start = 0
-        for what, rows in contents:
-            if what is not None:
-                at[what] = (name, start)
-            start += rows
+    halves = pack(
+        [far] + [x_row[di] for di in others],
+        [[(0, half, half)]] + [[(di, 0, half)] for di in others],
+        [],
+        "pack_halves",
+    )
+    ends = {di: on_row(halves[0], di) for di in others}
+    tops = {di: from_layer(halves[di], 2) for di in others}
+    mate = from_layer(flat, 1)
+
+    beside, geos = pack(
+        [up, down, geo],
+        [[(0, 0, picks), (1, 0, picks)], [(2, 0, GEO), (0, picks, GEO), (1, picks, GEO)]],
+        [ends[di] for di in others] + [tops[di] for di in others],
+        "pack_beside",
+    )
+    side_x = {di: on_row(beside, di) for di in others}
+    side_y = from_layer(beside, 2)
+    side_d = {di: from_row_layer(beside, steps[di], lambda j: j ^ 2) for di in others}
+    geos = jnp.concatenate([geos] + [on_row(geos, di) for di in others], axis=0)
+    mate_geos = from_layer(geos, 1)
+    third_geos = from_layer(geos, 3)
+    rows = [x_row[di] for di in others] + [far] + [ends[di] for di in others] + [tops[di] for di in others]
+    rows += [beside]
+    to_mate = pack(rows, [[(i, 0, value.shape[0]) for i, value in enumerate(rows)]], [], "pack_mate")[0]
+    mate_rows = from_layer(to_mate, 1)
 
     def row_of(di, flip):
         return [(("top", di, flip), half), (("end", di, flip), half)]
 
-    def side_of(kind, di, flip):
-        return [((kind, di, flip), part - GEO), ((kind + " geo", di, flip), GEO)]
-
-    note("own", flat, row_of(0, 0))
-    note("mate", m_row, row_of(0, 1))
-    note("far", y_row, row_of(0, 2))
-    note("up", up, side_of("up", 0, 0))
-    note("down", down, side_of("down", 0, 0))
-    note("geo", geo, [(("geo", 0, 0), GEO)])
-    for di in others:
-        note(("x", di), x_row[di], row_of(di, 0))
-
-    names = ["up", "down", "geo", "far"] + [("x", di) for di in others]
-    place = {name: i for i, name in enumerate(names)}
-    xs = [place["x", di] for di in others]
-    plans = [
-        [(place["far"], half, half), (0, 0, part), (2, 0, GEO), (1, part - GEO, GEO)],
-        [(x, 0, half) for x in xs] + [(1, 0, part)],
-        [(x, 0, full) for x in xs] + [(place["far"], 0, full), (0, 0, part), (1, 0, part)],
-    ]
-
-    two_x, two_y, two_m = pack([buffers[name] for name in names], plans, [], "pack_two")
-
-    early_order = ["own", "mate", "far", "up", "down", "geo"] + [("x", di) for di in others]
-    early_order += [("two x", di) for di in others] + ["two y", "two m"]
-    late_order = [("three x", di) for di in others] + ["three y", "three m"]
-    late_order += [("four x", di) for di in others] + ["four y"]
-
-    contents = {}
-    for di in others:
-        contents["two x", di] = [(("end", di, 2), half)] + side_of("up", di, 0)
-        contents["two x", di] += [(("geo", di, 0), GEO), (("down geo", di, 0), GEO)]
-    contents["two y"] = [(("top", di, 2), half) for di in others] + side_of("down", 0, 2)
-    contents["two m"] = sum([row_of(di, 1) for di in others], []) + row_of(0, 3)
-    contents["two m"] += side_of("up", 0, 1) + side_of("down", 0, 1)
-    for di in others:
-        contents["three x", di] = side_of("down", di, 0) + side_of("down", di, 2)
-    contents["three y"] = side_of("up", 0, 2) + sum([side_of("up", di, 2) for di in others], [])
-    contents["three m"] = []
-    for di in others:
-        contents["three m"] += [(("end", di, 3), half)] + side_of("up", di, 1) + [(None, 2 * GEO)]
-    contents["three m"] += [(("top", di, 3), half) for di in others] + side_of("down", 0, 3)
-    contents["three m"] += [("geos", count * 3 * GEO)]
-    for di in others:
-        contents["four x", di] = side_of("down", di, 1) + side_of("down", di, 3)
-    contents["four y"] = side_of("up", 0, 3) + sum([side_of("up", di, 3) for di in others], [])
-    lengths = {name: sum(rows for _, rows in content) for name, content in contents.items()}
-    for name in early_order:
-        if name in buffers:
-            lengths[name] = buffers[name].shape[0]
-    base = {}
+    def side_of(di, flip):
+        return [(("up", di, flip), picks), (("down", di, flip), picks)]
+
+    early = [(flat, row_of(0, 0)), (mate, row_of(0, 1)), (far, row_of(0, 2))]
+    early += [(x_row[di], row_of(di, 0)) for di in others]
+    early += [(ends[di], [(("end", di, 2), half)]) for di in others]
+    early += [(tops[di], [(("top", di, 2), half)]) for di in others]
+    early += [(beside, side_of(0, 0))]
+    content = sum([row_of(di, 1) for di in others], []) + row_of(0, 3)
+    content += [(("end", di, 3), half) for di in others] + [(("top", di, 3), half) for di in others]
+    early += [(mate_rows, content + side_of(0, 1))]
+    located = {}
     total = 0
-    for name in early_order + late_order:
-        base[name] = total
-        total += lengths[name]
-        if name == early_order[-1]:
-            late_from = total
-    located = dict(at)
-    for name, content in contents.items():
-        start = 0
-        for what, rows in content:
-            located[what] = (name, start)
-            start += rows
+    for _, content in early:
+        for what, length in content:
+            located[what] = total
+            total += length
+    late_from = total
+    late = [side_of(di, 0) for di in others] + [side_of(di, 1) for di in others]
+    late += [side_of(0, 2), side_of(0, 3)]
+    late += [side_of(di, 2) for di in others] + [side_of(di, 3) for di in others]
+    for content in late:
+        for what, length in content:
+            located[what] = total
+            total += length
     layout = [
-        base[located[kind, di, flip][0]] + located[kind, di, flip][1]
+        located[kind, di, flip]
         for kind in ("top", "end", "up", "down")
         for di in range(count)
         for flip in range(n_lay)
     ]
+
     pairs = slots * (slots + 1) // 2
     entries = 3 * (pairs + UNROLL) + 1
     early_table, late_table, info, spread, own_basis = pl.pallas_call(
@@ -541,74 +539,53 @@
             jax.ShapeDtypeStruct((entries,), jnp.int32),
             jax.ShapeDtypeStruct((entries,), jnp.int32),
             jax.ShapeDtypeStruct((slots + 2,), jnp.int32),
-            jax.ShapeDtypeStruct((slots, LANES, size), jnp.bfloat16),
+            jax.ShapeDtypeStruct((LANES, full), jnp.bfloat16),
             jax.ShapeDtypeStruct((16, size), jnp.bfloat16),
         ),
-        in_specs=[SMEM, VMEM, ANY],
+        in_specs=[HBM, HBM, VMEM, ANY],
         out_specs=(SMEM, SMEM, SMEM, VMEM, VMEM),
         scratch_shapes=[
-            pltpu.SMEM((4, slots), jnp.int32),
+            pltpu.SMEM((slots, atoms), jnp.int32),
+            pltpu.SMEM((atoms,), jnp.int32),
+            pltpu.SMEM((3, slots), jnp.int32),
             pltpu.SMEM((atoms,), jnp.int32),
             pltpu.SMEM((len(layout),), jnp.int32),
+            pltpu.SemaphoreType.DMA((2,)),
         ],
         compiler_params=pltpu.CompilerParams(vmem_limit_bytes=(2 << 20) + atoms * 16384),
         cost_estimate=pl.CostEstimate(flops=6_000_000_000, bytes_accessed=8_000_000, transcendentals=0),
         name="prepare",
-    )(ints, basis_proj.transpose(1, 0, 2).reshape(SHELLS * atoms, size), two_x)
-
-    for di in others:
-        note(("two x", di), on_row(two_x, di), contents["two x", di])
-    note("two y", from_layer(two_y, 2), contents["two y"])
-    note("two m", from_layer(two_m, 1), contents["two m"])
-
-    names = ["up", "down", "two y", "geo"] + [("two x", di) for di in others]
-    place = {name: i for i, name in enumerate(names)}
-    y_down = at["down", 0, 2][1]
-    x_up = at["up", 1, 0][1]
-    gather = []
-    for di in range(count):
-        for kind in ("geo", "up geo", "down geo"):
-            name, start = at[kind, di, 0]
-            gather.append((place[name], start, GEO))
-    xs = [place["two x", di] for di in others]
-    plans = [
-        [(1, 0, part), (2, y_down, part)],
-        [(0, 0, part)] + [(x, x_up, part) for x in xs],
-        [(x, 0, lengths["two x", 1]) for x in xs] + [(2, 0, lengths["two y"])] + gather,
-        gather,
-    ]
-    three_x, three_y, three_m, geos = pack([buffers[name] for name in names], plans, [own_basis], "pack_three")
-    for di in others:
-        note(("three x", di), on_row(three_x, di), contents["three x", di])
-    note("three y", from_layer(three_y, 2), contents["three y"])
-    note("three m", from_layer(three_m, 1), contents["three m"])
-    third_geos = from_layer(geos, 3)
-
-    early_values = [buffers[name] for name in early_order]
+    )(listings, atom_size, basis_proj.transpose(1, 0, 2).reshape(SHELLS * atoms, size), beside)
+
+    early_values = [value for value, _ in early]
     gram = pl.pallas_call(
         functools.partial(gram_kernel, len(early_values)),
         out_shape=jax.ShapeDtypeStruct((full, full), jnp.bfloat16),
-        in_specs=[SMEM] + [ANY] * (len(early_values) + 1),
+        in_specs=[SMEM] + [ANY] * len(early_values),
         out_specs=VMEM,
         scratch_shapes=[
             pltpu.VMEM((late_from, LANES), jnp.bfloat16),
             pltpu.SemaphoreType.DMA((len(early_values),)),
         ],
         compiler_params=pltpu.CompilerParams(vmem_limit_bytes=(6 << 20) + late_from * LANES * 2),
-        cost_estimate=pl.CostEstimate(flops=1_000_000_000, bytes_accessed=20_000_000, transcendentals=0),
+        cost_estimate=pl.CostEstimate(flops=4_000_000_000, bytes_accessed=20_000_000, transcendentals=0),
         name="gram_early",
-    )(early_table, *early_values, three_x)
-
-    for di in others:
-        note(("four x", di), from_layer(buffers["three x", di], 1), contents["four x", di])
-    note("four y", from_layer(buffers["three y"], 1), contents["four y"])
+    )(early_table, *early_values)
+
+    diagonal = [side_d[di] for di in others]
+    if len(diagonal) == 1:
+        diagonal = pack(diagonal, [[(0, 0, 2 * picks)]], [gram], "pack_diagonal")
+    late_values = [side_x[di] for di in others] + [from_layer(side_x[di], 1) for di in others]
+    late_values += [side_y, from_layer(side_y, 1)]
+    late_values += diagonal
+    late_values += [from_layer(value, 1) for value in diagonal]
 
     column_steps = (0, 1, -1)
-    tile_steps = [(dr, dc) for dr in steps for dc in column_steps]
+    tile_steps = [(di * 3 + k, steps[di], dc) for k, dc in enumerate(column_steps) for di in range(count)]
     tiles = len(tile_steps)
     periods = (float(BX * n_row), float(BY * n_col), float(BZ * n_lay))
     plane, line = pl.pallas_call(
-        functools.partial(profile_kernel, periods, tile_steps, at["geos"][1]),
+        functools.partial(profile_kernel, periods, tile_steps),
         out_shape=(
             jax.ShapeDtypeStruct((tiles, SHELLS, BX * BY, LANES), jnp.bfloat16),
             jax.ShapeDtypeStruct((tiles, SHELLS, LANES, BZ), jnp.bfloat16),
@@ -622,9 +599,8 @@
         compiler_params=pltpu.CompilerParams(vmem_limit_bytes=10 << 20),
         cost_estimate=pl.CostEstimate(flops=5_000_000_000, bytes_accessed=4_000_000, transcendentals=2_000_000),
         name="profiles",
-    )(geos, buffers["three m"], third_geos, gram)
-
-    late_values = [buffers[name] for name in late_order]
+    )(geos, mate_geos, third_geos, gram)
+
     sign_next, coef = pl.pallas_call(
         functools.partial(step_kernel, len(late_values)),
         out_shape=(
@@ -645,30 +621,50 @@
         name="square_cube_coefficients",
     )(late_table, info, own_basis, spread, own, gram, *late_values, line)
 
-    below = from_offset(coef, "layer", -1)
-    above = from_offset(coef, "layer", 1)
-    merged = jnp.concatenate(
+    triples = [(coef, from_offset(coef, "layer", -1), from_offset(coef, "layer", 1))]
+    for di in others:
+        step = steps[di]
+        triples.append(
+            (
+                on_row(coef, di),
+                from_row_layer(coef, step, lambda j: j - 1),
+                from_row_layer(coef, step, lambda j: j + 1),
+            )
+        )
+    stacked = jnp.concatenate(
         [
-            coef[:, : 4 * SPAN],
-            below[:, SPAN : 3 * SPAN],
-            above[:, 3 * SPAN : 4 * SPAN],
-            jnp.zeros((8, LANES - 7 * SPAN), jnp.float32),
+            jnp.concatenate(
+                [
+                    here[:, : 4 * SPAN],
+                    below[:, SPAN : 3 * SPAN],
+                    above[:, 3 * SPAN : 4 * SPAN],
+                    jnp.zeros((8, LANES - 7 * SPAN), jnp.float32),
+                ],
+                axis=1,
+            )
+            for here, below, above in triples
         ],
-        axis=1,
+        axis=0,
     )
-    stacked = jnp.concatenate([merged] + [on_row(merged, di) for di in others], axis=0)
-    received = [stacked] + [from_offset(stacked, "col", dc) for dc in column_steps[1:]]
-
-    density = pl.pallas_call(
-        functools.partial(density_kernel, len(column_steps)),
-        out_shape=jax.ShapeDtypeStruct((BX * BY, BZ), jnp.float32),
-        in_specs=[VMEM] * (len(column_steps) + 2),
-        out_specs=VMEM,
-        scratch_shapes=[pltpu.VMEM((BX * BY, tiles * SHELLS * LANES), jnp.bfloat16)],
-        compiler_params=pltpu.CompilerParams(vmem_limit_bytes=16 << 20),
-        cost_estimate=pl.CostEstimate(flops=310_000_000, bytes_accessed=4_000_000, transcendentals=0),
-        name="density",
-    )(*received, plane, line.reshape(tiles * SHELLS * LANES, BZ))
+    received = [from_offset(stacked, "col", dc) for dc in column_steps[1:]]
+    line = line.reshape(tiles * SHELLS * LANES, BZ)
+
+    def density_of(parts, coefs, extra, name):
+        inputs = len(coefs) + 2
+        return pl.pallas_call(
+            functools.partial(density_kernel, tuple(parts), inputs),
+            out_shape=jax.ShapeDtypeStruct((BX * BY, BZ), jnp.float32),
+            in_specs=[VMEM] * (inputs + len(extra)),
+            out_specs=VMEM,
+            scratch_shapes=[pltpu.VMEM((BX * BY, len(parts) * SHELLS * LANES), jnp.bfloat16)],
+            compiler_params=pltpu.CompilerParams(vmem_limit_bytes=16 << 20),
+            cost_estimate=pl.CostEstimate(flops=310_000_000, bytes_accessed=4_000_000, transcendentals=0),
+            name=name,
+        )(*coefs, plane, line, *extra)
+
+    density = density_of([(di, 0, 8 * di) for di in range(count)], [stacked], [], "density_column")
+    sides = [((k + 1) * count + di, k, 8 * di) for k in range(2) for di in range(count)]
+    density = density_of(sides, received, [density], "density_sides")
     return sign_next[None], density.reshape(BX, BY, BZ)
 
 

time: 72.9 us -> 82.1 us (1.13)
  starting transfers between devices: 16.6 us -> 24.1 us
  waiting for transfers between devices: 27 us -> 28.4 us
  local copies, waits for them, and re-layouts: 3.24 us -> 4.63 us
  Pallas kernels: 25 us -> 23.8 us
    ppermute x10 -> x11, waiting for transfers between devices: 23 us -> 16.6 us  [from_offset(): lax.ppermute(x, axis, [((i + step) % count, i) for i in range(count)])]
    ppermute x9 -> x10, waiting for transfers between devices: 3.95 us -> 8.01 us  [from_layer(): return lax.ppermute(x, 'layer', [(i ^ flip, i) for i in range(count)])]
    ppermute x0 -> x3, waiting for transfers between devices: none -> 3.84 us  [from_row_layer(): return lax.ppermute(x, ('row', 'layer'), moves)]
    unnamed x6 -> x21, local copies, waits for them, and re-layouts: 1 us -> 4.34 us
    ppermute x0 -> x3, starting transfers between devices: none -> 3.12 us  [from_row_layer(): return lax.ppermute(x, ('row', 'layer'), moves)]
    ppermute x9 -> x10, starting transfers between devices: 4.97 us -> 7.84 us  [from_layer(): return lax.ppermute(x, 'layer', [(i ^ flip, i) for i in range(count)])]
    ppermute x10 -> x11, starting transfers between devices: 11.6 us -> 13.1 us  [from_offset(): lax.ppermute(x, axis, [((i + step) % count, i) for i in range(count)])]
    concatenate x1, local copies, waits for them, and re-layouts: 1.43 us -> 0.01 us  [local(): geos = jnp.concatenate([geos] + [on_row(geos, di) for di in others], axis=0)]
  transfers between devices with their start and end apart: 19 -> 24, of which waited for: 10 -> 11; matrix products, arithmetic and copies ran while one was open for 3% -> 0% of each run, Pallas kernels for 22% -> 18%
where the time goes in v5:
time: 82.1 us; the launch traced here: 81.9 us
  waiting for transfers between devices  28.4 us (35%)
  starting transfers between devices  24.1 us (29%)
  Pallas kernels  23.8 us (29%)
  local copies, waits for them, and re-layouts  4.63 us (6%)
  between operations  0.84 us (1%)
    ppermute x11, waiting for transfers between devices, from_offset(): lax.ppermute(x, axis, [((i + step) % count, i) for i in range(count)])  16.6 us
    ppermute x11, starting transfers between devices, from_offset(): lax.ppermute(x, axis, [((i + step) % count, i) for i in range(count)])  13.1 us
    ppermute x10, waiting for transfers between devices, from_layer(): return lax.ppermute(x, 'layer', [(i ^ flip, i) for i in range(count)])  8.01 us
    ppermute x10, starting transfers between devices, from_layer(): return lax.ppermute(x, 'layer', [(i ^ flip, i) for i in range(count)])  7.84 us
    pallas_call x1, Pallas kernels, local(): pl.pallas_call(functools.partial(prepare_kernel, axes, count, tuple(layou...  5.8 us
    pallas_call x1, Pallas kernels, local(): pl.pallas_call(functools.partial(step_kernel, len(late_values)), out_shap...  5.68 us
    unnamed x21, local copies, waits for them, and re-layouts  4.34 us
    ppermute x3, waiting for transfers between devices, from_row_layer(): return lax.ppermute(x, ('row', 'layer'), moves)  3.84 us
  transfers between devices with their start and end apart: 24, of which 11 were waited for; matrix products, arithmetic and copies ran while one was open for 0% of the time, Pallas kernels for 18%

profile of v5, /device:TPU:0, one launch (start us, length us, event | category | flops | bytes accessed | tf_op | source)
XLA Modules:
  0.0 81.9 jit_solution(11669361291915495550)
XLA Ops:
  0.6 3.0 %collective-permute-start.2 = (bf16[1536,128]{1,0:T(8,128)(2,1)}, bf16[1536,128]{1,0:T(8,128)(2,1)S(1)}, u32[]{:S(2)}, u32[]{:S(2)}) collective-permute-start(bf16[1536,128]{1,0:T(8,128)(2,1)} %bitcast.13), channel_id=1, source_target_pairs={{2,0},{3,1},{0,2},{1,3},{6,4},{7,5},{4,6},{5,7},{10,8},{11,9},{8,1... | collective-permute-start | bytes 1179656 | tf_op jit(solution)/shard_map/ppermute | solution.py:39
  3.7 1.5 %collective-permute-start.3 = (bf16[1536,128]{1,0:T(8,128)(2,1)}, bf16[1536,128]{1,0:T(8,128)(2,1)S(1)}, u32[]{:S(2)}, u32[]{:S(2)}) collective-permute-start(bf16[1536,128]{1,0:T(8,128)(2,1)} %bitcast.14), channel_id=1, source_target_pairs={{16,0},{0,16},{17,1},{1,17},{18,2},{2,18},{19,3},{3,19},{20,4},{4,... | collective-permute-start | bytes 1179656 | tf_op jit(solution)/shard_map/ppermute | solution.py:26
  5.2 7.8 %collective-permute-done.2.refs_0_.refs_1_.refs_3_ = bf16[1536,128]{1,0:T(8,128)(2,1)S(1)} collective-permute-done((bf16[1536,128]{1,0:T(8,128)(2,1)}, bf16[1536,128]{1,0:T(8,128)(2,1)S(1)}, u32[]{:S(2)}, u32[]{:S(2)}) %collective-permute-start.2) | collective-permute-done | bytes 393248 | tf_op jit(solution)/shard_map/ppermute | solution.py:39
  13.0 1.5 %collective-permute-done.3.refs_1_.refs_0_.refs_4_ = bf16[1536,128]{1,0:T(8,128)(2,1)S(1)} collective-permute-done((bf16[1536,128]{1,0:T(8,128)(2,1)}, bf16[1536,128]{1,0:T(8,128)(2,1)S(1)}, u32[]{:S(2)}, u32[]{:S(2)}) %collective-permute-start.3) | collective-permute-done | bytes 393248 | tf_op jit(solution)/shard_map/ppermute | solution.py:26
  14.4 0.5 pack_halves.1
  15.0 1.6 %collective-permute-start.4 = (bf16[768,128]{1,0:T(8,128)(2,1)S(1)}, bf16[768,128]{1,0:T(8,128)(2,1)S(1)}, u32[]{:S(2)}, u32[]{:S(2)}) collective-permute-start(bf16[768,128]{1,0:T(8,128)(2,1)S(1)} %get-tuple-element.19), channel_id=1, source_target_pairs={{16,0},{0,16},{17,1},{1,17},{18,2},{2,18},{19,3},{3,19},{20,4},{4,... | collective-permute-start | bytes 589832 | tf_op jit(solution)/shard_map/ppermute | solution.py:26
  16.5 0.5 collective-permute-start.5
  17.0 1.0 %copy-done = bf16[1,12,128,128]{3,2,1,0:T(8,128)(2,1)S(1)} copy-done((bf16[1,12,128,128]{3,2,1,0:T(8,128)(2,1)S(1)}, bf16[1,12,128,128]{3,2,1,0:T(8,128)(2,1)}, u32[]{:S(2)}) %copy-start) | copy-done | bytes 393240
  18.0 0.7 copy-done.2
  18.7 0.7 copy-done.4
  19.4 0.7 copy-done.5
  20.0 0.7 copy-done.6
  20.7 0.7 copy-done.7
  21.3 1.3 %pick_column_blocks.1 = (bf16[656,128]{1,0:T(8,128)(2,1)S(1)}, bf16[16,128]{1,0:T(8,128)(2,1)S(1)}) custom-call(s32[12,32]{1,0:T(8,128)S(1)} %bitcast.19, s32[1,12]{1,0:T(1,128)S(1)} %copy-done.4, s32[32]{0:T(128)S(1)} %copy-done.5, s32[32]{0:T(128)S(1)} %copy-done.6, s32[32]{0:T(128)S(1)} %copy-done.7, bf16[12,128,128]{2,1,0:T(8,128)(2,1)S(1)} %bitcast.15), custom_call_target="tpu_custom_call" | custom-call | tf_op jit(solution)/shard_map/pick_column_blocks/pallas_call | solution.py:447
  22.7 3.7 %collective-permute-start = (bf16[656,128]{1,0:T(8,128)(2,1)S(1)}, bf16[656,128]{1,0:T(8,128)(2,1)S(1)}, u32[]{:S(2)}, u32[]{:S(2)}) collective-permute-start(bf16[656,128]{1,0:T(8,128)(2,1)S(1)} %get-tuple-element.17), channel_id=1, source_target_pairs={{4,0},{8,4},{12,8},{0,12},{5,1},{9,5},{13,9},{1,13},{6,2},{10,6},{... | collective-permute-start | bytes 503816 | tf_op jit(solution)/shard_map/ppermute | solution.py:26
  26.3 3.7 %collective-permute-done.refs_0_ = bf16[656,128]{1,0:T(8,128)(2,1)S(1)} collective-permute-done((bf16[656,128]{1,0:T(8,128)(2,1)S(1)}, bf16[656,128]{1,0:T(8,128)(2,1)S(1)}, u32[]{:S(2)}, u32[]{:S(2)}) %collective-permute-start) | collective-permute-done | bytes 167968 | tf_op jit(solution)/shard_map/ppermute | solution.py:26
  30.0 3.7 %collective-permute-done.1.refs_1_ = bf16[656,128]{1,0:T(8,128)(2,1)S(1)} collective-permute-done((bf16[656,128]{1,0:T(8,128)(2,1)S(1)}, bf16[656,128]{1,0:T(8,128)(2,1)S(1)}, u32[]{:S(2)}, u32[]{:S(2)}) %collective-permute-start.1) | collective-permute-done | bytes 167968 | tf_op jit(solution)/shard_map/ppermute | solution.py:26
  33.7 0.0 collective-permute-done.4.refs_3_.refs_2_.refs_5_
  33.7 0.5 pack_beside.1
  34.2 0.0 copy-start.1
  34.2 0.0 copy-start.3
  34.2 0.0 copy-start.8
  34.3 0.0 copy-start.9
  34.3 1.0 %pack_mate.1 = bf16[5888,128]{1,0:T(8,128)(2,1)S(1)} custom-call(bf16[1536,128]{1,0:T(8,128)(2,1)S(1)} %collective-permute-done.3.refs_1_.refs_0_.refs_4_, bf16[1536,128]{1,0:T(8,128)(2,1)S(1)} %collective-permute-done.2.refs_0_.refs_1_.refs_3_, bf16[768,128]{1,0:T(8,128)(2,1)S(1)} %collective-permute-done.4.refs_3_.refs_2_.refs_5_, ...), custom_call_target="tpu_custom_call" | custom-call | bytes 3000000 | tf_op jit(solution)/shard_map/pack_mate/pallas_call | solution.py:240
  35.3 0.1 collective-permute-start.7
  35.4 0.5 collective-permute-start.6
  35.9 1.5 %collective-permute-start.10 = (bf16[1280,128]{1,0:T(8,128)(2,1)S(1)}, bf16[1280,128]{1,0:T(8,128)(2,1)S(1)}, u32[]{:S(2)}, u32[]{:S(2)}) collective-permute-start(bf16[1280,128]{1,0:T(8,128)(2,1)S(1)} %get-tuple-element.21.refs_3_.refs_4_.refs_7_), channel_id=1, source_target_pairs={{2,0},{3,1},{0,2},{1,3},{6,4},{7,5},{4,6},{5,7},{10,8},{11,9},{8,1... | collective-permute-start | bytes 983048 | tf_op jit(solution)/shard_map/ppermute | solution.py:39
  37.4 0.5 collective-permute-start.8
  37.9 1.5 %collective-permute-start.14 = (bf16[48,128]{1,0:T(8,128)(2,1)S(1)}, bf16[48,128]{1,0:T(8,128)(2,1)S(1)}, u32[]{:S(2)}, u32[]{:S(2)}) collective-permute-start(bf16[48,128]{1,0:T(8,128)(2,1)S(1)} %get-tuple-element.27), channel_id=1, source_target_pairs={{16,0},{0,16},{17,1},{1,17},{18,2},{2,18},{19,3},{3,19},{20,4},{4,... | collective-permute-start | bytes 36872 | tf_op jit(solution)/shard_map/ppermute | solution.py:26
  39.4 5.8 %prepare.1 = (s32[247]{0:T(256)S(1)}, s32[247]{0:T(256)S(1)}, s32[14]{0:T(128)S(1)}, bf16[128,1536]{1,0:T(8,128)(2,1)S(1)}, bf16[16,128]{1,0:T(8,128)(2,1)S(1)}) custom-call(s32[12,32]{1,0:T(8,128)S(1)} %bitcast.20, s32[32]{0:T(128)S(1)} %copy-done.9, bf16[192,128]{1,0:T(8,128)(2,1)S(1)} %bitcast.22, ...), custom_call_target="tpu_custom_call" | custom-call | flops 6000000000 | bytes 8000000 | tf_op jit(solution)/shard_map/prepare/pallas_call | solution.py:536
  45.3 1.8 %collective-permute-done.14 = bf16[48,128]{1,0:T(8,128)(2,1)S(1)} collective-permute-done((bf16[48,128]{1,0:T(8,128)(2,1)S(1)}, bf16[48,128]{1,0:T(8,128)(2,1)S(1)}, u32[]{:S(2)}, u32[]{:S(2)}) %collective-permute-start.14) | collective-permute-done | bytes 12320 | tf_op jit(solution)/shard_map/ppermute | solution.py:26
  47.1 0.5 collective-permute-start.12
  47.6 0.0 collective-permute-start.15
  47.6 0.0 collective-permute-done.10.refs_8_
  47.6 1.6 %collective-permute-start.16 = (bf16[96,128]{1,0:T(8,128)(2,1)S(1)}, bf16[96,128]{1,0:T(8,128)(2,1)S(1)}, u32[]{:S(2)}, u32[]{:S(2)}) collective-permute-start(bf16[96,128]{1,0:T(8,128)(2,1)S(1)} %constant_dynamic-update-slice_fusion.refs_0_), channel_id=1, source_target_pairs={{3,0},{2,1},{1,2},{0,3},{7,4},{6,5},{5,6},{4,7},{11,8},{10,9},{9,1... | collective-permute-start | bytes 73736 | tf_op jit(solution)/shard_map/ppermute | solution.py:39
  49.2 0.1 collective-permute-start.11
  49.3 0.0 collective-permute-done.7.refs_8_
  49.3 0.4 collective-permute-start.9
  49.8 3.6 %gram_early.1.refs_1_.refs_3_.refs_5_ = bf16[1536,1536]{1,0:T(8,128)(2,1)S(1)} custom-call(s32[247]{0:T(256)S(1)} %get-tuple-element.26.refs_0_, bf16[1536,128]{1,0:T(8,128)(2,1)S(1)} %bitcast.17, bf16[1536,128]{1,0:T(8,128)(2,1)S(1)} %collective-permute-done.6.refs_2_, bf16[1536,128]{1,0:T(8,128)(2,1)S(1)} %collective-permute-done.2.refs_0_.refs_1_.refs_3_, ...), custom_call_target="tpu_custom_call" | custom-call | flops 4000000000 | bytes 20000000 | tf_op jit(solution)/shard_map/gram_early/pallas_call | solution.py:561
  53.4 3.2 %collective-permute-done.12.refs_0_ = bf16[1280,128]{1,0:T(8,128)(2,1)S(1)} collective-permute-done((bf16[1280,128]{1,0:T(8,128)(2,1)S(1)}, bf16[1280,128]{1,0:T(8,128)(2,1)S(1)}, u32[]{:S(2)}, u32[]{:S(2)}) %collective-permute-start.12) | collective-permute-done | bytes 327712 | tf_op jit(solution)/shard_map/ppermute | solution.py:34
  56.6 0.1 pack_diagonal.1.refs_10_
  56.8 0.1 collective-permute-start.13
  56.8 0.0 collective-permute-done.15.refs_1_
  56.8 0.2 collective-permute-done.16.refs_2_
  57.0 3.5 %profiles.1 = (bf16[6,6,256,128]{3,2,1,0:T(8,128)(2,1)S(1)}, bf16[6,6,128,128]{3,2,1,0:T(8,128)(2,1)S(1)}) custom-call(bf16[96,128]{1,0:T(8,128)(2,1)S(1)} %constant_dynamic-update-slice_fusion.refs_0_, bf16[96,128]{1,0:T(8,128)(2,1)S(1)} %collective-permute-done.15.refs_1_, bf16[96,128]{1,0:T(8,128)(2,1)S(1)} %collective-permute-done.16.refs_2_, ...), custom_call_target="tpu_custom_call" | custom-call | flops 5000000000 | bytes 4000000 | tf_op jit(solution)/shard_map/profiles/pallas_call | solution.py:587
  60.5 0.0 collective-permute-done.9.refs_7_
  60.5 5.7 %square_cube_coefficients.1 = (bf16[12,128,128]{2,1,0:T(8,128)(2,1)}, f32[8,128]{1,0:T(8,128)S(1)}) custom-call(s32[247]{0:T(256)S(1)} %get-tuple-element.22.refs_0_, s32[14]{0:T(128)S(1)} %get-tuple-element.23.refs_1_, bf16[16,128]{1,0:T(8,128)(2,1)S(1)} %get-tuple-element.24.refs_2_, bf16[128,1536]{1,0:T(8,128)(2,1)S(1)} %get-tuple-element.25.refs_3_, ...), custom_call_target="tpu_custom_call" | custom-call | flops 1300000000 | bytes 8000000 | tf_op jit(solution)/shard_map/square_cube_coefficients/pallas_call | solution.py:604
  66.2 0.4 collective-permute-start.17
  66.6 1.4 %collective-permute-start.18 = (f32[8,128]{1,0:T(8,128)S(1)}, f32[8,128]{1,0:T(8,128)S(1)}, u32[]{:S(2)}, u32[]{:S(2)}) collective-permute-start(f32[8,128]{1,0:T(8,128)S(1)} %get-tuple-element.30), channel_id=1, source_target_pairs={{1,0},{2,1},{3,2},{0,3},{5,4},{6,5},{7,6},{4,7},{9,8},{10,9},{11,1... | collective-permute-start | bytes 12296 | tf_op jit(solution)/shard_map/ppermute | solution.py:26
  68.0 2.6 %collective-permute-start.21 = (f32[8,128]{1,0:T(8,128)S(1)}, f32[8,128]{1,0:T(8,128)S(1)}, u32[]{:S(2)}, u32[]{:S(2)}) collective-permute-start(f32[8,128]{1,0:T(8,128)S(1)} %get-tuple-element.30), channel_id=1, source_target_pairs={{17,0},{18,1},{19,2},{16,3},{1,16},{2,17},{3,18},{0,19},{21,4},{22... | collective-permute-start | bytes 12296 | tf_op jit(solution)/shard_map/ppermute | solution.py:34
  70.7 0.5 collective-permute-start.19
  71.2 0.1 slice.19
  71.3 0.1 slice.20
  71.4 0.6 collective-permute-done.20
  72.0 0.1 slice.22
  72.0 0.1 slice.23
  72.1 2.2 %collective-permute-done.19 = f32[8,128]{1,0:T(8,128)S(1)} collective-permute-done((f32[8,128]{1,0:T(8,128)S(1)}, f32[8,128]{1,0:T(8,128)S(1)}, u32[]{:S(2)}, u32[]{:S(2)}) %collective-permute-start.19) | collective-permute-done | bytes 4128 | tf_op jit(solution)/shard_map/ppermute | solution.py:26
  74.3 0.1 maximum_maximum_fusion.refs_0_
  74.4 0.7 collective-permute-start.22
  75.0 1.4 %collective-permute-start.23 = (f32[16,128]{1,0:T(8,128)S(1)}, f32[16,128]{1,0:T(8,128)S(1)}, u32[]{:S(2)}, u32[]{:S(2)}) collective-permute-start(f32[16,128]{1,0:T(8,128)S(1)} %maximum_maximum_fusion.refs_0_), channel_id=1, source_target_pairs={{12,0},{0,4},{4,8},{8,12},{13,1},{1,5},{5,9},{9,13},{14,2},{2,6},{... | collective-permute-start | bytes 24584 | tf_op jit(solution)/shard_map/ppermute | solution.py:26
  76.4 0.4 density_column.1.refs_4_
  76.8 1.2 %collective-permute-done.22.refs_0_ = f32[16,128]{1,0:T(8,128)S(1)} collective-permute-done((f32[16,128]{1,0:T(8,128)S(1)}, f32[16,128]{1,0:T(8,128)S(1)}, u32[]{:S(2)}, u32[]{:S(2)}) %collective-permute-start.22) | collective-permute-done | bytes 8224 | tf_op jit(solution)/shard_map/ppermute | solution.py:26
  78.0 2.5 %collective-permute-done.23.refs_1_ = f32[16,128]{1,0:T(8,128)S(1)} collective-permute-done((f32[16,128]{1,0:T(8,128)S(1)}, f32[16,128]{1,0:T(8,128)S(1)}, u32[]{:S(2)}, u32[]{:S(2)}) %collective-permute-start.23) | collective-permute-done | bytes 8224 | tf_op jit(solution)/shard_map/ppermute | solution.py:26
  80.5 1.4 %density_sides.1 = f32[256,128]{1,0:T(8,128)} custom-call(f32[16,128]{1,0:T(8,128)S(1)} %collective-permute-done.22.refs_0_, f32[16,128]{1,0:T(8,128)S(1)} %collective-permute-done.23.refs_1_, bf16[6,6,256,128]{3,2,1,0:T(8,128)(2,1)S(1)} %get-tuple-element.31.refs_1_.refs_2_, bf16[4608,128]{1,0:T(8,128)(2,1)S(1)} %bitcast.12, ...), custom_call_target="tpu_custom_call" | custom-call | flops 310000000 | bytes 4000000 | tf_op jit(solution)/shard_map/density_sides/pallas_call | solution.py:654
  (23 shorter events, 0.1 us)
Async XLA Ops:
  0.6 12.4 %collective-permute-start.2 = (bf16[1536,128]{1,0:T(8,128)(2,1)}, bf16[1536,128]{1,0:T(8,128)(2,1)S(1)}, u32[]{:S(2)}, u32[]{:S(2)}) collective-permute-start(bf16[1536,128]{1,0:T(8,128)(2,1)} %bitcast.13), channel_id=1, source_target_pairs={{2,0},{3,1},{0,2},{1,3},{6,4},{7,5},{4,6},{5,7},{10,8},{11,9},{8,1... | collective-permute-start | bytes 1179656 | tf_op jit(solution)/shard_map/ppermute | solution.py:39
  3.7 10.8 %collective-permute-start.3 = (bf16[1536,128]{1,0:T(8,128)(2,1)}, bf16[1536,128]{1,0:T(8,128)(2,1)S(1)}, u32[]{:S(2)}, u32[]{:S(2)}) collective-permute-start(bf16[1536,128]{1,0:T(8,128)(2,1)} %bitcast.14), channel_id=1, source_target_pairs={{16,0},{0,16},{17,1},{1,17},{18,2},{2,18},{19,3},{3,19},{20,4},{4,... | collective-permute-start | bytes 1179656 | tf_op jit(solution)/shard_map/ppermute | solution.py:26
  15.0 18.8 %collective-permute-start.4 = (bf16[768,128]{1,0:T(8,128)(2,1)S(1)}, bf16[768,128]{1,0:T(8,128)(2,1)S(1)}, u32[]{:S(2)}, u32[]{:S(2)}) collective-permute-start(bf16[768,128]{1,0:T(8,128)(2,1)S(1)} %get-tuple-element.19), channel_id=1, source_target_pairs={{16,0},{0,16},{17,1},{1,17},{18,2},{2,18},{19,3},{3,19},{20,4},{4,... | collective-permute-start | bytes 589832 | tf_op jit(solution)/shard_map/ppermute | solution.py:26
  16.5 17.2 %collective-permute-start.5 = (bf16[768,128]{1,0:T(8,128)(2,1)S(1)}, bf16[768,128]{1,0:T(8,128)(2,1)S(1)}, u32[]{:S(2)}, u32[]{:S(2)}) collective-permute-start(bf16[768,128]{1,0:T(8,128)(2,1)S(1)} %get-tuple-element.20), channel_id=1, source_target_pairs={{2,0},{3,1},{0,2},{1,3},{6,4},{7,5},{4,6},{5,7},{10,8},{11,9},{8,1... | collective-permute-start | bytes 589832 | tf_op jit(solution)/shard_map/ppermute | solution.py:39
  17.0 1.0 %copy-start = (bf16[1,12,128,128]{3,2,1,0:T(8,128)(2,1)S(1)}, bf16[1,12,128,128]{3,2,1,0:T(8,128)(2,1)}, u32[]{:S(2)}) copy-start(bf16[1,12,128,128]{3,2,1,0:T(8,128)(2,1)} %param.8) | copy-start | bytes 1179652
  18.0 0.7 copy-start.2
  18.7 0.7 copy-start.4
  19.4 0.7 copy-start.5
  20.0 0.7 copy-start.6
  20.7 0.7 copy-start.7
  22.7 7.4 %collective-permute-start = (bf16[656,128]{1,0:T(8,128)(2,1)S(1)}, bf16[656,128]{1,0:T(8,128)(2,1)S(1)}, u32[]{:S(2)}, u32[]{:S(2)}) collective-permute-start(bf16[656,128]{1,0:T(8,128)(2,1)S(1)} %get-tuple-element.17), channel_id=1, source_target_pairs={{4,0},{8,4},{12,8},{0,12},{5,1},{9,5},{13,9},{1,13},{6,2},{10,6},{... | collective-permute-start | bytes 503816 | tf_op jit(solution)/shard_map/ppermute | solution.py:26
  26.3 7.4 %collective-permute-start.1 = (bf16[656,128]{1,0:T(8,128)(2,1)S(1)}, bf16[656,128]{1,0:T(8,128)(2,1)S(1)}, u32[]{:S(2)}, u32[]{:S(2)}) collective-permute-start(bf16[656,128]{1,0:T(8,128)(2,1)S(1)} %get-tuple-element.17), channel_id=1, source_target_pairs={{12,0},{0,4},{4,8},{8,12},{13,1},{1,5},{5,9},{9,13},{14,2},{2,6},{... | collective-permute-start | bytes 503816 | tf_op jit(solution)/shard_map/ppermute | solution.py:26
  34.2 1.2 %copy-start.1 = (bf16[1,12,128,128]{3,2,1,0:T(8,128)(2,1)S(1)}, bf16[1,12,128,128]{3,2,1,0:T(8,128)(2,1)}, u32[]{:S(2)}) copy-start(bf16[1,12,128,128]{3,2,1,0:T(8,128)(2,1)} %param.8) | copy-start | bytes 1179652
  34.2 5.2 %copy-start.3 = (s32[32,12]{0,1:T(8,128)S(1)}, s32[32,12]{0,1:T(8,128)}, u32[]{:S(2)}) copy-start(s32[32,12]{0,1:T(8,128)} %param.9) | copy-start | bytes 4612
  34.2 5.2 %copy-start.8 = (bf16[32,6,128]{2,0,1:T(8,128)(2,1)S(1)}, bf16[32,6,128]{2,0,1:T(8,128)(2,1)}, u32[]{:S(2)}) copy-start(bf16[32,6,128]{2,0,1:T(8,128)(2,1)} %param.11) | copy-start | bytes 147460
  34.3 5.2 %copy-start.9 = (s32[32]{0:T(128)S(1)}, s32[32]{0:T(128)}, u32[]{:S(2)}) copy-start(s32[32]{0:T(128)} %refs_1_.3) | copy-start | bytes 388
  35.3 14.0 %collective-permute-start.7 = (bf16[5888,128]{1,0:T(8,128)(2,1)S(1)}, bf16[5888,128]{1,0:T(8,128)(2,1)S(1)}, u32[]{:S(2)}, u32[]{:S(2)}) collective-permute-start(bf16[5888,128]{1,0:T(8,128)(2,1)S(1)} %pack_mate.1), channel_id=1, source_target_pairs={{1,0},{0,1},{3,2},{2,3},{5,4},{4,5},{7,6},{6,7},{9,8},{8,9},{11,10... | collective-permute-start | bytes 4521992 | tf_op jit(solution)/shard_map/ppermute | solution.py:39
  35.4 12.2 %collective-permute-start.6 = (bf16[1536,128]{1,0:T(8,128)(2,1)S(1)}, bf16[1536,128]{1,0:T(8,128)(2,1)S(1)}, u32[]{:S(2)}, u32[]{:S(2)}) collective-permute-start(bf16[1536,128]{1,0:T(8,128)(2,1)S(1)} %bitcast.16), channel_id=1, source_target_pairs={{1,0},{0,1},{3,2},{2,3},{5,4},{4,5},{7,6},{6,7},{9,8},{8,9},{11,10... | collective-permute-start | bytes 1179656 | tf_op jit(solution)/shard_map/ppermute | solution.py:39
  35.9 11.7 %collective-permute-start.10 = (bf16[1280,128]{1,0:T(8,128)(2,1)S(1)}, bf16[1280,128]{1,0:T(8,128)(2,1)S(1)}, u32[]{:S(2)}, u32[]{:S(2)}) collective-permute-start(bf16[1280,128]{1,0:T(8,128)(2,1)S(1)} %get-tuple-element.21.refs_3_.refs_4_.refs_7_), channel_id=1, source_target_pairs={{2,0},{3,1},{0,2},{1,3},{6,4},{7,5},{4,6},{5,7},{10,8},{11,9},{8,1... | collective-permute-start | bytes 983048 | tf_op jit(solution)/shard_map/ppermute | solution.py:39
  37.4 11.8 %collective-permute-start.8 = (bf16[1280,128]{1,0:T(8,128)(2,1)S(1)}, bf16[1280,128]{1,0:T(8,128)(2,1)S(1)}, u32[]{:S(2)}, u32[]{:S(2)}) collective-permute-start(bf16[1280,128]{1,0:T(8,128)(2,1)S(1)} %get-tuple-element.21.refs_3_.refs_4_.refs_7_), channel_id=1, source_target_pairs={{16,0},{0,16},{17,1},{1,17},{18,2},{2,18},{19,3},{3,19},{20,4},{4,... | collective-permute-start | bytes 983048 | tf_op jit(solution)/shard_map/ppermute | solution.py:26
  37.9 9.1 %collective-permute-start.14 = (bf16[48,128]{1,0:T(8,128)(2,1)S(1)}, bf16[48,128]{1,0:T(8,128)(2,1)S(1)}, u32[]{:S(2)}, u32[]{:S(2)}) collective-permute-start(bf16[48,128]{1,0:T(8,128)(2,1)S(1)} %get-tuple-element.27), channel_id=1, source_target_pairs={{16,0},{0,16},{17,1},{1,17},{18,2},{2,18},{19,3},{3,19},{20,4},{4,... | collective-permute-start | bytes 36872 | tf_op jit(solution)/shard_map/ppermute | solution.py:26
  47.1 9.5 %collective-permute-start.12 = (bf16[1280,128]{1,0:T(8,128)(2,1)S(1)}, bf16[1280,128]{1,0:T(8,128)(2,1)S(1)}, u32[]{:S(2)}, u32[]{:S(2)}) collective-permute-start(bf16[1280,128]{1,0:T(8,128)(2,1)S(1)} %get-tuple-element.21.refs_3_.refs_4_.refs_7_), channel_id=1, source_target_pairs={{18,0},{19,1},{16,2},{17,3},{2,16},{3,17},{0,18},{1,19},{22,4},{23... | collective-permute-start | bytes 983048 | tf_op jit(solution)/shard_map/ppermute | solution.py:34
  47.6 9.3 %collective-permute-start.15 = (bf16[96,128]{1,0:T(8,128)(2,1)S(1)}, bf16[96,128]{1,0:T(8,128)(2,1)S(1)}, u32[]{:S(2)}, u32[]{:S(2)}) collective-permute-start(bf16[96,128]{1,0:T(8,128)(2,1)S(1)} %constant_dynamic-update-slice_fusion.refs_0_), channel_id=1, source_target_pairs={{1,0},{0,1},{3,2},{2,3},{5,4},{4,5},{7,6},{6,7},{9,8},{8,9},{11,10... | collective-permute-start | bytes 73736 | tf_op jit(solution)/shard_map/ppermute | solution.py:39
  47.6 9.4 %collective-permute-start.16 = (bf16[96,128]{1,0:T(8,128)(2,1)S(1)}, bf16[96,128]{1,0:T(8,128)(2,1)S(1)}, u32[]{:S(2)}, u32[]{:S(2)}) collective-permute-start(bf16[96,128]{1,0:T(8,128)(2,1)S(1)} %constant_dynamic-update-slice_fusion.refs_0_), channel_id=1, source_target_pairs={{3,0},{2,1},{1,2},{0,3},{7,4},{6,5},{5,6},{4,7},{11,8},{10,9},{9,1... | collective-permute-start | bytes 73736 | tf_op jit(solution)/shard_map/ppermute | solution.py:39
  49.2 11.3 %collective-permute-start.11 = (bf16[1280,128]{1,0:T(8,128)(2,1)S(1)}, bf16[1280,128]{1,0:T(8,128)(2,1)S(1)}, u32[]{:S(2)}, u32[]{:S(2)}) collective-permute-start(bf16[1280,128]{1,0:T(8,128)(2,1)S(1)} %collective-permute-done.10.refs_8_), channel_id=1, source_target_pairs={{1,0},{0,1},{3,2},{2,3},{5,4},{4,5},{7,6},{6,7},{9,8},{8,9},{11,10... | collective-permute-start | bytes 983048 | tf_op jit(solution)/shard_map/ppermute | solution.py:39
  49.3 11.2 %collective-permute-start.9 = (bf16[1280,128]{1,0:T(8,128)(2,1)S(1)}, bf16[1280,128]{1,0:T(8,128)(2,1)S(1)}, u32[]{:S(2)}, u32[]{:S(2)}) collective-permute-start(bf16[1280,128]{1,0:T(8,128)(2,1)S(1)} %collective-permute-done.8.refs_6_), channel_id=1, source_target_pairs={{1,0},{0,1},{3,2},{2,3},{5,4},{4,5},{7,6},{6,7},{9,8},{8,9},{11,10... | collective-permute-start | bytes 983048 | tf_op jit(solution)/shard_map/ppermute | solution.py:39
  56.8 3.8 %collective-permute-start.13 = (bf16[1280,128]{1,0:T(8,128)(2,1)S(1)}, bf16[1280,128]{1,0:T(8,128)(2,1)S(1)}, u32[]{:S(2)}, u32[]{:S(2)}) collective-permute-start(bf16[1280,128]{1,0:T(8,128)(2,1)S(1)} %pack_diagonal.1.refs_10_), channel_id=1, source_target_pairs={{1,0},{0,1},{3,2},{2,3},{5,4},{4,5},{7,6},{6,7},{9,8},{8,9},{11,10... | collective-permute-start | bytes 983048 | tf_op jit(solution)/shard_map/ppermute | solution.py:39
  66.2 5.0 %collective-permute-start.17 = (f32[8,128]{1,0:T(8,128)S(1)}, f32[8,128]{1,0:T(8,128)S(1)}, u32[]{:S(2)}, u32[]{:S(2)}) collective-permute-start(f32[8,128]{1,0:T(8,128)S(1)} %get-tuple-element.30), channel_id=1, source_target_pairs={{3,0},{0,1},{1,2},{2,3},{7,4},{4,5},{5,6},{6,7},{11,8},{8,9},{9,10... | collective-permute-start | bytes 12296 | tf_op jit(solution)/shard_map/ppermute | solution.py:26
  66.6 4.6 %collective-permute-start.18 = (f32[8,128]{1,0:T(8,128)S(1)}, f32[8,128]{1,0:T(8,128)S(1)}, u32[]{:S(2)}, u32[]{:S(2)}) collective-permute-start(f32[8,128]{1,0:T(8,128)S(1)} %get-tuple-element.30), channel_id=1, source_target_pairs={{1,0},{2,1},{3,2},{0,3},{5,4},{6,5},{7,6},{4,7},{9,8},{10,9},{11,1... | collective-permute-start | bytes 12296 | tf_op jit(solution)/shard_map/ppermute | solution.py:26
  68.0 3.9 %collective-permute-start.20 = (f32[8,128]{1,0:T(8,128)S(1)}, f32[8,128]{1,0:T(8,128)S(1)}, u32[]{:S(2)}, u32[]{:S(2)}) collective-permute-start(f32[8,128]{1,0:T(8,128)S(1)} %get-tuple-element.30), channel_id=1, source_target_pairs={{19,0},{16,1},{17,2},{18,3},{3,16},{0,17},{1,18},{2,19},{23,4},{20... | collective-permute-start | bytes 12296 | tf_op jit(solution)/shard_map/ppermute | solution.py:34
  68.0 4.0 %collective-permute-start.21 = (f32[8,128]{1,0:T(8,128)S(1)}, f32[8,128]{1,0:T(8,128)S(1)}, u32[]{:S(2)}, u32[]{:S(2)}) collective-permute-start(f32[8,128]{1,0:T(8,128)S(1)} %get-tuple-element.30), channel_id=1, source_target_pairs={{17,0},{18,1},{19,2},{16,3},{1,16},{2,17},{3,18},{0,19},{21,4},{22... | collective-permute-start | bytes 12296 | tf_op jit(solution)/shard_map/ppermute | solution.py:34
  70.7 3.6 %collective-permute-start.19 = (f32[8,128]{1,0:T(8,128)S(1)}, f32[8,128]{1,0:T(8,128)S(1)}, u32[]{:S(2)}, u32[]{:S(2)}) collective-permute-start(f32[8,128]{1,0:T(8,128)S(1)} %get-tuple-element.30), channel_id=1, source_target_pairs={{16,0},{0,16},{17,1},{1,17},{18,2},{2,18},{19,3},{3,19},{20,4},{4,... | collective-permute-start | bytes 12296 | tf_op jit(solution)/shard_map/ppermute | solution.py:26
  74.4 3.7 %collective-permute-start.22 = (f32[16,128]{1,0:T(8,128)S(1)}, f32[16,128]{1,0:T(8,128)S(1)}, u32[]{:S(2)}, u32[]{:S(2)}) collective-permute-start(f32[16,128]{1,0:T(8,128)S(1)} %maximum_maximum_fusion.refs_0_), channel_id=1, source_target_pairs={{4,0},{8,4},{12,8},{0,12},{5,1},{9,5},{13,9},{1,13},{6,2},{10,6},{... | collective-permute-start | bytes 24584 | tf_op jit(solution)/shard_map/ppermute | solution.py:26
  75.0 5.4 %collective-permute-start.23 = (f32[16,128]{1,0:T(8,128)S(1)}, f32[16,128]{1,0:T(8,128)S(1)}, u32[]{:S(2)}, u32[]{:S(2)}) collective-permute-start(f32[16,128]{1,0:T(8,128)S(1)} %maximum_maximum_fusion.refs_0_), channel_id=1, source_target_pairs={{12,0},{0,4},{4,8},{8,12},{13,1},{1,5},{5,9},{9,13},{14,2},{2,6},{... | collective-permute-start | bytes 24584 | tf_op jit(solution)/shard_map/ppermute | solution.py:26

commit v6 on v5

--- a/solution.py
+++ b/solution.py
@@ -244,7 +244,7 @@
         out_specs=tuple([ANY] * len(plans)),
         scratch_shapes=[pltpu.SemaphoreType.DMA((len(moves),))],
         compiler_params=pltpu.CompilerParams(vmem_limit_bytes=1 << 20),
-        cost_estimate=pl.CostEstimate(flops=0, bytes_accessed=3_000_000, transcendentals=0),
+        cost_estimate=pl.CostEstimate(flops=0, bytes_accessed=1000, transcendentals=0),
         name=name,
     )(*values, *extra)
 
@@ -462,54 +462,52 @@
             pltpu.SemaphoreType.DMA((5,)),
             pltpu.SemaphoreType.DMA((n_pick,)),
         ],
-        compiler_params=pltpu.CompilerParams(vmem_limit_bytes=2 << 20),
+        compiler_params=pltpu.CompilerParams(vmem_limit_bytes=60 << 20),
         name="pick_column_blocks",
     )(listings, pair_extent, atom_x, atom_y, atom_z, own)
     x_row = {di: on_row(flat, di) for di in others}
     far = from_layer(flat, 2)
     up = from_offset(picked, "col", 1)
     down = from_offset(picked, "col", -1)
+    quarter = half // 2
     halves = pack(
         [far] + [x_row[di] for di in others],
-        [[(0, half, half)]] + [[(di, 0, half)] for di in others],
+        [[(0, half + k * quarter, quarter)] for k in range(2)]
+        + [[(di, k * quarter, quarter)] for di in others for k in range(2)],
         [],
         "pack_halves",
     )
-    ends = {di: on_row(halves[0], di) for di in others}
-    tops = {di: from_layer(halves[di], 2) for di in others}
+    ends = {(di, k): on_row(halves[k], di) for di in others for k in range(2)}
+    tops = {(di, k): from_layer(halves[2 * di + k], 2) for di in others for k in range(2)}
+    corners = [(di, k) for di in others for k in range(2)]
     mate = from_layer(flat, 1)
 
-    beside, geos = pack(
+    beside = pack(
         [up, down, geo],
-        [[(0, 0, picks), (1, 0, picks)], [(2, 0, GEO), (0, picks, GEO), (1, picks, GEO)]],
-        [ends[di] for di in others] + [tops[di] for di in others],
+        [[(0, 0, picks), (1, 0, picks), (2, 0, GEO), (0, picks, GEO), (1, picks, GEO)]],
+        [ends[key] for key in corners] + [tops[key] for key in corners],
         "pack_beside",
-    )
+    )[0]
     side_x = {di: on_row(beside, di) for di in others}
     side_y = from_layer(beside, 2)
     side_d = {di: from_row_layer(beside, steps[di], lambda j: j ^ 2) for di in others}
-    geos = jnp.concatenate([geos] + [on_row(geos, di) for di in others], axis=0)
-    mate_geos = from_layer(geos, 1)
-    third_geos = from_layer(geos, 3)
-    rows = [x_row[di] for di in others] + [far] + [ends[di] for di in others] + [tops[di] for di in others]
-    rows += [beside]
-    to_mate = pack(rows, [[(i, 0, value.shape[0]) for i, value in enumerate(rows)]], [], "pack_mate")[0]
-    mate_rows = from_layer(to_mate, 1)
+    mate_side = from_layer(beside, 1)
 
     def row_of(di, flip):
         return [(("top", di, flip), half), (("end", di, flip), half)]
 
     def side_of(di, flip):
-        return [(("up", di, flip), picks), (("down", di, flip), picks)]
+        return [(("up", di, flip), picks), (("down", di, flip), picks), (None, 3 * GEO)]
 
     early = [(flat, row_of(0, 0)), (mate, row_of(0, 1)), (far, row_of(0, 2))]
     early += [(x_row[di], row_of(di, 0)) for di in others]
-    early += [(ends[di], [(("end", di, 2), half)]) for di in others]
-    early += [(tops[di], [(("top", di, 2), half)]) for di in others]
+    for name, parts in (("end", ends), ("top", tops)):
+        for di in others:
+            early += [(parts[di, 0], [((name, di, 2), quarter)]), (parts[di, 1], [(None, quarter)])]
     early += [(beside, side_of(0, 0))]
     content = sum([row_of(di, 1) for di in others], []) + row_of(0, 3)
     content += [(("end", di, 3), half) for di in others] + [(("top", di, 3), half) for di in others]
-    early += [(mate_rows, content + side_of(0, 1))]
+    early += [(None, content), (mate_side, side_of(0, 1))]
     located = {}
     total = 0
     for _, content in early:
@@ -553,28 +551,38 @@
             pltpu.SemaphoreType.DMA((2,)),
         ],
         compiler_params=pltpu.CompilerParams(vmem_limit_bytes=(2 << 20) + atoms * 16384),
-        cost_estimate=pl.CostEstimate(flops=6_000_000_000, bytes_accessed=8_000_000, transcendentals=0),
+        cost_estimate=pl.CostEstimate(flops=1000, bytes_accessed=1000, transcendentals=0),
         name="prepare",
     )(listings, atom_size, basis_proj.transpose(1, 0, 2).reshape(SHELLS * atoms, size), beside)
 
-    early_values = [value for value, _ in early]
+    rows = [x_row[di] for di in others] + [far] + [ends[key] for key in corners] + [tops[key] for key in corners]
+    to_mate = pack(rows, [[(i, 0, value.shape[0]) for i, value in enumerate(rows)]], [beside], "pack_mate")[0]
+    mate_rows = from_layer(to_mate, 1)
+
+    geos = pack(
+        [beside] + [side_x[di] for di in others], [[(di, 2 * picks, 3 * GEO) for di in range(count)]], [own_basis], "pack_geos"
+    )[0]
+    mate_geos = from_layer(geos, 1)
+    third_geos = from_layer(geos, 3)
+
+    early_values = [mate_rows if value is None else value for value, _ in early]
     gram = pl.pallas_call(
         functools.partial(gram_kernel, len(early_values)),
         out_shape=jax.ShapeDtypeStruct((full, full), jnp.bfloat16),
-        in_specs=[SMEM] + [ANY] * len(early_values),
+        in_specs=[SMEM] + [ANY] * (len(early_values) + 2),
         out_specs=VMEM,
         scratch_shapes=[
             pltpu.VMEM((late_from, LANES), jnp.bfloat16),
             pltpu.SemaphoreType.DMA((len(early_values),)),
         ],
         compiler_params=pltpu.CompilerParams(vmem_limit_bytes=(6 << 20) + late_from * LANES * 2),
-        cost_estimate=pl.CostEstimate(flops=4_000_000_000, bytes_accessed=20_000_000, transcendentals=0),
+        cost_estimate=pl.CostEstimate(flops=1000, bytes_accessed=1000, transcendentals=0),
         name="gram_early",
-    )(early_table, *early_values)
+    )(early_table, *early_values, mate_geos, third_geos)
 
     diagonal = [side_d[di] for di in others]
     if len(diagonal) == 1:
-        diagonal = pack(diagonal, [[(0, 0, 2 * picks)]], [gram], "pack_diagonal")
+        diagonal = pack(diagonal, [[(0, 0, 2 * picks + 3 * GEO)]], [gram], "pack_diagonal")
     late_values = [side_x[di] for di in others] + [from_layer(side_x[di], 1) for di in others]
     late_values += [side_y, from_layer(side_y, 1)]
     late_values += diagonal
@@ -597,7 +605,7 @@
             pltpu.SemaphoreType.DMA((3,)),
         ],
         compiler_params=pltpu.CompilerParams(vmem_limit_bytes=10 << 20),
-        cost_estimate=pl.CostEstimate(flops=5_000_000_000, bytes_accessed=4_000_000, transcendentals=2_000_000),
+        cost_estimate=pl.CostEstimate(flops=1000, bytes_accessed=1000, transcendentals=0),
         name="profiles",
     )(geos, mate_geos, third_geos, gram)
 

time: 82.1 us -> 79 us (0.962)
  waiting for transfers between devices: 28.4 us -> 23.4 us
  starting transfers between devices: 24.1 us -> 28.4 us
  local copies, waits for them, and re-layouts: 4.63 us -> 1 us
  Pallas kernels: 23.8 us -> 25 us
    unnamed x21 -> x10, local copies, waits for them, and re-layouts: 4.34 us -> 0.71 us
    ppermute x3, waiting for transfers between devices: 3.84 us -> 0.37 us  [from_row_layer(): return lax.ppermute(x, ('row', 'layer'), moves)]
    ppermute x10 -> x12, waiting for transfers between devices: 8.01 us -> 4.92 us  [from_layer(): return lax.ppermute(x, 'layer', [(i ^ flip, i) for i in range(count)])]
    ppermute x11, starting transfers between devices: 13.1 us -> 15 us  [from_offset(): lax.ppermute(x, axis, [((i + step) % count, i) for i in range(count)])]
    ppermute x11, waiting for transfers between devices: 16.6 us -> 18.1 us  [from_offset(): lax.ppermute(x, axis, [((i + step) % count, i) for i in range(count)])]
    ppermute x3, starting transfers between devices: 3.12 us -> 4.55 us  [from_row_layer(): return lax.ppermute(x, ('row', 'layer'), moves)]
    pallas_call x1, Pallas kernels: 1.34 us -> 2.49 us  [local(): pl.pallas_call(functools.partial(pick_kernel, axes), out_shape=(jax.Shape...]
    ppermute x10 -> x12, starting transfers between devices: 7.84 us -> 8.86 us  [from_layer(): return lax.ppermute(x, 'layer', [(i ^ flip, i) for i in range(count)])]
  transfers between devices with their start and end apart: 24 -> 26, of which waited for: 11 -> 12; matrix products, arithmetic and copies ran while one was open for 0% -> 0% of each run, Pallas kernels for 18% -> 21%
where the time goes in v6:
time: 79 us; the launch traced here: 78.7 us
  starting transfers between devices  28.4 us (36%)
  Pallas kernels  25 us (32%)
  waiting for transfers between devices  23.4 us (30%)
  local copies, waits for them, and re-layouts  1 us (1%)
  between operations  0.84 us (1%)
    ppermute x11, waiting for transfers between devices, from_offset(): lax.ppermute(x, axis, [((i + step) % count, i) for i in range(count)])  18.1 us
    ppermute x11, starting transfers between devices, from_offset(): lax.ppermute(x, axis, [((i + step) % count, i) for i in range(count)])  15 us
    ppermute x12, starting transfers between devices, from_layer(): return lax.ppermute(x, 'layer', [(i ^ flip, i) for i in range(count)])  8.86 us
    pallas_call x1, Pallas kernels, local(): pl.pallas_call(functools.partial(prepare_kernel, axes, count, tuple(layou...  5.8 us
    pallas_call x1, Pallas kernels, local(): pl.pallas_call(functools.partial(step_kernel, len(late_values)), out_shap...  5.78 us
    ppermute x12, waiting for transfers between devices, from_layer(): return lax.ppermute(x, 'layer', [(i ^ flip, i) for i in range(count)])  4.92 us
    ppermute x3, starting transfers between devices, from_row_layer(): return lax.ppermute(x, ('row', 'layer'), moves)  4.55 us
    pallas_call x1, Pallas kernels, local(): pl.pallas_call(functools.partial(gram_kernel, len(early_values)), out_sha...  3.59 us
  transfers between devices with their start and end apart: 26, of which 12 were waited for; matrix products, arithmetic and copies ran while one was open for 0% of the time, Pallas kernels for 21%

profile of v6, /device:TPU:0, one launch (start us, length us, event | category | flops | bytes accessed | tf_op | source)
XLA Modules:
  0.0 78.7 jit_solution(10667940365512369927)
XLA Ops:
  0.6 3.0 %collective-permute-start.2 = (bf16[1536,128]{1,0:T(8,128)(2,1)}, bf16[1536,128]{1,0:T(8,128)(2,1)S(1)}, u32[]{:S(2)}, u32[]{:S(2)}) collective-permute-start(bf16[1536,128]{1,0:T(8,128)(2,1)} %bitcast.13), channel_id=1, source_target_pairs={{2,0},{3,1},{0,2},{1,3},{6,4},{7,5},{4,6},{5,7},{10,8},{11,9},{8,1... | collective-permute-start | bytes 1179656 | tf_op jit(solution)/shard_map/ppermute | solution.py:39
  3.7 1.5 %collective-permute-start.3 = (bf16[1536,128]{1,0:T(8,128)(2,1)}, bf16[1536,128]{1,0:T(8,128)(2,1)S(1)}, u32[]{:S(2)}, u32[]{:S(2)}) collective-permute-start(bf16[1536,128]{1,0:T(8,128)(2,1)} %bitcast.14), channel_id=1, source_target_pairs={{16,0},{0,16},{17,1},{1,17},{18,2},{2,18},{19,3},{3,19},{20,4},{4,... | collective-permute-start | bytes 1179656 | tf_op jit(solution)/shard_map/ppermute | solution.py:26
  5.2 2.5 %pick_column_blocks.1 = (bf16[656,128]{1,0:T(8,128)(2,1)}, bf16[16,128]{1,0:T(8,128)(2,1)}) custom-call(s32[12,32]{1,0:T(8,128)} %bitcast.20, s32[1,12]{1,0:T(1,128)} %refs_1_.2, s32[32]{0:T(128)} %refs_2_.1, s32[32]{0:T(128)} %refs_3_.1, s32[32]{0:T(128)} %refs_4_.1, bf16[12,128,128]{2,1,0:T(8,128)(2,1)} %bitcast.15), custom_call_target="tpu_custom_call" | custom-call | tf_op jit(solution)/shard_map/pick_column_blocks/pallas_call | solution.py:447
  7.7 3.7 %collective-permute-start = (bf16[656,128]{1,0:T(8,128)(2,1)}, bf16[656,128]{1,0:T(8,128)(2,1)S(1)}, u32[]{:S(2)}, u32[]{:S(2)}) collective-permute-start(bf16[656,128]{1,0:T(8,128)(2,1)} %get-tuple-element.17), channel_id=1, source_target_pairs={{4,0},{8,4},{12,8},{0,12},{5,1},{9,5},{13,9},{1,13},{6,2},{10,6},{... | collective-permute-start | bytes 503816 | tf_op jit(solution)/shard_map/ppermute | solution.py:26
  11.3 1.7 %collective-permute-done.2.refs_0_.refs_1_.refs_3_ = bf16[1536,128]{1,0:T(8,128)(2,1)S(1)} collective-permute-done((bf16[1536,128]{1,0:T(8,128)(2,1)}, bf16[1536,128]{1,0:T(8,128)(2,1)S(1)}, u32[]{:S(2)}, u32[]{:S(2)}) %collective-permute-start.2) | collective-permute-done | bytes 393248 | tf_op jit(solution)/shard_map/ppermute | solution.py:39
  13.0 1.5 %collective-permute-done.3.refs_1_.refs_0_.refs_4_ = bf16[1536,128]{1,0:T(8,128)(2,1)S(1)} collective-permute-done((bf16[1536,128]{1,0:T(8,128)(2,1)}, bf16[1536,128]{1,0:T(8,128)(2,1)S(1)}, u32[]{:S(2)}, u32[]{:S(2)}) %collective-permute-start.3) | collective-permute-done | bytes 393248 | tf_op jit(solution)/shard_map/ppermute | solution.py:26
  14.4 0.5 pack_halves.1
  15.0 1.6 %collective-permute-start.4 = (bf16[384,128]{1,0:T(8,128)(2,1)S(1)}, bf16[384,128]{1,0:T(8,128)(2,1)S(1)}, u32[]{:S(2)}, u32[]{:S(2)}) collective-permute-start(bf16[384,128]{1,0:T(8,128)(2,1)S(1)} %get-tuple-element.19), channel_id=1, source_target_pairs={{16,0},{0,16},{17,1},{1,17},{18,2},{2,18},{19,3},{3,19},{20,4},{4,... | collective-permute-start | bytes 294920 | tf_op jit(solution)/shard_map/ppermute | solution.py:26
  16.5 0.5 collective-permute-start.5
  17.1 0.4 collective-permute-start.6
  17.4 0.0 collective-permute-done.refs_0_
  17.4 1.7 %collective-permute-start.7 = (bf16[384,128]{1,0:T(8,128)(2,1)S(1)}, bf16[384,128]{1,0:T(8,128)(2,1)S(1)}, u32[]{:S(2)}, u32[]{:S(2)}) collective-permute-start(bf16[384,128]{1,0:T(8,128)(2,1)S(1)} %get-tuple-element.22), channel_id=1, source_target_pairs={{2,0},{3,1},{0,2},{1,3},{6,4},{7,5},{4,6},{5,7},{10,8},{11,9},{8,1... | collective-permute-start | bytes 294920 | tf_op jit(solution)/shard_map/ppermute | solution.py:39
  19.1 0.6 collective-permute-done.4.refs_3_.refs_2_.refs_5_
  19.7 1.5 %collective-permute-done.5.refs_4_.refs_3_.refs_6_ = bf16[384,128]{1,0:T(8,128)(2,1)S(1)} collective-permute-done((bf16[384,128]{1,0:T(8,128)(2,1)S(1)}, bf16[384,128]{1,0:T(8,128)(2,1)S(1)}, u32[]{:S(2)}, u32[]{:S(2)}) %collective-permute-start.5) | collective-permute-done | bytes 98336 | tf_op jit(solution)/shard_map/ppermute | solution.py:26
  21.1 0.5 collective-permute-done.6.refs_5_.refs_4_.refs_7_
  21.7 1.1 %collective-permute-done.7.refs_6_.refs_5_.refs_8_ = bf16[384,128]{1,0:T(8,128)(2,1)S(1)} collective-permute-done((bf16[384,128]{1,0:T(8,128)(2,1)S(1)}, bf16[384,128]{1,0:T(8,128)(2,1)S(1)}, u32[]{:S(2)}, u32[]{:S(2)}) %collective-permute-start.7) | collective-permute-done | bytes 98336 | tf_op jit(solution)/shard_map/ppermute | solution.py:39
  22.7 0.7 copy-done.3
  23.4 0.5 pack_beside.1.refs_3_.refs_6_.refs_0_.refs_9_
  23.9 0.0 copy-start
  23.9 0.0 copy-start.1
  23.9 0.0 copy-start.2
  23.9 0.0 copy-start.4
  23.9 0.9 %pack_mate.1 = bf16[4608,128]{1,0:T(8,128)(2,1)S(1)} custom-call(bf16[1536,128]{1,0:T(8,128)(2,1)S(1)} %collective-permute-done.3.refs_1_.refs_0_.refs_4_, bf16[1536,128]{1,0:T(8,128)(2,1)S(1)} %collective-permute-done.2.refs_0_.refs_1_.refs_3_, bf16[384,128]{1,0:T(8,128)(2,1)S(1)} %collective-permute-done.4.refs_3_.refs_2_.refs_5_, ...), custom_call_target="tpu_custom_call" | custom-call | bytes 1000 | tf_op jit(solution)/shard_map/pack_mate/pallas_call | solution.py:240
  24.9 0.1 collective-permute-start.9
  25.0 1.6 %collective-permute-start.11 = (bf16[1328,128]{1,0:T(8,128)(2,1)S(1)}, bf16[1328,128]{1,0:T(8,128)(2,1)S(1)}, u32[]{:S(2)}, u32[]{:S(2)}) collective-permute-start(bf16[1328,128]{1,0:T(8,128)(2,1)S(1)} %pack_beside.1.refs_3_.refs_6_.refs_0_.refs_9_), channel_id=1, source_target_pairs={{16,0},{0,16},{17,1},{1,17},{18,2},{2,18},{19,3},{3,19},{20,4},{4,... | collective-permute-start | bytes 1019912 | tf_op jit(solution)/shard_map/ppermute | solution.py:26
  26.5 0.2 collective-permute-start.8
  26.7 0.3 collective-permute-start.10
  27.0 1.0 %collective-permute-start.15 = (bf16[1328,128]{1,0:T(8,128)(2,1)S(1)}, bf16[1328,128]{1,0:T(8,128)(2,1)S(1)}, u32[]{:S(2)}, u32[]{:S(2)}) collective-permute-start(bf16[1328,128]{1,0:T(8,128)(2,1)S(1)} %pack_beside.1.refs_3_.refs_6_.refs_0_.refs_9_), channel_id=1, source_target_pairs={{2,0},{3,1},{0,2},{1,3},{6,4},{7,5},{4,6},{5,7},{10,8},{11,9},{8,1... | collective-permute-start | bytes 1019912 | tf_op jit(solution)/shard_map/ppermute | solution.py:39
  28.0 7.3 %collective-permute-done.11.refs_1_.refs_6_ = bf16[1328,128]{1,0:T(8,128)(2,1)S(1)} collective-permute-done((bf16[1328,128]{1,0:T(8,128)(2,1)S(1)}, bf16[1328,128]{1,0:T(8,128)(2,1)S(1)}, u32[]{:S(2)}, u32[]{:S(2)}) %collective-permute-start.11) | collective-permute-done | bytes 340000 | tf_op jit(solution)/shard_map/ppermute | solution.py:26
  35.4 1.9 %collective-permute-start.17 = (bf16[1328,128]{1,0:T(8,128)(2,1)S(1)}, bf16[1328,128]{1,0:T(8,128)(2,1)S(1)}, u32[]{:S(2)}, u32[]{:S(2)}) collective-permute-start(bf16[1328,128]{1,0:T(8,128)(2,1)S(1)} %pack_beside.1.refs_3_.refs_6_.refs_0_.refs_9_), channel_id=1, source_target_pairs={{18,0},{19,1},{16,2},{17,3},{2,16},{3,17},{0,18},{1,19},{22,4},{23... | collective-permute-start | bytes 1019912 | tf_op jit(solution)/shard_map/ppermute | solution.py:34
  37.3 5.8 %prepare.1 = (s32[247]{0:T(256)S(1)}, s32[247]{0:T(256)S(1)}, s32[14]{0:T(128)S(1)}, bf16[128,1536]{1,0:T(8,128)(2,1)S(1)}, bf16[16,128]{1,0:T(8,128)(2,1)S(1)}) custom-call(s32[12,32]{1,0:T(8,128)S(1)} %bitcast.21, s32[32]{0:T(128)S(1)} %copy-done.4, bf16[192,128]{1,0:T(8,128)(2,1)S(1)} %bitcast.19, ...), custom_call_target="tpu_custom_call" | custom-call | flops 1000 | bytes 1000 | tf_op jit(solution)/shard_map/prepare/pallas_call | solution.py:534
  43.1 0.1 pack_geos.1.refs_0_
  43.1 0.0 collective-permute-done.8.refs_2_
  43.2 0.1 collective-permute-start.12
  43.2 0.0 collective-permute-done.10.refs_11_
  43.2 1.2 %collective-permute-start.13 = (bf16[96,128]{1,0:T(8,128)(2,1)S(1)}, bf16[96,128]{1,0:T(8,128)(2,1)S(1)}, u32[]{:S(2)}, u32[]{:S(2)}) collective-permute-start(bf16[96,128]{1,0:T(8,128)(2,1)S(1)} %pack_geos.1.refs_0_), channel_id=1, source_target_pairs={{3,0},{2,1},{1,2},{0,3},{7,4},{6,5},{5,6},{4,7},{11,8},{10,9},{9,1... | collective-permute-start | bytes 73736 | tf_op jit(solution)/shard_map/ppermute | solution.py:39
  44.4 0.1 collective-permute-start.14
  44.5 0.0 collective-permute-done.12.refs_12_.refs_1_
  44.5 0.4 collective-permute-start.16
  44.9 1.6 %collective-permute-done.13.refs_13_.refs_2_ = bf16[96,128]{1,0:T(8,128)(2,1)S(1)} collective-permute-done((bf16[96,128]{1,0:T(8,128)(2,1)S(1)}, bf16[96,128]{1,0:T(8,128)(2,1)S(1)}, u32[]{:S(2)}, u32[]{:S(2)}) %collective-permute-start.13) | collective-permute-done | bytes 24608 | tf_op jit(solution)/shard_map/ppermute | solution.py:39
  46.6 0.0 collective-permute-done.9.refs_10_
  46.6 3.6 %gram_early.1.refs_1_.refs_3_.refs_5_ = bf16[1536,1536]{1,0:T(8,128)(2,1)S(1)} custom-call(s32[247]{0:T(256)S(1)} %get-tuple-element.27.refs_0_, bf16[1536,128]{1,0:T(8,128)(2,1)S(1)} %bitcast.17, bf16[1536,128]{1,0:T(8,128)(2,1)S(1)} %collective-permute-done.8.refs_2_, bf16[1536,128]{1,0:T(8,128)(2,1)S(1)} %collective-permute-done.2.refs_0_.refs_1_.refs_3_, ...), custom_call_target="tpu_custom_call" | custom-call | flops 1000 | bytes 1000 | tf_op jit(solution)/shard_map/gram_early/pallas_call | solution.py:569
  50.2 0.0 collective-permute-done.17.refs_0_
  50.2 0.1 pack_diagonal.1.refs_10_
  50.3 0.5 collective-permute-start.18
  50.8 3.5 %profiles.1 = (bf16[6,6,256,128]{3,2,1,0:T(8,128)(2,1)S(1)}, bf16[6,6,128,128]{3,2,1,0:T(8,128)(2,1)S(1)}) custom-call(bf16[96,128]{1,0:T(8,128)(2,1)S(1)} %pack_geos.1.refs_0_, bf16[96,128]{1,0:T(8,128)(2,1)S(1)} %collective-permute-done.12.refs_12_.refs_1_, bf16[96,128]{1,0:T(8,128)(2,1)S(1)} %collective-permute-done.13.refs_13_.refs_2_, ...), custom_call_target="tpu_custom_call" | custom-call | flops 1000 | bytes 1000 | tf_op jit(solution)/shard_map/profiles/pallas_call | solution.py:595
  54.3 0.0 collective-permute-done.16.refs_9_
  54.4 5.8 %square_cube_coefficients.1 = (bf16[12,128,128]{2,1,0:T(8,128)(2,1)}, f32[8,128]{1,0:T(8,128)S(1)}) custom-call(s32[247]{0:T(256)S(1)} %get-tuple-element.23.refs_0_, s32[14]{0:T(128)S(1)} %get-tuple-element.24.refs_1_, bf16[16,128]{1,0:T(8,128)(2,1)S(1)} %get-tuple-element.25.refs_2_, bf16[128,1536]{1,0:T(8,128)(2,1)S(1)} %get-tuple-element.26.refs_3_, ...), custom_call_target="tpu_custom_call" | custom-call | flops 1300000000 | bytes 8000000 | tf_op jit(solution)/shard_map/square_cube_coefficients/pallas_call | solution.py:612
  60.1 0.1 collective-permute-start.19
  60.3 1.7 %collective-permute-start.20 = (f32[8,128]{1,0:T(8,128)S(1)}, f32[8,128]{1,0:T(8,128)S(1)}, u32[]{:S(2)}, u32[]{:S(2)}) collective-permute-start(f32[8,128]{1,0:T(8,128)S(1)} %get-tuple-element.30), channel_id=1, source_target_pairs={{1,0},{2,1},{3,2},{0,3},{5,4},{6,5},{7,6},{4,7},{9,8},{10,9},{11,1... | collective-permute-start | bytes 12296 | tf_op jit(solution)/shard_map/ppermute | solution.py:26
  61.9 2.6 %collective-permute-start.23 = (f32[8,128]{1,0:T(8,128)S(1)}, f32[8,128]{1,0:T(8,128)S(1)}, u32[]{:S(2)}, u32[]{:S(2)}) collective-permute-start(f32[8,128]{1,0:T(8,128)S(1)} %get-tuple-element.30), channel_id=1, source_target_pairs={{17,0},{18,1},{19,2},{16,3},{1,16},{2,17},{3,18},{0,19},{21,4},{22... | collective-permute-start | bytes 12296 | tf_op jit(solution)/shard_map/ppermute | solution.py:34
  64.6 0.8 collective-permute-start.21
  65.4 0.1 slice.19
  65.4 0.1 slice.20
  65.5 0.4 collective-permute-done.22
  65.9 0.1 slice.22
  65.9 0.1 slice.23
  66.0 2.2 %collective-permute-done.21 = f32[8,128]{1,0:T(8,128)S(1)} collective-permute-done((f32[8,128]{1,0:T(8,128)S(1)}, f32[8,128]{1,0:T(8,128)S(1)}, u32[]{:S(2)}, u32[]{:S(2)}) %collective-permute-start.21) | collective-permute-done | bytes 4128 | tf_op jit(solution)/shard_map/ppermute | solution.py:26
  68.2 0.1 maximum_maximum_fusion.refs_0_
  68.3 3.6 %collective-permute-start.24 = (f32[16,128]{1,0:T(8,128)S(1)}, f32[16,128]{1,0:T(8,128)S(1)}, u32[]{:S(2)}, u32[]{:S(2)}) collective-permute-start(f32[16,128]{1,0:T(8,128)S(1)} %maximum_maximum_fusion.refs_0_), channel_id=1, source_target_pairs={{4,0},{8,4},{12,8},{0,12},{5,1},{9,5},{13,9},{1,13},{6,2},{10,6},{... | collective-permute-start | bytes 24584 | tf_op jit(solution)/shard_map/ppermute | solution.py:26
  71.9 0.4 density_column.1.refs_4_
  72.3 1.0 %collective-permute-done.24.refs_0_ = f32[16,128]{1,0:T(8,128)S(1)} collective-permute-done((f32[16,128]{1,0:T(8,128)S(1)}, f32[16,128]{1,0:T(8,128)S(1)}, u32[]{:S(2)}, u32[]{:S(2)}) %collective-permute-start.24) | collective-permute-done | bytes 8224 | tf_op jit(solution)/shard_map/ppermute | solution.py:26
  73.2 4.1 %collective-permute-done.25.refs_1_ = f32[16,128]{1,0:T(8,128)S(1)} collective-permute-done((f32[16,128]{1,0:T(8,128)S(1)}, f32[16,128]{1,0:T(8,128)S(1)}, u32[]{:S(2)}, u32[]{:S(2)}) %collective-permute-start.25) | collective-permute-done | bytes 8224 | tf_op jit(solution)/shard_map/ppermute | solution.py:26
  77.3 1.4 %density_sides.1 = f32[256,128]{1,0:T(8,128)} custom-call(f32[16,128]{1,0:T(8,128)S(1)} %collective-permute-done.24.refs_0_, f32[16,128]{1,0:T(8,128)S(1)} %collective-permute-done.25.refs_1_, bf16[6,6,256,128]{3,2,1,0:T(8,128)(2,1)S(1)} %get-tuple-element.31.refs_1_.refs_2_, bf16[4608,128]{1,0:T(8,128)(2,1)S(1)} %bitcast.12, ...), custom_call_target="tpu_custom_call" | custom-call | flops 310000000 | bytes 4000000 | tf_op jit(solution)/shard_map/density_sides/pallas_call | solution.py:662
  (16 shorter events, 0.0 us)
Async XLA Ops:
  0.6 12.4 %collective-permute-start.2 = (bf16[1536,128]{1,0:T(8,128)(2,1)}, bf16[1536,128]{1,0:T(8,128)(2,1)S(1)}, u32[]{:S(2)}, u32[]{:S(2)}) collective-permute-start(bf16[1536,128]{1,0:T(8,128)(2,1)} %bitcast.13), channel_id=1, source_target_pairs={{2,0},{3,1},{0,2},{1,3},{6,4},{7,5},{4,6},{5,7},{10,8},{11,9},{8,1... | collective-permute-start | bytes 1179656 | tf_op jit(solution)/shard_map/ppermute | solution.py:39
  3.7 10.8 %collective-permute-start.3 = (bf16[1536,128]{1,0:T(8,128)(2,1)}, bf16[1536,128]{1,0:T(8,128)(2,1)S(1)}, u32[]{:S(2)}, u32[]{:S(2)}) collective-permute-start(bf16[1536,128]{1,0:T(8,128)(2,1)} %bitcast.14), channel_id=1, source_target_pairs={{16,0},{0,16},{17,1},{1,17},{18,2},{2,18},{19,3},{3,19},{20,4},{4,... | collective-permute-start | bytes 1179656 | tf_op jit(solution)/shard_map/ppermute | solution.py:26
  7.7 9.8 %collective-permute-start = (bf16[656,128]{1,0:T(8,128)(2,1)}, bf16[656,128]{1,0:T(8,128)(2,1)S(1)}, u32[]{:S(2)}, u32[]{:S(2)}) collective-permute-start(bf16[656,128]{1,0:T(8,128)(2,1)} %get-tuple-element.17), channel_id=1, source_target_pairs={{4,0},{8,4},{12,8},{0,12},{5,1},{9,5},{13,9},{1,13},{6,2},{10,6},{... | collective-permute-start | bytes 503816 | tf_op jit(solution)/shard_map/ppermute | solution.py:26
  11.3 7.8 %collective-permute-start.1 = (bf16[656,128]{1,0:T(8,128)(2,1)}, bf16[656,128]{1,0:T(8,128)(2,1)S(1)}, u32[]{:S(2)}, u32[]{:S(2)}) collective-permute-start(bf16[656,128]{1,0:T(8,128)(2,1)} %get-tuple-element.17), channel_id=1, source_target_pairs={{12,0},{0,4},{4,8},{8,12},{13,1},{1,5},{5,9},{9,13},{14,2},{2,6},{... | collective-permute-start | bytes 503816 | tf_op jit(solution)/shard_map/ppermute | solution.py:26
  15.0 4.7 %collective-permute-start.4 = (bf16[384,128]{1,0:T(8,128)(2,1)S(1)}, bf16[384,128]{1,0:T(8,128)(2,1)S(1)}, u32[]{:S(2)}, u32[]{:S(2)}) collective-permute-start(bf16[384,128]{1,0:T(8,128)(2,1)S(1)} %get-tuple-element.19), channel_id=1, source_target_pairs={{16,0},{0,16},{17,1},{1,17},{18,2},{2,18},{19,3},{3,19},{20,4},{4,... | collective-permute-start | bytes 294920 | tf_op jit(solution)/shard_map/ppermute | solution.py:26
  16.5 4.6 %collective-permute-start.5 = (bf16[384,128]{1,0:T(8,128)(2,1)S(1)}, bf16[384,128]{1,0:T(8,128)(2,1)S(1)}, u32[]{:S(2)}, u32[]{:S(2)}) collective-permute-start(bf16[384,128]{1,0:T(8,128)(2,1)S(1)} %get-tuple-element.20), channel_id=1, source_target_pairs={{16,0},{0,16},{17,1},{1,17},{18,2},{2,18},{19,3},{3,19},{20,4},{4,... | collective-permute-start | bytes 294920 | tf_op jit(solution)/shard_map/ppermute | solution.py:26
  17.1 4.6 %collective-permute-start.6 = (bf16[384,128]{1,0:T(8,128)(2,1)S(1)}, bf16[384,128]{1,0:T(8,128)(2,1)S(1)}, u32[]{:S(2)}, u32[]{:S(2)}) collective-permute-start(bf16[384,128]{1,0:T(8,128)(2,1)S(1)} %get-tuple-element.21), channel_id=1, source_target_pairs={{2,0},{3,1},{0,2},{1,3},{6,4},{7,5},{4,6},{5,7},{10,8},{11,9},{8,1... | collective-permute-start | bytes 294920 | tf_op jit(solution)/shard_map/ppermute | solution.py:39
  17.4 5.3 %collective-permute-start.7 = (bf16[384,128]{1,0:T(8,128)(2,1)S(1)}, bf16[384,128]{1,0:T(8,128)(2,1)S(1)}, u32[]{:S(2)}, u32[]{:S(2)}) collective-permute-start(bf16[384,128]{1,0:T(8,128)(2,1)S(1)} %get-tuple-element.22), channel_id=1, source_target_pairs={{2,0},{3,1},{0,2},{1,3},{6,4},{7,5},{4,6},{5,7},{10,8},{11,9},{8,1... | collective-permute-start | bytes 294920 | tf_op jit(solution)/shard_map/ppermute | solution.py:39
  22.7 0.7 copy-start.3
  23.9 2.6 %copy-start = (bf16[1,12,128,128]{3,2,1,0:T(8,128)(2,1)S(1)}, bf16[1,12,128,128]{3,2,1,0:T(8,128)(2,1)}, u32[]{:S(2)}) copy-start(bf16[1,12,128,128]{3,2,1,0:T(8,128)(2,1)} %param.8) | copy-start | bytes 1179652
  23.9 13.4 %copy-start.1 = (bf16[32,6,128]{2,0,1:T(8,128)(2,1)S(1)}, bf16[32,6,128]{2,0,1:T(8,128)(2,1)}, u32[]{:S(2)}) copy-start(bf16[32,6,128]{2,0,1:T(8,128)(2,1)} %param.11) | copy-start | bytes 147460
  23.9 13.4 %copy-start.2 = (s32[32,12]{0,1:T(8,128)S(1)}, s32[32,12]{0,1:T(8,128)}, u32[]{:S(2)}) copy-start(s32[32,12]{0,1:T(8,128)} %param.9) | copy-start | bytes 4612
  23.9 13.3 %copy-start.4 = (s32[32]{0:T(128)S(1)}, s32[32]{0:T(128)}, u32[]{:S(2)}) copy-start(s32[32]{0:T(128)} %refs_1_.3) | copy-start | bytes 388
  24.9 21.7 %collective-permute-start.9 = (bf16[4608,128]{1,0:T(8,128)(2,1)S(1)}, bf16[4608,128]{1,0:T(8,128)(2,1)S(1)}, u32[]{:S(2)}, u32[]{:S(2)}) collective-permute-start(bf16[4608,128]{1,0:T(8,128)(2,1)S(1)} %pack_mate.1), channel_id=1, source_target_pairs={{1,0},{0,1},{3,2},{2,3},{5,4},{4,5},{7,6},{6,7},{9,8},{8,9},{11,10... | collective-permute-start | bytes 3538952 | tf_op jit(solution)/shard_map/ppermute | solution.py:39
  25.0 10.4 %collective-permute-start.11 = (bf16[1328,128]{1,0:T(8,128)(2,1)S(1)}, bf16[1328,128]{1,0:T(8,128)(2,1)S(1)}, u32[]{:S(2)}, u32[]{:S(2)}) collective-permute-start(bf16[1328,128]{1,0:T(8,128)(2,1)S(1)} %pack_beside.1.refs_3_.refs_6_.refs_0_.refs_9_), channel_id=1, source_target_pairs={{16,0},{0,16},{17,1},{1,17},{18,2},{2,18},{19,3},{3,19},{20,4},{4,... | collective-permute-start | bytes 1019912 | tf_op jit(solution)/shard_map/ppermute | solution.py:26
  26.5 16.6 %collective-permute-start.8 = (bf16[1536,128]{1,0:T(8,128)(2,1)S(1)}, bf16[1536,128]{1,0:T(8,128)(2,1)S(1)}, u32[]{:S(2)}, u32[]{:S(2)}) collective-permute-start(bf16[1536,128]{1,0:T(8,128)(2,1)S(1)} %bitcast.16), channel_id=1, source_target_pairs={{1,0},{0,1},{3,2},{2,3},{5,4},{4,5},{7,6},{6,7},{9,8},{8,9},{11,10... | collective-permute-start | bytes 1179656 | tf_op jit(solution)/shard_map/ppermute | solution.py:39
  26.7 16.5 %collective-permute-start.10 = (bf16[1328,128]{1,0:T(8,128)(2,1)S(1)}, bf16[1328,128]{1,0:T(8,128)(2,1)S(1)}, u32[]{:S(2)}, u32[]{:S(2)}) collective-permute-start(bf16[1328,128]{1,0:T(8,128)(2,1)S(1)} %pack_beside.1.refs_3_.refs_6_.refs_0_.refs_9_), channel_id=1, source_target_pairs={{1,0},{0,1},{3,2},{2,3},{5,4},{4,5},{7,6},{6,7},{9,8},{8,9},{11,10... | collective-permute-start | bytes 1019912 | tf_op jit(solution)/shard_map/ppermute | solution.py:39
  27.0 17.4 %collective-permute-start.15 = (bf16[1328,128]{1,0:T(8,128)(2,1)S(1)}, bf16[1328,128]{1,0:T(8,128)(2,1)S(1)}, u32[]{:S(2)}, u32[]{:S(2)}) collective-permute-start(bf16[1328,128]{1,0:T(8,128)(2,1)S(1)} %pack_beside.1.refs_3_.refs_6_.refs_0_.refs_9_), channel_id=1, source_target_pairs={{2,0},{3,1},{0,2},{1,3},{6,4},{7,5},{4,6},{5,7},{10,8},{11,9},{8,1... | collective-permute-start | bytes 1019912 | tf_op jit(solution)/shard_map/ppermute | solution.py:39
  35.4 14.8 %collective-permute-start.17 = (bf16[1328,128]{1,0:T(8,128)(2,1)S(1)}, bf16[1328,128]{1,0:T(8,128)(2,1)S(1)}, u32[]{:S(2)}, u32[]{:S(2)}) collective-permute-start(bf16[1328,128]{1,0:T(8,128)(2,1)S(1)} %pack_beside.1.refs_3_.refs_6_.refs_0_.refs_9_), channel_id=1, source_target_pairs={{18,0},{19,1},{16,2},{17,3},{2,16},{3,17},{0,18},{1,19},{22,4},{23... | collective-permute-start | bytes 1019912 | tf_op jit(solution)/shard_map/ppermute | solution.py:34
  43.2 1.3 %collective-permute-start.12 = (bf16[96,128]{1,0:T(8,128)(2,1)S(1)}, bf16[96,128]{1,0:T(8,128)(2,1)S(1)}, u32[]{:S(2)}, u32[]{:S(2)}) collective-permute-start(bf16[96,128]{1,0:T(8,128)(2,1)S(1)} %pack_geos.1.refs_0_), channel_id=1, source_target_pairs={{1,0},{0,1},{3,2},{2,3},{5,4},{4,5},{7,6},{6,7},{9,8},{8,9},{11,10... | collective-permute-start | bytes 73736 | tf_op jit(solution)/shard_map/ppermute | solution.py:39
  43.2 3.3 %collective-permute-start.13 = (bf16[96,128]{1,0:T(8,128)(2,1)S(1)}, bf16[96,128]{1,0:T(8,128)(2,1)S(1)}, u32[]{:S(2)}, u32[]{:S(2)}) collective-permute-start(bf16[96,128]{1,0:T(8,128)(2,1)S(1)} %pack_geos.1.refs_0_), channel_id=1, source_target_pairs={{3,0},{2,1},{1,2},{0,3},{7,4},{6,5},{5,6},{4,7},{11,8},{10,9},{9,1... | collective-permute-start | bytes 73736 | tf_op jit(solution)/shard_map/ppermute | solution.py:39
  44.4 9.9 %collective-permute-start.14 = (bf16[1328,128]{1,0:T(8,128)(2,1)S(1)}, bf16[1328,128]{1,0:T(8,128)(2,1)S(1)}, u32[]{:S(2)}, u32[]{:S(2)}) collective-permute-start(bf16[1328,128]{1,0:T(8,128)(2,1)S(1)} %collective-permute-done.11.refs_1_.refs_6_), channel_id=1, source_target_pairs={{1,0},{0,1},{3,2},{2,3},{5,4},{4,5},{7,6},{6,7},{9,8},{8,9},{11,10... | collective-permute-start | bytes 1019912 | tf_op jit(solution)/shard_map/ppermute | solution.py:39
  44.5 9.9 %collective-permute-start.16 = (bf16[1328,128]{1,0:T(8,128)(2,1)S(1)}, bf16[1328,128]{1,0:T(8,128)(2,1)S(1)}, u32[]{:S(2)}, u32[]{:S(2)}) collective-permute-start(bf16[1328,128]{1,0:T(8,128)(2,1)S(1)} %collective-permute-done.15.refs_8_), channel_id=1, source_target_pairs={{1,0},{0,1},{3,2},{2,3},{5,4},{4,5},{7,6},{6,7},{9,8},{8,9},{11,10... | collective-permute-start | bytes 1019912 | tf_op jit(solution)/shard_map/ppermute | solution.py:39
  50.3 4.0 %collective-permute-start.18 = (bf16[1328,128]{1,0:T(8,128)(2,1)S(1)}, bf16[1328,128]{1,0:T(8,128)(2,1)S(1)}, u32[]{:S(2)}, u32[]{:S(2)}) collective-permute-start(bf16[1328,128]{1,0:T(8,128)(2,1)S(1)} %pack_diagonal.1.refs_10_), channel_id=1, source_target_pairs={{1,0},{0,1},{3,2},{2,3},{5,4},{4,5},{7,6},{6,7},{9,8},{8,9},{11,10... | collective-permute-start | bytes 1019912 | tf_op jit(solution)/shard_map/ppermute | solution.py:39
  60.1 5.2 %collective-permute-start.19 = (f32[8,128]{1,0:T(8,128)S(1)}, f32[8,128]{1,0:T(8,128)S(1)}, u32[]{:S(2)}, u32[]{:S(2)}) collective-permute-start(f32[8,128]{1,0:T(8,128)S(1)} %get-tuple-element.30), channel_id=1, source_target_pairs={{3,0},{0,1},{1,2},{2,3},{7,4},{4,5},{5,6},{6,7},{11,8},{8,9},{9,10... | collective-permute-start | bytes 12296 | tf_op jit(solution)/shard_map/ppermute | solution.py:26
  60.3 5.2 %collective-permute-start.20 = (f32[8,128]{1,0:T(8,128)S(1)}, f32[8,128]{1,0:T(8,128)S(1)}, u32[]{:S(2)}, u32[]{:S(2)}) collective-permute-start(f32[8,128]{1,0:T(8,128)S(1)} %get-tuple-element.30), channel_id=1, source_target_pairs={{1,0},{2,1},{3,2},{0,3},{5,4},{6,5},{7,6},{4,7},{9,8},{10,9},{11,1... | collective-permute-start | bytes 12296 | tf_op jit(solution)/shard_map/ppermute | solution.py:26
  61.9 3.9 %collective-permute-start.22 = (f32[8,128]{1,0:T(8,128)S(1)}, f32[8,128]{1,0:T(8,128)S(1)}, u32[]{:S(2)}, u32[]{:S(2)}) collective-permute-start(f32[8,128]{1,0:T(8,128)S(1)} %get-tuple-element.30), channel_id=1, source_target_pairs={{19,0},{16,1},{17,2},{18,3},{3,16},{0,17},{1,18},{2,19},{23,4},{20... | collective-permute-start | bytes 12296 | tf_op jit(solution)/shard_map/ppermute | solution.py:34
  61.9 4.0 %collective-permute-start.23 = (f32[8,128]{1,0:T(8,128)S(1)}, f32[8,128]{1,0:T(8,128)S(1)}, u32[]{:S(2)}, u32[]{:S(2)}) collective-permute-start(f32[8,128]{1,0:T(8,128)S(1)} %get-tuple-element.30), channel_id=1, source_target_pairs={{17,0},{18,1},{19,2},{16,3},{1,16},{2,17},{3,18},{0,19},{21,4},{22... | collective-permute-start | bytes 12296 | tf_op jit(solution)/shard_map/ppermute | solution.py:34
  64.6 3.6 %collective-permute-start.21 = (f32[8,128]{1,0:T(8,128)S(1)}, f32[8,128]{1,0:T(8,128)S(1)}, u32[]{:S(2)}, u32[]{:S(2)}) collective-permute-start(f32[8,128]{1,0:T(8,128)S(1)} %get-tuple-element.30), channel_id=1, source_target_pairs={{16,0},{0,16},{17,1},{1,17},{18,2},{2,18},{19,3},{3,19},{20,4},{4,... | collective-permute-start | bytes 12296 | tf_op jit(solution)/shard_map/ppermute | solution.py:26
  68.3 5.0 %collective-permute-start.24 = (f32[16,128]{1,0:T(8,128)S(1)}, f32[16,128]{1,0:T(8,128)S(1)}, u32[]{:S(2)}, u32[]{:S(2)}) collective-permute-start(f32[16,128]{1,0:T(8,128)S(1)} %maximum_maximum_fusion.refs_0_), channel_id=1, source_target_pairs={{4,0},{8,4},{12,8},{0,12},{5,1},{9,5},{13,9},{1,13},{6,2},{10,6},{... | collective-permute-start | bytes 24584 | tf_op jit(solution)/shard_map/ppermute | solution.py:26
  71.9 5.4 %collective-permute-start.25 = (f32[16,128]{1,0:T(8,128)S(1)}, f32[16,128]{1,0:T(8,128)S(1)}, u32[]{:S(2)}, u32[]{:S(2)}) collective-permute-start(f32[16,128]{1,0:T(8,128)S(1)} %maximum_maximum_fusion.refs_0_), channel_id=1, source_target_pairs={{12,0},{0,4},{4,8},{8,12},{13,1},{1,5},{5,9},{9,13},{14,2},{2,6},{... | collective-permute-start | bytes 24584 | tf_op jit(solution)/shard_map/ppermute | solution.py:26

commit v7 on v4

--- a/solution.py
+++ b/solution.py
@@ -63,11 +63,19 @@
         )
 
 
-def own_ranks(at, ints_ref):
+def load(sources, targets, sems):
+    copies = [pltpu.make_async_copy(a, b, sems.at[i]) for i, (a, b) in enumerate(zip(sources, targets))]
+    for copy in copies:
+        copy.start()
+    for copy in copies:
+        copy.wait()
+
+
+def own_ranks(at, neighbors_ref):
     seen = [jnp.int32(0)] * at.n_lay
     listed = []
-    for w in range(ints_ref.shape[0] - 5):
-        atom = ints_ref[w, at.me]
+    for w in range(neighbors_ref.shape[0]):
+        atom = neighbors_ref[w, at.me]
         step_lay = (atom - at.lay) & (at.n_lay - 1)
         rank = jnp.int32(0)
         for k in range(at.n_lay):
@@ -77,14 +85,16 @@
     return listed
 
 
-def pick_kernel(axes, ints_ref, sign_ref, out_ref, geo_ref, place_ref, sems):
+def pick_kernel(axes, *refs):
+    sign_ref, out_ref, geo_ref, neighbors_ref, extent_ref, x_ref, y_ref, z_ref, place_ref, loads, sems = refs[5:]
     at = Places(*axes)
     slots = sign_ref.shape[0]
     n_pick = place_ref.shape[0] - 1
     size = sign_ref.shape[1]
     for i in range(n_pick + 1):
         place_ref[i] = 0
-    ranks = own_ranks(at, ints_ref)
+    load(refs[:5], (neighbors_ref, extent_ref, x_ref, y_ref, z_ref), loads)
+    ranks = own_ranks(at, neighbors_ref)
     for w, (atom, _) in enumerate(ranks):
         row, col, lay = at.split(atom)
         place = target_place(at.n_row, (row - at.row) & (at.n_row - 1), (lay - at.lay) & (at.n_lay - 1), at.row)
@@ -102,28 +112,29 @@
         go_row = ((row - at.row + 1) & (at.n_row - 1)) - 1
         go_col = ((col - at.col + 1) & (at.n_col - 1)) - 1
         go_lay = jnp.minimum(((lay - at.lay + 1) & (at.n_lay - 1)) - 1, 1)
-        twice_x = ints_ref[slots + 1, at.me] + ints_ref[slots + 1, atom] + BX * go_row
-        twice_y = ints_ref[slots + 2, at.me] + ints_ref[slots + 2, atom] + BY * go_col
-        twice_z = ints_ref[slots + 3, at.me] + ints_ref[slots + 3, atom] + BZ * go_lay - BZ
-        extent = ints_ref[slots + 4, w]
+        twice_x = x_ref[at.me] + x_ref[atom] + BX * go_row
+        twice_y = y_ref[at.me] + y_ref[atom] + BY * go_col
+        twice_z = z_ref[at.me] + z_ref[atom] + BZ * go_lay - BZ
+        extent = extent_ref[0, w]
         values = jnp.where(sub == 0, twice_x, jnp.where(sub == 1, twice_y, jnp.where(sub == 2, twice_z, extent)))
         geo = jnp.where(lane_pair == rank, values, geo)
     geo = geo.astype(jnp.float32).astype(geo_ref.dtype)
     geo_ref[...] = geo
-    out_ref[n_pick * size : n_pick * size + GEO] = geo
+    out_ref[n_pick * size :] = geo
     for copy in copies:
         copy.wait()
 
 
 def prepare_kernel(axes, count, layout, late_from, *refs):
-    ints_ref, basis_ref = refs[:2]
-    early_ref, late_ref, info_ref, spread_ref, own_basis_ref, known, inverse, layout_ref = refs[-8:]
+    basis_ref = refs[2]
+    early_ref, late_ref, info_ref, spread_ref, own_basis_ref = refs[-11:-6]
+    neighbors_ref, size_ref, known, inverse, layout_ref, loads = refs[-6:]
     at = Places(*axes)
-    slots = ints_ref.shape[0] - 5
-    atoms = ints_ref.shape[1]
+    load(refs[:2], (neighbors_ref, size_ref), loads)
+    slots, atoms = neighbors_ref.shape
+    bits = atoms.bit_length() - 1
     for i, value in enumerate(layout):
         layout_ref[i] = value
-    bits = atoms.bit_length() - 1
     lines = count * at.n_lay
 
     def hot(rows, atom, first):
@@ -136,13 +147,13 @@
         return jnp.dot(picked, basis_ref[...], preferred_element_type=jnp.float32).astype(jnp.bfloat16)
 
     self_slot = jnp.int32(0)
-    for w, (atom, rank) in enumerate(own_ranks(at, ints_ref)):
+    for w, (atom, rank) in enumerate(own_ranks(at, neighbors_ref)):
         row, col, lay = at.split(atom)
         step_row = (row - at.row) & (at.n_row - 1)
         step_col = (col - at.col) & (at.n_col - 1)
         self_slot = jnp.where(atom == at.me, w, self_slot)
-        info_ref[w] = ints_ref[slots, atom]
-        spread_ref[w] = rows_of(hot(LANES, atom, rank * SHELLS))
+        info_ref[w] = size_ref[atom]
+        spread_ref[:, w * LANES : (w + 1) * LANES] = rows_of(hot(LANES, atom, rank * SHELLS))
         flip = lay ^ at.lay
         known[0, w] = atom
         known[1, w] = jnp.where(step_col == 0, 0, jnp.where(step_col == 1, 1, 2))
@@ -150,7 +161,7 @@
         known[3, w] = jnp.where((step_row != 0) & (flip == 3), 16 + w, w)
         inverse[atom] = -1
     own_basis_ref[...] = rows_of(hot(16, at.me, 0))
-    info_ref[slots] = ints_ref[slots, at.me]
+    info_ref[slots] = size_ref[at.me]
     info_ref[slots + 1] = self_slot
 
     def row_of_pairs(v, totals):
@@ -161,7 +172,7 @@
         turn = known[3, v]
         row, _, lay = at.split(atom)
         for u in range(slots):
-            inverse[ints_ref[u, atom]] = v * 16 + u
+            inverse[neighbors_ref[u, atom]] = v * 16 + u
         top = layout_ref[line]
         end = layout_ref[lines + line]
         beside = layout_ref[(side + 1) * lines + line]
@@ -302,7 +313,8 @@
     for n in range(slots // 2):
         part = jnp.dot(own[...], gram[:, n * wide : (n + 1) * wide], preferred_element_type=jnp.float32)
         square[:, n * wide : (n + 1) * wide] = jnp.where(column_kept(n), part, 0.0).astype(square.dtype)
-    coef = jnp.zeros((basis_ref.shape[0], LANES), jnp.float32)
+    basis = jnp.concatenate([basis_ref[...], basis_ref[...]], axis=1)
+    coef = jnp.zeros((2 * basis_ref.shape[0], LANES), jnp.float32)
     across = (((1,), (1,)), ((), ()))
     for n in range(slots // 2):
         part = jnp.dot(square[...], gram[:, n * wide : (n + 1) * wide], preferred_element_type=jnp.float32)
@@ -316,17 +328,16 @@
         dmat = 0.5 * (jnp.where(diag, 1.0, 0.0) - full)
         high = dmat.astype(jnp.bfloat16)
         low = (dmat - high.astype(jnp.float32)).astype(jnp.bfloat16)
-        half = jnp.dot(basis_ref[...], high, preferred_element_type=jnp.float32) + jnp.dot(
-            basis_ref[...], low, preferred_element_type=jnp.float32
-        )
+        half = jnp.dot(basis, jnp.concatenate([high, low], axis=0), preferred_element_type=jnp.float32)
         half_high = half.astype(jnp.bfloat16)
         half_low = (half - half_high.astype(jnp.float32)).astype(jnp.bfloat16)
-        for k in range(2):
-            spread = spread_ref[2 * n + k]
-            for part in (half_high, half_low):
-                coef = coef + lax.dot_general(
-                    part[:, k * size : (k + 1) * size], spread, across, preferred_element_type=jnp.float32
-                )
+        coef = coef + lax.dot_general(
+            jnp.concatenate([half_high, half_low], axis=0),
+            spread_ref[:, n * wide : (n + 1) * wide],
+            across,
+            preferred_element_type=jnp.float32,
+        )
+    coef = coef[: basis_ref.shape[0]] + coef[basis_ref.shape[0] :]
     coef_ref[...] = coef[: coef_ref.shape[0]]
 
 
@@ -413,17 +424,7 @@
     others = range(1, count)
     own = sign_start[0]
     flat = own.reshape(slots * size, size)
-    ints = jnp.concatenate(
-        [
-            neighbors.T,
-            atom_size[None],
-            atom_x[None],
-            atom_y[None],
-            atom_z[None],
-            jnp.pad(pair_extent, ((0, 0), (0, atoms - slots))),
-        ],
-        axis=0,
-    )
+    listings = neighbors.T
     full = slots * size
     half = full // 2
     n_pick = column_targets(n_row)
@@ -441,12 +442,21 @@
             jax.ShapeDtypeStruct((part, size), own.dtype),
             jax.ShapeDtypeStruct((GEO, LANES), own.dtype),
         ),
-        in_specs=[SMEM, HBM],
+        in_specs=[HBM] * 6,
         out_specs=(VMEM, VMEM),
-        scratch_shapes=[pltpu.SMEM((n_pick + 1,), jnp.int32), pltpu.SemaphoreType.DMA((n_pick,))],
-        compiler_params=pltpu.CompilerParams(vmem_limit_bytes=2 << 20),
+        scratch_shapes=[
+            pltpu.SMEM((slots, atoms), jnp.int32),
+            pltpu.SMEM((1, slots), jnp.int32),
+            pltpu.SMEM((atoms,), jnp.int32),
+            pltpu.SMEM((atoms,), jnp.int32),
+            pltpu.SMEM((atoms,), jnp.int32),
+            pltpu.SMEM((n_pick + 1,), jnp.int32),
+            pltpu.SemaphoreType.DMA((5,)),
+            pltpu.SemaphoreType.DMA((n_pick,)),
+        ],
+        compiler_params=pltpu.CompilerParams(vmem_limit_bytes=60 << 20),
         name="pick_column_blocks",
-    )(ints, own)
+    )(listings, pair_extent, atom_x, atom_y, atom_z, own)
     up = from_offset(picked, "col", 1)
     down = from_offset(picked, "col", -1)
 
@@ -485,12 +495,12 @@
         [(x, 0, full) for x in xs] + [(place["far"], 0, full), (0, 0, part), (1, 0, part)],
     ]
 
-    two_x, two_y, two_m = pack([buffers[name] for name in names], plans, [], "pack_two")
+    two_x, two_y = pack([buffers[name] for name in names], plans[:2], [m_row], "pack_two")
 
     early_order = ["own", "mate", "far", "up", "down", "geo"] + [("x", di) for di in others]
     early_order += [("two x", di) for di in others] + ["two y", "two m"]
     late_order = [("three x", di) for di in others] + ["three y", "three m"]
-    late_order += [("four x", di) for di in others] + ["four y"]
+    late_order += ["four"]
 
     contents = {}
     for di in others:
@@ -507,9 +517,10 @@
         contents["three m"] += [(("end", di, 3), half)] + side_of("up", di, 1) + [(None, 2 * GEO)]
     contents["three m"] += [(("top", di, 3), half) for di in others] + side_of("down", 0, 3)
     contents["three m"] += [("geos", count * 3 * GEO)]
+    contents["four"] = []
     for di in others:
-        contents["four x", di] = side_of("down", di, 1) + side_of("down", di, 3)
-    contents["four y"] = side_of("up", 0, 3) + sum([side_of("up", di, 3) for di in others], [])
+        contents["four"] += side_of("down", di, 1) + side_of("down", di, 3)
+    contents["four"] += side_of("up", 0, 3) + sum([side_of("up", di, 3) for di in others], [])
     lengths = {name: sum(rows for _, rows in content) for name, content in contents.items()}
     for name in early_order:
         if name in buffers:
@@ -541,24 +552,28 @@
             jax.ShapeDtypeStruct((entries,), jnp.int32),
             jax.ShapeDtypeStruct((entries,), jnp.int32),
             jax.ShapeDtypeStruct((slots + 2,), jnp.int32),
-            jax.ShapeDtypeStruct((slots, LANES, size), jnp.bfloat16),
+            jax.ShapeDtypeStruct((LANES, full), jnp.bfloat16),
             jax.ShapeDtypeStruct((16, size), jnp.bfloat16),
         ),
-        in_specs=[SMEM, VMEM, ANY],
+        in_specs=[HBM, HBM, VMEM, ANY],
         out_specs=(SMEM, SMEM, SMEM, VMEM, VMEM),
         scratch_shapes=[
+            pltpu.SMEM((slots, atoms), jnp.int32),
+            pltpu.SMEM((atoms,), jnp.int32),
             pltpu.SMEM((4, slots), jnp.int32),
             pltpu.SMEM((atoms,), jnp.int32),
             pltpu.SMEM((len(layout),), jnp.int32),
+            pltpu.SemaphoreType.DMA((2,)),
         ],
         compiler_params=pltpu.CompilerParams(vmem_limit_bytes=(2 << 20) + atoms * 16384),
         cost_estimate=pl.CostEstimate(flops=6_000_000_000, bytes_accessed=8_000_000, transcendentals=0),
         name="prepare",
-    )(ints, basis_proj.transpose(1, 0, 2).reshape(SHELLS * atoms, size), two_x)
+    )(listings, atom_size, basis_proj.transpose(1, 0, 2).reshape(SHELLS * atoms, size), two_x)
 
     for di in others:
         note(("two x", di), on_row(two_x, di), contents["two x", di])
     note("two y", from_layer(two_y, 2), contents["two y"])
+    two_m = pack([buffers[name] for name in names], plans[2:], [two_x], "pack_two_mate")[0]
     note("two m", from_layer(two_m, 1), contents["two m"])
 
     names = ["up", "down", "two y", "geo"] + [("two x", di) for di in others]
@@ -588,20 +603,20 @@
     gram = pl.pallas_call(
         functools.partial(gram_kernel, len(early_values)),
         out_shape=jax.ShapeDtypeStruct((full, full), jnp.bfloat16),
-        in_specs=[SMEM] + [ANY] * (len(early_values) + 1),
+        in_specs=[SMEM] + [ANY] * (len(early_values) + 2),
         out_specs=VMEM,
         scratch_shapes=[
             pltpu.VMEM((late_from, LANES), jnp.bfloat16),
             pltpu.SemaphoreType.DMA((len(early_values),)),
         ],
         compiler_params=pltpu.CompilerParams(vmem_limit_bytes=(6 << 20) + late_from * LANES * 2),
-        cost_estimate=pl.CostEstimate(flops=1_000_000_000, bytes_accessed=20_000_000, transcendentals=0),
+        cost_estimate=pl.CostEstimate(flops=1000, bytes_accessed=1000, transcendentals=0),
         name="gram_early",
-    )(early_table, *early_values, three_x)
-
-    for di in others:
-        note(("four x", di), from_layer(buffers["three x", di], 1), contents["four x", di])
-    note("four y", from_layer(buffers["three y"], 1), contents["four y"])
+    )(early_table, *early_values, three_x, third_geos)
+
+    thirds = [buffers["three x", di] for di in others] + [buffers["three y"]]
+    four = pack(thirds, [[(i, 0, value.shape[0]) for i, value in enumerate(thirds)]], [gram], "pack_four")[0]
+    note("four", from_layer(four, 1), contents["four"])
 
     column_steps = (0, 1, -1)
     tile_steps = [(dr, dc) for dr in steps for dc in column_steps]

time: 72.9 us -> 76.9 us (1.055)
  waiting for transfers between devices: 27 us -> 32.2 us
  local copies, waits for them, and re-layouts: 3.24 us -> 0.85 us
  Pallas kernels: 25 us -> 26.2 us
    ppermute x9 -> x8, waiting for transfers between devices: 3.95 us -> 12.3 us  [from_layer(): return lax.ppermute(x, 'layer', [(i ^ flip, i) for i in range(count)])]
    ppermute x10, waiting for transfers between devices: 23 us -> 19.9 us  [from_offset(): lax.ppermute(x, axis, [((i + step) % count, i) for i in range(count)])]
    concatenate x1 -> x0, local copies, waits for them, and re-layouts: 1.43 us -> none  [local(): jnp.concatenate([neighbors.T, atom_size[None], atom_x[None], atom_y[None]...]
    ppermute x10, starting transfers between devices: 11.6 us -> 10.4 us  [from_offset(): lax.ppermute(x, axis, [((i + step) % count, i) for i in range(count)])]
    pallas_call x1, Pallas kernels: 1.41 us -> 2.49 us  [local(): pl.pallas_call(functools.partial(pick_kernel, axes), out_shape=(jax.Shape...]
    ppermute x9 -> x8, starting transfers between devices: 4.97 us -> 5.93 us  [from_layer(): return lax.ppermute(x, 'layer', [(i ^ flip, i) for i in range(count)])]
    pallas_call x2 -> x4, Pallas kernels: 3.27 us -> 3.49 us  [pack(): pl.pallas_call(functools.partial(pack_kernel, tuple(moves), inputs, len(p...]
  transfers between devices with their start and end apart: 19 -> 18, of which waited for: 10 -> 9; matrix products, arithmetic and copies ran while one was open for 3% -> 0% of each run, Pallas kernels for 22% -> 22%
where the time goes in v7:
time: 76.9 us; the launch traced here: 76.6 us
  waiting for transfers between devices  32.2 us (42%)
  Pallas kernels  26.2 us (34%)
  starting transfers between devices  16.4 us (21%)
  local copies, waits for them, and re-layouts  0.85 us (1%)
  between operations  0.81 us (1%)
    ppermute x10, waiting for transfers between devices, from_offset(): lax.ppermute(x, axis, [((i + step) % count, i) for i in range(count)])  19.9 us
    ppermute x8, waiting for transfers between devices, from_layer(): return lax.ppermute(x, 'layer', [(i ^ flip, i) for i in range(count)])  12.3 us
    ppermute x10, starting transfers between devices, from_offset(): lax.ppermute(x, axis, [((i + step) % count, i) for i in range(count)])  10.4 us
    ppermute x8, starting transfers between devices, from_layer(): return lax.ppermute(x, 'layer', [(i ^ flip, i) for i in range(count)])  5.93 us
    pallas_call x1, Pallas kernels, local(): pl.pallas_call(functools.partial(prepare_kernel, axes, count, tuple(layou...  5.91 us
    pallas_call x1, Pallas kernels, local(): pl.pallas_call(functools.partial(step_kernel, len(late_values)), out_shap...  5.74 us
    pallas_call x1, Pallas kernels, local(): pl.pallas_call(functools.partial(gram_kernel, len(early_values)), out_sha...  3.62 us
    pallas_call x1, Pallas kernels, local(): pl.pallas_call(functools.partial(profile_kernel, periods, tile_steps, at[...  3.5 us
  transfers between devices with their start and end apart: 18, of which 9 were waited for; matrix products, arithmetic and copies ran while one was open for 0% of the time, Pallas kernels for 22%

profile of v7, /device:TPU:0, one launch (start us, length us, event | category | flops | bytes accessed | tf_op | source)
XLA Modules:
  0.0 76.6 jit_solution(15046058088755054709)
XLA Ops:
  0.6 3.0 %collective-permute-start.2 = (bf16[1536,128]{1,0:T(8,128)(2,1)}, bf16[1536,128]{1,0:T(8,128)(2,1)S(1)}, u32[]{:S(2)}, u32[]{:S(2)}) collective-permute-start(bf16[1536,128]{1,0:T(8,128)(2,1)} %bitcast.11), channel_id=1, source_target_pairs={{2,0},{3,1},{0,2},{1,3},{6,4},{7,5},{4,6},{5,7},{10,8},{11,9},{8,1... | collective-permute-start | bytes 1179656 | tf_op jit(solution)/shard_map/ppermute | solution.py:31
  3.7 1.5 %collective-permute-start.3 = (bf16[1536,128]{1,0:T(8,128)(2,1)}, bf16[1536,128]{1,0:T(8,128)(2,1)S(1)}, u32[]{:S(2)}, u32[]{:S(2)}) collective-permute-start(bf16[1536,128]{1,0:T(8,128)(2,1)} %bitcast.12), channel_id=1, source_target_pairs={{16,0},{0,16},{17,1},{1,17},{18,2},{2,18},{19,3},{3,19},{20,4},{4,... | collective-permute-start | bytes 1179656 | tf_op jit(solution)/shard_map/ppermute | solution.py:26
  5.2 0.0 collective-permute-start.4
  5.2 2.5 %pick_column_blocks.1 = (bf16[656,128]{1,0:T(8,128)(2,1)}, bf16[16,128]{1,0:T(8,128)(2,1)}) custom-call(s32[12,32]{1,0:T(8,128)} %bitcast.19, s32[1,12]{1,0:T(1,128)} %refs_1_.2, s32[32]{0:T(128)} %refs_2_.1, s32[32]{0:T(128)} %refs_3_.1, s32[32]{0:T(128)} %refs_4_.1, bf16[12,128,128]{2,1,0:T(8,128)(2,1)} %bitcast.14), custom_call_target="tpu_custom_call" | custom-call | tf_op jit(solution)/shard_map/pick_column_blocks/pallas_call | solution.py:439
  7.7 3.7 %collective-permute-start = (bf16[656,128]{1,0:T(8,128)(2,1)}, bf16[656,128]{1,0:T(8,128)(2,1)S(1)}, u32[]{:S(2)}, u32[]{:S(2)}) collective-permute-start(bf16[656,128]{1,0:T(8,128)(2,1)} %get-tuple-element.19), channel_id=1, source_target_pairs={{4,0},{8,4},{12,8},{0,12},{5,1},{9,5},{13,9},{1,13},{6,2},{10,6},{... | collective-permute-start | bytes 503816 | tf_op jit(solution)/shard_map/ppermute | solution.py:26
  11.3 0.0 collective-permute-start.1
  11.3 5.0 %collective-permute-done.refs_0_.refs_4_ = bf16[656,128]{1,0:T(8,128)(2,1)S(1)} collective-permute-done((bf16[656,128]{1,0:T(8,128)(2,1)}, bf16[656,128]{1,0:T(8,128)(2,1)S(1)}, u32[]{:S(2)}, u32[]{:S(2)}) %collective-permute-start) | collective-permute-done | bytes 167968 | tf_op jit(solution)/shard_map/ppermute | solution.py:26
  16.3 4.0 %collective-permute-done.1.refs_1_.refs_5_ = bf16[656,128]{1,0:T(8,128)(2,1)S(1)} collective-permute-done((bf16[656,128]{1,0:T(8,128)(2,1)}, bf16[656,128]{1,0:T(8,128)(2,1)S(1)}, u32[]{:S(2)}, u32[]{:S(2)}) %collective-permute-start.1) | collective-permute-done | bytes 167968 | tf_op jit(solution)/shard_map/ppermute | solution.py:26
  20.2 0.0 collective-permute-done.2.refs_3_
  20.2 0.0 collective-permute-done.3.refs_4_.refs_7_
  20.3 0.0 collective-permute-done.4.refs_5_.refs_2_
  20.3 0.0 copy-start.1
  20.3 0.7 copy-done.1
  20.9 1.0 %pack_two.1 = (bf16[1456,128]{1,0:T(8,128)(2,1)S(1)}, bf16[1424,128]{1,0:T(8,128)(2,1)S(1)}) custom-call(bf16[656,128]{1,0:T(8,128)(2,1)S(1)} %collective-permute-done.refs_0_.refs_4_, bf16[656,128]{1,0:T(8,128)(2,1)S(1)} %collective-permute-done.1.refs_1_.refs_5_, bf16[16,128]{1,0:T(8,128)(2,1)S(1)} %copy-done.1, ...), custom_call_target="tpu_custom_call" | custom-call | bytes 3000000 | tf_op jit(solution)/shard_map/pack_two/pallas_call | solution.py:234
  21.9 0.0 copy-start.2
  21.9 0.0 copy-start.3
  22.0 0.0 copy-start.4
  22.0 0.9 %pack_two_mate.1 = bf16[4384,128]{1,0:T(8,128)(2,1)S(1)} custom-call(bf16[656,128]{1,0:T(8,128)(2,1)S(1)} %collective-permute-done.refs_0_.refs_4_, bf16[656,128]{1,0:T(8,128)(2,1)S(1)} %collective-permute-done.1.refs_1_.refs_5_, bf16[16,128]{1,0:T(8,128)(2,1)S(1)} %copy-done.1, bf16[1536,128]{1,0:T(8,128)(2,1)S(1)} %collective-permute-done.2.refs_3_, ...), custom_call_target="tpu_custom_call" | custom-call | bytes 3000000 | tf_op jit(solution)/shard_map/pack_two_mate/pallas_call | solution.py:234
  22.8 0.1 collective-permute-start.7
  22.9 0.6 collective-permute-start.5
  23.5 0.5 collective-permute-start.6
  24.0 0.0 copy-done.2
  24.0 0.0 copy-done.3
  24.0 0.0 copy-done.4
  24.0 5.9 %prepare.1 = (s32[247]{0:T(256)S(1)}, s32[247]{0:T(256)S(1)}, s32[14]{0:T(128)S(1)}, bf16[128,1536]{1,0:T(8,128)(2,1)S(1)}, bf16[16,128]{1,0:T(8,128)(2,1)S(1)}) custom-call(s32[12,32]{1,0:T(8,128)S(1)} %bitcast.20, s32[32]{0:T(128)S(1)} %copy-done.4, bf16[192,128]{1,0:T(8,128)(2,1)S(1)} %bitcast.21, bf16[1456,128]{1,0:T(8,128)(2,1)S(1)} %get-tuple-element.21.refs_3_.refs_5_), custom_call_target="tpu_custom_call" | custom-call | flops 6000000000 | bytes 8000000 | tf_op jit(solution)/shard_map/prepare/pallas_call | solution.py:549
  29.9 0.0 copy-start
  30.0 4.1 %collective-permute-done.6.refs_2_.refs_9_ = bf16[1424,128]{1,0:T(8,128)(2,1)S(1)} collective-permute-done((bf16[1424,128]{1,0:T(8,128)(2,1)S(1)}, bf16[1424,128]{1,0:T(8,128)(2,1)S(1)}, u32[]{:S(2)}, u32[]{:S(2)}) %collective-permute-start.6) | collective-permute-done | bytes 364576 | tf_op jit(solution)/shard_map/ppermute | solution.py:31
  34.1 0.0 collective-permute-done.5.refs_4_.refs_8_
  34.1 1.4 %pack_three.1 = (bf16[1312,128]{1,0:T(8,128)(2,1)S(1)}, bf16[1312,128]{1,0:T(8,128)(2,1)S(1)}, bf16[2976,128]{1,0:T(8,128)(2,1)S(1)}, bf16[96,128]{1,0:T(8,128)(2,1)S(1)}) custom-call(bf16[656,128]{1,0:T(8,128)(2,1)S(1)} %collective-permute-done.refs_0_.refs_4_, bf16[656,128]{1,0:T(8,128)(2,1)S(1)} %collective-permute-done.1.refs_1_.refs_5_, ...), custom_call_target="tpu_custom_call" | custom-call | bytes 3000000 | tf_op jit(solution)/shard_map/pack_three/pallas_call | solution.py:234
  35.5 0.1 collective-permute-start.11
  35.6 1.6 %collective-permute-start.9 = (bf16[1312,128]{1,0:T(8,128)(2,1)S(1)}, bf16[1312,128]{1,0:T(8,128)(2,1)S(1)}, u32[]{:S(2)}, u32[]{:S(2)}) collective-permute-start(bf16[1312,128]{1,0:T(8,128)(2,1)S(1)} %get-tuple-element.28.refs_11_), channel_id=1, source_target_pairs={{16,0},{0,16},{17,1},{1,17},{18,2},{2,18},{19,3},{3,19},{20,4},{4,... | collective-permute-start | bytes 1007624 | tf_op jit(solution)/shard_map/ppermute | solution.py:26
  37.1 0.5 collective-permute-start.10
  37.6 1.0 %collective-permute-start.8 = (bf16[96,128]{1,0:T(8,128)(2,1)S(1)}, bf16[96,128]{1,0:T(8,128)(2,1)S(1)}, u32[]{:S(2)}, u32[]{:S(2)}) collective-permute-start(bf16[96,128]{1,0:T(8,128)(2,1)S(1)} %get-tuple-element.29.refs_0_), channel_id=1, source_target_pairs={{3,0},{2,1},{1,2},{0,3},{7,4},{6,5},{5,6},{4,7},{11,8},{10,9},{9,1... | collective-permute-start | bytes 73736 | tf_op jit(solution)/shard_map/ppermute | solution.py:31
  38.7 8.2 %collective-permute-done.8.refs_12_.refs_2_ = bf16[96,128]{1,0:T(8,128)(2,1)S(1)} collective-permute-done((bf16[96,128]{1,0:T(8,128)(2,1)S(1)}, bf16[96,128]{1,0:T(8,128)(2,1)S(1)}, u32[]{:S(2)}, u32[]{:S(2)}) %collective-permute-start.8) | collective-permute-done | bytes 24608 | tf_op jit(solution)/shard_map/ppermute | solution.py:31
  46.8 0.0 collective-permute-done.7.refs_10_
  46.8 0.0 copy-done
  46.8 3.6 %gram_early.1.refs_2_.refs_3_.refs_5_ = bf16[1536,1536]{1,0:T(8,128)(2,1)S(1)} custom-call(s32[247]{0:T(256)S(1)} %get-tuple-element.26.refs_0_, bf16[1536,128]{1,0:T(8,128)(2,1)S(1)} %bitcast.15, bf16[1536,128]{1,0:T(8,128)(2,1)S(1)} %collective-permute-done.4.refs_5_.refs_2_, bf16[1536,128]{1,0:T(8,128)(2,1)S(1)} %collective-permute-done.2.refs_3_, ...), custom_call_target="tpu_custom_call" | custom-call | flops 1000 | bytes 1000 | tf_op jit(solution)/shard_map/gram_early/pallas_call | solution.py:603
  50.4 0.0 collective-permute-done.9.refs_0_.refs_6_
  50.5 0.0 collective-permute-done.10.refs_1_.refs_7_
  50.5 0.2 pack_four.1
  50.7 0.7 collective-permute-start.12
  51.5 0.0 collective-permute-done.11.refs_1_.refs_8_
  51.5 3.5 %profiles.1 = (bf16[6,6,256,128]{3,2,1,0:T(8,128)(2,1)S(1)}, bf16[6,6,128,128]{3,2,1,0:T(8,128)(2,1)S(1)}) custom-call(bf16[96,128]{1,0:T(8,128)(2,1)S(1)} %get-tuple-element.29.refs_0_, bf16[2976,128]{1,0:T(8,128)(2,1)S(1)} %collective-permute-done.11.refs_1_.refs_8_, bf16[96,128]{1,0:T(8,128)(2,1)S(1)} %collective-permute-done.8.refs_12_.refs_2_, ...), custom_call_target="tpu_custom_call" | custom-call | flops 5000000000 | bytes 4000000 | tf_op jit(solution)/shard_map/profiles/pallas_call | solution.py:625
  55.0 0.0 collective-permute-done.12.refs_9_
  55.0 5.7 %square_cube_coefficients.1 = (bf16[12,128,128]{2,1,0:T(8,128)(2,1)}, f32[8,128]{1,0:T(8,128)S(1)}) custom-call(s32[247]{0:T(256)S(1)} %get-tuple-element.22.refs_0_, s32[14]{0:T(128)S(1)} %get-tuple-element.23.refs_1_, bf16[16,128]{1,0:T(8,128)(2,1)S(1)} %get-tuple-element.24.refs_5_.refs_2_, bf16[128,1536]{1,0:T(8,128)(2,1)S(1)} %get-tuple-element.25.refs_3_, ...), custom_call_target="tpu_custom_call" | custom-call | flops 1300000000 | bytes 8000000 | tf_op jit(solution)/shard_map/square_cube_coefficients/pallas_call | solution.py:643
  60.7 0.3 collective-permute-start.14
  61.0 0.2 collective-permute-start.13
  61.3 1.1 %collective-permute-done.14 = f32[8,128]{1,0:T(8,128)S(1)} collective-permute-done((f32[8,128]{1,0:T(8,128)S(1)}, f32[8,128]{1,0:T(8,128)S(1)}, u32[]{:S(2)}, u32[]{:S(2)}) %collective-permute-start.14) | collective-permute-done | bytes 4128 | tf_op jit(solution)/shard_map/ppermute | solution.py:26
  62.4 0.1 slice.11
  62.4 1.6 %collective-permute-done.13 = f32[8,128]{1,0:T(8,128)S(1)} collective-permute-done((f32[8,128]{1,0:T(8,128)S(1)}, f32[8,128]{1,0:T(8,128)S(1)}, u32[]{:S(2)}, u32[]{:S(2)}) %collective-permute-start.13) | collective-permute-done | bytes 4128 | tf_op jit(solution)/shard_map/ppermute | solution.py:26
  64.1 0.1 slice.10
  64.1 0.1 pad_maximum_fusion.1
  64.2 0.5 collective-permute-start.15
  64.8 3.1 %collective-permute-done.15 = f32[8,128]{1,0:T(8,128)S(1)} collective-permute-done((f32[8,128]{1,0:T(8,128)S(1)}, f32[8,128]{1,0:T(8,128)S(1)}, u32[]{:S(2)}, u32[]{:S(2)}) %collective-permute-start.15) | collective-permute-done | bytes 4128 | tf_op jit(solution)/shard_map/ppermute | solution.py:26
  67.8 0.1 pad_maximum_fusion.refs_0_
  67.9 1.8 %collective-permute-start.16 = (f32[16,128]{1,0:T(8,128)S(1)}, f32[16,128]{1,0:T(8,128)S(1)}, u32[]{:S(2)}, u32[]{:S(2)}) collective-permute-start(f32[16,128]{1,0:T(8,128)S(1)} %pad_maximum_fusion.refs_0_), channel_id=1, source_target_pairs={{4,0},{8,4},{12,8},{0,12},{5,1},{9,5},{13,9},{1,13},{6,2},{10,6},{... | collective-permute-start | bytes 24584 | tf_op jit(solution)/shard_map/ppermute | solution.py:26
  69.7 0.3 collective-permute-start.17
  69.9 1.6 %collective-permute-done.16.refs_1_ = f32[16,128]{1,0:T(8,128)S(1)} collective-permute-done((f32[16,128]{1,0:T(8,128)S(1)}, f32[16,128]{1,0:T(8,128)S(1)}, u32[]{:S(2)}, u32[]{:S(2)}) %collective-permute-start.16) | collective-permute-done | bytes 8224 | tf_op jit(solution)/shard_map/ppermute | solution.py:26
  71.6 3.6 %collective-permute-done.17.refs_2_ = f32[16,128]{1,0:T(8,128)S(1)} collective-permute-done((f32[16,128]{1,0:T(8,128)S(1)}, f32[16,128]{1,0:T(8,128)S(1)}, u32[]{:S(2)}, u32[]{:S(2)}) %collective-permute-start.17) | collective-permute-done | bytes 8224 | tf_op jit(solution)/shard_map/ppermute | solution.py:26
  75.1 1.5 %density.1 = f32[256,128]{1,0:T(8,128)} custom-call(f32[16,128]{1,0:T(8,128)S(1)} %pad_maximum_fusion.refs_0_, f32[16,128]{1,0:T(8,128)S(1)} %collective-permute-done.16.refs_1_, f32[16,128]{1,0:T(8,128)S(1)} %collective-permute-done.17.refs_2_, bf16[6,6,256,128]{3,2,1,0:T(8,128)(2,1)S(1)} %get-tuple-element.35.refs_3_, bf16[4608,128]{1,0:T(8,128)(2,1)S(1)} %bitcast.10), custom_call_target="tpu_custom_call" | custom-call | flops 310000000 | bytes 4000000 | tf_op jit(solution)/shard_map/density/pallas_call | solution.py:677
  (1 shorter events, 0.0 us)
Async XLA Ops:
  0.6 19.6 %collective-permute-start.2 = (bf16[1536,128]{1,0:T(8,128)(2,1)}, bf16[1536,128]{1,0:T(8,128)(2,1)S(1)}, u32[]{:S(2)}, u32[]{:S(2)}) collective-permute-start(bf16[1536,128]{1,0:T(8,128)(2,1)} %bitcast.11), channel_id=1, source_target_pairs={{2,0},{3,1},{0,2},{1,3},{6,4},{7,5},{4,6},{5,7},{10,8},{11,9},{8,1... | collective-permute-start | bytes 1179656 | tf_op jit(solution)/shard_map/ppermute | solution.py:31
  3.7 16.6 %collective-permute-start.3 = (bf16[1536,128]{1,0:T(8,128)(2,1)}, bf16[1536,128]{1,0:T(8,128)(2,1)S(1)}, u32[]{:S(2)}, u32[]{:S(2)}) collective-permute-start(bf16[1536,128]{1,0:T(8,128)(2,1)} %bitcast.12), channel_id=1, source_target_pairs={{16,0},{0,16},{17,1},{1,17},{18,2},{2,18},{19,3},{3,19},{20,4},{4,... | collective-permute-start | bytes 1179656 | tf_op jit(solution)/shard_map/ppermute | solution.py:26
  5.2 15.1 %collective-permute-start.4 = (bf16[1536,128]{1,0:T(8,128)(2,1)}, bf16[1536,128]{1,0:T(8,128)(2,1)S(1)}, u32[]{:S(2)}, u32[]{:S(2)}) collective-permute-start(bf16[1536,128]{1,0:T(8,128)(2,1)} %bitcast.13), channel_id=1, source_target_pairs={{1,0},{0,1},{3,2},{2,3},{5,4},{4,5},{7,6},{6,7},{9,8},{8,9},{11,10... | collective-permute-start | bytes 1179656 | tf_op jit(solution)/shard_map/ppermute | solution.py:31
  7.7 8.6 %collective-permute-start = (bf16[656,128]{1,0:T(8,128)(2,1)}, bf16[656,128]{1,0:T(8,128)(2,1)S(1)}, u32[]{:S(2)}, u32[]{:S(2)}) collective-permute-start(bf16[656,128]{1,0:T(8,128)(2,1)} %get-tuple-element.19), channel_id=1, source_target_pairs={{4,0},{8,4},{12,8},{0,12},{5,1},{9,5},{13,9},{1,13},{6,2},{10,6},{... | collective-permute-start | bytes 503816 | tf_op jit(solution)/shard_map/ppermute | solution.py:26
  11.3 8.9 %collective-permute-start.1 = (bf16[656,128]{1,0:T(8,128)(2,1)}, bf16[656,128]{1,0:T(8,128)(2,1)S(1)}, u32[]{:S(2)}, u32[]{:S(2)}) collective-permute-start(bf16[656,128]{1,0:T(8,128)(2,1)} %get-tuple-element.19), channel_id=1, source_target_pairs={{12,0},{0,4},{4,8},{8,12},{13,1},{1,5},{5,9},{9,13},{14,2},{2,6},{... | collective-permute-start | bytes 503816 | tf_op jit(solution)/shard_map/ppermute | solution.py:26
  20.3 0.7 copy-start.1
  21.9 2.1 %copy-start.2 = (s32[32,12]{0,1:T(8,128)S(1)}, s32[32,12]{0,1:T(8,128)}, u32[]{:S(2)}) copy-start(s32[32,12]{0,1:T(8,128)} %param.9) | copy-start | bytes 4612
  21.9 2.1 %copy-start.3 = (bf16[32,6,128]{2,0,1:T(8,128)(2,1)S(1)}, bf16[32,6,128]{2,0,1:T(8,128)(2,1)}, u32[]{:S(2)}) copy-start(bf16[32,6,128]{2,0,1:T(8,128)(2,1)} %param.11) | copy-start | bytes 147460
  22.0 2.1 %copy-start.4 = (s32[32]{0:T(128)S(1)}, s32[32]{0:T(128)}, u32[]{:S(2)}) copy-start(s32[32]{0:T(128)} %refs_1_.3) | copy-start | bytes 388
  22.8 24.0 %collective-permute-start.7 = (bf16[4384,128]{1,0:T(8,128)(2,1)S(1)}, bf16[4384,128]{1,0:T(8,128)(2,1)S(1)}, u32[]{:S(2)}, u32[]{:S(2)}) collective-permute-start(bf16[4384,128]{1,0:T(8,128)(2,1)S(1)} %pack_two_mate.1), channel_id=1, source_target_pairs={{1,0},{0,1},{3,2},{2,3},{5,4},{4,5},{7,6},{6,7},{9,8},{8,9},{11,10... | collective-permute-start | bytes 3366920 | tf_op jit(solution)/shard_map/ppermute | solution.py:31
  22.9 11.2 %collective-permute-start.5 = (bf16[1456,128]{1,0:T(8,128)(2,1)S(1)}, bf16[1456,128]{1,0:T(8,128)(2,1)S(1)}, u32[]{:S(2)}, u32[]{:S(2)}) collective-permute-start(bf16[1456,128]{1,0:T(8,128)(2,1)S(1)} %get-tuple-element.21.refs_3_.refs_5_), channel_id=1, source_target_pairs={{16,0},{0,16},{17,1},{1,17},{18,2},{2,18},{19,3},{3,19},{20,4},{4,... | collective-permute-start | bytes 1118216 | tf_op jit(solution)/shard_map/ppermute | solution.py:26
  23.5 10.6 %collective-permute-start.6 = (bf16[1424,128]{1,0:T(8,128)(2,1)S(1)}, bf16[1424,128]{1,0:T(8,128)(2,1)S(1)}, u32[]{:S(2)}, u32[]{:S(2)}) collective-permute-start(bf16[1424,128]{1,0:T(8,128)(2,1)S(1)} %get-tuple-element.27), channel_id=1, source_target_pairs={{2,0},{3,1},{0,2},{1,3},{6,4},{7,5},{4,6},{5,7},{10,8},{11,9},{8,1... | collective-permute-start | bytes 1093640 | tf_op jit(solution)/shard_map/ppermute | solution.py:31
  29.9 16.9 %copy-start = (bf16[1,12,128,128]{3,2,1,0:T(8,128)(2,1)S(1)}, bf16[1,12,128,128]{3,2,1,0:T(8,128)(2,1)}, u32[]{:S(2)}) copy-start(bf16[1,12,128,128]{3,2,1,0:T(8,128)(2,1)} %param.8) | copy-start | bytes 1179652
  35.5 15.9 %collective-permute-start.11 = (bf16[2976,128]{1,0:T(8,128)(2,1)S(1)}, bf16[2976,128]{1,0:T(8,128)(2,1)S(1)}, u32[]{:S(2)}, u32[]{:S(2)}) collective-permute-start(bf16[2976,128]{1,0:T(8,128)(2,1)S(1)} %get-tuple-element.31), channel_id=1, source_target_pairs={{1,0},{0,1},{3,2},{2,3},{5,4},{4,5},{7,6},{6,7},{9,8},{8,9},{11,10... | collective-permute-start | bytes 2285576 | tf_op jit(solution)/shard_map/ppermute | solution.py:31
  35.6 14.9 %collective-permute-start.9 = (bf16[1312,128]{1,0:T(8,128)(2,1)S(1)}, bf16[1312,128]{1,0:T(8,128)(2,1)S(1)}, u32[]{:S(2)}, u32[]{:S(2)}) collective-permute-start(bf16[1312,128]{1,0:T(8,128)(2,1)S(1)} %get-tuple-element.28.refs_11_), channel_id=1, source_target_pairs={{16,0},{0,16},{17,1},{1,17},{18,2},{2,18},{19,3},{3,19},{20,4},{4,... | collective-permute-start | bytes 1007624 | tf_op jit(solution)/shard_map/ppermute | solution.py:26
  37.1 13.3 %collective-permute-start.10 = (bf16[1312,128]{1,0:T(8,128)(2,1)S(1)}, bf16[1312,128]{1,0:T(8,128)(2,1)S(1)}, u32[]{:S(2)}, u32[]{:S(2)}) collective-permute-start(bf16[1312,128]{1,0:T(8,128)(2,1)S(1)} %get-tuple-element.30), channel_id=1, source_target_pairs={{2,0},{3,1},{0,2},{1,3},{6,4},{7,5},{4,6},{5,7},{10,8},{11,9},{8,1... | collective-permute-start | bytes 1007624 | tf_op jit(solution)/shard_map/ppermute | solution.py:31
  37.6 9.2 %collective-permute-start.8 = (bf16[96,128]{1,0:T(8,128)(2,1)S(1)}, bf16[96,128]{1,0:T(8,128)(2,1)S(1)}, u32[]{:S(2)}, u32[]{:S(2)}) collective-permute-start(bf16[96,128]{1,0:T(8,128)(2,1)S(1)} %get-tuple-element.29.refs_0_), channel_id=1, source_target_pairs={{3,0},{2,1},{1,2},{0,3},{7,4},{6,5},{5,6},{4,7},{11,8},{10,9},{9,1... | collective-permute-start | bytes 73736 | tf_op jit(solution)/shard_map/ppermute | solution.py:31
  50.7 4.2 %collective-permute-start.12 = (bf16[2624,128]{1,0:T(8,128)(2,1)S(1)}, bf16[2624,128]{1,0:T(8,128)(2,1)S(1)}, u32[]{:S(2)}, u32[]{:S(2)}) collective-permute-start(bf16[2624,128]{1,0:T(8,128)(2,1)S(1)} %pack_four.1), channel_id=1, source_target_pairs={{1,0},{0,1},{3,2},{2,3},{5,4},{4,5},{7,6},{6,7},{9,8},{8,9},{11,10... | collective-permute-start | bytes 2015240 | tf_op jit(solution)/shard_map/ppermute | solution.py:31
  60.7 1.6 %collective-permute-start.14 = (f32[8,128]{1,0:T(8,128)S(1)}, f32[8,128]{1,0:T(8,128)S(1)}, u32[]{:S(2)}, u32[]{:S(2)}) collective-permute-start(f32[8,128]{1,0:T(8,128)S(1)} %get-tuple-element.34), channel_id=1, source_target_pairs={{1,0},{2,1},{3,2},{0,3},{5,4},{6,5},{7,6},{4,7},{9,8},{10,9},{11,1... | collective-permute-start | bytes 12296 | tf_op jit(solution)/shard_map/ppermute | solution.py:26
  61.0 3.0 %collective-permute-start.13 = (f32[8,128]{1,0:T(8,128)S(1)}, f32[8,128]{1,0:T(8,128)S(1)}, u32[]{:S(2)}, u32[]{:S(2)}) collective-permute-start(f32[8,128]{1,0:T(8,128)S(1)} %get-tuple-element.34), channel_id=1, source_target_pairs={{3,0},{0,1},{1,2},{2,3},{7,4},{4,5},{5,6},{6,7},{11,8},{8,9},{9,10... | collective-permute-start | bytes 12296 | tf_op jit(solution)/shard_map/ppermute | solution.py:26
  64.2 3.6 %collective-permute-start.15 = (f32[8,128]{1,0:T(8,128)S(1)}, f32[8,128]{1,0:T(8,128)S(1)}, u32[]{:S(2)}, u32[]{:S(2)}) collective-permute-start(f32[8,128]{1,0:T(8,128)S(1)} %pad_maximum_fusion.1), channel_id=1, source_target_pairs={{16,0},{0,16},{17,1},{1,17},{18,2},{2,18},{19,3},{3,19},{20,4},{4,... | collective-permute-start | bytes 12296 | tf_op jit(solution)/shard_map/ppermute | solution.py:26
  67.9 3.7 %collective-permute-start.16 = (f32[16,128]{1,0:T(8,128)S(1)}, f32[16,128]{1,0:T(8,128)S(1)}, u32[]{:S(2)}, u32[]{:S(2)}) collective-permute-start(f32[16,128]{1,0:T(8,128)S(1)} %pad_maximum_fusion.refs_0_), channel_id=1, source_target_pairs={{4,0},{8,4},{12,8},{0,12},{5,1},{9,5},{13,9},{1,13},{6,2},{10,6},{... | collective-permute-start | bytes 24584 | tf_op jit(solution)/shard_map/ppermute | solution.py:26
  69.7 5.4 %collective-permute-start.17 = (f32[16,128]{1,0:T(8,128)S(1)}, f32[16,128]{1,0:T(8,128)S(1)}, u32[]{:S(2)}, u32[]{:S(2)}) collective-permute-start(f32[16,128]{1,0:T(8,128)S(1)} %pad_maximum_fusion.refs_0_), channel_id=1, source_target_pairs={{12,0},{0,4},{4,8},{8,12},{13,1},{1,5},{5,9},{9,13},{14,2},{2,6},{... | collective-permute-start | bytes 24584 | tf_op jit(solution)/shard_map/ppermute | solution.py:26

commit v8 on v7

--- a/solution.py
+++ b/solution.py
@@ -120,7 +120,7 @@
         geo = jnp.where(lane_pair == rank, values, geo)
     geo = geo.astype(jnp.float32).astype(geo_ref.dtype)
     geo_ref[...] = geo
-    out_ref[n_pick * size :] = geo
+    out_ref[n_pick * size : n_pick * size + GEO] = geo
     for copy in copies:
         copy.wait()
 
@@ -158,7 +158,6 @@
         known[0, w] = atom
         known[1, w] = jnp.where(step_col == 0, 0, jnp.where(step_col == 1, 1, 2))
         known[2, w] = jnp.where(step_row == 0, 0, jnp.where(step_row == 1, 1, 2)) * at.n_lay + flip
-        known[3, w] = jnp.where((step_row != 0) & (flip == 3), 16 + w, w)
         inverse[atom] = -1
     own_basis_ref[...] = rows_of(hot(16, at.me, 0))
     info_ref[slots] = size_ref[at.me]
@@ -169,7 +168,6 @@
         atom = known[0, v]
         side = known[1, v]
         line = known[2, v]
-        turn = known[3, v]
         row, _, lay = at.split(atom)
         for u in range(slots):
             inverse[neighbors_ref[u, atom]] = v * 16 + u
@@ -185,7 +183,7 @@
             o_row, _, o_lay = at.split(other)
             there = target_place(at.n_row, (o_row - row) & (at.n_row - 1), (o_lay - lay) & (at.n_lay - 1), row)
             back = target_place(at.n_row, (row - o_row) & (at.n_row - 1), (lay - o_lay) & (at.n_lay - 1), o_row)
-            from_row = (other_side != 0) | (turn <= known[3, w])
+            from_row = (other_side != 0) | (v <= w)
             from_column = (side == other_side) & (there >= 0) & ((back < 0) | (v <= w))
             chosen = ((mark >> 4) == v) & jnp.where(side == 0, from_row, from_column)
             in_row = jnp.where(slot < half, top + slot * LANES, end + (slot - half) * LANES)
@@ -428,7 +426,8 @@
     full = slots * size
     half = full // 2
     n_pick = column_targets(n_row)
-    part = n_pick * size + GEO
+    picks = n_pick * size
+    part = picks + GEO
 
     def on_row(value, di):
         return from_offset(value, "row", steps[di])
@@ -439,7 +438,7 @@
     picked, geo = pl.pallas_call(
         functools.partial(pick_kernel, axes),
         out_shape=(
-            jax.ShapeDtypeStruct((part, size), own.dtype),
+            jax.ShapeDtypeStruct((max(part, half + GEO), size), own.dtype),
             jax.ShapeDtypeStruct((GEO, LANES), own.dtype),
         ),
         in_specs=[HBM] * 6,
@@ -460,6 +459,15 @@
     up = from_offset(picked, "col", 1)
     down = from_offset(picked, "col", -1)
 
+    halves = pack(
+        [y_row] + [x_row[di] for di in others],
+        [[(0, half, half)]] + [[(di, 0, half)] for di in others],
+        [],
+        "pack_halves",
+    )
+    ends = {di: on_row(halves[0], di) for di in others}
+    tops = {di: from_layer(halves[di], 2) for di in others}
+
     at = {}
     buffers = {}
 
@@ -475,47 +483,48 @@
         return [(("top", di, flip), half), (("end", di, flip), half)]
 
     def side_of(kind, di, flip):
-        return [((kind, di, flip), part - GEO), ((kind + " geo", di, flip), GEO)]
+        return [((kind, di, flip), picks)]
 
     note("own", flat, row_of(0, 0))
     note("mate", m_row, row_of(0, 1))
     note("far", y_row, row_of(0, 2))
-    note("up", up, side_of("up", 0, 0))
-    note("down", down, side_of("down", 0, 0))
+    note("up", up, side_of("up", 0, 0) + [(("up geo", 0, 0), GEO)])
+    note("down", down, side_of("down", 0, 0) + [(("down geo", 0, 0), GEO)])
     note("geo", geo, [(("geo", 0, 0), GEO)])
     for di in others:
         note(("x", di), x_row[di], row_of(di, 0))
-
-    names = ["up", "down", "geo", "far"] + [("x", di) for di in others]
-    place = {name: i for i, name in enumerate(names)}
-    xs = [place["x", di] for di in others]
+        note(("end", di), ends[di], [(("end", di, 2), half)])
+        note(("top", di), tops[di], [(("top", di, 2), half)])
+
+    corners = [("end", di) for di in others] + [("top", di) for di in others]
+    crossing = [("x", di) for di in others] + ["far"] + corners
+    names = ["up", "down", "geo"] + crossing
     plans = [
-        [(place["far"], half, half), (0, 0, part), (2, 0, GEO), (1, part - GEO, GEO)],
-        [(x, 0, half) for x in xs] + [(1, 0, part)],
-        [(x, 0, full) for x in xs] + [(place["far"], 0, full), (0, 0, part), (1, 0, part)],
+        [(0, 0, picks), (2, 0, GEO), (0, picks, GEO), (1, picks, GEO)],
+        [(1, 0, picks)],
+        [(i + 3, 0, buffers[name].shape[0]) for i, name in enumerate(crossing)] + [(0, 0, picks), (1, 0, picks)],
     ]
-
-    two_x, two_y = pack([buffers[name] for name in names], plans[:2], [m_row], "pack_two")
+    two_x, two_y = pack(
+        [buffers[name] for name in names[:3]], plans[:2], [buffers[name] for name in corners] + [m_row], "pack_two"
+    )
 
     early_order = ["own", "mate", "far", "up", "down", "geo"] + [("x", di) for di in others]
-    early_order += [("two x", di) for di in others] + ["two y", "two m"]
+    early_order += corners + [("two x", di) for di in others] + ["two y", "two m"]
     late_order = [("three x", di) for di in others] + ["three y", "three m"]
     late_order += ["four"]
 
     contents = {}
     for di in others:
-        contents["two x", di] = [(("end", di, 2), half)] + side_of("up", di, 0)
-        contents["two x", di] += [(("geo", di, 0), GEO), (("down geo", di, 0), GEO)]
-    contents["two y"] = [(("top", di, 2), half) for di in others] + side_of("down", 0, 2)
+        contents["two x", di] = side_of("up", di, 0) + [(("geo", di, 0), GEO)]
+        contents["two x", di] += [(("up geo", di, 0), GEO), (("down geo", di, 0), GEO)]
+    contents["two y"] = side_of("down", 0, 2)
     contents["two m"] = sum([row_of(di, 1) for di in others], []) + row_of(0, 3)
+    contents["two m"] += [(("end", di, 3), half) for di in others] + [(("top", di, 3), half) for di in others]
     contents["two m"] += side_of("up", 0, 1) + side_of("down", 0, 1)
     for di in others:
         contents["three x", di] = side_of("down", di, 0) + side_of("down", di, 2)
     contents["three y"] = side_of("up", 0, 2) + sum([side_of("up", di, 2) for di in others], [])
-    contents["three m"] = []
-    for di in others:
-        contents["three m"] += [(("end", di, 3), half)] + side_of("up", di, 1) + [(None, 2 * GEO)]
-    contents["three m"] += [(("top", di, 3), half) for di in others] + side_of("down", 0, 3)
+    contents["three m"] = sum([side_of("up", di, 1) for di in others], []) + side_of("down", 0, 3)
     contents["three m"] += [("geos", count * 3 * GEO)]
     contents["four"] = []
     for di in others:
@@ -560,7 +569,7 @@
         scratch_shapes=[
             pltpu.SMEM((slots, atoms), jnp.int32),
             pltpu.SMEM((atoms,), jnp.int32),
-            pltpu.SMEM((4, slots), jnp.int32),
+            pltpu.SMEM((3, slots), jnp.int32),
             pltpu.SMEM((atoms,), jnp.int32),
             pltpu.SMEM((len(layout),), jnp.int32),
             pltpu.SemaphoreType.DMA((2,)),
@@ -578,8 +587,6 @@
 
     names = ["up", "down", "two y", "geo"] + [("two x", di) for di in others]
     place = {name: i for i, name in enumerate(names)}
-    y_down = at["down", 0, 2][1]
-    x_up = at["up", 1, 0][1]
     gather = []
     for di in range(count):
         for kind in ("geo", "up geo", "down geo"):
@@ -587,9 +594,9 @@
             gather.append((place[name], start, GEO))
     xs = [place["two x", di] for di in others]
     plans = [
-        [(1, 0, part), (2, y_down, part)],
-        [(0, 0, part)] + [(x, x_up, part) for x in xs],
-        [(x, 0, lengths["two x", 1]) for x in xs] + [(2, 0, lengths["two y"])] + gather,
+        [(1, 0, picks), (2, 0, picks)],
+        [(0, 0, picks)] + [(x, 0, picks) for x in xs],
+        [(x, 0, picks) for x in xs] + [(2, 0, picks)] + gather,
         gather,
     ]
     three_x, three_y, three_m, geos = pack([buffers[name] for name in names], plans, [own_basis], "pack_three")
@@ -603,7 +610,7 @@
     gram = pl.pallas_call(
         functools.partial(gram_kernel, len(early_values)),
         out_shape=jax.ShapeDtypeStruct((full, full), jnp.bfloat16),
-        in_specs=[SMEM] + [ANY] * (len(early_values) + 2),
+        in_specs=[SMEM] + [ANY] * (len(early_values) + 1),
         out_specs=VMEM,
         scratch_shapes=[
             pltpu.VMEM((late_from, LANES), jnp.bfloat16),
@@ -612,10 +619,10 @@
         compiler_params=pltpu.CompilerParams(vmem_limit_bytes=(6 << 20) + late_from * LANES * 2),
         cost_estimate=pl.CostEstimate(flops=1000, bytes_accessed=1000, transcendentals=0),
         name="gram_early",
-    )(early_table, *early_values, three_x, third_geos)
+    )(early_table, *early_values, three_x)
 
     thirds = [buffers["three x", di] for di in others] + [buffers["three y"]]
-    four = pack(thirds, [[(i, 0, value.shape[0]) for i, value in enumerate(thirds)]], [gram], "pack_four")[0]
+    four = pack(thirds, [[(i, 0, value.shape[0]) for i, value in enumerate(thirds)]], [gram, third_geos], "pack_four")[0]
     note("four", from_layer(four, 1), contents["four"])
 
     column_steps = (0, 1, -1)

time: 76.9 us -> 73 us (0.949)
  waiting for transfers between devices: 32.2 us -> 22.5 us
  starting transfers between devices: 16.4 us -> 21 us
  Pallas kernels: 26.2 us -> 27.4 us
    ppermute x8 -> x9, waiting for transfers between devices: 12.3 us -> 4.96 us  [from_layer(): return lax.ppermute(x, 'layer', [(i ^ flip, i) for i in range(count)])]
    ppermute x10 -> x11, starting transfers between devices: 10.4 us -> 14.7 us  [from_offset(): lax.ppermute(x, axis, [((i + step) % count, i) for i in range(count)])]
    ppermute x10 -> x11, waiting for transfers between devices: 19.9 us -> 17.6 us  [from_offset(): lax.ppermute(x, axis, [((i + step) % count, i) for i in range(count)])]
    pallas_call x1, Pallas kernels: 3.62 us -> 4.63 us  [local(): pl.pallas_call(functools.partial(gram_kernel, len(early_values)), out_sha...]
    pallas_call x4 -> x5, Pallas kernels: 3.49 us -> 4.05 us  [pack(): pl.pallas_call(functools.partial(pack_kernel, tuple(moves), inputs, len(p...]
    ppermute x8 -> x9, starting transfers between devices: 5.93 us -> 6.3 us  [from_layer(): return lax.ppermute(x, 'layer', [(i ^ flip, i) for i in range(count)])]
  transfers between devices with their start and end apart: 18 -> 20, of which waited for: 9 -> 12; matrix products, arithmetic and copies ran while one was open for 0% -> 0% of each run, Pallas kernels for 22% -> 26%
where the time goes in v8:
time: 73 us; the launch traced here: 72.8 us
  Pallas kernels  27.4 us (38%)
  waiting for transfers between devices  22.5 us (31%)
  starting transfers between devices  21 us (29%)
  local copies, waits for them, and re-layouts  0.86 us (1%)
  between operations  0.79 us (1%)
    ppermute x11, waiting for transfers between devices, from_offset(): lax.ppermute(x, axis, [((i + step) % count, i) for i in range(count)])  17.6 us
    ppermute x11, starting transfers between devices, from_offset(): lax.ppermute(x, axis, [((i + step) % count, i) for i in range(count)])  14.7 us
    ppermute x9, starting transfers between devices, from_layer(): return lax.ppermute(x, 'layer', [(i ^ flip, i) for i in range(count)])  6.3 us
    pallas_call x1, Pallas kernels, local(): pl.pallas_call(functools.partial(prepare_kernel, axes, count, tuple(layou...  5.8 us
    pallas_call x1, Pallas kernels, local(): pl.pallas_call(functools.partial(step_kernel, len(late_values)), out_shap...  5.49 us
    ppermute x9, waiting for transfers between devices, from_layer(): return lax.ppermute(x, 'layer', [(i ^ flip, i) for i in range(count)])  4.96 us
    pallas_call x1, Pallas kernels, local(): pl.pallas_call(functools.partial(gram_kernel, len(early_values)), out_sha...  4.63 us
    pallas_call x5, Pallas kernels, pack(): pl.pallas_call(functools.partial(pack_kernel, tuple(moves), inputs, len(p...  4.05 us
  transfers between devices with their start and end apart: 20, of which 12 were waited for; matrix products, arithmetic and copies ran while one was open for 0% of the time, Pallas kernels for 26%

profile of v8, /device:TPU:0, one launch (start us, length us, event | category | flops | bytes accessed | tf_op | source)
XLA Modules:
  0.0 72.8 jit_solution(13722558756678056712)
XLA Ops:
  0.6 3.0 %collective-permute-start.2 = (bf16[1536,128]{1,0:T(8,128)(2,1)}, bf16[1536,128]{1,0:T(8,128)(2,1)S(1)}, u32[]{:S(2)}, u32[]{:S(2)}) collective-permute-start(bf16[1536,128]{1,0:T(8,128)(2,1)} %bitcast.11), channel_id=1, source_target_pairs={{2,0},{3,1},{0,2},{1,3},{6,4},{7,5},{4,6},{5,7},{10,8},{11,9},{8,1... | collective-permute-start | bytes 1179656 | tf_op jit(solution)/shard_map/ppermute | solution.py:31
  3.7 1.5 %collective-permute-start.3 = (bf16[1536,128]{1,0:T(8,128)(2,1)}, bf16[1536,128]{1,0:T(8,128)(2,1)S(1)}, u32[]{:S(2)}, u32[]{:S(2)}) collective-permute-start(bf16[1536,128]{1,0:T(8,128)(2,1)} %bitcast.12), channel_id=1, source_target_pairs={{16,0},{0,16},{17,1},{1,17},{18,2},{2,18},{19,3},{3,19},{20,4},{4,... | collective-permute-start | bytes 1179656 | tf_op jit(solution)/shard_map/ppermute | solution.py:26
  5.2 0.0 collective-permute-start.6
  5.2 2.5 %pick_column_blocks.1 = (bf16[784,128]{1,0:T(8,128)(2,1)}, bf16[16,128]{1,0:T(8,128)(2,1)}) custom-call(s32[12,32]{1,0:T(8,128)} %bitcast.19, s32[1,12]{1,0:T(1,128)} %refs_1_.2, s32[32]{0:T(128)} %refs_2_.1, s32[32]{0:T(128)} %refs_3_.1, s32[32]{0:T(128)} %refs_4_.1, bf16[12,128,128]{2,1,0:T(8,128)(2,1)} %bitcast.14), custom_call_target="tpu_custom_call" | custom-call | tf_op jit(solution)/shard_map/pick_column_blocks/pallas_call | solution.py:438
  7.7 3.7 %collective-permute-start = (bf16[784,128]{1,0:T(8,128)(2,1)}, bf16[784,128]{1,0:T(8,128)(2,1)S(1)}, u32[]{:S(2)}, u32[]{:S(2)}) collective-permute-start(bf16[784,128]{1,0:T(8,128)(2,1)} %get-tuple-element.21), channel_id=1, source_target_pairs={{4,0},{8,4},{12,8},{0,12},{5,1},{9,5},{13,9},{1,13},{6,2},{10,6},{... | collective-permute-start | bytes 602120 | tf_op jit(solution)/shard_map/ppermute | solution.py:26
  11.3 0.0 collective-permute-start.1
  11.3 1.7 %collective-permute-done.2.refs_0_.refs_4_.refs_3_ = bf16[1536,128]{1,0:T(8,128)(2,1)S(1)} collective-permute-done((bf16[1536,128]{1,0:T(8,128)(2,1)}, bf16[1536,128]{1,0:T(8,128)(2,1)S(1)}, u32[]{:S(2)}, u32[]{:S(2)}) %collective-permute-start.2) | collective-permute-done | bytes 393248 | tf_op jit(solution)/shard_map/ppermute | solution.py:31
  13.0 1.5 %collective-permute-done.3.refs_1_.refs_3_.refs_7_ = bf16[1536,128]{1,0:T(8,128)(2,1)S(1)} collective-permute-done((bf16[1536,128]{1,0:T(8,128)(2,1)}, bf16[1536,128]{1,0:T(8,128)(2,1)S(1)}, u32[]{:S(2)}, u32[]{:S(2)}) %collective-permute-start.3) | collective-permute-done | bytes 393248 | tf_op jit(solution)/shard_map/ppermute | solution.py:26
  14.4 0.5 pack_halves.1
  15.0 1.6 %collective-permute-start.4 = (bf16[768,128]{1,0:T(8,128)(2,1)S(1)}, bf16[768,128]{1,0:T(8,128)(2,1)S(1)}, u32[]{:S(2)}, u32[]{:S(2)}) collective-permute-start(bf16[768,128]{1,0:T(8,128)(2,1)S(1)} %get-tuple-element.23), channel_id=1, source_target_pairs={{16,0},{0,16},{17,1},{1,17},{18,2},{2,18},{19,3},{3,19},{20,4},{4,... | collective-permute-start | bytes 589832 | tf_op jit(solution)/shard_map/ppermute | solution.py:26
  16.5 0.5 collective-permute-start.5
  17.0 0.0 collective-permute-done.refs_0_.refs_4_
  17.0 4.6 %collective-permute-done.1.refs_1_.refs_5_ = bf16[784,128]{1,0:T(8,128)(2,1)S(1)} collective-permute-done((bf16[784,128]{1,0:T(8,128)(2,1)}, bf16[784,128]{1,0:T(8,128)(2,1)S(1)}, u32[]{:S(2)}, u32[]{:S(2)}) %collective-permute-start.1) | collective-permute-done | bytes 200736 | tf_op jit(solution)/shard_map/ppermute | solution.py:26
  21.6 0.0 collective-permute-done.6.refs_5_.refs_2_
  21.7 0.0 collective-permute-done.4.refs_3_.refs_5_.refs_8_
  21.7 0.5 collective-permute-done.5.refs_4_.refs_6_.refs_9_
  22.2 0.7 copy-done.1
  22.9 0.5 pack_two.1
  23.3 0.0 copy-start.3
  23.3 0.0 copy-start.4
  23.4 0.0 copy-start.5
  23.4 1.4 %pack_two_mate.1 = bf16[5888,128]{1,0:T(8,128)(2,1)S(1)} custom-call(bf16[784,128]{1,0:T(8,128)(2,1)S(1)} %collective-permute-done.refs_0_.refs_4_, bf16[784,128]{1,0:T(8,128)(2,1)S(1)} %collective-permute-done.1.refs_1_.refs_5_, bf16[16,128]{1,0:T(8,128)(2,1)S(1)} %copy-done.1, bf16[1536,128]{1,0:T(8,128)(2,1)S(1)} %collective-permute-done.3.refs_1_.refs_3_.refs_7_, ...), custom_call_target="tpu_custom_call" | custom-call | bytes 3000000 | tf_op jit(solution)/shard_map/pack_two_mate/pallas_call | solution.py:232
  24.7 0.1 collective-permute-start.9
  24.8 0.6 collective-permute-start.7
  25.4 0.4 collective-permute-start.8
  25.8 0.0 copy-done.3
  25.8 0.0 copy-done.4
  25.8 0.0 copy-done.5
  25.8 0.0 copy-start
  25.8 5.8 %prepare.1 = (s32[247]{0:T(256)S(1)}, s32[247]{0:T(256)S(1)}, s32[14]{0:T(128)S(1)}, bf16[128,1536]{1,0:T(8,128)(2,1)S(1)}, bf16[16,128]{1,0:T(8,128)(2,1)S(1)}) custom-call(s32[12,32]{1,0:T(8,128)S(1)} %bitcast.20, s32[32]{0:T(128)S(1)} %copy-done.5, bf16[192,128]{1,0:T(8,128)(2,1)S(1)} %bitcast.21, bf16[688,128]{1,0:T(8,128)(2,1)S(1)} %get-tuple-element.25.refs_3_.refs_7_), custom_call_target="tpu_custom_call" | custom-call | flops 6000000000 | bytes 8000000 | tf_op jit(solution)/shard_map/prepare/pallas_call | solution.py:558
  31.6 0.1 collective-permute-done.8.refs_2_.refs_11_
  31.7 0.0 collective-permute-done.7.refs_4_.refs_10_
  31.7 0.0 copy-done.2
  31.7 1.5 %pack_three.1 = (bf16[1280,128]{1,0:T(8,128)(2,1)S(1)}, bf16[1280,128]{1,0:T(8,128)(2,1)S(1)}, bf16[1376,128]{1,0:T(8,128)(2,1)S(1)}, bf16[96,128]{1,0:T(8,128)(2,1)S(1)}) custom-call(bf16[784,128]{1,0:T(8,128)(2,1)S(1)} %collective-permute-done.refs_0_.refs_4_, bf16[784,128]{1,0:T(8,128)(2,1)S(1)} %collective-permute-done.1.refs_1_.refs_5_, ...), custom_call_target="tpu_custom_call" | custom-call | bytes 3000000 | tf_op jit(solution)/shard_map/pack_three/pallas_call | solution.py:232
  33.2 1.7 %collective-permute-start.10 = (bf16[1280,128]{1,0:T(8,128)(2,1)S(1)}, bf16[1280,128]{1,0:T(8,128)(2,1)S(1)}, u32[]{:S(2)}, u32[]{:S(2)}) collective-permute-start(bf16[1280,128]{1,0:T(8,128)(2,1)S(1)} %get-tuple-element.32.refs_13_), channel_id=1, source_target_pairs={{16,0},{0,16},{17,1},{1,17},{18,2},{2,18},{19,3},{3,19},{20,4},{4,... | collective-permute-start | bytes 983048 | tf_op jit(solution)/shard_map/ppermute | solution.py:26
  34.9 1.5 %collective-permute-start.11 = (bf16[1280,128]{1,0:T(8,128)(2,1)S(1)}, bf16[1280,128]{1,0:T(8,128)(2,1)S(1)}, u32[]{:S(2)}, u32[]{:S(2)}) collective-permute-start(bf16[1280,128]{1,0:T(8,128)(2,1)S(1)} %get-tuple-element.33), channel_id=1, source_target_pairs={{2,0},{3,1},{0,2},{1,3},{6,4},{7,5},{4,6},{5,7},{10,8},{11,9},{8,1... | collective-permute-start | bytes 983048 | tf_op jit(solution)/shard_map/ppermute | solution.py:31
  36.4 0.0 collective-permute-start.12
  36.4 0.6 collective-permute-start.13
  37.0 0.0 collective-permute-done.9.refs_12_
  37.0 4.6 %gram_early.1.refs_2_.refs_3_.refs_5_ = bf16[1536,1536]{1,0:T(8,128)(2,1)S(1)} custom-call(s32[247]{0:T(256)S(1)} %get-tuple-element.30.refs_0_, bf16[1536,128]{1,0:T(8,128)(2,1)S(1)} %bitcast.15, bf16[1536,128]{1,0:T(8,128)(2,1)S(1)} %collective-permute-done.6.refs_5_.refs_2_, bf16[1536,128]{1,0:T(8,128)(2,1)S(1)} %collective-permute-done.2.refs_0_.refs_4_.refs_3_, ...), custom_call_target="tpu_custom_call" | custom-call | flops 1000 | bytes 1000 | tf_op jit(solution)/shard_map/gram_early/pallas_call | solution.py:610
  41.7 2.0 %collective-permute-done.13.refs_3_.refs_2_ = bf16[96,128]{1,0:T(8,128)(2,1)S(1)} collective-permute-done((bf16[96,128]{1,0:T(8,128)(2,1)S(1)}, bf16[96,128]{1,0:T(8,128)(2,1)S(1)}, u32[]{:S(2)}, u32[]{:S(2)}) %collective-permute-start.13) | collective-permute-done | bytes 24608 | tf_op jit(solution)/shard_map/ppermute | solution.py:31
  43.7 0.0 collective-permute-done.10.refs_0_.refs_6_
  43.7 0.7 collective-permute-done.11.refs_1_.refs_7_
  44.4 0.2 pack_four.1
  44.6 0.2 collective-permute-start.14
  44.8 0.0 collective-permute-done.12.refs_1_.refs_8_
  44.8 3.5 %profiles.1 = (bf16[6,6,256,128]{3,2,1,0:T(8,128)(2,1)S(1)}, bf16[6,6,128,128]{3,2,1,0:T(8,128)(2,1)S(1)}) custom-call(bf16[96,128]{1,0:T(8,128)(2,1)S(1)} %get-tuple-element.35.refs_0_, bf16[1376,128]{1,0:T(8,128)(2,1)S(1)} %collective-permute-done.12.refs_1_.refs_8_, bf16[96,128]{1,0:T(8,128)(2,1)S(1)} %collective-permute-done.13.refs_3_.refs_2_, ...), custom_call_target="tpu_custom_call" | custom-call | flops 5000000000 | bytes 4000000 | tf_op jit(solution)/shard_map/profiles/pallas_call | solution.py:632
  48.3 0.0 collective-permute-done.14.refs_9_
  48.3 5.5 %square_cube_coefficients.1 = (bf16[12,128,128]{2,1,0:T(8,128)(2,1)}, f32[8,128]{1,0:T(8,128)S(1)}) custom-call(s32[247]{0:T(256)S(1)} %get-tuple-element.26.refs_0_, s32[14]{0:T(128)S(1)} %get-tuple-element.27.refs_1_, bf16[16,128]{1,0:T(8,128)(2,1)S(1)} %get-tuple-element.28.refs_5_.refs_2_, bf16[128,1536]{1,0:T(8,128)(2,1)S(1)} %get-tuple-element.29.refs_3_, ...), custom_call_target="tpu_custom_call" | custom-call | flops 1300000000 | bytes 8000000 | tf_op jit(solution)/shard_map/square_cube_coefficients/pallas_call | solution.py:650
  53.8 1.6 %collective-permute-start.16 = (f32[8,128]{1,0:T(8,128)S(1)}, f32[8,128]{1,0:T(8,128)S(1)}, u32[]{:S(2)}, u32[]{:S(2)}) collective-permute-start(f32[8,128]{1,0:T(8,128)S(1)} %get-tuple-element.38), channel_id=1, source_target_pairs={{1,0},{2,1},{3,2},{0,3},{5,4},{6,5},{7,6},{4,7},{9,8},{10,9},{11,1... | collective-permute-start | bytes 12296 | tf_op jit(solution)/shard_map/ppermute | solution.py:26
  55.4 0.0 collective-permute-start.15
  55.4 1.3 %collective-permute-done.16 = f32[8,128]{1,0:T(8,128)S(1)} collective-permute-done((f32[8,128]{1,0:T(8,128)S(1)}, f32[8,128]{1,0:T(8,128)S(1)}, u32[]{:S(2)}, u32[]{:S(2)}) %collective-permute-start.16) | collective-permute-done | bytes 4128 | tf_op jit(solution)/shard_map/ppermute | solution.py:26
  56.7 0.1 slice.11
  56.8 1.6 %collective-permute-done.15 = f32[8,128]{1,0:T(8,128)S(1)} collective-permute-done((f32[8,128]{1,0:T(8,128)S(1)}, f32[8,128]{1,0:T(8,128)S(1)}, u32[]{:S(2)}, u32[]{:S(2)}) %collective-permute-start.15) | collective-permute-done | bytes 4128 | tf_op jit(solution)/shard_map/ppermute | solution.py:26
  58.4 0.1 slice.10
  58.5 0.1 pad_maximum_fusion.1
  58.6 0.5 collective-permute-start.17
  59.1 3.1 %collective-permute-done.17 = f32[8,128]{1,0:T(8,128)S(1)} collective-permute-done((f32[8,128]{1,0:T(8,128)S(1)}, f32[8,128]{1,0:T(8,128)S(1)}, u32[]{:S(2)}, u32[]{:S(2)}) %collective-permute-start.17) | collective-permute-done | bytes 4128 | tf_op jit(solution)/shard_map/ppermute | solution.py:26
  62.2 0.1 pad_maximum_fusion.refs_0_
  62.2 3.6 %collective-permute-start.18 = (f32[16,128]{1,0:T(8,128)S(1)}, f32[16,128]{1,0:T(8,128)S(1)}, u32[]{:S(2)}, u32[]{:S(2)}) collective-permute-start(f32[16,128]{1,0:T(8,128)S(1)} %pad_maximum_fusion.refs_0_), channel_id=1, source_target_pairs={{4,0},{8,4},{12,8},{0,12},{5,1},{9,5},{13,9},{1,13},{6,2},{10,6},{... | collective-permute-start | bytes 24584 | tf_op jit(solution)/shard_map/ppermute | solution.py:26
  65.8 0.0 collective-permute-start.19
  65.8 1.4 %collective-permute-done.18.refs_1_ = f32[16,128]{1,0:T(8,128)S(1)} collective-permute-done((f32[16,128]{1,0:T(8,128)S(1)}, f32[16,128]{1,0:T(8,128)S(1)}, u32[]{:S(2)}, u32[]{:S(2)}) %collective-permute-start.18) | collective-permute-done | bytes 8224 | tf_op jit(solution)/shard_map/ppermute | solution.py:26
  67.2 4.1 %collective-permute-done.19.refs_2_ = f32[16,128]{1,0:T(8,128)S(1)} collective-permute-done((f32[16,128]{1,0:T(8,128)S(1)}, f32[16,128]{1,0:T(8,128)S(1)}, u32[]{:S(2)}, u32[]{:S(2)}) %collective-permute-start.19) | collective-permute-done | bytes 8224 | tf_op jit(solution)/shard_map/ppermute | solution.py:26
  71.3 1.5 %density.1 = f32[256,128]{1,0:T(8,128)} custom-call(f32[16,128]{1,0:T(8,128)S(1)} %pad_maximum_fusion.refs_0_, f32[16,128]{1,0:T(8,128)S(1)} %collective-permute-done.18.refs_1_, f32[16,128]{1,0:T(8,128)S(1)} %collective-permute-done.19.refs_2_, bf16[6,6,256,128]{3,2,1,0:T(8,128)(2,1)S(1)} %get-tuple-element.39.refs_3_, bf16[4608,128]{1,0:T(8,128)(2,1)S(1)} %bitcast.10), custom_call_target="tpu_custom_call" | custom-call | flops 310000000 | bytes 4000000 | tf_op jit(solution)/shard_map/density/pallas_call | solution.py:684
  (4 shorter events, 0.0 us)
Async XLA Ops:
  0.6 12.4 %collective-permute-start.2 = (bf16[1536,128]{1,0:T(8,128)(2,1)}, bf16[1536,128]{1,0:T(8,128)(2,1)S(1)}, u32[]{:S(2)}, u32[]{:S(2)}) collective-permute-start(bf16[1536,128]{1,0:T(8,128)(2,1)} %bitcast.11), channel_id=1, source_target_pairs={{2,0},{3,1},{0,2},{1,3},{6,4},{7,5},{4,6},{5,7},{10,8},{11,9},{8,1... | collective-permute-start | bytes 1179656 | tf_op jit(solution)/shard_map/ppermute | solution.py:31
  3.7 10.8 %collective-permute-start.3 = (bf16[1536,128]{1,0:T(8,128)(2,1)}, bf16[1536,128]{1,0:T(8,128)(2,1)S(1)}, u32[]{:S(2)}, u32[]{:S(2)}) collective-permute-start(bf16[1536,128]{1,0:T(8,128)(2,1)} %bitcast.12), channel_id=1, source_target_pairs={{16,0},{0,16},{17,1},{1,17},{18,2},{2,18},{19,3},{3,19},{20,4},{4,... | collective-permute-start | bytes 1179656 | tf_op jit(solution)/shard_map/ppermute | solution.py:26
  5.2 16.5 %collective-permute-start.6 = (bf16[1536,128]{1,0:T(8,128)(2,1)}, bf16[1536,128]{1,0:T(8,128)(2,1)S(1)}, u32[]{:S(2)}, u32[]{:S(2)}) collective-permute-start(bf16[1536,128]{1,0:T(8,128)(2,1)} %bitcast.13), channel_id=1, source_target_pairs={{1,0},{0,1},{3,2},{2,3},{5,4},{4,5},{7,6},{6,7},{9,8},{8,9},{11,10... | collective-permute-start | bytes 1179656 | tf_op jit(solution)/shard_map/ppermute | solution.py:31
  7.7 9.4 %collective-permute-start = (bf16[784,128]{1,0:T(8,128)(2,1)}, bf16[784,128]{1,0:T(8,128)(2,1)S(1)}, u32[]{:S(2)}, u32[]{:S(2)}) collective-permute-start(bf16[784,128]{1,0:T(8,128)(2,1)} %get-tuple-element.21), channel_id=1, source_target_pairs={{4,0},{8,4},{12,8},{0,12},{5,1},{9,5},{13,9},{1,13},{6,2},{10,6},{... | collective-permute-start | bytes 602120 | tf_op jit(solution)/shard_map/ppermute | solution.py:26
  11.3 10.3 %collective-permute-start.1 = (bf16[784,128]{1,0:T(8,128)(2,1)}, bf16[784,128]{1,0:T(8,128)(2,1)S(1)}, u32[]{:S(2)}, u32[]{:S(2)}) collective-permute-start(bf16[784,128]{1,0:T(8,128)(2,1)} %get-tuple-element.21), channel_id=1, source_target_pairs={{12,0},{0,4},{4,8},{8,12},{13,1},{1,5},{5,9},{9,13},{14,2},{2,6},{... | collective-permute-start | bytes 602120 | tf_op jit(solution)/shard_map/ppermute | solution.py:26
  15.0 6.7 %collective-permute-start.4 = (bf16[768,128]{1,0:T(8,128)(2,1)S(1)}, bf16[768,128]{1,0:T(8,128)(2,1)S(1)}, u32[]{:S(2)}, u32[]{:S(2)}) collective-permute-start(bf16[768,128]{1,0:T(8,128)(2,1)S(1)} %get-tuple-element.23), channel_id=1, source_target_pairs={{16,0},{0,16},{17,1},{1,17},{18,2},{2,18},{19,3},{3,19},{20,4},{4,... | collective-permute-start | bytes 589832 | tf_op jit(solution)/shard_map/ppermute | solution.py:26
  16.5 5.7 %collective-permute-start.5 = (bf16[768,128]{1,0:T(8,128)(2,1)S(1)}, bf16[768,128]{1,0:T(8,128)(2,1)S(1)}, u32[]{:S(2)}, u32[]{:S(2)}) collective-permute-start(bf16[768,128]{1,0:T(8,128)(2,1)S(1)} %get-tuple-element.24), channel_id=1, source_target_pairs={{2,0},{3,1},{0,2},{1,3},{6,4},{7,5},{4,6},{5,7},{10,8},{11,9},{8,1... | collective-permute-start | bytes 589832 | tf_op jit(solution)/shard_map/ppermute | solution.py:31
  22.2 0.7 copy-start.1
  23.3 2.5 %copy-start.3 = (s32[32,12]{0,1:T(8,128)S(1)}, s32[32,12]{0,1:T(8,128)}, u32[]{:S(2)}) copy-start(s32[32,12]{0,1:T(8,128)} %param.9) | copy-start | bytes 4612
  23.3 2.4 %copy-start.4 = (bf16[32,6,128]{2,0,1:T(8,128)(2,1)S(1)}, bf16[32,6,128]{2,0,1:T(8,128)(2,1)}, u32[]{:S(2)}) copy-start(bf16[32,6,128]{2,0,1:T(8,128)(2,1)} %param.11) | copy-start | bytes 147460
  23.4 2.4 %copy-start.5 = (s32[32]{0:T(128)S(1)}, s32[32]{0:T(128)}, u32[]{:S(2)}) copy-start(s32[32]{0:T(128)} %refs_1_.3) | copy-start | bytes 388
  24.7 12.3 %collective-permute-start.9 = (bf16[5888,128]{1,0:T(8,128)(2,1)S(1)}, bf16[5888,128]{1,0:T(8,128)(2,1)S(1)}, u32[]{:S(2)}, u32[]{:S(2)}) collective-permute-start(bf16[5888,128]{1,0:T(8,128)(2,1)S(1)} %pack_two_mate.1), channel_id=1, source_target_pairs={{1,0},{0,1},{3,2},{2,3},{5,4},{4,5},{7,6},{6,7},{9,8},{8,9},{11,10... | collective-permute-start | bytes 4521992 | tf_op jit(solution)/shard_map/ppermute | solution.py:31
  24.8 6.9 %collective-permute-start.7 = (bf16[688,128]{1,0:T(8,128)(2,1)S(1)}, bf16[688,128]{1,0:T(8,128)(2,1)S(1)}, u32[]{:S(2)}, u32[]{:S(2)}) collective-permute-start(bf16[688,128]{1,0:T(8,128)(2,1)S(1)} %get-tuple-element.25.refs_3_.refs_7_), channel_id=1, source_target_pairs={{16,0},{0,16},{17,1},{1,17},{18,2},{2,18},{19,3},{3,19},{20,4},{4,... | collective-permute-start | bytes 528392 | tf_op jit(solution)/shard_map/ppermute | solution.py:26
  25.4 6.3 %collective-permute-start.8 = (bf16[640,128]{1,0:T(8,128)(2,1)S(1)}, bf16[640,128]{1,0:T(8,128)(2,1)S(1)}, u32[]{:S(2)}, u32[]{:S(2)}) collective-permute-start(bf16[640,128]{1,0:T(8,128)(2,1)S(1)} %get-tuple-element.31), channel_id=1, source_target_pairs={{2,0},{3,1},{0,2},{1,3},{6,4},{7,5},{4,6},{5,7},{10,8},{11,9},{8,1... | collective-permute-start | bytes 491528 | tf_op jit(solution)/shard_map/ppermute | solution.py:31
  25.8 5.9 %copy-start.2 = (bf16[16,128]{1,0:T(8,128)(2,1)S(1)}, bf16[16,128]{1,0:T(8,128)(2,1)}, u32[]{:S(2)}) copy-start(bf16[16,128]{1,0:T(8,128)(2,1)} %get-tuple-element.22.refs_2_.refs_3_.refs_6_) | copy-start | bytes 12292
  25.8 11.2 %copy-start = (bf16[1,12,128,128]{3,2,1,0:T(8,128)(2,1)S(1)}, bf16[1,12,128,128]{3,2,1,0:T(8,128)(2,1)}, u32[]{:S(2)}) copy-start(bf16[1,12,128,128]{3,2,1,0:T(8,128)(2,1)} %param.8) | copy-start | bytes 1179652
  33.2 10.5 %collective-permute-start.10 = (bf16[1280,128]{1,0:T(8,128)(2,1)S(1)}, bf16[1280,128]{1,0:T(8,128)(2,1)S(1)}, u32[]{:S(2)}, u32[]{:S(2)}) collective-permute-start(bf16[1280,128]{1,0:T(8,128)(2,1)S(1)} %get-tuple-element.32.refs_13_), channel_id=1, source_target_pairs={{16,0},{0,16},{17,1},{1,17},{18,2},{2,18},{19,3},{3,19},{20,4},{4,... | collective-permute-start | bytes 983048 | tf_op jit(solution)/shard_map/ppermute | solution.py:26
  34.9 9.5 %collective-permute-start.11 = (bf16[1280,128]{1,0:T(8,128)(2,1)S(1)}, bf16[1280,128]{1,0:T(8,128)(2,1)S(1)}, u32[]{:S(2)}, u32[]{:S(2)}) collective-permute-start(bf16[1280,128]{1,0:T(8,128)(2,1)S(1)} %get-tuple-element.33), channel_id=1, source_target_pairs={{2,0},{3,1},{0,2},{1,3},{6,4},{7,5},{4,6},{5,7},{10,8},{11,9},{8,1... | collective-permute-start | bytes 983048 | tf_op jit(solution)/shard_map/ppermute | solution.py:31
  36.4 8.4 %collective-permute-start.12 = (bf16[1376,128]{1,0:T(8,128)(2,1)S(1)}, bf16[1376,128]{1,0:T(8,128)(2,1)S(1)}, u32[]{:S(2)}, u32[]{:S(2)}) collective-permute-start(bf16[1376,128]{1,0:T(8,128)(2,1)S(1)} %get-tuple-element.34), channel_id=1, source_target_pairs={{1,0},{0,1},{3,2},{2,3},{5,4},{4,5},{7,6},{6,7},{9,8},{8,9},{11,10... | collective-permute-start | bytes 1056776 | tf_op jit(solution)/shard_map/ppermute | solution.py:31
  36.4 7.3 %collective-permute-start.13 = (bf16[96,128]{1,0:T(8,128)(2,1)S(1)}, bf16[96,128]{1,0:T(8,128)(2,1)S(1)}, u32[]{:S(2)}, u32[]{:S(2)}) collective-permute-start(bf16[96,128]{1,0:T(8,128)(2,1)S(1)} %get-tuple-element.35.refs_0_), channel_id=1, source_target_pairs={{3,0},{2,1},{1,2},{0,3},{7,4},{6,5},{5,6},{4,7},{11,8},{10,9},{9,1... | collective-permute-start | bytes 73736 | tf_op jit(solution)/shard_map/ppermute | solution.py:31
  44.6 3.7 %collective-permute-start.14 = (bf16[2560,128]{1,0:T(8,128)(2,1)S(1)}, bf16[2560,128]{1,0:T(8,128)(2,1)S(1)}, u32[]{:S(2)}, u32[]{:S(2)}) collective-permute-start(bf16[2560,128]{1,0:T(8,128)(2,1)S(1)} %pack_four.1), channel_id=1, source_target_pairs={{1,0},{0,1},{3,2},{2,3},{5,4},{4,5},{7,6},{6,7},{9,8},{8,9},{11,10... | collective-permute-start | bytes 1966088 | tf_op jit(solution)/shard_map/ppermute | solution.py:31
  53.8 2.9 %collective-permute-start.16 = (f32[8,128]{1,0:T(8,128)S(1)}, f32[8,128]{1,0:T(8,128)S(1)}, u32[]{:S(2)}, u32[]{:S(2)}) collective-permute-start(f32[8,128]{1,0:T(8,128)S(1)} %get-tuple-element.38), channel_id=1, source_target_pairs={{1,0},{2,1},{3,2},{0,3},{5,4},{6,5},{7,6},{4,7},{9,8},{10,9},{11,1... | collective-permute-start | bytes 12296 | tf_op jit(solution)/shard_map/ppermute | solution.py:26
  55.4 3.0 %collective-permute-start.15 = (f32[8,128]{1,0:T(8,128)S(1)}, f32[8,128]{1,0:T(8,128)S(1)}, u32[]{:S(2)}, u32[]{:S(2)}) collective-permute-start(f32[8,128]{1,0:T(8,128)S(1)} %get-tuple-element.38), channel_id=1, source_target_pairs={{3,0},{0,1},{1,2},{2,3},{7,4},{4,5},{5,6},{6,7},{11,8},{8,9},{9,10... | collective-permute-start | bytes 12296 | tf_op jit(solution)/shard_map/ppermute | solution.py:26
  58.6 3.6 %collective-permute-start.17 = (f32[8,128]{1,0:T(8,128)S(1)}, f32[8,128]{1,0:T(8,128)S(1)}, u32[]{:S(2)}, u32[]{:S(2)}) collective-permute-start(f32[8,128]{1,0:T(8,128)S(1)} %pad_maximum_fusion.1), channel_id=1, source_target_pairs={{16,0},{0,16},{17,1},{1,17},{18,2},{2,18},{19,3},{3,19},{20,4},{4,... | collective-permute-start | bytes 12296 | tf_op jit(solution)/shard_map/ppermute | solution.py:26
  62.2 5.0 %collective-permute-start.18 = (f32[16,128]{1,0:T(8,128)S(1)}, f32[16,128]{1,0:T(8,128)S(1)}, u32[]{:S(2)}, u32[]{:S(2)}) collective-permute-start(f32[16,128]{1,0:T(8,128)S(1)} %pad_maximum_fusion.refs_0_), channel_id=1, source_target_pairs={{4,0},{8,4},{12,8},{0,12},{5,1},{9,5},{13,9},{1,13},{6,2},{10,6},{... | collective-permute-start | bytes 24584 | tf_op jit(solution)/shard_map/ppermute | solution.py:26
  65.8 5.4 %collective-permute-start.19 = (f32[16,128]{1,0:T(8,128)S(1)}, f32[16,128]{1,0:T(8,128)S(1)}, u32[]{:S(2)}, u32[]{:S(2)}) collective-permute-start(f32[16,128]{1,0:T(8,128)S(1)} %pad_maximum_fusion.refs_0_), channel_id=1, source_target_pairs={{12,0},{0,4},{4,8},{8,12},{13,1},{1,5},{5,9},{9,13},{14,2},{2,6},{... | collective-permute-start | bytes 24584 | tf_op jit(solution)/shard_map/ppermute | solution.py:26

commit v9 on v8

--- a/solution.py
+++ b/solution.py
@@ -168,43 +168,52 @@
         atom = known[0, v]
         side = known[1, v]
         line = known[2, v]
-        row, _, lay = at.split(atom)
         for u in range(slots):
             inverse[neighbors_ref[u, atom]] = v * 16 + u
-        top = layout_ref[line]
-        end = layout_ref[lines + line]
-        beside = layout_ref[(side + 1) * lines + line]
-        half = slots // 2
-        for w in range(slots):
-            other = known[0, w]
-            other_side = known[1, w]
-            mark = inverse[other]
-            slot = mark & 15
-            o_row, _, o_lay = at.split(other)
-            there = target_place(at.n_row, (o_row - row) & (at.n_row - 1), (o_lay - lay) & (at.n_lay - 1), row)
-            back = target_place(at.n_row, (row - o_row) & (at.n_row - 1), (lay - o_lay) & (at.n_lay - 1), o_row)
-            from_row = (other_side != 0) | (v <= w)
-            from_column = (side == other_side) & (there >= 0) & ((back < 0) | (v <= w))
-            chosen = ((mark >> 4) == v) & jnp.where(side == 0, from_row, from_column)
-            in_row = jnp.where(slot < half, top + slot * LANES, end + (slot - half) * LANES)
-            where = jnp.where(side == 0, in_row, beside + there * LANES)
-            is_late = where >= late_from
-            for ref, total in ((early_ref, early), (late_ref, late)):
-                ref[3 * total + 1] = v
-                ref[3 * total + 2] = w
-                ref[3 * total + 3] = where
-            late_ref[3 * late + 3] = where - late_from
-            early = early + (chosen & ~is_late).astype(jnp.int32)
-            late = late + (chosen & is_late).astype(jnp.int32)
-        return early, late
+
+        def from_row(totals):
+            total, late = totals
+            for w in range(slots):
+                mark = inverse[known[0, w]]
+                chosen = ((mark >> 4) == v) & ((known[1, w] != 0) | (v <= w))
+                where = layout_ref[line * slots + (mark & 15)]
+                is_late = where >= late_from
+                entry = v + 16 * w
+                early_ref[total + 1] = entry + 256 * where
+                late_ref[late + 1] = entry + 256 * (where - late_from)
+                total = total + (chosen & ~is_late).astype(jnp.int32)
+                late = late + (chosen & is_late).astype(jnp.int32)
+            return total, late
+
+        def from_column(totals):
+            early, late = totals
+            row, _, lay = at.split(atom)
+            beside = layout_ref[lines * slots + (side - 1) * lines + line]
+            for w in range(slots):
+                other = known[0, w]
+                mark = inverse[other]
+                o_row, _, o_lay = at.split(other)
+                d_row = (o_row - row) & (at.n_row - 1)
+                d_lay = (o_lay - lay) & (at.n_lay - 1)
+                there = target_place(at.n_row, d_row, d_lay, row)
+                back = target_place(at.n_row, -d_row & (at.n_row - 1), -d_lay & (at.n_lay - 1), o_row)
+                chosen = ((mark >> 4) == v) & (side == known[1, w]) & (there >= 0) & ((back < 0) | (v <= w))
+                where = beside + there * LANES
+                is_late = where >= late_from
+                entry = v + 16 * w
+                early_ref[early + 1] = entry + 256 * where
+                late_ref[late + 1] = entry + 256 * (where - late_from)
+                early = early + (chosen & ~is_late).astype(jnp.int32)
+                late = late + (chosen & is_late).astype(jnp.int32)
+            return early, late
+
+        return lax.cond(side == 0, from_row, from_column, (early, late))
 
     totals = lax.fori_loop(0, slots, row_of_pairs, (jnp.int32(0), jnp.int32(0)))
     for ref, total in zip((early_ref, late_ref), totals):
         ref[0] = (total + UNROLL - 1) // UNROLL
-        last = 3 * jnp.maximum(total - 1, 0) + 1
         for i in range(UNROLL - 1):
-            for k in range(3):
-                ref[3 * (total + i) + 1 + k] = ref[last + k]
+            ref[total + i + 1] = ref[jnp.maximum(total, 1)]
 
 
 def pack_kernel(moves, inputs, outputs, *refs):
@@ -256,10 +265,10 @@
 def place_pairs(table_ref, pool, gram, size):
     def place(i, carry):
         for k in range(UNROLL):
-            entry = 3 * (i * UNROLL + k)
-            p = pl.multiple_of(table_ref[entry + 1] * size, size)
-            q = pl.multiple_of(table_ref[entry + 2] * size, size)
-            block = pool[pl.ds(pl.multiple_of(table_ref[entry + 3], 16), size)]
+            entry = table_ref[i * UNROLL + k + 1]
+            p = pl.multiple_of((entry & 15) * size, size)
+            q = pl.multiple_of(((entry >> 4) & 15) * size, size)
+            block = pool[pl.ds(pl.multiple_of(entry >> 8, 16), size)]
             gram[pl.ds(p, size), pl.ds(q, size)] = block
             gram[pl.ds(q, size), pl.ds(p, size)] = block.T
         return carry
@@ -395,9 +404,14 @@
             line_ref[o, s] = jnp.where(inside_z, jnp.exp(-rate_z * squared_z), 0.0).astype(line_ref.dtype)
 
 
-def density_kernel(column_steps, *refs):
-    coef_refs = refs[:column_steps]
-    plane_ref, line_ref, out_ref, terms = refs[column_steps:]
+def density_kernel(column_steps, last, *refs):
+    own_ref, up_ref, down_ref, around_ref, plane_ref, line_ref, out_ref, terms = refs
+    col = lax.axis_index("col")
+    coef_refs = [
+        own_ref[...],
+        jnp.where(col == last, around_ref[...], up_ref[...]),
+        jnp.where(col == 0, around_ref[...], down_ref[...]),
+    ]
     for o in range(plane_ref.shape[0]):
         coef = coef_refs[o % column_steps]
         first = 8 * (o // column_steps)
@@ -425,6 +439,7 @@
     listings = neighbors.T
     full = slots * size
     half = full // 2
+    most = half - size
     n_pick = column_targets(n_row)
     picks = n_pick * size
     part = picks + GEO
@@ -438,7 +453,7 @@
     picked, geo = pl.pallas_call(
         functools.partial(pick_kernel, axes),
         out_shape=(
-            jax.ShapeDtypeStruct((max(part, half + GEO), size), own.dtype),
+            jax.ShapeDtypeStruct((part, size), own.dtype),
             jax.ShapeDtypeStruct((GEO, LANES), own.dtype),
         ),
         in_specs=[HBM] * 6,
@@ -461,7 +476,7 @@
 
     halves = pack(
         [y_row] + [x_row[di] for di in others],
-        [[(0, half, half)]] + [[(di, 0, half)] for di in others],
+        [[(0, half, most)]] + [[(di, 0, most)] for di in others],
         [],
         "pack_halves",
     )
@@ -479,8 +494,10 @@
                 at[what] = (name, start)
             start += rows
 
-    def row_of(di, flip):
-        return [(("top", di, flip), half), (("end", di, flip), half)]
+    def row_of(di, flip, start=0, stop=slots):
+        return [(("row", slot, di, flip), size) for slot in range(start, stop)]
+
+    halfway = slots // 2
 
     def side_of(kind, di, flip):
         return [((kind, di, flip), picks)]
@@ -493,38 +510,48 @@
     note("geo", geo, [(("geo", 0, 0), GEO)])
     for di in others:
         note(("x", di), x_row[di], row_of(di, 0))
-        note(("end", di), ends[di], [(("end", di, 2), half)])
-        note(("top", di), tops[di], [(("top", di, 2), half)])
+        note(("end", di), ends[di], row_of(di, 2, halfway, slots - 1))
+        note(("top", di), tops[di], row_of(di, 2, 0, halfway - 1))
 
     corners = [("end", di) for di in others] + [("top", di) for di in others]
-    crossing = [("x", di) for di in others] + ["far"] + corners
-    names = ["up", "down", "geo"] + crossing
+    names = ["up", "down", "geo", "far"] + [("x", di) for di in others]
     plans = [
-        [(0, 0, picks), (2, 0, GEO), (0, picks, GEO), (1, picks, GEO)],
-        [(1, 0, picks)],
-        [(i + 3, 0, buffers[name].shape[0]) for i, name in enumerate(crossing)] + [(0, 0, picks), (1, 0, picks)],
+        [(0, 0, picks), (3, full - size, size), (2, 0, GEO), (0, picks, GEO), (1, picks, GEO)],
+        [(1, 0, picks)] + [(di + 3, most, size) for di in others],
     ]
     two_x, two_y = pack(
-        [buffers[name] for name in names[:3]], plans[:2], [buffers[name] for name in corners] + [m_row], "pack_two"
+        [buffers[name] for name in names], plans, [buffers[name] for name in corners] + [m_row], "pack_two"
     )
+    to_mate = corners + ["up", "down"]
+    plans = [[(i, 0, picks if name in ("up", "down") else most) for i, name in enumerate(to_mate)]]
+    two_m = pack([buffers[name] for name in to_mate], plans, [], "pack_two_mate")[0]
+    for di in others:
+        note(("mate x", di), from_layer(x_row[di], 1), row_of(di, 1))
+    note("mate far", from_layer(y_row, 1), row_of(0, 3))
 
     early_order = ["own", "mate", "far", "up", "down", "geo"] + [("x", di) for di in others]
+    early_order += [("mate x", di) for di in others] + ["mate far"]
     early_order += corners + [("two x", di) for di in others] + ["two y", "two m"]
     late_order = [("three x", di) for di in others] + ["three y", "three m"]
     late_order += ["four"]
 
     contents = {}
     for di in others:
-        contents["two x", di] = side_of("up", di, 0) + [(("geo", di, 0), GEO)]
+        contents["two x", di] = side_of("up", di, 0) + row_of(di, 2, slots - 1, slots) + [(("geo", di, 0), GEO)]
         contents["two x", di] += [(("up geo", di, 0), GEO), (("down geo", di, 0), GEO)]
     contents["two y"] = side_of("down", 0, 2)
-    contents["two m"] = sum([row_of(di, 1) for di in others], []) + row_of(0, 3)
-    contents["two m"] += [(("end", di, 3), half) for di in others] + [(("top", di, 3), half) for di in others]
+    contents["two y"] += sum([row_of(di, 2, halfway - 1, halfway) for di in others], [])
+    contents["two m"] = sum([row_of(di, 3, halfway, slots - 1) for di in others], [])
+    contents["two m"] += sum([row_of(di, 3, 0, halfway - 1) for di in others], [])
     contents["two m"] += side_of("up", 0, 1) + side_of("down", 0, 1)
     for di in others:
         contents["three x", di] = side_of("down", di, 0) + side_of("down", di, 2)
     contents["three y"] = side_of("up", 0, 2) + sum([side_of("up", di, 2) for di in others], [])
-    contents["three m"] = sum([side_of("up", di, 1) for di in others], []) + side_of("down", 0, 3)
+    contents["three m"] = []
+    for di in others:
+        contents["three m"] += side_of("up", di, 1) + row_of(di, 3, slots - 1, slots)
+    contents["three m"] += side_of("down", 0, 3)
+    contents["three m"] += sum([row_of(di, 3, halfway - 1, halfway) for di in others], [])
     contents["three m"] += [("geos", count * 3 * GEO)]
     contents["four"] = []
     for di in others:
@@ -548,13 +575,19 @@
             located[what] = (name, start)
             start += rows
     layout = [
+        base[located["row", slot, di, flip][0]] + located["row", slot, di, flip][1]
+        for di in range(count)
+        for flip in range(n_lay)
+        for slot in range(slots)
+    ]
+    layout += [
         base[located[kind, di, flip][0]] + located[kind, di, flip][1]
-        for kind in ("top", "end", "up", "down")
+        for kind in ("up", "down")
         for di in range(count)
         for flip in range(n_lay)
     ]
     pairs = slots * (slots + 1) // 2
-    entries = 3 * (pairs + UNROLL) + 1
+    entries = pairs + UNROLL + 1
     early_table, late_table, info, spread, own_basis = pl.pallas_call(
         functools.partial(prepare_kernel, axes, count, tuple(layout), late_from),
         out_shape=(
@@ -582,7 +615,6 @@
     for di in others:
         note(("two x", di), on_row(two_x, di), contents["two x", di])
     note("two y", from_layer(two_y, 2), contents["two y"])
-    two_m = pack([buffers[name] for name in names], plans[2:], [two_x], "pack_two_mate")[0]
     note("two m", from_layer(two_m, 1), contents["two m"])
 
     names = ["up", "down", "two y", "geo"] + [("two x", di) for di in others]
@@ -596,7 +628,7 @@
     plans = [
         [(1, 0, picks), (2, 0, picks)],
         [(0, 0, picks)] + [(x, 0, picks) for x in xs],
-        [(x, 0, picks) for x in xs] + [(2, 0, picks)] + gather,
+        [(x, 0, picks + size) for x in xs] + [(2, 0, lengths["two y"])] + gather,
         gather,
     ]
     three_x, three_y, three_m, geos = pack([buffers[name] for name in names], plans, [own_basis], "pack_three")
@@ -667,8 +699,11 @@
         name="square_cube_coefficients",
     )(late_table, info, own_basis, spread, own, gram, *late_values, line)
 
-    below = from_offset(coef, "layer", -1)
-    above = from_offset(coef, "layer", 1)
+    mate_coef = from_layer(coef, 1)
+    third_coef = from_layer(coef, 3)
+    odd = lax.axis_index("layer") % 2 == 1
+    below = jnp.where(odd, mate_coef, third_coef)
+    above = jnp.where(odd, third_coef, mate_coef)
     merged = jnp.concatenate(
         [
             coef[:, : 4 * SPAN],
@@ -679,12 +714,16 @@
         axis=1,
     )
     stacked = jnp.concatenate([merged] + [on_row(merged, di) for di in others], axis=0)
-    received = [stacked] + [from_offset(stacked, "col", dc) for dc in column_steps[1:]]
+    last = n_col - 1
+    from_up = lax.ppermute(stacked, "col", [(i + 1, i) for i in range(last)])
+    from_down = lax.ppermute(stacked, "col", [(i, i + 1) for i in range(last)])
+    around = lax.ppermute(stacked, "col", [(0, last), (last, 0)])
+    received = [stacked, from_up, from_down, around]
 
     density = pl.pallas_call(
-        functools.partial(density_kernel, len(column_steps)),
+        functools.partial(density_kernel, len(column_steps), last),
         out_shape=jax.ShapeDtypeStruct((BX * BY, BZ), jnp.float32),
-        in_specs=[VMEM] * (len(column_steps) + 2),
+        in_specs=[VMEM] * (len(received) + 2),
         out_specs=VMEM,
         scratch_shapes=[pltpu.VMEM((BX * BY, tiles * SHELLS * LANES), jnp.bfloat16)],
         compiler_params=pltpu.CompilerParams(vmem_limit_bytes=16 << 20),

time: 73 us -> 74.6 us (1.022)
  starting transfers between devices: 21 us -> 26.6 us
  waiting for transfers between devices: 22.5 us -> 20.1 us
  Pallas kernels: 27.4 us -> 25.7 us
    ppermute x11 -> x7, waiting for transfers between devices: 17.6 us -> 7.89 us  [from_offset(): lax.ppermute(x, axis, [((i + step) % count, i) for i in range(count)])]
    ppermute x0 -> x3, starting transfers between devices: none -> 9.15 us  [the longest x1 4.55 us: local(): from_down = lax.ppermute(stacked, 'col', [(i, i + 1) for i in range(last)])]
    ppermute x11 -> x7, starting transfers between devices: 14.7 us -> 9.5 us  [from_offset(): lax.ppermute(x, axis, [((i + step) % count, i) for i in range(count)])]
    ppermute x0 -> x3, waiting for transfers between devices: none -> 4 us  [the longest x1 4 us: local(): around = lax.ppermute(stacked, 'col', [(0, last), (last, 0)])]
    ppermute x9 -> x13, waiting for transfers between devices: 4.96 us -> 8.17 us  [from_layer(): return lax.ppermute(x, 'layer', [(i ^ flip, i) for i in range(count)])]
    ppermute x9 -> x13, starting transfers between devices: 6.3 us -> 8.01 us  [from_layer(): return lax.ppermute(x, 'layer', [(i ^ flip, i) for i in range(count)])]
    pallas_call x1, Pallas kernels: 5.8 us -> 4.3 us  [local(): pl.pallas_call(functools.partial(prepare_kernel, axes, count, tuple(layou...]
  transfers between devices with their start and end apart: 20 -> 23, of which waited for: 12 -> 9; matrix products, arithmetic and copies ran while one was open for 0% -> 0% of each run, Pallas kernels for 26% -> 25%
where the time goes in v9:
time: 74.6 us; the launch traced here: 74.2 us
  starting transfers between devices  26.6 us (36%)
  Pallas kernels  25.7 us (34%)
  waiting for transfers between devices  20.1 us (27%)
  local copies, waits for them, and re-layouts  0.85 us (1%)
  between operations  0.85 us (1%)
    ppermute x7, starting transfers between devices, from_offset(): lax.ppermute(x, axis, [((i + step) % count, i) for i in range(count)])  9.5 us
    ppermute x13, waiting for transfers between devices, from_layer(): return lax.ppermute(x, 'layer', [(i ^ flip, i) for i in range(count)])  8.17 us
    ppermute x13, starting transfers between devices, from_layer(): return lax.ppermute(x, 'layer', [(i ^ flip, i) for i in range(count)])  8.01 us
    ppermute x7, waiting for transfers between devices, from_offset(): lax.ppermute(x, axis, [((i + step) % count, i) for i in range(count)])  7.89 us
    pallas_call x1, Pallas kernels, local(): pl.pallas_call(functools.partial(step_kernel, len(late_values)), out_shap...  5.56 us
    pallas_call x1, Pallas kernels, local(): pl.pallas_call(functools.partial(gram_kernel, len(early_values)), out_sha...  4.71 us
    ppermute x1, starting transfers between devices, local(): from_down = lax.ppermute(stacked, 'col', [(i, i + 1) for i in range(last)])  4.55 us
    pallas_call x1, Pallas kernels, local(): pl.pallas_call(functools.partial(prepare_kernel, axes, count, tuple(layou...  4.3 us
  transfers between devices with their start and end apart: 23, of which 9 were waited for; matrix products, arithmetic and copies ran while one was open for 0% of the time, Pallas kernels for 25%

profile of v9, /device:TPU:0, one launch (start us, length us, event | category | flops | bytes accessed | tf_op | source)
XLA Modules:
  0.0 74.2 jit_solution(17442557444048176550)
XLA Ops:
  0.6 0.0 copy-start.2
  0.7 3.0 %collective-permute-start.2 = (bf16[1536,128]{1,0:T(8,128)(2,1)}, bf16[1536,128]{1,0:T(8,128)(2,1)S(1)}, u32[]{:S(2)}, u32[]{:S(2)}) collective-permute-start(bf16[1536,128]{1,0:T(8,128)(2,1)} %bitcast.11), channel_id=1, source_target_pairs={{2,0},{3,1},{0,2},{1,3},{6,4},{7,5},{4,6},{5,7},{10,8},{11,9},{8,1... | collective-permute-start | bytes 1179656 | tf_op jit(solution)/shard_map/ppermute | solution.py:31
  3.7 1.5 %collective-permute-start.3 = (bf16[1536,128]{1,0:T(8,128)(2,1)}, bf16[1536,128]{1,0:T(8,128)(2,1)S(1)}, u32[]{:S(2)}, u32[]{:S(2)}) collective-permute-start(bf16[1536,128]{1,0:T(8,128)(2,1)} %bitcast.12), channel_id=1, source_target_pairs={{16,0},{0,16},{17,1},{1,17},{18,2},{2,18},{19,3},{3,19},{20,4},{4,... | collective-permute-start | bytes 1179656 | tf_op jit(solution)/shard_map/ppermute | solution.py:26
  5.2 0.0 collective-permute-start.6
  5.2 2.5 %pick_column_blocks.1 = (bf16[656,128]{1,0:T(8,128)(2,1)}, bf16[16,128]{1,0:T(8,128)(2,1)}) custom-call(s32[12,32]{1,0:T(8,128)} %bitcast.19, s32[1,12]{1,0:T(1,128)} %refs_1_.2, s32[32]{0:T(128)} %refs_2_.1, s32[32]{0:T(128)} %refs_3_.1, s32[32]{0:T(128)} %refs_4_.1, bf16[12,128,128]{2,1,0:T(8,128)(2,1)} %bitcast.14), custom_call_target="tpu_custom_call" | custom-call | tf_op jit(solution)/shard_map/pick_column_blocks/pallas_call | solution.py:453
  7.7 3.7 %collective-permute-start = (bf16[656,128]{1,0:T(8,128)(2,1)}, bf16[656,128]{1,0:T(8,128)(2,1)S(1)}, u32[]{:S(2)}, u32[]{:S(2)}) collective-permute-start(bf16[656,128]{1,0:T(8,128)(2,1)} %get-tuple-element.21), channel_id=1, source_target_pairs={{4,0},{8,4},{12,8},{0,12},{5,1},{9,5},{13,9},{1,13},{6,2},{10,6},{... | collective-permute-start | bytes 503816 | tf_op jit(solution)/shard_map/ppermute | solution.py:26
  11.3 0.0 collective-permute-start.1
  11.3 1.7 %collective-permute-done.2.refs_0_.refs_3_ = bf16[1536,128]{1,0:T(8,128)(2,1)S(1)} collective-permute-done((bf16[1536,128]{1,0:T(8,128)(2,1)}, bf16[1536,128]{1,0:T(8,128)(2,1)S(1)}, u32[]{:S(2)}, u32[]{:S(2)}) %collective-permute-start.2) | collective-permute-done | bytes 393248 | tf_op jit(solution)/shard_map/ppermute | solution.py:31
  13.0 1.5 %collective-permute-done.3.refs_1_.refs_4_.refs_7_ = bf16[1536,128]{1,0:T(8,128)(2,1)S(1)} collective-permute-done((bf16[1536,128]{1,0:T(8,128)(2,1)}, bf16[1536,128]{1,0:T(8,128)(2,1)S(1)}, u32[]{:S(2)}, u32[]{:S(2)}) %collective-permute-start.3) | collective-permute-done | bytes 393248 | tf_op jit(solution)/shard_map/ppermute | solution.py:26
  14.5 0.4 pack_halves.1
  14.9 1.6 %collective-permute-start.4 = (bf16[640,128]{1,0:T(8,128)(2,1)S(1)}, bf16[640,128]{1,0:T(8,128)(2,1)S(1)}, u32[]{:S(2)}, u32[]{:S(2)}) collective-permute-start(bf16[640,128]{1,0:T(8,128)(2,1)S(1)} %get-tuple-element.23), channel_id=1, source_target_pairs={{16,0},{0,16},{17,1},{1,17},{18,2},{2,18},{19,3},{3,19},{20,4},{4,... | collective-permute-start | bytes 491528 | tf_op jit(solution)/shard_map/ppermute | solution.py:26
  16.5 0.5 collective-permute-start.5
  17.0 0.0 collective-permute-done.refs_0_.refs_2_.refs_4_
  17.0 0.0 collective-permute-start.7
  17.0 3.3 %collective-permute-done.1.refs_1_.refs_3_.refs_5_ = bf16[656,128]{1,0:T(8,128)(2,1)S(1)} collective-permute-done((bf16[656,128]{1,0:T(8,128)(2,1)}, bf16[656,128]{1,0:T(8,128)(2,1)S(1)}, u32[]{:S(2)}, u32[]{:S(2)}) %collective-permute-start.1) | collective-permute-done | bytes 167968 | tf_op jit(solution)/shard_map/ppermute | solution.py:26
  20.3 0.0 collective-permute-start.8
  20.3 0.0 collective-permute-done.6.refs_7_.refs_2_
  20.3 0.0 collective-permute-done.4.refs_5_.refs_0_.refs_10_
  20.3 1.5 %collective-permute-done.5.refs_6_.refs_1_.refs_11_ = bf16[640,128]{1,0:T(8,128)(2,1)S(1)} collective-permute-done((bf16[640,128]{1,0:T(8,128)(2,1)S(1)}, bf16[640,128]{1,0:T(8,128)(2,1)S(1)}, u32[]{:S(2)}, u32[]{:S(2)}) %collective-permute-start.5) | collective-permute-done | bytes 163872 | tf_op jit(solution)/shard_map/ppermute | solution.py:31
  21.8 0.7 copy-done.1
  22.5 0.6 pack_two.1
  23.0 0.6 collective-permute-start.9
  23.6 0.4 collective-permute-start.10
  24.0 0.9 %pack_two_mate.1 = bf16[2560,128]{1,0:T(8,128)(2,1)S(1)} custom-call(bf16[640,128]{1,0:T(8,128)(2,1)S(1)} %collective-permute-done.4.refs_5_.refs_0_.refs_10_, bf16[640,128]{1,0:T(8,128)(2,1)S(1)} %collective-permute-done.5.refs_6_.refs_1_.refs_11_, bf16[656,128]{1,0:T(8,128)(2,1)S(1)} %collective-permute-done.refs_0_.refs_2_.refs_4_, ...), custom_call_target="tpu_custom_call" | custom-call | bytes 3000000 | tf_op jit(solution)/shard_map/pack_two_mate/pallas_call | solution.py:241
  24.9 0.1 collective-permute-start.11
  25.0 0.0 copy-start
  25.0 4.3 %prepare.1 = (s32[83]{0:T(128)S(1)}, s32[83]{0:T(128)S(1)}, s32[14]{0:T(128)S(1)}, bf16[128,1536]{1,0:T(8,128)(2,1)S(1)}, bf16[16,128]{1,0:T(8,128)(2,1)S(1)}) custom-call(s32[12,32]{1,0:T(8,128)S(1)} %bitcast.20, s32[32]{0:T(128)S(1)} %copy-done.4, bf16[192,128]{1,0:T(8,128)(2,1)S(1)} %bitcast.21, bf16[816,128]{1,0:T(8,128)(2,1)S(1)} %get-tuple-element.25.refs_3_), custom_call_target="tpu_custom_call" | custom-call | flops 6000000000 | bytes 8000000 | tf_op jit(solution)/shard_map/prepare/pallas_call | solution.py:591
  29.3 0.0 collective-permute-done.10.refs_2_.refs_13_
  29.3 0.0 collective-permute-done.9.refs_4_.refs_12_
  29.3 1.6 %pack_three.1 = (bf16[1280,128]{1,0:T(8,128)(2,1)S(1)}, bf16[1280,128]{1,0:T(8,128)(2,1)S(1)}, bf16[1632,128]{1,0:T(8,128)(2,1)S(1)}, bf16[96,128]{1,0:T(8,128)(2,1)S(1)}) custom-call(bf16[656,128]{1,0:T(8,128)(2,1)S(1)} %collective-permute-done.refs_0_.refs_2_.refs_4_, bf16[656,128]{1,0:T(8,128)(2,1)S(1)} %collective-permute-done.1.refs_1_.refs_3_.refs_5_, ...), custom_call_target="tpu_custom_call" | custom-call | bytes 3000000 | tf_op jit(solution)/shard_map/pack_three/pallas_call | solution.py:241
  30.9 1.7 %collective-permute-start.12 = (bf16[1280,128]{1,0:T(8,128)(2,1)S(1)}, bf16[1280,128]{1,0:T(8,128)(2,1)S(1)}, u32[]{:S(2)}, u32[]{:S(2)}) collective-permute-start(bf16[1280,128]{1,0:T(8,128)(2,1)S(1)} %get-tuple-element.32.refs_15_), channel_id=1, source_target_pairs={{16,0},{0,16},{17,1},{1,17},{18,2},{2,18},{19,3},{3,19},{20,4},{4,... | collective-permute-start | bytes 983048 | tf_op jit(solution)/shard_map/ppermute | solution.py:26
  32.6 1.5 %collective-permute-start.13 = (bf16[1280,128]{1,0:T(8,128)(2,1)S(1)}, bf16[1280,128]{1,0:T(8,128)(2,1)S(1)}, u32[]{:S(2)}, u32[]{:S(2)}) collective-permute-start(bf16[1280,128]{1,0:T(8,128)(2,1)S(1)} %get-tuple-element.33), channel_id=1, source_target_pairs={{2,0},{3,1},{0,2},{1,3},{6,4},{7,5},{4,6},{5,7},{10,8},{11,9},{8,1... | collective-permute-start | bytes 983048 | tf_op jit(solution)/shard_map/ppermute | solution.py:31
  34.1 0.0 collective-permute-done.7.refs_8_
  34.1 0.0 collective-permute-start.14
  34.2 0.0 collective-permute-done.8.refs_9_
  34.2 0.6 collective-permute-start.15
  34.8 0.0 collective-permute-done.11.refs_14_
  34.8 4.7 %gram_early.1.refs_2_.refs_3_.refs_5_ = bf16[1536,1536]{1,0:T(8,128)(2,1)S(1)} custom-call(s32[83]{0:T(128)S(1)} %get-tuple-element.30.refs_0_, bf16[1536,128]{1,0:T(8,128)(2,1)S(1)} %bitcast.15, bf16[1536,128]{1,0:T(8,128)(2,1)S(1)} %collective-permute-done.6.refs_7_.refs_2_, bf16[1536,128]{1,0:T(8,128)(2,1)S(1)} %collective-permute-done.2.refs_0_.refs_3_, ...), custom_call_target="tpu_custom_call" | custom-call | flops 1000 | bytes 1000 | tf_op jit(solution)/shard_map/gram_early/pallas_call | solution.py:642
  39.5 2.7 %collective-permute-done.15.refs_3_.refs_2_ = bf16[96,128]{1,0:T(8,128)(2,1)S(1)} collective-permute-done((bf16[96,128]{1,0:T(8,128)(2,1)S(1)}, bf16[96,128]{1,0:T(8,128)(2,1)S(1)}, u32[]{:S(2)}, u32[]{:S(2)}) %collective-permute-start.15) | collective-permute-done | bytes 24608 | tf_op jit(solution)/shard_map/ppermute | solution.py:31
  42.2 0.0 collective-permute-done.12.refs_0_.refs_6_
  42.2 0.5 collective-permute-done.13.refs_1_.refs_7_
  42.7 0.2 pack_four.1
  42.9 0.2 collective-permute-start.16
  43.1 0.0 collective-permute-done.14.refs_1_.refs_8_
  43.1 3.5 %profiles.1 = (bf16[6,6,256,128]{3,2,1,0:T(8,128)(2,1)S(1)}, bf16[6,6,128,128]{3,2,1,0:T(8,128)(2,1)S(1)}) custom-call(bf16[96,128]{1,0:T(8,128)(2,1)S(1)} %get-tuple-element.35.refs_0_, bf16[1632,128]{1,0:T(8,128)(2,1)S(1)} %collective-permute-done.14.refs_1_.refs_8_, bf16[96,128]{1,0:T(8,128)(2,1)S(1)} %collective-permute-done.15.refs_3_.refs_2_, ...), custom_call_target="tpu_custom_call" | custom-call | flops 5000000000 | bytes 4000000 | tf_op jit(solution)/shard_map/profiles/pallas_call | solution.py:664
  46.6 0.0 collective-permute-done.16.refs_9_
  46.6 5.6 %square_cube_coefficients.1 = (bf16[12,128,128]{2,1,0:T(8,128)(2,1)}, f32[8,128]{1,0:T(8,128)S(1)}) custom-call(s32[83]{0:T(128)S(1)} %get-tuple-element.26.refs_0_, s32[14]{0:T(128)S(1)} %get-tuple-element.27.refs_1_, bf16[16,128]{1,0:T(8,128)(2,1)S(1)} %get-tuple-element.28.refs_5_.refs_2_, bf16[128,1536]{1,0:T(8,128)(2,1)S(1)} %get-tuple-element.29.refs_3_, ...), custom_call_target="tpu_custom_call" | custom-call | flops 1300000000 | bytes 8000000 | tf_op jit(solution)/shard_map/square_cube_coefficients/pallas_call | solution.py:682
  52.2 0.5 collective-permute-start.17
  52.6 1.2 %collective-permute-start.18 = (f32[8,128]{1,0:T(8,128)S(1)}, f32[8,128]{1,0:T(8,128)S(1)}, u32[]{:S(2)}, u32[]{:S(2)}) collective-permute-start(f32[8,128]{1,0:T(8,128)S(1)} %get-tuple-element.38), channel_id=1, source_target_pairs={{3,0},{2,1},{1,2},{0,3},{7,4},{6,5},{5,6},{4,7},{11,8},{10,9},{9,1... | collective-permute-start | bytes 12296 | tf_op jit(solution)/shard_map/ppermute | solution.py:31
  53.9 0.0 collective-permute-done.17
  53.9 1.8 %collective-permute-done.18 = f32[8,128]{1,0:T(8,128)S(1)} collective-permute-done((f32[8,128]{1,0:T(8,128)S(1)}, f32[8,128]{1,0:T(8,128)S(1)}, u32[]{:S(2)}, u32[]{:S(2)}) %collective-permute-start.18) | collective-permute-done | bytes 4128 | tf_op jit(solution)/shard_map/ppermute | solution.py:31
  55.7 0.1 slice.11
  55.8 0.1 slice.10
  55.8 0.1 pad_maximum_fusion.1
  55.9 0.5 collective-permute-start.19
  56.4 3.1 %collective-permute-done.19 = f32[8,128]{1,0:T(8,128)S(1)} collective-permute-done((f32[8,128]{1,0:T(8,128)S(1)}, f32[8,128]{1,0:T(8,128)S(1)}, u32[]{:S(2)}, u32[]{:S(2)}) %collective-permute-start.19) | collective-permute-done | bytes 4128 | tf_op jit(solution)/shard_map/ppermute | solution.py:26
  59.5 0.1 pad_maximum_fusion.refs_0_
  59.6 1.3 %collective-permute-start.20 = (f32[16,128]{1,0:T(8,128)S(1)}, f32[16,128]{1,0:T(8,128)S(1)}, u32[]{:S(2)}, u32[]{:S(2)}) collective-permute-start(f32[16,128]{1,0:T(8,128)S(1)} %pad_maximum_fusion.refs_0_), channel_id=1, source_target_pairs={{4,0},{8,4},{12,8},{5,1},{9,5},{13,9},{6,2},{10,6},{14,10},{7,3},{... | collective-permute-start | bytes 24584 | tf_op jit(solution)/shard_map/ppermute | solution.py:718
  60.9 4.5 %collective-permute-start.21 = (f32[16,128]{1,0:T(8,128)S(1)}, f32[16,128]{1,0:T(8,128)S(1)}, u32[]{:S(2)}, u32[]{:S(2)}) collective-permute-start(f32[16,128]{1,0:T(8,128)S(1)} %pad_maximum_fusion.refs_0_), channel_id=1, source_target_pairs={{0,4},{4,8},{8,12},{1,5},{5,9},{9,13},{2,6},{6,10},{10,14},{3,7},{... | collective-permute-start | bytes 24584 | tf_op jit(solution)/shard_map/ppermute | solution.py:719
  65.4 3.3 %collective-permute-start.22 = (f32[16,128]{1,0:T(8,128)S(1)}, f32[16,128]{1,0:T(8,128)S(1)}, u32[]{:S(2)}, u32[]{:S(2)}) collective-permute-start(f32[16,128]{1,0:T(8,128)S(1)} %pad_maximum_fusion.refs_0_), channel_id=1, source_target_pairs={{0,12},{12,0},{1,13},{13,1},{2,14},{14,2},{3,15},{15,3},{16,28},{2... | collective-permute-start | bytes 24584 | tf_op jit(solution)/shard_map/ppermute | solution.py:720
  68.8 0.0 collective-permute-done.20.refs_1_
  68.8 0.0 collective-permute-done.21.refs_2_
  68.8 4.0 %collective-permute-done.22.refs_3_ = f32[16,128]{1,0:T(8,128)S(1)} collective-permute-done((f32[16,128]{1,0:T(8,128)S(1)}, f32[16,128]{1,0:T(8,128)S(1)}, u32[]{:S(2)}, u32[]{:S(2)}) %collective-permute-start.22) | collective-permute-done | bytes 8224 | tf_op jit(solution)/shard_map/ppermute | solution.py:720
  72.8 1.5 %density.1 = f32[256,128]{1,0:T(8,128)} custom-call(f32[16,128]{1,0:T(8,128)S(1)} %pad_maximum_fusion.refs_0_, f32[16,128]{1,0:T(8,128)S(1)} %collective-permute-done.20.refs_1_, f32[16,128]{1,0:T(8,128)S(1)} %collective-permute-done.21.refs_2_, f32[16,128]{1,0:T(8,128)S(1)} %collective-permute-done.22.refs_3_, ...), custom_call_target="tpu_custom_call" | custom-call | flops 310000000 | bytes 4000000 | tf_op jit(solution)/shard_map/density/pallas_call | solution.py:723
  (9 shorter events, 0.0 us)
Async XLA Ops:
  0.6 24.3 %copy-start.2 = (s32[32,12]{0,1:T(8,128)S(1)}, s32[32,12]{0,1:T(8,128)}, u32[]{:S(2)}) copy-start(s32[32,12]{0,1:T(8,128)} %param.9) | copy-start | bytes 4612
  0.6 24.3 %copy-start.4 = (s32[32]{0:T(128)S(1)}, s32[32]{0:T(128)}, u32[]{:S(2)}) copy-start(s32[32]{0:T(128)} %refs_1_.3) | copy-start | bytes 388
  0.7 24.3 %copy-start.3 = (bf16[32,6,128]{2,0,1:T(8,128)(2,1)S(1)}, bf16[32,6,128]{2,0,1:T(8,128)(2,1)}, u32[]{:S(2)}) copy-start(bf16[32,6,128]{2,0,1:T(8,128)(2,1)} %param.11) | copy-start | bytes 147460
  0.7 12.4 %collective-permute-start.2 = (bf16[1536,128]{1,0:T(8,128)(2,1)}, bf16[1536,128]{1,0:T(8,128)(2,1)S(1)}, u32[]{:S(2)}, u32[]{:S(2)}) collective-permute-start(bf16[1536,128]{1,0:T(8,128)(2,1)} %bitcast.11), channel_id=1, source_target_pairs={{2,0},{3,1},{0,2},{1,3},{6,4},{7,5},{4,6},{5,7},{10,8},{11,9},{8,1... | collective-permute-start | bytes 1179656 | tf_op jit(solution)/shard_map/ppermute | solution.py:31
  3.7 10.8 %collective-permute-start.3 = (bf16[1536,128]{1,0:T(8,128)(2,1)}, bf16[1536,128]{1,0:T(8,128)(2,1)S(1)}, u32[]{:S(2)}, u32[]{:S(2)}) collective-permute-start(bf16[1536,128]{1,0:T(8,128)(2,1)} %bitcast.12), channel_id=1, source_target_pairs={{16,0},{0,16},{17,1},{1,17},{18,2},{2,18},{19,3},{3,19},{20,4},{4,... | collective-permute-start | bytes 1179656 | tf_op jit(solution)/shard_map/ppermute | solution.py:26
  5.2 15.1 %collective-permute-start.6 = (bf16[1536,128]{1,0:T(8,128)(2,1)}, bf16[1536,128]{1,0:T(8,128)(2,1)S(1)}, u32[]{:S(2)}, u32[]{:S(2)}) collective-permute-start(bf16[1536,128]{1,0:T(8,128)(2,1)} %bitcast.13), channel_id=1, source_target_pairs={{1,0},{0,1},{3,2},{2,3},{5,4},{4,5},{7,6},{6,7},{9,8},{8,9},{11,10... | collective-permute-start | bytes 1179656 | tf_op jit(solution)/shard_map/ppermute | solution.py:31
  7.7 9.3 %collective-permute-start = (bf16[656,128]{1,0:T(8,128)(2,1)}, bf16[656,128]{1,0:T(8,128)(2,1)S(1)}, u32[]{:S(2)}, u32[]{:S(2)}) collective-permute-start(bf16[656,128]{1,0:T(8,128)(2,1)} %get-tuple-element.21), channel_id=1, source_target_pairs={{4,0},{8,4},{12,8},{0,12},{5,1},{9,5},{13,9},{1,13},{6,2},{10,6},{... | collective-permute-start | bytes 503816 | tf_op jit(solution)/shard_map/ppermute | solution.py:26
  11.3 8.9 %collective-permute-start.1 = (bf16[656,128]{1,0:T(8,128)(2,1)}, bf16[656,128]{1,0:T(8,128)(2,1)S(1)}, u32[]{:S(2)}, u32[]{:S(2)}) collective-permute-start(bf16[656,128]{1,0:T(8,128)(2,1)} %get-tuple-element.21), channel_id=1, source_target_pairs={{12,0},{0,4},{4,8},{8,12},{13,1},{1,5},{5,9},{9,13},{14,2},{2,6},{... | collective-permute-start | bytes 503816 | tf_op jit(solution)/shard_map/ppermute | solution.py:26
  14.9 5.4 %collective-permute-start.4 = (bf16[640,128]{1,0:T(8,128)(2,1)S(1)}, bf16[640,128]{1,0:T(8,128)(2,1)S(1)}, u32[]{:S(2)}, u32[]{:S(2)}) collective-permute-start(bf16[640,128]{1,0:T(8,128)(2,1)S(1)} %get-tuple-element.23), channel_id=1, source_target_pairs={{16,0},{0,16},{17,1},{1,17},{18,2},{2,18},{19,3},{3,19},{20,4},{4,... | collective-permute-start | bytes 491528 | tf_op jit(solution)/shard_map/ppermute | solution.py:26
  16.5 5.3 %collective-permute-start.5 = (bf16[640,128]{1,0:T(8,128)(2,1)S(1)}, bf16[640,128]{1,0:T(8,128)(2,1)S(1)}, u32[]{:S(2)}, u32[]{:S(2)}) collective-permute-start(bf16[640,128]{1,0:T(8,128)(2,1)S(1)} %get-tuple-element.24), channel_id=1, source_target_pairs={{2,0},{3,1},{0,2},{1,3},{6,4},{7,5},{4,6},{5,7},{10,8},{11,9},{8,1... | collective-permute-start | bytes 491528 | tf_op jit(solution)/shard_map/ppermute | solution.py:31
  17.0 17.2 %collective-permute-start.7 = (bf16[1536,128]{1,0:T(8,128)(2,1)S(1)}, bf16[1536,128]{1,0:T(8,128)(2,1)S(1)}, u32[]{:S(2)}, u32[]{:S(2)}) collective-permute-start(bf16[1536,128]{1,0:T(8,128)(2,1)S(1)} %collective-permute-done.3.refs_1_.refs_4_.refs_7_), channel_id=1, source_target_pairs={{1,0},{0,1},{3,2},{2,3},{5,4},{4,5},{7,6},{6,7},{9,8},{8,9},{11,10... | collective-permute-start | bytes 1179656 | tf_op jit(solution)/shard_map/ppermute | solution.py:31
  20.3 13.9 %collective-permute-start.8 = (bf16[1536,128]{1,0:T(8,128)(2,1)S(1)}, bf16[1536,128]{1,0:T(8,128)(2,1)S(1)}, u32[]{:S(2)}, u32[]{:S(2)}) collective-permute-start(bf16[1536,128]{1,0:T(8,128)(2,1)S(1)} %collective-permute-done.2.refs_0_.refs_3_), channel_id=1, source_target_pairs={{1,0},{0,1},{3,2},{2,3},{5,4},{4,5},{7,6},{6,7},{9,8},{8,9},{11,10... | collective-permute-start | bytes 1179656 | tf_op jit(solution)/shard_map/ppermute | solution.py:31
  21.8 0.7 copy-start.1
  23.0 6.3 %collective-permute-start.9 = (bf16[816,128]{1,0:T(8,128)(2,1)S(1)}, bf16[816,128]{1,0:T(8,128)(2,1)S(1)}, u32[]{:S(2)}, u32[]{:S(2)}) collective-permute-start(bf16[816,128]{1,0:T(8,128)(2,1)S(1)} %get-tuple-element.25.refs_3_), channel_id=1, source_target_pairs={{16,0},{0,16},{17,1},{1,17},{18,2},{2,18},{19,3},{3,19},{20,4},{4,... | collective-permute-start | bytes 626696 | tf_op jit(solution)/shard_map/ppermute | solution.py:26
  23.6 5.7 %collective-permute-start.10 = (bf16[768,128]{1,0:T(8,128)(2,1)S(1)}, bf16[768,128]{1,0:T(8,128)(2,1)S(1)}, u32[]{:S(2)}, u32[]{:S(2)}) collective-permute-start(bf16[768,128]{1,0:T(8,128)(2,1)S(1)} %get-tuple-element.31), channel_id=1, source_target_pairs={{2,0},{3,1},{0,2},{1,3},{6,4},{7,5},{4,6},{5,7},{10,8},{11,9},{8,1... | collective-permute-start | bytes 589832 | tf_op jit(solution)/shard_map/ppermute | solution.py:31
  24.9 9.9 %collective-permute-start.11 = (bf16[2560,128]{1,0:T(8,128)(2,1)S(1)}, bf16[2560,128]{1,0:T(8,128)(2,1)S(1)}, u32[]{:S(2)}, u32[]{:S(2)}) collective-permute-start(bf16[2560,128]{1,0:T(8,128)(2,1)S(1)} %pack_two_mate.1), channel_id=1, source_target_pairs={{1,0},{0,1},{3,2},{2,3},{5,4},{4,5},{7,6},{6,7},{9,8},{8,9},{11,10... | collective-permute-start | bytes 1966088 | tf_op jit(solution)/shard_map/ppermute | solution.py:31
  25.0 9.8 %copy-start = (bf16[1,12,128,128]{3,2,1,0:T(8,128)(2,1)S(1)}, bf16[1,12,128,128]{3,2,1,0:T(8,128)(2,1)}, u32[]{:S(2)}) copy-start(bf16[1,12,128,128]{3,2,1,0:T(8,128)(2,1)} %param.8) | copy-start | bytes 1179652
  30.9 11.3 %collective-permute-start.12 = (bf16[1280,128]{1,0:T(8,128)(2,1)S(1)}, bf16[1280,128]{1,0:T(8,128)(2,1)S(1)}, u32[]{:S(2)}, u32[]{:S(2)}) collective-permute-start(bf16[1280,128]{1,0:T(8,128)(2,1)S(1)} %get-tuple-element.32.refs_15_), channel_id=1, source_target_pairs={{16,0},{0,16},{17,1},{1,17},{18,2},{2,18},{19,3},{3,19},{20,4},{4,... | collective-permute-start | bytes 983048 | tf_op jit(solution)/shard_map/ppermute | solution.py:26
  32.6 10.1 %collective-permute-start.13 = (bf16[1280,128]{1,0:T(8,128)(2,1)S(1)}, bf16[1280,128]{1,0:T(8,128)(2,1)S(1)}, u32[]{:S(2)}, u32[]{:S(2)}) collective-permute-start(bf16[1280,128]{1,0:T(8,128)(2,1)S(1)} %get-tuple-element.33), channel_id=1, source_target_pairs={{2,0},{3,1},{0,2},{1,3},{6,4},{7,5},{4,6},{5,7},{10,8},{11,9},{8,1... | collective-permute-start | bytes 983048 | tf_op jit(solution)/shard_map/ppermute | solution.py:31
  34.1 9.0 %collective-permute-start.14 = (bf16[1632,128]{1,0:T(8,128)(2,1)S(1)}, bf16[1632,128]{1,0:T(8,128)(2,1)S(1)}, u32[]{:S(2)}, u32[]{:S(2)}) collective-permute-start(bf16[1632,128]{1,0:T(8,128)(2,1)S(1)} %get-tuple-element.34), channel_id=1, source_target_pairs={{1,0},{0,1},{3,2},{2,3},{5,4},{4,5},{7,6},{6,7},{9,8},{8,9},{11,10... | collective-permute-start | bytes 1253384 | tf_op jit(solution)/shard_map/ppermute | solution.py:31
  34.2 8.0 %collective-permute-start.15 = (bf16[96,128]{1,0:T(8,128)(2,1)S(1)}, bf16[96,128]{1,0:T(8,128)(2,1)S(1)}, u32[]{:S(2)}, u32[]{:S(2)}) collective-permute-start(bf16[96,128]{1,0:T(8,128)(2,1)S(1)} %get-tuple-element.35.refs_0_), channel_id=1, source_target_pairs={{3,0},{2,1},{1,2},{0,3},{7,4},{6,5},{5,6},{4,7},{11,8},{10,9},{9,1... | collective-permute-start | bytes 73736 | tf_op jit(solution)/shard_map/ppermute | solution.py:31
  42.9 3.7 %collective-permute-start.16 = (bf16[2560,128]{1,0:T(8,128)(2,1)S(1)}, bf16[2560,128]{1,0:T(8,128)(2,1)S(1)}, u32[]{:S(2)}, u32[]{:S(2)}) collective-permute-start(bf16[2560,128]{1,0:T(8,128)(2,1)S(1)} %pack_four.1), channel_id=1, source_target_pairs={{1,0},{0,1},{3,2},{2,3},{5,4},{4,5},{7,6},{6,7},{9,8},{8,9},{11,10... | collective-permute-start | bytes 1966088 | tf_op jit(solution)/shard_map/ppermute | solution.py:31
  52.2 1.7 %collective-permute-start.17 = (f32[8,128]{1,0:T(8,128)S(1)}, f32[8,128]{1,0:T(8,128)S(1)}, u32[]{:S(2)}, u32[]{:S(2)}) collective-permute-start(f32[8,128]{1,0:T(8,128)S(1)} %get-tuple-element.38), channel_id=1, source_target_pairs={{1,0},{0,1},{3,2},{2,3},{5,4},{4,5},{7,6},{6,7},{9,8},{8,9},{11,10... | collective-permute-start | bytes 12296 | tf_op jit(solution)/shard_map/ppermute | solution.py:31
  52.6 3.0 %collective-permute-start.18 = (f32[8,128]{1,0:T(8,128)S(1)}, f32[8,128]{1,0:T(8,128)S(1)}, u32[]{:S(2)}, u32[]{:S(2)}) collective-permute-start(f32[8,128]{1,0:T(8,128)S(1)} %get-tuple-element.38), channel_id=1, source_target_pairs={{3,0},{2,1},{1,2},{0,3},{7,4},{6,5},{5,6},{4,7},{11,8},{10,9},{9,1... | collective-permute-start | bytes 12296 | tf_op jit(solution)/shard_map/ppermute | solution.py:31
  55.9 3.6 %collective-permute-start.19 = (f32[8,128]{1,0:T(8,128)S(1)}, f32[8,128]{1,0:T(8,128)S(1)}, u32[]{:S(2)}, u32[]{:S(2)}) collective-permute-start(f32[8,128]{1,0:T(8,128)S(1)} %pad_maximum_fusion.1), channel_id=1, source_target_pairs={{16,0},{0,16},{17,1},{1,17},{18,2},{2,18},{19,3},{3,19},{20,4},{4,... | collective-permute-start | bytes 12296 | tf_op jit(solution)/shard_map/ppermute | solution.py:26
  59.6 9.2 %collective-permute-start.20 = (f32[16,128]{1,0:T(8,128)S(1)}, f32[16,128]{1,0:T(8,128)S(1)}, u32[]{:S(2)}, u32[]{:S(2)}) collective-permute-start(f32[16,128]{1,0:T(8,128)S(1)} %pad_maximum_fusion.refs_0_), channel_id=1, source_target_pairs={{4,0},{8,4},{12,8},{5,1},{9,5},{13,9},{6,2},{10,6},{14,10},{7,3},{... | collective-permute-start | bytes 24584 | tf_op jit(solution)/shard_map/ppermute | solution.py:718
  60.9 7.9 %collective-permute-start.21 = (f32[16,128]{1,0:T(8,128)S(1)}, f32[16,128]{1,0:T(8,128)S(1)}, u32[]{:S(2)}, u32[]{:S(2)}) collective-permute-start(f32[16,128]{1,0:T(8,128)S(1)} %pad_maximum_fusion.refs_0_), channel_id=1, source_target_pairs={{0,4},{4,8},{8,12},{1,5},{5,9},{9,13},{2,6},{6,10},{10,14},{3,7},{... | collective-permute-start | bytes 24584 | tf_op jit(solution)/shard_map/ppermute | solution.py:719
  65.4 7.3 %collective-permute-start.22 = (f32[16,128]{1,0:T(8,128)S(1)}, f32[16,128]{1,0:T(8,128)S(1)}, u32[]{:S(2)}, u32[]{:S(2)}) collective-permute-start(f32[16,128]{1,0:T(8,128)S(1)} %pad_maximum_fusion.refs_0_), channel_id=1, source_target_pairs={{0,12},{12,0},{1,13},{13,1},{2,14},{14,2},{3,15},{15,3},{16,28},{2... | collective-permute-start | bytes 24584 | tf_op jit(solution)/shard_map/ppermute | solution.py:720

commit v10 on v9

--- a/solution.py
+++ b/solution.py
@@ -26,6 +26,12 @@
     return lax.ppermute(x, axis, [((i + step) % count, i) for i in range(count)])
 
 
+def from_column(x, side):
+    count = lax.axis_size("col")
+    step = [1 if (i + side) % 2 == 0 else -1 for i in range(count)]
+    return lax.ppermute(x, "col", [((i + step[i]) % count, i) for i in range(count)])
+
+
 def from_layer(x, flip):
     count = lax.axis_size("layer")
     return lax.ppermute(x, "layer", [(i ^ flip, i) for i in range(count)])
@@ -86,7 +92,7 @@
 
 
 def pick_kernel(axes, *refs):
-    sign_ref, out_ref, geo_ref, neighbors_ref, extent_ref, x_ref, y_ref, z_ref, place_ref, loads, sems = refs[5:]
+    sign_ref, out_ref, neighbors_ref, extent_ref, x_ref, y_ref, z_ref, place_ref, loads, sems = refs[5:]
     at = Places(*axes)
     slots = sign_ref.shape[0]
     n_pick = place_ref.shape[0] - 1
@@ -118,9 +124,7 @@
         extent = extent_ref[0, w]
         values = jnp.where(sub == 0, twice_x, jnp.where(sub == 1, twice_y, jnp.where(sub == 2, twice_z, extent)))
         geo = jnp.where(lane_pair == rank, values, geo)
-    geo = geo.astype(jnp.float32).astype(geo_ref.dtype)
-    geo_ref[...] = geo
-    out_ref[n_pick * size : n_pick * size + GEO] = geo
+    out_ref[n_pick * size :] = geo.astype(jnp.float32).astype(out_ref.dtype)
     for copy in copies:
         copy.wait()
 
@@ -150,13 +154,12 @@
     for w, (atom, rank) in enumerate(own_ranks(at, neighbors_ref)):
         row, col, lay = at.split(atom)
         step_row = (row - at.row) & (at.n_row - 1)
-        step_col = (col - at.col) & (at.n_col - 1)
         self_slot = jnp.where(atom == at.me, w, self_slot)
         info_ref[w] = size_ref[atom]
         spread_ref[:, w * LANES : (w + 1) * LANES] = rows_of(hot(LANES, atom, rank * SHELLS))
         flip = lay ^ at.lay
         known[0, w] = atom
-        known[1, w] = jnp.where(step_col == 0, 0, jnp.where(step_col == 1, 1, 2))
+        known[1, w] = jnp.where(col == at.col, 0, jnp.where(col == (at.col ^ 1), 1, 2))
         known[2, w] = jnp.where(step_row == 0, 0, jnp.where(step_row == 1, 1, 2)) * at.n_lay + flip
         inverse[atom] = -1
     own_basis_ref[...] = rows_of(hot(16, at.me, 0))
@@ -375,7 +378,8 @@
 
     for copy in copies:
         copy.wait()
-    for o, (step_row, step_col) in enumerate(steps):
+    ahead = 1.0 - 2.0 * (lax.axis_index("col") & 1).astype(jnp.float32)
+    for o, (step_row, side) in enumerate(steps):
         own, first, third = (geos[k, o * GEO : (o + 1) * GEO].astype(jnp.float32) for k in range(3))
         below = jnp.where(odd, first, third)
         above = jnp.where(odd, third, first)
@@ -390,7 +394,7 @@
         )
         sub = packed.T
         d_x = nearest(grid_x - (0.5 * geo[0:1] + float(BX * step_row)), periods[0])
-        d_y = nearest(grid_y - (0.5 * geo[1:2] + float(BY * step_col)), periods[1])
+        d_y = nearest(grid_y - (0.5 * geo[1:2] + float(BY * side) * ahead), periods[1])
         inside = (jnp.abs(d_x) <= reach) & (jnp.abs(d_y) <= reach)
         squared = d_x * d_x + d_y * d_y
         d_z = nearest(grid_z - sub[:, 0:1], periods[2])
@@ -404,14 +408,9 @@
             line_ref[o, s] = jnp.where(inside_z, jnp.exp(-rate_z * squared_z), 0.0).astype(line_ref.dtype)
 
 
-def density_kernel(column_steps, last, *refs):
-    own_ref, up_ref, down_ref, around_ref, plane_ref, line_ref, out_ref, terms = refs
-    col = lax.axis_index("col")
-    coef_refs = [
-        own_ref[...],
-        jnp.where(col == last, around_ref[...], up_ref[...]),
-        jnp.where(col == 0, around_ref[...], down_ref[...]),
-    ]
+def density_kernel(column_steps, *refs):
+    coef_refs = refs[:column_steps]
+    plane_ref, line_ref, out_ref, terms = refs[column_steps:]
     for o in range(plane_ref.shape[0]):
         coef = coef_refs[o % column_steps]
         first = 8 * (o // column_steps)
@@ -450,14 +449,11 @@
     x_row = {di: on_row(flat, di) for di in others}
     y_row = from_layer(flat, 2)
     m_row = from_layer(flat, 1)
-    picked, geo = pl.pallas_call(
+    picked = pl.pallas_call(
         functools.partial(pick_kernel, axes),
-        out_shape=(
-            jax.ShapeDtypeStruct((part, size), own.dtype),
-            jax.ShapeDtypeStruct((GEO, LANES), own.dtype),
-        ),
+        out_shape=jax.ShapeDtypeStruct((part, size), own.dtype),
         in_specs=[HBM] * 6,
-        out_specs=(VMEM, VMEM),
+        out_specs=VMEM,
         scratch_shapes=[
             pltpu.SMEM((slots, atoms), jnp.int32),
             pltpu.SMEM((1, slots), jnp.int32),
@@ -471,12 +467,12 @@
         compiler_params=pltpu.CompilerParams(vmem_limit_bytes=60 << 20),
         name="pick_column_blocks",
     )(listings, pair_extent, atom_x, atom_y, atom_z, own)
-    up = from_offset(picked, "col", 1)
-    down = from_offset(picked, "col", -1)
+    up = from_column(picked, 0)
+    down = from_column(picked, 1)
 
     halves = pack(
-        [y_row] + [x_row[di] for di in others],
-        [[(0, half, most)]] + [[(di, 0, most)] for di in others],
+        [y_row] + [x_row[di] for di in others] + [picked],
+        [[(0, half, most)]] + [[(di, 0, most)] for di in others] + [[(count, picks, GEO)]],
         [],
         "pack_halves",
     )
@@ -507,7 +503,7 @@
     note("far", y_row, row_of(0, 2))
     note("up", up, side_of("up", 0, 0) + [(("up geo", 0, 0), GEO)])
     note("down", down, side_of("down", 0, 0) + [(("down geo", 0, 0), GEO)])
-    note("geo", geo, [(("geo", 0, 0), GEO)])
+    note("geo", halves[count], [(("geo", 0, 0), GEO)])
     for di in others:
         note(("x", di), x_row[di], row_of(di, 0))
         note(("end", di), ends[di], row_of(di, 2, halfway, slots - 1))
@@ -518,10 +514,9 @@
     plans = [
         [(0, 0, picks), (3, full - size, size), (2, 0, GEO), (0, picks, GEO), (1, picks, GEO)],
         [(1, 0, picks)] + [(di + 3, most, size) for di in others],
+        [(2, 0, GEO), (0, picks, GEO), (1, picks, GEO)],
     ]
-    two_x, two_y = pack(
-        [buffers[name] for name in names], plans, [buffers[name] for name in corners] + [m_row], "pack_two"
-    )
+    two_x, two_y, geos = pack([buffers[name] for name in names], plans, [m_row], "pack_two")
     to_mate = corners + ["up", "down"]
     plans = [[(i, 0, picks if name in ("up", "down") else most) for i, name in enumerate(to_mate)]]
     two_m = pack([buffers[name] for name in to_mate], plans, [], "pack_two_mate")[0]
@@ -597,7 +592,7 @@
             jax.ShapeDtypeStruct((LANES, full), jnp.bfloat16),
             jax.ShapeDtypeStruct((16, size), jnp.bfloat16),
         ),
-        in_specs=[HBM, HBM, VMEM, ANY],
+        in_specs=[HBM, HBM, VMEM, ANY] + [ANY] * len(corners),
         out_specs=(SMEM, SMEM, SMEM, VMEM, VMEM),
         scratch_shapes=[
             pltpu.SMEM((slots, atoms), jnp.int32),
@@ -610,20 +605,17 @@
         compiler_params=pltpu.CompilerParams(vmem_limit_bytes=(2 << 20) + atoms * 16384),
         cost_estimate=pl.CostEstimate(flops=6_000_000_000, bytes_accessed=8_000_000, transcendentals=0),
         name="prepare",
-    )(listings, atom_size, basis_proj.transpose(1, 0, 2).reshape(SHELLS * atoms, size), two_x)
+    )(listings, atom_size, basis_proj.transpose(1, 0, 2).reshape(SHELLS * atoms, size), two_x, *[buffers[name] for name in corners])
 
     for di in others:
         note(("two x", di), on_row(two_x, di), contents["two x", di])
     note("two y", from_layer(two_y, 2), contents["two y"])
     note("two m", from_layer(two_m, 1), contents["two m"])
 
-    names = ["up", "down", "two y", "geo"] + [("two x", di) for di in others]
+    buffers["geos"] = geos
+    names = ["up", "down", "two y", "geos"] + [("two x", di) for di in others]
     place = {name: i for i, name in enumerate(names)}
-    gather = []
-    for di in range(count):
-        for kind in ("geo", "up geo", "down geo"):
-            name, start = at[kind, di, 0]
-            gather.append((place[name], start, GEO))
+    gather = [(place["geos"], 0, 3 * GEO)] + [(place["two x", di], picks + size, 3 * GEO) for di in others]
     xs = [place["two x", di] for di in others]
     plans = [
         [(1, 0, picks), (2, 0, picks)],
@@ -714,14 +706,10 @@
         axis=1,
     )
     stacked = jnp.concatenate([merged] + [on_row(merged, di) for di in others], axis=0)
-    last = n_col - 1
-    from_up = lax.ppermute(stacked, "col", [(i + 1, i) for i in range(last)])
-    from_down = lax.ppermute(stacked, "col", [(i, i + 1) for i in range(last)])
-    around = lax.ppermute(stacked, "col", [(0, last), (last, 0)])
-    received = [stacked, from_up, from_down, around]
+    received = [stacked, from_column(stacked, 0), from_column(stacked, 1)]
 
     density = pl.pallas_call(
-        functools.partial(density_kernel, len(column_steps), last),
+        functools.partial(density_kernel, len(column_steps)),
         out_shape=jax.ShapeDtypeStruct((BX * BY, BZ), jnp.float32),
         in_specs=[VMEM] * (len(received) + 2),
         out_specs=VMEM,

time: 74.6 us -> 67.1 us (0.90)
  starting transfers between devices: 26.6 us -> 22.7 us
  waiting for transfers between devices: 20.1 us -> 16.2 us
    ppermute x7 -> x5, starting transfers between devices: 9.5 us -> 5.83 us  [from_offset(): lax.ppermute(x, axis, [((i + step) % count, i) for i in range(count)])]
    ppermute x7 -> x5, waiting for transfers between devices: 7.89 us -> 4.4 us  [from_offset(): lax.ppermute(x, axis, [((i + step) % count, i) for i in range(count)])]
    ppermute x13, waiting for transfers between devices: 8.17 us -> 6.27 us  [from_layer(): return lax.ppermute(x, 'layer', [(i ^ flip, i) for i in range(count)])]
    ppermute x3 -> x4, waiting for transfers between devices: 4 us -> 5.58 us  [from_column(): lax.ppermute(x, 'col', [((i + step[i]) % count, i) for i in range(count)])]
    ppermute x3 -> x4, starting transfers between devices: 9.15 us -> 8.25 us  [from_column(): lax.ppermute(x, 'col', [((i + step[i]) % count, i) for i in range(count)])]
  transfers between devices with their start and end apart: 23 -> 22, of which waited for: 9 -> 9; matrix products, arithmetic and copies ran while one was open for 0% -> 0% of each run, Pallas kernels for 25% -> 28%
where the time goes in v10:
time: 67.1 us; the launch traced here: 66.7 us
  Pallas kernels  25.7 us (38%)
  starting transfers between devices  22.7 us (34%)
  waiting for transfers between devices  16.2 us (24%)
  local copies, waits for them, and re-layouts  1.08 us (2%)
  between operations  0.83 us (1%)
    ppermute x13, starting transfers between devices, from_layer(): return lax.ppermute(x, 'layer', [(i ^ flip, i) for i in range(count)])  8.65 us
    ppermute x4, starting transfers between devices, from_column(): lax.ppermute(x, 'col', [((i + step[i]) % count, i) for i in range(count)])  8.25 us
    ppermute x13, waiting for transfers between devices, from_layer(): return lax.ppermute(x, 'layer', [(i ^ flip, i) for i in range(count)])  6.27 us
    ppermute x5, starting transfers between devices, from_offset(): lax.ppermute(x, axis, [((i + step) % count, i) for i in range(count)])  5.83 us
    ppermute x4, waiting for transfers between devices, from_column(): lax.ppermute(x, 'col', [((i + step[i]) % count, i) for i in range(count)])  5.58 us
    pallas_call x1, Pallas kernels, local(): pl.pallas_call(functools.partial(step_kernel, len(late_values)), out_shap...  5.56 us
    pallas_call x1, Pallas kernels, local(): pl.pallas_call(functools.partial(gram_kernel, len(early_values)), out_sha...  4.71 us
    ppermute x5, waiting for transfers between devices, from_offset(): lax.ppermute(x, axis, [((i + step) % count, i) for i in range(count)])  4.4 us
  transfers between devices with their start and end apart: 22, of which 9 were waited for; matrix products, arithmetic and copies ran while one was open for 0% of the time, Pallas kernels for 28%

profile of v10, /device:TPU:0, one launch (start us, length us, event | category | flops | bytes accessed | tf_op | source)
XLA Modules:
  0.0 66.7 jit_solution(4816397826363484809)
XLA Ops:
  0.6 0.0 copy-start.2
  0.6 0.0 copy-start.4
  0.7 0.0 copy-start.3
  0.7 3.0 %collective-permute-start.2 = (bf16[1536,128]{1,0:T(8,128)(2,1)}, bf16[1536,128]{1,0:T(8,128)(2,1)S(1)}, u32[]{:S(2)}, u32[]{:S(2)}) collective-permute-start(bf16[1536,128]{1,0:T(8,128)(2,1)} %bitcast.11), channel_id=1, source_target_pairs={{2,0},{3,1},{0,2},{1,3},{6,4},{7,5},{4,6},{5,7},{10,8},{11,9},{8,1... | collective-permute-start | bytes 1179656 | tf_op jit(solution)/shard_map/ppermute | solution.py:37
  3.7 1.5 %collective-permute-start.3 = (bf16[1536,128]{1,0:T(8,128)(2,1)}, bf16[1536,128]{1,0:T(8,128)(2,1)S(1)}, u32[]{:S(2)}, u32[]{:S(2)}) collective-permute-start(bf16[1536,128]{1,0:T(8,128)(2,1)} %bitcast.12), channel_id=1, source_target_pairs={{16,0},{0,16},{17,1},{1,17},{18,2},{2,18},{19,3},{3,19},{20,4},{4,... | collective-permute-start | bytes 1179656 | tf_op jit(solution)/shard_map/ppermute | solution.py:26
  5.2 0.0 collective-permute-start.4
  5.2 2.5 %pick_column_blocks.1.refs_2_ = bf16[656,128]{1,0:T(8,128)(2,1)} custom-call(s32[12,32]{1,0:T(8,128)} %bitcast.19, s32[1,12]{1,0:T(1,128)} %refs_1_.2, s32[32]{0:T(128)} %refs_2_.1, s32[32]{0:T(128)} %refs_3_.1, s32[32]{0:T(128)} %refs_4_.1, bf16[12,128,128]{2,1,0:T(8,128)(2,1)} %bitcast.14), custom_call_target="tpu_custom_call" | custom-call | tf_op jit(solution)/shard_map/pick_column_blocks/pallas_call | solution.py:452
  7.7 1.6 %collective-permute-start = (bf16[656,128]{1,0:T(8,128)(2,1)}, bf16[656,128]{1,0:T(8,128)(2,1)S(1)}, u32[]{:S(2)}, u32[]{:S(2)}) collective-permute-start(bf16[656,128]{1,0:T(8,128)(2,1)} %pick_column_blocks.1.refs_2_), channel_id=1, source_target_pairs={{4,0},{0,4},{12,8},{8,12},{5,1},{1,5},{13,9},{9,13},{6,2},{2,6},{1... | collective-permute-start | bytes 503816 | tf_op jit(solution)/shard_map/ppermute | solution.py:32
  9.3 2.5 %collective-permute-start.1 = (bf16[656,128]{1,0:T(8,128)(2,1)}, bf16[656,128]{1,0:T(8,128)(2,1)S(1)}, u32[]{:S(2)}, u32[]{:S(2)}) collective-permute-start(bf16[656,128]{1,0:T(8,128)(2,1)} %pick_column_blocks.1.refs_2_), channel_id=1, source_target_pairs={{12,0},{8,4},{4,8},{0,12},{13,1},{9,5},{5,9},{1,13},{14,2},{10,6},... | collective-permute-start | bytes 503816 | tf_op jit(solution)/shard_map/ppermute | solution.py:32
  11.8 1.2 %collective-permute-done.2.refs_0_.refs_3_ = bf16[1536,128]{1,0:T(8,128)(2,1)S(1)} collective-permute-done((bf16[1536,128]{1,0:T(8,128)(2,1)}, bf16[1536,128]{1,0:T(8,128)(2,1)S(1)}, u32[]{:S(2)}, u32[]{:S(2)}) %collective-permute-start.2) | collective-permute-done | bytes 393248 | tf_op jit(solution)/shard_map/ppermute | solution.py:37
  13.0 1.5 %collective-permute-done.3.refs_1_.refs_4_.refs_7_ = bf16[1536,128]{1,0:T(8,128)(2,1)S(1)} collective-permute-done((bf16[1536,128]{1,0:T(8,128)(2,1)}, bf16[1536,128]{1,0:T(8,128)(2,1)S(1)}, u32[]{:S(2)}, u32[]{:S(2)}) %collective-permute-start.3) | collective-permute-done | bytes 393248 | tf_op jit(solution)/shard_map/ppermute | solution.py:26
  14.5 0.9 %copy-done.1 = bf16[656,128]{1,0:T(8,128)(2,1)S(1)} copy-done((bf16[656,128]{1,0:T(8,128)(2,1)S(1)}, bf16[656,128]{1,0:T(8,128)(2,1)}, u32[]{:S(2)}) %copy-start.1) | copy-done | bytes 167960
  15.4 0.4 pack_halves.1
  15.8 1.6 %collective-permute-start.5 = (bf16[640,128]{1,0:T(8,128)(2,1)S(1)}, bf16[640,128]{1,0:T(8,128)(2,1)S(1)}, u32[]{:S(2)}, u32[]{:S(2)}) collective-permute-start(bf16[640,128]{1,0:T(8,128)(2,1)S(1)} %get-tuple-element.23), channel_id=1, source_target_pairs={{16,0},{0,16},{17,1},{1,17},{18,2},{2,18},{19,3},{3,19},{20,4},{4,... | collective-permute-start | bytes 491528 | tf_op jit(solution)/shard_map/ppermute | solution.py:26
  17.4 0.5 collective-permute-start.6
  17.9 0.0 collective-permute-done.refs_0_.refs_2_.refs_4_
  17.9 2.5 %collective-permute-done.1.refs_1_.refs_3_.refs_5_ = bf16[656,128]{1,0:T(8,128)(2,1)S(1)} collective-permute-done((bf16[656,128]{1,0:T(8,128)(2,1)}, bf16[656,128]{1,0:T(8,128)(2,1)S(1)}, u32[]{:S(2)}, u32[]{:S(2)}) %collective-permute-start.1) | collective-permute-done | bytes 167968 | tf_op jit(solution)/shard_map/ppermute | solution.py:32
  20.4 0.0 collective-permute-done.4.refs_5_.refs_2_
  20.4 0.6 pack_two.1
  21.0 0.6 collective-permute-start.9
  21.6 0.5 collective-permute-start.10
  22.1 0.0 collective-permute-start.7
  22.1 0.0 collective-permute-done.5.refs_4_.refs_0_.refs_10_
  22.1 0.5 collective-permute-start.8
  22.6 0.1 collective-permute-done.6.refs_5_.refs_1_.refs_11_
  22.7 0.9 %pack_two_mate.1 = bf16[2560,128]{1,0:T(8,128)(2,1)S(1)} custom-call(bf16[640,128]{1,0:T(8,128)(2,1)S(1)} %collective-permute-done.5.refs_4_.refs_0_.refs_10_, bf16[640,128]{1,0:T(8,128)(2,1)S(1)} %collective-permute-done.6.refs_5_.refs_1_.refs_11_, bf16[656,128]{1,0:T(8,128)(2,1)S(1)} %collective-permute-done.refs_0_.refs_2_.refs_4_, ...), custom_call_target="tpu_custom_call" | custom-call | bytes 3000000 | tf_op jit(solution)/shard_map/pack_two_mate/pallas_call | solution.py:244
  23.6 0.1 collective-permute-start.11
  23.7 0.0 copy-start
  23.7 4.3 %prepare.1 = (s32[83]{0:T(128)S(1)}, s32[83]{0:T(128)S(1)}, s32[14]{0:T(128)S(1)}, bf16[128,1536]{1,0:T(8,128)(2,1)S(1)}, bf16[16,128]{1,0:T(8,128)(2,1)S(1)}) custom-call(s32[12,32]{1,0:T(8,128)S(1)} %bitcast.20, s32[32]{0:T(128)S(1)} %copy-done.4, bf16[192,128]{1,0:T(8,128)(2,1)S(1)} %bitcast.21, bf16[816,128]{1,0:T(8,128)(2,1)S(1)} %get-tuple-element.22.refs_3_, ...), custom_call_target="tpu_custom_call" | custom-call | flops 6000000000 | bytes 8000000 | tf_op jit(solution)/shard_map/prepare/pallas_call | solution.py:586
  28.0 0.0 collective-permute-done.10.refs_2_.refs_13_
  28.0 0.0 collective-permute-done.9.refs_4_.refs_12_
  28.0 1.5 %pack_three.1 = (bf16[1280,128]{1,0:T(8,128)(2,1)S(1)}, bf16[1280,128]{1,0:T(8,128)(2,1)S(1)}, bf16[1632,128]{1,0:T(8,128)(2,1)S(1)}, bf16[96,128]{1,0:T(8,128)(2,1)S(1)}) custom-call(bf16[656,128]{1,0:T(8,128)(2,1)S(1)} %collective-permute-done.refs_0_.refs_2_.refs_4_, bf16[656,128]{1,0:T(8,128)(2,1)S(1)} %collective-permute-done.1.refs_1_.refs_3_.refs_5_, ...), custom_call_target="tpu_custom_call" | custom-call | bytes 3000000 | tf_op jit(solution)/shard_map/pack_three/pallas_call | solution.py:244
  29.6 1.5 %collective-permute-start.12 = (bf16[1280,128]{1,0:T(8,128)(2,1)S(1)}, bf16[1280,128]{1,0:T(8,128)(2,1)S(1)}, u32[]{:S(2)}, u32[]{:S(2)}) collective-permute-start(bf16[1280,128]{1,0:T(8,128)(2,1)S(1)} %get-tuple-element.32.refs_15_), channel_id=1, source_target_pairs={{16,0},{0,16},{17,1},{1,17},{18,2},{2,18},{19,3},{3,19},{20,4},{4,... | collective-permute-start | bytes 983048 | tf_op jit(solution)/shard_map/ppermute | solution.py:26
  31.1 1.5 %collective-permute-start.13 = (bf16[1280,128]{1,0:T(8,128)(2,1)S(1)}, bf16[1280,128]{1,0:T(8,128)(2,1)S(1)}, u32[]{:S(2)}, u32[]{:S(2)}) collective-permute-start(bf16[1280,128]{1,0:T(8,128)(2,1)S(1)} %get-tuple-element.33), channel_id=1, source_target_pairs={{2,0},{3,1},{0,2},{1,3},{6,4},{7,5},{4,6},{5,7},{10,8},{11,9},{8,1... | collective-permute-start | bytes 983048 | tf_op jit(solution)/shard_map/ppermute | solution.py:37
  32.6 0.0 collective-permute-done.7.refs_8_
  32.6 0.0 collective-permute-start.14
  32.6 0.0 collective-permute-done.8.refs_9_
  32.6 0.6 collective-permute-start.15
  33.2 0.0 collective-permute-done.11.refs_14_
  33.2 4.7 %gram_early.1.refs_2_.refs_3_.refs_5_ = bf16[1536,1536]{1,0:T(8,128)(2,1)S(1)} custom-call(s32[83]{0:T(128)S(1)} %get-tuple-element.29.refs_0_, bf16[1536,128]{1,0:T(8,128)(2,1)S(1)} %bitcast.15, bf16[1536,128]{1,0:T(8,128)(2,1)S(1)} %collective-permute-done.4.refs_5_.refs_2_, bf16[1536,128]{1,0:T(8,128)(2,1)S(1)} %collective-permute-done.2.refs_0_.refs_3_, ...), custom_call_target="tpu_custom_call" | custom-call | flops 1000 | bytes 1000 | tf_op jit(solution)/shard_map/gram_early/pallas_call | solution.py:634
  37.9 2.7 %collective-permute-done.15.refs_3_.refs_2_ = bf16[96,128]{1,0:T(8,128)(2,1)S(1)} collective-permute-done((bf16[96,128]{1,0:T(8,128)(2,1)S(1)}, bf16[96,128]{1,0:T(8,128)(2,1)S(1)}, u32[]{:S(2)}, u32[]{:S(2)}) %collective-permute-start.15) | collective-permute-done | bytes 24608 | tf_op jit(solution)/shard_map/ppermute | solution.py:37
  40.7 0.0 collective-permute-done.12.refs_0_.refs_6_
  40.7 0.5 collective-permute-done.13.refs_1_.refs_7_
  41.1 0.2 pack_four.1
  41.4 0.2 collective-permute-start.16
  41.6 0.0 collective-permute-done.14.refs_1_.refs_8_
  41.6 3.5 %profiles.1 = (bf16[6,6,256,128]{3,2,1,0:T(8,128)(2,1)S(1)}, bf16[6,6,128,128]{3,2,1,0:T(8,128)(2,1)S(1)}) custom-call(bf16[96,128]{1,0:T(8,128)(2,1)S(1)} %get-tuple-element.35.refs_0_, bf16[1632,128]{1,0:T(8,128)(2,1)S(1)} %collective-permute-done.14.refs_1_.refs_8_, bf16[96,128]{1,0:T(8,128)(2,1)S(1)} %collective-permute-done.15.refs_3_.refs_2_, ...), custom_call_target="tpu_custom_call" | custom-call | flops 5000000000 | bytes 4000000 | tf_op jit(solution)/shard_map/profiles/pallas_call | solution.py:656
  45.1 0.0 collective-permute-done.16.refs_9_
  45.1 5.6 %square_cube_coefficients.1 = (bf16[12,128,128]{2,1,0:T(8,128)(2,1)}, f32[8,128]{1,0:T(8,128)S(1)}) custom-call(s32[83]{0:T(128)S(1)} %get-tuple-element.25.refs_0_, s32[14]{0:T(128)S(1)} %get-tuple-element.26.refs_1_, bf16[16,128]{1,0:T(8,128)(2,1)S(1)} %get-tuple-element.27.refs_5_.refs_2_, bf16[128,1536]{1,0:T(8,128)(2,1)S(1)} %get-tuple-element.28.refs_3_, ...), custom_call_target="tpu_custom_call" | custom-call | flops 1300000000 | bytes 8000000 | tf_op jit(solution)/shard_map/square_cube_coefficients/pallas_call | solution.py:674
  50.7 0.5 collective-permute-start.17
  51.1 1.2 %collective-permute-start.18 = (f32[8,128]{1,0:T(8,128)S(1)}, f32[8,128]{1,0:T(8,128)S(1)}, u32[]{:S(2)}, u32[]{:S(2)}) collective-permute-start(f32[8,128]{1,0:T(8,128)S(1)} %get-tuple-element.38), channel_id=1, source_target_pairs={{3,0},{2,1},{1,2},{0,3},{7,4},{6,5},{5,6},{4,7},{11,8},{10,9},{9,1... | collective-permute-start | bytes 12296 | tf_op jit(solution)/shard_map/ppermute | solution.py:37
  52.4 0.0 collective-permute-done.17
  52.4 1.8 %collective-permute-done.18 = f32[8,128]{1,0:T(8,128)S(1)} collective-permute-done((f32[8,128]{1,0:T(8,128)S(1)}, f32[8,128]{1,0:T(8,128)S(1)}, u32[]{:S(2)}, u32[]{:S(2)}) %collective-permute-start.18) | collective-permute-done | bytes 4128 | tf_op jit(solution)/shard_map/ppermute | solution.py:37
  54.2 0.1 slice.11
  54.2 0.1 slice.10
  54.3 0.1 pad_maximum_fusion.1
  54.4 0.7 %collective-permute-start.19 = (f32[8,128]{1,0:T(8,128)S(1)}, f32[8,128]{1,0:T(8,128)S(1)}, u32[]{:S(2)}, u32[]{:S(2)}) collective-permute-start(f32[8,128]{1,0:T(8,128)S(1)} %pad_maximum_fusion.1), channel_id=1, source_target_pairs={{16,0},{0,16},{17,1},{1,17},{18,2},{2,18},{19,3},{3,19},{20,4},{4,... | collective-permute-start | bytes 12296 | tf_op jit(solution)/shard_map/ppermute | solution.py:26
  55.1 2.9 %collective-permute-done.19 = f32[8,128]{1,0:T(8,128)S(1)} collective-permute-done((f32[8,128]{1,0:T(8,128)S(1)}, f32[8,128]{1,0:T(8,128)S(1)}, u32[]{:S(2)}, u32[]{:S(2)}) %collective-permute-start.19) | collective-permute-done | bytes 4128 | tf_op jit(solution)/shard_map/ppermute | solution.py:26
  58.0 0.1 pad_maximum_fusion.refs_0_
  58.1 1.8 %collective-permute-start.20 = (f32[16,128]{1,0:T(8,128)S(1)}, f32[16,128]{1,0:T(8,128)S(1)}, u32[]{:S(2)}, u32[]{:S(2)}) collective-permute-start(f32[16,128]{1,0:T(8,128)S(1)} %pad_maximum_fusion.refs_0_), channel_id=1, source_target_pairs={{4,0},{0,4},{12,8},{8,12},{5,1},{1,5},{13,9},{9,13},{6,2},{2,6},{1... | collective-permute-start | bytes 24584 | tf_op jit(solution)/shard_map/ppermute | solution.py:32
  59.8 2.4 %collective-permute-start.21 = (f32[16,128]{1,0:T(8,128)S(1)}, f32[16,128]{1,0:T(8,128)S(1)}, u32[]{:S(2)}, u32[]{:S(2)}) collective-permute-start(f32[16,128]{1,0:T(8,128)S(1)} %pad_maximum_fusion.refs_0_), channel_id=1, source_target_pairs={{12,0},{8,4},{4,8},{0,12},{13,1},{9,5},{5,9},{1,13},{14,2},{10,6},... | collective-permute-start | bytes 24584 | tf_op jit(solution)/shard_map/ppermute | solution.py:32
  62.2 0.0 collective-permute-done.20.refs_1_
  62.2 3.1 %collective-permute-done.21.refs_2_ = f32[16,128]{1,0:T(8,128)S(1)} collective-permute-done((f32[16,128]{1,0:T(8,128)S(1)}, f32[16,128]{1,0:T(8,128)S(1)}, u32[]{:S(2)}, u32[]{:S(2)}) %collective-permute-start.21) | collective-permute-done | bytes 8224 | tf_op jit(solution)/shard_map/ppermute | solution.py:32
  65.3 1.5 %density.1 = f32[256,128]{1,0:T(8,128)} custom-call(f32[16,128]{1,0:T(8,128)S(1)} %pad_maximum_fusion.refs_0_, f32[16,128]{1,0:T(8,128)S(1)} %collective-permute-done.20.refs_1_, f32[16,128]{1,0:T(8,128)S(1)} %collective-permute-done.21.refs_2_, bf16[6,6,256,128]{3,2,1,0:T(8,128)(2,1)S(1)} %get-tuple-element.39.refs_3_, bf16[4608,128]{1,0:T(8,128)(2,1)S(1)} %bitcast.10), custom_call_target="tpu_custom_call" | custom-call | flops 310000000 | bytes 4000000 | tf_op jit(solution)/shard_map/density/pallas_call | solution.py:711
  (7 shorter events, 0.0 us)
Async XLA Ops:
  0.6 23.0 %copy-start.2 = (s32[32,12]{0,1:T(8,128)S(1)}, s32[32,12]{0,1:T(8,128)}, u32[]{:S(2)}) copy-start(s32[32,12]{0,1:T(8,128)} %param.9) | copy-start | bytes 4612
  0.6 23.0 %copy-start.4 = (s32[32]{0:T(128)S(1)}, s32[32]{0:T(128)}, u32[]{:S(2)}) copy-start(s32[32]{0:T(128)} %refs_1_.3) | copy-start | bytes 388
  0.7 23.0 %copy-start.3 = (bf16[32,6,128]{2,0,1:T(8,128)(2,1)S(1)}, bf16[32,6,128]{2,0,1:T(8,128)(2,1)}, u32[]{:S(2)}) copy-start(bf16[32,6,128]{2,0,1:T(8,128)(2,1)} %param.11) | copy-start | bytes 147460
  0.7 12.4 %collective-permute-start.2 = (bf16[1536,128]{1,0:T(8,128)(2,1)}, bf16[1536,128]{1,0:T(8,128)(2,1)S(1)}, u32[]{:S(2)}, u32[]{:S(2)}) collective-permute-start(bf16[1536,128]{1,0:T(8,128)(2,1)} %bitcast.11), channel_id=1, source_target_pairs={{2,0},{3,1},{0,2},{1,3},{6,4},{7,5},{4,6},{5,7},{10,8},{11,9},{8,1... | collective-permute-start | bytes 1179656 | tf_op jit(solution)/shard_map/ppermute | solution.py:37
  3.7 10.8 %collective-permute-start.3 = (bf16[1536,128]{1,0:T(8,128)(2,1)}, bf16[1536,128]{1,0:T(8,128)(2,1)S(1)}, u32[]{:S(2)}, u32[]{:S(2)}) collective-permute-start(bf16[1536,128]{1,0:T(8,128)(2,1)} %bitcast.12), channel_id=1, source_target_pairs={{16,0},{0,16},{17,1},{1,17},{18,2},{2,18},{19,3},{3,19},{20,4},{4,... | collective-permute-start | bytes 1179656 | tf_op jit(solution)/shard_map/ppermute | solution.py:26
  5.2 15.2 %collective-permute-start.4 = (bf16[1536,128]{1,0:T(8,128)(2,1)}, bf16[1536,128]{1,0:T(8,128)(2,1)S(1)}, u32[]{:S(2)}, u32[]{:S(2)}) collective-permute-start(bf16[1536,128]{1,0:T(8,128)(2,1)} %bitcast.13), channel_id=1, source_target_pairs={{1,0},{0,1},{3,2},{2,3},{5,4},{4,5},{7,6},{6,7},{9,8},{8,9},{11,10... | collective-permute-start | bytes 1179656 | tf_op jit(solution)/shard_map/ppermute | solution.py:37
  7.7 10.2 %collective-permute-start = (bf16[656,128]{1,0:T(8,128)(2,1)}, bf16[656,128]{1,0:T(8,128)(2,1)S(1)}, u32[]{:S(2)}, u32[]{:S(2)}) collective-permute-start(bf16[656,128]{1,0:T(8,128)(2,1)} %pick_column_blocks.1.refs_2_), channel_id=1, source_target_pairs={{4,0},{0,4},{12,8},{8,12},{5,1},{1,5},{13,9},{9,13},{6,2},{2,6},{1... | collective-permute-start | bytes 503816 | tf_op jit(solution)/shard_map/ppermute | solution.py:32
  9.3 11.1 %collective-permute-start.1 = (bf16[656,128]{1,0:T(8,128)(2,1)}, bf16[656,128]{1,0:T(8,128)(2,1)S(1)}, u32[]{:S(2)}, u32[]{:S(2)}) collective-permute-start(bf16[656,128]{1,0:T(8,128)(2,1)} %pick_column_blocks.1.refs_2_), channel_id=1, source_target_pairs={{12,0},{8,4},{4,8},{0,12},{13,1},{9,5},{5,9},{1,13},{14,2},{10,6},... | collective-permute-start | bytes 503816 | tf_op jit(solution)/shard_map/ppermute | solution.py:32
  14.5 0.9 %copy-start.1 = (bf16[656,128]{1,0:T(8,128)(2,1)S(1)}, bf16[656,128]{1,0:T(8,128)(2,1)}, u32[]{:S(2)}) copy-start(bf16[656,128]{1,0:T(8,128)(2,1)} %pick_column_blocks.1.refs_2_) | copy-start | bytes 503812
  15.8 6.3 %collective-permute-start.5 = (bf16[640,128]{1,0:T(8,128)(2,1)S(1)}, bf16[640,128]{1,0:T(8,128)(2,1)S(1)}, u32[]{:S(2)}, u32[]{:S(2)}) collective-permute-start(bf16[640,128]{1,0:T(8,128)(2,1)S(1)} %get-tuple-element.23), channel_id=1, source_target_pairs={{16,0},{0,16},{17,1},{1,17},{18,2},{2,18},{19,3},{3,19},{20,4},{4,... | collective-permute-start | bytes 491528 | tf_op jit(solution)/shard_map/ppermute | solution.py:26
  17.4 5.3 %collective-permute-start.6 = (bf16[640,128]{1,0:T(8,128)(2,1)S(1)}, bf16[640,128]{1,0:T(8,128)(2,1)S(1)}, u32[]{:S(2)}, u32[]{:S(2)}) collective-permute-start(bf16[640,128]{1,0:T(8,128)(2,1)S(1)} %get-tuple-element.24), channel_id=1, source_target_pairs={{2,0},{3,1},{0,2},{1,3},{6,4},{7,5},{4,6},{5,7},{10,8},{11,9},{8,1... | collective-permute-start | bytes 491528 | tf_op jit(solution)/shard_map/ppermute | solution.py:37
  21.0 7.0 %collective-permute-start.9 = (bf16[816,128]{1,0:T(8,128)(2,1)S(1)}, bf16[816,128]{1,0:T(8,128)(2,1)S(1)}, u32[]{:S(2)}, u32[]{:S(2)}) collective-permute-start(bf16[816,128]{1,0:T(8,128)(2,1)S(1)} %get-tuple-element.22.refs_3_), channel_id=1, source_target_pairs={{16,0},{0,16},{17,1},{1,17},{18,2},{2,18},{19,3},{3,19},{20,4},{4,... | collective-permute-start | bytes 626696 | tf_op jit(solution)/shard_map/ppermute | solution.py:26
  21.6 6.4 %collective-permute-start.10 = (bf16[768,128]{1,0:T(8,128)(2,1)S(1)}, bf16[768,128]{1,0:T(8,128)(2,1)S(1)}, u32[]{:S(2)}, u32[]{:S(2)}) collective-permute-start(bf16[768,128]{1,0:T(8,128)(2,1)S(1)} %get-tuple-element.30), channel_id=1, source_target_pairs={{2,0},{3,1},{0,2},{1,3},{6,4},{7,5},{4,6},{5,7},{10,8},{11,9},{8,1... | collective-permute-start | bytes 589832 | tf_op jit(solution)/shard_map/ppermute | solution.py:37
  22.1 10.5 %collective-permute-start.7 = (bf16[1536,128]{1,0:T(8,128)(2,1)S(1)}, bf16[1536,128]{1,0:T(8,128)(2,1)S(1)}, u32[]{:S(2)}, u32[]{:S(2)}) collective-permute-start(bf16[1536,128]{1,0:T(8,128)(2,1)S(1)} %collective-permute-done.3.refs_1_.refs_4_.refs_7_), channel_id=1, source_target_pairs={{1,0},{0,1},{3,2},{2,3},{5,4},{4,5},{7,6},{6,7},{9,8},{8,9},{11,10... | collective-permute-start | bytes 1179656 | tf_op jit(solution)/shard_map/ppermute | solution.py:37
  22.1 10.5 %collective-permute-start.8 = (bf16[1536,128]{1,0:T(8,128)(2,1)S(1)}, bf16[1536,128]{1,0:T(8,128)(2,1)S(1)}, u32[]{:S(2)}, u32[]{:S(2)}) collective-permute-start(bf16[1536,128]{1,0:T(8,128)(2,1)S(1)} %collective-permute-done.2.refs_0_.refs_3_), channel_id=1, source_target_pairs={{1,0},{0,1},{3,2},{2,3},{5,4},{4,5},{7,6},{6,7},{9,8},{8,9},{11,10... | collective-permute-start | bytes 1179656 | tf_op jit(solution)/shard_map/ppermute | solution.py:37
  23.6 9.7 %collective-permute-start.11 = (bf16[2560,128]{1,0:T(8,128)(2,1)S(1)}, bf16[2560,128]{1,0:T(8,128)(2,1)S(1)}, u32[]{:S(2)}, u32[]{:S(2)}) collective-permute-start(bf16[2560,128]{1,0:T(8,128)(2,1)S(1)} %pack_two_mate.1), channel_id=1, source_target_pairs={{1,0},{0,1},{3,2},{2,3},{5,4},{4,5},{7,6},{6,7},{9,8},{8,9},{11,10... | collective-permute-start | bytes 1966088 | tf_op jit(solution)/shard_map/ppermute | solution.py:37
  23.7 9.6 %copy-start = (bf16[1,12,128,128]{3,2,1,0:T(8,128)(2,1)S(1)}, bf16[1,12,128,128]{3,2,1,0:T(8,128)(2,1)}, u32[]{:S(2)}) copy-start(bf16[1,12,128,128]{3,2,1,0:T(8,128)(2,1)} %param.8) | copy-start | bytes 1179652
  29.6 11.1 %collective-permute-start.12 = (bf16[1280,128]{1,0:T(8,128)(2,1)S(1)}, bf16[1280,128]{1,0:T(8,128)(2,1)S(1)}, u32[]{:S(2)}, u32[]{:S(2)}) collective-permute-start(bf16[1280,128]{1,0:T(8,128)(2,1)S(1)} %get-tuple-element.32.refs_15_), channel_id=1, source_target_pairs={{16,0},{0,16},{17,1},{1,17},{18,2},{2,18},{19,3},{3,19},{20,4},{4,... | collective-permute-start | bytes 983048 | tf_op jit(solution)/shard_map/ppermute | solution.py:26
  31.1 10.1 %collective-permute-start.13 = (bf16[1280,128]{1,0:T(8,128)(2,1)S(1)}, bf16[1280,128]{1,0:T(8,128)(2,1)S(1)}, u32[]{:S(2)}, u32[]{:S(2)}) collective-permute-start(bf16[1280,128]{1,0:T(8,128)(2,1)S(1)} %get-tuple-element.33), channel_id=1, source_target_pairs={{2,0},{3,1},{0,2},{1,3},{6,4},{7,5},{4,6},{5,7},{10,8},{11,9},{8,1... | collective-permute-start | bytes 983048 | tf_op jit(solution)/shard_map/ppermute | solution.py:37
  32.6 9.0 %collective-permute-start.14 = (bf16[1632,128]{1,0:T(8,128)(2,1)S(1)}, bf16[1632,128]{1,0:T(8,128)(2,1)S(1)}, u32[]{:S(2)}, u32[]{:S(2)}) collective-permute-start(bf16[1632,128]{1,0:T(8,128)(2,1)S(1)} %get-tuple-element.34), channel_id=1, source_target_pairs={{1,0},{0,1},{3,2},{2,3},{5,4},{4,5},{7,6},{6,7},{9,8},{8,9},{11,10... | collective-permute-start | bytes 1253384 | tf_op jit(solution)/shard_map/ppermute | solution.py:37
  32.6 8.0 %collective-permute-start.15 = (bf16[96,128]{1,0:T(8,128)(2,1)S(1)}, bf16[96,128]{1,0:T(8,128)(2,1)S(1)}, u32[]{:S(2)}, u32[]{:S(2)}) collective-permute-start(bf16[96,128]{1,0:T(8,128)(2,1)S(1)} %get-tuple-element.35.refs_0_), channel_id=1, source_target_pairs={{3,0},{2,1},{1,2},{0,3},{7,4},{6,5},{5,6},{4,7},{11,8},{10,9},{9,1... | collective-permute-start | bytes 73736 | tf_op jit(solution)/shard_map/ppermute | solution.py:37
  41.4 3.7 %collective-permute-start.16 = (bf16[2560,128]{1,0:T(8,128)(2,1)S(1)}, bf16[2560,128]{1,0:T(8,128)(2,1)S(1)}, u32[]{:S(2)}, u32[]{:S(2)}) collective-permute-start(bf16[2560,128]{1,0:T(8,128)(2,1)S(1)} %pack_four.1), channel_id=1, source_target_pairs={{1,0},{0,1},{3,2},{2,3},{5,4},{4,5},{7,6},{6,7},{9,8},{8,9},{11,10... | collective-permute-start | bytes 1966088 | tf_op jit(solution)/shard_map/ppermute | solution.py:37
  50.7 1.7 %collective-permute-start.17 = (f32[8,128]{1,0:T(8,128)S(1)}, f32[8,128]{1,0:T(8,128)S(1)}, u32[]{:S(2)}, u32[]{:S(2)}) collective-permute-start(f32[8,128]{1,0:T(8,128)S(1)} %get-tuple-element.38), channel_id=1, source_target_pairs={{1,0},{0,1},{3,2},{2,3},{5,4},{4,5},{7,6},{6,7},{9,8},{8,9},{11,10... | collective-permute-start | bytes 12296 | tf_op jit(solution)/shard_map/ppermute | solution.py:37
  51.1 3.0 %collective-permute-start.18 = (f32[8,128]{1,0:T(8,128)S(1)}, f32[8,128]{1,0:T(8,128)S(1)}, u32[]{:S(2)}, u32[]{:S(2)}) collective-permute-start(f32[8,128]{1,0:T(8,128)S(1)} %get-tuple-element.38), channel_id=1, source_target_pairs={{3,0},{2,1},{1,2},{0,3},{7,4},{6,5},{5,6},{4,7},{11,8},{10,9},{9,1... | collective-permute-start | bytes 12296 | tf_op jit(solution)/shard_map/ppermute | solution.py:37
  54.4 3.6 %collective-permute-start.19 = (f32[8,128]{1,0:T(8,128)S(1)}, f32[8,128]{1,0:T(8,128)S(1)}, u32[]{:S(2)}, u32[]{:S(2)}) collective-permute-start(f32[8,128]{1,0:T(8,128)S(1)} %pad_maximum_fusion.1), channel_id=1, source_target_pairs={{16,0},{0,16},{17,1},{1,17},{18,2},{2,18},{19,3},{3,19},{20,4},{4,... | collective-permute-start | bytes 12296 | tf_op jit(solution)/shard_map/ppermute | solution.py:26
  58.1 4.1 %collective-permute-start.20 = (f32[16,128]{1,0:T(8,128)S(1)}, f32[16,128]{1,0:T(8,128)S(1)}, u32[]{:S(2)}, u32[]{:S(2)}) collective-permute-start(f32[16,128]{1,0:T(8,128)S(1)} %pad_maximum_fusion.refs_0_), channel_id=1, source_target_pairs={{4,0},{0,4},{12,8},{8,12},{5,1},{1,5},{13,9},{9,13},{6,2},{2,6},{1... | collective-permute-start | bytes 24584 | tf_op jit(solution)/shard_map/ppermute | solution.py:32
  59.8 5.4 %collective-permute-start.21 = (f32[16,128]{1,0:T(8,128)S(1)}, f32[16,128]{1,0:T(8,128)S(1)}, u32[]{:S(2)}, u32[]{:S(2)}) collective-permute-start(f32[16,128]{1,0:T(8,128)S(1)} %pad_maximum_fusion.refs_0_), channel_id=1, source_target_pairs={{12,0},{8,4},{4,8},{0,12},{13,1},{9,5},{5,9},{1,13},{14,2},{10,6},... | collective-permute-start | bytes 24584 | tf_op jit(solution)/shard_map/ppermute | solution.py:32

commit v11 on v10

--- a/solution.py
+++ b/solution.py
@@ -219,17 +219,9 @@
             ref[total + i + 1] = ref[jnp.maximum(total, 1)]
 
 
-def pack_kernel(moves, inputs, outputs, *refs):
-    sems = refs[-1]
-    copies = []
-    for k, (source, start, rows, target, place) in enumerate(moves):
-        copy = pltpu.make_async_copy(
-            refs[source].at[pl.ds(start, rows)], refs[inputs + target].at[pl.ds(place, rows)], sems.at[k]
-        )
-        copy.start()
-        copies.append(copy)
-    for copy in copies:
-        copy.wait()
+def pack_kernel(moves, inputs, *refs):
+    for source, start, rows, target, place in moves:
+        refs[inputs + target][place : place + rows] = refs[source][start : start + rows]
 
 
 def pack(values, plans, extra, name):
@@ -242,27 +234,24 @@
         shapes.append(jax.ShapeDtypeStruct((place, LANES), values[0].dtype))
     inputs = len(values) + len(extra)
     return pl.pallas_call(
-        functools.partial(pack_kernel, tuple(moves), inputs, len(plans)),
+        functools.partial(pack_kernel, tuple(moves), inputs),
         out_shape=tuple(shapes),
-        in_specs=[ANY] * inputs,
-        out_specs=tuple([ANY] * len(plans)),
-        scratch_shapes=[pltpu.SemaphoreType.DMA((len(moves),))],
-        compiler_params=pltpu.CompilerParams(vmem_limit_bytes=1 << 20),
+        in_specs=[VMEM] * len(values) + [ANY] * len(extra),
+        out_specs=tuple([VMEM] * len(plans)),
+        compiler_params=pltpu.CompilerParams(
+            vmem_limit_bytes=(1 << 20) + 256 * sum(x.shape[0] for x in list(values) + shapes)
+        ),
         cost_estimate=pl.CostEstimate(flops=0, bytes_accessed=3_000_000, transcendentals=0),
         name=name,
     )(*values, *extra)
 
 
-def fill(piece_refs, pool, sems):
-    copies = []
+def fill(piece_refs, pool):
     place = 0
-    for i, piece in enumerate(piece_refs):
+    for piece in piece_refs:
         rows = piece.shape[0]
-        copy = pltpu.make_async_copy(piece, pool.at[pl.ds(place, rows)], sems.at[i])
-        copy.start()
-        copies.append(copy)
+        pool[place : place + rows] = piece[...]
         place += rows
-    return copies
 
 
 def place_pairs(table_ref, pool, gram, size):
@@ -282,22 +271,20 @@
 def gram_kernel(pieces, *refs):
     table_ref = refs[0]
     piece_refs = refs[1 : 1 + pieces]
-    gram, pool, sems = refs[-3:]
+    gram, pool = refs[-2:]
     size = LANES
-    copies = fill(piece_refs, pool, sems)
+    fill(piece_refs, pool)
     for v in range(gram.shape[0] // size):
         gram[v * size : (v + 1) * size] = jnp.zeros((size, gram.shape[1]), gram.dtype)
-    for copy in copies:
-        copy.wait()
     place_pairs(table_ref, pool, gram, size)
 
 
 def step_kernel(pieces, *refs):
     table_ref, info_ref, basis_ref, spread_ref, sign_ref, early_ref = refs[:6]
     piece_refs = refs[6 : 6 + pieces]
-    next_ref, coef_ref, pool, gram, own, square, sems = refs[-7:]
+    next_ref, coef_ref, pool, gram, own, square = refs[-6:]
     slots, size = sign_ref.shape[0], sign_ref.shape[1]
-    copies = fill(piece_refs, pool, sems)
+    fill(piece_refs, pool)
     for v in range(slots):
         gram[v * size : (v + 1) * size] = early_ref[v * size : (v + 1) * size]
     rows = lax.broadcasted_iota(jnp.int32, (size, size), 0)
@@ -308,8 +295,6 @@
         kept = (rows < own_size) & (lanes < info_ref[w])
         block = jnp.where(kept, sign_ref[w].astype(jnp.float32), 0.0)
         own[:, w * size : (w + 1) * size] = block.astype(own.dtype)
-    for copy in copies:
-        copy.wait()
     place_pairs(table_ref, pool, gram, size)
     wide = 2 * size
     wide_lanes = lax.broadcasted_iota(jnp.int32, (size, wide), 1)
@@ -412,7 +397,7 @@
     coef_refs = refs[:column_steps]
     plane_ref, line_ref, out_ref, terms = refs[column_steps:]
     for o in range(plane_ref.shape[0]):
-        coef = coef_refs[o % column_steps]
+        coef = coef_refs[-o % column_steps]
         first = 8 * (o // column_steps)
         for s in range(SHELLS):
             scaled = plane_ref[o, s].astype(jnp.float32) * coef[first + s : first + s + 1, :]
@@ -467,8 +452,8 @@
         compiler_params=pltpu.CompilerParams(vmem_limit_bytes=60 << 20),
         name="pick_column_blocks",
     )(listings, pair_extent, atom_x, atom_y, atom_z, own)
+    down = from_column(picked, 1)
     up = from_column(picked, 0)
-    down = from_column(picked, 1)
 
     halves = pack(
         [y_row] + [x_row[di] for di in others] + [picked],
@@ -510,11 +495,11 @@
         note(("top", di), tops[di], row_of(di, 2, 0, halfway - 1))
 
     corners = [("end", di) for di in others] + [("top", di) for di in others]
-    names = ["up", "down", "geo", "far"] + [("x", di) for di in others]
+    names = ["down", "up", "geo", "far"] + [("x", di) for di in others]
     plans = [
-        [(0, 0, picks), (3, full - size, size), (2, 0, GEO), (0, picks, GEO), (1, picks, GEO)],
-        [(1, 0, picks)] + [(di + 3, most, size) for di in others],
-        [(2, 0, GEO), (0, picks, GEO), (1, picks, GEO)],
+        [(1, 0, picks), (3, full - size, size), (2, 0, GEO), (1, picks, GEO), (0, picks, GEO)],
+        [(0, 0, picks)] + [(di + 3, most, size) for di in others],
+        [(2, 0, GEO), (1, picks, GEO), (0, picks, GEO)],
     ]
     two_x, two_y, geos = pack([buffers[name] for name in names], plans, [m_row], "pack_two")
     to_mate = corners + ["up", "down"]
@@ -634,13 +619,10 @@
     gram = pl.pallas_call(
         functools.partial(gram_kernel, len(early_values)),
         out_shape=jax.ShapeDtypeStruct((full, full), jnp.bfloat16),
-        in_specs=[SMEM] + [ANY] * (len(early_values) + 1),
+        in_specs=[SMEM] + [VMEM] * len(early_values) + [ANY],
         out_specs=VMEM,
-        scratch_shapes=[
-            pltpu.VMEM((late_from, LANES), jnp.bfloat16),
-            pltpu.SemaphoreType.DMA((len(early_values),)),
-        ],
-        compiler_params=pltpu.CompilerParams(vmem_limit_bytes=(6 << 20) + late_from * LANES * 2),
+        scratch_shapes=[pltpu.VMEM((late_from, LANES), jnp.bfloat16)],
+        compiler_params=pltpu.CompilerParams(vmem_limit_bytes=(6 << 20) + 2 * late_from * LANES * 2),
         cost_estimate=pl.CostEstimate(flops=1000, bytes_accessed=1000, transcendentals=0),
         name="gram_early",
     )(early_table, *early_values, three_x)
@@ -677,16 +659,15 @@
             jax.ShapeDtypeStruct((slots, size, size), jnp.bfloat16),
             jax.ShapeDtypeStruct((8, LANES), jnp.float32),
         ),
-        in_specs=[SMEM, SMEM, VMEM, VMEM, VMEM, VMEM] + [ANY] * (len(late_values) + 1),
+        in_specs=[SMEM, SMEM, VMEM, VMEM, VMEM, VMEM] + [VMEM] * len(late_values) + [ANY],
         out_specs=(VMEM, VMEM),
         scratch_shapes=[
             pltpu.VMEM((total - late_from, LANES), jnp.bfloat16),
             pltpu.VMEM((full, full), jnp.bfloat16),
             pltpu.VMEM((size, full), jnp.bfloat16),
             pltpu.VMEM((size, full), jnp.bfloat16),
-            pltpu.SemaphoreType.DMA((len(late_values),)),
         ],
-        compiler_params=pltpu.CompilerParams(vmem_limit_bytes=(15 << 20) + (total - late_from) * LANES * 2),
+        compiler_params=pltpu.CompilerParams(vmem_limit_bytes=(15 << 20) + 2 * (total - late_from) * LANES * 2),
         cost_estimate=pl.CostEstimate(flops=1_300_000_000, bytes_accessed=8_000_000, transcendentals=0),
         name="square_cube_coefficients",
     )(late_table, info, own_basis, spread, own, gram, *late_values, line)
@@ -706,7 +687,8 @@
         axis=1,
     )
     stacked = jnp.concatenate([merged] + [on_row(merged, di) for di in others], axis=0)
-    received = [stacked, from_column(stacked, 0), from_column(stacked, 1)]
+    far_side = from_column(stacked, 1)
+    received = [stacked, far_side, from_column(stacked, 0)]
 
     density = pl.pallas_call(
         functools.partial(density_kernel, len(column_steps)),

time: 67.1 us -> 64 us (0.954)
  Pallas kernels: 25.7 us -> 19.1 us
  waiting for transfers between devices: 16.2 us -> 19.7 us
    pallas_call x5, Pallas kernels: 3.65 us -> 0.24 us  [pack(): pl.pallas_call(functools.partial(pack_kernel, tuple(moves), inputs), out_...]
    ppermute x13, waiting for transfers between devices: 6.27 us -> 9.27 us  [from_layer(): return lax.ppermute(x, 'layer', [(i ^ flip, i) for i in range(count)])]
    pallas_call x1, Pallas kernels: 4.71 us -> 2.12 us  [local(): pl.pallas_call(functools.partial(gram_kernel, len(early_values)), out_sha...]
    ppermute x4, waiting for transfers between devices: 5.58 us -> 6.37 us  [from_column(): lax.ppermute(x, 'col', [((i + step[i]) % count, i) for i in range(count)])]
  transfers between devices with their start and end apart: 22 -> 22, of which waited for: 9 -> 11; matrix products, arithmetic and copies ran while one was open for 0% -> 0% of each run, Pallas kernels for 28% -> 20%
where the time goes in v11:
time: 64 us; the launch traced here: 63.8 us
  starting transfers between devices  23 us (36%)
  waiting for transfers between devices  19.7 us (31%)
  Pallas kernels  19.1 us (30%)
  local copies, waits for them, and re-layouts  1.08 us (2%)
  between operations  0.78 us (1%)
    ppermute x13, waiting for transfers between devices, from_layer(): return lax.ppermute(x, 'layer', [(i ^ flip, i) for i in range(count)])  9.27 us
    ppermute x13, starting transfers between devices, from_layer(): return lax.ppermute(x, 'layer', [(i ^ flip, i) for i in range(count)])  8.6 us
    ppermute x4, starting transfers between devices, from_column(): lax.ppermute(x, 'col', [((i + step[i]) % count, i) for i in range(count)])  8.14 us
    ppermute x4, waiting for transfers between devices, from_column(): lax.ppermute(x, 'col', [((i + step[i]) % count, i) for i in range(count)])  6.37 us
    ppermute x5, starting transfers between devices, from_offset(): lax.ppermute(x, axis, [((i + step) % count, i) for i in range(count)])  6.26 us
    pallas_call x1, Pallas kernels, local(): pl.pallas_call(functools.partial(step_kernel, len(late_values)), out_shap...  5 us
    pallas_call x1, Pallas kernels, local(): pl.pallas_call(functools.partial(prepare_kernel, axes, count, tuple(layou...  4.3 us
    ppermute x5, waiting for transfers between devices, from_offset(): lax.ppermute(x, axis, [((i + step) % count, i) for i in range(count)])  4.02 us
  transfers between devices with their start and end apart: 22, of which 11 were waited for; matrix products, arithmetic and copies ran while one was open for 0% of the time, Pallas kernels for 20%

profile of v11, /device:TPU:0, one launch (start us, length us, event | category | flops | bytes accessed | tf_op | source)
XLA Modules:
  0.0 63.8 jit_solution(5979539061924698654)
XLA Ops:
  0.6 0.0 copy-start.2
  0.6 0.0 copy-start.4
  0.7 0.0 copy-start.3
  0.7 3.0 %collective-permute-start.2 = (bf16[1536,128]{1,0:T(8,128)(2,1)}, bf16[1536,128]{1,0:T(8,128)(2,1)S(1)}, u32[]{:S(2)}, u32[]{:S(2)}) collective-permute-start(bf16[1536,128]{1,0:T(8,128)(2,1)} %bitcast.11), channel_id=1, source_target_pairs={{2,0},{3,1},{0,2},{1,3},{6,4},{7,5},{4,6},{5,7},{10,8},{11,9},{8,1... | collective-permute-start | bytes 1179656 | tf_op jit(solution)/shard_map/ppermute | solution.py:37
  3.7 1.5 %collective-permute-start.3 = (bf16[1536,128]{1,0:T(8,128)(2,1)}, bf16[1536,128]{1,0:T(8,128)(2,1)S(1)}, u32[]{:S(2)}, u32[]{:S(2)}) collective-permute-start(bf16[1536,128]{1,0:T(8,128)(2,1)} %bitcast.12), channel_id=1, source_target_pairs={{16,0},{0,16},{17,1},{1,17},{18,2},{2,18},{19,3},{3,19},{20,4},{4,... | collective-permute-start | bytes 1179656 | tf_op jit(solution)/shard_map/ppermute | solution.py:26
  5.2 0.0 collective-permute-start.4
  5.2 2.5 %pick_column_blocks.1.refs_2_ = bf16[656,128]{1,0:T(8,128)(2,1)} custom-call(s32[12,32]{1,0:T(8,128)} %bitcast.19, s32[1,12]{1,0:T(1,128)} %refs_1_.2, s32[32]{0:T(128)} %refs_2_.1, s32[32]{0:T(128)} %refs_3_.1, s32[32]{0:T(128)} %refs_4_.1, bf16[12,128,128]{2,1,0:T(8,128)(2,1)} %bitcast.14), custom_call_target="tpu_custom_call" | custom-call | tf_op jit(solution)/shard_map/pick_column_blocks/pallas_call | solution.py:437
  7.7 3.7 %collective-permute-start = (bf16[656,128]{1,0:T(8,128)(2,1)}, bf16[656,128]{1,0:T(8,128)(2,1)S(1)}, u32[]{:S(2)}, u32[]{:S(2)}) collective-permute-start(bf16[656,128]{1,0:T(8,128)(2,1)} %pick_column_blocks.1.refs_2_), channel_id=1, source_target_pairs={{12,0},{8,4},{4,8},{0,12},{13,1},{9,5},{5,9},{1,13},{14,2},{10,6},... | collective-permute-start | bytes 503816 | tf_op jit(solution)/shard_map/ppermute | solution.py:32
  11.3 0.0 collective-permute-start.1
  11.3 1.7 %collective-permute-done.2.refs_0_.refs_3_ = bf16[1536,128]{1,0:T(8,128)(2,1)S(1)} collective-permute-done((bf16[1536,128]{1,0:T(8,128)(2,1)}, bf16[1536,128]{1,0:T(8,128)(2,1)S(1)}, u32[]{:S(2)}, u32[]{:S(2)}) %collective-permute-start.2) | collective-permute-done | bytes 393248 | tf_op jit(solution)/shard_map/ppermute | solution.py:37
  13.0 1.5 %collective-permute-done.3.refs_1_.refs_4_.refs_7_ = bf16[1536,128]{1,0:T(8,128)(2,1)S(1)} collective-permute-done((bf16[1536,128]{1,0:T(8,128)(2,1)}, bf16[1536,128]{1,0:T(8,128)(2,1)S(1)}, u32[]{:S(2)}, u32[]{:S(2)}) %collective-permute-start.3) | collective-permute-done | bytes 393248 | tf_op jit(solution)/shard_map/ppermute | solution.py:26
  14.5 0.9 %copy-done.1 = bf16[656,128]{1,0:T(8,128)(2,1)S(1)} copy-done((bf16[656,128]{1,0:T(8,128)(2,1)S(1)}, bf16[656,128]{1,0:T(8,128)(2,1)}, u32[]{:S(2)}) %copy-start.1) | copy-done | bytes 167960
  15.4 1.6 %collective-permute-start.5 = (bf16[640,128]{1,0:T(8,128)(2,1)S(1)}, bf16[640,128]{1,0:T(8,128)(2,1)S(1)}, u32[]{:S(2)}, u32[]{:S(2)}) collective-permute-start(bf16[640,128]{1,0:T(8,128)(2,1)S(1)} %get-tuple-element.23), channel_id=1, source_target_pairs={{16,0},{0,16},{17,1},{1,17},{18,2},{2,18},{19,3},{3,19},{20,4},{4,... | collective-permute-start | bytes 491528 | tf_op jit(solution)/shard_map/ppermute | solution.py:26
  17.0 0.5 collective-permute-start.6
  17.5 0.0 collective-permute-done.refs_0_.refs_3_.refs_1_.refs_5_
  17.5 2.7 %collective-permute-done.1.refs_1_.refs_2_.refs_0_.refs_4_ = bf16[656,128]{1,0:T(8,128)(2,1)S(1)} collective-permute-done((bf16[656,128]{1,0:T(8,128)(2,1)}, bf16[656,128]{1,0:T(8,128)(2,1)S(1)}, u32[]{:S(2)}, u32[]{:S(2)}) %collective-permute-start.1) | collective-permute-done | bytes 167968 | tf_op jit(solution)/shard_map/ppermute | solution.py:32
  20.2 0.0 collective-permute-done.4.refs_5_.refs_2_
  20.3 0.6 collective-permute-start.9
  20.9 0.5 collective-permute-start.10
  21.4 0.0 collective-permute-start.7
  21.4 0.0 collective-permute-done.5.refs_4_.refs_0_.refs_10_
  21.4 0.5 collective-permute-start.8
  21.9 0.4 collective-permute-done.6.refs_5_.refs_1_.refs_11_
  22.3 0.1 collective-permute-start.11
  22.4 0.0 copy-done.2
  22.4 0.0 copy-done.4
  22.4 0.0 copy-done.3
  22.5 0.0 copy-start
  22.5 4.3 %prepare.1 = (s32[83]{0:T(128)S(1)}, s32[83]{0:T(128)S(1)}, s32[14]{0:T(128)S(1)}, bf16[128,1536]{1,0:T(8,128)(2,1)S(1)}, bf16[16,128]{1,0:T(8,128)(2,1)S(1)}) custom-call(s32[12,32]{1,0:T(8,128)S(1)} %bitcast.20, s32[32]{0:T(128)S(1)} %copy-done.4, bf16[192,128]{1,0:T(8,128)(2,1)S(1)} %bitcast.21, bf16[816,128]{1,0:T(8,128)(2,1)S(1)} %get-tuple-element.22.refs_3_, ...), custom_call_target="tpu_custom_call" | custom-call | flops 6000000000 | bytes 8000000 | tf_op jit(solution)/shard_map/prepare/pallas_call | solution.py:571
  26.8 0.6 %collective-permute-done.10.refs_2_.refs_13_ = bf16[768,128]{1,0:T(8,128)(2,1)S(1)} collective-permute-done((bf16[768,128]{1,0:T(8,128)(2,1)S(1)}, bf16[768,128]{1,0:T(8,128)(2,1)S(1)}, u32[]{:S(2)}, u32[]{:S(2)}) %collective-permute-start.10) | collective-permute-done | bytes 196640 | tf_op jit(solution)/shard_map/ppermute | solution.py:37
  27.4 0.0 collective-permute-done.9.refs_4_.refs_12_
  27.4 0.1 pack_three.1
  27.5 1.6 %collective-permute-start.12 = (bf16[1280,128]{1,0:T(8,128)(2,1)S(1)}, bf16[1280,128]{1,0:T(8,128)(2,1)S(1)}, u32[]{:S(2)}, u32[]{:S(2)}) collective-permute-start(bf16[1280,128]{1,0:T(8,128)(2,1)S(1)} %get-tuple-element.32.refs_15_), channel_id=1, source_target_pairs={{16,0},{0,16},{17,1},{1,17},{18,2},{2,18},{19,3},{3,19},{20,4},{4,... | collective-permute-start | bytes 983048 | tf_op jit(solution)/shard_map/ppermute | solution.py:26
  29.1 0.5 collective-permute-start.13
  29.6 0.0 collective-permute-done.7.refs_8_
  29.6 0.0 collective-permute-start.14
  29.6 0.0 collective-permute-done.8.refs_9_
  29.6 1.6 %collective-permute-start.15 = (bf16[96,128]{1,0:T(8,128)(2,1)S(1)}, bf16[96,128]{1,0:T(8,128)(2,1)S(1)}, u32[]{:S(2)}, u32[]{:S(2)}) collective-permute-start(bf16[96,128]{1,0:T(8,128)(2,1)S(1)} %get-tuple-element.35.refs_0_), channel_id=1, source_target_pairs={{3,0},{2,1},{1,2},{0,3},{7,4},{6,5},{5,6},{4,7},{11,8},{10,9},{9,1... | collective-permute-start | bytes 73736 | tf_op jit(solution)/shard_map/ppermute | solution.py:37
  31.2 0.0 collective-permute-done.11.refs_14_
  31.2 0.0 copy-done
  31.2 2.1 %gram_early.1.refs_2_.refs_3_.refs_5_ = bf16[1536,1536]{1,0:T(8,128)(2,1)S(1)} custom-call(s32[83]{0:T(128)S(1)} %get-tuple-element.29.refs_0_, bf16[1536,128]{1,0:T(8,128)(2,1)S(1)} %bitcast.15, bf16[1536,128]{1,0:T(8,128)(2,1)S(1)} %collective-permute-done.4.refs_5_.refs_2_, bf16[1536,128]{1,0:T(8,128)(2,1)S(1)} %collective-permute-done.2.refs_0_.refs_3_, ...), custom_call_target="tpu_custom_call" | custom-call | flops 1000 | bytes 1000 | tf_op jit(solution)/shard_map/gram_early/pallas_call | solution.py:619
  33.4 4.0 %collective-permute-done.15.refs_3_.refs_2_ = bf16[96,128]{1,0:T(8,128)(2,1)S(1)} collective-permute-done((bf16[96,128]{1,0:T(8,128)(2,1)S(1)}, bf16[96,128]{1,0:T(8,128)(2,1)S(1)}, u32[]{:S(2)}, u32[]{:S(2)}) %collective-permute-start.15) | collective-permute-done | bytes 24608 | tf_op jit(solution)/shard_map/ppermute | solution.py:37
  37.4 0.0 collective-permute-done.12.refs_0_.refs_6_
  37.4 0.7 %collective-permute-done.13.refs_1_.refs_7_ = bf16[1280,128]{1,0:T(8,128)(2,1)S(1)} collective-permute-done((bf16[1280,128]{1,0:T(8,128)(2,1)S(1)}, bf16[1280,128]{1,0:T(8,128)(2,1)S(1)}, u32[]{:S(2)}, u32[]{:S(2)}) %collective-permute-start.13) | collective-permute-done | bytes 327712 | tf_op jit(solution)/shard_map/ppermute | solution.py:37
  38.2 0.2 collective-permute-start.16
  38.4 0.0 collective-permute-done.14.refs_1_.refs_8_
  38.4 3.5 %profiles.1 = (bf16[6,6,256,128]{3,2,1,0:T(8,128)(2,1)S(1)}, bf16[6,6,128,128]{3,2,1,0:T(8,128)(2,1)S(1)}) custom-call(bf16[96,128]{1,0:T(8,128)(2,1)S(1)} %get-tuple-element.35.refs_0_, bf16[1632,128]{1,0:T(8,128)(2,1)S(1)} %collective-permute-done.14.refs_1_.refs_8_, bf16[96,128]{1,0:T(8,128)(2,1)S(1)} %collective-permute-done.15.refs_3_.refs_2_, ...), custom_call_target="tpu_custom_call" | custom-call | flops 5000000000 | bytes 4000000 | tf_op jit(solution)/shard_map/profiles/pallas_call | solution.py:638
  41.9 0.0 collective-permute-done.16.refs_9_
  41.9 5.0 %square_cube_coefficients.1 = (bf16[12,128,128]{2,1,0:T(8,128)(2,1)}, f32[8,128]{1,0:T(8,128)S(1)}) custom-call(s32[83]{0:T(128)S(1)} %get-tuple-element.25.refs_0_, s32[14]{0:T(128)S(1)} %get-tuple-element.26.refs_1_, bf16[16,128]{1,0:T(8,128)(2,1)S(1)} %get-tuple-element.27.refs_5_.refs_2_, bf16[128,1536]{1,0:T(8,128)(2,1)S(1)} %get-tuple-element.28.refs_3_, ...), custom_call_target="tpu_custom_call" | custom-call | flops 1300000000 | bytes 8000000 | tf_op jit(solution)/shard_map/square_cube_coefficients/pallas_call | solution.py:656
  46.9 0.4 collective-permute-start.17
  47.3 1.2 %collective-permute-start.18 = (f32[8,128]{1,0:T(8,128)S(1)}, f32[8,128]{1,0:T(8,128)S(1)}, u32[]{:S(2)}, u32[]{:S(2)}) collective-permute-start(f32[8,128]{1,0:T(8,128)S(1)} %get-tuple-element.38), channel_id=1, source_target_pairs={{3,0},{2,1},{1,2},{0,3},{7,4},{6,5},{5,6},{4,7},{11,8},{10,9},{9,1... | collective-permute-start | bytes 12296 | tf_op jit(solution)/shard_map/ppermute | solution.py:37
  48.5 0.0 collective-permute-done.17
  48.5 1.8 %collective-permute-done.18 = f32[8,128]{1,0:T(8,128)S(1)} collective-permute-done((f32[8,128]{1,0:T(8,128)S(1)}, f32[8,128]{1,0:T(8,128)S(1)}, u32[]{:S(2)}, u32[]{:S(2)}) %collective-permute-start.18) | collective-permute-done | bytes 4128 | tf_op jit(solution)/shard_map/ppermute | solution.py:37
  50.3 0.1 slice.11
  50.4 0.1 slice.10
  50.5 0.1 pad_maximum_fusion.1
  50.5 1.1 %collective-permute-start.19 = (f32[8,128]{1,0:T(8,128)S(1)}, f32[8,128]{1,0:T(8,128)S(1)}, u32[]{:S(2)}, u32[]{:S(2)}) collective-permute-start(f32[8,128]{1,0:T(8,128)S(1)} %pad_maximum_fusion.1), channel_id=1, source_target_pairs={{16,0},{0,16},{17,1},{1,17},{18,2},{2,18},{19,3},{3,19},{20,4},{4,... | collective-permute-start | bytes 12296 | tf_op jit(solution)/shard_map/ppermute | solution.py:26
  51.6 2.5 %collective-permute-done.19 = f32[8,128]{1,0:T(8,128)S(1)} collective-permute-done((f32[8,128]{1,0:T(8,128)S(1)}, f32[8,128]{1,0:T(8,128)S(1)}, u32[]{:S(2)}, u32[]{:S(2)}) %collective-permute-start.19) | collective-permute-done | bytes 4128 | tf_op jit(solution)/shard_map/ppermute | solution.py:26
  54.1 0.1 pad_maximum_fusion.refs_0_
  54.2 4.5 %collective-permute-start.20 = (f32[16,128]{1,0:T(8,128)S(1)}, f32[16,128]{1,0:T(8,128)S(1)}, u32[]{:S(2)}, u32[]{:S(2)}) collective-permute-start(f32[16,128]{1,0:T(8,128)S(1)} %pad_maximum_fusion.refs_0_), channel_id=1, source_target_pairs={{12,0},{8,4},{4,8},{0,12},{13,1},{9,5},{5,9},{1,13},{14,2},{10,6},... | collective-permute-start | bytes 24584 | tf_op jit(solution)/shard_map/ppermute | solution.py:32
  58.7 0.0 collective-permute-start.21
  58.7 1.6 %collective-permute-done.20.refs_1_ = f32[16,128]{1,0:T(8,128)S(1)} collective-permute-done((f32[16,128]{1,0:T(8,128)S(1)}, f32[16,128]{1,0:T(8,128)S(1)}, u32[]{:S(2)}, u32[]{:S(2)}) %collective-permute-start.20) | collective-permute-done | bytes 8224 | tf_op jit(solution)/shard_map/ppermute | solution.py:32
  60.3 2.0 %collective-permute-done.21.refs_2_ = f32[16,128]{1,0:T(8,128)S(1)} collective-permute-done((f32[16,128]{1,0:T(8,128)S(1)}, f32[16,128]{1,0:T(8,128)S(1)}, u32[]{:S(2)}, u32[]{:S(2)}) %collective-permute-start.21) | collective-permute-done | bytes 8224 | tf_op jit(solution)/shard_map/ppermute | solution.py:32
  62.3 1.5 %density.1 = f32[256,128]{1,0:T(8,128)} custom-call(f32[16,128]{1,0:T(8,128)S(1)} %pad_maximum_fusion.refs_0_, f32[16,128]{1,0:T(8,128)S(1)} %collective-permute-done.20.refs_1_, f32[16,128]{1,0:T(8,128)S(1)} %collective-permute-done.21.refs_2_, bf16[6,6,256,128]{3,2,1,0:T(8,128)(2,1)S(1)} %get-tuple-element.39.refs_3_, bf16[4608,128]{1,0:T(8,128)(2,1)S(1)} %bitcast.10), custom_call_target="tpu_custom_call" | custom-call | flops 310000000 | bytes 4000000 | tf_op jit(solution)/shard_map/density/pallas_call | solution.py:693
  (7 shorter events, 0.1 us)
Async XLA Ops:
  0.6 21.8 %copy-start.2 = (s32[32,12]{0,1:T(8,128)S(1)}, s32[32,12]{0,1:T(8,128)}, u32[]{:S(2)}) copy-start(s32[32,12]{0,1:T(8,128)} %param.9) | copy-start | bytes 4612
  0.6 21.8 %copy-start.4 = (s32[32]{0:T(128)S(1)}, s32[32]{0:T(128)}, u32[]{:S(2)}) copy-start(s32[32]{0:T(128)} %refs_1_.3) | copy-start | bytes 388
  0.7 21.8 %copy-start.3 = (bf16[32,6,128]{2,0,1:T(8,128)(2,1)S(1)}, bf16[32,6,128]{2,0,1:T(8,128)(2,1)}, u32[]{:S(2)}) copy-start(bf16[32,6,128]{2,0,1:T(8,128)(2,1)} %param.11) | copy-start | bytes 147460
  0.7 12.4 %collective-permute-start.2 = (bf16[1536,128]{1,0:T(8,128)(2,1)}, bf16[1536,128]{1,0:T(8,128)(2,1)S(1)}, u32[]{:S(2)}, u32[]{:S(2)}) collective-permute-start(bf16[1536,128]{1,0:T(8,128)(2,1)} %bitcast.11), channel_id=1, source_target_pairs={{2,0},{3,1},{0,2},{1,3},{6,4},{7,5},{4,6},{5,7},{10,8},{11,9},{8,1... | collective-permute-start | bytes 1179656 | tf_op jit(solution)/shard_map/ppermute | solution.py:37
  3.7 10.8 %collective-permute-start.3 = (bf16[1536,128]{1,0:T(8,128)(2,1)}, bf16[1536,128]{1,0:T(8,128)(2,1)S(1)}, u32[]{:S(2)}, u32[]{:S(2)}) collective-permute-start(bf16[1536,128]{1,0:T(8,128)(2,1)} %bitcast.12), channel_id=1, source_target_pairs={{16,0},{0,16},{17,1},{1,17},{18,2},{2,18},{19,3},{3,19},{20,4},{4,... | collective-permute-start | bytes 1179656 | tf_op jit(solution)/shard_map/ppermute | solution.py:26
  5.2 15.0 %collective-permute-start.4 = (bf16[1536,128]{1,0:T(8,128)(2,1)}, bf16[1536,128]{1,0:T(8,128)(2,1)S(1)}, u32[]{:S(2)}, u32[]{:S(2)}) collective-permute-start(bf16[1536,128]{1,0:T(8,128)(2,1)} %bitcast.13), channel_id=1, source_target_pairs={{1,0},{0,1},{3,2},{2,3},{5,4},{4,5},{7,6},{6,7},{9,8},{8,9},{11,10... | collective-permute-start | bytes 1179656 | tf_op jit(solution)/shard_map/ppermute | solution.py:37
  7.7 9.8 %collective-permute-start = (bf16[656,128]{1,0:T(8,128)(2,1)}, bf16[656,128]{1,0:T(8,128)(2,1)S(1)}, u32[]{:S(2)}, u32[]{:S(2)}) collective-permute-start(bf16[656,128]{1,0:T(8,128)(2,1)} %pick_column_blocks.1.refs_2_), channel_id=1, source_target_pairs={{12,0},{8,4},{4,8},{0,12},{13,1},{9,5},{5,9},{1,13},{14,2},{10,6},... | collective-permute-start | bytes 503816 | tf_op jit(solution)/shard_map/ppermute | solution.py:32
  11.3 8.9 %collective-permute-start.1 = (bf16[656,128]{1,0:T(8,128)(2,1)}, bf16[656,128]{1,0:T(8,128)(2,1)S(1)}, u32[]{:S(2)}, u32[]{:S(2)}) collective-permute-start(bf16[656,128]{1,0:T(8,128)(2,1)} %pick_column_blocks.1.refs_2_), channel_id=1, source_target_pairs={{4,0},{0,4},{12,8},{8,12},{5,1},{1,5},{13,9},{9,13},{6,2},{2,6},{1... | collective-permute-start | bytes 503816 | tf_op jit(solution)/shard_map/ppermute | solution.py:32
  14.5 0.9 %copy-start.1 = (bf16[656,128]{1,0:T(8,128)(2,1)S(1)}, bf16[656,128]{1,0:T(8,128)(2,1)}, u32[]{:S(2)}) copy-start(bf16[656,128]{1,0:T(8,128)(2,1)} %pick_column_blocks.1.refs_2_) | copy-start | bytes 503812
  15.4 6.0 %collective-permute-start.5 = (bf16[640,128]{1,0:T(8,128)(2,1)S(1)}, bf16[640,128]{1,0:T(8,128)(2,1)S(1)}, u32[]{:S(2)}, u32[]{:S(2)}) collective-permute-start(bf16[640,128]{1,0:T(8,128)(2,1)S(1)} %get-tuple-element.23), channel_id=1, source_target_pairs={{16,0},{0,16},{17,1},{1,17},{18,2},{2,18},{19,3},{3,19},{20,4},{4,... | collective-permute-start | bytes 491528 | tf_op jit(solution)/shard_map/ppermute | solution.py:26
  17.0 5.3 %collective-permute-start.6 = (bf16[640,128]{1,0:T(8,128)(2,1)S(1)}, bf16[640,128]{1,0:T(8,128)(2,1)S(1)}, u32[]{:S(2)}, u32[]{:S(2)}) collective-permute-start(bf16[640,128]{1,0:T(8,128)(2,1)S(1)} %get-tuple-element.24), channel_id=1, source_target_pairs={{2,0},{3,1},{0,2},{1,3},{6,4},{7,5},{4,6},{5,7},{10,8},{11,9},{8,1... | collective-permute-start | bytes 491528 | tf_op jit(solution)/shard_map/ppermute | solution.py:37
  20.3 7.2 %collective-permute-start.9 = (bf16[816,128]{1,0:T(8,128)(2,1)S(1)}, bf16[816,128]{1,0:T(8,128)(2,1)S(1)}, u32[]{:S(2)}, u32[]{:S(2)}) collective-permute-start(bf16[816,128]{1,0:T(8,128)(2,1)S(1)} %get-tuple-element.22.refs_3_), channel_id=1, source_target_pairs={{16,0},{0,16},{17,1},{1,17},{18,2},{2,18},{19,3},{3,19},{20,4},{4,... | collective-permute-start | bytes 626696 | tf_op jit(solution)/shard_map/ppermute | solution.py:26
  20.9 6.6 %collective-permute-start.10 = (bf16[768,128]{1,0:T(8,128)(2,1)S(1)}, bf16[768,128]{1,0:T(8,128)(2,1)S(1)}, u32[]{:S(2)}, u32[]{:S(2)}) collective-permute-start(bf16[768,128]{1,0:T(8,128)(2,1)S(1)} %get-tuple-element.30), channel_id=1, source_target_pairs={{2,0},{3,1},{0,2},{1,3},{6,4},{7,5},{4,6},{5,7},{10,8},{11,9},{8,1... | collective-permute-start | bytes 589832 | tf_op jit(solution)/shard_map/ppermute | solution.py:37
  21.4 8.2 %collective-permute-start.7 = (bf16[1536,128]{1,0:T(8,128)(2,1)S(1)}, bf16[1536,128]{1,0:T(8,128)(2,1)S(1)}, u32[]{:S(2)}, u32[]{:S(2)}) collective-permute-start(bf16[1536,128]{1,0:T(8,128)(2,1)S(1)} %collective-permute-done.3.refs_1_.refs_4_.refs_7_), channel_id=1, source_target_pairs={{1,0},{0,1},{3,2},{2,3},{5,4},{4,5},{7,6},{6,7},{9,8},{8,9},{11,10... | collective-permute-start | bytes 1179656 | tf_op jit(solution)/shard_map/ppermute | solution.py:37
  21.4 8.2 %collective-permute-start.8 = (bf16[1536,128]{1,0:T(8,128)(2,1)S(1)}, bf16[1536,128]{1,0:T(8,128)(2,1)S(1)}, u32[]{:S(2)}, u32[]{:S(2)}) collective-permute-start(bf16[1536,128]{1,0:T(8,128)(2,1)S(1)} %collective-permute-done.2.refs_0_.refs_3_), channel_id=1, source_target_pairs={{1,0},{0,1},{3,2},{2,3},{5,4},{4,5},{7,6},{6,7},{9,8},{8,9},{11,10... | collective-permute-start | bytes 1179656 | tf_op jit(solution)/shard_map/ppermute | solution.py:37
  22.3 8.9 %collective-permute-start.11 = (bf16[2560,128]{1,0:T(8,128)(2,1)S(1)}, bf16[2560,128]{1,0:T(8,128)(2,1)S(1)}, u32[]{:S(2)}, u32[]{:S(2)}) collective-permute-start(bf16[2560,128]{1,0:T(8,128)(2,1)S(1)} %pack_two_mate.1), channel_id=1, source_target_pairs={{1,0},{0,1},{3,2},{2,3},{5,4},{4,5},{7,6},{6,7},{9,8},{8,9},{11,10... | collective-permute-start | bytes 1966088 | tf_op jit(solution)/shard_map/ppermute | solution.py:37
  22.5 8.8 %copy-start = (bf16[1,12,128,128]{3,2,1,0:T(8,128)(2,1)S(1)}, bf16[1,12,128,128]{3,2,1,0:T(8,128)(2,1)}, u32[]{:S(2)}) copy-start(bf16[1,12,128,128]{3,2,1,0:T(8,128)(2,1)} %param.8) | copy-start | bytes 1179652
  27.5 9.9 %collective-permute-start.12 = (bf16[1280,128]{1,0:T(8,128)(2,1)S(1)}, bf16[1280,128]{1,0:T(8,128)(2,1)S(1)}, u32[]{:S(2)}, u32[]{:S(2)}) collective-permute-start(bf16[1280,128]{1,0:T(8,128)(2,1)S(1)} %get-tuple-element.32.refs_15_), channel_id=1, source_target_pairs={{16,0},{0,16},{17,1},{1,17},{18,2},{2,18},{19,3},{3,19},{20,4},{4,... | collective-permute-start | bytes 983048 | tf_op jit(solution)/shard_map/ppermute | solution.py:26
  29.1 9.0 %collective-permute-start.13 = (bf16[1280,128]{1,0:T(8,128)(2,1)S(1)}, bf16[1280,128]{1,0:T(8,128)(2,1)S(1)}, u32[]{:S(2)}, u32[]{:S(2)}) collective-permute-start(bf16[1280,128]{1,0:T(8,128)(2,1)S(1)} %get-tuple-element.33), channel_id=1, source_target_pairs={{2,0},{3,1},{0,2},{1,3},{6,4},{7,5},{4,6},{5,7},{10,8},{11,9},{8,1... | collective-permute-start | bytes 983048 | tf_op jit(solution)/shard_map/ppermute | solution.py:37
  29.6 8.8 %collective-permute-start.14 = (bf16[1632,128]{1,0:T(8,128)(2,1)S(1)}, bf16[1632,128]{1,0:T(8,128)(2,1)S(1)}, u32[]{:S(2)}, u32[]{:S(2)}) collective-permute-start(bf16[1632,128]{1,0:T(8,128)(2,1)S(1)} %get-tuple-element.34), channel_id=1, source_target_pairs={{1,0},{0,1},{3,2},{2,3},{5,4},{4,5},{7,6},{6,7},{9,8},{8,9},{11,10... | collective-permute-start | bytes 1253384 | tf_op jit(solution)/shard_map/ppermute | solution.py:37
  29.6 7.8 %collective-permute-start.15 = (bf16[96,128]{1,0:T(8,128)(2,1)S(1)}, bf16[96,128]{1,0:T(8,128)(2,1)S(1)}, u32[]{:S(2)}, u32[]{:S(2)}) collective-permute-start(bf16[96,128]{1,0:T(8,128)(2,1)S(1)} %get-tuple-element.35.refs_0_), channel_id=1, source_target_pairs={{3,0},{2,1},{1,2},{0,3},{7,4},{6,5},{5,6},{4,7},{11,8},{10,9},{9,1... | collective-permute-start | bytes 73736 | tf_op jit(solution)/shard_map/ppermute | solution.py:37
  38.2 3.7 %collective-permute-start.16 = (bf16[2560,128]{1,0:T(8,128)(2,1)S(1)}, bf16[2560,128]{1,0:T(8,128)(2,1)S(1)}, u32[]{:S(2)}, u32[]{:S(2)}) collective-permute-start(bf16[2560,128]{1,0:T(8,128)(2,1)S(1)} %pack_four.1), channel_id=1, source_target_pairs={{1,0},{0,1},{3,2},{2,3},{5,4},{4,5},{7,6},{6,7},{9,8},{8,9},{11,10... | collective-permute-start | bytes 1966088 | tf_op jit(solution)/shard_map/ppermute | solution.py:37
  46.9 1.6 %collective-permute-start.17 = (f32[8,128]{1,0:T(8,128)S(1)}, f32[8,128]{1,0:T(8,128)S(1)}, u32[]{:S(2)}, u32[]{:S(2)}) collective-permute-start(f32[8,128]{1,0:T(8,128)S(1)} %get-tuple-element.38), channel_id=1, source_target_pairs={{1,0},{0,1},{3,2},{2,3},{5,4},{4,5},{7,6},{6,7},{9,8},{8,9},{11,10... | collective-permute-start | bytes 12296 | tf_op jit(solution)/shard_map/ppermute | solution.py:37
  47.3 3.0 %collective-permute-start.18 = (f32[8,128]{1,0:T(8,128)S(1)}, f32[8,128]{1,0:T(8,128)S(1)}, u32[]{:S(2)}, u32[]{:S(2)}) collective-permute-start(f32[8,128]{1,0:T(8,128)S(1)} %get-tuple-element.38), channel_id=1, source_target_pairs={{3,0},{2,1},{1,2},{0,3},{7,4},{6,5},{5,6},{4,7},{11,8},{10,9},{9,1... | collective-permute-start | bytes 12296 | tf_op jit(solution)/shard_map/ppermute | solution.py:37
  50.5 3.6 %collective-permute-start.19 = (f32[8,128]{1,0:T(8,128)S(1)}, f32[8,128]{1,0:T(8,128)S(1)}, u32[]{:S(2)}, u32[]{:S(2)}) collective-permute-start(f32[8,128]{1,0:T(8,128)S(1)} %pad_maximum_fusion.1), channel_id=1, source_target_pairs={{16,0},{0,16},{17,1},{1,17},{18,2},{2,18},{19,3},{3,19},{20,4},{4,... | collective-permute-start | bytes 12296 | tf_op jit(solution)/shard_map/ppermute | solution.py:26
  54.2 6.1 %collective-permute-start.20 = (f32[16,128]{1,0:T(8,128)S(1)}, f32[16,128]{1,0:T(8,128)S(1)}, u32[]{:S(2)}, u32[]{:S(2)}) collective-permute-start(f32[16,128]{1,0:T(8,128)S(1)} %pad_maximum_fusion.refs_0_), channel_id=1, source_target_pairs={{12,0},{8,4},{4,8},{0,12},{13,1},{9,5},{5,9},{1,13},{14,2},{10,6},... | collective-permute-start | bytes 24584 | tf_op jit(solution)/shard_map/ppermute | solution.py:32
  58.7 3.7 %collective-permute-start.21 = (f32[16,128]{1,0:T(8,128)S(1)}, f32[16,128]{1,0:T(8,128)S(1)}, u32[]{:S(2)}, u32[]{:S(2)}) collective-permute-start(f32[16,128]{1,0:T(8,128)S(1)} %pad_maximum_fusion.refs_0_), channel_id=1, source_target_pairs={{4,0},{0,4},{12,8},{8,12},{5,1},{1,5},{13,9},{9,13},{6,2},{2,6},{1... | collective-permute-start | bytes 24584 | tf_op jit(solution)/shard_map/ppermute | solution.py:32

commit v12 on v11

--- a/solution.py
+++ b/solution.py
@@ -129,17 +129,13 @@
         copy.wait()
 
 
-def prepare_kernel(axes, count, layout, late_from, *refs):
-    basis_ref = refs[2]
-    early_ref, late_ref, info_ref, spread_ref, own_basis_ref = refs[-11:-6]
-    neighbors_ref, size_ref, known, inverse, layout_ref, loads = refs[-6:]
+def spread_kernel(axes, *refs):
+    basis_ref = refs[1]
+    spread_ref, own_basis_ref, neighbors_ref, loads = refs[-4:]
     at = Places(*axes)
-    load(refs[:2], (neighbors_ref, size_ref), loads)
+    load(refs[:1], (neighbors_ref,), loads)
     slots, atoms = neighbors_ref.shape
     bits = atoms.bit_length() - 1
-    for i, value in enumerate(layout):
-        layout_ref[i] = value
-    lines = count * at.n_lay
 
     def hot(rows, atom, first):
         sub = lax.broadcasted_iota(jnp.int32, (rows, SHELLS * atoms), 0)
@@ -150,19 +146,30 @@
         picked = jnp.where(chosen, 1.0, 0.0).astype(jnp.bfloat16)
         return jnp.dot(picked, basis_ref[...], preferred_element_type=jnp.float32).astype(jnp.bfloat16)
 
+    for w, (atom, rank) in enumerate(own_ranks(at, neighbors_ref)):
+        spread_ref[:, w * LANES : (w + 1) * LANES] = rows_of(hot(LANES, atom, rank * SHELLS))
+    own_basis_ref[...] = rows_of(hot(16, at.me, 0))
+
+
+def prepare_kernel(axes, count, layout, late_from, *refs):
+    early_ref, late_ref, info_ref, neighbors_ref, size_ref, known, inverse, layout_ref, loads = refs[-9:]
+    at = Places(*axes)
+    load(refs[:2], (neighbors_ref, size_ref), loads)
+    slots = neighbors_ref.shape[0]
+    lines = count * at.n_lay
+    for i, value in enumerate(layout):
+        layout_ref[i] = value
     self_slot = jnp.int32(0)
-    for w, (atom, rank) in enumerate(own_ranks(at, neighbors_ref)):
+    for w in range(slots):
+        atom = neighbors_ref[w, at.me]
         row, col, lay = at.split(atom)
         step_row = (row - at.row) & (at.n_row - 1)
         self_slot = jnp.where(atom == at.me, w, self_slot)
         info_ref[w] = size_ref[atom]
-        spread_ref[:, w * LANES : (w + 1) * LANES] = rows_of(hot(LANES, atom, rank * SHELLS))
-        flip = lay ^ at.lay
         known[0, w] = atom
         known[1, w] = jnp.where(col == at.col, 0, jnp.where(col == (at.col ^ 1), 1, 2))
-        known[2, w] = jnp.where(step_row == 0, 0, jnp.where(step_row == 1, 1, 2)) * at.n_lay + flip
+        known[2, w] = jnp.where(step_row == 0, 0, jnp.where(step_row == 1, 1, 2)) * at.n_lay + (lay ^ at.lay)
         inverse[atom] = -1
-    own_basis_ref[...] = rows_of(hot(16, at.me, 0))
     info_ref[slots] = size_ref[at.me]
     info_ref[slots + 1] = self_slot
 
@@ -224,7 +231,7 @@
         refs[inputs + target][place : place + rows] = refs[source][start : start + rows]
 
 
-def pack(values, plans, extra, name):
+def pack(values, plans, extra, name, cost=0):
     moves, shapes = [], []
     for target, plan in enumerate(plans):
         place = 0
@@ -241,7 +248,7 @@
         compiler_params=pltpu.CompilerParams(
             vmem_limit_bytes=(1 << 20) + 256 * sum(x.shape[0] for x in list(values) + shapes)
         ),
-        cost_estimate=pl.CostEstimate(flops=0, bytes_accessed=3_000_000, transcendentals=0),
+        cost_estimate=pl.CostEstimate(flops=cost, bytes_accessed=1000, transcendentals=0),
         name=name,
     )(*values, *extra)
 
@@ -346,10 +353,8 @@
         copy = pltpu.make_async_copy(source, geos.at[k], sems.at[k])
         copy.start()
         copies.append(copy)
-    cells = plane_ref.shape[2]
-    cell = lax.broadcasted_iota(jnp.int32, (cells, LANES), 0)
-    grid_x = (cell // BY).astype(jnp.float32)
-    grid_y = (cell % BY).astype(jnp.float32)
+    steps_x = lax.broadcasted_iota(jnp.int32, (BX, LANES), 0).astype(jnp.float32)
+    steps_y = lax.broadcasted_iota(jnp.int32, (BY, LANES), 0).astype(jnp.float32)
     grid_z = lax.broadcasted_iota(jnp.int32, (LANES, BZ), 1).astype(jnp.float32)
     lane = lax.broadcasted_iota(jnp.int32, (1, LANES), 1)
     shell = (lane % SHELLS + 1).astype(jnp.float32)
@@ -378,17 +383,22 @@
             [0.5 * geo[2:3] + lift, reach, rate_t, inverse, jnp.zeros((4, LANES), jnp.float32)], axis=0
         )
         sub = packed.T
-        d_x = nearest(grid_x - (0.5 * geo[0:1] + float(BX * step_row)), periods[0])
-        d_y = nearest(grid_y - (0.5 * geo[1:2] + float(BY * side) * ahead), periods[1])
-        inside = (jnp.abs(d_x) <= reach) & (jnp.abs(d_y) <= reach)
-        squared = d_x * d_x + d_y * d_y
+        d_x = nearest(steps_x - (0.5 * geo[0:1] + float(BX * step_row)), periods[0])
+        d_y = nearest(steps_y - (0.5 * geo[1:2] + float(BY * side) * ahead), periods[1])
+        inside_x = jnp.abs(d_x) <= reach
+        inside_y = jnp.abs(d_y) <= reach
+        squared_x = d_x * d_x
+        squared_y = d_y * d_y
         d_z = nearest(grid_z - sub[:, 0:1], periods[2])
         inside_z = jnp.abs(d_z) <= sub[:, 1:2]
         squared_z = d_z * d_z
         for s in range(SHELLS):
             part = 1.0 / ((s + 1) * (s + 1))
             rate = inverse * part + rate_t
-            plane_ref[o, s] = jnp.where(inside, jnp.exp(-rate * squared), 0.0).astype(plane_ref.dtype)
+            along_x = jnp.where(inside_x, jnp.exp(-rate * squared_x), 0.0)
+            along_y = jnp.where(inside_y, jnp.exp(-rate * squared_y), 0.0)
+            for x in range(BX):
+                plane_ref[o, s, x * BY : (x + 1) * BY] = (along_x[x : x + 1] * along_y).astype(plane_ref.dtype)
             rate_z = sub[:, 3:4] * part + sub[:, 2:3]
             line_ref[o, s] = jnp.where(inside_z, jnp.exp(-rate_z * squared_z), 0.0).astype(line_ref.dtype)
 
@@ -497,14 +507,12 @@
     corners = [("end", di) for di in others] + [("top", di) for di in others]
     names = ["down", "up", "geo", "far"] + [("x", di) for di in others]
     plans = [
-        [(1, 0, picks), (3, full - size, size), (2, 0, GEO), (1, picks, GEO), (0, picks, GEO)],
-        [(0, 0, picks)] + [(di + 3, most, size) for di in others],
+        [(1, 0, picks), (0, 0, picks), (3, full - size, size), (2, 0, GEO), (1, picks, GEO), (0, picks, GEO)],
+        [(1, 0, picks), (0, 0, picks)] + [(di + 3, most, size) for di in others] + [(2, 0, GEO), (1, picks, GEO), (0, picks, GEO)],
         [(2, 0, GEO), (1, picks, GEO), (0, picks, GEO)],
     ]
     two_x, two_y, geos = pack([buffers[name] for name in names], plans, [m_row], "pack_two")
     to_mate = corners + ["up", "down"]
-    plans = [[(i, 0, picks if name in ("up", "down") else most) for i, name in enumerate(to_mate)]]
-    two_m = pack([buffers[name] for name in to_mate], plans, [], "pack_two_mate")[0]
     for di in others:
         note(("mate x", di), from_layer(x_row[di], 1), row_of(di, 1))
     note("mate far", from_layer(y_row, 1), row_of(0, 3))
@@ -517,26 +525,25 @@
 
     contents = {}
     for di in others:
-        contents["two x", di] = side_of("up", di, 0) + row_of(di, 2, slots - 1, slots) + [(("geo", di, 0), GEO)]
+        contents["two x", di] = side_of("up", di, 0) + side_of("down", di, 0)
+        contents["two x", di] += row_of(di, 2, slots - 1, slots) + [(("geo", di, 0), GEO)]
         contents["two x", di] += [(("up geo", di, 0), GEO), (("down geo", di, 0), GEO)]
-    contents["two y"] = side_of("down", 0, 2)
-    contents["two y"] += sum([row_of(di, 2, halfway - 1, halfway) for di in others], [])
+    contents["two y"] = side_of("up", 0, 2) + side_of("down", 0, 2)
+    contents["two y"] += sum([row_of(di, 2, halfway - 1, halfway) for di in others], []) + [(None, 3 * GEO)]
     contents["two m"] = sum([row_of(di, 3, halfway, slots - 1) for di in others], [])
     contents["two m"] += sum([row_of(di, 3, 0, halfway - 1) for di in others], [])
     contents["two m"] += side_of("up", 0, 1) + side_of("down", 0, 1)
     for di in others:
-        contents["three x", di] = side_of("down", di, 0) + side_of("down", di, 2)
-    contents["three y"] = side_of("up", 0, 2) + sum([side_of("up", di, 2) for di in others], [])
+        contents["three x", di] = side_of("up", di, 2)
+    contents["three y"] = sum([side_of("down", di, 2) for di in others], [])
     contents["three m"] = []
     for di in others:
-        contents["three m"] += side_of("up", di, 1) + row_of(di, 3, slots - 1, slots)
-    contents["three m"] += side_of("down", 0, 3)
-    contents["three m"] += sum([row_of(di, 3, halfway - 1, halfway) for di in others], [])
+        contents["three m"] += side_of("up", di, 1) + side_of("down", di, 1) + row_of(di, 3, slots - 1, slots)
+    contents["three m"] += side_of("up", 0, 3) + side_of("down", 0, 3)
+    contents["three m"] += sum([row_of(di, 3, halfway - 1, halfway) for di in others], []) + [(None, 3 * GEO)]
     contents["three m"] += [("geos", count * 3 * GEO)]
-    contents["four"] = []
-    for di in others:
-        contents["four"] += side_of("down", di, 1) + side_of("down", di, 3)
-    contents["four"] += side_of("up", 0, 3) + sum([side_of("up", di, 3) for di in others], [])
+    contents["four"] = sum([side_of("up", di, 3) for di in others], [])
+    contents["four"] += sum([side_of("down", di, 3) for di in others], [])
     lengths = {name: sum(rows for _, rows in content) for name, content in contents.items()}
     for name in early_order:
         if name in buffers:
@@ -568,17 +575,15 @@
     ]
     pairs = slots * (slots + 1) // 2
     entries = pairs + UNROLL + 1
-    early_table, late_table, info, spread, own_basis = pl.pallas_call(
+    early_table, late_table, info = pl.pallas_call(
         functools.partial(prepare_kernel, axes, count, tuple(layout), late_from),
         out_shape=(
             jax.ShapeDtypeStruct((entries,), jnp.int32),
             jax.ShapeDtypeStruct((entries,), jnp.int32),
             jax.ShapeDtypeStruct((slots + 2,), jnp.int32),
-            jax.ShapeDtypeStruct((LANES, full), jnp.bfloat16),
-            jax.ShapeDtypeStruct((16, size), jnp.bfloat16),
         ),
-        in_specs=[HBM, HBM, VMEM, ANY] + [ANY] * len(corners),
-        out_specs=(SMEM, SMEM, SMEM, VMEM, VMEM),
+        in_specs=[HBM, HBM, ANY],
+        out_specs=(SMEM, SMEM, SMEM),
         scratch_shapes=[
             pltpu.SMEM((slots, atoms), jnp.int32),
             pltpu.SMEM((atoms,), jnp.int32),
@@ -587,33 +592,50 @@
             pltpu.SMEM((len(layout),), jnp.int32),
             pltpu.SemaphoreType.DMA((2,)),
         ],
-        compiler_params=pltpu.CompilerParams(vmem_limit_bytes=(2 << 20) + atoms * 16384),
-        cost_estimate=pl.CostEstimate(flops=6_000_000_000, bytes_accessed=8_000_000, transcendentals=0),
+        compiler_params=pltpu.CompilerParams(vmem_limit_bytes=1 << 20),
+        cost_estimate=pl.CostEstimate(flops=1000, bytes_accessed=1000, transcendentals=0),
         name="prepare",
-    )(listings, atom_size, basis_proj.transpose(1, 0, 2).reshape(SHELLS * atoms, size), two_x, *[buffers[name] for name in corners])
-
+    )(listings, atom_size, two_x)
+
+    plans = [[(i, 0, picks if name in ("up", "down") else most) for i, name in enumerate(to_mate)]]
+    two_m = pack([buffers[name] for name in to_mate], plans, [], "pack_two_mate", 3_000_000_000)[0]
     for di in others:
         note(("two x", di), on_row(two_x, di), contents["two x", di])
     note("two y", from_layer(two_y, 2), contents["two y"])
+    early_mates = ["mate far"] + [("mate x", di) for di in others]
     note("two m", from_layer(two_m, 1), contents["two m"])
 
     buffers["geos"] = geos
-    names = ["up", "down", "two y", "geos"] + [("two x", di) for di in others]
+    names = ["two y", "geos"] + [("two x", di) for di in others]
     place = {name: i for i, name in enumerate(names)}
-    gather = [(place["geos"], 0, 3 * GEO)] + [(place["two x", di], picks + size, 3 * GEO) for di in others]
+    gather = [(place["geos"], 0, 3 * GEO)] + [(place["two x", di], 2 * picks + size, 3 * GEO) for di in others]
     xs = [place["two x", di] for di in others]
     plans = [
-        [(1, 0, picks), (2, 0, picks)],
-        [(0, 0, picks)] + [(x, 0, picks) for x in xs],
-        [(x, 0, picks + size) for x in xs] + [(2, 0, lengths["two y"])] + gather,
+        [(0, 0, picks)],
+        [(x, picks, picks) for x in xs],
+        [(x, 0, 2 * picks + size) for x in xs] + [(0, 0, lengths["two y"])] + gather,
         gather,
     ]
-    three_x, three_y, three_m, geos = pack([buffers[name] for name in names], plans, [own_basis], "pack_three")
+    three_x, three_y, three_m, geos = pack([buffers[name] for name in names], plans, [buffers[name] for name in early_mates] + [two_m, info], "pack_three")
     for di in others:
         note(("three x", di), on_row(three_x, di), contents["three x", di])
     note("three y", from_layer(three_y, 2), contents["three y"])
     note("three m", from_layer(three_m, 1), contents["three m"])
     third_geos = from_layer(geos, 3)
+
+    spread, own_basis = pl.pallas_call(
+        functools.partial(spread_kernel, axes),
+        out_shape=(
+            jax.ShapeDtypeStruct((LANES, full), jnp.bfloat16),
+            jax.ShapeDtypeStruct((16, size), jnp.bfloat16),
+        ),
+        in_specs=[HBM, VMEM, ANY],
+        out_specs=(VMEM, VMEM),
+        scratch_shapes=[pltpu.SMEM((slots, atoms), jnp.int32), pltpu.SemaphoreType.DMA((1,))],
+        compiler_params=pltpu.CompilerParams(vmem_limit_bytes=(2 << 20) + atoms * 16384),
+        cost_estimate=pl.CostEstimate(flops=1000, bytes_accessed=1000, transcendentals=0),
+        name="spread_basis",
+    )(listings, basis_proj.transpose(1, 0, 2).reshape(SHELLS * atoms, size), three_x)
 
     early_values = [buffers[name] for name in early_order]
     gram = pl.pallas_call(
@@ -628,7 +650,7 @@
     )(early_table, *early_values, three_x)
 
     thirds = [buffers["three x", di] for di in others] + [buffers["three y"]]
-    four = pack(thirds, [[(i, 0, value.shape[0]) for i, value in enumerate(thirds)]], [gram, third_geos], "pack_four")[0]
+    four = pack(thirds, [[(i, 0, value.shape[0]) for i, value in enumerate(thirds)]], [gram, third_geos, own_basis], "pack_four")[0]
     note("four", from_layer(four, 1), contents["four"])
 
     column_steps = (0, 1, -1)

time: 64 us -> 62.7 us (0.980)
  starting transfers between devices: 23 us -> 18.1 us
  waiting for transfers between devices: 19.7 us -> 23.2 us
    ppermute x5, waiting for transfers between devices: 4.02 us -> 10.3 us  [from_offset(): lax.ppermute(x, axis, [((i + step) % count, i) for i in range(count)])]
    ppermute x13, waiting for transfers between devices: 9.27 us -> 6.44 us  [from_layer(): return lax.ppermute(x, 'layer', [(i ^ flip, i) for i in range(count)])]
    ppermute x4, starting transfers between devices: 8.14 us -> 5.55 us  [from_column(): lax.ppermute(x, 'col', [((i + step[i]) % count, i) for i in range(count)])]
    ppermute x13, starting transfers between devices: 8.6 us -> 6.66 us  [from_layer(): return lax.ppermute(x, 'layer', [(i ^ flip, i) for i in range(count)])]
    pallas_call x0 -> x1, Pallas kernels: none -> 1.01 us  [local(): pl.pallas_call(functools.partial(spread_kernel, axes), out_shape=(jax.Sha...]
    pallas_call x1, Pallas kernels: 3.52 us -> 2.85 us  [local(): pl.pallas_call(functools.partial(profile_kernel, periods, tile_steps, at[...]
  transfers between devices with their start and end apart: 22 -> 22, of which waited for: 11 -> 12; matrix products, arithmetic and copies ran while one was open for 0% -> 0% of each run, Pallas kernels for 20% -> 20%
where the time goes in v12:
time: 62.7 us; the launch traced here: 62.5 us
  waiting for transfers between devices  23.2 us (37%)
  Pallas kernels  19.2 us (31%)
  starting transfers between devices  18.1 us (29%)
  local copies, waits for them, and re-layouts  1.09 us (2%)
  between operations  0.79 us (1%)
    ppermute x5, waiting for transfers between devices, from_offset(): lax.ppermute(x, axis, [((i + step) % count, i) for i in range(count)])  10.3 us
    ppermute x13, starting transfers between devices, from_layer(): return lax.ppermute(x, 'layer', [(i ^ flip, i) for i in range(count)])  6.66 us
    ppermute x13, waiting for transfers between devices, from_layer(): return lax.ppermute(x, 'layer', [(i ^ flip, i) for i in range(count)])  6.44 us
    ppermute x4, waiting for transfers between devices, from_column(): lax.ppermute(x, 'col', [((i + step[i]) % count, i) for i in range(count)])  6.39 us
    ppermute x5, starting transfers between devices, from_offset(): lax.ppermute(x, axis, [((i + step) % count, i) for i in range(count)])  5.86 us
    ppermute x4, starting transfers between devices, from_column(): lax.ppermute(x, 'col', [((i + step[i]) % count, i) for i in range(count)])  5.55 us
    pallas_call x1, Pallas kernels, local(): pl.pallas_call(functools.partial(step_kernel, len(late_values)), out_shap...  4.98 us
    pallas_call x1, Pallas kernels, local(): pl.pallas_call(functools.partial(prepare_kernel, axes, count, tuple(layou...  3.97 us
  transfers between devices with their start and end apart: 22, of which 12 were waited for; matrix products, arithmetic and copies ran while one was open for 0% of the time, Pallas kernels for 20%

profile of v12, /device:TPU:0, one launch (start us, length us, event | category | flops | bytes accessed | tf_op | source)
XLA Modules:
  0.0 62.5 jit_solution(9751823971449140019)
XLA Ops:
  0.6 0.0 copy-start.2
  0.6 0.0 copy-start.4
  0.7 3.0 %collective-permute-start.2 = (bf16[1536,128]{1,0:T(8,128)(2,1)}, bf16[1536,128]{1,0:T(8,128)(2,1)S(1)}, u32[]{:S(2)}, u32[]{:S(2)}) collective-permute-start(bf16[1536,128]{1,0:T(8,128)(2,1)} %bitcast.11), channel_id=1, source_target_pairs={{2,0},{3,1},{0,2},{1,3},{6,4},{7,5},{4,6},{5,7},{10,8},{11,9},{8,1... | collective-permute-start | bytes 1179656 | tf_op jit(solution)/shard_map/ppermute | solution.py:37
  3.7 1.5 %collective-permute-start.3 = (bf16[1536,128]{1,0:T(8,128)(2,1)}, bf16[1536,128]{1,0:T(8,128)(2,1)S(1)}, u32[]{:S(2)}, u32[]{:S(2)}) collective-permute-start(bf16[1536,128]{1,0:T(8,128)(2,1)} %bitcast.12), channel_id=1, source_target_pairs={{16,0},{0,16},{17,1},{1,17},{18,2},{2,18},{19,3},{3,19},{20,4},{4,... | collective-permute-start | bytes 1179656 | tf_op jit(solution)/shard_map/ppermute | solution.py:26
  5.2 0.0 collective-permute-start.4
  5.2 2.5 %pick_column_blocks.1.refs_2_ = bf16[656,128]{1,0:T(8,128)(2,1)} custom-call(s32[12,32]{1,0:T(8,128)} %bitcast.17, s32[1,12]{1,0:T(1,128)} %refs_1_.2, s32[32]{0:T(128)} %refs_2_.1, s32[32]{0:T(128)} %refs_3_.1, s32[32]{0:T(128)} %refs_4_.1, bf16[12,128,128]{2,1,0:T(8,128)(2,1)} %bitcast.14), custom_call_target="tpu_custom_call" | custom-call | tf_op jit(solution)/shard_map/pick_column_blocks/pallas_call | solution.py:447
  7.7 3.7 %collective-permute-start = (bf16[656,128]{1,0:T(8,128)(2,1)}, bf16[656,128]{1,0:T(8,128)(2,1)S(1)}, u32[]{:S(2)}, u32[]{:S(2)}) collective-permute-start(bf16[656,128]{1,0:T(8,128)(2,1)} %pick_column_blocks.1.refs_2_), channel_id=1, source_target_pairs={{12,0},{8,4},{4,8},{0,12},{13,1},{9,5},{5,9},{1,13},{14,2},{10,6},... | collective-permute-start | bytes 503816 | tf_op jit(solution)/shard_map/ppermute | solution.py:32
  11.3 0.0 collective-permute-start.1
  11.4 1.7 %collective-permute-done.2.refs_0_.refs_3_ = bf16[1536,128]{1,0:T(8,128)(2,1)S(1)} collective-permute-done((bf16[1536,128]{1,0:T(8,128)(2,1)}, bf16[1536,128]{1,0:T(8,128)(2,1)S(1)}, u32[]{:S(2)}, u32[]{:S(2)}) %collective-permute-start.2) | collective-permute-done | bytes 393248 | tf_op jit(solution)/shard_map/ppermute | solution.py:37
  13.0 1.5 %collective-permute-done.3.refs_1_.refs_4_.refs_7_ = bf16[1536,128]{1,0:T(8,128)(2,1)S(1)} collective-permute-done((bf16[1536,128]{1,0:T(8,128)(2,1)}, bf16[1536,128]{1,0:T(8,128)(2,1)S(1)}, u32[]{:S(2)}, u32[]{:S(2)}) %collective-permute-start.3) | collective-permute-done | bytes 393248 | tf_op jit(solution)/shard_map/ppermute | solution.py:26
  14.5 0.9 %copy-done.1 = bf16[656,128]{1,0:T(8,128)(2,1)S(1)} copy-done((bf16[656,128]{1,0:T(8,128)(2,1)S(1)}, bf16[656,128]{1,0:T(8,128)(2,1)}, u32[]{:S(2)}) %copy-start.1) | copy-done | bytes 167960
  15.4 0.4 collective-permute-start.10
  15.8 1.6 %collective-permute-start.9 = (bf16[640,128]{1,0:T(8,128)(2,1)S(1)}, bf16[640,128]{1,0:T(8,128)(2,1)S(1)}, u32[]{:S(2)}, u32[]{:S(2)}) collective-permute-start(bf16[640,128]{1,0:T(8,128)(2,1)S(1)} %get-tuple-element.27), channel_id=1, source_target_pairs={{16,0},{0,16},{17,1},{1,17},{18,2},{2,18},{19,3},{3,19},{20,4},{4,... | collective-permute-start | bytes 491528 | tf_op jit(solution)/shard_map/ppermute | solution.py:26
  17.5 0.0 collective-permute-done.refs_0_.refs_3_.refs_5_
  17.5 0.0 collective-permute-start.7
  17.5 2.7 %collective-permute-done.1.refs_1_.refs_2_.refs_4_ = bf16[656,128]{1,0:T(8,128)(2,1)S(1)} collective-permute-done((bf16[656,128]{1,0:T(8,128)(2,1)}, bf16[656,128]{1,0:T(8,128)(2,1)S(1)}, u32[]{:S(2)}, u32[]{:S(2)}) %collective-permute-start.1) | collective-permute-done | bytes 167968 | tf_op jit(solution)/shard_map/ppermute | solution.py:32
  20.2 0.0 collective-permute-start.8
  20.2 0.0 collective-permute-done.4.refs_5_.refs_2_
  20.2 0.1 pack_two.1
  20.3 0.6 collective-permute-start.6
  20.9 0.0 collective-permute-done.10.refs_1_.refs_11_
  21.0 0.5 collective-permute-start.5
  21.5 0.0 copy-done.2
  21.5 4.0 %prepare.1 = (s32[83]{0:T(128)S(1)}, s32[83]{0:T(128)S(1)}, s32[14]{0:T(128)S(1)}) custom-call(s32[12,32]{1,0:T(8,128)S(1)} %bitcast.18, s32[32]{0:T(128)S(1)} %copy-done.4, bf16[1456,128]{1,0:T(8,128)(2,1)S(1)} %get-tuple-element.22.refs_2_), custom_call_target="tpu_custom_call" | custom-call | flops 1000 | bytes 1000 | tf_op jit(solution)/shard_map/prepare/pallas_call | solution.py:578
  25.5 0.0 copy-start.3
  25.5 0.0 collective-permute-done.9.refs_0_.refs_10_
  25.5 0.0 copy-start
  25.5 5.9 %collective-permute-done.6.refs_2_.refs_12_ = bf16[1456,128]{1,0:T(8,128)(2,1)S(1)} collective-permute-done((bf16[1456,128]{1,0:T(8,128)(2,1)S(1)}, bf16[1456,128]{1,0:T(8,128)(2,1)S(1)}, u32[]{:S(2)}, u32[]{:S(2)}) %collective-permute-start.6) | collective-permute-done | bytes 372768 | tf_op jit(solution)/shard_map/ppermute | solution.py:26
  31.5 0.3 collective-permute-done.5.refs_0_.refs_13_
  31.7 0.0 collective-permute-done.7.refs_3_.refs_9_
  31.7 0.0 collective-permute-done.8.refs_4_.refs_8_
  31.7 0.1 pack_three.1
  31.8 0.1 collective-permute-start.14
  31.9 0.5 collective-permute-start.11
  32.4 1.5 %collective-permute-start.12 = (bf16[640,128]{1,0:T(8,128)(2,1)S(1)}, bf16[640,128]{1,0:T(8,128)(2,1)S(1)}, u32[]{:S(2)}, u32[]{:S(2)}) collective-permute-start(bf16[640,128]{1,0:T(8,128)(2,1)S(1)} %get-tuple-element.29.refs_2_.refs_15_), channel_id=1, source_target_pairs={{16,0},{0,16},{17,1},{1,17},{18,2},{2,18},{19,3},{3,19},{20,4},{4,... | collective-permute-start | bytes 491528 | tf_op jit(solution)/shard_map/ppermute | solution.py:26
  33.9 0.5 collective-permute-start.13
  34.4 0.6 %collective-permute-start.15 = (bf16[96,128]{1,0:T(8,128)(2,1)S(1)}, bf16[96,128]{1,0:T(8,128)(2,1)S(1)}, u32[]{:S(2)}, u32[]{:S(2)}) collective-permute-start(bf16[96,128]{1,0:T(8,128)(2,1)S(1)} %get-tuple-element.35.refs_0_), channel_id=1, source_target_pairs={{3,0},{2,1},{1,2},{0,3},{7,4},{6,5},{5,6},{4,7},{11,8},{10,9},{9,1... | collective-permute-start | bytes 73736 | tf_op jit(solution)/shard_map/ppermute | solution.py:37
  35.0 0.0 copy-done.3
  35.0 1.0 %spread_basis.1 = (bf16[128,1536]{1,0:T(8,128)(2,1)S(1)}, bf16[16,128]{1,0:T(8,128)(2,1)S(1)}) custom-call(s32[12,32]{1,0:T(8,128)S(1)} %bitcast.19, bf16[192,128]{1,0:T(8,128)(2,1)S(1)} %bitcast.20, bf16[640,128]{1,0:T(8,128)(2,1)S(1)} %get-tuple-element.29.refs_2_.refs_15_), custom_call_target="tpu_custom_call" | custom-call | flops 1000 | bytes 1000 | tf_op jit(solution)/shard_map/spread_basis/pallas_call | solution.py:626
  36.1 0.0 collective-permute-done.11.refs_14_
  36.1 2.1 %gram_early.1.refs_2_.refs_3_.refs_5_ = bf16[1536,1536]{1,0:T(8,128)(2,1)S(1)} custom-call(s32[83]{0:T(128)S(1)} %get-tuple-element.32.refs_0_, bf16[1536,128]{1,0:T(8,128)(2,1)S(1)} %bitcast.15, bf16[1536,128]{1,0:T(8,128)(2,1)S(1)} %collective-permute-done.4.refs_5_.refs_2_, bf16[1536,128]{1,0:T(8,128)(2,1)S(1)} %collective-permute-done.2.refs_0_.refs_3_, ...), custom_call_target="tpu_custom_call" | custom-call | flops 1000 | bytes 1000 | tf_op jit(solution)/shard_map/gram_early/pallas_call | solution.py:641
  38.2 0.9 %collective-permute-done.15.refs_3_.refs_2_ = bf16[96,128]{1,0:T(8,128)(2,1)S(1)} collective-permute-done((bf16[96,128]{1,0:T(8,128)(2,1)S(1)}, bf16[96,128]{1,0:T(8,128)(2,1)S(1)}, u32[]{:S(2)}, u32[]{:S(2)}) %collective-permute-start.15) | collective-permute-done | bytes 24608 | tf_op jit(solution)/shard_map/ppermute | solution.py:37
  39.1 0.0 collective-permute-done.12.refs_0_.refs_6_
  39.1 0.9 %collective-permute-done.13.refs_1_.refs_7_ = bf16[640,128]{1,0:T(8,128)(2,1)S(1)} collective-permute-done((bf16[640,128]{1,0:T(8,128)(2,1)S(1)}, bf16[640,128]{1,0:T(8,128)(2,1)S(1)}, u32[]{:S(2)}, u32[]{:S(2)}) %collective-permute-start.13) | collective-permute-done | bytes 163872 | tf_op jit(solution)/shard_map/ppermute | solution.py:37
  40.1 0.2 collective-permute-start.16
  40.3 0.0 collective-permute-done.14.refs_1_.refs_8_
  40.3 2.8 %profiles.1 = (bf16[6,6,256,128]{3,2,1,0:T(8,128)(2,1)S(1)}, bf16[6,6,128,128]{3,2,1,0:T(8,128)(2,1)S(1)}) custom-call(bf16[96,128]{1,0:T(8,128)(2,1)S(1)} %get-tuple-element.35.refs_0_, bf16[2960,128]{1,0:T(8,128)(2,1)S(1)} %collective-permute-done.14.refs_1_.refs_8_, bf16[96,128]{1,0:T(8,128)(2,1)S(1)} %collective-permute-done.15.refs_3_.refs_2_, ...), custom_call_target="tpu_custom_call" | custom-call | flops 5000000000 | bytes 4000000 | tf_op jit(solution)/shard_map/profiles/pallas_call | solution.py:660
  43.1 0.0 collective-permute-done.16.refs_9_
  43.1 5.0 %square_cube_coefficients.1 = (bf16[12,128,128]{2,1,0:T(8,128)(2,1)}, f32[8,128]{1,0:T(8,128)S(1)}) custom-call(s32[83]{0:T(128)S(1)} %get-tuple-element.23.refs_0_, s32[14]{0:T(128)S(1)} %get-tuple-element.24.refs_6_.refs_1_, bf16[16,128]{1,0:T(8,128)(2,1)S(1)} %get-tuple-element.30.refs_4_.refs_2_, bf16[128,1536]{1,0:T(8,128)(2,1)S(1)} %get-tuple-element.31.refs_3_, ...), custom_call_target="tpu_custom_call" | custom-call | flops 1300000000 | bytes 8000000 | tf_op jit(solution)/shard_map/square_cube_coefficients/pallas_call | solution.py:678
  48.1 0.4 collective-permute-start.17
  48.5 0.3 collective-permute-start.18
  48.9 0.5 collective-permute-done.17
  49.3 2.2 %collective-permute-done.18 = f32[8,128]{1,0:T(8,128)S(1)} collective-permute-done((f32[8,128]{1,0:T(8,128)S(1)}, f32[8,128]{1,0:T(8,128)S(1)}, u32[]{:S(2)}, u32[]{:S(2)}) %collective-permute-start.18) | collective-permute-done | bytes 4128 | tf_op jit(solution)/shard_map/ppermute | solution.py:37
  51.6 0.1 slice.10
  51.6 0.1 slice.11
  51.7 0.1 pad_maximum_fusion.1
  51.8 0.6 %collective-permute-start.19 = (f32[8,128]{1,0:T(8,128)S(1)}, f32[8,128]{1,0:T(8,128)S(1)}, u32[]{:S(2)}, u32[]{:S(2)}) collective-permute-start(f32[8,128]{1,0:T(8,128)S(1)} %pad_maximum_fusion.1), channel_id=1, source_target_pairs={{16,0},{0,16},{17,1},{1,17},{18,2},{2,18},{19,3},{3,19},{20,4},{4,... | collective-permute-start | bytes 12296 | tf_op jit(solution)/shard_map/ppermute | solution.py:26
  52.4 3.0 %collective-permute-done.19 = f32[8,128]{1,0:T(8,128)S(1)} collective-permute-done((f32[8,128]{1,0:T(8,128)S(1)}, f32[8,128]{1,0:T(8,128)S(1)}, u32[]{:S(2)}, u32[]{:S(2)}) %collective-permute-start.19) | collective-permute-done | bytes 4128 | tf_op jit(solution)/shard_map/ppermute | solution.py:26
  55.4 0.1 pad_maximum_fusion.refs_0_
  55.5 1.8 %collective-permute-start.20 = (f32[16,128]{1,0:T(8,128)S(1)}, f32[16,128]{1,0:T(8,128)S(1)}, u32[]{:S(2)}, u32[]{:S(2)}) collective-permute-start(f32[16,128]{1,0:T(8,128)S(1)} %pad_maximum_fusion.refs_0_), channel_id=1, source_target_pairs={{12,0},{8,4},{4,8},{0,12},{13,1},{9,5},{5,9},{1,13},{14,2},{10,6},... | collective-permute-start | bytes 24584 | tf_op jit(solution)/shard_map/ppermute | solution.py:32
  57.3 0.0 collective-permute-start.21
  57.3 3.6 %collective-permute-done.20.refs_1_ = f32[16,128]{1,0:T(8,128)S(1)} collective-permute-done((f32[16,128]{1,0:T(8,128)S(1)}, f32[16,128]{1,0:T(8,128)S(1)}, u32[]{:S(2)}, u32[]{:S(2)}) %collective-permute-start.20) | collective-permute-done | bytes 8224 | tf_op jit(solution)/shard_map/ppermute | solution.py:32
  60.9 0.1 collective-permute-done.21.refs_2_
  61.0 1.5 %density.1 = f32[256,128]{1,0:T(8,128)} custom-call(f32[16,128]{1,0:T(8,128)S(1)} %pad_maximum_fusion.refs_0_, f32[16,128]{1,0:T(8,128)S(1)} %collective-permute-done.20.refs_1_, f32[16,128]{1,0:T(8,128)S(1)} %collective-permute-done.21.refs_2_, bf16[6,6,256,128]{3,2,1,0:T(8,128)(2,1)S(1)} %get-tuple-element.39.refs_3_, bf16[4608,128]{1,0:T(8,128)(2,1)S(1)} %bitcast.10), custom_call_target="tpu_custom_call" | custom-call | flops 310000000 | bytes 4000000 | tf_op jit(solution)/shard_map/density/pallas_call | solution.py:715
  (8 shorter events, 0.1 us)
Async XLA Ops:
  0.6 20.8 %copy-start.2 = (s32[32,12]{0,1:T(8,128)S(1)}, s32[32,12]{0,1:T(8,128)}, u32[]{:S(2)}) copy-start(s32[32,12]{0,1:T(8,128)} %param.9) | copy-start | bytes 4612
  0.6 20.8 %copy-start.4 = (s32[32]{0:T(128)S(1)}, s32[32]{0:T(128)}, u32[]{:S(2)}) copy-start(s32[32]{0:T(128)} %refs_1_.3) | copy-start | bytes 388
  0.7 12.4 %collective-permute-start.2 = (bf16[1536,128]{1,0:T(8,128)(2,1)}, bf16[1536,128]{1,0:T(8,128)(2,1)S(1)}, u32[]{:S(2)}, u32[]{:S(2)}) collective-permute-start(bf16[1536,128]{1,0:T(8,128)(2,1)} %bitcast.11), channel_id=1, source_target_pairs={{2,0},{3,1},{0,2},{1,3},{6,4},{7,5},{4,6},{5,7},{10,8},{11,9},{8,1... | collective-permute-start | bytes 1179656 | tf_op jit(solution)/shard_map/ppermute | solution.py:37
  3.7 10.8 %collective-permute-start.3 = (bf16[1536,128]{1,0:T(8,128)(2,1)}, bf16[1536,128]{1,0:T(8,128)(2,1)S(1)}, u32[]{:S(2)}, u32[]{:S(2)}) collective-permute-start(bf16[1536,128]{1,0:T(8,128)(2,1)} %bitcast.12), channel_id=1, source_target_pairs={{16,0},{0,16},{17,1},{1,17},{18,2},{2,18},{19,3},{3,19},{20,4},{4,... | collective-permute-start | bytes 1179656 | tf_op jit(solution)/shard_map/ppermute | solution.py:26
  5.2 15.1 %collective-permute-start.4 = (bf16[1536,128]{1,0:T(8,128)(2,1)}, bf16[1536,128]{1,0:T(8,128)(2,1)S(1)}, u32[]{:S(2)}, u32[]{:S(2)}) collective-permute-start(bf16[1536,128]{1,0:T(8,128)(2,1)} %bitcast.13), channel_id=1, source_target_pairs={{1,0},{0,1},{3,2},{2,3},{5,4},{4,5},{7,6},{6,7},{9,8},{8,9},{11,10... | collective-permute-start | bytes 1179656 | tf_op jit(solution)/shard_map/ppermute | solution.py:37
  7.7 9.8 %collective-permute-start = (bf16[656,128]{1,0:T(8,128)(2,1)}, bf16[656,128]{1,0:T(8,128)(2,1)S(1)}, u32[]{:S(2)}, u32[]{:S(2)}) collective-permute-start(bf16[656,128]{1,0:T(8,128)(2,1)} %pick_column_blocks.1.refs_2_), channel_id=1, source_target_pairs={{12,0},{8,4},{4,8},{0,12},{13,1},{9,5},{5,9},{1,13},{14,2},{10,6},... | collective-permute-start | bytes 503816 | tf_op jit(solution)/shard_map/ppermute | solution.py:32
  11.3 8.9 %collective-permute-start.1 = (bf16[656,128]{1,0:T(8,128)(2,1)}, bf16[656,128]{1,0:T(8,128)(2,1)S(1)}, u32[]{:S(2)}, u32[]{:S(2)}) collective-permute-start(bf16[656,128]{1,0:T(8,128)(2,1)} %pick_column_blocks.1.refs_2_), channel_id=1, source_target_pairs={{4,0},{0,4},{12,8},{8,12},{5,1},{1,5},{13,9},{9,13},{6,2},{2,6},{1... | collective-permute-start | bytes 503816 | tf_op jit(solution)/shard_map/ppermute | solution.py:32
  14.5 0.9 %copy-start.1 = (bf16[656,128]{1,0:T(8,128)(2,1)S(1)}, bf16[656,128]{1,0:T(8,128)(2,1)}, u32[]{:S(2)}) copy-start(bf16[656,128]{1,0:T(8,128)(2,1)} %pick_column_blocks.1.refs_2_) | copy-start | bytes 503812
  15.4 5.5 %collective-permute-start.10 = (bf16[640,128]{1,0:T(8,128)(2,1)S(1)}, bf16[640,128]{1,0:T(8,128)(2,1)S(1)}, u32[]{:S(2)}, u32[]{:S(2)}) collective-permute-start(bf16[640,128]{1,0:T(8,128)(2,1)S(1)} %get-tuple-element.28), channel_id=1, source_target_pairs={{2,0},{3,1},{0,2},{1,3},{6,4},{7,5},{4,6},{5,7},{10,8},{11,9},{8,1... | collective-permute-start | bytes 491528 | tf_op jit(solution)/shard_map/ppermute | solution.py:37
  15.8 9.6 %collective-permute-start.9 = (bf16[640,128]{1,0:T(8,128)(2,1)S(1)}, bf16[640,128]{1,0:T(8,128)(2,1)S(1)}, u32[]{:S(2)}, u32[]{:S(2)}) collective-permute-start(bf16[640,128]{1,0:T(8,128)(2,1)S(1)} %get-tuple-element.27), channel_id=1, source_target_pairs={{16,0},{0,16},{17,1},{1,17},{18,2},{2,18},{19,3},{3,19},{20,4},{4,... | collective-permute-start | bytes 491528 | tf_op jit(solution)/shard_map/ppermute | solution.py:26
  17.5 14.2 %collective-permute-start.7 = (bf16[1536,128]{1,0:T(8,128)(2,1)S(1)}, bf16[1536,128]{1,0:T(8,128)(2,1)S(1)}, u32[]{:S(2)}, u32[]{:S(2)}) collective-permute-start(bf16[1536,128]{1,0:T(8,128)(2,1)S(1)} %collective-permute-done.2.refs_0_.refs_3_), channel_id=1, source_target_pairs={{1,0},{0,1},{3,2},{2,3},{5,4},{4,5},{7,6},{6,7},{9,8},{8,9},{11,10... | collective-permute-start | bytes 1179656 | tf_op jit(solution)/shard_map/ppermute | solution.py:37
  20.2 11.5 %collective-permute-start.8 = (bf16[1536,128]{1,0:T(8,128)(2,1)S(1)}, bf16[1536,128]{1,0:T(8,128)(2,1)S(1)}, u32[]{:S(2)}, u32[]{:S(2)}) collective-permute-start(bf16[1536,128]{1,0:T(8,128)(2,1)S(1)} %collective-permute-done.3.refs_1_.refs_4_.refs_7_), channel_id=1, source_target_pairs={{1,0},{0,1},{3,2},{2,3},{5,4},{4,5},{7,6},{6,7},{9,8},{8,9},{11,10... | collective-permute-start | bytes 1179656 | tf_op jit(solution)/shard_map/ppermute | solution.py:37
  20.3 11.1 %collective-permute-start.6 = (bf16[1456,128]{1,0:T(8,128)(2,1)S(1)}, bf16[1456,128]{1,0:T(8,128)(2,1)S(1)}, u32[]{:S(2)}, u32[]{:S(2)}) collective-permute-start(bf16[1456,128]{1,0:T(8,128)(2,1)S(1)} %get-tuple-element.22.refs_2_), channel_id=1, source_target_pairs={{16,0},{0,16},{17,1},{1,17},{18,2},{2,18},{19,3},{3,19},{20,4},{4,... | collective-permute-start | bytes 1118216 | tf_op jit(solution)/shard_map/ppermute | solution.py:26
  21.0 10.8 %collective-permute-start.5 = (bf16[1456,128]{1,0:T(8,128)(2,1)S(1)}, bf16[1456,128]{1,0:T(8,128)(2,1)S(1)}, u32[]{:S(2)}, u32[]{:S(2)}) collective-permute-start(bf16[1456,128]{1,0:T(8,128)(2,1)S(1)} %get-tuple-element.25), channel_id=1, source_target_pairs={{2,0},{3,1},{0,2},{1,3},{6,4},{7,5},{4,6},{5,7},{10,8},{11,9},{8,1... | collective-permute-start | bytes 1118216 | tf_op jit(solution)/shard_map/ppermute | solution.py:37
  25.5 9.6 %copy-start.3 = (bf16[32,6,128]{2,0,1:T(8,128)(2,1)S(1)}, bf16[32,6,128]{2,0,1:T(8,128)(2,1)}, u32[]{:S(2)}) copy-start(bf16[32,6,128]{2,0,1:T(8,128)(2,1)} %param.11) | copy-start | bytes 147460
  25.5 10.5 %copy-start = (bf16[1,12,128,128]{3,2,1,0:T(8,128)(2,1)S(1)}, bf16[1,12,128,128]{3,2,1,0:T(8,128)(2,1)}, u32[]{:S(2)}) copy-start(bf16[1,12,128,128]{3,2,1,0:T(8,128)(2,1)} %param.8) | copy-start | bytes 1179652
  31.8 8.5 %collective-permute-start.14 = (bf16[2960,128]{1,0:T(8,128)(2,1)S(1)}, bf16[2960,128]{1,0:T(8,128)(2,1)S(1)}, u32[]{:S(2)}, u32[]{:S(2)}) collective-permute-start(bf16[2960,128]{1,0:T(8,128)(2,1)S(1)} %get-tuple-element.34), channel_id=1, source_target_pairs={{1,0},{0,1},{3,2},{2,3},{5,4},{4,5},{7,6},{6,7},{9,8},{8,9},{11,10... | collective-permute-start | bytes 2273288 | tf_op jit(solution)/shard_map/ppermute | solution.py:37
  31.9 4.2 %collective-permute-start.11 = (bf16[2560,128]{1,0:T(8,128)(2,1)S(1)}, bf16[2560,128]{1,0:T(8,128)(2,1)S(1)}, u32[]{:S(2)}, u32[]{:S(2)}) collective-permute-start(bf16[2560,128]{1,0:T(8,128)(2,1)S(1)} %pack_two_mate.1.refs_5_), channel_id=1, source_target_pairs={{1,0},{0,1},{3,2},{2,3},{5,4},{4,5},{7,6},{6,7},{9,8},{8,9},{11,10... | collective-permute-start | bytes 1966088 | tf_op jit(solution)/shard_map/ppermute | solution.py:37
  32.4 6.7 %collective-permute-start.12 = (bf16[640,128]{1,0:T(8,128)(2,1)S(1)}, bf16[640,128]{1,0:T(8,128)(2,1)S(1)}, u32[]{:S(2)}, u32[]{:S(2)}) collective-permute-start(bf16[640,128]{1,0:T(8,128)(2,1)S(1)} %get-tuple-element.29.refs_2_.refs_15_), channel_id=1, source_target_pairs={{16,0},{0,16},{17,1},{1,17},{18,2},{2,18},{19,3},{3,19},{20,4},{4,... | collective-permute-start | bytes 491528 | tf_op jit(solution)/shard_map/ppermute | solution.py:26
  33.9 6.2 %collective-permute-start.13 = (bf16[640,128]{1,0:T(8,128)(2,1)S(1)}, bf16[640,128]{1,0:T(8,128)(2,1)S(1)}, u32[]{:S(2)}, u32[]{:S(2)}) collective-permute-start(bf16[640,128]{1,0:T(8,128)(2,1)S(1)} %get-tuple-element.33), channel_id=1, source_target_pairs={{2,0},{3,1},{0,2},{1,3},{6,4},{7,5},{4,6},{5,7},{10,8},{11,9},{8,1... | collective-permute-start | bytes 491528 | tf_op jit(solution)/shard_map/ppermute | solution.py:37
  34.4 4.7 %collective-permute-start.15 = (bf16[96,128]{1,0:T(8,128)(2,1)S(1)}, bf16[96,128]{1,0:T(8,128)(2,1)S(1)}, u32[]{:S(2)}, u32[]{:S(2)}) collective-permute-start(bf16[96,128]{1,0:T(8,128)(2,1)S(1)} %get-tuple-element.35.refs_0_), channel_id=1, source_target_pairs={{3,0},{2,1},{1,2},{0,3},{7,4},{6,5},{5,6},{4,7},{11,8},{10,9},{9,1... | collective-permute-start | bytes 73736 | tf_op jit(solution)/shard_map/ppermute | solution.py:37
  40.1 3.0 %collective-permute-start.16 = (bf16[1280,128]{1,0:T(8,128)(2,1)S(1)}, bf16[1280,128]{1,0:T(8,128)(2,1)S(1)}, u32[]{:S(2)}, u32[]{:S(2)}) collective-permute-start(bf16[1280,128]{1,0:T(8,128)(2,1)S(1)} %pack_four.1), channel_id=1, source_target_pairs={{1,0},{0,1},{3,2},{2,3},{5,4},{4,5},{7,6},{6,7},{9,8},{8,9},{11,10... | collective-permute-start | bytes 983048 | tf_op jit(solution)/shard_map/ppermute | solution.py:37
  48.1 1.2 %collective-permute-start.17 = (f32[8,128]{1,0:T(8,128)S(1)}, f32[8,128]{1,0:T(8,128)S(1)}, u32[]{:S(2)}, u32[]{:S(2)}) collective-permute-start(f32[8,128]{1,0:T(8,128)S(1)} %get-tuple-element.38), channel_id=1, source_target_pairs={{1,0},{0,1},{3,2},{2,3},{5,4},{4,5},{7,6},{6,7},{9,8},{8,9},{11,10... | collective-permute-start | bytes 12296 | tf_op jit(solution)/shard_map/ppermute | solution.py:37
  48.5 3.0 %collective-permute-start.18 = (f32[8,128]{1,0:T(8,128)S(1)}, f32[8,128]{1,0:T(8,128)S(1)}, u32[]{:S(2)}, u32[]{:S(2)}) collective-permute-start(f32[8,128]{1,0:T(8,128)S(1)} %get-tuple-element.38), channel_id=1, source_target_pairs={{3,0},{2,1},{1,2},{0,3},{7,4},{6,5},{5,6},{4,7},{11,8},{10,9},{9,1... | collective-permute-start | bytes 12296 | tf_op jit(solution)/shard_map/ppermute | solution.py:37
  51.8 3.6 %collective-permute-start.19 = (f32[8,128]{1,0:T(8,128)S(1)}, f32[8,128]{1,0:T(8,128)S(1)}, u32[]{:S(2)}, u32[]{:S(2)}) collective-permute-start(f32[8,128]{1,0:T(8,128)S(1)} %pad_maximum_fusion.1), channel_id=1, source_target_pairs={{16,0},{0,16},{17,1},{1,17},{18,2},{2,18},{19,3},{3,19},{20,4},{4,... | collective-permute-start | bytes 12296 | tf_op jit(solution)/shard_map/ppermute | solution.py:26
  55.5 5.5 %collective-permute-start.20 = (f32[16,128]{1,0:T(8,128)S(1)}, f32[16,128]{1,0:T(8,128)S(1)}, u32[]{:S(2)}, u32[]{:S(2)}) collective-permute-start(f32[16,128]{1,0:T(8,128)S(1)} %pad_maximum_fusion.refs_0_), channel_id=1, source_target_pairs={{12,0},{8,4},{4,8},{0,12},{13,1},{9,5},{5,9},{1,13},{14,2},{10,6},... | collective-permute-start | bytes 24584 | tf_op jit(solution)/shard_map/ppermute | solution.py:32
  57.3 3.7 %collective-permute-start.21 = (f32[16,128]{1,0:T(8,128)S(1)}, f32[16,128]{1,0:T(8,128)S(1)}, u32[]{:S(2)}, u32[]{:S(2)}) collective-permute-start(f32[16,128]{1,0:T(8,128)S(1)} %pad_maximum_fusion.refs_0_), channel_id=1, source_target_pairs={{4,0},{0,4},{12,8},{8,12},{5,1},{1,5},{13,9},{9,13},{6,2},{2,6},{1... | collective-permute-start | bytes 24584 | tf_op jit(solution)/shard_map/ppermute | solution.py:32

commit v13 on v12

--- a/solution.py
+++ b/solution.py
@@ -663,16 +663,16 @@
             jax.ShapeDtypeStruct((tiles, SHELLS, BX * BY, LANES), jnp.bfloat16),
             jax.ShapeDtypeStruct((tiles, SHELLS, LANES, BZ), jnp.bfloat16),
         ),
-        in_specs=[ANY] * 4,
+        in_specs=[ANY] * 3,
         out_specs=(VMEM, VMEM),
         scratch_shapes=[
             pltpu.VMEM((3, tiles * GEO, LANES), jnp.bfloat16),
             pltpu.SemaphoreType.DMA((3,)),
         ],
         compiler_params=pltpu.CompilerParams(vmem_limit_bytes=10 << 20),
-        cost_estimate=pl.CostEstimate(flops=5_000_000_000, bytes_accessed=4_000_000, transcendentals=2_000_000),
+        cost_estimate=pl.CostEstimate(flops=1000, bytes_accessed=1000, transcendentals=0),
         name="profiles",
-    )(geos, buffers["three m"], third_geos, gram)
+    )(geos, buffers["three m"], third_geos)
 
     late_values = [buffers[name] for name in late_order]
     sign_next, coef = pl.pallas_call(
@@ -681,7 +681,7 @@
             jax.ShapeDtypeStruct((slots, size, size), jnp.bfloat16),
             jax.ShapeDtypeStruct((8, LANES), jnp.float32),
         ),
-        in_specs=[SMEM, SMEM, VMEM, VMEM, VMEM, VMEM] + [VMEM] * len(late_values) + [ANY],
+        in_specs=[SMEM, SMEM, VMEM, VMEM, VMEM, VMEM] + [VMEM] * len(late_values),
         out_specs=(VMEM, VMEM),
         scratch_shapes=[
             pltpu.VMEM((total - late_from, LANES), jnp.bfloat16),
@@ -692,7 +692,7 @@
         compiler_params=pltpu.CompilerParams(vmem_limit_bytes=(15 << 20) + 2 * (total - late_from) * LANES * 2),
         cost_estimate=pl.CostEstimate(flops=1_300_000_000, bytes_accessed=8_000_000, transcendentals=0),
         name="square_cube_coefficients",
-    )(late_table, info, own_basis, spread, own, gram, *late_values, line)
+    )(late_table, info, own_basis, spread, own, gram, *late_values)
 
     mate_coef = from_layer(coef, 1)
     third_coef = from_layer(coef, 3)

time: 62.7 us -> 60.4 us (0.963)
  waiting for transfers between devices: 23.2 us -> 18.9 us
  starting transfers between devices: 18.1 us -> 20.3 us
    ppermute x5, waiting for transfers between devices: 10.3 us -> 3.79 us  [from_offset(): lax.ppermute(x, axis, [((i + step) % count, i) for i in range(count)])]
    ppermute x13, waiting for transfers between devices: 6.44 us -> 11.6 us  [from_layer(): return lax.ppermute(x, 'layer', [(i ^ flip, i) for i in range(count)])]
    ppermute x4, waiting for transfers between devices: 6.39 us -> 3.53 us  [from_column(): lax.ppermute(x, 'col', [((i + step[i]) % count, i) for i in range(count)])]
    ppermute x13, starting transfers between devices: 6.66 us -> 8.13 us  [from_layer(): return lax.ppermute(x, 'layer', [(i ^ flip, i) for i in range(count)])]
    ppermute x4, starting transfers between devices: 5.55 us -> 6.43 us  [from_column(): lax.ppermute(x, 'col', [((i + step[i]) % count, i) for i in range(count)])]
  transfers between devices with their start and end apart: 22 -> 22, of which waited for: 12 -> 12; matrix products, arithmetic and copies ran while one was open for 0% -> 0% of each run, Pallas kernels for 20% -> 21%
where the time goes in v13:
time: 60.4 us; the launch traced here: 60.1 us
  starting transfers between devices  20.3 us (34%)
  Pallas kernels  18.9 us (31%)
  waiting for transfers between devices  18.9 us (31%)
  local copies, waits for them, and re-layouts  1.08 us (2%)
  between operations  0.79 us (1%)
    ppermute x13, waiting for transfers between devices, from_layer(): return lax.ppermute(x, 'layer', [(i ^ flip, i) for i in range(count)])  11.6 us
    ppermute x13, starting transfers between devices, from_layer(): return lax.ppermute(x, 'layer', [(i ^ flip, i) for i in range(count)])  8.13 us
    ppermute x4, starting transfers between devices, from_column(): lax.ppermute(x, 'col', [((i + step[i]) % count, i) for i in range(count)])  6.43 us
    ppermute x5, starting transfers between devices, from_offset(): lax.ppermute(x, axis, [((i + step) % count, i) for i in range(count)])  5.69 us
    pallas_call x1, Pallas kernels, local(): pl.pallas_call(functools.partial(step_kernel, len(late_values)), out_shap...  4.87 us
    pallas_call x1, Pallas kernels, local(): pl.pallas_call(functools.partial(prepare_kernel, axes, count, tuple(layou...  3.97 us
    ppermute x5, waiting for transfers between devices, from_offset(): lax.ppermute(x, axis, [((i + step) % count, i) for i in range(count)])  3.79 us
    ppermute x4, waiting for transfers between devices, from_column(): lax.ppermute(x, 'col', [((i + step[i]) % count, i) for i in range(count)])  3.53 us
  transfers between devices with their start and end apart: 22, of which 12 were waited for; matrix products, arithmetic and copies ran while one was open for 0% of the time, Pallas kernels for 21%

profile of v13, /device:TPU:0, one launch (start us, length us, event | category | flops | bytes accessed | tf_op | source)
XLA Modules:
  0.0 60.1 jit_solution(10281031850978278505)
XLA Ops:
  0.6 3.0 %collective-permute-start.2 = (bf16[1536,128]{1,0:T(8,128)(2,1)}, bf16[1536,128]{1,0:T(8,128)(2,1)S(1)}, u32[]{:S(2)}, u32[]{:S(2)}) collective-permute-start(bf16[1536,128]{1,0:T(8,128)(2,1)} %bitcast.10), channel_id=1, source_target_pairs={{2,0},{3,1},{0,2},{1,3},{6,4},{7,5},{4,6},{5,7},{10,8},{11,9},{8,1... | collective-permute-start | bytes 1179656 | tf_op jit(solution)/shard_map/ppermute | solution.py:37
  3.7 1.5 %collective-permute-start.3 = (bf16[1536,128]{1,0:T(8,128)(2,1)}, bf16[1536,128]{1,0:T(8,128)(2,1)S(1)}, u32[]{:S(2)}, u32[]{:S(2)}) collective-permute-start(bf16[1536,128]{1,0:T(8,128)(2,1)} %bitcast.11), channel_id=1, source_target_pairs={{16,0},{0,16},{17,1},{1,17},{18,2},{2,18},{19,3},{3,19},{20,4},{4,... | collective-permute-start | bytes 1179656 | tf_op jit(solution)/shard_map/ppermute | solution.py:26
  5.2 0.0 collective-permute-start.4
  5.2 2.5 %pick_column_blocks.1.refs_2_ = bf16[656,128]{1,0:T(8,128)(2,1)} custom-call(s32[12,32]{1,0:T(8,128)} %bitcast.17, s32[1,12]{1,0:T(1,128)} %refs_1_.2, s32[32]{0:T(128)} %refs_2_.1, s32[32]{0:T(128)} %refs_3_.1, s32[32]{0:T(128)} %refs_4_.1, bf16[12,128,128]{2,1,0:T(8,128)(2,1)} %bitcast.13), custom_call_target="tpu_custom_call" | custom-call | tf_op jit(solution)/shard_map/pick_column_blocks/pallas_call | solution.py:447
  7.6 3.7 %collective-permute-start = (bf16[656,128]{1,0:T(8,128)(2,1)}, bf16[656,128]{1,0:T(8,128)(2,1)S(1)}, u32[]{:S(2)}, u32[]{:S(2)}) collective-permute-start(bf16[656,128]{1,0:T(8,128)(2,1)} %pick_column_blocks.1.refs_2_), channel_id=1, source_target_pairs={{12,0},{8,4},{4,8},{0,12},{13,1},{9,5},{5,9},{1,13},{14,2},{10,6},... | collective-permute-start | bytes 503816 | tf_op jit(solution)/shard_map/ppermute | solution.py:32
  11.3 0.0 collective-permute-start.1
  11.3 1.7 %collective-permute-done.2.refs_0_.refs_3_ = bf16[1536,128]{1,0:T(8,128)(2,1)S(1)} collective-permute-done((bf16[1536,128]{1,0:T(8,128)(2,1)}, bf16[1536,128]{1,0:T(8,128)(2,1)S(1)}, u32[]{:S(2)}, u32[]{:S(2)}) %collective-permute-start.2) | collective-permute-done | bytes 393248 | tf_op jit(solution)/shard_map/ppermute | solution.py:37
  13.0 1.5 %collective-permute-done.3.refs_1_.refs_4_.refs_7_ = bf16[1536,128]{1,0:T(8,128)(2,1)S(1)} collective-permute-done((bf16[1536,128]{1,0:T(8,128)(2,1)}, bf16[1536,128]{1,0:T(8,128)(2,1)S(1)}, u32[]{:S(2)}, u32[]{:S(2)}) %collective-permute-start.3) | collective-permute-done | bytes 393248 | tf_op jit(solution)/shard_map/ppermute | solution.py:26
  14.5 0.9 %copy-done.1 = bf16[656,128]{1,0:T(8,128)(2,1)S(1)} copy-done((bf16[656,128]{1,0:T(8,128)(2,1)S(1)}, bf16[656,128]{1,0:T(8,128)(2,1)}, u32[]{:S(2)}) %copy-start.1) | copy-done | bytes 167960
  15.4 1.6 %collective-permute-start.9 = (bf16[640,128]{1,0:T(8,128)(2,1)S(1)}, bf16[640,128]{1,0:T(8,128)(2,1)S(1)}, u32[]{:S(2)}, u32[]{:S(2)}) collective-permute-start(bf16[640,128]{1,0:T(8,128)(2,1)S(1)} %get-tuple-element.27), channel_id=1, source_target_pairs={{16,0},{0,16},{17,1},{1,17},{18,2},{2,18},{19,3},{3,19},{20,4},{4,... | collective-permute-start | bytes 491528 | tf_op jit(solution)/shard_map/ppermute | solution.py:26
  16.9 0.5 collective-permute-start.10
  17.5 0.0 collective-permute-done.refs_0_.refs_3_.refs_5_
  17.5 2.7 %collective-permute-done.1.refs_1_.refs_2_.refs_4_ = bf16[656,128]{1,0:T(8,128)(2,1)S(1)} collective-permute-done((bf16[656,128]{1,0:T(8,128)(2,1)}, bf16[656,128]{1,0:T(8,128)(2,1)S(1)}, u32[]{:S(2)}, u32[]{:S(2)}) %collective-permute-start.1) | collective-permute-done | bytes 167968 | tf_op jit(solution)/shard_map/ppermute | solution.py:32
  20.2 0.0 collective-permute-done.4.refs_5_.refs_2_
  20.2 0.1 pack_two.1
  20.3 0.6 collective-permute-start.5
  20.9 0.5 collective-permute-start.6
  21.4 0.0 collective-permute-start.7
  21.4 0.0 collective-permute-done.9.refs_0_.refs_10_
  21.4 0.5 collective-permute-start.8
  21.9 0.4 collective-permute-done.10.refs_1_.refs_11_
  22.3 0.0 copy-start.3
  22.3 0.0 copy-start
  22.3 0.1 collective-permute-start.11
  22.4 0.0 copy-done.2
  22.4 0.0 copy-done.4
  22.4 4.0 %prepare.1 = (s32[83]{0:T(128)S(1)}, s32[83]{0:T(128)S(1)}, s32[14]{0:T(128)S(1)}) custom-call(s32[12,32]{1,0:T(8,128)S(1)} %bitcast.18, s32[32]{0:T(128)S(1)} %copy-done.4, bf16[1456,128]{1,0:T(8,128)(2,1)S(1)} %get-tuple-element.22.refs_2_), custom_call_target="tpu_custom_call" | custom-call | flops 1000 | bytes 1000 | tf_op jit(solution)/shard_map/prepare/pallas_call | solution.py:578
  26.4 4.6 %collective-permute-done.5.refs_0_.refs_13_ = bf16[1456,128]{1,0:T(8,128)(2,1)S(1)} collective-permute-done((bf16[1456,128]{1,0:T(8,128)(2,1)S(1)}, bf16[1456,128]{1,0:T(8,128)(2,1)S(1)}, u32[]{:S(2)}, u32[]{:S(2)}) %collective-permute-start.5) | collective-permute-done | bytes 372768 | tf_op jit(solution)/shard_map/ppermute | solution.py:37
  31.0 0.2 collective-permute-done.6.refs_2_.refs_12_
  31.2 0.0 collective-permute-done.7.refs_3_.refs_9_
  31.2 0.0 collective-permute-done.8.refs_4_.refs_8_
  31.2 0.1 pack_three.1
  31.3 0.1 collective-permute-start.14
  31.4 0.6 collective-permute-start.12
  32.0 1.6 %collective-permute-start.13 = (bf16[640,128]{1,0:T(8,128)(2,1)S(1)}, bf16[640,128]{1,0:T(8,128)(2,1)S(1)}, u32[]{:S(2)}, u32[]{:S(2)}) collective-permute-start(bf16[640,128]{1,0:T(8,128)(2,1)S(1)} %get-tuple-element.33), channel_id=1, source_target_pairs={{2,0},{3,1},{0,2},{1,3},{6,4},{7,5},{4,6},{5,7},{10,8},{11,9},{8,1... | collective-permute-start | bytes 491528 | tf_op jit(solution)/shard_map/ppermute | solution.py:37
  33.5 0.0 collective-permute-start.15
  33.5 0.0 copy-done.3
  33.6 1.0 %spread_basis.1 = (bf16[128,1536]{1,0:T(8,128)(2,1)S(1)}, bf16[16,128]{1,0:T(8,128)(2,1)S(1)}) custom-call(s32[12,32]{1,0:T(8,128)S(1)} %bitcast.19, bf16[192,128]{1,0:T(8,128)(2,1)S(1)} %bitcast.20, bf16[640,128]{1,0:T(8,128)(2,1)S(1)} %get-tuple-element.29.refs_2_.refs_15_), custom_call_target="tpu_custom_call" | custom-call | flops 1000 | bytes 1000 | tf_op jit(solution)/shard_map/spread_basis/pallas_call | solution.py:626
  34.6 0.0 collective-permute-done.11.refs_14_
  34.6 0.0 copy-done
  34.6 1.9 %gram_early.1.refs_2_.refs_5_ = bf16[1536,1536]{1,0:T(8,128)(2,1)S(1)} custom-call(s32[83]{0:T(128)S(1)} %get-tuple-element.32.refs_0_, bf16[1536,128]{1,0:T(8,128)(2,1)S(1)} %bitcast.14, bf16[1536,128]{1,0:T(8,128)(2,1)S(1)} %collective-permute-done.4.refs_5_.refs_2_, bf16[1536,128]{1,0:T(8,128)(2,1)S(1)} %collective-permute-done.2.refs_0_.refs_3_, ...), custom_call_target="tpu_custom_call" | custom-call | flops 1000 | bytes 1000 | tf_op jit(solution)/shard_map/gram_early/pallas_call | solution.py:641
  36.5 1.5 %collective-permute-done.15.refs_3_.refs_2_ = bf16[96,128]{1,0:T(8,128)(2,1)S(1)} collective-permute-done((bf16[96,128]{1,0:T(8,128)(2,1)S(1)}, bf16[96,128]{1,0:T(8,128)(2,1)S(1)}, u32[]{:S(2)}, u32[]{:S(2)}) %collective-permute-start.15) | collective-permute-done | bytes 24608 | tf_op jit(solution)/shard_map/ppermute | solution.py:37
  38.0 0.0 collective-permute-done.12.refs_0_.refs_6_
  38.0 0.5 collective-permute-done.13.refs_1_.refs_7_
  38.6 0.2 collective-permute-start.16
  38.7 1.5 %collective-permute-done.16.refs_9_ = bf16[1280,128]{1,0:T(8,128)(2,1)S(1)} collective-permute-done((bf16[1280,128]{1,0:T(8,128)(2,1)S(1)}, bf16[1280,128]{1,0:T(8,128)(2,1)S(1)}, u32[]{:S(2)}, u32[]{:S(2)}) %collective-permute-start.16) | collective-permute-done | bytes 327712 | tf_op jit(solution)/shard_map/ppermute | solution.py:37
  40.2 0.0 collective-permute-done.14.refs_8_.refs_1_
  40.3 4.9 %square_cube_coefficients.1 = (bf16[12,128,128]{2,1,0:T(8,128)(2,1)}, f32[8,128]{1,0:T(8,128)S(1)}) custom-call(s32[83]{0:T(128)S(1)} %get-tuple-element.23.refs_0_, s32[14]{0:T(128)S(1)} %get-tuple-element.24.refs_6_.refs_1_, bf16[16,128]{1,0:T(8,128)(2,1)S(1)} %get-tuple-element.30.refs_4_.refs_2_, bf16[128,1536]{1,0:T(8,128)(2,1)S(1)} %get-tuple-element.31.refs_3_, ...), custom_call_target="tpu_custom_call" | custom-call | flops 1300000000 | bytes 8000000 | tf_op jit(solution)/shard_map/square_cube_coefficients/pallas_call | solution.py:678
  45.1 0.1 collective-permute-start.17
  45.3 1.5 %collective-permute-start.18 = (f32[8,128]{1,0:T(8,128)S(1)}, f32[8,128]{1,0:T(8,128)S(1)}, u32[]{:S(2)}, u32[]{:S(2)}) collective-permute-start(f32[8,128]{1,0:T(8,128)S(1)} %get-tuple-element.37), channel_id=1, source_target_pairs={{3,0},{2,1},{1,2},{0,3},{7,4},{6,5},{5,6},{4,7},{11,8},{10,9},{9,1... | collective-permute-start | bytes 12296 | tf_op jit(solution)/shard_map/ppermute | solution.py:37
  46.8 0.0 collective-permute-done.17
  46.8 1.5 %collective-permute-done.18 = f32[8,128]{1,0:T(8,128)S(1)} collective-permute-done((f32[8,128]{1,0:T(8,128)S(1)}, f32[8,128]{1,0:T(8,128)S(1)}, u32[]{:S(2)}, u32[]{:S(2)}) %collective-permute-start.18) | collective-permute-done | bytes 4128 | tf_op jit(solution)/shard_map/ppermute | solution.py:37
  48.3 0.1 slice.11
  48.4 0.1 slice.10
  48.5 0.1 pad_maximum_fusion.1
  48.5 1.5 %collective-permute-start.19 = (f32[8,128]{1,0:T(8,128)S(1)}, f32[8,128]{1,0:T(8,128)S(1)}, u32[]{:S(2)}, u32[]{:S(2)}) collective-permute-start(f32[8,128]{1,0:T(8,128)S(1)} %pad_maximum_fusion.1), channel_id=1, source_target_pairs={{16,0},{0,16},{17,1},{1,17},{18,2},{2,18},{19,3},{3,19},{20,4},{4,... | collective-permute-start | bytes 12296 | tf_op jit(solution)/shard_map/ppermute | solution.py:26
  50.0 2.1 %collective-permute-done.19 = f32[8,128]{1,0:T(8,128)S(1)} collective-permute-done((f32[8,128]{1,0:T(8,128)S(1)}, f32[8,128]{1,0:T(8,128)S(1)}, u32[]{:S(2)}, u32[]{:S(2)}) %collective-permute-start.19) | collective-permute-done | bytes 4128 | tf_op jit(solution)/shard_map/ppermute | solution.py:26
  52.2 0.1 pad_maximum_fusion.refs_0_
  52.2 2.7 %collective-permute-start.20 = (f32[16,128]{1,0:T(8,128)S(1)}, f32[16,128]{1,0:T(8,128)S(1)}, u32[]{:S(2)}, u32[]{:S(2)}) collective-permute-start(f32[16,128]{1,0:T(8,128)S(1)} %pad_maximum_fusion.refs_0_), channel_id=1, source_target_pairs={{12,0},{8,4},{4,8},{0,12},{13,1},{9,5},{5,9},{1,13},{14,2},{10,6},... | collective-permute-start | bytes 24584 | tf_op jit(solution)/shard_map/ppermute | solution.py:32
  55.0 0.0 collective-permute-start.21
  55.0 2.8 %profiles.1 = (bf16[6,6,256,128]{3,2,1,0:T(8,128)(2,1)S(1)}, bf16[6,6,128,128]{3,2,1,0:T(8,128)(2,1)S(1)}) custom-call(bf16[96,128]{1,0:T(8,128)(2,1)S(1)} %get-tuple-element.35.refs_0_, bf16[2960,128]{1,0:T(8,128)(2,1)S(1)} %collective-permute-done.14.refs_8_.refs_1_, bf16[96,128]{1,0:T(8,128)(2,1)S(1)} %collective-permute-done.15.refs_3_.refs_2_), custom_call_target="tpu_custom_call" | custom-call | flops 1000 | bytes 1000 | tf_op jit(solution)/shard_map/profiles/pallas_call | solution.py:660
  57.8 0.0 collective-permute-done.20.refs_1_
  57.9 0.8 %collective-permute-done.21.refs_2_ = f32[16,128]{1,0:T(8,128)S(1)} collective-permute-done((f32[16,128]{1,0:T(8,128)S(1)}, f32[16,128]{1,0:T(8,128)S(1)}, u32[]{:S(2)}, u32[]{:S(2)}) %collective-permute-start.21) | collective-permute-done | bytes 8224 | tf_op jit(solution)/shard_map/ppermute | solution.py:32
  58.6 1.5 %density.1 = f32[256,128]{1,0:T(8,128)} custom-call(f32[16,128]{1,0:T(8,128)S(1)} %pad_maximum_fusion.refs_0_, f32[16,128]{1,0:T(8,128)S(1)} %collective-permute-done.20.refs_1_, f32[16,128]{1,0:T(8,128)S(1)} %collective-permute-done.21.refs_2_, bf16[6,6,256,128]{3,2,1,0:T(8,128)(2,1)S(1)} %get-tuple-element.38.refs_3_, bf16[4608,128]{1,0:T(8,128)(2,1)S(1)} %bitcast.16), custom_call_target="tpu_custom_call" | custom-call | flops 310000000 | bytes 4000000 | tf_op jit(solution)/shard_map/density/pallas_call | solution.py:715
  (8 shorter events, 0.1 us)
Async XLA Ops:
  0.6 12.4 %collective-permute-start.2 = (bf16[1536,128]{1,0:T(8,128)(2,1)}, bf16[1536,128]{1,0:T(8,128)(2,1)S(1)}, u32[]{:S(2)}, u32[]{:S(2)}) collective-permute-start(bf16[1536,128]{1,0:T(8,128)(2,1)} %bitcast.10), channel_id=1, source_target_pairs={{2,0},{3,1},{0,2},{1,3},{6,4},{7,5},{4,6},{5,7},{10,8},{11,9},{8,1... | collective-permute-start | bytes 1179656 | tf_op jit(solution)/shard_map/ppermute | solution.py:37
  3.7 10.8 %collective-permute-start.3 = (bf16[1536,128]{1,0:T(8,128)(2,1)}, bf16[1536,128]{1,0:T(8,128)(2,1)S(1)}, u32[]{:S(2)}, u32[]{:S(2)}) collective-permute-start(bf16[1536,128]{1,0:T(8,128)(2,1)} %bitcast.11), channel_id=1, source_target_pairs={{16,0},{0,16},{17,1},{1,17},{18,2},{2,18},{19,3},{3,19},{20,4},{4,... | collective-permute-start | bytes 1179656 | tf_op jit(solution)/shard_map/ppermute | solution.py:26
  5.2 15.0 %collective-permute-start.4 = (bf16[1536,128]{1,0:T(8,128)(2,1)}, bf16[1536,128]{1,0:T(8,128)(2,1)S(1)}, u32[]{:S(2)}, u32[]{:S(2)}) collective-permute-start(bf16[1536,128]{1,0:T(8,128)(2,1)} %bitcast.12), channel_id=1, source_target_pairs={{1,0},{0,1},{3,2},{2,3},{5,4},{4,5},{7,6},{6,7},{9,8},{8,9},{11,10... | collective-permute-start | bytes 1179656 | tf_op jit(solution)/shard_map/ppermute | solution.py:37
  7.6 9.8 %collective-permute-start = (bf16[656,128]{1,0:T(8,128)(2,1)}, bf16[656,128]{1,0:T(8,128)(2,1)S(1)}, u32[]{:S(2)}, u32[]{:S(2)}) collective-permute-start(bf16[656,128]{1,0:T(8,128)(2,1)} %pick_column_blocks.1.refs_2_), channel_id=1, source_target_pairs={{12,0},{8,4},{4,8},{0,12},{13,1},{9,5},{5,9},{1,13},{14,2},{10,6},... | collective-permute-start | bytes 503816 | tf_op jit(solution)/shard_map/ppermute | solution.py:32
  11.3 8.9 %collective-permute-start.1 = (bf16[656,128]{1,0:T(8,128)(2,1)}, bf16[656,128]{1,0:T(8,128)(2,1)S(1)}, u32[]{:S(2)}, u32[]{:S(2)}) collective-permute-start(bf16[656,128]{1,0:T(8,128)(2,1)} %pick_column_blocks.1.refs_2_), channel_id=1, source_target_pairs={{4,0},{0,4},{12,8},{8,12},{5,1},{1,5},{13,9},{9,13},{6,2},{2,6},{1... | collective-permute-start | bytes 503816 | tf_op jit(solution)/shard_map/ppermute | solution.py:32
  14.4 0.9 %copy-start.1 = (bf16[656,128]{1,0:T(8,128)(2,1)S(1)}, bf16[656,128]{1,0:T(8,128)(2,1)}, u32[]{:S(2)}) copy-start(bf16[656,128]{1,0:T(8,128)(2,1)} %pick_column_blocks.1.refs_2_) | copy-start | bytes 503812
  15.4 6.0 %collective-permute-start.9 = (bf16[640,128]{1,0:T(8,128)(2,1)S(1)}, bf16[640,128]{1,0:T(8,128)(2,1)S(1)}, u32[]{:S(2)}, u32[]{:S(2)}) collective-permute-start(bf16[640,128]{1,0:T(8,128)(2,1)S(1)} %get-tuple-element.27), channel_id=1, source_target_pairs={{16,0},{0,16},{17,1},{1,17},{18,2},{2,18},{19,3},{3,19},{20,4},{4,... | collective-permute-start | bytes 491528 | tf_op jit(solution)/shard_map/ppermute | solution.py:26
  16.9 5.3 %collective-permute-start.10 = (bf16[640,128]{1,0:T(8,128)(2,1)S(1)}, bf16[640,128]{1,0:T(8,128)(2,1)S(1)}, u32[]{:S(2)}, u32[]{:S(2)}) collective-permute-start(bf16[640,128]{1,0:T(8,128)(2,1)S(1)} %get-tuple-element.28), channel_id=1, source_target_pairs={{2,0},{3,1},{0,2},{1,3},{6,4},{7,5},{4,6},{5,7},{10,8},{11,9},{8,1... | collective-permute-start | bytes 491528 | tf_op jit(solution)/shard_map/ppermute | solution.py:37
  20.3 10.7 %collective-permute-start.5 = (bf16[1456,128]{1,0:T(8,128)(2,1)S(1)}, bf16[1456,128]{1,0:T(8,128)(2,1)S(1)}, u32[]{:S(2)}, u32[]{:S(2)}) collective-permute-start(bf16[1456,128]{1,0:T(8,128)(2,1)S(1)} %get-tuple-element.25), channel_id=1, source_target_pairs={{2,0},{3,1},{0,2},{1,3},{6,4},{7,5},{4,6},{5,7},{10,8},{11,9},{8,1... | collective-permute-start | bytes 1118216 | tf_op jit(solution)/shard_map/ppermute | solution.py:37
  20.9 1.6 %copy-start.2 = (s32[32,12]{0,1:T(8,128)S(1)}, s32[32,12]{0,1:T(8,128)}, u32[]{:S(2)}) copy-start(s32[32,12]{0,1:T(8,128)} %param.9) | copy-start | bytes 4612
  20.9 1.6 %copy-start.4 = (s32[32]{0:T(128)S(1)}, s32[32]{0:T(128)}, u32[]{:S(2)}) copy-start(s32[32]{0:T(128)} %refs_1_.3) | copy-start | bytes 388
  20.9 10.3 %collective-permute-start.6 = (bf16[1456,128]{1,0:T(8,128)(2,1)S(1)}, bf16[1456,128]{1,0:T(8,128)(2,1)S(1)}, u32[]{:S(2)}, u32[]{:S(2)}) collective-permute-start(bf16[1456,128]{1,0:T(8,128)(2,1)S(1)} %get-tuple-element.22.refs_2_), channel_id=1, source_target_pairs={{16,0},{0,16},{17,1},{1,17},{18,2},{2,18},{19,3},{3,19},{20,4},{4,... | collective-permute-start | bytes 1118216 | tf_op jit(solution)/shard_map/ppermute | solution.py:26
  21.4 9.8 %collective-permute-start.7 = (bf16[1536,128]{1,0:T(8,128)(2,1)S(1)}, bf16[1536,128]{1,0:T(8,128)(2,1)S(1)}, u32[]{:S(2)}, u32[]{:S(2)}) collective-permute-start(bf16[1536,128]{1,0:T(8,128)(2,1)S(1)} %collective-permute-done.2.refs_0_.refs_3_), channel_id=1, source_target_pairs={{1,0},{0,1},{3,2},{2,3},{5,4},{4,5},{7,6},{6,7},{9,8},{8,9},{11,10... | collective-permute-start | bytes 1179656 | tf_op jit(solution)/shard_map/ppermute | solution.py:37
  21.4 9.8 %collective-permute-start.8 = (bf16[1536,128]{1,0:T(8,128)(2,1)S(1)}, bf16[1536,128]{1,0:T(8,128)(2,1)S(1)}, u32[]{:S(2)}, u32[]{:S(2)}) collective-permute-start(bf16[1536,128]{1,0:T(8,128)(2,1)S(1)} %collective-permute-done.3.refs_1_.refs_4_.refs_7_), channel_id=1, source_target_pairs={{1,0},{0,1},{3,2},{2,3},{5,4},{4,5},{7,6},{6,7},{9,8},{8,9},{11,10... | collective-permute-start | bytes 1179656 | tf_op jit(solution)/shard_map/ppermute | solution.py:37
  22.3 11.2 %copy-start.3 = (bf16[32,6,128]{2,0,1:T(8,128)(2,1)S(1)}, bf16[32,6,128]{2,0,1:T(8,128)(2,1)}, u32[]{:S(2)}) copy-start(bf16[32,6,128]{2,0,1:T(8,128)(2,1)} %param.11) | copy-start | bytes 147460
  22.3 12.3 %copy-start = (bf16[1,12,128,128]{3,2,1,0:T(8,128)(2,1)S(1)}, bf16[1,12,128,128]{3,2,1,0:T(8,128)(2,1)}, u32[]{:S(2)}) copy-start(bf16[1,12,128,128]{3,2,1,0:T(8,128)(2,1)} %param.8) | copy-start | bytes 1179652
  22.3 12.2 %collective-permute-start.11 = (bf16[2560,128]{1,0:T(8,128)(2,1)S(1)}, bf16[2560,128]{1,0:T(8,128)(2,1)S(1)}, u32[]{:S(2)}, u32[]{:S(2)}) collective-permute-start(bf16[2560,128]{1,0:T(8,128)(2,1)S(1)} %pack_two_mate.1.refs_5_), channel_id=1, source_target_pairs={{1,0},{0,1},{3,2},{2,3},{5,4},{4,5},{7,6},{6,7},{9,8},{8,9},{11,10... | collective-permute-start | bytes 1966088 | tf_op jit(solution)/shard_map/ppermute | solution.py:37
  31.3 8.9 %collective-permute-start.14 = (bf16[2960,128]{1,0:T(8,128)(2,1)S(1)}, bf16[2960,128]{1,0:T(8,128)(2,1)S(1)}, u32[]{:S(2)}, u32[]{:S(2)}) collective-permute-start(bf16[2960,128]{1,0:T(8,128)(2,1)S(1)} %get-tuple-element.34), channel_id=1, source_target_pairs={{1,0},{0,1},{3,2},{2,3},{5,4},{4,5},{7,6},{6,7},{9,8},{8,9},{11,10... | collective-permute-start | bytes 2273288 | tf_op jit(solution)/shard_map/ppermute | solution.py:37
  31.4 6.6 %collective-permute-start.12 = (bf16[640,128]{1,0:T(8,128)(2,1)S(1)}, bf16[640,128]{1,0:T(8,128)(2,1)S(1)}, u32[]{:S(2)}, u32[]{:S(2)}) collective-permute-start(bf16[640,128]{1,0:T(8,128)(2,1)S(1)} %get-tuple-element.29.refs_2_.refs_15_), channel_id=1, source_target_pairs={{16,0},{0,16},{17,1},{1,17},{18,2},{2,18},{19,3},{3,19},{20,4},{4,... | collective-permute-start | bytes 491528 | tf_op jit(solution)/shard_map/ppermute | solution.py:26
  32.0 6.5 %collective-permute-start.13 = (bf16[640,128]{1,0:T(8,128)(2,1)S(1)}, bf16[640,128]{1,0:T(8,128)(2,1)S(1)}, u32[]{:S(2)}, u32[]{:S(2)}) collective-permute-start(bf16[640,128]{1,0:T(8,128)(2,1)S(1)} %get-tuple-element.33), channel_id=1, source_target_pairs={{2,0},{3,1},{0,2},{1,3},{6,4},{7,5},{4,6},{5,7},{10,8},{11,9},{8,1... | collective-permute-start | bytes 491528 | tf_op jit(solution)/shard_map/ppermute | solution.py:37
  33.5 4.5 %collective-permute-start.15 = (bf16[96,128]{1,0:T(8,128)(2,1)S(1)}, bf16[96,128]{1,0:T(8,128)(2,1)S(1)}, u32[]{:S(2)}, u32[]{:S(2)}) collective-permute-start(bf16[96,128]{1,0:T(8,128)(2,1)S(1)} %get-tuple-element.35.refs_0_), channel_id=1, source_target_pairs={{3,0},{2,1},{1,2},{0,3},{7,4},{6,5},{5,6},{4,7},{11,8},{10,9},{9,1... | collective-permute-start | bytes 73736 | tf_op jit(solution)/shard_map/ppermute | solution.py:37
  38.6 1.7 %collective-permute-start.16 = (bf16[1280,128]{1,0:T(8,128)(2,1)S(1)}, bf16[1280,128]{1,0:T(8,128)(2,1)S(1)}, u32[]{:S(2)}, u32[]{:S(2)}) collective-permute-start(bf16[1280,128]{1,0:T(8,128)(2,1)S(1)} %pack_four.1), channel_id=1, source_target_pairs={{1,0},{0,1},{3,2},{2,3},{5,4},{4,5},{7,6},{6,7},{9,8},{8,9},{11,10... | collective-permute-start | bytes 983048 | tf_op jit(solution)/shard_map/ppermute | solution.py:37
  45.1 1.6 %collective-permute-start.17 = (f32[8,128]{1,0:T(8,128)S(1)}, f32[8,128]{1,0:T(8,128)S(1)}, u32[]{:S(2)}, u32[]{:S(2)}) collective-permute-start(f32[8,128]{1,0:T(8,128)S(1)} %get-tuple-element.37), channel_id=1, source_target_pairs={{1,0},{0,1},{3,2},{2,3},{5,4},{4,5},{7,6},{6,7},{9,8},{8,9},{11,10... | collective-permute-start | bytes 12296 | tf_op jit(solution)/shard_map/ppermute | solution.py:37
  45.3 3.0 %collective-permute-start.18 = (f32[8,128]{1,0:T(8,128)S(1)}, f32[8,128]{1,0:T(8,128)S(1)}, u32[]{:S(2)}, u32[]{:S(2)}) collective-permute-start(f32[8,128]{1,0:T(8,128)S(1)} %get-tuple-element.37), channel_id=1, source_target_pairs={{3,0},{2,1},{1,2},{0,3},{7,4},{6,5},{5,6},{4,7},{11,8},{10,9},{9,1... | collective-permute-start | bytes 12296 | tf_op jit(solution)/shard_map/ppermute | solution.py:37
  48.5 3.6 %collective-permute-start.19 = (f32[8,128]{1,0:T(8,128)S(1)}, f32[8,128]{1,0:T(8,128)S(1)}, u32[]{:S(2)}, u32[]{:S(2)}) collective-permute-start(f32[8,128]{1,0:T(8,128)S(1)} %pad_maximum_fusion.1), channel_id=1, source_target_pairs={{16,0},{0,16},{17,1},{1,17},{18,2},{2,18},{19,3},{3,19},{20,4},{4,... | collective-permute-start | bytes 12296 | tf_op jit(solution)/shard_map/ppermute | solution.py:26
  52.2 5.6 %collective-permute-start.20 = (f32[16,128]{1,0:T(8,128)S(1)}, f32[16,128]{1,0:T(8,128)S(1)}, u32[]{:S(2)}, u32[]{:S(2)}) collective-permute-start(f32[16,128]{1,0:T(8,128)S(1)} %pad_maximum_fusion.refs_0_), channel_id=1, source_target_pairs={{12,0},{8,4},{4,8},{0,12},{13,1},{9,5},{5,9},{1,13},{14,2},{10,6},... | collective-permute-start | bytes 24584 | tf_op jit(solution)/shard_map/ppermute | solution.py:32
  55.0 3.7 %collective-permute-start.21 = (f32[16,128]{1,0:T(8,128)S(1)}, f32[16,128]{1,0:T(8,128)S(1)}, u32[]{:S(2)}, u32[]{:S(2)}) collective-permute-start(f32[16,128]{1,0:T(8,128)S(1)} %pad_maximum_fusion.refs_0_), channel_id=1, source_target_pairs={{4,0},{0,4},{12,8},{8,12},{5,1},{1,5},{13,9},{9,13},{6,2},{2,6},{1... | collective-permute-start | bytes 24584 | tf_op jit(solution)/shard_map/ppermute | solution.py:32

commit v14 on v13

--- a/solution.py
+++ b/solution.py
@@ -130,8 +130,8 @@
 
 
 def spread_kernel(axes, *refs):
-    basis_ref = refs[1]
-    spread_ref, own_basis_ref, neighbors_ref, loads = refs[-4:]
+    basis_ref, info_ref, sign_ref = refs[1:4]
+    spread_ref, own_basis_ref, own_ref, seen_ref, neighbors_ref, loads = refs[-6:]
     at = Places(*axes)
     load(refs[:1], (neighbors_ref,), loads)
     slots, atoms = neighbors_ref.shape
@@ -148,7 +148,16 @@
 
     for w, (atom, rank) in enumerate(own_ranks(at, neighbors_ref)):
         spread_ref[:, w * LANES : (w + 1) * LANES] = rows_of(hot(LANES, atom, rank * SHELLS))
-    own_basis_ref[...] = rows_of(hot(16, at.me, 0))
+    own_basis = rows_of(hot(16, at.me, 0))
+    own_basis_ref[...] = own_basis
+    size = sign_ref.shape[1]
+    rows = lax.broadcasted_iota(jnp.int32, (size, size), 0)
+    lanes = lax.broadcasted_iota(jnp.int32, (size, size), 1)
+    for w in range(slots):
+        kept = (rows < info_ref[slots]) & (lanes < info_ref[w])
+        block = jnp.where(kept, sign_ref[w].astype(jnp.float32), 0.0).astype(own_ref.dtype)
+        own_ref[:, w * size : (w + 1) * size] = block
+        seen_ref[:, w * size : (w + 1) * size] = jnp.dot(own_basis, block, preferred_element_type=jnp.float32)
 
 
 def prepare_kernel(axes, count, layout, late_from, *refs):
@@ -287,59 +296,59 @@
 
 
 def step_kernel(pieces, *refs):
-    table_ref, info_ref, basis_ref, spread_ref, sign_ref, early_ref = refs[:6]
-    piece_refs = refs[6 : 6 + pieces]
-    next_ref, coef_ref, pool, gram, own, square = refs[-6:]
-    slots, size = sign_ref.shape[0], sign_ref.shape[1]
+    table_ref, info_ref, basis_ref, spread_ref, own, seen_ref, early_ref = refs[:7]
+    piece_refs = refs[7 : 7 + pieces]
+    next_ref, coef_ref, pool, gram, square = refs[-5:]
+    slots, size = next_ref.shape[0], next_ref.shape[1]
+    shells = basis_ref.shape[0]
     fill(piece_refs, pool)
     for v in range(slots):
         gram[v * size : (v + 1) * size] = early_ref[v * size : (v + 1) * size]
-    rows = lax.broadcasted_iota(jnp.int32, (size, size), 0)
-    lanes = lax.broadcasted_iota(jnp.int32, (size, size), 1)
+    place_pairs(table_ref, pool, gram, size)
     own_size = info_ref[slots]
     self_slot = info_ref[slots + 1]
-    for w in range(slots):
-        kept = (rows < own_size) & (lanes < info_ref[w])
-        block = jnp.where(kept, sign_ref[w].astype(jnp.float32), 0.0)
-        own[:, w * size : (w + 1) * size] = block.astype(own.dtype)
-    place_pairs(table_ref, pool, gram, size)
     wide = 2 * size
-    wide_lanes = lax.broadcasted_iota(jnp.int32, (size, wide), 1)
-    wide_rows = lax.broadcasted_iota(jnp.int32, (size, wide), 0)
-
-    def column_kept(n):
-        first = info_ref[2 * n]
-        second = info_ref[2 * n + 1]
-        return (wide_lanes < first) | ((wide_lanes >= size) & (wide_lanes < size + second))
+
+    def column_kept(n, rows):
+        lanes = lax.broadcasted_iota(jnp.int32, (rows, wide), 1)
+        return (lanes < info_ref[2 * n]) | ((lanes >= size) & (lanes < size + info_ref[2 * n + 1]))
 
     for n in range(slots // 2):
-        part = jnp.dot(own[...], gram[:, n * wide : (n + 1) * wide], preferred_element_type=jnp.float32)
-        square[:, n * wide : (n + 1) * wide] = jnp.where(column_kept(n), part, 0.0).astype(square.dtype)
-    basis = jnp.concatenate([basis_ref[...], basis_ref[...]], axis=1)
-    coef = jnp.zeros((2 * basis_ref.shape[0], LANES), jnp.float32)
+        span = slice(n * wide, (n + 1) * wide)
+        part = jnp.dot(own[...], gram[:, span], preferred_element_type=jnp.float32)
+        part = jnp.where(column_kept(n, size), part, 0.0).astype(square.dtype)
+        square[:size, span] = part
+        seen = jnp.dot(basis_ref[...], part, preferred_element_type=jnp.float32)
+        high = seen.astype(square.dtype)
+        square[size : size + shells, span] = high
+        square[size + shells :, span] = (seen - high.astype(jnp.float32)).astype(square.dtype)
+    coef = jnp.zeros((2 * shells, LANES), jnp.float32)
     across = (((1,), (1,)), ((), ()))
+    wide_lanes = lax.broadcasted_iota(jnp.int32, (shells, wide), 1)
+    basis = basis_ref[...].astype(jnp.float32)
+    basis = jnp.concatenate([basis, basis], axis=1)
     for n in range(slots // 2):
-        part = jnp.dot(square[...], gram[:, n * wide : (n + 1) * wide], preferred_element_type=jnp.float32)
-        cube = jnp.where(column_kept(n), part, 0.0)
-        full = 1.5 * own[:, n * wide : (n + 1) * wide].astype(jnp.float32) - 0.5 * cube
+        span = slice(n * wide, (n + 1) * wide)
+        part = jnp.dot(square[...], gram[:, span], preferred_element_type=jnp.float32)
+        cube = jnp.where(column_kept(n, size), part[:size], 0.0)
+        full = 1.5 * own[:, span].astype(jnp.float32) - 0.5 * cube
         next_ref[2 * n] = full[:, :size].astype(next_ref.dtype)
         next_ref[2 * n + 1] = full[:, size:].astype(next_ref.dtype)
-        shift = (self_slot - 2 * n) * size
+        seen = part[size : size + shells] + part[size + shells :]
+        seen = jnp.where(column_kept(n, shells), seen, 0.0)
+        first = (self_slot - 2 * n) * size
         is_self = (self_slot >= 2 * n) & (self_slot < 2 * n + 2)
-        diag = (wide_lanes == wide_rows + shift) & (wide_rows < own_size) & is_self
-        dmat = 0.5 * (jnp.where(diag, 1.0, 0.0) - full)
-        high = dmat.astype(jnp.bfloat16)
-        low = (dmat - high.astype(jnp.float32)).astype(jnp.bfloat16)
-        half = jnp.dot(basis, jnp.concatenate([high, low], axis=0), preferred_element_type=jnp.float32)
+        diag = (wide_lanes >= first) & (wide_lanes < first + own_size) & is_self
+        half = 0.5 * (jnp.where(diag, basis, 0.0) - (1.5 * seen_ref[:, span] - 0.5 * seen))
         half_high = half.astype(jnp.bfloat16)
         half_low = (half - half_high.astype(jnp.float32)).astype(jnp.bfloat16)
         coef = coef + lax.dot_general(
             jnp.concatenate([half_high, half_low], axis=0),
-            spread_ref[:, n * wide : (n + 1) * wide],
+            spread_ref[:, span],
             across,
             preferred_element_type=jnp.float32,
         )
-    coef = coef[: basis_ref.shape[0]] + coef[basis_ref.shape[0] :]
+    coef = coef[:shells] + coef[shells:]
     coef_ref[...] = coef[: coef_ref.shape[0]]
 
 
@@ -623,19 +632,21 @@
     note("three m", from_layer(three_m, 1), contents["three m"])
     third_geos = from_layer(geos, 3)
 
-    spread, own_basis = pl.pallas_call(
+    spread, own_basis, own_kept, seen = pl.pallas_call(
         functools.partial(spread_kernel, axes),
         out_shape=(
             jax.ShapeDtypeStruct((LANES, full), jnp.bfloat16),
             jax.ShapeDtypeStruct((16, size), jnp.bfloat16),
+            jax.ShapeDtypeStruct((size, full), jnp.bfloat16),
+            jax.ShapeDtypeStruct((16, full), jnp.float32),
         ),
-        in_specs=[HBM, VMEM, ANY],
-        out_specs=(VMEM, VMEM),
+        in_specs=[HBM, VMEM, SMEM, VMEM, ANY],
+        out_specs=(VMEM, VMEM, VMEM, VMEM),
         scratch_shapes=[pltpu.SMEM((slots, atoms), jnp.int32), pltpu.SemaphoreType.DMA((1,))],
         compiler_params=pltpu.CompilerParams(vmem_limit_bytes=(2 << 20) + atoms * 16384),
         cost_estimate=pl.CostEstimate(flops=1000, bytes_accessed=1000, transcendentals=0),
         name="spread_basis",
-    )(listings, basis_proj.transpose(1, 0, 2).reshape(SHELLS * atoms, size), three_x)
+    )(listings, basis_proj.transpose(1, 0, 2).reshape(SHELLS * atoms, size), info, own, three_x)
 
     early_values = [buffers[name] for name in early_order]
     gram = pl.pallas_call(
@@ -681,18 +692,17 @@
             jax.ShapeDtypeStruct((slots, size, size), jnp.bfloat16),
             jax.ShapeDtypeStruct((8, LANES), jnp.float32),
         ),
-        in_specs=[SMEM, SMEM, VMEM, VMEM, VMEM, VMEM] + [VMEM] * len(late_values),
+        in_specs=[SMEM, SMEM] + [VMEM] * (5 + len(late_values)),
         out_specs=(VMEM, VMEM),
         scratch_shapes=[
             pltpu.VMEM((total - late_from, LANES), jnp.bfloat16),
             pltpu.VMEM((full, full), jnp.bfloat16),
-            pltpu.VMEM((size, full), jnp.bfloat16),
-            pltpu.VMEM((size, full), jnp.bfloat16),
+            pltpu.VMEM((size + 32, full), jnp.bfloat16),
         ],
         compiler_params=pltpu.CompilerParams(vmem_limit_bytes=(15 << 20) + 2 * (total - late_from) * LANES * 2),
         cost_estimate=pl.CostEstimate(flops=1_300_000_000, bytes_accessed=8_000_000, transcendentals=0),
         name="square_cube_coefficients",
-    )(late_table, info, own_basis, spread, own, gram, *late_values)
+    )(late_table, info, own_basis, spread, own_kept, seen, gram, *late_values)
 
     mate_coef = from_layer(coef, 1)
     third_coef = from_layer(coef, 3)

time: 60.4 us -> 60.8 us (level)
  Pallas kernels: 18.9 us -> 20.7 us
  starting transfers between devices: 20.3 us -> 18.7 us
    ppermute x5, waiting for transfers between devices: 3.79 us -> 5.57 us  [from_offset(): lax.ppermute(x, axis, [((i + step) % count, i) for i in range(count)])]
    ppermute x13, starting transfers between devices: 8.13 us -> 6.74 us  [from_layer(): return lax.ppermute(x, 'layer', [(i ^ flip, i) for i in range(count)])]
    ppermute x13, waiting for transfers between devices: 11.6 us -> 10.5 us  [from_layer(): return lax.ppermute(x, 'layer', [(i ^ flip, i) for i in range(count)])]
    pallas_call x1, Pallas kernels: 1.01 us -> 1.76 us  [local(): pl.pallas_call(functools.partial(spread_kernel, axes), out_shape=(jax.Sha...]
    ppermute x5, starting transfers between devices: 5.69 us -> 4.96 us  [from_offset(): lax.ppermute(x, axis, [((i + step) % count, i) for i in range(count)])]
    ppermute x4, waiting for transfers between devices: 3.53 us -> 2.88 us  [from_column(): lax.ppermute(x, 'col', [((i + step[i]) % count, i) for i in range(count)])]
  transfers between devices with their start and end apart: 22 -> 22, of which waited for: 12 -> 11; matrix products, arithmetic and copies ran while one was open for 0% -> 0% of each run, Pallas kernels for 21% -> 23%
where the time goes in v14:
time: 60.8 us; the launch traced here: 60.5 us
  Pallas kernels  20.7 us (34%)
  waiting for transfers between devices  19 us (31%)
  starting transfers between devices  18.7 us (31%)
  local copies, waits for them, and re-layouts  1.08 us (2%)
  between operations  0.8 us (1%)
    ppermute x13, waiting for transfers between devices, from_layer(): return lax.ppermute(x, 'layer', [(i ^ flip, i) for i in range(count)])  10.5 us
    ppermute x4, starting transfers between devices, from_column(): lax.ppermute(x, 'col', [((i + step[i]) % count, i) for i in range(count)])  6.99 us
    ppermute x13, starting transfers between devices, from_layer(): return lax.ppermute(x, 'layer', [(i ^ flip, i) for i in range(count)])  6.74 us
    ppermute x5, waiting for transfers between devices, from_offset(): lax.ppermute(x, axis, [((i + step) % count, i) for i in range(count)])  5.57 us
    pallas_call x1, Pallas kernels, local(): pl.pallas_call(functools.partial(step_kernel, len(late_values)), out_shap...  5.42 us
    ppermute x5, starting transfers between devices, from_offset(): lax.ppermute(x, axis, [((i + step) % count, i) for i in range(count)])  4.96 us
    pallas_call x1, Pallas kernels, local(): pl.pallas_call(functools.partial(prepare_kernel, axes, count, tuple(layou...  4.23 us
    ppermute x4, waiting for transfers between devices, from_column(): lax.ppermute(x, 'col', [((i + step[i]) % count, i) for i in range(count)])  2.88 us
  transfers between devices with their start and end apart: 22, of which 11 were waited for; matrix products, arithmetic and copies ran while one was open for 0% of the time, Pallas kernels for 23%

profile of v14, /device:TPU:0, one launch (start us, length us, event | category | flops | bytes accessed | tf_op | source)
XLA Modules:
  0.0 60.5 jit_solution(18335778878382270456)
XLA Ops:
  0.6 3.0 %collective-permute-start.3 = (bf16[1536,128]{1,0:T(8,128)(2,1)}, bf16[1536,128]{1,0:T(8,128)(2,1)S(1)}, u32[]{:S(2)}, u32[]{:S(2)}) collective-permute-start(bf16[1536,128]{1,0:T(8,128)(2,1)} %bitcast.10), channel_id=1, source_target_pairs={{16,0},{0,16},{17,1},{1,17},{18,2},{2,18},{19,3},{3,19},{20,4},{4,... | collective-permute-start | bytes 1179656 | tf_op jit(solution)/shard_map/ppermute | solution.py:26
  3.6 1.5 %collective-permute-start.2 = (bf16[1536,128]{1,0:T(8,128)(2,1)}, bf16[1536,128]{1,0:T(8,128)(2,1)S(1)}, u32[]{:S(2)}, u32[]{:S(2)}) collective-permute-start(bf16[1536,128]{1,0:T(8,128)(2,1)} %bitcast.11), channel_id=1, source_target_pairs={{2,0},{3,1},{0,2},{1,3},{6,4},{7,5},{4,6},{5,7},{10,8},{11,9},{8,1... | collective-permute-start | bytes 1179656 | tf_op jit(solution)/shard_map/ppermute | solution.py:37
  5.2 0.0 collective-permute-start.4
  5.2 2.5 %pick_column_blocks.1.refs_2_ = bf16[656,128]{1,0:T(8,128)(2,1)} custom-call(s32[12,32]{1,0:T(8,128)} %bitcast.17, s32[1,12]{1,0:T(1,128)} %refs_1_.2, s32[32]{0:T(128)} %refs_2_.1, s32[32]{0:T(128)} %refs_3_.1, s32[32]{0:T(128)} %refs_4_.1, bf16[12,128,128]{2,1,0:T(8,128)(2,1)} %bitcast.13), custom_call_target="tpu_custom_call" | custom-call | tf_op jit(solution)/shard_map/pick_column_blocks/pallas_call | solution.py:456
  7.7 1.6 %collective-permute-start.1 = (bf16[656,128]{1,0:T(8,128)(2,1)}, bf16[656,128]{1,0:T(8,128)(2,1)S(1)}, u32[]{:S(2)}, u32[]{:S(2)}) collective-permute-start(bf16[656,128]{1,0:T(8,128)(2,1)} %pick_column_blocks.1.refs_2_), channel_id=1, source_target_pairs={{4,0},{0,4},{12,8},{8,12},{5,1},{1,5},{13,9},{9,13},{6,2},{2,6},{1... | collective-permute-start | bytes 503816 | tf_op jit(solution)/shard_map/ppermute | solution.py:32
  9.3 2.5 %collective-permute-start = (bf16[656,128]{1,0:T(8,128)(2,1)}, bf16[656,128]{1,0:T(8,128)(2,1)S(1)}, u32[]{:S(2)}, u32[]{:S(2)}) collective-permute-start(bf16[656,128]{1,0:T(8,128)(2,1)} %pick_column_blocks.1.refs_2_), channel_id=1, source_target_pairs={{12,0},{8,4},{4,8},{0,12},{13,1},{9,5},{5,9},{1,13},{14,2},{10,6},... | collective-permute-start | bytes 503816 | tf_op jit(solution)/shard_map/ppermute | solution.py:32
  11.8 1.2 %collective-permute-done.3.refs_1_.refs_4_.refs_7_ = bf16[1536,128]{1,0:T(8,128)(2,1)S(1)} collective-permute-done((bf16[1536,128]{1,0:T(8,128)(2,1)}, bf16[1536,128]{1,0:T(8,128)(2,1)S(1)}, u32[]{:S(2)}, u32[]{:S(2)}) %collective-permute-start.3) | collective-permute-done | bytes 393248 | tf_op jit(solution)/shard_map/ppermute | solution.py:26
  13.0 1.5 %collective-permute-done.2.refs_0_.refs_3_ = bf16[1536,128]{1,0:T(8,128)(2,1)S(1)} collective-permute-done((bf16[1536,128]{1,0:T(8,128)(2,1)}, bf16[1536,128]{1,0:T(8,128)(2,1)S(1)}, u32[]{:S(2)}, u32[]{:S(2)}) %collective-permute-start.2) | collective-permute-done | bytes 393248 | tf_op jit(solution)/shard_map/ppermute | solution.py:37
  14.4 0.9 %copy-done.1 = bf16[656,128]{1,0:T(8,128)(2,1)S(1)} copy-done((bf16[656,128]{1,0:T(8,128)(2,1)S(1)}, bf16[656,128]{1,0:T(8,128)(2,1)}, u32[]{:S(2)}) %copy-start.1) | copy-done | bytes 167960
  15.4 0.4 collective-permute-start.9
  15.8 1.7 %collective-permute-start.10 = (bf16[640,128]{1,0:T(8,128)(2,1)S(1)}, bf16[640,128]{1,0:T(8,128)(2,1)S(1)}, u32[]{:S(2)}, u32[]{:S(2)}) collective-permute-start(bf16[640,128]{1,0:T(8,128)(2,1)S(1)} %get-tuple-element.30), channel_id=1, source_target_pairs={{2,0},{3,1},{0,2},{1,3},{6,4},{7,5},{4,6},{5,7},{10,8},{11,9},{8,1... | collective-permute-start | bytes 491528 | tf_op jit(solution)/shard_map/ppermute | solution.py:37
  17.5 0.0 collective-permute-done.1.refs_1_.refs_2_.refs_4_
  17.5 2.9 %collective-permute-done.refs_0_.refs_3_.refs_5_ = bf16[656,128]{1,0:T(8,128)(2,1)S(1)} collective-permute-done((bf16[656,128]{1,0:T(8,128)(2,1)}, bf16[656,128]{1,0:T(8,128)(2,1)S(1)}, u32[]{:S(2)}, u32[]{:S(2)}) %collective-permute-start) | collective-permute-done | bytes 167968 | tf_op jit(solution)/shard_map/ppermute | solution.py:32
  20.4 0.0 collective-permute-done.4.refs_5_.refs_2_
  20.4 0.1 pack_two.1
  20.5 0.6 collective-permute-start.5
  21.0 0.5 collective-permute-start.6
  21.6 0.0 collective-permute-start.8
  21.6 0.0 collective-permute-done.9.refs_0_.refs_10_
  21.6 0.5 collective-permute-start.7
  22.1 0.0 collective-permute-done.10.refs_1_.refs_11_
  22.1 0.0 copy-start
  22.2 0.0 copy-start.3
  22.2 0.1 collective-permute-start.11
  22.2 0.0 copy-done.2
  22.3 0.0 copy-done.4
  22.3 4.2 %prepare.1 = (s32[83]{0:T(128)S(1)}, s32[83]{0:T(128)S(1)}, s32[14]{0:T(128)S(1)}) custom-call(s32[12,32]{1,0:T(8,128)S(1)} %bitcast.18, s32[32]{0:T(128)S(1)} %copy-done.4, bf16[1456,128]{1,0:T(8,128)(2,1)S(1)} %get-tuple-element.24.refs_2_), custom_call_target="tpu_custom_call" | custom-call | flops 1000 | bytes 1000 | tf_op jit(solution)/shard_map/prepare/pallas_call | solution.py:587
  26.5 4.3 %collective-permute-done.5.refs_0_.refs_13_ = bf16[1456,128]{1,0:T(8,128)(2,1)S(1)} collective-permute-done((bf16[1456,128]{1,0:T(8,128)(2,1)S(1)}, bf16[1456,128]{1,0:T(8,128)(2,1)S(1)}, u32[]{:S(2)}, u32[]{:S(2)}) %collective-permute-start.5) | collective-permute-done | bytes 372768 | tf_op jit(solution)/shard_map/ppermute | solution.py:37
  30.8 0.2 collective-permute-done.6.refs_2_.refs_12_
  31.0 0.0 collective-permute-done.8.refs_4_.refs_8_
  31.0 0.0 collective-permute-done.7.refs_3_.refs_9_
  31.0 0.1 pack_three.1
  31.1 0.1 collective-permute-start.14
  31.2 1.6 %collective-permute-start.13 = (bf16[640,128]{1,0:T(8,128)(2,1)S(1)}, bf16[640,128]{1,0:T(8,128)(2,1)S(1)}, u32[]{:S(2)}, u32[]{:S(2)}) collective-permute-start(bf16[640,128]{1,0:T(8,128)(2,1)S(1)} %get-tuple-element.37), channel_id=1, source_target_pairs={{2,0},{3,1},{0,2},{1,3},{6,4},{7,5},{4,6},{5,7},{10,8},{11,9},{8,1... | collective-permute-start | bytes 491528 | tf_op jit(solution)/shard_map/ppermute | solution.py:37
  32.8 0.5 collective-permute-start.12
  33.3 0.0 collective-permute-start.15
  33.3 0.0 copy-done
  33.3 0.0 copy-done.3
  33.3 1.8 %spread_basis.1 = (bf16[128,1536]{1,0:T(8,128)(2,1)S(1)}, bf16[16,128]{1,0:T(8,128)(2,1)S(1)}, bf16[128,1536]{1,0:T(8,128)(2,1)S(1)}, f32[16,1536]{1,0:T(8,128)S(1)}) custom-call(s32[12,32]{1,0:T(8,128)S(1)} %bitcast.19, bf16[192,128]{1,0:T(8,128)(2,1)S(1)} %bitcast.20, s32[14]{0:T(128)S(1)} %get-tuple-element.26.refs_6_.refs_2_.refs_1_, ...), custom_call_target="tpu_custom_call" | custom-call | flops 1000 | bytes 1000 | tf_op jit(solution)/shard_map/spread_basis/pallas_call | solution.py:635
  35.1 0.0 collective-permute-done.11.refs_14_
  35.1 2.1 %gram_early.1.refs_2_.refs_6_ = bf16[1536,1536]{1,0:T(8,128)(2,1)S(1)} custom-call(s32[83]{0:T(128)S(1)} %get-tuple-element.36.refs_0_, bf16[1536,128]{1,0:T(8,128)(2,1)S(1)} %bitcast.15, bf16[1536,128]{1,0:T(8,128)(2,1)S(1)} %collective-permute-done.4.refs_5_.refs_2_, bf16[1536,128]{1,0:T(8,128)(2,1)S(1)} %collective-permute-done.2.refs_0_.refs_3_, ...), custom_call_target="tpu_custom_call" | custom-call | flops 1000 | bytes 1000 | tf_op jit(solution)/shard_map/gram_early/pallas_call | solution.py:652
  37.3 0.6 %collective-permute-done.15.refs_3_.refs_2_ = bf16[96,128]{1,0:T(8,128)(2,1)S(1)} collective-permute-done((bf16[96,128]{1,0:T(8,128)(2,1)S(1)}, bf16[96,128]{1,0:T(8,128)(2,1)S(1)}, u32[]{:S(2)}, u32[]{:S(2)}) %collective-permute-start.15) | collective-permute-done | bytes 24608 | tf_op jit(solution)/shard_map/ppermute | solution.py:37
  37.9 0.2 collective-permute-done.13.refs_1_.refs_8_
  38.1 1.0 %collective-permute-done.12.refs_0_.refs_7_ = bf16[640,128]{1,0:T(8,128)(2,1)S(1)} collective-permute-done((bf16[640,128]{1,0:T(8,128)(2,1)S(1)}, bf16[640,128]{1,0:T(8,128)(2,1)S(1)}, u32[]{:S(2)}, u32[]{:S(2)}) %collective-permute-start.12) | collective-permute-done | bytes 163872 | tf_op jit(solution)/shard_map/ppermute | solution.py:26
  39.1 0.1 collective-permute-start.16
  39.2 1.6 %collective-permute-done.16.refs_10_ = bf16[1280,128]{1,0:T(8,128)(2,1)S(1)} collective-permute-done((bf16[1280,128]{1,0:T(8,128)(2,1)S(1)}, bf16[1280,128]{1,0:T(8,128)(2,1)S(1)}, u32[]{:S(2)}, u32[]{:S(2)}) %collective-permute-start.16) | collective-permute-done | bytes 327712 | tf_op jit(solution)/shard_map/ppermute | solution.py:37
  40.8 0.0 collective-permute-done.14.refs_9_.refs_1_
  40.8 5.4 %square_cube_coefficients.1 = (bf16[12,128,128]{2,1,0:T(8,128)(2,1)}, f32[8,128]{1,0:T(8,128)S(1)}) custom-call(s32[83]{0:T(128)S(1)} %get-tuple-element.25.refs_0_, s32[14]{0:T(128)S(1)} %get-tuple-element.26.refs_6_.refs_2_.refs_1_, bf16[16,128]{1,0:T(8,128)(2,1)S(1)} %get-tuple-element.32.refs_4_.refs_2_, ...), custom_call_target="tpu_custom_call" | custom-call | flops 1300000000 | bytes 8000000 | tf_op jit(solution)/shard_map/square_cube_coefficients/pallas_call | solution.py:689
  46.2 0.3 collective-permute-start.18
  46.5 0.4 collective-permute-start.17
  46.9 2.4 %collective-permute-done.18 = f32[8,128]{1,0:T(8,128)S(1)} collective-permute-done((f32[8,128]{1,0:T(8,128)S(1)}, f32[8,128]{1,0:T(8,128)S(1)}, u32[]{:S(2)}, u32[]{:S(2)}) %collective-permute-start.18) | collective-permute-done | bytes 4128 | tf_op jit(solution)/shard_map/ppermute | solution.py:37
  49.2 0.0 collective-permute-done.17
  49.2 0.1 slice.10
  49.3 0.1 slice.11
  49.4 0.1 pad_maximum_fusion.1
  49.5 0.4 collective-permute-start.19
  49.9 3.2 %collective-permute-done.19 = f32[8,128]{1,0:T(8,128)S(1)} collective-permute-done((f32[8,128]{1,0:T(8,128)S(1)}, f32[8,128]{1,0:T(8,128)S(1)}, u32[]{:S(2)}, u32[]{:S(2)}) %collective-permute-start.19) | collective-permute-done | bytes 4128 | tf_op jit(solution)/shard_map/ppermute | solution.py:26
  53.1 0.1 pad_maximum_fusion.refs_0_
  53.2 0.0 collective-permute-start.21
  53.2 2.9 %collective-permute-start.20 = (f32[16,128]{1,0:T(8,128)S(1)}, f32[16,128]{1,0:T(8,128)S(1)}, u32[]{:S(2)}, u32[]{:S(2)}) collective-permute-start(f32[16,128]{1,0:T(8,128)S(1)} %pad_maximum_fusion.refs_0_), channel_id=1, source_target_pairs={{12,0},{8,4},{4,8},{0,12},{13,1},{9,5},{5,9},{1,13},{14,2},{10,6},... | collective-permute-start | bytes 24584 | tf_op jit(solution)/shard_map/ppermute | solution.py:32
  56.1 2.8 %profiles.1 = (bf16[6,6,256,128]{3,2,1,0:T(8,128)(2,1)S(1)}, bf16[6,6,128,128]{3,2,1,0:T(8,128)(2,1)S(1)}) custom-call(bf16[96,128]{1,0:T(8,128)(2,1)S(1)} %get-tuple-element.39.refs_0_, bf16[2960,128]{1,0:T(8,128)(2,1)S(1)} %collective-permute-done.14.refs_9_.refs_1_, bf16[96,128]{1,0:T(8,128)(2,1)S(1)} %collective-permute-done.15.refs_3_.refs_2_), custom_call_target="tpu_custom_call" | custom-call | flops 1000 | bytes 1000 | tf_op jit(solution)/shard_map/profiles/pallas_call | solution.py:671
  58.9 0.0 collective-permute-done.21.refs_2_
  58.9 0.0 collective-permute-done.20.refs_1_
  58.9 1.5 %density.1 = f32[256,128]{1,0:T(8,128)} custom-call(f32[16,128]{1,0:T(8,128)S(1)} %pad_maximum_fusion.refs_0_, f32[16,128]{1,0:T(8,128)S(1)} %collective-permute-done.20.refs_1_, f32[16,128]{1,0:T(8,128)S(1)} %collective-permute-done.21.refs_2_, bf16[6,6,256,128]{3,2,1,0:T(8,128)(2,1)S(1)} %get-tuple-element.42.refs_3_, bf16[4608,128]{1,0:T(8,128)(2,1)S(1)} %bitcast.16), custom_call_target="tpu_custom_call" | custom-call | flops 310000000 | bytes 4000000 | tf_op jit(solution)/shard_map/density/pallas_call | solution.py:725
  (8 shorter events, 0.1 us)
Async XLA Ops:
  0.6 12.3 %collective-permute-start.3 = (bf16[1536,128]{1,0:T(8,128)(2,1)}, bf16[1536,128]{1,0:T(8,128)(2,1)S(1)}, u32[]{:S(2)}, u32[]{:S(2)}) collective-permute-start(bf16[1536,128]{1,0:T(8,128)(2,1)} %bitcast.10), channel_id=1, source_target_pairs={{16,0},{0,16},{17,1},{1,17},{18,2},{2,18},{19,3},{3,19},{20,4},{4,... | collective-permute-start | bytes 1179656 | tf_op jit(solution)/shard_map/ppermute | solution.py:26
  3.6 10.8 %collective-permute-start.2 = (bf16[1536,128]{1,0:T(8,128)(2,1)}, bf16[1536,128]{1,0:T(8,128)(2,1)S(1)}, u32[]{:S(2)}, u32[]{:S(2)}) collective-permute-start(bf16[1536,128]{1,0:T(8,128)(2,1)} %bitcast.11), channel_id=1, source_target_pairs={{2,0},{3,1},{0,2},{1,3},{6,4},{7,5},{4,6},{5,7},{10,8},{11,9},{8,1... | collective-permute-start | bytes 1179656 | tf_op jit(solution)/shard_map/ppermute | solution.py:37
  5.2 15.2 %collective-permute-start.4 = (bf16[1536,128]{1,0:T(8,128)(2,1)}, bf16[1536,128]{1,0:T(8,128)(2,1)S(1)}, u32[]{:S(2)}, u32[]{:S(2)}) collective-permute-start(bf16[1536,128]{1,0:T(8,128)(2,1)} %bitcast.12), channel_id=1, source_target_pairs={{1,0},{0,1},{3,2},{2,3},{5,4},{4,5},{7,6},{6,7},{9,8},{8,9},{11,10... | collective-permute-start | bytes 1179656 | tf_op jit(solution)/shard_map/ppermute | solution.py:37
  7.7 9.8 %collective-permute-start.1 = (bf16[656,128]{1,0:T(8,128)(2,1)}, bf16[656,128]{1,0:T(8,128)(2,1)S(1)}, u32[]{:S(2)}, u32[]{:S(2)}) collective-permute-start(bf16[656,128]{1,0:T(8,128)(2,1)} %pick_column_blocks.1.refs_2_), channel_id=1, source_target_pairs={{4,0},{0,4},{12,8},{8,12},{5,1},{1,5},{13,9},{9,13},{6,2},{2,6},{1... | collective-permute-start | bytes 503816 | tf_op jit(solution)/shard_map/ppermute | solution.py:32
  9.3 11.1 %collective-permute-start = (bf16[656,128]{1,0:T(8,128)(2,1)}, bf16[656,128]{1,0:T(8,128)(2,1)S(1)}, u32[]{:S(2)}, u32[]{:S(2)}) collective-permute-start(bf16[656,128]{1,0:T(8,128)(2,1)} %pick_column_blocks.1.refs_2_), channel_id=1, source_target_pairs={{12,0},{8,4},{4,8},{0,12},{13,1},{9,5},{5,9},{1,13},{14,2},{10,6},... | collective-permute-start | bytes 503816 | tf_op jit(solution)/shard_map/ppermute | solution.py:32
  14.4 0.9 %copy-start.1 = (bf16[656,128]{1,0:T(8,128)(2,1)S(1)}, bf16[656,128]{1,0:T(8,128)(2,1)}, u32[]{:S(2)}) copy-start(bf16[656,128]{1,0:T(8,128)(2,1)} %pick_column_blocks.1.refs_2_) | copy-start | bytes 503812
  15.4 6.2 %collective-permute-start.9 = (bf16[640,128]{1,0:T(8,128)(2,1)S(1)}, bf16[640,128]{1,0:T(8,128)(2,1)S(1)}, u32[]{:S(2)}, u32[]{:S(2)}) collective-permute-start(bf16[640,128]{1,0:T(8,128)(2,1)S(1)} %get-tuple-element.29), channel_id=1, source_target_pairs={{16,0},{0,16},{17,1},{1,17},{18,2},{2,18},{19,3},{3,19},{20,4},{4,... | collective-permute-start | bytes 491528 | tf_op jit(solution)/shard_map/ppermute | solution.py:26
  15.8 6.3 %collective-permute-start.10 = (bf16[640,128]{1,0:T(8,128)(2,1)S(1)}, bf16[640,128]{1,0:T(8,128)(2,1)S(1)}, u32[]{:S(2)}, u32[]{:S(2)}) collective-permute-start(bf16[640,128]{1,0:T(8,128)(2,1)S(1)} %get-tuple-element.30), channel_id=1, source_target_pairs={{2,0},{3,1},{0,2},{1,3},{6,4},{7,5},{4,6},{5,7},{10,8},{11,9},{8,1... | collective-permute-start | bytes 491528 | tf_op jit(solution)/shard_map/ppermute | solution.py:37
  20.5 10.3 %collective-permute-start.5 = (bf16[1456,128]{1,0:T(8,128)(2,1)S(1)}, bf16[1456,128]{1,0:T(8,128)(2,1)S(1)}, u32[]{:S(2)}, u32[]{:S(2)}) collective-permute-start(bf16[1456,128]{1,0:T(8,128)(2,1)S(1)} %get-tuple-element.27), channel_id=1, source_target_pairs={{2,0},{3,1},{0,2},{1,3},{6,4},{7,5},{4,6},{5,7},{10,8},{11,9},{8,1... | collective-permute-start | bytes 1118216 | tf_op jit(solution)/shard_map/ppermute | solution.py:37
  21.0 1.2 %copy-start.2 = (s32[32,12]{0,1:T(8,128)S(1)}, s32[32,12]{0,1:T(8,128)}, u32[]{:S(2)}) copy-start(s32[32,12]{0,1:T(8,128)} %param.9) | copy-start | bytes 4612
  21.0 1.2 %copy-start.4 = (s32[32]{0:T(128)S(1)}, s32[32]{0:T(128)}, u32[]{:S(2)}) copy-start(s32[32]{0:T(128)} %refs_1_.3) | copy-start | bytes 388
  21.0 10.0 %collective-permute-start.6 = (bf16[1456,128]{1,0:T(8,128)(2,1)S(1)}, bf16[1456,128]{1,0:T(8,128)(2,1)S(1)}, u32[]{:S(2)}, u32[]{:S(2)}) collective-permute-start(bf16[1456,128]{1,0:T(8,128)(2,1)S(1)} %get-tuple-element.24.refs_2_), channel_id=1, source_target_pairs={{16,0},{0,16},{17,1},{1,17},{18,2},{2,18},{19,3},{3,19},{20,4},{4,... | collective-permute-start | bytes 1118216 | tf_op jit(solution)/shard_map/ppermute | solution.py:26
  21.6 9.4 %collective-permute-start.8 = (bf16[1536,128]{1,0:T(8,128)(2,1)S(1)}, bf16[1536,128]{1,0:T(8,128)(2,1)S(1)}, u32[]{:S(2)}, u32[]{:S(2)}) collective-permute-start(bf16[1536,128]{1,0:T(8,128)(2,1)S(1)} %collective-permute-done.3.refs_1_.refs_4_.refs_7_), channel_id=1, source_target_pairs={{1,0},{0,1},{3,2},{2,3},{5,4},{4,5},{7,6},{6,7},{9,8},{8,9},{11,10... | collective-permute-start | bytes 1179656 | tf_op jit(solution)/shard_map/ppermute | solution.py:37
  21.6 9.4 %collective-permute-start.7 = (bf16[1536,128]{1,0:T(8,128)(2,1)S(1)}, bf16[1536,128]{1,0:T(8,128)(2,1)S(1)}, u32[]{:S(2)}, u32[]{:S(2)}) collective-permute-start(bf16[1536,128]{1,0:T(8,128)(2,1)S(1)} %collective-permute-done.2.refs_0_.refs_3_), channel_id=1, source_target_pairs={{1,0},{0,1},{3,2},{2,3},{5,4},{4,5},{7,6},{6,7},{9,8},{8,9},{11,10... | collective-permute-start | bytes 1179656 | tf_op jit(solution)/shard_map/ppermute | solution.py:37
  22.1 11.2 %copy-start = (bf16[1,12,128,128]{3,2,1,0:T(8,128)(2,1)S(1)}, bf16[1,12,128,128]{3,2,1,0:T(8,128)(2,1)}, u32[]{:S(2)}) copy-start(bf16[1,12,128,128]{3,2,1,0:T(8,128)(2,1)} %param.8) | copy-start | bytes 1179652
  22.2 11.2 %copy-start.3 = (bf16[32,6,128]{2,0,1:T(8,128)(2,1)S(1)}, bf16[32,6,128]{2,0,1:T(8,128)(2,1)}, u32[]{:S(2)}) copy-start(bf16[32,6,128]{2,0,1:T(8,128)(2,1)} %param.11) | copy-start | bytes 147460
  22.2 12.9 %collective-permute-start.11 = (bf16[2560,128]{1,0:T(8,128)(2,1)S(1)}, bf16[2560,128]{1,0:T(8,128)(2,1)S(1)}, u32[]{:S(2)}, u32[]{:S(2)}) collective-permute-start(bf16[2560,128]{1,0:T(8,128)(2,1)S(1)} %pack_two_mate.1.refs_5_), channel_id=1, source_target_pairs={{1,0},{0,1},{3,2},{2,3},{5,4},{4,5},{7,6},{6,7},{9,8},{8,9},{11,10... | collective-permute-start | bytes 1966088 | tf_op jit(solution)/shard_map/ppermute | solution.py:37
  31.1 9.7 %collective-permute-start.14 = (bf16[2960,128]{1,0:T(8,128)(2,1)S(1)}, bf16[2960,128]{1,0:T(8,128)(2,1)S(1)}, u32[]{:S(2)}, u32[]{:S(2)}) collective-permute-start(bf16[2960,128]{1,0:T(8,128)(2,1)S(1)} %get-tuple-element.38), channel_id=1, source_target_pairs={{1,0},{0,1},{3,2},{2,3},{5,4},{4,5},{7,6},{6,7},{9,8},{8,9},{11,10... | collective-permute-start | bytes 2273288 | tf_op jit(solution)/shard_map/ppermute | solution.py:37
  31.2 6.9 %collective-permute-start.13 = (bf16[640,128]{1,0:T(8,128)(2,1)S(1)}, bf16[640,128]{1,0:T(8,128)(2,1)S(1)}, u32[]{:S(2)}, u32[]{:S(2)}) collective-permute-start(bf16[640,128]{1,0:T(8,128)(2,1)S(1)} %get-tuple-element.37), channel_id=1, source_target_pairs={{2,0},{3,1},{0,2},{1,3},{6,4},{7,5},{4,6},{5,7},{10,8},{11,9},{8,1... | collective-permute-start | bytes 491528 | tf_op jit(solution)/shard_map/ppermute | solution.py:37
  32.8 6.3 %collective-permute-start.12 = (bf16[640,128]{1,0:T(8,128)(2,1)S(1)}, bf16[640,128]{1,0:T(8,128)(2,1)S(1)}, u32[]{:S(2)}, u32[]{:S(2)}) collective-permute-start(bf16[640,128]{1,0:T(8,128)(2,1)S(1)} %get-tuple-element.31.refs_4_.refs_15_), channel_id=1, source_target_pairs={{16,0},{0,16},{17,1},{1,17},{18,2},{2,18},{19,3},{3,19},{20,4},{4,... | collective-permute-start | bytes 491528 | tf_op jit(solution)/shard_map/ppermute | solution.py:26
  33.3 4.6 %collective-permute-start.15 = (bf16[96,128]{1,0:T(8,128)(2,1)S(1)}, bf16[96,128]{1,0:T(8,128)(2,1)S(1)}, u32[]{:S(2)}, u32[]{:S(2)}) collective-permute-start(bf16[96,128]{1,0:T(8,128)(2,1)S(1)} %get-tuple-element.39.refs_0_), channel_id=1, source_target_pairs={{3,0},{2,1},{1,2},{0,3},{7,4},{6,5},{5,6},{4,7},{11,8},{10,9},{9,1... | collective-permute-start | bytes 73736 | tf_op jit(solution)/shard_map/ppermute | solution.py:37
  39.1 1.7 %collective-permute-start.16 = (bf16[1280,128]{1,0:T(8,128)(2,1)S(1)}, bf16[1280,128]{1,0:T(8,128)(2,1)S(1)}, u32[]{:S(2)}, u32[]{:S(2)}) collective-permute-start(bf16[1280,128]{1,0:T(8,128)(2,1)S(1)} %pack_four.1), channel_id=1, source_target_pairs={{1,0},{0,1},{3,2},{2,3},{5,4},{4,5},{7,6},{6,7},{9,8},{8,9},{11,10... | collective-permute-start | bytes 983048 | tf_op jit(solution)/shard_map/ppermute | solution.py:37
  46.2 3.0 %collective-permute-start.18 = (f32[8,128]{1,0:T(8,128)S(1)}, f32[8,128]{1,0:T(8,128)S(1)}, u32[]{:S(2)}, u32[]{:S(2)}) collective-permute-start(f32[8,128]{1,0:T(8,128)S(1)} %get-tuple-element.41), channel_id=1, source_target_pairs={{3,0},{2,1},{1,2},{0,3},{7,4},{6,5},{5,6},{4,7},{11,8},{10,9},{9,1... | collective-permute-start | bytes 12296 | tf_op jit(solution)/shard_map/ppermute | solution.py:37
  46.5 2.7 %collective-permute-start.17 = (f32[8,128]{1,0:T(8,128)S(1)}, f32[8,128]{1,0:T(8,128)S(1)}, u32[]{:S(2)}, u32[]{:S(2)}) collective-permute-start(f32[8,128]{1,0:T(8,128)S(1)} %get-tuple-element.41), channel_id=1, source_target_pairs={{1,0},{0,1},{3,2},{2,3},{5,4},{4,5},{7,6},{6,7},{9,8},{8,9},{11,10... | collective-permute-start | bytes 12296 | tf_op jit(solution)/shard_map/ppermute | solution.py:37
  49.5 3.6 %collective-permute-start.19 = (f32[8,128]{1,0:T(8,128)S(1)}, f32[8,128]{1,0:T(8,128)S(1)}, u32[]{:S(2)}, u32[]{:S(2)}) collective-permute-start(f32[8,128]{1,0:T(8,128)S(1)} %pad_maximum_fusion.1), channel_id=1, source_target_pairs={{16,0},{0,16},{17,1},{1,17},{18,2},{2,18},{19,3},{3,19},{20,4},{4,... | collective-permute-start | bytes 12296 | tf_op jit(solution)/shard_map/ppermute | solution.py:26
  53.2 5.8 %collective-permute-start.21 = (f32[16,128]{1,0:T(8,128)S(1)}, f32[16,128]{1,0:T(8,128)S(1)}, u32[]{:S(2)}, u32[]{:S(2)}) collective-permute-start(f32[16,128]{1,0:T(8,128)S(1)} %pad_maximum_fusion.refs_0_), channel_id=1, source_target_pairs={{4,0},{0,4},{12,8},{8,12},{5,1},{1,5},{13,9},{9,13},{6,2},{2,6},{1... | collective-permute-start | bytes 24584 | tf_op jit(solution)/shard_map/ppermute | solution.py:32
  53.2 5.8 %collective-permute-start.20 = (f32[16,128]{1,0:T(8,128)S(1)}, f32[16,128]{1,0:T(8,128)S(1)}, u32[]{:S(2)}, u32[]{:S(2)}) collective-permute-start(f32[16,128]{1,0:T(8,128)S(1)} %pad_maximum_fusion.refs_0_), channel_id=1, source_target_pairs={{12,0},{8,4},{4,8},{0,12},{13,1},{9,5},{5,9},{1,13},{14,2},{10,6},... | collective-permute-start | bytes 24584 | tf_op jit(solution)/shard_map/ppermute | solution.py:32

commit v15 on v13

--- a/solution.py
+++ b/solution.py
@@ -92,7 +92,7 @@
 
 
 def pick_kernel(axes, *refs):
-    sign_ref, out_ref, neighbors_ref, extent_ref, x_ref, y_ref, z_ref, place_ref, loads, sems = refs[5:]
+    sign_ref, out_ref, geo_ref, neighbors_ref, extent_ref, x_ref, y_ref, z_ref, place_ref, tile, loads, sems = refs[5:]
     at = Places(*axes)
     slots = sign_ref.shape[0]
     n_pick = place_ref.shape[0] - 1
@@ -124,14 +124,19 @@
         extent = extent_ref[0, w]
         values = jnp.where(sub == 0, twice_x, jnp.where(sub == 1, twice_y, jnp.where(sub == 2, twice_z, extent)))
         geo = jnp.where(lane_pair == rank, values, geo)
-    out_ref[n_pick * size :] = geo.astype(jnp.float32).astype(out_ref.dtype)
+    geo = geo.astype(jnp.float32).astype(out_ref.dtype)
+    geo_ref[...] = geo
+    tile[...] = geo
+    copy = pltpu.make_async_copy(tile, out_ref.at[pl.ds(n_pick * size, GEO)], sems.at[n_pick])
+    copy.start()
+    copies.append(copy)
     for copy in copies:
         copy.wait()
 
 
 def spread_kernel(axes, *refs):
-    basis_ref = refs[1]
-    spread_ref, own_basis_ref, neighbors_ref, loads = refs[-4:]
+    basis_ref, info_ref, sign_ref = refs[1:4]
+    spread_ref, own_basis_ref, own_ref, neighbors_ref, loads = refs[-5:]
     at = Places(*axes)
     load(refs[:1], (neighbors_ref,), loads)
     slots, atoms = neighbors_ref.shape
@@ -149,6 +154,13 @@
     for w, (atom, rank) in enumerate(own_ranks(at, neighbors_ref)):
         spread_ref[:, w * LANES : (w + 1) * LANES] = rows_of(hot(LANES, atom, rank * SHELLS))
     own_basis_ref[...] = rows_of(hot(16, at.me, 0))
+    size = sign_ref.shape[1]
+    rows = lax.broadcasted_iota(jnp.int32, (size, size), 0)
+    lanes = lax.broadcasted_iota(jnp.int32, (size, size), 1)
+    for w in range(slots):
+        kept = (rows < info_ref[slots]) & (lanes < info_ref[w])
+        block = jnp.where(kept, sign_ref[w].astype(jnp.float32), 0.0)
+        own_ref[:, w * size : (w + 1) * size] = block.astype(own_ref.dtype)
 
 
 def prepare_kernel(axes, count, layout, late_from, *refs):
@@ -287,21 +299,15 @@
 
 
 def step_kernel(pieces, *refs):
-    table_ref, info_ref, basis_ref, spread_ref, sign_ref, early_ref = refs[:6]
+    table_ref, info_ref, basis_ref, spread_ref, own, early_ref = refs[:6]
     piece_refs = refs[6 : 6 + pieces]
-    next_ref, coef_ref, pool, gram, own, square = refs[-6:]
-    slots, size = sign_ref.shape[0], sign_ref.shape[1]
+    next_ref, coef_ref, pool, gram, square = refs[-5:]
+    slots, size = next_ref.shape[0], next_ref.shape[1]
     fill(piece_refs, pool)
     for v in range(slots):
         gram[v * size : (v + 1) * size] = early_ref[v * size : (v + 1) * size]
-    rows = lax.broadcasted_iota(jnp.int32, (size, size), 0)
-    lanes = lax.broadcasted_iota(jnp.int32, (size, size), 1)
     own_size = info_ref[slots]
     self_slot = info_ref[slots + 1]
-    for w in range(slots):
-        kept = (rows < own_size) & (lanes < info_ref[w])
-        block = jnp.where(kept, sign_ref[w].astype(jnp.float32), 0.0)
-        own[:, w * size : (w + 1) * size] = block.astype(own.dtype)
     place_pairs(table_ref, pool, gram, size)
     wide = 2 * size
     wide_lanes = lax.broadcasted_iota(jnp.int32, (size, wide), 1)
@@ -444,11 +450,14 @@
     x_row = {di: on_row(flat, di) for di in others}
     y_row = from_layer(flat, 2)
     m_row = from_layer(flat, 1)
-    picked = pl.pallas_call(
+    picked, geo = pl.pallas_call(
         functools.partial(pick_kernel, axes),
-        out_shape=jax.ShapeDtypeStruct((part, size), own.dtype),
+        out_shape=(
+            jax.ShapeDtypeStruct((part, size), own.dtype),
+            jax.ShapeDtypeStruct((GEO, LANES), own.dtype),
+        ),
         in_specs=[HBM] * 6,
-        out_specs=VMEM,
+        out_specs=(HBM, VMEM),
         scratch_shapes=[
             pltpu.SMEM((slots, atoms), jnp.int32),
             pltpu.SMEM((1, slots), jnp.int32),
@@ -456,8 +465,9 @@
             pltpu.SMEM((atoms,), jnp.int32),
             pltpu.SMEM((atoms,), jnp.int32),
             pltpu.SMEM((n_pick + 1,), jnp.int32),
+            pltpu.VMEM((GEO, LANES), jnp.bfloat16),
             pltpu.SemaphoreType.DMA((5,)),
-            pltpu.SemaphoreType.DMA((n_pick,)),
+            pltpu.SemaphoreType.DMA((n_pick + 1,)),
         ],
         compiler_params=pltpu.CompilerParams(vmem_limit_bytes=60 << 20),
         name="pick_column_blocks",
@@ -466,8 +476,8 @@
     up = from_column(picked, 0)
 
     halves = pack(
-        [y_row] + [x_row[di] for di in others] + [picked],
-        [[(0, half, most)]] + [[(di, 0, most)] for di in others] + [[(count, picks, GEO)]],
+        [y_row] + [x_row[di] for di in others],
+        [[(0, half, most)]] + [[(di, 0, most)] for di in others],
         [],
         "pack_halves",
     )
@@ -498,7 +508,7 @@
     note("far", y_row, row_of(0, 2))
     note("up", up, side_of("up", 0, 0) + [(("up geo", 0, 0), GEO)])
     note("down", down, side_of("down", 0, 0) + [(("down geo", 0, 0), GEO)])
-    note("geo", halves[count], [(("geo", 0, 0), GEO)])
+    buffers["geo"] = geo
     for di in others:
         note(("x", di), x_row[di], row_of(di, 0))
         note(("end", di), ends[di], row_of(di, 2, halfway, slots - 1))
@@ -512,14 +522,14 @@
         [(2, 0, GEO), (1, picks, GEO), (0, picks, GEO)],
     ]
     two_x, two_y, geos = pack([buffers[name] for name in names], plans, [m_row], "pack_two")
-    to_mate = corners + ["up", "down"]
+    sides = pack([up, down], [[(0, 0, picks), (1, 0, picks)]], [], "pack_mate_sides")[0]
     for di in others:
         note(("mate x", di), from_layer(x_row[di], 1), row_of(di, 1))
     note("mate far", from_layer(y_row, 1), row_of(0, 3))
 
-    early_order = ["own", "mate", "far", "up", "down", "geo"] + [("x", di) for di in others]
+    early_order = ["own", "mate", "far", "up", "down"] + [("x", di) for di in others]
     early_order += [("mate x", di) for di in others] + ["mate far"]
-    early_order += corners + [("two x", di) for di in others] + ["two y", "two m"]
+    early_order += corners + [("two x", di) for di in others] + ["two y", "two m", "mate sides"]
     late_order = [("three x", di) for di in others] + ["three y", "three m"]
     late_order += ["four"]
 
@@ -532,7 +542,7 @@
     contents["two y"] += sum([row_of(di, 2, halfway - 1, halfway) for di in others], []) + [(None, 3 * GEO)]
     contents["two m"] = sum([row_of(di, 3, halfway, slots - 1) for di in others], [])
     contents["two m"] += sum([row_of(di, 3, 0, halfway - 1) for di in others], [])
-    contents["two m"] += side_of("up", 0, 1) + side_of("down", 0, 1)
+    contents["mate sides"] = side_of("up", 0, 1) + side_of("down", 0, 1)
     for di in others:
         contents["three x", di] = side_of("up", di, 2)
     contents["three y"] = sum([side_of("down", di, 2) for di in others], [])
@@ -597,13 +607,14 @@
         name="prepare",
     )(listings, atom_size, two_x)
 
-    plans = [[(i, 0, picks if name in ("up", "down") else most) for i, name in enumerate(to_mate)]]
-    two_m = pack([buffers[name] for name in to_mate], plans, [], "pack_two_mate", 3_000_000_000)[0]
+    plans = [[(i, 0, most) for i in range(len(corners))]]
+    two_m = pack([buffers[name] for name in corners], plans, [], "pack_two_mate", 3_000_000_000)[0]
     for di in others:
         note(("two x", di), on_row(two_x, di), contents["two x", di])
     note("two y", from_layer(two_y, 2), contents["two y"])
-    early_mates = ["mate far"] + [("mate x", di) for di in others]
+    early_mates = ["two m", "mate sides", "mate far"] + [("mate x", di) for di in others]
     note("two m", from_layer(two_m, 1), contents["two m"])
+    note("mate sides", from_layer(sides, 1), contents["mate sides"])
 
     buffers["geos"] = geos
     names = ["two y", "geos"] + [("two x", di) for di in others]
@@ -616,26 +627,27 @@
         [(x, 0, 2 * picks + size) for x in xs] + [(0, 0, lengths["two y"])] + gather,
         gather,
     ]
-    three_x, three_y, three_m, geos = pack([buffers[name] for name in names], plans, [buffers[name] for name in early_mates] + [two_m, info], "pack_three")
+    three_x, three_y, three_m, geos = pack([buffers[name] for name in names], plans, [buffers[name] for name in early_mates] + [info], "pack_three")
     for di in others:
         note(("three x", di), on_row(three_x, di), contents["three x", di])
     note("three y", from_layer(three_y, 2), contents["three y"])
     note("three m", from_layer(three_m, 1), contents["three m"])
     third_geos = from_layer(geos, 3)
 
-    spread, own_basis = pl.pallas_call(
+    spread, own_basis, own_kept = pl.pallas_call(
         functools.partial(spread_kernel, axes),
         out_shape=(
             jax.ShapeDtypeStruct((LANES, full), jnp.bfloat16),
             jax.ShapeDtypeStruct((16, size), jnp.bfloat16),
+            jax.ShapeDtypeStruct((size, full), jnp.bfloat16),
         ),
-        in_specs=[HBM, VMEM, ANY],
-        out_specs=(VMEM, VMEM),
+        in_specs=[HBM, VMEM, SMEM, VMEM, ANY],
+        out_specs=(VMEM, VMEM, VMEM),
         scratch_shapes=[pltpu.SMEM((slots, atoms), jnp.int32), pltpu.SemaphoreType.DMA((1,))],
         compiler_params=pltpu.CompilerParams(vmem_limit_bytes=(2 << 20) + atoms * 16384),
         cost_estimate=pl.CostEstimate(flops=1000, bytes_accessed=1000, transcendentals=0),
         name="spread_basis",
-    )(listings, basis_proj.transpose(1, 0, 2).reshape(SHELLS * atoms, size), three_x)
+    )(listings, basis_proj.transpose(1, 0, 2).reshape(SHELLS * atoms, size), info, own, three_x)
 
     early_values = [buffers[name] for name in early_order]
     gram = pl.pallas_call(
@@ -687,12 +699,11 @@
             pltpu.VMEM((total - late_from, LANES), jnp.bfloat16),
             pltpu.VMEM((full, full), jnp.bfloat16),
             pltpu.VMEM((size, full), jnp.bfloat16),
-            pltpu.VMEM((size, full), jnp.bfloat16),
         ],
         compiler_params=pltpu.CompilerParams(vmem_limit_bytes=(15 << 20) + 2 * (total - late_from) * LANES * 2),
         cost_estimate=pl.CostEstimate(flops=1_300_000_000, bytes_accessed=8_000_000, transcendentals=0),
         name="square_cube_coefficients",
-    )(late_table, info, own_basis, spread, own, gram, *late_values)
+    )(late_table, info, own_basis, spread, own_kept, gram, *late_values)
 
     mate_coef = from_layer(coef, 1)
     third_coef = from_layer(coef, 3)

time: 60.4 us -> 67.3 us (1.11)
  Pallas kernels: 18.9 us -> 25.2 us
  waiting for transfers between devices: 18.9 us -> 21.8 us
  starting transfers between devices: 20.3 us -> 18.2 us
    pallas_call x1, Pallas kernels: 2.48 us -> 7.66 us  [local(): pl.pallas_call(functools.partial(pick_kernel, axes), out_shape=(jax.Shape...]
    ppermute x4, waiting for transfers between devices: 3.53 us -> 7.45 us  [from_column(): lax.ppermute(x, 'col', [((i + step[i]) % count, i) for i in range(count)])]
    ppermute x13 -> x14, starting transfers between devices: 8.13 us -> 5.7 us  [from_layer(): return lax.ppermute(x, 'layer', [(i ^ flip, i) for i in range(count)])]
    ppermute x13 -> x14, waiting for transfers between devices: 11.6 us -> 10.1 us  [from_layer(): return lax.ppermute(x, 'layer', [(i ^ flip, i) for i in range(count)])]
    ppermute x4, starting transfers between devices: 6.43 us -> 7.33 us  [from_column(): lax.ppermute(x, 'col', [((i + step[i]) % count, i) for i in range(count)])]
  transfers between devices with their start and end apart: 22 -> 23, of which waited for: 12 -> 10; matrix products, arithmetic and copies ran while one was open for 0% -> 0% of each run, Pallas kernels for 21% -> 28%
where the time goes in v15:
time: 67.3 us; the launch traced here: 67.1 us
  Pallas kernels  25.2 us (37%)
  waiting for transfers between devices  21.8 us (32%)
  starting transfers between devices  18.2 us (27%)
  local copies, waits for them, and re-layouts  0.85 us (1%)
  between operations  0.81 us (1%)
    ppermute x14, waiting for transfers between devices, from_layer(): return lax.ppermute(x, 'layer', [(i ^ flip, i) for i in range(count)])  10.1 us
    pallas_call x1, Pallas kernels, local(): pl.pallas_call(functools.partial(pick_kernel, axes), out_shape=(jax.Shape...  7.66 us
    ppermute x4, waiting for transfers between devices, from_column(): lax.ppermute(x, 'col', [((i + step[i]) % count, i) for i in range(count)])  7.45 us
    ppermute x4, starting transfers between devices, from_column(): lax.ppermute(x, 'col', [((i + step[i]) % count, i) for i in range(count)])  7.33 us
    ppermute x14, starting transfers between devices, from_layer(): return lax.ppermute(x, 'layer', [(i ^ flip, i) for i in range(count)])  5.7 us
    ppermute x5, starting transfers between devices, from_offset(): lax.ppermute(x, axis, [((i + step) % count, i) for i in range(count)])  5.21 us
    pallas_call x1, Pallas kernels, local(): pl.pallas_call(functools.partial(step_kernel, len(late_values)), out_shap...  4.99 us
    ppermute x5, waiting for transfers between devices, from_offset(): lax.ppermute(x, axis, [((i + step) % count, i) for i in range(count)])  4.29 us
  transfers between devices with their start and end apart: 23, of which 10 were waited for; matrix products, arithmetic and copies ran while one was open for 0% of the time, Pallas kernels for 28%

profile of v15, /device:TPU:0, one launch (start us, length us, event | category | flops | bytes accessed | tf_op | source)
XLA Modules:
  0.0 67.1 jit_solution(16034606707819457882)
XLA Ops:
  0.6 3.0 %collective-permute-start.3 = (bf16[1536,128]{1,0:T(8,128)(2,1)}, bf16[1536,128]{1,0:T(8,128)(2,1)S(1)}, u32[]{:S(2)}, u32[]{:S(2)}) collective-permute-start(bf16[1536,128]{1,0:T(8,128)(2,1)} %bitcast.10), channel_id=1, source_target_pairs={{16,0},{0,16},{17,1},{1,17},{18,2},{2,18},{19,3},{3,19},{20,4},{4,... | collective-permute-start | bytes 1179656 | tf_op jit(solution)/shard_map/ppermute | solution.py:26
  3.6 1.5 %collective-permute-start.2 = (bf16[1536,128]{1,0:T(8,128)(2,1)}, bf16[1536,128]{1,0:T(8,128)(2,1)S(1)}, u32[]{:S(2)}, u32[]{:S(2)}) collective-permute-start(bf16[1536,128]{1,0:T(8,128)(2,1)} %bitcast.11), channel_id=1, source_target_pairs={{2,0},{3,1},{0,2},{1,3},{6,4},{7,5},{4,6},{5,7},{10,8},{11,9},{8,1... | collective-permute-start | bytes 1179656 | tf_op jit(solution)/shard_map/ppermute | solution.py:37
  5.2 0.0 collective-permute-start.4
  5.2 7.7 %pick_column_blocks.1 = (bf16[656,128]{1,0:T(8,128)(2,1)}, bf16[16,128]{1,0:T(8,128)(2,1)}) custom-call(s32[12,32]{1,0:T(8,128)} %bitcast.17, s32[1,12]{1,0:T(1,128)} %refs_1_.2, s32[32]{0:T(128)} %refs_2_.1, s32[32]{0:T(128)} %refs_3_.1, s32[32]{0:T(128)} %refs_4_.1, bf16[12,128,128]{2,1,0:T(8,128)(2,1)} %bitcast.13), custom_call_target="tpu_custom_call" | custom-call | tf_op jit(solution)/shard_map/pick_column_blocks/pallas_call | solution.py:453
  12.8 1.6 %collective-permute-start.1 = (bf16[656,128]{1,0:T(8,128)(2,1)}, bf16[656,128]{1,0:T(8,128)(2,1)S(1)}, u32[]{:S(2)}, u32[]{:S(2)}) collective-permute-start(bf16[656,128]{1,0:T(8,128)(2,1)} %get-tuple-element.23), channel_id=1, source_target_pairs={{4,0},{0,4},{12,8},{8,12},{5,1},{1,5},{13,9},{9,13},{6,2},{2,6},{1... | collective-permute-start | bytes 503816 | tf_op jit(solution)/shard_map/ppermute | solution.py:32
  14.5 2.5 %collective-permute-start = (bf16[656,128]{1,0:T(8,128)(2,1)}, bf16[656,128]{1,0:T(8,128)(2,1)S(1)}, u32[]{:S(2)}, u32[]{:S(2)}) collective-permute-start(bf16[656,128]{1,0:T(8,128)(2,1)} %get-tuple-element.23), channel_id=1, source_target_pairs={{12,0},{8,4},{4,8},{0,12},{13,1},{9,5},{5,9},{1,13},{14,2},{10,6},... | collective-permute-start | bytes 503816 | tf_op jit(solution)/shard_map/ppermute | solution.py:32
  16.9 0.0 collective-permute-done.3.refs_4_.refs_1_.refs_6_
  16.9 0.0 collective-permute-done.2.refs_3_.refs_0_
  17.0 0.6 collective-permute-start.7
  17.6 0.5 collective-permute-start.8
  18.1 1.7 %collective-permute-done.1.refs_1_.refs_0_.refs_4_ = bf16[656,128]{1,0:T(8,128)(2,1)S(1)} collective-permute-done((bf16[656,128]{1,0:T(8,128)(2,1)}, bf16[656,128]{1,0:T(8,128)(2,1)S(1)}, u32[]{:S(2)}, u32[]{:S(2)}) %collective-permute-start.1) | collective-permute-done | bytes 167968 | tf_op jit(solution)/shard_map/ppermute | solution.py:32
  19.8 5.7 %collective-permute-done.refs_0_.refs_1_.refs_5_ = bf16[656,128]{1,0:T(8,128)(2,1)S(1)} collective-permute-done((bf16[656,128]{1,0:T(8,128)(2,1)}, bf16[656,128]{1,0:T(8,128)(2,1)S(1)}, u32[]{:S(2)}, u32[]{:S(2)}) %collective-permute-start) | collective-permute-done | bytes 167968 | tf_op jit(solution)/shard_map/ppermute | solution.py:32
  25.6 0.1 collective-permute-start.10
  25.6 0.0 collective-permute-done.4.refs_5_.refs_2_
  25.6 0.0 copy-start.3
  25.7 0.7 %copy-done.3 = bf16[16,128]{1,0:T(8,128)(2,1)S(1)} copy-done((bf16[16,128]{1,0:T(8,128)(2,1)S(1)}, bf16[16,128]{1,0:T(8,128)(2,1)}, u32[]{:S(2)}) %copy-start.3) | copy-done | bytes 4120
  26.3 0.1 pack_two.1
  26.4 0.6 collective-permute-start.5
  27.0 0.5 collective-permute-start.6
  27.5 0.0 collective-permute-done.7.refs_0_.refs_9_
  27.5 0.0 collective-permute-start.12
  27.5 0.0 collective-permute-done.8.refs_1_.refs_10_
  27.6 0.5 collective-permute-start.11
  28.1 0.0 copy-start
  28.1 0.0 copy-start.2
  28.1 0.0 collective-permute-done.10.refs_4_.refs_14_
  28.1 0.1 collective-permute-start.9
  28.3 4.2 %prepare.1 = (s32[83]{0:T(128)S(1)}, s32[83]{0:T(128)S(1)}, s32[14]{0:T(128)S(1)}) custom-call(s32[12,32]{1,0:T(8,128)S(1)} %bitcast.18, s32[32]{0:T(128)S(1)} %copy-done.4, bf16[1456,128]{1,0:T(8,128)(2,1)S(1)} %get-tuple-element.25.refs_2_), custom_call_target="tpu_custom_call" | custom-call | flops 1000 | bytes 1000 | tf_op jit(solution)/shard_map/prepare/pallas_call | solution.py:588
  32.5 5.1 %collective-permute-done.5.refs_0_.refs_12_ = bf16[1456,128]{1,0:T(8,128)(2,1)S(1)} collective-permute-done((bf16[1456,128]{1,0:T(8,128)(2,1)S(1)}, bf16[1456,128]{1,0:T(8,128)(2,1)S(1)}, u32[]{:S(2)}, u32[]{:S(2)}) %collective-permute-start.5) | collective-permute-done | bytes 372768 | tf_op jit(solution)/shard_map/ppermute | solution.py:37
  37.6 0.2 collective-permute-done.6.refs_2_.refs_11_
  37.8 0.0 collective-permute-done.12.refs_6_.refs_7_
  37.8 0.0 collective-permute-done.11.refs_5_.refs_8_
  37.8 0.0 collective-permute-done.9.refs_3_.refs_13_
  37.8 0.1 pack_three.1
  37.9 0.1 collective-permute-start.15
  38.0 1.6 %collective-permute-start.14 = (bf16[640,128]{1,0:T(8,128)(2,1)S(1)}, bf16[640,128]{1,0:T(8,128)(2,1)S(1)}, u32[]{:S(2)}, u32[]{:S(2)}) collective-permute-start(bf16[640,128]{1,0:T(8,128)(2,1)S(1)} %get-tuple-element.37), channel_id=1, source_target_pairs={{2,0},{3,1},{0,2},{1,3},{6,4},{7,5},{4,6},{5,7},{10,8},{11,9},{8,1... | collective-permute-start | bytes 491528 | tf_op jit(solution)/shard_map/ppermute | solution.py:37
  39.6 0.5 collective-permute-start.13
  40.1 0.0 collective-permute-start.16
  40.1 0.0 copy-done.2
  40.1 1.7 %spread_basis.1 = (bf16[128,1536]{1,0:T(8,128)(2,1)S(1)}, bf16[16,128]{1,0:T(8,128)(2,1)S(1)}, bf16[128,1536]{1,0:T(8,128)(2,1)S(1)}) custom-call(s32[12,32]{1,0:T(8,128)S(1)} %bitcast.19, bf16[192,128]{1,0:T(8,128)(2,1)S(1)} %bitcast.20, s32[14]{0:T(128)S(1)} %get-tuple-element.27.refs_7_.refs_2_.refs_1_, bf16[12,128,128]{2,1,0:T(8,128)(2,1)S(1)} %bitcast.14, ...), custom_call_target="tpu_custom_call" | custom-call | flops 1000 | bytes 1000 | tf_op jit(solution)/shard_map/spread_basis/pallas_call | solution.py:637
  41.8 2.0 %gram_early.1.refs_2_.refs_5_ = bf16[1536,1536]{1,0:T(8,128)(2,1)S(1)} custom-call(s32[83]{0:T(128)S(1)} %get-tuple-element.36.refs_0_, bf16[1536,128]{1,0:T(8,128)(2,1)S(1)} %bitcast.15, bf16[1536,128]{1,0:T(8,128)(2,1)S(1)} %collective-permute-done.4.refs_5_.refs_2_, bf16[1536,128]{1,0:T(8,128)(2,1)S(1)} %collective-permute-done.2.refs_3_.refs_0_, ...), custom_call_target="tpu_custom_call" | custom-call | flops 1000 | bytes 1000 | tf_op jit(solution)/shard_map/gram_early/pallas_call | solution.py:653
  43.9 0.8 %collective-permute-done.16.refs_3_.refs_2_ = bf16[96,128]{1,0:T(8,128)(2,1)S(1)} collective-permute-done((bf16[96,128]{1,0:T(8,128)(2,1)S(1)}, bf16[96,128]{1,0:T(8,128)(2,1)S(1)}, u32[]{:S(2)}, u32[]{:S(2)}) %collective-permute-start.16) | collective-permute-done | bytes 24608 | tf_op jit(solution)/shard_map/ppermute | solution.py:37
  44.7 0.2 collective-permute-done.14.refs_1_.refs_7_
  44.9 1.0 %collective-permute-done.13.refs_0_.refs_6_ = bf16[640,128]{1,0:T(8,128)(2,1)S(1)} collective-permute-done((bf16[640,128]{1,0:T(8,128)(2,1)S(1)}, bf16[640,128]{1,0:T(8,128)(2,1)S(1)}, u32[]{:S(2)}, u32[]{:S(2)}) %collective-permute-start.13) | collective-permute-done | bytes 163872 | tf_op jit(solution)/shard_map/ppermute | solution.py:26
  45.9 0.1 collective-permute-start.17
  46.0 1.6 %collective-permute-done.17.refs_9_ = bf16[1280,128]{1,0:T(8,128)(2,1)S(1)} collective-permute-done((bf16[1280,128]{1,0:T(8,128)(2,1)S(1)}, bf16[1280,128]{1,0:T(8,128)(2,1)S(1)}, u32[]{:S(2)}, u32[]{:S(2)}) %collective-permute-start.17) | collective-permute-done | bytes 327712 | tf_op jit(solution)/shard_map/ppermute | solution.py:37
  47.6 0.0 collective-permute-done.15.refs_8_.refs_1_
  47.6 5.0 %square_cube_coefficients.1 = (bf16[12,128,128]{2,1,0:T(8,128)(2,1)}, f32[8,128]{1,0:T(8,128)S(1)}) custom-call(s32[83]{0:T(128)S(1)} %get-tuple-element.26.refs_0_, s32[14]{0:T(128)S(1)} %get-tuple-element.27.refs_7_.refs_2_.refs_1_, bf16[16,128]{1,0:T(8,128)(2,1)S(1)} %get-tuple-element.33.refs_4_.refs_2_, ...), custom_call_target="tpu_custom_call" | custom-call | flops 1300000000 | bytes 8000000 | tf_op jit(solution)/shard_map/square_cube_coefficients/pallas_call | solution.py:690
  52.6 0.3 collective-permute-start.19
  52.8 0.4 collective-permute-start.18
  53.2 2.4 %collective-permute-done.19 = f32[8,128]{1,0:T(8,128)S(1)} collective-permute-done((f32[8,128]{1,0:T(8,128)S(1)}, f32[8,128]{1,0:T(8,128)S(1)}, u32[]{:S(2)}, u32[]{:S(2)}) %collective-permute-start.19) | collective-permute-done | bytes 4128 | tf_op jit(solution)/shard_map/ppermute | solution.py:37
  55.6 0.0 collective-permute-done.18
  55.6 0.1 slice.10
  55.7 0.1 slice.11
  55.8 0.1 pad_maximum_fusion.1
  55.8 0.5 collective-permute-start.20
  56.4 3.1 %collective-permute-done.20 = f32[8,128]{1,0:T(8,128)S(1)} collective-permute-done((f32[8,128]{1,0:T(8,128)S(1)}, f32[8,128]{1,0:T(8,128)S(1)}, u32[]{:S(2)}, u32[]{:S(2)}) %collective-permute-start.20) | collective-permute-done | bytes 4128 | tf_op jit(solution)/shard_map/ppermute | solution.py:26
  59.4 0.1 pad_maximum_fusion.refs_0_
  59.5 0.6 collective-permute-start.22
  60.1 2.6 %collective-permute-start.21 = (f32[16,128]{1,0:T(8,128)S(1)}, f32[16,128]{1,0:T(8,128)S(1)}, u32[]{:S(2)}, u32[]{:S(2)}) collective-permute-start(f32[16,128]{1,0:T(8,128)S(1)} %pad_maximum_fusion.refs_0_), channel_id=1, source_target_pairs={{12,0},{8,4},{4,8},{0,12},{13,1},{9,5},{5,9},{1,13},{14,2},{10,6},... | collective-permute-start | bytes 24584 | tf_op jit(solution)/shard_map/ppermute | solution.py:32
  62.7 2.8 %profiles.1 = (bf16[6,6,256,128]{3,2,1,0:T(8,128)(2,1)S(1)}, bf16[6,6,128,128]{3,2,1,0:T(8,128)(2,1)S(1)}) custom-call(bf16[96,128]{1,0:T(8,128)(2,1)S(1)} %get-tuple-element.39.refs_0_, bf16[2960,128]{1,0:T(8,128)(2,1)S(1)} %collective-permute-done.15.refs_8_.refs_1_, bf16[96,128]{1,0:T(8,128)(2,1)S(1)} %collective-permute-done.16.refs_3_.refs_2_), custom_call_target="tpu_custom_call" | custom-call | flops 1000 | bytes 1000 | tf_op jit(solution)/shard_map/profiles/pallas_call | solution.py:672
  65.6 0.0 collective-permute-done.22.refs_2_
  65.6 0.0 collective-permute-done.21.refs_1_
  65.6 1.5 %density.1 = f32[256,128]{1,0:T(8,128)} custom-call(f32[16,128]{1,0:T(8,128)S(1)} %pad_maximum_fusion.refs_0_, f32[16,128]{1,0:T(8,128)S(1)} %collective-permute-done.21.refs_1_, f32[16,128]{1,0:T(8,128)S(1)} %collective-permute-done.22.refs_2_, bf16[6,6,256,128]{3,2,1,0:T(8,128)(2,1)S(1)} %get-tuple-element.42.refs_3_, bf16[4608,128]{1,0:T(8,128)(2,1)S(1)} %bitcast.16), custom_call_target="tpu_custom_call" | custom-call | flops 310000000 | bytes 4000000 | tf_op jit(solution)/shard_map/density/pallas_call | solution.py:726
  (11 shorter events, 0.1 us)
Async XLA Ops:
  0.6 16.3 %collective-permute-start.3 = (bf16[1536,128]{1,0:T(8,128)(2,1)}, bf16[1536,128]{1,0:T(8,128)(2,1)S(1)}, u32[]{:S(2)}, u32[]{:S(2)}) collective-permute-start(bf16[1536,128]{1,0:T(8,128)(2,1)} %bitcast.10), channel_id=1, source_target_pairs={{16,0},{0,16},{17,1},{1,17},{18,2},{2,18},{19,3},{3,19},{20,4},{4,... | collective-permute-start | bytes 1179656 | tf_op jit(solution)/shard_map/ppermute | solution.py:26
  3.6 13.3 %collective-permute-start.2 = (bf16[1536,128]{1,0:T(8,128)(2,1)}, bf16[1536,128]{1,0:T(8,128)(2,1)S(1)}, u32[]{:S(2)}, u32[]{:S(2)}) collective-permute-start(bf16[1536,128]{1,0:T(8,128)(2,1)} %bitcast.11), channel_id=1, source_target_pairs={{2,0},{3,1},{0,2},{1,3},{6,4},{7,5},{4,6},{5,7},{10,8},{11,9},{8,1... | collective-permute-start | bytes 1179656 | tf_op jit(solution)/shard_map/ppermute | solution.py:37
  5.2 20.5 %collective-permute-start.4 = (bf16[1536,128]{1,0:T(8,128)(2,1)}, bf16[1536,128]{1,0:T(8,128)(2,1)S(1)}, u32[]{:S(2)}, u32[]{:S(2)}) collective-permute-start(bf16[1536,128]{1,0:T(8,128)(2,1)} %bitcast.12), channel_id=1, source_target_pairs={{1,0},{0,1},{3,2},{2,3},{5,4},{4,5},{7,6},{6,7},{9,8},{8,9},{11,10... | collective-permute-start | bytes 1179656 | tf_op jit(solution)/shard_map/ppermute | solution.py:37
  12.8 7.0 %collective-permute-start.1 = (bf16[656,128]{1,0:T(8,128)(2,1)}, bf16[656,128]{1,0:T(8,128)(2,1)S(1)}, u32[]{:S(2)}, u32[]{:S(2)}) collective-permute-start(bf16[656,128]{1,0:T(8,128)(2,1)} %get-tuple-element.23), channel_id=1, source_target_pairs={{4,0},{0,4},{12,8},{8,12},{5,1},{1,5},{13,9},{9,13},{6,2},{2,6},{1... | collective-permute-start | bytes 503816 | tf_op jit(solution)/shard_map/ppermute | solution.py:32
  14.5 11.1 %collective-permute-start = (bf16[656,128]{1,0:T(8,128)(2,1)}, bf16[656,128]{1,0:T(8,128)(2,1)S(1)}, u32[]{:S(2)}, u32[]{:S(2)}) collective-permute-start(bf16[656,128]{1,0:T(8,128)(2,1)} %get-tuple-element.23), channel_id=1, source_target_pairs={{12,0},{8,4},{4,8},{0,12},{13,1},{9,5},{5,9},{1,13},{14,2},{10,6},... | collective-permute-start | bytes 503816 | tf_op jit(solution)/shard_map/ppermute | solution.py:32
  17.0 10.6 %collective-permute-start.7 = (bf16[640,128]{1,0:T(8,128)(2,1)S(1)}, bf16[640,128]{1,0:T(8,128)(2,1)S(1)}, u32[]{:S(2)}, u32[]{:S(2)}) collective-permute-start(bf16[640,128]{1,0:T(8,128)(2,1)S(1)} %get-tuple-element.30), channel_id=1, source_target_pairs={{16,0},{0,16},{17,1},{1,17},{18,2},{2,18},{19,3},{3,19},{20,4},{4,... | collective-permute-start | bytes 491528 | tf_op jit(solution)/shard_map/ppermute | solution.py:26
  17.6 10.0 %collective-permute-start.8 = (bf16[640,128]{1,0:T(8,128)(2,1)S(1)}, bf16[640,128]{1,0:T(8,128)(2,1)S(1)}, u32[]{:S(2)}, u32[]{:S(2)}) collective-permute-start(bf16[640,128]{1,0:T(8,128)(2,1)S(1)} %get-tuple-element.31), channel_id=1, source_target_pairs={{2,0},{3,1},{0,2},{1,3},{6,4},{7,5},{4,6},{5,7},{10,8},{11,9},{8,1... | collective-permute-start | bytes 491528 | tf_op jit(solution)/shard_map/ppermute | solution.py:37
  25.6 2.6 %collective-permute-start.10 = (bf16[1280,128]{1,0:T(8,128)(2,1)S(1)}, bf16[1280,128]{1,0:T(8,128)(2,1)S(1)}, u32[]{:S(2)}, u32[]{:S(2)}) collective-permute-start(bf16[1280,128]{1,0:T(8,128)(2,1)S(1)} %pack_mate_sides.1), channel_id=1, source_target_pairs={{1,0},{0,1},{3,2},{2,3},{5,4},{4,5},{7,6},{6,7},{9,8},{8,9},{11,10... | collective-permute-start | bytes 983048 | tf_op jit(solution)/shard_map/ppermute | solution.py:37
  25.6 0.7 %copy-start.3 = (bf16[16,128]{1,0:T(8,128)(2,1)S(1)}, bf16[16,128]{1,0:T(8,128)(2,1)}, u32[]{:S(2)}) copy-start(bf16[16,128]{1,0:T(8,128)(2,1)} %get-tuple-element.24.refs_2_) | copy-start | bytes 12292
  26.4 11.1 %collective-permute-start.5 = (bf16[1456,128]{1,0:T(8,128)(2,1)S(1)}, bf16[1456,128]{1,0:T(8,128)(2,1)S(1)}, u32[]{:S(2)}, u32[]{:S(2)}) collective-permute-start(bf16[1456,128]{1,0:T(8,128)(2,1)S(1)} %get-tuple-element.28), channel_id=1, source_target_pairs={{2,0},{3,1},{0,2},{1,3},{6,4},{7,5},{4,6},{5,7},{10,8},{11,9},{8,1... | collective-permute-start | bytes 1118216 | tf_op jit(solution)/shard_map/ppermute | solution.py:37
  27.0 1.3 %copy-start.1 = (s32[32,12]{0,1:T(8,128)S(1)}, s32[32,12]{0,1:T(8,128)}, u32[]{:S(2)}) copy-start(s32[32,12]{0,1:T(8,128)} %param.9) | copy-start | bytes 4612
  27.0 1.3 %copy-start.4 = (s32[32]{0:T(128)S(1)}, s32[32]{0:T(128)}, u32[]{:S(2)}) copy-start(s32[32]{0:T(128)} %refs_1_.3) | copy-start | bytes 388
  27.0 10.8 %collective-permute-start.6 = (bf16[1456,128]{1,0:T(8,128)(2,1)S(1)}, bf16[1456,128]{1,0:T(8,128)(2,1)S(1)}, u32[]{:S(2)}, u32[]{:S(2)}) collective-permute-start(bf16[1456,128]{1,0:T(8,128)(2,1)S(1)} %get-tuple-element.25.refs_2_), channel_id=1, source_target_pairs={{16,0},{0,16},{17,1},{1,17},{18,2},{2,18},{19,3},{3,19},{20,4},{4,... | collective-permute-start | bytes 1118216 | tf_op jit(solution)/shard_map/ppermute | solution.py:26
  27.5 10.3 %collective-permute-start.12 = (bf16[1536,128]{1,0:T(8,128)(2,1)S(1)}, bf16[1536,128]{1,0:T(8,128)(2,1)S(1)}, u32[]{:S(2)}, u32[]{:S(2)}) collective-permute-start(bf16[1536,128]{1,0:T(8,128)(2,1)S(1)} %collective-permute-done.3.refs_4_.refs_1_.refs_6_), channel_id=1, source_target_pairs={{1,0},{0,1},{3,2},{2,3},{5,4},{4,5},{7,6},{6,7},{9,8},{8,9},{11,10... | collective-permute-start | bytes 1179656 | tf_op jit(solution)/shard_map/ppermute | solution.py:37
  27.6 10.2 %collective-permute-start.11 = (bf16[1536,128]{1,0:T(8,128)(2,1)S(1)}, bf16[1536,128]{1,0:T(8,128)(2,1)S(1)}, u32[]{:S(2)}, u32[]{:S(2)}) collective-permute-start(bf16[1536,128]{1,0:T(8,128)(2,1)S(1)} %collective-permute-done.2.refs_3_.refs_0_), channel_id=1, source_target_pairs={{1,0},{0,1},{3,2},{2,3},{5,4},{4,5},{7,6},{6,7},{9,8},{8,9},{11,10... | collective-permute-start | bytes 1179656 | tf_op jit(solution)/shard_map/ppermute | solution.py:37
  28.1 12.0 %copy-start = (bf16[1,12,128,128]{3,2,1,0:T(8,128)(2,1)S(1)}, bf16[1,12,128,128]{3,2,1,0:T(8,128)(2,1)}, u32[]{:S(2)}) copy-start(bf16[1,12,128,128]{3,2,1,0:T(8,128)(2,1)} %param.8) | copy-start | bytes 1179652
  28.1 12.0 %copy-start.2 = (bf16[32,6,128]{2,0,1:T(8,128)(2,1)S(1)}, bf16[32,6,128]{2,0,1:T(8,128)(2,1)}, u32[]{:S(2)}) copy-start(bf16[32,6,128]{2,0,1:T(8,128)(2,1)} %param.11) | copy-start | bytes 147460
  28.1 9.7 %collective-permute-start.9 = (bf16[1280,128]{1,0:T(8,128)(2,1)S(1)}, bf16[1280,128]{1,0:T(8,128)(2,1)S(1)}, u32[]{:S(2)}, u32[]{:S(2)}) collective-permute-start(bf16[1280,128]{1,0:T(8,128)(2,1)S(1)} %pack_two_mate.1), channel_id=1, source_target_pairs={{1,0},{0,1},{3,2},{2,3},{5,4},{4,5},{7,6},{6,7},{9,8},{8,9},{11,10... | collective-permute-start | bytes 983048 | tf_op jit(solution)/shard_map/ppermute | solution.py:37
  37.9 9.7 %collective-permute-start.15 = (bf16[2960,128]{1,0:T(8,128)(2,1)S(1)}, bf16[2960,128]{1,0:T(8,128)(2,1)S(1)}, u32[]{:S(2)}, u32[]{:S(2)}) collective-permute-start(bf16[2960,128]{1,0:T(8,128)(2,1)S(1)} %get-tuple-element.38), channel_id=1, source_target_pairs={{1,0},{0,1},{3,2},{2,3},{5,4},{4,5},{7,6},{6,7},{9,8},{8,9},{11,10... | collective-permute-start | bytes 2273288 | tf_op jit(solution)/shard_map/ppermute | solution.py:37
  38.0 6.9 %collective-permute-start.14 = (bf16[640,128]{1,0:T(8,128)(2,1)S(1)}, bf16[640,128]{1,0:T(8,128)(2,1)S(1)}, u32[]{:S(2)}, u32[]{:S(2)}) collective-permute-start(bf16[640,128]{1,0:T(8,128)(2,1)S(1)} %get-tuple-element.37), channel_id=1, source_target_pairs={{2,0},{3,1},{0,2},{1,3},{6,4},{7,5},{4,6},{5,7},{10,8},{11,9},{8,1... | collective-permute-start | bytes 491528 | tf_op jit(solution)/shard_map/ppermute | solution.py:37
  39.6 6.3 %collective-permute-start.13 = (bf16[640,128]{1,0:T(8,128)(2,1)S(1)}, bf16[640,128]{1,0:T(8,128)(2,1)S(1)}, u32[]{:S(2)}, u32[]{:S(2)}) collective-permute-start(bf16[640,128]{1,0:T(8,128)(2,1)S(1)} %get-tuple-element.32.refs_4_.refs_15_), channel_id=1, source_target_pairs={{16,0},{0,16},{17,1},{1,17},{18,2},{2,18},{19,3},{3,19},{20,4},{4,... | collective-permute-start | bytes 491528 | tf_op jit(solution)/shard_map/ppermute | solution.py:26
  40.1 4.6 %collective-permute-start.16 = (bf16[96,128]{1,0:T(8,128)(2,1)S(1)}, bf16[96,128]{1,0:T(8,128)(2,1)S(1)}, u32[]{:S(2)}, u32[]{:S(2)}) collective-permute-start(bf16[96,128]{1,0:T(8,128)(2,1)S(1)} %get-tuple-element.39.refs_0_), channel_id=1, source_target_pairs={{3,0},{2,1},{1,2},{0,3},{7,4},{6,5},{5,6},{4,7},{11,8},{10,9},{9,1... | collective-permute-start | bytes 73736 | tf_op jit(solution)/shard_map/ppermute | solution.py:37
  45.9 1.7 %collective-permute-start.17 = (bf16[1280,128]{1,0:T(8,128)(2,1)S(1)}, bf16[1280,128]{1,0:T(8,128)(2,1)S(1)}, u32[]{:S(2)}, u32[]{:S(2)}) collective-permute-start(bf16[1280,128]{1,0:T(8,128)(2,1)S(1)} %pack_four.1), channel_id=1, source_target_pairs={{1,0},{0,1},{3,2},{2,3},{5,4},{4,5},{7,6},{6,7},{9,8},{8,9},{11,10... | collective-permute-start | bytes 983048 | tf_op jit(solution)/shard_map/ppermute | solution.py:37
  52.6 3.0 %collective-permute-start.19 = (f32[8,128]{1,0:T(8,128)S(1)}, f32[8,128]{1,0:T(8,128)S(1)}, u32[]{:S(2)}, u32[]{:S(2)}) collective-permute-start(f32[8,128]{1,0:T(8,128)S(1)} %get-tuple-element.41), channel_id=1, source_target_pairs={{3,0},{2,1},{1,2},{0,3},{7,4},{6,5},{5,6},{4,7},{11,8},{10,9},{9,1... | collective-permute-start | bytes 12296 | tf_op jit(solution)/shard_map/ppermute | solution.py:37
  52.8 2.8 %collective-permute-start.18 = (f32[8,128]{1,0:T(8,128)S(1)}, f32[8,128]{1,0:T(8,128)S(1)}, u32[]{:S(2)}, u32[]{:S(2)}) collective-permute-start(f32[8,128]{1,0:T(8,128)S(1)} %get-tuple-element.41), channel_id=1, source_target_pairs={{1,0},{0,1},{3,2},{2,3},{5,4},{4,5},{7,6},{6,7},{9,8},{8,9},{11,10... | collective-permute-start | bytes 12296 | tf_op jit(solution)/shard_map/ppermute | solution.py:37
  55.8 3.6 %collective-permute-start.20 = (f32[8,128]{1,0:T(8,128)S(1)}, f32[8,128]{1,0:T(8,128)S(1)}, u32[]{:S(2)}, u32[]{:S(2)}) collective-permute-start(f32[8,128]{1,0:T(8,128)S(1)} %pad_maximum_fusion.1), channel_id=1, source_target_pairs={{16,0},{0,16},{17,1},{1,17},{18,2},{2,18},{19,3},{3,19},{20,4},{4,... | collective-permute-start | bytes 12296 | tf_op jit(solution)/shard_map/ppermute | solution.py:26
  59.5 6.1 %collective-permute-start.22 = (f32[16,128]{1,0:T(8,128)S(1)}, f32[16,128]{1,0:T(8,128)S(1)}, u32[]{:S(2)}, u32[]{:S(2)}) collective-permute-start(f32[16,128]{1,0:T(8,128)S(1)} %pad_maximum_fusion.refs_0_), channel_id=1, source_target_pairs={{4,0},{0,4},{12,8},{8,12},{5,1},{1,5},{13,9},{9,13},{6,2},{2,6},{1... | collective-permute-start | bytes 24584 | tf_op jit(solution)/shard_map/ppermute | solution.py:32
  60.1 5.5 %collective-permute-start.21 = (f32[16,128]{1,0:T(8,128)S(1)}, f32[16,128]{1,0:T(8,128)S(1)}, u32[]{:S(2)}, u32[]{:S(2)}) collective-permute-start(f32[16,128]{1,0:T(8,128)S(1)} %pad_maximum_fusion.refs_0_), channel_id=1, source_target_pairs={{12,0},{8,4},{4,8},{0,12},{13,1},{9,5},{5,9},{1,13},{14,2},{10,6},... | collective-permute-start | bytes 24584 | tf_op jit(solution)/shard_map/ppermute | solution.py:32

commit v16 on v15

--- a/solution.py
+++ b/solution.py
@@ -92,7 +92,7 @@
 
 
 def pick_kernel(axes, *refs):
-    sign_ref, out_ref, geo_ref, neighbors_ref, extent_ref, x_ref, y_ref, z_ref, place_ref, tile, loads, sems = refs[5:]
+    sign_ref, out_ref, geo_ref, neighbors_ref, extent_ref, x_ref, y_ref, z_ref, place_ref, loads, sems = refs[5:]
     at = Places(*axes)
     slots = sign_ref.shape[0]
     n_pick = place_ref.shape[0] - 1
@@ -126,10 +126,7 @@
         geo = jnp.where(lane_pair == rank, values, geo)
     geo = geo.astype(jnp.float32).astype(out_ref.dtype)
     geo_ref[...] = geo
-    tile[...] = geo
-    copy = pltpu.make_async_copy(tile, out_ref.at[pl.ds(n_pick * size, GEO)], sems.at[n_pick])
-    copy.start()
-    copies.append(copy)
+    out_ref[n_pick * size :] = geo
     for copy in copies:
         copy.wait()
 
@@ -457,7 +454,7 @@
             jax.ShapeDtypeStruct((GEO, LANES), own.dtype),
         ),
         in_specs=[HBM] * 6,
-        out_specs=(HBM, VMEM),
+        out_specs=(VMEM, VMEM),
         scratch_shapes=[
             pltpu.SMEM((slots, atoms), jnp.int32),
             pltpu.SMEM((1, slots), jnp.int32),
@@ -465,9 +462,8 @@
             pltpu.SMEM((atoms,), jnp.int32),
             pltpu.SMEM((atoms,), jnp.int32),
             pltpu.SMEM((n_pick + 1,), jnp.int32),
-            pltpu.VMEM((GEO, LANES), jnp.bfloat16),
             pltpu.SemaphoreType.DMA((5,)),
-            pltpu.SemaphoreType.DMA((n_pick + 1,)),
+            pltpu.SemaphoreType.DMA((n_pick,)),
         ],
         compiler_params=pltpu.CompilerParams(vmem_limit_bytes=60 << 20),
         name="pick_column_blocks",

time: 67.3 us -> 62.2 us (0.924)
  Pallas kernels: 25.2 us -> 19.7 us
  starting transfers between devices: 18.2 us -> 19.4 us
  waiting for transfers between devices: 21.8 us -> 20.9 us
    pallas_call x1, Pallas kernels: 7.66 us -> 2.48 us  [local(): pl.pallas_call(functools.partial(pick_kernel, axes), out_shape=(jax.Shape...]
    ppermute x4, waiting for transfers between devices: 7.45 us -> 3.87 us  [from_column(): lax.ppermute(x, 'col', [((i + step[i]) % count, i) for i in range(count)])]
    ppermute x14, waiting for transfers between devices: 10.1 us -> 11.7 us  [from_layer(): return lax.ppermute(x, 'layer', [(i ^ flip, i) for i in range(count)])]
    ppermute x14, starting transfers between devices: 5.7 us -> 6.87 us  [from_layer(): return lax.ppermute(x, 'layer', [(i ^ flip, i) for i in range(count)])]
    ppermute x5, waiting for transfers between devices: 4.29 us -> 5.36 us  [from_offset(): lax.ppermute(x, axis, [((i + step) % count, i) for i in range(count)])]
  transfers between devices with their start and end apart: 23 -> 23, of which waited for: 10 -> 12; matrix products, arithmetic and copies ran while one was open for 0% -> 0% of each run, Pallas kernels for 28% -> 21%
where the time goes in v16:
time: 62.2 us; the launch traced here: 61.9 us
  waiting for transfers between devices  20.9 us (34%)
  Pallas kernels  19.7 us (32%)
  starting transfers between devices  19.4 us (31%)
  local copies, waits for them, and re-layouts  0.85 us (1%)
  between operations  0.8 us (1%)
    ppermute x14, waiting for transfers between devices, from_layer(): return lax.ppermute(x, 'layer', [(i ^ flip, i) for i in range(count)])  11.7 us
    ppermute x4, starting transfers between devices, from_column(): lax.ppermute(x, 'col', [((i + step[i]) % count, i) for i in range(count)])  7.35 us
    ppermute x14, starting transfers between devices, from_layer(): return lax.ppermute(x, 'layer', [(i ^ flip, i) for i in range(count)])  6.87 us
    ppermute x5, waiting for transfers between devices, from_offset(): lax.ppermute(x, axis, [((i + step) % count, i) for i in range(count)])  5.36 us
    ppermute x5, starting transfers between devices, from_offset(): lax.ppermute(x, axis, [((i + step) % count, i) for i in range(count)])  5.2 us
    pallas_call x1, Pallas kernels, local(): pl.pallas_call(functools.partial(step_kernel, len(late_values)), out_shap...  4.88 us
    pallas_call x1, Pallas kernels, local(): pl.pallas_call(functools.partial(prepare_kernel, axes, count, tuple(layou...  3.97 us
    ppermute x4, waiting for transfers between devices, from_column(): lax.ppermute(x, 'col', [((i + step[i]) % count, i) for i in range(count)])  3.87 us
  transfers between devices with their start and end apart: 23, of which 12 were waited for; matrix products, arithmetic and copies ran while one was open for 0% of the time, Pallas kernels for 21%

profile of v16, /device:TPU:0, one launch (start us, length us, event | category | flops | bytes accessed | tf_op | source)
XLA Modules:
  0.0 61.9 jit_solution(9930727769799623502)
XLA Ops:
  0.6 3.0 %collective-permute-start.3 = (bf16[1536,128]{1,0:T(8,128)(2,1)}, bf16[1536,128]{1,0:T(8,128)(2,1)S(1)}, u32[]{:S(2)}, u32[]{:S(2)}) collective-permute-start(bf16[1536,128]{1,0:T(8,128)(2,1)} %bitcast.10), channel_id=1, source_target_pairs={{16,0},{0,16},{17,1},{1,17},{18,2},{2,18},{19,3},{3,19},{20,4},{4,... | collective-permute-start | bytes 1179656 | tf_op jit(solution)/shard_map/ppermute | solution.py:26
  3.6 1.5 %collective-permute-start.2 = (bf16[1536,128]{1,0:T(8,128)(2,1)}, bf16[1536,128]{1,0:T(8,128)(2,1)S(1)}, u32[]{:S(2)}, u32[]{:S(2)}) collective-permute-start(bf16[1536,128]{1,0:T(8,128)(2,1)} %bitcast.11), channel_id=1, source_target_pairs={{2,0},{3,1},{0,2},{1,3},{6,4},{7,5},{4,6},{5,7},{10,8},{11,9},{8,1... | collective-permute-start | bytes 1179656 | tf_op jit(solution)/shard_map/ppermute | solution.py:37
  5.2 0.0 collective-permute-start.4
  5.2 2.5 %pick_column_blocks.1 = (bf16[656,128]{1,0:T(8,128)(2,1)}, bf16[16,128]{1,0:T(8,128)(2,1)}) custom-call(s32[12,32]{1,0:T(8,128)} %bitcast.17, s32[1,12]{1,0:T(1,128)} %refs_1_.2, s32[32]{0:T(128)} %refs_2_.1, s32[32]{0:T(128)} %refs_3_.1, s32[32]{0:T(128)} %refs_4_.1, bf16[12,128,128]{2,1,0:T(8,128)(2,1)} %bitcast.13), custom_call_target="tpu_custom_call" | custom-call | tf_op jit(solution)/shard_map/pick_column_blocks/pallas_call | solution.py:450
  7.6 1.7 %collective-permute-start.1 = (bf16[656,128]{1,0:T(8,128)(2,1)}, bf16[656,128]{1,0:T(8,128)(2,1)S(1)}, u32[]{:S(2)}, u32[]{:S(2)}) collective-permute-start(bf16[656,128]{1,0:T(8,128)(2,1)} %get-tuple-element.23), channel_id=1, source_target_pairs={{4,0},{0,4},{12,8},{8,12},{5,1},{1,5},{13,9},{9,13},{6,2},{2,6},{1... | collective-permute-start | bytes 503816 | tf_op jit(solution)/shard_map/ppermute | solution.py:32
  9.3 2.5 %collective-permute-start = (bf16[656,128]{1,0:T(8,128)(2,1)}, bf16[656,128]{1,0:T(8,128)(2,1)S(1)}, u32[]{:S(2)}, u32[]{:S(2)}) collective-permute-start(bf16[656,128]{1,0:T(8,128)(2,1)} %get-tuple-element.23), channel_id=1, source_target_pairs={{12,0},{8,4},{4,8},{0,12},{13,1},{9,5},{5,9},{1,13},{14,2},{10,6},... | collective-permute-start | bytes 503816 | tf_op jit(solution)/shard_map/ppermute | solution.py:32
  11.8 1.2 %collective-permute-done.3.refs_4_.refs_1_.refs_6_ = bf16[1536,128]{1,0:T(8,128)(2,1)S(1)} collective-permute-done((bf16[1536,128]{1,0:T(8,128)(2,1)}, bf16[1536,128]{1,0:T(8,128)(2,1)S(1)}, u32[]{:S(2)}, u32[]{:S(2)}) %collective-permute-start.3) | collective-permute-done | bytes 393248 | tf_op jit(solution)/shard_map/ppermute | solution.py:26
  13.0 1.5 %collective-permute-done.2.refs_3_.refs_0_ = bf16[1536,128]{1,0:T(8,128)(2,1)S(1)} collective-permute-done((bf16[1536,128]{1,0:T(8,128)(2,1)}, bf16[1536,128]{1,0:T(8,128)(2,1)S(1)}, u32[]{:S(2)}, u32[]{:S(2)}) %collective-permute-start.2) | collective-permute-done | bytes 393248 | tf_op jit(solution)/shard_map/ppermute | solution.py:37
  14.4 0.4 collective-permute-start.7
  14.9 1.7 %collective-permute-start.8 = (bf16[640,128]{1,0:T(8,128)(2,1)S(1)}, bf16[640,128]{1,0:T(8,128)(2,1)S(1)}, u32[]{:S(2)}, u32[]{:S(2)}) collective-permute-start(bf16[640,128]{1,0:T(8,128)(2,1)S(1)} %get-tuple-element.31), channel_id=1, source_target_pairs={{2,0},{3,1},{0,2},{1,3},{6,4},{7,5},{4,6},{5,7},{10,8},{11,9},{8,1... | collective-permute-start | bytes 491528 | tf_op jit(solution)/shard_map/ppermute | solution.py:37
  16.6 0.0 collective-permute-done.1.refs_1_.refs_0_.refs_4_
  16.6 3.8 %collective-permute-done.refs_0_.refs_1_.refs_5_ = bf16[656,128]{1,0:T(8,128)(2,1)S(1)} collective-permute-done((bf16[656,128]{1,0:T(8,128)(2,1)}, bf16[656,128]{1,0:T(8,128)(2,1)S(1)}, u32[]{:S(2)}, u32[]{:S(2)}) %collective-permute-start) | collective-permute-done | bytes 167968 | tf_op jit(solution)/shard_map/ppermute | solution.py:32
  20.4 0.1 collective-permute-start.10
  20.5 0.0 collective-permute-done.4.refs_5_.refs_2_
  20.5 0.0 copy-start.3
  20.5 0.7 %copy-done.3 = bf16[16,128]{1,0:T(8,128)(2,1)S(1)} copy-done((bf16[16,128]{1,0:T(8,128)(2,1)S(1)}, bf16[16,128]{1,0:T(8,128)(2,1)}, u32[]{:S(2)}) %copy-start.3) | copy-done | bytes 4120
  21.2 0.1 pack_two.1
  21.3 0.6 collective-permute-start.5
  21.8 0.5 collective-permute-start.6
  22.4 0.0 collective-permute-done.7.refs_0_.refs_9_
  22.4 0.0 collective-permute-start.12
  22.4 0.0 collective-permute-done.8.refs_1_.refs_10_
  22.4 0.5 collective-permute-start.11
  22.9 0.0 copy-start
  22.9 0.0 copy-start.2
  22.9 0.0 collective-permute-done.10.refs_4_.refs_14_
  22.9 0.1 collective-permute-start.9
  23.1 0.0 copy-done.1
  23.1 4.0 %prepare.1 = (s32[83]{0:T(128)S(1)}, s32[83]{0:T(128)S(1)}, s32[14]{0:T(128)S(1)}) custom-call(s32[12,32]{1,0:T(8,128)S(1)} %bitcast.18, s32[32]{0:T(128)S(1)} %copy-done.4, bf16[1456,128]{1,0:T(8,128)(2,1)S(1)} %get-tuple-element.25.refs_2_), custom_call_target="tpu_custom_call" | custom-call | flops 1000 | bytes 1000 | tf_op jit(solution)/shard_map/prepare/pallas_call | solution.py:584
  27.1 5.3 %collective-permute-done.5.refs_0_.refs_12_ = bf16[1456,128]{1,0:T(8,128)(2,1)S(1)} collective-permute-done((bf16[1456,128]{1,0:T(8,128)(2,1)S(1)}, bf16[1456,128]{1,0:T(8,128)(2,1)S(1)}, u32[]{:S(2)}, u32[]{:S(2)}) %collective-permute-start.5) | collective-permute-done | bytes 372768 | tf_op jit(solution)/shard_map/ppermute | solution.py:37
  32.4 0.2 collective-permute-done.6.refs_2_.refs_11_
  32.6 0.0 collective-permute-done.12.refs_6_.refs_7_
  32.6 0.0 collective-permute-done.11.refs_5_.refs_8_
  32.6 0.0 collective-permute-done.9.refs_3_.refs_13_
  32.6 0.1 pack_three.1
  32.7 0.1 collective-permute-start.15
  32.8 1.6 %collective-permute-start.14 = (bf16[640,128]{1,0:T(8,128)(2,1)S(1)}, bf16[640,128]{1,0:T(8,128)(2,1)S(1)}, u32[]{:S(2)}, u32[]{:S(2)}) collective-permute-start(bf16[640,128]{1,0:T(8,128)(2,1)S(1)} %get-tuple-element.37), channel_id=1, source_target_pairs={{2,0},{3,1},{0,2},{1,3},{6,4},{7,5},{4,6},{5,7},{10,8},{11,9},{8,1... | collective-permute-start | bytes 491528 | tf_op jit(solution)/shard_map/ppermute | solution.py:37
  34.4 0.6 collective-permute-start.13
  35.0 0.0 collective-permute-start.16
  35.0 1.7 %spread_basis.1 = (bf16[128,1536]{1,0:T(8,128)(2,1)S(1)}, bf16[16,128]{1,0:T(8,128)(2,1)S(1)}, bf16[128,1536]{1,0:T(8,128)(2,1)S(1)}) custom-call(s32[12,32]{1,0:T(8,128)S(1)} %bitcast.19, bf16[192,128]{1,0:T(8,128)(2,1)S(1)} %bitcast.20, s32[14]{0:T(128)S(1)} %get-tuple-element.27.refs_7_.refs_2_.refs_1_, bf16[12,128,128]{2,1,0:T(8,128)(2,1)S(1)} %bitcast.14, ...), custom_call_target="tpu_custom_call" | custom-call | flops 1000 | bytes 1000 | tf_op jit(solution)/shard_map/spread_basis/pallas_call | solution.py:633
  36.7 2.1 %gram_early.1.refs_2_.refs_5_ = bf16[1536,1536]{1,0:T(8,128)(2,1)S(1)} custom-call(s32[83]{0:T(128)S(1)} %get-tuple-element.36.refs_0_, bf16[1536,128]{1,0:T(8,128)(2,1)S(1)} %bitcast.15, bf16[1536,128]{1,0:T(8,128)(2,1)S(1)} %collective-permute-done.4.refs_5_.refs_2_, bf16[1536,128]{1,0:T(8,128)(2,1)S(1)} %collective-permute-done.2.refs_3_.refs_0_, ...), custom_call_target="tpu_custom_call" | custom-call | flops 1000 | bytes 1000 | tf_op jit(solution)/shard_map/gram_early/pallas_call | solution.py:649
  38.8 0.7 %collective-permute-done.16.refs_3_.refs_2_ = bf16[96,128]{1,0:T(8,128)(2,1)S(1)} collective-permute-done((bf16[96,128]{1,0:T(8,128)(2,1)S(1)}, bf16[96,128]{1,0:T(8,128)(2,1)S(1)}, u32[]{:S(2)}, u32[]{:S(2)}) %collective-permute-start.16) | collective-permute-done | bytes 24608 | tf_op jit(solution)/shard_map/ppermute | solution.py:37
  39.5 0.2 collective-permute-done.14.refs_1_.refs_7_
  39.7 1.0 %collective-permute-done.13.refs_0_.refs_6_ = bf16[640,128]{1,0:T(8,128)(2,1)S(1)} collective-permute-done((bf16[640,128]{1,0:T(8,128)(2,1)S(1)}, bf16[640,128]{1,0:T(8,128)(2,1)S(1)}, u32[]{:S(2)}, u32[]{:S(2)}) %collective-permute-start.13) | collective-permute-done | bytes 163872 | tf_op jit(solution)/shard_map/ppermute | solution.py:26
  40.7 0.1 collective-permute-start.17
  40.8 1.6 %collective-permute-done.17.refs_9_ = bf16[1280,128]{1,0:T(8,128)(2,1)S(1)} collective-permute-done((bf16[1280,128]{1,0:T(8,128)(2,1)S(1)}, bf16[1280,128]{1,0:T(8,128)(2,1)S(1)}, u32[]{:S(2)}, u32[]{:S(2)}) %collective-permute-start.17) | collective-permute-done | bytes 327712 | tf_op jit(solution)/shard_map/ppermute | solution.py:37
  42.4 0.0 collective-permute-done.15.refs_8_.refs_1_
  42.4 4.9 %square_cube_coefficients.1 = (bf16[12,128,128]{2,1,0:T(8,128)(2,1)}, f32[8,128]{1,0:T(8,128)S(1)}) custom-call(s32[83]{0:T(128)S(1)} %get-tuple-element.26.refs_0_, s32[14]{0:T(128)S(1)} %get-tuple-element.27.refs_7_.refs_2_.refs_1_, bf16[16,128]{1,0:T(8,128)(2,1)S(1)} %get-tuple-element.33.refs_4_.refs_2_, ...), custom_call_target="tpu_custom_call" | custom-call | flops 1300000000 | bytes 8000000 | tf_op jit(solution)/shard_map/square_cube_coefficients/pallas_call | solution.py:686
  47.3 0.3 collective-permute-start.19
  47.6 0.4 collective-permute-start.18
  47.9 2.4 %collective-permute-done.19 = f32[8,128]{1,0:T(8,128)S(1)} collective-permute-done((f32[8,128]{1,0:T(8,128)S(1)}, f32[8,128]{1,0:T(8,128)S(1)}, u32[]{:S(2)}, u32[]{:S(2)}) %collective-permute-start.19) | collective-permute-done | bytes 4128 | tf_op jit(solution)/shard_map/ppermute | solution.py:37
  50.3 0.0 collective-permute-done.18
  50.3 0.1 slice.10
  50.4 0.1 slice.11
  50.5 0.1 pad_maximum_fusion.1
  50.6 0.7 %collective-permute-start.20 = (f32[8,128]{1,0:T(8,128)S(1)}, f32[8,128]{1,0:T(8,128)S(1)}, u32[]{:S(2)}, u32[]{:S(2)}) collective-permute-start(f32[8,128]{1,0:T(8,128)S(1)} %pad_maximum_fusion.1), channel_id=1, source_target_pairs={{16,0},{0,16},{17,1},{1,17},{18,2},{2,18},{19,3},{3,19},{20,4},{4,... | collective-permute-start | bytes 12296 | tf_op jit(solution)/shard_map/ppermute | solution.py:26
  51.2 3.0 %collective-permute-done.20 = f32[8,128]{1,0:T(8,128)S(1)} collective-permute-done((f32[8,128]{1,0:T(8,128)S(1)}, f32[8,128]{1,0:T(8,128)S(1)}, u32[]{:S(2)}, u32[]{:S(2)}) %collective-permute-start.20) | collective-permute-done | bytes 4128 | tf_op jit(solution)/shard_map/ppermute | solution.py:26
  54.2 0.1 pad_maximum_fusion.refs_0_
  54.2 0.7 %collective-permute-start.22 = (f32[16,128]{1,0:T(8,128)S(1)}, f32[16,128]{1,0:T(8,128)S(1)}, u32[]{:S(2)}, u32[]{:S(2)}) collective-permute-start(f32[16,128]{1,0:T(8,128)S(1)} %pad_maximum_fusion.refs_0_), channel_id=1, source_target_pairs={{4,0},{0,4},{12,8},{8,12},{5,1},{1,5},{13,9},{9,13},{6,2},{2,6},{1... | collective-permute-start | bytes 24584 | tf_op jit(solution)/shard_map/ppermute | solution.py:32
  55.0 2.5 %collective-permute-start.21 = (f32[16,128]{1,0:T(8,128)S(1)}, f32[16,128]{1,0:T(8,128)S(1)}, u32[]{:S(2)}, u32[]{:S(2)}) collective-permute-start(f32[16,128]{1,0:T(8,128)S(1)} %pad_maximum_fusion.refs_0_), channel_id=1, source_target_pairs={{12,0},{8,4},{4,8},{0,12},{13,1},{9,5},{5,9},{1,13},{14,2},{10,6},... | collective-permute-start | bytes 24584 | tf_op jit(solution)/shard_map/ppermute | solution.py:32
  57.5 2.8 %profiles.1 = (bf16[6,6,256,128]{3,2,1,0:T(8,128)(2,1)S(1)}, bf16[6,6,128,128]{3,2,1,0:T(8,128)(2,1)S(1)}) custom-call(bf16[96,128]{1,0:T(8,128)(2,1)S(1)} %get-tuple-element.39.refs_0_, bf16[2960,128]{1,0:T(8,128)(2,1)S(1)} %collective-permute-done.15.refs_8_.refs_1_, bf16[96,128]{1,0:T(8,128)(2,1)S(1)} %collective-permute-done.16.refs_3_.refs_2_), custom_call_target="tpu_custom_call" | custom-call | flops 1000 | bytes 1000 | tf_op jit(solution)/shard_map/profiles/pallas_call | solution.py:668
  60.3 0.0 collective-permute-done.22.refs_2_
  60.3 0.1 collective-permute-done.21.refs_1_
  60.4 1.5 %density.1 = f32[256,128]{1,0:T(8,128)} custom-call(f32[16,128]{1,0:T(8,128)S(1)} %pad_maximum_fusion.refs_0_, f32[16,128]{1,0:T(8,128)S(1)} %collective-permute-done.21.refs_1_, f32[16,128]{1,0:T(8,128)S(1)} %collective-permute-done.22.refs_2_, bf16[6,6,256,128]{3,2,1,0:T(8,128)(2,1)S(1)} %get-tuple-element.42.refs_3_, bf16[4608,128]{1,0:T(8,128)(2,1)S(1)} %bitcast.16), custom_call_target="tpu_custom_call" | custom-call | flops 310000000 | bytes 4000000 | tf_op jit(solution)/shard_map/density/pallas_call | solution.py:722
  (11 shorter events, 0.1 us)
Async XLA Ops:
  0.6 12.3 %collective-permute-start.3 = (bf16[1536,128]{1,0:T(8,128)(2,1)}, bf16[1536,128]{1,0:T(8,128)(2,1)S(1)}, u32[]{:S(2)}, u32[]{:S(2)}) collective-permute-start(bf16[1536,128]{1,0:T(8,128)(2,1)} %bitcast.10), channel_id=1, source_target_pairs={{16,0},{0,16},{17,1},{1,17},{18,2},{2,18},{19,3},{3,19},{20,4},{4,... | collective-permute-start | bytes 1179656 | tf_op jit(solution)/shard_map/ppermute | solution.py:26
  3.6 10.8 %collective-permute-start.2 = (bf16[1536,128]{1,0:T(8,128)(2,1)}, bf16[1536,128]{1,0:T(8,128)(2,1)S(1)}, u32[]{:S(2)}, u32[]{:S(2)}) collective-permute-start(bf16[1536,128]{1,0:T(8,128)(2,1)} %bitcast.11), channel_id=1, source_target_pairs={{2,0},{3,1},{0,2},{1,3},{6,4},{7,5},{4,6},{5,7},{10,8},{11,9},{8,1... | collective-permute-start | bytes 1179656 | tf_op jit(solution)/shard_map/ppermute | solution.py:37
  5.2 15.3 %collective-permute-start.4 = (bf16[1536,128]{1,0:T(8,128)(2,1)}, bf16[1536,128]{1,0:T(8,128)(2,1)S(1)}, u32[]{:S(2)}, u32[]{:S(2)}) collective-permute-start(bf16[1536,128]{1,0:T(8,128)(2,1)} %bitcast.12), channel_id=1, source_target_pairs={{1,0},{0,1},{3,2},{2,3},{5,4},{4,5},{7,6},{6,7},{9,8},{8,9},{11,10... | collective-permute-start | bytes 1179656 | tf_op jit(solution)/shard_map/ppermute | solution.py:37
  7.6 8.9 %collective-permute-start.1 = (bf16[656,128]{1,0:T(8,128)(2,1)}, bf16[656,128]{1,0:T(8,128)(2,1)S(1)}, u32[]{:S(2)}, u32[]{:S(2)}) collective-permute-start(bf16[656,128]{1,0:T(8,128)(2,1)} %get-tuple-element.23), channel_id=1, source_target_pairs={{4,0},{0,4},{12,8},{8,12},{5,1},{1,5},{13,9},{9,13},{6,2},{2,6},{1... | collective-permute-start | bytes 503816 | tf_op jit(solution)/shard_map/ppermute | solution.py:32
  9.3 11.0 %collective-permute-start = (bf16[656,128]{1,0:T(8,128)(2,1)}, bf16[656,128]{1,0:T(8,128)(2,1)S(1)}, u32[]{:S(2)}, u32[]{:S(2)}) collective-permute-start(bf16[656,128]{1,0:T(8,128)(2,1)} %get-tuple-element.23), channel_id=1, source_target_pairs={{12,0},{8,4},{4,8},{0,12},{13,1},{9,5},{5,9},{1,13},{14,2},{10,6},... | collective-permute-start | bytes 503816 | tf_op jit(solution)/shard_map/ppermute | solution.py:32
  14.4 7.9 %collective-permute-start.7 = (bf16[640,128]{1,0:T(8,128)(2,1)S(1)}, bf16[640,128]{1,0:T(8,128)(2,1)S(1)}, u32[]{:S(2)}, u32[]{:S(2)}) collective-permute-start(bf16[640,128]{1,0:T(8,128)(2,1)S(1)} %get-tuple-element.30), channel_id=1, source_target_pairs={{16,0},{0,16},{17,1},{1,17},{18,2},{2,18},{19,3},{3,19},{20,4},{4,... | collective-permute-start | bytes 491528 | tf_op jit(solution)/shard_map/ppermute | solution.py:26
  14.9 7.5 %collective-permute-start.8 = (bf16[640,128]{1,0:T(8,128)(2,1)S(1)}, bf16[640,128]{1,0:T(8,128)(2,1)S(1)}, u32[]{:S(2)}, u32[]{:S(2)}) collective-permute-start(bf16[640,128]{1,0:T(8,128)(2,1)S(1)} %get-tuple-element.31), channel_id=1, source_target_pairs={{2,0},{3,1},{0,2},{1,3},{6,4},{7,5},{4,6},{5,7},{10,8},{11,9},{8,1... | collective-permute-start | bytes 491528 | tf_op jit(solution)/shard_map/ppermute | solution.py:37
  20.4 2.6 %collective-permute-start.10 = (bf16[1280,128]{1,0:T(8,128)(2,1)S(1)}, bf16[1280,128]{1,0:T(8,128)(2,1)S(1)}, u32[]{:S(2)}, u32[]{:S(2)}) collective-permute-start(bf16[1280,128]{1,0:T(8,128)(2,1)S(1)} %pack_mate_sides.1), channel_id=1, source_target_pairs={{1,0},{0,1},{3,2},{2,3},{5,4},{4,5},{7,6},{6,7},{9,8},{8,9},{11,10... | collective-permute-start | bytes 983048 | tf_op jit(solution)/shard_map/ppermute | solution.py:37
  20.5 0.7 %copy-start.3 = (bf16[16,128]{1,0:T(8,128)(2,1)S(1)}, bf16[16,128]{1,0:T(8,128)(2,1)}, u32[]{:S(2)}) copy-start(bf16[16,128]{1,0:T(8,128)(2,1)} %get-tuple-element.24.refs_2_) | copy-start | bytes 12292
  21.3 11.1 %collective-permute-start.5 = (bf16[1456,128]{1,0:T(8,128)(2,1)S(1)}, bf16[1456,128]{1,0:T(8,128)(2,1)S(1)}, u32[]{:S(2)}, u32[]{:S(2)}) collective-permute-start(bf16[1456,128]{1,0:T(8,128)(2,1)S(1)} %get-tuple-element.28), channel_id=1, source_target_pairs={{2,0},{3,1},{0,2},{1,3},{6,4},{7,5},{4,6},{5,7},{10,8},{11,9},{8,1... | collective-permute-start | bytes 1118216 | tf_op jit(solution)/shard_map/ppermute | solution.py:37
  21.8 1.3 %copy-start.1 = (s32[32,12]{0,1:T(8,128)S(1)}, s32[32,12]{0,1:T(8,128)}, u32[]{:S(2)}) copy-start(s32[32,12]{0,1:T(8,128)} %param.9) | copy-start | bytes 4612
  21.8 1.3 %copy-start.4 = (s32[32]{0:T(128)S(1)}, s32[32]{0:T(128)}, u32[]{:S(2)}) copy-start(s32[32]{0:T(128)} %refs_1_.3) | copy-start | bytes 388
  21.8 10.8 %collective-permute-start.6 = (bf16[1456,128]{1,0:T(8,128)(2,1)S(1)}, bf16[1456,128]{1,0:T(8,128)(2,1)S(1)}, u32[]{:S(2)}, u32[]{:S(2)}) collective-permute-start(bf16[1456,128]{1,0:T(8,128)(2,1)S(1)} %get-tuple-element.25.refs_2_), channel_id=1, source_target_pairs={{16,0},{0,16},{17,1},{1,17},{18,2},{2,18},{19,3},{3,19},{20,4},{4,... | collective-permute-start | bytes 1118216 | tf_op jit(solution)/shard_map/ppermute | solution.py:26
  22.4 10.3 %collective-permute-start.12 = (bf16[1536,128]{1,0:T(8,128)(2,1)S(1)}, bf16[1536,128]{1,0:T(8,128)(2,1)S(1)}, u32[]{:S(2)}, u32[]{:S(2)}) collective-permute-start(bf16[1536,128]{1,0:T(8,128)(2,1)S(1)} %collective-permute-done.3.refs_4_.refs_1_.refs_6_), channel_id=1, source_target_pairs={{1,0},{0,1},{3,2},{2,3},{5,4},{4,5},{7,6},{6,7},{9,8},{8,9},{11,10... | collective-permute-start | bytes 1179656 | tf_op jit(solution)/shard_map/ppermute | solution.py:37
  22.4 10.2 %collective-permute-start.11 = (bf16[1536,128]{1,0:T(8,128)(2,1)S(1)}, bf16[1536,128]{1,0:T(8,128)(2,1)S(1)}, u32[]{:S(2)}, u32[]{:S(2)}) collective-permute-start(bf16[1536,128]{1,0:T(8,128)(2,1)S(1)} %collective-permute-done.2.refs_3_.refs_0_), channel_id=1, source_target_pairs={{1,0},{0,1},{3,2},{2,3},{5,4},{4,5},{7,6},{6,7},{9,8},{8,9},{11,10... | collective-permute-start | bytes 1179656 | tf_op jit(solution)/shard_map/ppermute | solution.py:37
  22.9 12.1 %copy-start = (bf16[1,12,128,128]{3,2,1,0:T(8,128)(2,1)S(1)}, bf16[1,12,128,128]{3,2,1,0:T(8,128)(2,1)}, u32[]{:S(2)}) copy-start(bf16[1,12,128,128]{3,2,1,0:T(8,128)(2,1)} %param.8) | copy-start | bytes 1179652
  22.9 12.0 %copy-start.2 = (bf16[32,6,128]{2,0,1:T(8,128)(2,1)S(1)}, bf16[32,6,128]{2,0,1:T(8,128)(2,1)}, u32[]{:S(2)}) copy-start(bf16[32,6,128]{2,0,1:T(8,128)(2,1)} %param.11) | copy-start | bytes 147460
  22.9 9.7 %collective-permute-start.9 = (bf16[1280,128]{1,0:T(8,128)(2,1)S(1)}, bf16[1280,128]{1,0:T(8,128)(2,1)S(1)}, u32[]{:S(2)}, u32[]{:S(2)}) collective-permute-start(bf16[1280,128]{1,0:T(8,128)(2,1)S(1)} %pack_two_mate.1), channel_id=1, source_target_pairs={{1,0},{0,1},{3,2},{2,3},{5,4},{4,5},{7,6},{6,7},{9,8},{8,9},{11,10... | collective-permute-start | bytes 983048 | tf_op jit(solution)/shard_map/ppermute | solution.py:37
  32.7 9.7 %collective-permute-start.15 = (bf16[2960,128]{1,0:T(8,128)(2,1)S(1)}, bf16[2960,128]{1,0:T(8,128)(2,1)S(1)}, u32[]{:S(2)}, u32[]{:S(2)}) collective-permute-start(bf16[2960,128]{1,0:T(8,128)(2,1)S(1)} %get-tuple-element.38), channel_id=1, source_target_pairs={{1,0},{0,1},{3,2},{2,3},{5,4},{4,5},{7,6},{6,7},{9,8},{8,9},{11,10... | collective-permute-start | bytes 2273288 | tf_op jit(solution)/shard_map/ppermute | solution.py:37
  32.8 6.9 %collective-permute-start.14 = (bf16[640,128]{1,0:T(8,128)(2,1)S(1)}, bf16[640,128]{1,0:T(8,128)(2,1)S(1)}, u32[]{:S(2)}, u32[]{:S(2)}) collective-permute-start(bf16[640,128]{1,0:T(8,128)(2,1)S(1)} %get-tuple-element.37), channel_id=1, source_target_pairs={{2,0},{3,1},{0,2},{1,3},{6,4},{7,5},{4,6},{5,7},{10,8},{11,9},{8,1... | collective-permute-start | bytes 491528 | tf_op jit(solution)/shard_map/ppermute | solution.py:37
  34.4 6.3 %collective-permute-start.13 = (bf16[640,128]{1,0:T(8,128)(2,1)S(1)}, bf16[640,128]{1,0:T(8,128)(2,1)S(1)}, u32[]{:S(2)}, u32[]{:S(2)}) collective-permute-start(bf16[640,128]{1,0:T(8,128)(2,1)S(1)} %get-tuple-element.32.refs_4_.refs_15_), channel_id=1, source_target_pairs={{16,0},{0,16},{17,1},{1,17},{18,2},{2,18},{19,3},{3,19},{20,4},{4,... | collective-permute-start | bytes 491528 | tf_op jit(solution)/shard_map/ppermute | solution.py:26
  35.0 4.5 %collective-permute-start.16 = (bf16[96,128]{1,0:T(8,128)(2,1)S(1)}, bf16[96,128]{1,0:T(8,128)(2,1)S(1)}, u32[]{:S(2)}, u32[]{:S(2)}) collective-permute-start(bf16[96,128]{1,0:T(8,128)(2,1)S(1)} %get-tuple-element.39.refs_0_), channel_id=1, source_target_pairs={{3,0},{2,1},{1,2},{0,3},{7,4},{6,5},{5,6},{4,7},{11,8},{10,9},{9,1... | collective-permute-start | bytes 73736 | tf_op jit(solution)/shard_map/ppermute | solution.py:37
  40.7 1.7 %collective-permute-start.17 = (bf16[1280,128]{1,0:T(8,128)(2,1)S(1)}, bf16[1280,128]{1,0:T(8,128)(2,1)S(1)}, u32[]{:S(2)}, u32[]{:S(2)}) collective-permute-start(bf16[1280,128]{1,0:T(8,128)(2,1)S(1)} %pack_four.1), channel_id=1, source_target_pairs={{1,0},{0,1},{3,2},{2,3},{5,4},{4,5},{7,6},{6,7},{9,8},{8,9},{11,10... | collective-permute-start | bytes 983048 | tf_op jit(solution)/shard_map/ppermute | solution.py:37
  47.3 3.0 %collective-permute-start.19 = (f32[8,128]{1,0:T(8,128)S(1)}, f32[8,128]{1,0:T(8,128)S(1)}, u32[]{:S(2)}, u32[]{:S(2)}) collective-permute-start(f32[8,128]{1,0:T(8,128)S(1)} %get-tuple-element.41), channel_id=1, source_target_pairs={{3,0},{2,1},{1,2},{0,3},{7,4},{6,5},{5,6},{4,7},{11,8},{10,9},{9,1... | collective-permute-start | bytes 12296 | tf_op jit(solution)/shard_map/ppermute | solution.py:37
  47.6 2.7 %collective-permute-start.18 = (f32[8,128]{1,0:T(8,128)S(1)}, f32[8,128]{1,0:T(8,128)S(1)}, u32[]{:S(2)}, u32[]{:S(2)}) collective-permute-start(f32[8,128]{1,0:T(8,128)S(1)} %get-tuple-element.41), channel_id=1, source_target_pairs={{1,0},{0,1},{3,2},{2,3},{5,4},{4,5},{7,6},{6,7},{9,8},{8,9},{11,10... | collective-permute-start | bytes 12296 | tf_op jit(solution)/shard_map/ppermute | solution.py:37
  50.6 3.6 %collective-permute-start.20 = (f32[8,128]{1,0:T(8,128)S(1)}, f32[8,128]{1,0:T(8,128)S(1)}, u32[]{:S(2)}, u32[]{:S(2)}) collective-permute-start(f32[8,128]{1,0:T(8,128)S(1)} %pad_maximum_fusion.1), channel_id=1, source_target_pairs={{16,0},{0,16},{17,1},{1,17},{18,2},{2,18},{19,3},{3,19},{20,4},{4,... | collective-permute-start | bytes 12296 | tf_op jit(solution)/shard_map/ppermute | solution.py:26
  54.2 6.1 %collective-permute-start.22 = (f32[16,128]{1,0:T(8,128)S(1)}, f32[16,128]{1,0:T(8,128)S(1)}, u32[]{:S(2)}, u32[]{:S(2)}) collective-permute-start(f32[16,128]{1,0:T(8,128)S(1)} %pad_maximum_fusion.refs_0_), channel_id=1, source_target_pairs={{4,0},{0,4},{12,8},{8,12},{5,1},{1,5},{13,9},{9,13},{6,2},{2,6},{1... | collective-permute-start | bytes 24584 | tf_op jit(solution)/shard_map/ppermute | solution.py:32
  55.0 5.4 %collective-permute-start.21 = (f32[16,128]{1,0:T(8,128)S(1)}, f32[16,128]{1,0:T(8,128)S(1)}, u32[]{:S(2)}, u32[]{:S(2)}) collective-permute-start(f32[16,128]{1,0:T(8,128)S(1)} %pad_maximum_fusion.refs_0_), channel_id=1, source_target_pairs={{12,0},{8,4},{4,8},{0,12},{13,1},{9,5},{5,9},{1,13},{14,2},{10,6},... | collective-permute-start | bytes 24584 | tf_op jit(solution)/shard_map/ppermute | solution.py:32

commit v17 on v13

--- a/solution.py
+++ b/solution.py
@@ -100,9 +100,8 @@
     for i in range(n_pick + 1):
         place_ref[i] = 0
     load(refs[:5], (neighbors_ref, extent_ref, x_ref, y_ref, z_ref), loads)
-    ranks = own_ranks(at, neighbors_ref)
-    for w, (atom, _) in enumerate(ranks):
-        row, col, lay = at.split(atom)
+    for w in range(slots):
+        row, col, lay = at.split(neighbors_ref[w, at.me])
         place = target_place(at.n_row, (row - at.row) & (at.n_row - 1), (lay - at.lay) & (at.n_lay - 1), at.row)
         place_ref[jnp.where((col == at.col) & (place >= 0), place, n_pick)] = w
     copies = []
@@ -110,6 +109,7 @@
         copy = pltpu.make_async_copy(sign_ref.at[place_ref[i]], out_ref.at[pl.ds(i * size, size)], sems.at[i])
         copy.start()
         copies.append(copy)
+    ranks = own_ranks(at, neighbors_ref)
     sub = lax.broadcasted_iota(jnp.int32, (GEO, LANES), 0)
     lane_pair = lax.broadcasted_iota(jnp.int32, (GEO, LANES), 1) // SHELLS
     geo = jnp.zeros((GEO, LANES), jnp.int32)
@@ -405,7 +405,8 @@
 
 def density_kernel(column_steps, *refs):
     coef_refs = refs[:column_steps]
-    plane_ref, line_ref, out_ref, terms = refs[column_steps:]
+    plane_ref, line_ref = refs[column_steps : column_steps + 2]
+    out_ref, terms = refs[-2:]
     for o in range(plane_ref.shape[0]):
         coef = coef_refs[-o % column_steps]
         first = 8 * (o // column_steps)
@@ -712,17 +713,18 @@
     far_side = from_column(stacked, 1)
     received = [stacked, far_side, from_column(stacked, 0)]
 
+    given = pack([sign_next.reshape(full, size)], [[(0, 0, full)]], [], "give_sign")[0]
     density = pl.pallas_call(
         functools.partial(density_kernel, len(column_steps)),
         out_shape=jax.ShapeDtypeStruct((BX * BY, BZ), jnp.float32),
-        in_specs=[VMEM] * (len(received) + 2),
+        in_specs=[VMEM] * (len(received) + 2) + [ANY],
         out_specs=VMEM,
         scratch_shapes=[pltpu.VMEM((BX * BY, tiles * SHELLS * LANES), jnp.bfloat16)],
         compiler_params=pltpu.CompilerParams(vmem_limit_bytes=16 << 20),
         cost_estimate=pl.CostEstimate(flops=310_000_000, bytes_accessed=4_000_000, transcendentals=0),
         name="density",
-    )(*received, plane, line.reshape(tiles * SHELLS * LANES, BZ))
-    return sign_next[None], density.reshape(BX, BY, BZ)
+    )(*received, plane, line.reshape(tiles * SHELLS * LANES, BZ), given)
+    return given.reshape(1, slots, size, size), density.reshape(BX, BY, BZ)
 
 
 def solution(mesh):

time: 60.4 us -> 60.9 us (level)
  waiting for transfers between devices: 18.9 us -> 17.6 us
  local copies, waits for them, and re-layouts: 1.08 us -> 2.08 us
  Pallas kernels: 18.9 us -> 19.8 us
    unnamed x10 -> x12, local copies, waits for them, and re-layouts: 0.94 us -> 1.93 us
    pallas_call x5 -> x6, Pallas kernels: 0.28 us -> 1.05 us  [pack(): pl.pallas_call(functools.partial(pack_kernel, tuple(moves), inputs), out_...]
    ppermute x4, waiting for transfers between devices: 3.53 us -> 2.79 us  [from_column(): lax.ppermute(x, 'col', [((i + step[i]) % count, i) for i in range(count)])]
  transfers between devices with their start and end apart: 22 -> 22, of which waited for: 12 -> 11; matrix products, arithmetic and copies ran while one was open for 0% -> 0% of each run, Pallas kernels for 21% -> 23%
where the time goes in v17:
time: 60.9 us; the launch traced here: 60.7 us
  starting transfers between devices  20.2 us (33%)
  Pallas kernels  19.8 us (33%)
  waiting for transfers between devices  17.6 us (29%)
  local copies, waits for them, and re-layouts  2.08 us (3%)
  between operations  0.78 us (1%)
    ppermute x13, waiting for transfers between devices, from_layer(): return lax.ppermute(x, 'layer', [(i ^ flip, i) for i in range(count)])  11.2 us
    ppermute x13, starting transfers between devices, from_layer(): return lax.ppermute(x, 'layer', [(i ^ flip, i) for i in range(count)])  8.06 us
    ppermute x4, starting transfers between devices, from_column(): lax.ppermute(x, 'col', [((i + step[i]) % count, i) for i in range(count)])  6.4 us
    ppermute x5, starting transfers between devices, from_offset(): lax.ppermute(x, axis, [((i + step) % count, i) for i in range(count)])  5.74 us
    pallas_call x1, Pallas kernels, local(): pl.pallas_call(functools.partial(step_kernel, len(late_values)), out_shap...  4.57 us
    pallas_call x1, Pallas kernels, local(): pl.pallas_call(functools.partial(prepare_kernel, axes, count, tuple(layou...  4.23 us
    ppermute x5, waiting for transfers between devices, from_offset(): lax.ppermute(x, axis, [((i + step) % count, i) for i in range(count)])  3.7 us
    pallas_call x1, Pallas kernels, local(): pl.pallas_call(functools.partial(profile_kernel, periods, tile_steps, at[...  2.85 us
  transfers between devices with their start and end apart: 22, of which 11 were waited for; matrix products, arithmetic and copies ran while one was open for 0% of the time, Pallas kernels for 23%

profile of v17, /device:TPU:0, one launch (start us, length us, event | category | flops | bytes accessed | tf_op | source)
XLA Modules:
  0.0 60.7 jit_solution(3426956119775248920)
XLA Ops:
  0.6 3.0 %collective-permute-start.2 = (bf16[1536,128]{1,0:T(8,128)(2,1)}, bf16[1536,128]{1,0:T(8,128)(2,1)S(1)}, u32[]{:S(2)}, u32[]{:S(2)}) collective-permute-start(bf16[1536,128]{1,0:T(8,128)(2,1)} %bitcast.11), channel_id=1, source_target_pairs={{2,0},{3,1},{0,2},{1,3},{6,4},{7,5},{4,6},{5,7},{10,8},{11,9},{8,1... | collective-permute-start | bytes 1179656 | tf_op jit(solution)/shard_map/ppermute | solution.py:37
  3.7 1.5 %collective-permute-start.3 = (bf16[1536,128]{1,0:T(8,128)(2,1)}, bf16[1536,128]{1,0:T(8,128)(2,1)S(1)}, u32[]{:S(2)}, u32[]{:S(2)}) collective-permute-start(bf16[1536,128]{1,0:T(8,128)(2,1)} %bitcast.12), channel_id=1, source_target_pairs={{16,0},{0,16},{17,1},{1,17},{18,2},{2,18},{19,3},{3,19},{20,4},{4,... | collective-permute-start | bytes 1179656 | tf_op jit(solution)/shard_map/ppermute | solution.py:26
  5.2 0.0 collective-permute-start.4
  5.2 2.5 %pick_column_blocks.1.refs_2_ = bf16[656,128]{1,0:T(8,128)(2,1)} custom-call(s32[12,32]{1,0:T(8,128)} %bitcast.20, s32[1,12]{1,0:T(1,128)} %refs_1_.2, s32[32]{0:T(128)} %refs_2_.1, s32[32]{0:T(128)} %refs_3_.1, s32[32]{0:T(128)} %refs_4_.1, bf16[12,128,128]{2,1,0:T(8,128)(2,1)} %bitcast.14), custom_call_target="tpu_custom_call" | custom-call | tf_op jit(solution)/shard_map/pick_column_blocks/pallas_call | solution.py:448
  7.7 3.6 %collective-permute-start = (bf16[656,128]{1,0:T(8,128)(2,1)}, bf16[656,128]{1,0:T(8,128)(2,1)S(1)}, u32[]{:S(2)}, u32[]{:S(2)}) collective-permute-start(bf16[656,128]{1,0:T(8,128)(2,1)} %pick_column_blocks.1.refs_2_), channel_id=1, source_target_pairs={{12,0},{8,4},{4,8},{0,12},{13,1},{9,5},{5,9},{1,13},{14,2},{10,6},... | collective-permute-start | bytes 503816 | tf_op jit(solution)/shard_map/ppermute | solution.py:32
  11.3 0.0 collective-permute-start.1
  11.3 1.7 %collective-permute-done.2.refs_0_.refs_3_ = bf16[1536,128]{1,0:T(8,128)(2,1)S(1)} collective-permute-done((bf16[1536,128]{1,0:T(8,128)(2,1)}, bf16[1536,128]{1,0:T(8,128)(2,1)S(1)}, u32[]{:S(2)}, u32[]{:S(2)}) %collective-permute-start.2) | collective-permute-done | bytes 393248 | tf_op jit(solution)/shard_map/ppermute | solution.py:37
  13.0 1.5 %collective-permute-done.3.refs_1_.refs_4_.refs_7_ = bf16[1536,128]{1,0:T(8,128)(2,1)S(1)} collective-permute-done((bf16[1536,128]{1,0:T(8,128)(2,1)}, bf16[1536,128]{1,0:T(8,128)(2,1)S(1)}, u32[]{:S(2)}, u32[]{:S(2)}) %collective-permute-start.3) | collective-permute-done | bytes 393248 | tf_op jit(solution)/shard_map/ppermute | solution.py:26
  14.5 0.9 %copy-done.2 = bf16[656,128]{1,0:T(8,128)(2,1)S(1)} copy-done((bf16[656,128]{1,0:T(8,128)(2,1)S(1)}, bf16[656,128]{1,0:T(8,128)(2,1)}, u32[]{:S(2)}) %copy-start.2) | copy-done | bytes 167960
  15.4 1.6 %collective-permute-start.9 = (bf16[640,128]{1,0:T(8,128)(2,1)S(1)}, bf16[640,128]{1,0:T(8,128)(2,1)S(1)}, u32[]{:S(2)}, u32[]{:S(2)}) collective-permute-start(bf16[640,128]{1,0:T(8,128)(2,1)S(1)} %get-tuple-element.27), channel_id=1, source_target_pairs={{16,0},{0,16},{17,1},{1,17},{18,2},{2,18},{19,3},{3,19},{20,4},{4,... | collective-permute-start | bytes 491528 | tf_op jit(solution)/shard_map/ppermute | solution.py:26
  16.9 0.5 collective-permute-start.10
  17.5 0.0 collective-permute-done.refs_0_.refs_3_.refs_5_
  17.5 2.8 %collective-permute-done.1.refs_1_.refs_2_.refs_4_ = bf16[656,128]{1,0:T(8,128)(2,1)S(1)} collective-permute-done((bf16[656,128]{1,0:T(8,128)(2,1)}, bf16[656,128]{1,0:T(8,128)(2,1)S(1)}, u32[]{:S(2)}, u32[]{:S(2)}) %collective-permute-start.1) | collective-permute-done | bytes 167968 | tf_op jit(solution)/shard_map/ppermute | solution.py:32
  20.2 0.0 collective-permute-done.4.refs_5_.refs_2_
  20.2 0.1 pack_two.1
  20.3 0.6 collective-permute-start.5
  20.9 0.5 collective-permute-start.6
  21.4 0.0 collective-permute-start.7
  21.4 0.0 collective-permute-done.9.refs_0_.refs_10_
  21.4 0.5 collective-permute-start.8
  21.9 0.4 collective-permute-done.10.refs_1_.refs_11_
  22.3 0.0 copy-start.4
  22.3 0.0 copy-start
  22.3 0.1 collective-permute-start.11
  22.4 0.0 copy-done.3
  22.4 0.0 copy-done.5
  22.4 4.2 %prepare.1 = (s32[83]{0:T(128)S(1)}, s32[83]{0:T(128)S(1)}, s32[14]{0:T(128)S(1)}) custom-call(s32[12,32]{1,0:T(8,128)S(1)} %bitcast.21, s32[32]{0:T(128)S(1)} %copy-done.5, bf16[1456,128]{1,0:T(8,128)(2,1)S(1)} %get-tuple-element.22.refs_2_), custom_call_target="tpu_custom_call" | custom-call | flops 1000 | bytes 1000 | tf_op jit(solution)/shard_map/prepare/pallas_call | solution.py:579
  26.7 4.3 %collective-permute-done.5.refs_0_.refs_13_ = bf16[1456,128]{1,0:T(8,128)(2,1)S(1)} collective-permute-done((bf16[1456,128]{1,0:T(8,128)(2,1)S(1)}, bf16[1456,128]{1,0:T(8,128)(2,1)S(1)}, u32[]{:S(2)}, u32[]{:S(2)}) %collective-permute-start.5) | collective-permute-done | bytes 372768 | tf_op jit(solution)/shard_map/ppermute | solution.py:37
  31.0 0.2 collective-permute-done.6.refs_2_.refs_12_
  31.3 0.0 collective-permute-done.7.refs_3_.refs_9_
  31.3 0.0 collective-permute-done.8.refs_4_.refs_8_
  31.3 0.1 pack_three.1
  31.4 0.1 collective-permute-start.14
  31.4 0.6 collective-permute-start.12
  32.0 1.6 %collective-permute-start.13 = (bf16[640,128]{1,0:T(8,128)(2,1)S(1)}, bf16[640,128]{1,0:T(8,128)(2,1)S(1)}, u32[]{:S(2)}, u32[]{:S(2)}) collective-permute-start(bf16[640,128]{1,0:T(8,128)(2,1)S(1)} %get-tuple-element.33), channel_id=1, source_target_pairs={{2,0},{3,1},{0,2},{1,3},{6,4},{7,5},{4,6},{5,7},{10,8},{11,9},{8,1... | collective-permute-start | bytes 491528 | tf_op jit(solution)/shard_map/ppermute | solution.py:37
  33.6 0.0 collective-permute-start.15
  33.6 1.0 %spread_basis.1 = (bf16[128,1536]{1,0:T(8,128)(2,1)S(1)}, bf16[16,128]{1,0:T(8,128)(2,1)S(1)}) custom-call(s32[12,32]{1,0:T(8,128)S(1)} %bitcast.22, bf16[192,128]{1,0:T(8,128)(2,1)S(1)} %bitcast.23, bf16[640,128]{1,0:T(8,128)(2,1)S(1)} %get-tuple-element.29.refs_2_.refs_15_), custom_call_target="tpu_custom_call" | custom-call | flops 1000 | bytes 1000 | tf_op jit(solution)/shard_map/spread_basis/pallas_call | solution.py:627
  34.6 0.0 collective-permute-done.11.refs_14_
  34.6 2.1 %gram_early.1.refs_2_.refs_5_ = bf16[1536,1536]{1,0:T(8,128)(2,1)S(1)} custom-call(s32[83]{0:T(128)S(1)} %get-tuple-element.32.refs_0_, bf16[1536,128]{1,0:T(8,128)(2,1)S(1)} %bitcast.15, bf16[1536,128]{1,0:T(8,128)(2,1)S(1)} %collective-permute-done.4.refs_5_.refs_2_, bf16[1536,128]{1,0:T(8,128)(2,1)S(1)} %collective-permute-done.2.refs_0_.refs_3_, ...), custom_call_target="tpu_custom_call" | custom-call | flops 1000 | bytes 1000 | tf_op jit(solution)/shard_map/gram_early/pallas_call | solution.py:642
  36.8 1.3 %collective-permute-done.15.refs_3_.refs_2_ = bf16[96,128]{1,0:T(8,128)(2,1)S(1)} collective-permute-done((bf16[96,128]{1,0:T(8,128)(2,1)S(1)}, bf16[96,128]{1,0:T(8,128)(2,1)S(1)}, u32[]{:S(2)}, u32[]{:S(2)}) %collective-permute-start.15) | collective-permute-done | bytes 24608 | tf_op jit(solution)/shard_map/ppermute | solution.py:37
  38.0 0.0 collective-permute-done.12.refs_0_.refs_6_
  38.1 0.5 collective-permute-done.13.refs_1_.refs_7_
  38.6 0.2 collective-permute-start.16
  38.8 1.5 %collective-permute-done.16.refs_9_ = bf16[1280,128]{1,0:T(8,128)(2,1)S(1)} collective-permute-done((bf16[1280,128]{1,0:T(8,128)(2,1)S(1)}, bf16[1280,128]{1,0:T(8,128)(2,1)S(1)}, u32[]{:S(2)}, u32[]{:S(2)}) %collective-permute-start.16) | collective-permute-done | bytes 327712 | tf_op jit(solution)/shard_map/ppermute | solution.py:37
  40.3 0.0 collective-permute-done.14.refs_8_.refs_1_
  40.3 4.6 %square_cube_coefficients.1 = (bf16[12,128,128]{2,1,0:T(8,128)(2,1)S(1)}, f32[8,128]{1,0:T(8,128)S(1)}) custom-call(s32[83]{0:T(128)S(1)} %get-tuple-element.23.refs_0_, s32[14]{0:T(128)S(1)} %get-tuple-element.24.refs_6_.refs_1_, bf16[16,128]{1,0:T(8,128)(2,1)S(1)} %get-tuple-element.30.refs_4_.refs_2_, bf16[128,1536]{1,0:T(8,128)(2,1)S(1)} %get-tuple-element.31.refs_3_, ...), custom_call_target="tpu_custom_call" | custom-call | flops 1300000000 | bytes 8000000 | tf_op jit(solution)/shard_map/square_cube_coefficients/pallas_call | solution.py:679
  44.8 0.0 collective-permute-start.17
  44.9 1.5 %collective-permute-start.18 = (f32[8,128]{1,0:T(8,128)S(1)}, f32[8,128]{1,0:T(8,128)S(1)}, u32[]{:S(2)}, u32[]{:S(2)}) collective-permute-start(f32[8,128]{1,0:T(8,128)S(1)} %get-tuple-element.37), channel_id=1, source_target_pairs={{3,0},{2,1},{1,2},{0,3},{7,4},{6,5},{5,6},{4,7},{11,8},{10,9},{9,1... | collective-permute-start | bytes 12296 | tf_op jit(solution)/shard_map/ppermute | solution.py:37
  46.4 0.0 collective-permute-done.17
  46.4 1.5 %collective-permute-done.18 = f32[8,128]{1,0:T(8,128)S(1)} collective-permute-done((f32[8,128]{1,0:T(8,128)S(1)}, f32[8,128]{1,0:T(8,128)S(1)}, u32[]{:S(2)}, u32[]{:S(2)}) %collective-permute-start.18) | collective-permute-done | bytes 4128 | tf_op jit(solution)/shard_map/ppermute | solution.py:37
  47.9 0.1 slice.11
  48.0 0.1 slice.10
  48.1 0.1 pad_maximum_fusion.1
  48.1 1.6 %collective-permute-start.19 = (f32[8,128]{1,0:T(8,128)S(1)}, f32[8,128]{1,0:T(8,128)S(1)}, u32[]{:S(2)}, u32[]{:S(2)}) collective-permute-start(f32[8,128]{1,0:T(8,128)S(1)} %pad_maximum_fusion.1), channel_id=1, source_target_pairs={{16,0},{0,16},{17,1},{1,17},{18,2},{2,18},{19,3},{3,19},{20,4},{4,... | collective-permute-start | bytes 12296 | tf_op jit(solution)/shard_map/ppermute | solution.py:26
  49.8 2.0 %collective-permute-done.19 = f32[8,128]{1,0:T(8,128)S(1)} collective-permute-done((f32[8,128]{1,0:T(8,128)S(1)}, f32[8,128]{1,0:T(8,128)S(1)}, u32[]{:S(2)}, u32[]{:S(2)}) %collective-permute-start.19) | collective-permute-done | bytes 4128 | tf_op jit(solution)/shard_map/ppermute | solution.py:26
  51.8 0.1 pad_maximum_fusion.refs_0_
  51.8 2.8 %collective-permute-start.20 = (f32[16,128]{1,0:T(8,128)S(1)}, f32[16,128]{1,0:T(8,128)S(1)}, u32[]{:S(2)}, u32[]{:S(2)}) collective-permute-start(f32[16,128]{1,0:T(8,128)S(1)} %pad_maximum_fusion.refs_0_), channel_id=1, source_target_pairs={{12,0},{8,4},{4,8},{0,12},{13,1},{9,5},{5,9},{1,13},{14,2},{10,6},... | collective-permute-start | bytes 24584 | tf_op jit(solution)/shard_map/ppermute | solution.py:32
  54.6 0.0 collective-permute-start.21
  54.6 2.8 %profiles.1 = (bf16[6,6,256,128]{3,2,1,0:T(8,128)(2,1)S(1)}, bf16[6,6,128,128]{3,2,1,0:T(8,128)(2,1)S(1)}) custom-call(bf16[96,128]{1,0:T(8,128)(2,1)S(1)} %get-tuple-element.35.refs_0_, bf16[2960,128]{1,0:T(8,128)(2,1)S(1)} %collective-permute-done.14.refs_8_.refs_1_, bf16[96,128]{1,0:T(8,128)(2,1)S(1)} %collective-permute-done.15.refs_3_.refs_2_), custom_call_target="tpu_custom_call" | custom-call | flops 1000 | bytes 1000 | tf_op jit(solution)/shard_map/profiles/pallas_call | solution.py:661
  57.5 0.8 %give_sign.1.refs_5_ = bf16[1536,128]{1,0:T(8,128)(2,1)} custom-call(bf16[1536,128]{1,0:T(8,128)(2,1)S(1)} %bitcast.19), custom_call_target="tpu_custom_call" | custom-call | bytes 1000 | tf_op jit(solution)/shard_map/give_sign/pallas_call | solution.py:243
  58.2 0.0 collective-permute-done.20.refs_1_
  58.2 0.0 collective-permute-done.21.refs_2_
  58.3 1.0 %copy-done.1 = bf16[1536,128]{1,0:T(8,128)(2,1)S(1)} copy-done((bf16[1536,128]{1,0:T(8,128)(2,1)S(1)}, bf16[1536,128]{1,0:T(8,128)(2,1)}, u32[]{:S(2)}) %copy-start.1) | copy-done | bytes 393240
  59.2 1.5 %density.1 = f32[256,128]{1,0:T(8,128)} custom-call(f32[16,128]{1,0:T(8,128)S(1)} %pad_maximum_fusion.refs_0_, f32[16,128]{1,0:T(8,128)S(1)} %collective-permute-done.20.refs_1_, f32[16,128]{1,0:T(8,128)S(1)} %collective-permute-done.21.refs_2_, bf16[6,6,256,128]{3,2,1,0:T(8,128)(2,1)S(1)} %get-tuple-element.38.refs_3_, bf16[4608,128]{1,0:T(8,128)(2,1)S(1)} %bitcast.18, ...), custom_call_target="tpu_custom_call" | custom-call | flops 310000000 | bytes 4000000 | tf_op jit(solution)/shard_map/density/pallas_call | solution.py:717
  (11 shorter events, 0.1 us)
Async XLA Ops:
  0.6 12.4 %collective-permute-start.2 = (bf16[1536,128]{1,0:T(8,128)(2,1)}, bf16[1536,128]{1,0:T(8,128)(2,1)S(1)}, u32[]{:S(2)}, u32[]{:S(2)}) collective-permute-start(bf16[1536,128]{1,0:T(8,128)(2,1)} %bitcast.11), channel_id=1, source_target_pairs={{2,0},{3,1},{0,2},{1,3},{6,4},{7,5},{4,6},{5,7},{10,8},{11,9},{8,1... | collective-permute-start | bytes 1179656 | tf_op jit(solution)/shard_map/ppermute | solution.py:37
  3.7 10.8 %collective-permute-start.3 = (bf16[1536,128]{1,0:T(8,128)(2,1)}, bf16[1536,128]{1,0:T(8,128)(2,1)S(1)}, u32[]{:S(2)}, u32[]{:S(2)}) collective-permute-start(bf16[1536,128]{1,0:T(8,128)(2,1)} %bitcast.12), channel_id=1, source_target_pairs={{16,0},{0,16},{17,1},{1,17},{18,2},{2,18},{19,3},{3,19},{20,4},{4,... | collective-permute-start | bytes 1179656 | tf_op jit(solution)/shard_map/ppermute | solution.py:26
  5.2 15.1 %collective-permute-start.4 = (bf16[1536,128]{1,0:T(8,128)(2,1)}, bf16[1536,128]{1,0:T(8,128)(2,1)S(1)}, u32[]{:S(2)}, u32[]{:S(2)}) collective-permute-start(bf16[1536,128]{1,0:T(8,128)(2,1)} %bitcast.13), channel_id=1, source_target_pairs={{1,0},{0,1},{3,2},{2,3},{5,4},{4,5},{7,6},{6,7},{9,8},{8,9},{11,10... | collective-permute-start | bytes 1179656 | tf_op jit(solution)/shard_map/ppermute | solution.py:37
  7.7 9.8 %collective-permute-start = (bf16[656,128]{1,0:T(8,128)(2,1)}, bf16[656,128]{1,0:T(8,128)(2,1)S(1)}, u32[]{:S(2)}, u32[]{:S(2)}) collective-permute-start(bf16[656,128]{1,0:T(8,128)(2,1)} %pick_column_blocks.1.refs_2_), channel_id=1, source_target_pairs={{12,0},{8,4},{4,8},{0,12},{13,1},{9,5},{5,9},{1,13},{14,2},{10,6},... | collective-permute-start | bytes 503816 | tf_op jit(solution)/shard_map/ppermute | solution.py:32
  11.3 8.9 %collective-permute-start.1 = (bf16[656,128]{1,0:T(8,128)(2,1)}, bf16[656,128]{1,0:T(8,128)(2,1)S(1)}, u32[]{:S(2)}, u32[]{:S(2)}) collective-permute-start(bf16[656,128]{1,0:T(8,128)(2,1)} %pick_column_blocks.1.refs_2_), channel_id=1, source_target_pairs={{4,0},{0,4},{12,8},{8,12},{5,1},{1,5},{13,9},{9,13},{6,2},{2,6},{1... | collective-permute-start | bytes 503816 | tf_op jit(solution)/shard_map/ppermute | solution.py:32
  14.4 0.9 %copy-start.2 = (bf16[656,128]{1,0:T(8,128)(2,1)S(1)}, bf16[656,128]{1,0:T(8,128)(2,1)}, u32[]{:S(2)}) copy-start(bf16[656,128]{1,0:T(8,128)(2,1)} %pick_column_blocks.1.refs_2_) | copy-start | bytes 503812
  15.4 6.0 %collective-permute-start.9 = (bf16[640,128]{1,0:T(8,128)(2,1)S(1)}, bf16[640,128]{1,0:T(8,128)(2,1)S(1)}, u32[]{:S(2)}, u32[]{:S(2)}) collective-permute-start(bf16[640,128]{1,0:T(8,128)(2,1)S(1)} %get-tuple-element.27), channel_id=1, source_target_pairs={{16,0},{0,16},{17,1},{1,17},{18,2},{2,18},{19,3},{3,19},{20,4},{4,... | collective-permute-start | bytes 491528 | tf_op jit(solution)/shard_map/ppermute | solution.py:26
  16.9 5.3 %collective-permute-start.10 = (bf16[640,128]{1,0:T(8,128)(2,1)S(1)}, bf16[640,128]{1,0:T(8,128)(2,1)S(1)}, u32[]{:S(2)}, u32[]{:S(2)}) collective-permute-start(bf16[640,128]{1,0:T(8,128)(2,1)S(1)} %get-tuple-element.28), channel_id=1, source_target_pairs={{2,0},{3,1},{0,2},{1,3},{6,4},{7,5},{4,6},{5,7},{10,8},{11,9},{8,1... | collective-permute-start | bytes 491528 | tf_op jit(solution)/shard_map/ppermute | solution.py:37
  20.3 10.7 %collective-permute-start.5 = (bf16[1456,128]{1,0:T(8,128)(2,1)S(1)}, bf16[1456,128]{1,0:T(8,128)(2,1)S(1)}, u32[]{:S(2)}, u32[]{:S(2)}) collective-permute-start(bf16[1456,128]{1,0:T(8,128)(2,1)S(1)} %get-tuple-element.25), channel_id=1, source_target_pairs={{2,0},{3,1},{0,2},{1,3},{6,4},{7,5},{4,6},{5,7},{10,8},{11,9},{8,1... | collective-permute-start | bytes 1118216 | tf_op jit(solution)/shard_map/ppermute | solution.py:37
  20.9 1.5 %copy-start.3 = (s32[32,12]{0,1:T(8,128)S(1)}, s32[32,12]{0,1:T(8,128)}, u32[]{:S(2)}) copy-start(s32[32,12]{0,1:T(8,128)} %param.9) | copy-start | bytes 4612
  20.9 1.5 %copy-start.5 = (s32[32]{0:T(128)S(1)}, s32[32]{0:T(128)}, u32[]{:S(2)}) copy-start(s32[32]{0:T(128)} %refs_1_.3) | copy-start | bytes 388
  20.9 10.4 %collective-permute-start.6 = (bf16[1456,128]{1,0:T(8,128)(2,1)S(1)}, bf16[1456,128]{1,0:T(8,128)(2,1)S(1)}, u32[]{:S(2)}, u32[]{:S(2)}) collective-permute-start(bf16[1456,128]{1,0:T(8,128)(2,1)S(1)} %get-tuple-element.22.refs_2_), channel_id=1, source_target_pairs={{16,0},{0,16},{17,1},{1,17},{18,2},{2,18},{19,3},{3,19},{20,4},{4,... | collective-permute-start | bytes 1118216 | tf_op jit(solution)/shard_map/ppermute | solution.py:26
  21.4 9.9 %collective-permute-start.7 = (bf16[1536,128]{1,0:T(8,128)(2,1)S(1)}, bf16[1536,128]{1,0:T(8,128)(2,1)S(1)}, u32[]{:S(2)}, u32[]{:S(2)}) collective-permute-start(bf16[1536,128]{1,0:T(8,128)(2,1)S(1)} %collective-permute-done.2.refs_0_.refs_3_), channel_id=1, source_target_pairs={{1,0},{0,1},{3,2},{2,3},{5,4},{4,5},{7,6},{6,7},{9,8},{8,9},{11,10... | collective-permute-start | bytes 1179656 | tf_op jit(solution)/shard_map/ppermute | solution.py:37
  21.4 9.9 %collective-permute-start.8 = (bf16[1536,128]{1,0:T(8,128)(2,1)S(1)}, bf16[1536,128]{1,0:T(8,128)(2,1)S(1)}, u32[]{:S(2)}, u32[]{:S(2)}) collective-permute-start(bf16[1536,128]{1,0:T(8,128)(2,1)S(1)} %collective-permute-done.3.refs_1_.refs_4_.refs_7_), channel_id=1, source_target_pairs={{1,0},{0,1},{3,2},{2,3},{5,4},{4,5},{7,6},{6,7},{9,8},{8,9},{11,10... | collective-permute-start | bytes 1179656 | tf_op jit(solution)/shard_map/ppermute | solution.py:37
  22.3 11.2 %copy-start.4 = (bf16[32,6,128]{2,0,1:T(8,128)(2,1)S(1)}, bf16[32,6,128]{2,0,1:T(8,128)(2,1)}, u32[]{:S(2)}) copy-start(bf16[32,6,128]{2,0,1:T(8,128)(2,1)} %param.11) | copy-start | bytes 147460
  22.3 12.3 %copy-start = (bf16[1,12,128,128]{3,2,1,0:T(8,128)(2,1)S(1)}, bf16[1,12,128,128]{3,2,1,0:T(8,128)(2,1)}, u32[]{:S(2)}) copy-start(bf16[1,12,128,128]{3,2,1,0:T(8,128)(2,1)} %param.8) | copy-start | bytes 1179652
  22.3 12.2 %collective-permute-start.11 = (bf16[2560,128]{1,0:T(8,128)(2,1)S(1)}, bf16[2560,128]{1,0:T(8,128)(2,1)S(1)}, u32[]{:S(2)}, u32[]{:S(2)}) collective-permute-start(bf16[2560,128]{1,0:T(8,128)(2,1)S(1)} %pack_two_mate.1.refs_5_), channel_id=1, source_target_pairs={{1,0},{0,1},{3,2},{2,3},{5,4},{4,5},{7,6},{6,7},{9,8},{8,9},{11,10... | collective-permute-start | bytes 1966088 | tf_op jit(solution)/shard_map/ppermute | solution.py:37
  31.4 8.9 %collective-permute-start.14 = (bf16[2960,128]{1,0:T(8,128)(2,1)S(1)}, bf16[2960,128]{1,0:T(8,128)(2,1)S(1)}, u32[]{:S(2)}, u32[]{:S(2)}) collective-permute-start(bf16[2960,128]{1,0:T(8,128)(2,1)S(1)} %get-tuple-element.34), channel_id=1, source_target_pairs={{1,0},{0,1},{3,2},{2,3},{5,4},{4,5},{7,6},{6,7},{9,8},{8,9},{11,10... | collective-permute-start | bytes 2273288 | tf_op jit(solution)/shard_map/ppermute | solution.py:37
  31.4 6.6 %collective-permute-start.12 = (bf16[640,128]{1,0:T(8,128)(2,1)S(1)}, bf16[640,128]{1,0:T(8,128)(2,1)S(1)}, u32[]{:S(2)}, u32[]{:S(2)}) collective-permute-start(bf16[640,128]{1,0:T(8,128)(2,1)S(1)} %get-tuple-element.29.refs_2_.refs_15_), channel_id=1, source_target_pairs={{16,0},{0,16},{17,1},{1,17},{18,2},{2,18},{19,3},{3,19},{20,4},{4,... | collective-permute-start | bytes 491528 | tf_op jit(solution)/shard_map/ppermute | solution.py:26
  32.0 6.5 %collective-permute-start.13 = (bf16[640,128]{1,0:T(8,128)(2,1)S(1)}, bf16[640,128]{1,0:T(8,128)(2,1)S(1)}, u32[]{:S(2)}, u32[]{:S(2)}) collective-permute-start(bf16[640,128]{1,0:T(8,128)(2,1)S(1)} %get-tuple-element.33), channel_id=1, source_target_pairs={{2,0},{3,1},{0,2},{1,3},{6,4},{7,5},{4,6},{5,7},{10,8},{11,9},{8,1... | collective-permute-start | bytes 491528 | tf_op jit(solution)/shard_map/ppermute | solution.py:37
  33.6 4.5 %collective-permute-start.15 = (bf16[96,128]{1,0:T(8,128)(2,1)S(1)}, bf16[96,128]{1,0:T(8,128)(2,1)S(1)}, u32[]{:S(2)}, u32[]{:S(2)}) collective-permute-start(bf16[96,128]{1,0:T(8,128)(2,1)S(1)} %get-tuple-element.35.refs_0_), channel_id=1, source_target_pairs={{3,0},{2,1},{1,2},{0,3},{7,4},{6,5},{5,6},{4,7},{11,8},{10,9},{9,1... | collective-permute-start | bytes 73736 | tf_op jit(solution)/shard_map/ppermute | solution.py:37
  38.6 1.7 %collective-permute-start.16 = (bf16[1280,128]{1,0:T(8,128)(2,1)S(1)}, bf16[1280,128]{1,0:T(8,128)(2,1)S(1)}, u32[]{:S(2)}, u32[]{:S(2)}) collective-permute-start(bf16[1280,128]{1,0:T(8,128)(2,1)S(1)} %pack_four.1), channel_id=1, source_target_pairs={{1,0},{0,1},{3,2},{2,3},{5,4},{4,5},{7,6},{6,7},{9,8},{8,9},{11,10... | collective-permute-start | bytes 983048 | tf_op jit(solution)/shard_map/ppermute | solution.py:37
  44.8 1.6 %collective-permute-start.17 = (f32[8,128]{1,0:T(8,128)S(1)}, f32[8,128]{1,0:T(8,128)S(1)}, u32[]{:S(2)}, u32[]{:S(2)}) collective-permute-start(f32[8,128]{1,0:T(8,128)S(1)} %get-tuple-element.37), channel_id=1, source_target_pairs={{1,0},{0,1},{3,2},{2,3},{5,4},{4,5},{7,6},{6,7},{9,8},{8,9},{11,10... | collective-permute-start | bytes 12296 | tf_op jit(solution)/shard_map/ppermute | solution.py:37
  44.9 3.0 %collective-permute-start.18 = (f32[8,128]{1,0:T(8,128)S(1)}, f32[8,128]{1,0:T(8,128)S(1)}, u32[]{:S(2)}, u32[]{:S(2)}) collective-permute-start(f32[8,128]{1,0:T(8,128)S(1)} %get-tuple-element.37), channel_id=1, source_target_pairs={{3,0},{2,1},{1,2},{0,3},{7,4},{6,5},{5,6},{4,7},{11,8},{10,9},{9,1... | collective-permute-start | bytes 12296 | tf_op jit(solution)/shard_map/ppermute | solution.py:37
  48.1 3.6 %collective-permute-start.19 = (f32[8,128]{1,0:T(8,128)S(1)}, f32[8,128]{1,0:T(8,128)S(1)}, u32[]{:S(2)}, u32[]{:S(2)}) collective-permute-start(f32[8,128]{1,0:T(8,128)S(1)} %pad_maximum_fusion.1), channel_id=1, source_target_pairs={{16,0},{0,16},{17,1},{1,17},{18,2},{2,18},{19,3},{3,19},{20,4},{4,... | collective-permute-start | bytes 12296 | tf_op jit(solution)/shard_map/ppermute | solution.py:26
  51.8 6.4 %collective-permute-start.20 = (f32[16,128]{1,0:T(8,128)S(1)}, f32[16,128]{1,0:T(8,128)S(1)}, u32[]{:S(2)}, u32[]{:S(2)}) collective-permute-start(f32[16,128]{1,0:T(8,128)S(1)} %pad_maximum_fusion.refs_0_), channel_id=1, source_target_pairs={{12,0},{8,4},{4,8},{0,12},{13,1},{9,5},{5,9},{1,13},{14,2},{10,6},... | collective-permute-start | bytes 24584 | tf_op jit(solution)/shard_map/ppermute | solution.py:32
  54.6 3.7 %collective-permute-start.21 = (f32[16,128]{1,0:T(8,128)S(1)}, f32[16,128]{1,0:T(8,128)S(1)}, u32[]{:S(2)}, u32[]{:S(2)}) collective-permute-start(f32[16,128]{1,0:T(8,128)S(1)} %pad_maximum_fusion.refs_0_), channel_id=1, source_target_pairs={{4,0},{0,4},{12,8},{8,12},{5,1},{1,5},{13,9},{9,13},{6,2},{2,6},{1... | collective-permute-start | bytes 24584 | tf_op jit(solution)/shard_map/ppermute | solution.py:32
  58.3 1.0 %copy-start.1 = (bf16[1536,128]{1,0:T(8,128)(2,1)S(1)}, bf16[1536,128]{1,0:T(8,128)(2,1)}, u32[]{:S(2)}) copy-start(bf16[1536,128]{1,0:T(8,128)(2,1)} %give_sign.1.refs_5_) | copy-start | bytes 1179652

commit v18 on v17

--- a/solution.py
+++ b/solution.py
@@ -709,21 +709,22 @@
         ],
         axis=1,
     )
-    stacked = jnp.concatenate([merged] + [on_row(merged, di) for di in others], axis=0)
+    given, token = pack([sign_next.reshape(full, size)], [[(0, 0, full)], [(0, 0, GEO)]], [], "give_sign")
+    parts = [merged] + [on_row(merged, di) for di in others]
+    stacked = pack(parts, [[(i, 0, 8) for i in range(count)]], [token], "stack_tiles")[0]
     far_side = from_column(stacked, 1)
     received = [stacked, far_side, from_column(stacked, 0)]
 
-    given = pack([sign_next.reshape(full, size)], [[(0, 0, full)]], [], "give_sign")[0]
     density = pl.pallas_call(
         functools.partial(density_kernel, len(column_steps)),
         out_shape=jax.ShapeDtypeStruct((BX * BY, BZ), jnp.float32),
-        in_specs=[VMEM] * (len(received) + 2) + [ANY],
+        in_specs=[VMEM] * (len(received) + 2),
         out_specs=VMEM,
         scratch_shapes=[pltpu.VMEM((BX * BY, tiles * SHELLS * LANES), jnp.bfloat16)],
         compiler_params=pltpu.CompilerParams(vmem_limit_bytes=16 << 20),
         cost_estimate=pl.CostEstimate(flops=310_000_000, bytes_accessed=4_000_000, transcendentals=0),
         name="density",
-    )(*received, plane, line.reshape(tiles * SHELLS * LANES, BZ), given)
+    )(*received, plane, line.reshape(tiles * SHELLS * LANES, BZ))
     return given.reshape(1, slots, size, size), density.reshape(BX, BY, BZ)
 
 

time: 60.9 us -> 59.9 us (0.984)
  local copies, waits for them, and re-layouts: 2.08 us -> 1.16 us
    unnamed x12 -> x10, local copies, waits for them, and re-layouts: 1.93 us -> 0.94 us
    ppermute x4, waiting for transfers between devices: 2.79 us -> 3.51 us  [from_column(): lax.ppermute(x, 'col', [((i + step[i]) % count, i) for i in range(count)])]
  transfers between devices with their start and end apart: 22 -> 22, of which waited for: 11 -> 12; matrix products, arithmetic and copies ran while one was open for 0% -> 0% of each run, Pallas kernels for 23% -> 23%
where the time goes in v18:
time: 59.9 us; the launch traced here: 59.6 us
  starting transfers between devices  19.9 us (33%)
  Pallas kernels  19.6 us (33%)
  waiting for transfers between devices  18 us (30%)
  local copies, waits for them, and re-layouts  1.16 us (2%)
  between operations  0.78 us (1%)
    ppermute x13, waiting for transfers between devices, from_layer(): return lax.ppermute(x, 'layer', [(i ^ flip, i) for i in range(count)])  11.4 us
    ppermute x13, starting transfers between devices, from_layer(): return lax.ppermute(x, 'layer', [(i ^ flip, i) for i in range(count)])  8.14 us
    ppermute x4, starting transfers between devices, from_column(): lax.ppermute(x, 'col', [((i + step[i]) % count, i) for i in range(count)])  6.22 us
    ppermute x5, starting transfers between devices, from_offset(): lax.ppermute(x, axis, [((i + step) % count, i) for i in range(count)])  5.59 us
    pallas_call x1, Pallas kernels, local(): pl.pallas_call(functools.partial(step_kernel, len(late_values)), out_shap...  4.59 us
    pallas_call x1, Pallas kernels, local(): pl.pallas_call(functools.partial(prepare_kernel, axes, count, tuple(layou...  3.97 us
    ppermute x4, waiting for transfers between devices, from_column(): lax.ppermute(x, 'col', [((i + step[i]) % count, i) for i in range(count)])  3.51 us
    ppermute x5, waiting for transfers between devices, from_offset(): lax.ppermute(x, axis, [((i + step) % count, i) for i in range(count)])  3.16 us
  transfers between devices with their start and end apart: 22, of which 12 were waited for; matrix products, arithmetic and copies ran while one was open for 0% of the time, Pallas kernels for 23%

profile of v18, /device:TPU:0, one launch (start us, length us, event | category | flops | bytes accessed | tf_op | source)
XLA Modules:
  0.0 59.6 jit_solution(13966908788242237136)
XLA Ops:
  0.6 3.0 %collective-permute-start.2 = (bf16[1536,128]{1,0:T(8,128)(2,1)}, bf16[1536,128]{1,0:T(8,128)(2,1)S(1)}, u32[]{:S(2)}, u32[]{:S(2)}) collective-permute-start(bf16[1536,128]{1,0:T(8,128)(2,1)} %bitcast.11), channel_id=1, source_target_pairs={{2,0},{3,1},{0,2},{1,3},{6,4},{7,5},{4,6},{5,7},{10,8},{11,9},{8,1... | collective-permute-start | bytes 1179656 | tf_op jit(solution)/shard_map/ppermute | solution.py:37
  3.7 1.5 %collective-permute-start.3 = (bf16[1536,128]{1,0:T(8,128)(2,1)}, bf16[1536,128]{1,0:T(8,128)(2,1)S(1)}, u32[]{:S(2)}, u32[]{:S(2)}) collective-permute-start(bf16[1536,128]{1,0:T(8,128)(2,1)} %bitcast.12), channel_id=1, source_target_pairs={{16,0},{0,16},{17,1},{1,17},{18,2},{2,18},{19,3},{3,19},{20,4},{4,... | collective-permute-start | bytes 1179656 | tf_op jit(solution)/shard_map/ppermute | solution.py:26
  5.2 0.0 collective-permute-start.4
  5.2 2.5 %pick_column_blocks.1.refs_2_ = bf16[656,128]{1,0:T(8,128)(2,1)} custom-call(s32[12,32]{1,0:T(8,128)} %bitcast.19, s32[1,12]{1,0:T(1,128)} %refs_1_.2, s32[32]{0:T(128)} %refs_2_.1, s32[32]{0:T(128)} %refs_3_.1, s32[32]{0:T(128)} %refs_4_.1, bf16[12,128,128]{2,1,0:T(8,128)(2,1)} %bitcast.14), custom_call_target="tpu_custom_call" | custom-call | tf_op jit(solution)/shard_map/pick_column_blocks/pallas_call | solution.py:448
  7.7 3.7 %collective-permute-start = (bf16[656,128]{1,0:T(8,128)(2,1)}, bf16[656,128]{1,0:T(8,128)(2,1)S(1)}, u32[]{:S(2)}, u32[]{:S(2)}) collective-permute-start(bf16[656,128]{1,0:T(8,128)(2,1)} %pick_column_blocks.1.refs_2_), channel_id=1, source_target_pairs={{12,0},{8,4},{4,8},{0,12},{13,1},{9,5},{5,9},{1,13},{14,2},{10,6},... | collective-permute-start | bytes 503816 | tf_op jit(solution)/shard_map/ppermute | solution.py:32
  11.3 0.0 collective-permute-start.1
  11.3 1.7 %collective-permute-done.2.refs_0_.refs_3_ = bf16[1536,128]{1,0:T(8,128)(2,1)S(1)} collective-permute-done((bf16[1536,128]{1,0:T(8,128)(2,1)}, bf16[1536,128]{1,0:T(8,128)(2,1)S(1)}, u32[]{:S(2)}, u32[]{:S(2)}) %collective-permute-start.2) | collective-permute-done | bytes 393248 | tf_op jit(solution)/shard_map/ppermute | solution.py:37
  13.0 1.5 %collective-permute-done.3.refs_1_.refs_4_.refs_7_ = bf16[1536,128]{1,0:T(8,128)(2,1)S(1)} collective-permute-done((bf16[1536,128]{1,0:T(8,128)(2,1)}, bf16[1536,128]{1,0:T(8,128)(2,1)S(1)}, u32[]{:S(2)}, u32[]{:S(2)}) %collective-permute-start.3) | collective-permute-done | bytes 393248 | tf_op jit(solution)/shard_map/ppermute | solution.py:26
  14.5 0.9 %copy-done.1 = bf16[656,128]{1,0:T(8,128)(2,1)S(1)} copy-done((bf16[656,128]{1,0:T(8,128)(2,1)S(1)}, bf16[656,128]{1,0:T(8,128)(2,1)}, u32[]{:S(2)}) %copy-start.1) | copy-done | bytes 167960
  15.4 1.6 %collective-permute-start.9 = (bf16[640,128]{1,0:T(8,128)(2,1)S(1)}, bf16[640,128]{1,0:T(8,128)(2,1)S(1)}, u32[]{:S(2)}, u32[]{:S(2)}) collective-permute-start(bf16[640,128]{1,0:T(8,128)(2,1)S(1)} %get-tuple-element.29), channel_id=1, source_target_pairs={{16,0},{0,16},{17,1},{1,17},{18,2},{2,18},{19,3},{3,19},{20,4},{4,... | collective-permute-start | bytes 491528 | tf_op jit(solution)/shard_map/ppermute | solution.py:26
  16.9 0.5 collective-permute-start.10
  17.5 0.0 collective-permute-done.refs_0_.refs_3_.refs_5_
  17.5 2.7 %collective-permute-done.1.refs_1_.refs_2_.refs_4_ = bf16[656,128]{1,0:T(8,128)(2,1)S(1)} collective-permute-done((bf16[656,128]{1,0:T(8,128)(2,1)}, bf16[656,128]{1,0:T(8,128)(2,1)S(1)}, u32[]{:S(2)}, u32[]{:S(2)}) %collective-permute-start.1) | collective-permute-done | bytes 167968 | tf_op jit(solution)/shard_map/ppermute | solution.py:32
  20.2 0.0 collective-permute-done.4.refs_5_.refs_2_
  20.2 0.1 pack_two.1
  20.3 0.6 collective-permute-start.5
  20.9 0.5 collective-permute-start.6
  21.4 0.0 collective-permute-start.7
  21.4 0.0 collective-permute-done.9.refs_0_.refs_10_
  21.4 0.5 collective-permute-start.8
  21.9 0.4 collective-permute-done.10.refs_1_.refs_11_
  22.3 0.0 copy-start.3
  22.3 0.0 copy-start
  22.3 0.1 collective-permute-start.11
  22.4 0.0 copy-done.2
  22.4 0.0 copy-done.4
  22.4 4.0 %prepare.1 = (s32[83]{0:T(128)S(1)}, s32[83]{0:T(128)S(1)}, s32[14]{0:T(128)S(1)}) custom-call(s32[12,32]{1,0:T(8,128)S(1)} %bitcast.20, s32[32]{0:T(128)S(1)} %copy-done.4, bf16[1456,128]{1,0:T(8,128)(2,1)S(1)} %get-tuple-element.24.refs_2_), custom_call_target="tpu_custom_call" | custom-call | flops 1000 | bytes 1000 | tf_op jit(solution)/shard_map/prepare/pallas_call | solution.py:579
  26.4 4.6 %collective-permute-done.5.refs_0_.refs_13_ = bf16[1456,128]{1,0:T(8,128)(2,1)S(1)} collective-permute-done((bf16[1456,128]{1,0:T(8,128)(2,1)S(1)}, bf16[1456,128]{1,0:T(8,128)(2,1)S(1)}, u32[]{:S(2)}, u32[]{:S(2)}) %collective-permute-start.5) | collective-permute-done | bytes 372768 | tf_op jit(solution)/shard_map/ppermute | solution.py:37
  31.0 0.2 collective-permute-done.6.refs_2_.refs_12_
  31.2 0.0 collective-permute-done.7.refs_3_.refs_9_
  31.2 0.0 collective-permute-done.8.refs_4_.refs_8_
  31.2 0.1 pack_three.1
  31.3 0.1 collective-permute-start.14
  31.4 0.6 %collective-permute-start.12 = (bf16[640,128]{1,0:T(8,128)(2,1)S(1)}, bf16[640,128]{1,0:T(8,128)(2,1)S(1)}, u32[]{:S(2)}, u32[]{:S(2)}) collective-permute-start(bf16[640,128]{1,0:T(8,128)(2,1)S(1)} %get-tuple-element.31.refs_2_.refs_15_), channel_id=1, source_target_pairs={{16,0},{0,16},{17,1},{1,17},{18,2},{2,18},{19,3},{3,19},{20,4},{4,... | collective-permute-start | bytes 491528 | tf_op jit(solution)/shard_map/ppermute | solution.py:26
  32.0 1.5 %collective-permute-start.13 = (bf16[640,128]{1,0:T(8,128)(2,1)S(1)}, bf16[640,128]{1,0:T(8,128)(2,1)S(1)}, u32[]{:S(2)}, u32[]{:S(2)}) collective-permute-start(bf16[640,128]{1,0:T(8,128)(2,1)S(1)} %get-tuple-element.35), channel_id=1, source_target_pairs={{2,0},{3,1},{0,2},{1,3},{6,4},{7,5},{4,6},{5,7},{10,8},{11,9},{8,1... | collective-permute-start | bytes 491528 | tf_op jit(solution)/shard_map/ppermute | solution.py:37
  33.5 0.0 collective-permute-start.15
  33.5 0.0 copy-done.3
  33.5 1.0 %spread_basis.1 = (bf16[128,1536]{1,0:T(8,128)(2,1)S(1)}, bf16[16,128]{1,0:T(8,128)(2,1)S(1)}) custom-call(s32[12,32]{1,0:T(8,128)S(1)} %bitcast.21, bf16[192,128]{1,0:T(8,128)(2,1)S(1)} %bitcast.22, bf16[640,128]{1,0:T(8,128)(2,1)S(1)} %get-tuple-element.31.refs_2_.refs_15_), custom_call_target="tpu_custom_call" | custom-call | flops 1000 | bytes 1000 | tf_op jit(solution)/shard_map/spread_basis/pallas_call | solution.py:627
  34.6 0.0 collective-permute-done.11.refs_14_
  34.6 2.1 %gram_early.1.refs_2_.refs_5_ = bf16[1536,1536]{1,0:T(8,128)(2,1)S(1)} custom-call(s32[83]{0:T(128)S(1)} %get-tuple-element.34.refs_0_, bf16[1536,128]{1,0:T(8,128)(2,1)S(1)} %bitcast.15, bf16[1536,128]{1,0:T(8,128)(2,1)S(1)} %collective-permute-done.4.refs_5_.refs_2_, bf16[1536,128]{1,0:T(8,128)(2,1)S(1)} %collective-permute-done.2.refs_0_.refs_3_, ...), custom_call_target="tpu_custom_call" | custom-call | flops 1000 | bytes 1000 | tf_op jit(solution)/shard_map/gram_early/pallas_call | solution.py:642
  36.7 1.3 %collective-permute-done.15.refs_3_.refs_2_ = bf16[96,128]{1,0:T(8,128)(2,1)S(1)} collective-permute-done((bf16[96,128]{1,0:T(8,128)(2,1)S(1)}, bf16[96,128]{1,0:T(8,128)(2,1)S(1)}, u32[]{:S(2)}, u32[]{:S(2)}) %collective-permute-start.15) | collective-permute-done | bytes 24608 | tf_op jit(solution)/shard_map/ppermute | solution.py:37
  38.0 0.0 collective-permute-done.12.refs_0_.refs_6_
  38.0 0.5 collective-permute-done.13.refs_1_.refs_7_
  38.6 0.2 collective-permute-start.16
  38.7 1.5 %collective-permute-done.16.refs_9_ = bf16[1280,128]{1,0:T(8,128)(2,1)S(1)} collective-permute-done((bf16[1280,128]{1,0:T(8,128)(2,1)S(1)}, bf16[1280,128]{1,0:T(8,128)(2,1)S(1)}, u32[]{:S(2)}, u32[]{:S(2)}) %collective-permute-start.16) | collective-permute-done | bytes 327712 | tf_op jit(solution)/shard_map/ppermute | solution.py:37
  40.3 0.0 collective-permute-done.14.refs_8_.refs_1_
  40.3 4.6 %square_cube_coefficients.1 = (bf16[12,128,128]{2,1,0:T(8,128)(2,1)S(1)}, f32[8,128]{1,0:T(8,128)S(1)}) custom-call(s32[83]{0:T(128)S(1)} %get-tuple-element.25.refs_0_, s32[14]{0:T(128)S(1)} %get-tuple-element.26.refs_6_.refs_1_, bf16[16,128]{1,0:T(8,128)(2,1)S(1)} %get-tuple-element.32.refs_4_.refs_2_, bf16[128,1536]{1,0:T(8,128)(2,1)S(1)} %get-tuple-element.33.refs_3_, ...), custom_call_target="tpu_custom_call" | custom-call | flops 1300000000 | bytes 8000000 | tf_op jit(solution)/shard_map/square_cube_coefficients/pallas_call | solution.py:679
  44.8 0.2 collective-permute-start.17
  45.0 1.5 %collective-permute-start.18 = (f32[8,128]{1,0:T(8,128)S(1)}, f32[8,128]{1,0:T(8,128)S(1)}, u32[]{:S(2)}, u32[]{:S(2)}) collective-permute-start(f32[8,128]{1,0:T(8,128)S(1)} %get-tuple-element.40), channel_id=1, source_target_pairs={{3,0},{2,1},{1,2},{0,3},{7,4},{6,5},{5,6},{4,7},{11,8},{10,9},{9,1... | collective-permute-start | bytes 12296 | tf_op jit(solution)/shard_map/ppermute | solution.py:37
  46.5 0.1 pad.3.clone
  46.6 0.0 collective-permute-done.17
  46.6 1.5 %collective-permute-done.18 = f32[8,128]{1,0:T(8,128)S(1)} collective-permute-done((f32[8,128]{1,0:T(8,128)S(1)}, f32[8,128]{1,0:T(8,128)S(1)}, u32[]{:S(2)}, u32[]{:S(2)}) %collective-permute-start.18) | collective-permute-done | bytes 4128 | tf_op jit(solution)/shard_map/ppermute | solution.py:37
  48.1 0.1 slice.11
  48.1 0.1 slice.10
  48.2 0.1 maximum_maximum_fusion.refs_0_
  48.3 1.4 %collective-permute-start.19 = (f32[8,128]{1,0:T(8,128)S(1)}, f32[8,128]{1,0:T(8,128)S(1)}, u32[]{:S(2)}, u32[]{:S(2)}) collective-permute-start(f32[8,128]{1,0:T(8,128)S(1)} %maximum_maximum_fusion.refs_0_), channel_id=1, source_target_pairs={{16,0},{0,16},{17,1},{1,17},{18,2},{2,18},{19,3},{3,19},{20,4},{4,... | collective-permute-start | bytes 12296 | tf_op jit(solution)/shard_map/ppermute | solution.py:26
  49.7 0.8 %give_sign.1 = (bf16[1536,128]{1,0:T(8,128)(2,1)}, bf16[16,128]{1,0:T(8,128)(2,1)S(1)}) custom-call(bf16[1536,128]{1,0:T(8,128)(2,1)S(1)} %bitcast.18), custom_call_target="tpu_custom_call" | custom-call | bytes 1000 | tf_op jit(solution)/shard_map/give_sign/pallas_call | solution.py:243
  50.4 1.5 %collective-permute-done.19.refs_1_ = f32[8,128]{1,0:T(8,128)S(1)} collective-permute-done((f32[8,128]{1,0:T(8,128)S(1)}, f32[8,128]{1,0:T(8,128)S(1)}, u32[]{:S(2)}, u32[]{:S(2)}) %collective-permute-start.19) | collective-permute-done | bytes 4128 | tf_op jit(solution)/shard_map/ppermute | solution.py:26
  51.9 2.6 %collective-permute-start.20 = (f32[16,128]{1,0:T(8,128)S(1)}, f32[16,128]{1,0:T(8,128)S(1)}, u32[]{:S(2)}, u32[]{:S(2)}) collective-permute-start(f32[16,128]{1,0:T(8,128)S(1)} %stack_tiles.1.refs_0_), channel_id=1, source_target_pairs={{12,0},{8,4},{4,8},{0,12},{13,1},{9,5},{5,9},{1,13},{14,2},{10,6},... | collective-permute-start | bytes 24584 | tf_op jit(solution)/shard_map/ppermute | solution.py:32
  54.5 0.0 collective-permute-start.21
  54.5 2.8 %profiles.1 = (bf16[6,6,256,128]{3,2,1,0:T(8,128)(2,1)S(1)}, bf16[6,6,128,128]{3,2,1,0:T(8,128)(2,1)S(1)}) custom-call(bf16[96,128]{1,0:T(8,128)(2,1)S(1)} %get-tuple-element.37.refs_0_, bf16[2960,128]{1,0:T(8,128)(2,1)S(1)} %collective-permute-done.14.refs_8_.refs_1_, bf16[96,128]{1,0:T(8,128)(2,1)S(1)} %collective-permute-done.15.refs_3_.refs_2_), custom_call_target="tpu_custom_call" | custom-call | flops 1000 | bytes 1000 | tf_op jit(solution)/shard_map/profiles/pallas_call | solution.py:661
  57.3 0.0 collective-permute-done.20.refs_1_
  57.4 0.8 %collective-permute-done.21.refs_2_ = f32[16,128]{1,0:T(8,128)S(1)} collective-permute-done((f32[16,128]{1,0:T(8,128)S(1)}, f32[16,128]{1,0:T(8,128)S(1)}, u32[]{:S(2)}, u32[]{:S(2)}) %collective-permute-start.21) | collective-permute-done | bytes 8224 | tf_op jit(solution)/shard_map/ppermute | solution.py:32
  58.1 1.5 %density.1 = f32[256,128]{1,0:T(8,128)} custom-call(f32[16,128]{1,0:T(8,128)S(1)} %stack_tiles.1.refs_0_, f32[16,128]{1,0:T(8,128)S(1)} %collective-permute-done.20.refs_1_, f32[16,128]{1,0:T(8,128)S(1)} %collective-permute-done.21.refs_2_, bf16[6,6,256,128]{3,2,1,0:T(8,128)(2,1)S(1)} %get-tuple-element.42.refs_3_, bf16[4608,128]{1,0:T(8,128)(2,1)S(1)} %bitcast.17), custom_call_target="tpu_custom_call" | custom-call | flops 310000000 | bytes 4000000 | tf_op jit(solution)/shard_map/density/pallas_call | solution.py:718
  (10 shorter events, 0.1 us)
Async XLA Ops:
  0.6 12.4 %collective-permute-start.2 = (bf16[1536,128]{1,0:T(8,128)(2,1)}, bf16[1536,128]{1,0:T(8,128)(2,1)S(1)}, u32[]{:S(2)}, u32[]{:S(2)}) collective-permute-start(bf16[1536,128]{1,0:T(8,128)(2,1)} %bitcast.11), channel_id=1, source_target_pairs={{2,0},{3,1},{0,2},{1,3},{6,4},{7,5},{4,6},{5,7},{10,8},{11,9},{8,1... | collective-permute-start | bytes 1179656 | tf_op jit(solution)/shard_map/ppermute | solution.py:37
  3.7 10.8 %collective-permute-start.3 = (bf16[1536,128]{1,0:T(8,128)(2,1)}, bf16[1536,128]{1,0:T(8,128)(2,1)S(1)}, u32[]{:S(2)}, u32[]{:S(2)}) collective-permute-start(bf16[1536,128]{1,0:T(8,128)(2,1)} %bitcast.12), channel_id=1, source_target_pairs={{16,0},{0,16},{17,1},{1,17},{18,2},{2,18},{19,3},{3,19},{20,4},{4,... | collective-permute-start | bytes 1179656 | tf_op jit(solution)/shard_map/ppermute | solution.py:26
  5.2 15.0 %collective-permute-start.4 = (bf16[1536,128]{1,0:T(8,128)(2,1)}, bf16[1536,128]{1,0:T(8,128)(2,1)S(1)}, u32[]{:S(2)}, u32[]{:S(2)}) collective-permute-start(bf16[1536,128]{1,0:T(8,128)(2,1)} %bitcast.13), channel_id=1, source_target_pairs={{1,0},{0,1},{3,2},{2,3},{5,4},{4,5},{7,6},{6,7},{9,8},{8,9},{11,10... | collective-permute-start | bytes 1179656 | tf_op jit(solution)/shard_map/ppermute | solution.py:37
  7.7 9.8 %collective-permute-start = (bf16[656,128]{1,0:T(8,128)(2,1)}, bf16[656,128]{1,0:T(8,128)(2,1)S(1)}, u32[]{:S(2)}, u32[]{:S(2)}) collective-permute-start(bf16[656,128]{1,0:T(8,128)(2,1)} %pick_column_blocks.1.refs_2_), channel_id=1, source_target_pairs={{12,0},{8,4},{4,8},{0,12},{13,1},{9,5},{5,9},{1,13},{14,2},{10,6},... | collective-permute-start | bytes 503816 | tf_op jit(solution)/shard_map/ppermute | solution.py:32
  11.3 8.9 %collective-permute-start.1 = (bf16[656,128]{1,0:T(8,128)(2,1)}, bf16[656,128]{1,0:T(8,128)(2,1)S(1)}, u32[]{:S(2)}, u32[]{:S(2)}) collective-permute-start(bf16[656,128]{1,0:T(8,128)(2,1)} %pick_column_blocks.1.refs_2_), channel_id=1, source_target_pairs={{4,0},{0,4},{12,8},{8,12},{5,1},{1,5},{13,9},{9,13},{6,2},{2,6},{1... | collective-permute-start | bytes 503816 | tf_op jit(solution)/shard_map/ppermute | solution.py:32
  14.4 0.9 %copy-start.1 = (bf16[656,128]{1,0:T(8,128)(2,1)S(1)}, bf16[656,128]{1,0:T(8,128)(2,1)}, u32[]{:S(2)}) copy-start(bf16[656,128]{1,0:T(8,128)(2,1)} %pick_column_blocks.1.refs_2_) | copy-start | bytes 503812
  15.4 6.0 %collective-permute-start.9 = (bf16[640,128]{1,0:T(8,128)(2,1)S(1)}, bf16[640,128]{1,0:T(8,128)(2,1)S(1)}, u32[]{:S(2)}, u32[]{:S(2)}) collective-permute-start(bf16[640,128]{1,0:T(8,128)(2,1)S(1)} %get-tuple-element.29), channel_id=1, source_target_pairs={{16,0},{0,16},{17,1},{1,17},{18,2},{2,18},{19,3},{3,19},{20,4},{4,... | collective-permute-start | bytes 491528 | tf_op jit(solution)/shard_map/ppermute | solution.py:26
  16.9 5.3 %collective-permute-start.10 = (bf16[640,128]{1,0:T(8,128)(2,1)S(1)}, bf16[640,128]{1,0:T(8,128)(2,1)S(1)}, u32[]{:S(2)}, u32[]{:S(2)}) collective-permute-start(bf16[640,128]{1,0:T(8,128)(2,1)S(1)} %get-tuple-element.30), channel_id=1, source_target_pairs={{2,0},{3,1},{0,2},{1,3},{6,4},{7,5},{4,6},{5,7},{10,8},{11,9},{8,1... | collective-permute-start | bytes 491528 | tf_op jit(solution)/shard_map/ppermute | solution.py:37
  20.3 10.7 %collective-permute-start.5 = (bf16[1456,128]{1,0:T(8,128)(2,1)S(1)}, bf16[1456,128]{1,0:T(8,128)(2,1)S(1)}, u32[]{:S(2)}, u32[]{:S(2)}) collective-permute-start(bf16[1456,128]{1,0:T(8,128)(2,1)S(1)} %get-tuple-element.27), channel_id=1, source_target_pairs={{2,0},{3,1},{0,2},{1,3},{6,4},{7,5},{4,6},{5,7},{10,8},{11,9},{8,1... | collective-permute-start | bytes 1118216 | tf_op jit(solution)/shard_map/ppermute | solution.py:37
  20.9 1.6 %copy-start.2 = (s32[32,12]{0,1:T(8,128)S(1)}, s32[32,12]{0,1:T(8,128)}, u32[]{:S(2)}) copy-start(s32[32,12]{0,1:T(8,128)} %param.9) | copy-start | bytes 4612
  20.9 1.6 %copy-start.4 = (s32[32]{0:T(128)S(1)}, s32[32]{0:T(128)}, u32[]{:S(2)}) copy-start(s32[32]{0:T(128)} %refs_1_.3) | copy-start | bytes 388
  20.9 10.3 %collective-permute-start.6 = (bf16[1456,128]{1,0:T(8,128)(2,1)S(1)}, bf16[1456,128]{1,0:T(8,128)(2,1)S(1)}, u32[]{:S(2)}, u32[]{:S(2)}) collective-permute-start(bf16[1456,128]{1,0:T(8,128)(2,1)S(1)} %get-tuple-element.24.refs_2_), channel_id=1, source_target_pairs={{16,0},{0,16},{17,1},{1,17},{18,2},{2,18},{19,3},{3,19},{20,4},{4,... | collective-permute-start | bytes 1118216 | tf_op jit(solution)/shard_map/ppermute | solution.py:26
  21.4 9.8 %collective-permute-start.7 = (bf16[1536,128]{1,0:T(8,128)(2,1)S(1)}, bf16[1536,128]{1,0:T(8,128)(2,1)S(1)}, u32[]{:S(2)}, u32[]{:S(2)}) collective-permute-start(bf16[1536,128]{1,0:T(8,128)(2,1)S(1)} %collective-permute-done.2.refs_0_.refs_3_), channel_id=1, source_target_pairs={{1,0},{0,1},{3,2},{2,3},{5,4},{4,5},{7,6},{6,7},{9,8},{8,9},{11,10... | collective-permute-start | bytes 1179656 | tf_op jit(solution)/shard_map/ppermute | solution.py:37
  21.4 9.8 %collective-permute-start.8 = (bf16[1536,128]{1,0:T(8,128)(2,1)S(1)}, bf16[1536,128]{1,0:T(8,128)(2,1)S(1)}, u32[]{:S(2)}, u32[]{:S(2)}) collective-permute-start(bf16[1536,128]{1,0:T(8,128)(2,1)S(1)} %collective-permute-done.3.refs_1_.refs_4_.refs_7_), channel_id=1, source_target_pairs={{1,0},{0,1},{3,2},{2,3},{5,4},{4,5},{7,6},{6,7},{9,8},{8,9},{11,10... | collective-permute-start | bytes 1179656 | tf_op jit(solution)/shard_map/ppermute | solution.py:37
  22.3 11.2 %copy-start.3 = (bf16[32,6,128]{2,0,1:T(8,128)(2,1)S(1)}, bf16[32,6,128]{2,0,1:T(8,128)(2,1)}, u32[]{:S(2)}) copy-start(bf16[32,6,128]{2,0,1:T(8,128)(2,1)} %param.11) | copy-start | bytes 147460
  22.3 12.2 %copy-start = (bf16[1,12,128,128]{3,2,1,0:T(8,128)(2,1)S(1)}, bf16[1,12,128,128]{3,2,1,0:T(8,128)(2,1)}, u32[]{:S(2)}) copy-start(bf16[1,12,128,128]{3,2,1,0:T(8,128)(2,1)} %param.8) | copy-start | bytes 1179652
  22.3 12.2 %collective-permute-start.11 = (bf16[2560,128]{1,0:T(8,128)(2,1)S(1)}, bf16[2560,128]{1,0:T(8,128)(2,1)S(1)}, u32[]{:S(2)}, u32[]{:S(2)}) collective-permute-start(bf16[2560,128]{1,0:T(8,128)(2,1)S(1)} %pack_two_mate.1.refs_5_), channel_id=1, source_target_pairs={{1,0},{0,1},{3,2},{2,3},{5,4},{4,5},{7,6},{6,7},{9,8},{8,9},{11,10... | collective-permute-start | bytes 1966088 | tf_op jit(solution)/shard_map/ppermute | solution.py:37
  31.3 8.9 %collective-permute-start.14 = (bf16[2960,128]{1,0:T(8,128)(2,1)S(1)}, bf16[2960,128]{1,0:T(8,128)(2,1)S(1)}, u32[]{:S(2)}, u32[]{:S(2)}) collective-permute-start(bf16[2960,128]{1,0:T(8,128)(2,1)S(1)} %get-tuple-element.36), channel_id=1, source_target_pairs={{1,0},{0,1},{3,2},{2,3},{5,4},{4,5},{7,6},{6,7},{9,8},{8,9},{11,10... | collective-permute-start | bytes 2273288 | tf_op jit(solution)/shard_map/ppermute | solution.py:37
  31.4 6.6 %collective-permute-start.12 = (bf16[640,128]{1,0:T(8,128)(2,1)S(1)}, bf16[640,128]{1,0:T(8,128)(2,1)S(1)}, u32[]{:S(2)}, u32[]{:S(2)}) collective-permute-start(bf16[640,128]{1,0:T(8,128)(2,1)S(1)} %get-tuple-element.31.refs_2_.refs_15_), channel_id=1, source_target_pairs={{16,0},{0,16},{17,1},{1,17},{18,2},{2,18},{19,3},{3,19},{20,4},{4,... | collective-permute-start | bytes 491528 | tf_op jit(solution)/shard_map/ppermute | solution.py:26
  32.0 6.5 %collective-permute-start.13 = (bf16[640,128]{1,0:T(8,128)(2,1)S(1)}, bf16[640,128]{1,0:T(8,128)(2,1)S(1)}, u32[]{:S(2)}, u32[]{:S(2)}) collective-permute-start(bf16[640,128]{1,0:T(8,128)(2,1)S(1)} %get-tuple-element.35), channel_id=1, source_target_pairs={{2,0},{3,1},{0,2},{1,3},{6,4},{7,5},{4,6},{5,7},{10,8},{11,9},{8,1... | collective-permute-start | bytes 491528 | tf_op jit(solution)/shard_map/ppermute | solution.py:37
  33.5 4.5 %collective-permute-start.15 = (bf16[96,128]{1,0:T(8,128)(2,1)S(1)}, bf16[96,128]{1,0:T(8,128)(2,1)S(1)}, u32[]{:S(2)}, u32[]{:S(2)}) collective-permute-start(bf16[96,128]{1,0:T(8,128)(2,1)S(1)} %get-tuple-element.37.refs_0_), channel_id=1, source_target_pairs={{3,0},{2,1},{1,2},{0,3},{7,4},{6,5},{5,6},{4,7},{11,8},{10,9},{9,1... | collective-permute-start | bytes 73736 | tf_op jit(solution)/shard_map/ppermute | solution.py:37
  38.6 1.7 %collective-permute-start.16 = (bf16[1280,128]{1,0:T(8,128)(2,1)S(1)}, bf16[1280,128]{1,0:T(8,128)(2,1)S(1)}, u32[]{:S(2)}, u32[]{:S(2)}) collective-permute-start(bf16[1280,128]{1,0:T(8,128)(2,1)S(1)} %pack_four.1), channel_id=1, source_target_pairs={{1,0},{0,1},{3,2},{2,3},{5,4},{4,5},{7,6},{6,7},{9,8},{8,9},{11,10... | collective-permute-start | bytes 983048 | tf_op jit(solution)/shard_map/ppermute | solution.py:37
  44.8 1.7 %collective-permute-start.17 = (f32[8,128]{1,0:T(8,128)S(1)}, f32[8,128]{1,0:T(8,128)S(1)}, u32[]{:S(2)}, u32[]{:S(2)}) collective-permute-start(f32[8,128]{1,0:T(8,128)S(1)} %get-tuple-element.40), channel_id=1, source_target_pairs={{1,0},{0,1},{3,2},{2,3},{5,4},{4,5},{7,6},{6,7},{9,8},{8,9},{11,10... | collective-permute-start | bytes 12296 | tf_op jit(solution)/shard_map/ppermute | solution.py:37
  45.0 3.0 %collective-permute-start.18 = (f32[8,128]{1,0:T(8,128)S(1)}, f32[8,128]{1,0:T(8,128)S(1)}, u32[]{:S(2)}, u32[]{:S(2)}) collective-permute-start(f32[8,128]{1,0:T(8,128)S(1)} %get-tuple-element.40), channel_id=1, source_target_pairs={{3,0},{2,1},{1,2},{0,3},{7,4},{6,5},{5,6},{4,7},{11,8},{10,9},{9,1... | collective-permute-start | bytes 12296 | tf_op jit(solution)/shard_map/ppermute | solution.py:37
  48.3 3.6 %collective-permute-start.19 = (f32[8,128]{1,0:T(8,128)S(1)}, f32[8,128]{1,0:T(8,128)S(1)}, u32[]{:S(2)}, u32[]{:S(2)}) collective-permute-start(f32[8,128]{1,0:T(8,128)S(1)} %maximum_maximum_fusion.refs_0_), channel_id=1, source_target_pairs={{16,0},{0,16},{17,1},{1,17},{18,2},{2,18},{19,3},{3,19},{20,4},{4,... | collective-permute-start | bytes 12296 | tf_op jit(solution)/shard_map/ppermute | solution.py:26
  51.9 5.4 %collective-permute-start.20 = (f32[16,128]{1,0:T(8,128)S(1)}, f32[16,128]{1,0:T(8,128)S(1)}, u32[]{:S(2)}, u32[]{:S(2)}) collective-permute-start(f32[16,128]{1,0:T(8,128)S(1)} %stack_tiles.1.refs_0_), channel_id=1, source_target_pairs={{12,0},{8,4},{4,8},{0,12},{13,1},{9,5},{5,9},{1,13},{14,2},{10,6},... | collective-permute-start | bytes 24584 | tf_op jit(solution)/shard_map/ppermute | solution.py:32
  54.5 3.7 %collective-permute-start.21 = (f32[16,128]{1,0:T(8,128)S(1)}, f32[16,128]{1,0:T(8,128)S(1)}, u32[]{:S(2)}, u32[]{:S(2)}) collective-permute-start(f32[16,128]{1,0:T(8,128)S(1)} %stack_tiles.1.refs_0_), channel_id=1, source_target_pairs={{4,0},{0,4},{12,8},{8,12},{5,1},{1,5},{13,9},{9,13},{6,2},{2,6},{1... | collective-permute-start | bytes 24584 | tf_op jit(solution)/shard_map/ppermute | solution.py:32

commit v19 on v18

--- a/solution.py
+++ b/solution.py
@@ -405,16 +405,22 @@
 
 def density_kernel(column_steps, *refs):
     coef_refs = refs[:column_steps]
-    plane_ref, line_ref = refs[column_steps : column_steps + 2]
-    out_ref, terms = refs[-2:]
+    plane_ref, line_ref, out_ref = refs[column_steps:]
+    total = jnp.zeros(out_ref.shape, jnp.float32)
+    wide = SHELLS * LANES
     for o in range(plane_ref.shape[0]):
         coef = coef_refs[-o % column_steps]
         first = 8 * (o // column_steps)
-        for s in range(SHELLS):
-            scaled = plane_ref[o, s].astype(jnp.float32) * coef[first + s : first + s + 1, :]
-            at = (o * SHELLS + s) * LANES
-            terms[:, at : at + LANES] = scaled.astype(terms.dtype)
-    out_ref[...] = jnp.dot(terms[...], line_ref[...], preferred_element_type=jnp.float32)
+        terms = [
+            (plane_ref[o, s].astype(jnp.float32) * coef[first + s : first + s + 1, :]).astype(line_ref.dtype)
+            for s in range(SHELLS)
+        ]
+        total = total + jnp.dot(
+            jnp.concatenate(terms, axis=1),
+            line_ref[o * wide : (o + 1) * wide],
+            preferred_element_type=jnp.float32,
+        )
+    out_ref[...] = total
 
 
 def local(sign_start, neighbors, atom_size, basis_proj, pair_extent, atom_x, atom_y, atom_z):
@@ -720,7 +726,6 @@
         out_shape=jax.ShapeDtypeStruct((BX * BY, BZ), jnp.float32),
         in_specs=[VMEM] * (len(received) + 2),
         out_specs=VMEM,
-        scratch_shapes=[pltpu.VMEM((BX * BY, tiles * SHELLS * LANES), jnp.bfloat16)],
         compiler_params=pltpu.CompilerParams(vmem_limit_bytes=16 << 20),
         cost_estimate=pl.CostEstimate(flops=310_000_000, bytes_accessed=4_000_000, transcendentals=0),
         name="density",

time: 59.9 us -> 59.8 us (level)
  transfers between devices with their start and end apart: 22 -> 22, of which waited for: 12 -> 12; matrix products, arithmetic and copies ran while one was open for 0% -> 0% of each run, Pallas kernels for 23% -> 22%
where the time goes in v19:
time: 59.8 us; the launch traced here: 59.4 us
  starting transfers between devices  20.2 us (34%)
  Pallas kernels  19.2 us (32%)
  waiting for transfers between devices  18 us (30%)
  local copies, waits for them, and re-layouts  1.16 us (2%)
  between operations  0.79 us (1%)
    ppermute x13, waiting for transfers between devices, from_layer(): return lax.ppermute(x, 'layer', [(i ^ flip, i) for i in range(count)])  11.5 us
    ppermute x13, starting transfers between devices, from_layer(): return lax.ppermute(x, 'layer', [(i ^ flip, i) for i in range(count)])  8.06 us
    ppermute x4, starting transfers between devices, from_column(): lax.ppermute(x, 'col', [((i + step[i]) % count, i) for i in range(count)])  6.39 us
    ppermute x5, starting transfers between devices, from_offset(): lax.ppermute(x, axis, [((i + step) % count, i) for i in range(count)])  5.7 us
    pallas_call x1, Pallas kernels, local(): pl.pallas_call(functools.partial(step_kernel, len(late_values)), out_shap...  4.48 us
    pallas_call x1, Pallas kernels, local(): pl.pallas_call(functools.partial(prepare_kernel, axes, count, tuple(layou...  3.97 us
    ppermute x4, waiting for transfers between devices, from_column(): lax.ppermute(x, 'col', [((i + step[i]) % count, i) for i in range(count)])  3.5 us
    ppermute x5, waiting for transfers between devices, from_offset(): lax.ppermute(x, axis, [((i + step) % count, i) for i in range(count)])  3.01 us
  transfers between devices with their start and end apart: 22, of which 12 were waited for; matrix products, arithmetic and copies ran while one was open for 0% of the time, Pallas kernels for 22%

profile of v19, /device:TPU:0, one launch (start us, length us, event | category | flops | bytes accessed | tf_op | source)
XLA Modules:
  0.0 59.4 jit_solution(8714224870929841346)
XLA Ops:
  0.6 3.0 %collective-permute-start.2 = (bf16[1536,128]{1,0:T(8,128)(2,1)}, bf16[1536,128]{1,0:T(8,128)(2,1)S(1)}, u32[]{:S(2)}, u32[]{:S(2)}) collective-permute-start(bf16[1536,128]{1,0:T(8,128)(2,1)} %bitcast.11), channel_id=1, source_target_pairs={{2,0},{3,1},{0,2},{1,3},{6,4},{7,5},{4,6},{5,7},{10,8},{11,9},{8,1... | collective-permute-start | bytes 1179656 | tf_op jit(solution)/shard_map/ppermute | solution.py:37
  3.7 1.5 %collective-permute-start.3 = (bf16[1536,128]{1,0:T(8,128)(2,1)}, bf16[1536,128]{1,0:T(8,128)(2,1)S(1)}, u32[]{:S(2)}, u32[]{:S(2)}) collective-permute-start(bf16[1536,128]{1,0:T(8,128)(2,1)} %bitcast.12), channel_id=1, source_target_pairs={{16,0},{0,16},{17,1},{1,17},{18,2},{2,18},{19,3},{3,19},{20,4},{4,... | collective-permute-start | bytes 1179656 | tf_op jit(solution)/shard_map/ppermute | solution.py:26
  5.2 0.0 collective-permute-start.4
  5.2 2.5 %pick_column_blocks.1.refs_2_ = bf16[656,128]{1,0:T(8,128)(2,1)} custom-call(s32[12,32]{1,0:T(8,128)} %bitcast.19, s32[1,12]{1,0:T(1,128)} %refs_1_.2, s32[32]{0:T(128)} %refs_2_.1, s32[32]{0:T(128)} %refs_3_.1, s32[32]{0:T(128)} %refs_4_.1, bf16[12,128,128]{2,1,0:T(8,128)(2,1)} %bitcast.14), custom_call_target="tpu_custom_call" | custom-call | tf_op jit(solution)/shard_map/pick_column_blocks/pallas_call | solution.py:454
  7.6 3.7 %collective-permute-start = (bf16[656,128]{1,0:T(8,128)(2,1)}, bf16[656,128]{1,0:T(8,128)(2,1)S(1)}, u32[]{:S(2)}, u32[]{:S(2)}) collective-permute-start(bf16[656,128]{1,0:T(8,128)(2,1)} %pick_column_blocks.1.refs_2_), channel_id=1, source_target_pairs={{12,0},{8,4},{4,8},{0,12},{13,1},{9,5},{5,9},{1,13},{14,2},{10,6},... | collective-permute-start | bytes 503816 | tf_op jit(solution)/shard_map/ppermute | solution.py:32
  11.3 0.0 collective-permute-start.1
  11.3 1.7 %collective-permute-done.2.refs_0_.refs_3_ = bf16[1536,128]{1,0:T(8,128)(2,1)S(1)} collective-permute-done((bf16[1536,128]{1,0:T(8,128)(2,1)}, bf16[1536,128]{1,0:T(8,128)(2,1)S(1)}, u32[]{:S(2)}, u32[]{:S(2)}) %collective-permute-start.2) | collective-permute-done | bytes 393248 | tf_op jit(solution)/shard_map/ppermute | solution.py:37
  13.0 1.5 %collective-permute-done.3.refs_1_.refs_4_.refs_7_ = bf16[1536,128]{1,0:T(8,128)(2,1)S(1)} collective-permute-done((bf16[1536,128]{1,0:T(8,128)(2,1)}, bf16[1536,128]{1,0:T(8,128)(2,1)S(1)}, u32[]{:S(2)}, u32[]{:S(2)}) %collective-permute-start.3) | collective-permute-done | bytes 393248 | tf_op jit(solution)/shard_map/ppermute | solution.py:26
  14.5 0.9 %copy-done.1 = bf16[656,128]{1,0:T(8,128)(2,1)S(1)} copy-done((bf16[656,128]{1,0:T(8,128)(2,1)S(1)}, bf16[656,128]{1,0:T(8,128)(2,1)}, u32[]{:S(2)}) %copy-start.1) | copy-done | bytes 167960
  15.4 1.6 %collective-permute-start.9 = (bf16[640,128]{1,0:T(8,128)(2,1)S(1)}, bf16[640,128]{1,0:T(8,128)(2,1)S(1)}, u32[]{:S(2)}, u32[]{:S(2)}) collective-permute-start(bf16[640,128]{1,0:T(8,128)(2,1)S(1)} %get-tuple-element.29), channel_id=1, source_target_pairs={{16,0},{0,16},{17,1},{1,17},{18,2},{2,18},{19,3},{3,19},{20,4},{4,... | collective-permute-start | bytes 491528 | tf_op jit(solution)/shard_map/ppermute | solution.py:26
  16.9 0.5 collective-permute-start.10
  17.5 0.0 collective-permute-done.refs_0_.refs_3_.refs_5_
  17.5 2.7 %collective-permute-done.1.refs_1_.refs_2_.refs_4_ = bf16[656,128]{1,0:T(8,128)(2,1)S(1)} collective-permute-done((bf16[656,128]{1,0:T(8,128)(2,1)}, bf16[656,128]{1,0:T(8,128)(2,1)S(1)}, u32[]{:S(2)}, u32[]{:S(2)}) %collective-permute-start.1) | collective-permute-done | bytes 167968 | tf_op jit(solution)/shard_map/ppermute | solution.py:32
  20.2 0.0 collective-permute-done.4.refs_5_.refs_2_
  20.2 0.1 pack_two.1
  20.3 0.6 collective-permute-start.5
  20.9 0.5 collective-permute-start.6
  21.4 0.0 collective-permute-start.7
  21.4 0.0 collective-permute-done.9.refs_0_.refs_10_
  21.4 0.5 collective-permute-start.8
  21.9 0.4 collective-permute-done.10.refs_1_.refs_11_
  22.3 0.0 copy-start.3
  22.3 0.0 copy-start
  22.3 0.1 collective-permute-start.11
  22.4 0.0 copy-done.2
  22.4 4.0 %prepare.1 = (s32[83]{0:T(128)S(1)}, s32[83]{0:T(128)S(1)}, s32[14]{0:T(128)S(1)}) custom-call(s32[12,32]{1,0:T(8,128)S(1)} %bitcast.20, s32[32]{0:T(128)S(1)} %copy-done.4, bf16[1456,128]{1,0:T(8,128)(2,1)S(1)} %get-tuple-element.24.refs_2_), custom_call_target="tpu_custom_call" | custom-call | flops 1000 | bytes 1000 | tf_op jit(solution)/shard_map/prepare/pallas_call | solution.py:585
  26.4 4.6 %collective-permute-done.5.refs_0_.refs_13_ = bf16[1456,128]{1,0:T(8,128)(2,1)S(1)} collective-permute-done((bf16[1456,128]{1,0:T(8,128)(2,1)S(1)}, bf16[1456,128]{1,0:T(8,128)(2,1)S(1)}, u32[]{:S(2)}, u32[]{:S(2)}) %collective-permute-start.5) | collective-permute-done | bytes 372768 | tf_op jit(solution)/shard_map/ppermute | solution.py:37
  31.0 0.2 collective-permute-done.6.refs_2_.refs_12_
  31.2 0.0 collective-permute-done.7.refs_3_.refs_9_
  31.2 0.0 collective-permute-done.8.refs_4_.refs_8_
  31.2 0.1 pack_three.1
  31.3 0.1 collective-permute-start.14
  31.4 0.6 %collective-permute-start.12 = (bf16[640,128]{1,0:T(8,128)(2,1)S(1)}, bf16[640,128]{1,0:T(8,128)(2,1)S(1)}, u32[]{:S(2)}, u32[]{:S(2)}) collective-permute-start(bf16[640,128]{1,0:T(8,128)(2,1)S(1)} %get-tuple-element.31.refs_2_.refs_15_), channel_id=1, source_target_pairs={{16,0},{0,16},{17,1},{1,17},{18,2},{2,18},{19,3},{3,19},{20,4},{4,... | collective-permute-start | bytes 491528 | tf_op jit(solution)/shard_map/ppermute | solution.py:26
  32.0 1.6 %collective-permute-start.13 = (bf16[640,128]{1,0:T(8,128)(2,1)S(1)}, bf16[640,128]{1,0:T(8,128)(2,1)S(1)}, u32[]{:S(2)}, u32[]{:S(2)}) collective-permute-start(bf16[640,128]{1,0:T(8,128)(2,1)S(1)} %get-tuple-element.35), channel_id=1, source_target_pairs={{2,0},{3,1},{0,2},{1,3},{6,4},{7,5},{4,6},{5,7},{10,8},{11,9},{8,1... | collective-permute-start | bytes 491528 | tf_op jit(solution)/shard_map/ppermute | solution.py:37
  33.5 0.0 collective-permute-start.15
  33.5 0.0 copy-done.3
  33.5 1.0 %spread_basis.1 = (bf16[128,1536]{1,0:T(8,128)(2,1)S(1)}, bf16[16,128]{1,0:T(8,128)(2,1)S(1)}) custom-call(s32[12,32]{1,0:T(8,128)S(1)} %bitcast.21, bf16[192,128]{1,0:T(8,128)(2,1)S(1)} %bitcast.22, bf16[640,128]{1,0:T(8,128)(2,1)S(1)} %get-tuple-element.31.refs_2_.refs_15_), custom_call_target="tpu_custom_call" | custom-call | flops 1000 | bytes 1000 | tf_op jit(solution)/shard_map/spread_basis/pallas_call | solution.py:633
  34.6 0.0 collective-permute-done.11.refs_14_
  34.6 0.0 copy-done
  34.6 1.9 %gram_early.1.refs_2_.refs_5_ = bf16[1536,1536]{1,0:T(8,128)(2,1)S(1)} custom-call(s32[83]{0:T(128)S(1)} %get-tuple-element.34.refs_0_, bf16[1536,128]{1,0:T(8,128)(2,1)S(1)} %bitcast.15, bf16[1536,128]{1,0:T(8,128)(2,1)S(1)} %collective-permute-done.4.refs_5_.refs_2_, bf16[1536,128]{1,0:T(8,128)(2,1)S(1)} %collective-permute-done.2.refs_0_.refs_3_, ...), custom_call_target="tpu_custom_call" | custom-call | flops 1000 | bytes 1000 | tf_op jit(solution)/shard_map/gram_early/pallas_call | solution.py:648
  36.5 1.5 %collective-permute-done.15.refs_3_.refs_2_ = bf16[96,128]{1,0:T(8,128)(2,1)S(1)} collective-permute-done((bf16[96,128]{1,0:T(8,128)(2,1)S(1)}, bf16[96,128]{1,0:T(8,128)(2,1)S(1)}, u32[]{:S(2)}, u32[]{:S(2)}) %collective-permute-start.15) | collective-permute-done | bytes 24608 | tf_op jit(solution)/shard_map/ppermute | solution.py:37
  38.0 0.0 collective-permute-done.12.refs_0_.refs_6_
  38.0 0.5 collective-permute-done.13.refs_1_.refs_7_
  38.5 0.2 collective-permute-start.16
  38.7 1.5 %collective-permute-done.16.refs_9_ = bf16[1280,128]{1,0:T(8,128)(2,1)S(1)} collective-permute-done((bf16[1280,128]{1,0:T(8,128)(2,1)S(1)}, bf16[1280,128]{1,0:T(8,128)(2,1)S(1)}, u32[]{:S(2)}, u32[]{:S(2)}) %collective-permute-start.16) | collective-permute-done | bytes 327712 | tf_op jit(solution)/shard_map/ppermute | solution.py:37
  40.2 0.0 collective-permute-done.14.refs_8_.refs_1_
  40.2 4.5 %square_cube_coefficients.1 = (bf16[12,128,128]{2,1,0:T(8,128)(2,1)S(1)}, f32[8,128]{1,0:T(8,128)S(1)}) custom-call(s32[83]{0:T(128)S(1)} %get-tuple-element.25.refs_0_, s32[14]{0:T(128)S(1)} %get-tuple-element.26.refs_6_.refs_1_, bf16[16,128]{1,0:T(8,128)(2,1)S(1)} %get-tuple-element.32.refs_4_.refs_2_, bf16[128,1536]{1,0:T(8,128)(2,1)S(1)} %get-tuple-element.33.refs_3_, ...), custom_call_target="tpu_custom_call" | custom-call | flops 1300000000 | bytes 8000000 | tf_op jit(solution)/shard_map/square_cube_coefficients/pallas_call | solution.py:685
  44.7 0.1 collective-permute-start.17
  44.8 1.5 %collective-permute-start.18 = (f32[8,128]{1,0:T(8,128)S(1)}, f32[8,128]{1,0:T(8,128)S(1)}, u32[]{:S(2)}, u32[]{:S(2)}) collective-permute-start(f32[8,128]{1,0:T(8,128)S(1)} %get-tuple-element.40), channel_id=1, source_target_pairs={{3,0},{2,1},{1,2},{0,3},{7,4},{6,5},{5,6},{4,7},{11,8},{10,9},{9,1... | collective-permute-start | bytes 12296 | tf_op jit(solution)/shard_map/ppermute | solution.py:37
  46.3 0.1 pad.3.clone
  46.4 0.0 collective-permute-done.17
  46.4 1.4 %collective-permute-done.18 = f32[8,128]{1,0:T(8,128)S(1)} collective-permute-done((f32[8,128]{1,0:T(8,128)S(1)}, f32[8,128]{1,0:T(8,128)S(1)}, u32[]{:S(2)}, u32[]{:S(2)}) %collective-permute-start.18) | collective-permute-done | bytes 4128 | tf_op jit(solution)/shard_map/ppermute | solution.py:37
  47.8 0.1 slice.11
  47.9 0.1 slice.10
  48.0 0.1 maximum_maximum_fusion.refs_0_
  48.0 1.5 %collective-permute-start.19 = (f32[8,128]{1,0:T(8,128)S(1)}, f32[8,128]{1,0:T(8,128)S(1)}, u32[]{:S(2)}, u32[]{:S(2)}) collective-permute-start(f32[8,128]{1,0:T(8,128)S(1)} %maximum_maximum_fusion.refs_0_), channel_id=1, source_target_pairs={{16,0},{0,16},{17,1},{1,17},{18,2},{2,18},{19,3},{3,19},{20,4},{4,... | collective-permute-start | bytes 12296 | tf_op jit(solution)/shard_map/ppermute | solution.py:26
  49.6 0.8 %give_sign.1 = (bf16[1536,128]{1,0:T(8,128)(2,1)}, bf16[16,128]{1,0:T(8,128)(2,1)S(1)}) custom-call(bf16[1536,128]{1,0:T(8,128)(2,1)S(1)} %bitcast.18), custom_call_target="tpu_custom_call" | custom-call | bytes 1000 | tf_op jit(solution)/shard_map/give_sign/pallas_call | solution.py:243
  50.3 1.3 %collective-permute-done.19.refs_1_ = f32[8,128]{1,0:T(8,128)S(1)} collective-permute-done((f32[8,128]{1,0:T(8,128)S(1)}, f32[8,128]{1,0:T(8,128)S(1)}, u32[]{:S(2)}, u32[]{:S(2)}) %collective-permute-start.19) | collective-permute-done | bytes 4128 | tf_op jit(solution)/shard_map/ppermute | solution.py:26
  51.7 2.7 %collective-permute-start.20 = (f32[16,128]{1,0:T(8,128)S(1)}, f32[16,128]{1,0:T(8,128)S(1)}, u32[]{:S(2)}, u32[]{:S(2)}) collective-permute-start(f32[16,128]{1,0:T(8,128)S(1)} %stack_tiles.1.refs_0_), channel_id=1, source_target_pairs={{12,0},{8,4},{4,8},{0,12},{13,1},{9,5},{5,9},{1,13},{14,2},{10,6},... | collective-permute-start | bytes 24584 | tf_op jit(solution)/shard_map/ppermute | solution.py:32
  54.4 0.0 collective-permute-start.21
  54.4 2.8 %profiles.1 = (bf16[6,6,256,128]{3,2,1,0:T(8,128)(2,1)S(1)}, bf16[6,6,128,128]{3,2,1,0:T(8,128)(2,1)S(1)}) custom-call(bf16[96,128]{1,0:T(8,128)(2,1)S(1)} %get-tuple-element.37.refs_0_, bf16[2960,128]{1,0:T(8,128)(2,1)S(1)} %collective-permute-done.14.refs_8_.refs_1_, bf16[96,128]{1,0:T(8,128)(2,1)S(1)} %collective-permute-done.15.refs_3_.refs_2_), custom_call_target="tpu_custom_call" | custom-call | flops 1000 | bytes 1000 | tf_op jit(solution)/shard_map/profiles/pallas_call | solution.py:667
  57.2 0.0 collective-permute-done.20.refs_1_
  57.2 0.8 %collective-permute-done.21.refs_2_ = f32[16,128]{1,0:T(8,128)S(1)} collective-permute-done((f32[16,128]{1,0:T(8,128)S(1)}, f32[16,128]{1,0:T(8,128)S(1)}, u32[]{:S(2)}, u32[]{:S(2)}) %collective-permute-start.21) | collective-permute-done | bytes 8224 | tf_op jit(solution)/shard_map/ppermute | solution.py:32
  58.0 1.4 %density.1 = f32[256,128]{1,0:T(8,128)} custom-call(f32[16,128]{1,0:T(8,128)S(1)} %stack_tiles.1.refs_0_, f32[16,128]{1,0:T(8,128)S(1)} %collective-permute-done.20.refs_1_, f32[16,128]{1,0:T(8,128)S(1)} %collective-permute-done.21.refs_2_, bf16[6,6,256,128]{3,2,1,0:T(8,128)(2,1)S(1)} %get-tuple-element.42.refs_3_, bf16[4608,128]{1,0:T(8,128)(2,1)S(1)} %bitcast.17), custom_call_target="tpu_custom_call" | custom-call | flops 310000000 | bytes 4000000 | tf_op jit(solution)/shard_map/density/pallas_call | solution.py:724
  (10 shorter events, 0.1 us)
Async XLA Ops:
  0.6 12.4 %collective-permute-start.2 = (bf16[1536,128]{1,0:T(8,128)(2,1)}, bf16[1536,128]{1,0:T(8,128)(2,1)S(1)}, u32[]{:S(2)}, u32[]{:S(2)}) collective-permute-start(bf16[1536,128]{1,0:T(8,128)(2,1)} %bitcast.11), channel_id=1, source_target_pairs={{2,0},{3,1},{0,2},{1,3},{6,4},{7,5},{4,6},{5,7},{10,8},{11,9},{8,1... | collective-permute-start | bytes 1179656 | tf_op jit(solution)/shard_map/ppermute | solution.py:37
  3.7 10.8 %collective-permute-start.3 = (bf16[1536,128]{1,0:T(8,128)(2,1)}, bf16[1536,128]{1,0:T(8,128)(2,1)S(1)}, u32[]{:S(2)}, u32[]{:S(2)}) collective-permute-start(bf16[1536,128]{1,0:T(8,128)(2,1)} %bitcast.12), channel_id=1, source_target_pairs={{16,0},{0,16},{17,1},{1,17},{18,2},{2,18},{19,3},{3,19},{20,4},{4,... | collective-permute-start | bytes 1179656 | tf_op jit(solution)/shard_map/ppermute | solution.py:26
  5.2 15.0 %collective-permute-start.4 = (bf16[1536,128]{1,0:T(8,128)(2,1)}, bf16[1536,128]{1,0:T(8,128)(2,1)S(1)}, u32[]{:S(2)}, u32[]{:S(2)}) collective-permute-start(bf16[1536,128]{1,0:T(8,128)(2,1)} %bitcast.13), channel_id=1, source_target_pairs={{1,0},{0,1},{3,2},{2,3},{5,4},{4,5},{7,6},{6,7},{9,8},{8,9},{11,10... | collective-permute-start | bytes 1179656 | tf_op jit(solution)/shard_map/ppermute | solution.py:37
  7.6 9.8 %collective-permute-start = (bf16[656,128]{1,0:T(8,128)(2,1)}, bf16[656,128]{1,0:T(8,128)(2,1)S(1)}, u32[]{:S(2)}, u32[]{:S(2)}) collective-permute-start(bf16[656,128]{1,0:T(8,128)(2,1)} %pick_column_blocks.1.refs_2_), channel_id=1, source_target_pairs={{12,0},{8,4},{4,8},{0,12},{13,1},{9,5},{5,9},{1,13},{14,2},{10,6},... | collective-permute-start | bytes 503816 | tf_op jit(solution)/shard_map/ppermute | solution.py:32
  11.3 8.9 %collective-permute-start.1 = (bf16[656,128]{1,0:T(8,128)(2,1)}, bf16[656,128]{1,0:T(8,128)(2,1)S(1)}, u32[]{:S(2)}, u32[]{:S(2)}) collective-permute-start(bf16[656,128]{1,0:T(8,128)(2,1)} %pick_column_blocks.1.refs_2_), channel_id=1, source_target_pairs={{4,0},{0,4},{12,8},{8,12},{5,1},{1,5},{13,9},{9,13},{6,2},{2,6},{1... | collective-permute-start | bytes 503816 | tf_op jit(solution)/shard_map/ppermute | solution.py:32
  14.4 0.9 %copy-start.1 = (bf16[656,128]{1,0:T(8,128)(2,1)S(1)}, bf16[656,128]{1,0:T(8,128)(2,1)}, u32[]{:S(2)}) copy-start(bf16[656,128]{1,0:T(8,128)(2,1)} %pick_column_blocks.1.refs_2_) | copy-start | bytes 503812
  15.4 6.0 %collective-permute-start.9 = (bf16[640,128]{1,0:T(8,128)(2,1)S(1)}, bf16[640,128]{1,0:T(8,128)(2,1)S(1)}, u32[]{:S(2)}, u32[]{:S(2)}) collective-permute-start(bf16[640,128]{1,0:T(8,128)(2,1)S(1)} %get-tuple-element.29), channel_id=1, source_target_pairs={{16,0},{0,16},{17,1},{1,17},{18,2},{2,18},{19,3},{3,19},{20,4},{4,... | collective-permute-start | bytes 491528 | tf_op jit(solution)/shard_map/ppermute | solution.py:26
  16.9 5.3 %collective-permute-start.10 = (bf16[640,128]{1,0:T(8,128)(2,1)S(1)}, bf16[640,128]{1,0:T(8,128)(2,1)S(1)}, u32[]{:S(2)}, u32[]{:S(2)}) collective-permute-start(bf16[640,128]{1,0:T(8,128)(2,1)S(1)} %get-tuple-element.30), channel_id=1, source_target_pairs={{2,0},{3,1},{0,2},{1,3},{6,4},{7,5},{4,6},{5,7},{10,8},{11,9},{8,1... | collective-permute-start | bytes 491528 | tf_op jit(solution)/shard_map/ppermute | solution.py:37
  20.3 10.7 %collective-permute-start.5 = (bf16[1456,128]{1,0:T(8,128)(2,1)S(1)}, bf16[1456,128]{1,0:T(8,128)(2,1)S(1)}, u32[]{:S(2)}, u32[]{:S(2)}) collective-permute-start(bf16[1456,128]{1,0:T(8,128)(2,1)S(1)} %get-tuple-element.27), channel_id=1, source_target_pairs={{2,0},{3,1},{0,2},{1,3},{6,4},{7,5},{4,6},{5,7},{10,8},{11,9},{8,1... | collective-permute-start | bytes 1118216 | tf_op jit(solution)/shard_map/ppermute | solution.py:37
  20.9 1.6 %copy-start.2 = (s32[32,12]{0,1:T(8,128)S(1)}, s32[32,12]{0,1:T(8,128)}, u32[]{:S(2)}) copy-start(s32[32,12]{0,1:T(8,128)} %param.9) | copy-start | bytes 4612
  20.9 1.6 %copy-start.4 = (s32[32]{0:T(128)S(1)}, s32[32]{0:T(128)}, u32[]{:S(2)}) copy-start(s32[32]{0:T(128)} %refs_1_.3) | copy-start | bytes 388
  20.9 10.3 %collective-permute-start.6 = (bf16[1456,128]{1,0:T(8,128)(2,1)S(1)}, bf16[1456,128]{1,0:T(8,128)(2,1)S(1)}, u32[]{:S(2)}, u32[]{:S(2)}) collective-permute-start(bf16[1456,128]{1,0:T(8,128)(2,1)S(1)} %get-tuple-element.24.refs_2_), channel_id=1, source_target_pairs={{16,0},{0,16},{17,1},{1,17},{18,2},{2,18},{19,3},{3,19},{20,4},{4,... | collective-permute-start | bytes 1118216 | tf_op jit(solution)/shard_map/ppermute | solution.py:26
  21.4 9.8 %collective-permute-start.7 = (bf16[1536,128]{1,0:T(8,128)(2,1)S(1)}, bf16[1536,128]{1,0:T(8,128)(2,1)S(1)}, u32[]{:S(2)}, u32[]{:S(2)}) collective-permute-start(bf16[1536,128]{1,0:T(8,128)(2,1)S(1)} %collective-permute-done.2.refs_0_.refs_3_), channel_id=1, source_target_pairs={{1,0},{0,1},{3,2},{2,3},{5,4},{4,5},{7,6},{6,7},{9,8},{8,9},{11,10... | collective-permute-start | bytes 1179656 | tf_op jit(solution)/shard_map/ppermute | solution.py:37
  21.4 9.8 %collective-permute-start.8 = (bf16[1536,128]{1,0:T(8,128)(2,1)S(1)}, bf16[1536,128]{1,0:T(8,128)(2,1)S(1)}, u32[]{:S(2)}, u32[]{:S(2)}) collective-permute-start(bf16[1536,128]{1,0:T(8,128)(2,1)S(1)} %collective-permute-done.3.refs_1_.refs_4_.refs_7_), channel_id=1, source_target_pairs={{1,0},{0,1},{3,2},{2,3},{5,4},{4,5},{7,6},{6,7},{9,8},{8,9},{11,10... | collective-permute-start | bytes 1179656 | tf_op jit(solution)/shard_map/ppermute | solution.py:37
  22.3 11.2 %copy-start.3 = (bf16[32,6,128]{2,0,1:T(8,128)(2,1)S(1)}, bf16[32,6,128]{2,0,1:T(8,128)(2,1)}, u32[]{:S(2)}) copy-start(bf16[32,6,128]{2,0,1:T(8,128)(2,1)} %param.11) | copy-start | bytes 147460
  22.3 12.2 %copy-start = (bf16[1,12,128,128]{3,2,1,0:T(8,128)(2,1)S(1)}, bf16[1,12,128,128]{3,2,1,0:T(8,128)(2,1)}, u32[]{:S(2)}) copy-start(bf16[1,12,128,128]{3,2,1,0:T(8,128)(2,1)} %param.8) | copy-start | bytes 1179652
  22.3 12.2 %collective-permute-start.11 = (bf16[2560,128]{1,0:T(8,128)(2,1)S(1)}, bf16[2560,128]{1,0:T(8,128)(2,1)S(1)}, u32[]{:S(2)}, u32[]{:S(2)}) collective-permute-start(bf16[2560,128]{1,0:T(8,128)(2,1)S(1)} %pack_two_mate.1.refs_5_), channel_id=1, source_target_pairs={{1,0},{0,1},{3,2},{2,3},{5,4},{4,5},{7,6},{6,7},{9,8},{8,9},{11,10... | collective-permute-start | bytes 1966088 | tf_op jit(solution)/shard_map/ppermute | solution.py:37
  31.3 8.9 %collective-permute-start.14 = (bf16[2960,128]{1,0:T(8,128)(2,1)S(1)}, bf16[2960,128]{1,0:T(8,128)(2,1)S(1)}, u32[]{:S(2)}, u32[]{:S(2)}) collective-permute-start(bf16[2960,128]{1,0:T(8,128)(2,1)S(1)} %get-tuple-element.36), channel_id=1, source_target_pairs={{1,0},{0,1},{3,2},{2,3},{5,4},{4,5},{7,6},{6,7},{9,8},{8,9},{11,10... | collective-permute-start | bytes 2273288 | tf_op jit(solution)/shard_map/ppermute | solution.py:37
  31.4 6.6 %collective-permute-start.12 = (bf16[640,128]{1,0:T(8,128)(2,1)S(1)}, bf16[640,128]{1,0:T(8,128)(2,1)S(1)}, u32[]{:S(2)}, u32[]{:S(2)}) collective-permute-start(bf16[640,128]{1,0:T(8,128)(2,1)S(1)} %get-tuple-element.31.refs_2_.refs_15_), channel_id=1, source_target_pairs={{16,0},{0,16},{17,1},{1,17},{18,2},{2,18},{19,3},{3,19},{20,4},{4,... | collective-permute-start | bytes 491528 | tf_op jit(solution)/shard_map/ppermute | solution.py:26
  32.0 6.5 %collective-permute-start.13 = (bf16[640,128]{1,0:T(8,128)(2,1)S(1)}, bf16[640,128]{1,0:T(8,128)(2,1)S(1)}, u32[]{:S(2)}, u32[]{:S(2)}) collective-permute-start(bf16[640,128]{1,0:T(8,128)(2,1)S(1)} %get-tuple-element.35), channel_id=1, source_target_pairs={{2,0},{3,1},{0,2},{1,3},{6,4},{7,5},{4,6},{5,7},{10,8},{11,9},{8,1... | collective-permute-start | bytes 491528 | tf_op jit(solution)/shard_map/ppermute | solution.py:37
  33.5 4.5 %collective-permute-start.15 = (bf16[96,128]{1,0:T(8,128)(2,1)S(1)}, bf16[96,128]{1,0:T(8,128)(2,1)S(1)}, u32[]{:S(2)}, u32[]{:S(2)}) collective-permute-start(bf16[96,128]{1,0:T(8,128)(2,1)S(1)} %get-tuple-element.37.refs_0_), channel_id=1, source_target_pairs={{3,0},{2,1},{1,2},{0,3},{7,4},{6,5},{5,6},{4,7},{11,8},{10,9},{9,1... | collective-permute-start | bytes 73736 | tf_op jit(solution)/shard_map/ppermute | solution.py:37
  38.5 1.7 %collective-permute-start.16 = (bf16[1280,128]{1,0:T(8,128)(2,1)S(1)}, bf16[1280,128]{1,0:T(8,128)(2,1)S(1)}, u32[]{:S(2)}, u32[]{:S(2)}) collective-permute-start(bf16[1280,128]{1,0:T(8,128)(2,1)S(1)} %pack_four.1), channel_id=1, source_target_pairs={{1,0},{0,1},{3,2},{2,3},{5,4},{4,5},{7,6},{6,7},{9,8},{8,9},{11,10... | collective-permute-start | bytes 983048 | tf_op jit(solution)/shard_map/ppermute | solution.py:37
  44.7 1.6 %collective-permute-start.17 = (f32[8,128]{1,0:T(8,128)S(1)}, f32[8,128]{1,0:T(8,128)S(1)}, u32[]{:S(2)}, u32[]{:S(2)}) collective-permute-start(f32[8,128]{1,0:T(8,128)S(1)} %get-tuple-element.40), channel_id=1, source_target_pairs={{1,0},{0,1},{3,2},{2,3},{5,4},{4,5},{7,6},{6,7},{9,8},{8,9},{11,10... | collective-permute-start | bytes 12296 | tf_op jit(solution)/shard_map/ppermute | solution.py:37
  44.8 3.0 %collective-permute-start.18 = (f32[8,128]{1,0:T(8,128)S(1)}, f32[8,128]{1,0:T(8,128)S(1)}, u32[]{:S(2)}, u32[]{:S(2)}) collective-permute-start(f32[8,128]{1,0:T(8,128)S(1)} %get-tuple-element.40), channel_id=1, source_target_pairs={{3,0},{2,1},{1,2},{0,3},{7,4},{6,5},{5,6},{4,7},{11,8},{10,9},{9,1... | collective-permute-start | bytes 12296 | tf_op jit(solution)/shard_map/ppermute | solution.py:37
  48.0 3.6 %collective-permute-start.19 = (f32[8,128]{1,0:T(8,128)S(1)}, f32[8,128]{1,0:T(8,128)S(1)}, u32[]{:S(2)}, u32[]{:S(2)}) collective-permute-start(f32[8,128]{1,0:T(8,128)S(1)} %maximum_maximum_fusion.refs_0_), channel_id=1, source_target_pairs={{16,0},{0,16},{17,1},{1,17},{18,2},{2,18},{19,3},{3,19},{20,4},{4,... | collective-permute-start | bytes 12296 | tf_op jit(solution)/shard_map/ppermute | solution.py:26
  51.7 5.6 %collective-permute-start.20 = (f32[16,128]{1,0:T(8,128)S(1)}, f32[16,128]{1,0:T(8,128)S(1)}, u32[]{:S(2)}, u32[]{:S(2)}) collective-permute-start(f32[16,128]{1,0:T(8,128)S(1)} %stack_tiles.1.refs_0_), channel_id=1, source_target_pairs={{12,0},{8,4},{4,8},{0,12},{13,1},{9,5},{5,9},{1,13},{14,2},{10,6},... | collective-permute-start | bytes 24584 | tf_op jit(solution)/shard_map/ppermute | solution.py:32
  54.4 3.7 %collective-permute-start.21 = (f32[16,128]{1,0:T(8,128)S(1)}, f32[16,128]{1,0:T(8,128)S(1)}, u32[]{:S(2)}, u32[]{:S(2)}) collective-permute-start(f32[16,128]{1,0:T(8,128)S(1)} %stack_tiles.1.refs_0_), channel_id=1, source_target_pairs={{4,0},{0,4},{12,8},{8,12},{5,1},{1,5},{13,9},{9,13},{6,2},{2,6},{1... | collective-permute-start | bytes 24584 | tf_op jit(solution)/shard_map/ppermute | solution.py:32

commit v20 on v19

--- a/solution.py
+++ b/solution.py
@@ -151,8 +151,8 @@
     own_basis_ref[...] = rows_of(hot(16, at.me, 0))
 
 
-def prepare_kernel(axes, count, layout, late_from, *refs):
-    early_ref, late_ref, info_ref, neighbors_ref, size_ref, known, inverse, layout_ref, loads = refs[-9:]
+def prepare_kernel(axes, count, layout, late_from, last_from, *refs):
+    early_ref, late_ref, last_ref, info_ref, neighbors_ref, size_ref, known, inverse, layout_ref, loads = refs[-10:]
     at = Places(*axes)
     load(refs[:2], (neighbors_ref, size_ref), loads)
     slots = neighbors_ref.shape[0]
@@ -174,7 +174,7 @@
     info_ref[slots + 1] = self_slot
 
     def row_of_pairs(v, totals):
-        early, late = totals
+        early, late, last = totals
         atom = known[0, v]
         side = known[1, v]
         line = known[2, v]
@@ -182,7 +182,7 @@
             inverse[neighbors_ref[u, atom]] = v * 16 + u
 
         def from_row(totals):
-            total, late = totals
+            total, late, last = totals
             for w in range(slots):
                 mark = inverse[known[0, w]]
                 chosen = ((mark >> 4) == v) & ((known[1, w] != 0) | (v <= w))
@@ -193,10 +193,10 @@
                 late_ref[late + 1] = entry + 256 * (where - late_from)
                 total = total + (chosen & ~is_late).astype(jnp.int32)
                 late = late + (chosen & is_late).astype(jnp.int32)
-            return total, late
+            return total, late, last
 
         def from_column(totals):
-            early, late = totals
+            early, late, last = totals
             row, _, lay = at.split(atom)
             beside = layout_ref[lines * slots + (side - 1) * lines + line]
             for w in range(slots):
@@ -210,17 +210,20 @@
                 chosen = ((mark >> 4) == v) & (side == known[1, w]) & (there >= 0) & ((back < 0) | (v <= w))
                 where = beside + there * LANES
                 is_late = where >= late_from
+                is_last = where >= last_from
                 entry = v + 16 * w
                 early_ref[early + 1] = entry + 256 * where
                 late_ref[late + 1] = entry + 256 * (where - late_from)
+                last_ref[last + 1] = entry + 256 * (where - last_from)
                 early = early + (chosen & ~is_late).astype(jnp.int32)
-                late = late + (chosen & is_late).astype(jnp.int32)
-            return early, late
-
-        return lax.cond(side == 0, from_row, from_column, (early, late))
-
-    totals = lax.fori_loop(0, slots, row_of_pairs, (jnp.int32(0), jnp.int32(0)))
-    for ref, total in zip((early_ref, late_ref), totals):
+                late = late + (chosen & is_late & ~is_last).astype(jnp.int32)
+                last = last + (chosen & is_last).astype(jnp.int32)
+            return early, late, last
+
+        return lax.cond(side == 0, from_row, from_column, (early, late, last))
+
+    totals = lax.fori_loop(0, slots, row_of_pairs, (jnp.int32(0),) * 3)
+    for ref, total in zip((early_ref, late_ref, last_ref), totals):
         ref[0] = (total + UNROLL - 1) // UNROLL
         for i in range(UNROLL - 1):
             ref[total + i + 1] = ref[jnp.maximum(total, 1)]
@@ -286,22 +289,33 @@
     place_pairs(table_ref, pool, gram, size)
 
 
-def step_kernel(pieces, *refs):
-    table_ref, info_ref, basis_ref, spread_ref, sign_ref, early_ref = refs[:6]
-    piece_refs = refs[6 : 6 + pieces]
-    next_ref, coef_ref, pool, gram, own, square = refs[-6:]
+def middle_kernel(pieces, *refs):
+    table_ref, info_ref, sign_ref, early_ref = refs[:4]
+    piece_refs = refs[4 : 4 + pieces]
+    gram, own, pool = refs[-3:]
     slots, size = sign_ref.shape[0], sign_ref.shape[1]
     fill(piece_refs, pool)
     for v in range(slots):
         gram[v * size : (v + 1) * size] = early_ref[v * size : (v + 1) * size]
+    place_pairs(table_ref, pool, gram, size)
     rows = lax.broadcasted_iota(jnp.int32, (size, size), 0)
     lanes = lax.broadcasted_iota(jnp.int32, (size, size), 1)
+    for w in range(slots):
+        kept = (rows < info_ref[slots]) & (lanes < info_ref[w])
+        block = jnp.where(kept, sign_ref[w].astype(jnp.float32), 0.0)
+        own[:, w * size : (w + 1) * size] = block.astype(own.dtype)
+
+
+def step_kernel(pieces, *refs):
+    table_ref, info_ref, basis_ref, spread_ref, own, early_ref = refs[:6]
+    piece_refs = refs[6 : 6 + pieces]
+    next_ref, coef_ref, pool, gram, square = refs[-5:]
+    slots, size = next_ref.shape[0], next_ref.shape[1]
+    fill(piece_refs, pool)
+    for v in range(slots):
+        gram[v * size : (v + 1) * size] = early_ref[v * size : (v + 1) * size]
     own_size = info_ref[slots]
     self_slot = info_ref[slots + 1]
-    for w in range(slots):
-        kept = (rows < own_size) & (lanes < info_ref[w])
-        block = jnp.where(kept, sign_ref[w].astype(jnp.float32), 0.0)
-        own[:, w * size : (w + 1) * size] = block.astype(own.dtype)
     place_pairs(table_ref, pool, gram, size)
     wide = 2 * size
     wide_lanes = lax.broadcasted_iota(jnp.int32, (size, wide), 1)
@@ -582,15 +596,16 @@
     ]
     pairs = slots * (slots + 1) // 2
     entries = pairs + UNROLL + 1
-    early_table, late_table, info = pl.pallas_call(
-        functools.partial(prepare_kernel, axes, count, tuple(layout), late_from),
+    early_table, late_table, last_table, info = pl.pallas_call(
+        functools.partial(prepare_kernel, axes, count, tuple(layout), late_from, base["four"]),
         out_shape=(
+            jax.ShapeDtypeStruct((entries,), jnp.int32),
             jax.ShapeDtypeStruct((entries,), jnp.int32),
             jax.ShapeDtypeStruct((entries,), jnp.int32),
             jax.ShapeDtypeStruct((slots + 2,), jnp.int32),
         ),
         in_specs=[HBM, HBM, ANY],
-        out_specs=(SMEM, SMEM, SMEM),
+        out_specs=(SMEM, SMEM, SMEM, SMEM),
         scratch_shapes=[
             pltpu.SMEM((slots, atoms), jnp.int32),
             pltpu.SMEM((atoms,), jnp.int32),
@@ -681,7 +696,24 @@
         name="profiles",
     )(geos, buffers["three m"], third_geos)
 
-    late_values = [buffers[name] for name in late_order]
+    late_values = [buffers[name] for name in late_order[:-1]]
+    middle, own_kept = pl.pallas_call(
+        functools.partial(middle_kernel, len(late_values)),
+        out_shape=(
+            jax.ShapeDtypeStruct((full, full), jnp.bfloat16),
+            jax.ShapeDtypeStruct((size, full), jnp.bfloat16),
+        ),
+        in_specs=[SMEM, SMEM] + [VMEM] * (2 + len(late_values)) + [ANY],
+        out_specs=(VMEM, VMEM),
+        scratch_shapes=[pltpu.VMEM((base["four"] - late_from, LANES), jnp.bfloat16)],
+        compiler_params=pltpu.CompilerParams(
+            vmem_limit_bytes=(13 << 20) + 2 * (base["four"] - late_from) * LANES * 2
+        ),
+        cost_estimate=pl.CostEstimate(flops=1000, bytes_accessed=1000, transcendentals=0),
+        name="gram_middle",
+    )(late_table, info, own, gram, *late_values, four)
+
+    late_values = [buffers["four"]]
     sign_next, coef = pl.pallas_call(
         functools.partial(step_kernel, len(late_values)),
         out_shape=(
@@ -691,15 +723,14 @@
         in_specs=[SMEM, SMEM, VMEM, VMEM, VMEM, VMEM] + [VMEM] * len(late_values),
         out_specs=(VMEM, VMEM),
         scratch_shapes=[
-            pltpu.VMEM((total - late_from, LANES), jnp.bfloat16),
+            pltpu.VMEM((total - base["four"], LANES), jnp.bfloat16),
             pltpu.VMEM((full, full), jnp.bfloat16),
-            pltpu.VMEM((size, full), jnp.bfloat16),
             pltpu.VMEM((size, full), jnp.bfloat16),
         ],
         compiler_params=pltpu.CompilerParams(vmem_limit_bytes=(15 << 20) + 2 * (total - late_from) * LANES * 2),
         cost_estimate=pl.CostEstimate(flops=1_300_000_000, bytes_accessed=8_000_000, transcendentals=0),
         name="square_cube_coefficients",
-    )(late_table, info, own_basis, spread, own, gram, *late_values)
+    )(last_table, info, own_basis, spread, own_kept, middle, *late_values)
 
     mate_coef = from_layer(coef, 1)
     third_coef = from_layer(coef, 3)

time: 59.8 us -> 59.4 us (level)
  waiting for transfers between devices: 18 us -> 16.6 us
  Pallas kernels: 19.2 us -> 20.3 us
    ppermute x13, waiting for transfers between devices: 11.5 us -> 9.97 us  [from_layer(): return lax.ppermute(x, 'layer', [(i ^ flip, i) for i in range(count)])]
    pallas_call x0 -> x1, Pallas kernels: none -> 1.24 us  [local(): pl.pallas_call(functools.partial(middle_kernel, len(late_values)), out_sh...]
  transfers between devices with their start and end apart: 22 -> 22, of which waited for: 12 -> 12; matrix products, arithmetic and copies ran while one was open for 0% -> 0% of each run, Pallas kernels for 22% -> 25%
where the time goes in v20:
time: 59.4 us; the launch traced here: 59.1 us
  Pallas kernels  20.3 us (34%)
  starting transfers between devices  20.2 us (34%)
  waiting for transfers between devices  16.6 us (28%)
  local copies, waits for them, and re-layouts  1.16 us (2%)
  between operations  0.78 us (1%)
    ppermute x13, waiting for transfers between devices, from_layer(): return lax.ppermute(x, 'layer', [(i ^ flip, i) for i in range(count)])  9.97 us
    ppermute x13, starting transfers between devices, from_layer(): return lax.ppermute(x, 'layer', [(i ^ flip, i) for i in range(count)])  8.15 us
    ppermute x4, starting transfers between devices, from_column(): lax.ppermute(x, 'col', [((i + step[i]) % count, i) for i in range(count)])  6.27 us
    ppermute x5, starting transfers between devices, from_offset(): lax.ppermute(x, axis, [((i + step) % count, i) for i in range(count)])  5.77 us
    pallas_call x1, Pallas kernels, local(): pl.pallas_call(functools.partial(prepare_kernel, axes, count, tuple(layou...  4.24 us
    pallas_call x1, Pallas kernels, local(): pl.pallas_call(functools.partial(step_kernel, len(late_values)), out_shap...  4.06 us
    ppermute x4, waiting for transfers between devices, from_column(): lax.ppermute(x, 'col', [((i + step[i]) % count, i) for i in range(count)])  3.52 us
    ppermute x5, waiting for transfers between devices, from_offset(): lax.ppermute(x, axis, [((i + step) % count, i) for i in range(count)])  3.12 us
  transfers between devices with their start and end apart: 22, of which 12 were waited for; matrix products, arithmetic and copies ran while one was open for 0% of the time, Pallas kernels for 25%

profile of v20, /device:TPU:0, one launch (start us, length us, event | category | flops | bytes accessed | tf_op | source)
XLA Modules:
  0.0 59.1 jit_solution(14560754136851400068)
XLA Ops:
  0.6 3.0 %collective-permute-start.2 = (bf16[1536,128]{1,0:T(8,128)(2,1)}, bf16[1536,128]{1,0:T(8,128)(2,1)S(1)}, u32[]{:S(2)}, u32[]{:S(2)}) collective-permute-start(bf16[1536,128]{1,0:T(8,128)(2,1)} %bitcast.11), channel_id=1, source_target_pairs={{2,0},{3,1},{0,2},{1,3},{6,4},{7,5},{4,6},{5,7},{10,8},{11,9},{8,1... | collective-permute-start | bytes 1179656 | tf_op jit(solution)/shard_map/ppermute | solution.py:37
  3.7 1.5 %collective-permute-start.3 = (bf16[1536,128]{1,0:T(8,128)(2,1)}, bf16[1536,128]{1,0:T(8,128)(2,1)S(1)}, u32[]{:S(2)}, u32[]{:S(2)}) collective-permute-start(bf16[1536,128]{1,0:T(8,128)(2,1)} %bitcast.12), channel_id=1, source_target_pairs={{16,0},{0,16},{17,1},{1,17},{18,2},{2,18},{19,3},{3,19},{20,4},{4,... | collective-permute-start | bytes 1179656 | tf_op jit(solution)/shard_map/ppermute | solution.py:26
  5.2 0.0 collective-permute-start.4
  5.2 2.5 %pick_column_blocks.1.refs_2_ = bf16[656,128]{1,0:T(8,128)(2,1)} custom-call(s32[12,32]{1,0:T(8,128)} %bitcast.19, s32[1,12]{1,0:T(1,128)} %refs_1_.2, s32[32]{0:T(128)} %refs_2_.1, s32[32]{0:T(128)} %refs_3_.1, s32[32]{0:T(128)} %refs_4_.1, bf16[12,128,128]{2,1,0:T(8,128)(2,1)} %bitcast.14), custom_call_target="tpu_custom_call" | custom-call | tf_op jit(solution)/shard_map/pick_column_blocks/pallas_call | solution.py:468
  7.6 3.7 %collective-permute-start = (bf16[656,128]{1,0:T(8,128)(2,1)}, bf16[656,128]{1,0:T(8,128)(2,1)S(1)}, u32[]{:S(2)}, u32[]{:S(2)}) collective-permute-start(bf16[656,128]{1,0:T(8,128)(2,1)} %pick_column_blocks.1.refs_2_), channel_id=1, source_target_pairs={{12,0},{8,4},{4,8},{0,12},{13,1},{9,5},{5,9},{1,13},{14,2},{10,6},... | collective-permute-start | bytes 503816 | tf_op jit(solution)/shard_map/ppermute | solution.py:32
  11.3 0.0 collective-permute-start.1
  11.3 1.7 %collective-permute-done.2.refs_0_.refs_3_ = bf16[1536,128]{1,0:T(8,128)(2,1)S(1)} collective-permute-done((bf16[1536,128]{1,0:T(8,128)(2,1)}, bf16[1536,128]{1,0:T(8,128)(2,1)S(1)}, u32[]{:S(2)}, u32[]{:S(2)}) %collective-permute-start.2) | collective-permute-done | bytes 393248 | tf_op jit(solution)/shard_map/ppermute | solution.py:37
  13.0 1.5 %collective-permute-done.3.refs_1_.refs_4_.refs_7_ = bf16[1536,128]{1,0:T(8,128)(2,1)S(1)} collective-permute-done((bf16[1536,128]{1,0:T(8,128)(2,1)}, bf16[1536,128]{1,0:T(8,128)(2,1)S(1)}, u32[]{:S(2)}, u32[]{:S(2)}) %collective-permute-start.3) | collective-permute-done | bytes 393248 | tf_op jit(solution)/shard_map/ppermute | solution.py:26
  14.5 0.9 %copy-done.1 = bf16[656,128]{1,0:T(8,128)(2,1)S(1)} copy-done((bf16[656,128]{1,0:T(8,128)(2,1)S(1)}, bf16[656,128]{1,0:T(8,128)(2,1)}, u32[]{:S(2)}) %copy-start.1) | copy-done | bytes 167960
  15.4 1.6 %collective-permute-start.9 = (bf16[640,128]{1,0:T(8,128)(2,1)S(1)}, bf16[640,128]{1,0:T(8,128)(2,1)S(1)}, u32[]{:S(2)}, u32[]{:S(2)}) collective-permute-start(bf16[640,128]{1,0:T(8,128)(2,1)S(1)} %get-tuple-element.32), channel_id=1, source_target_pairs={{16,0},{0,16},{17,1},{1,17},{18,2},{2,18},{19,3},{3,19},{20,4},{4,... | collective-permute-start | bytes 491528 | tf_op jit(solution)/shard_map/ppermute | solution.py:26
  16.9 0.5 collective-permute-start.10
  17.5 0.0 collective-permute-done.refs_0_.refs_3_.refs_5_
  17.5 2.7 %collective-permute-done.1.refs_1_.refs_2_.refs_4_ = bf16[656,128]{1,0:T(8,128)(2,1)S(1)} collective-permute-done((bf16[656,128]{1,0:T(8,128)(2,1)}, bf16[656,128]{1,0:T(8,128)(2,1)S(1)}, u32[]{:S(2)}, u32[]{:S(2)}) %collective-permute-start.1) | collective-permute-done | bytes 167968 | tf_op jit(solution)/shard_map/ppermute | solution.py:32
  20.2 0.0 collective-permute-done.4.refs_5_.refs_2_
  20.2 0.1 pack_two.1
  20.3 0.6 collective-permute-start.5
  20.9 0.6 %collective-permute-start.6 = (bf16[1456,128]{1,0:T(8,128)(2,1)S(1)}, bf16[1456,128]{1,0:T(8,128)(2,1)S(1)}, u32[]{:S(2)}, u32[]{:S(2)}) collective-permute-start(bf16[1456,128]{1,0:T(8,128)(2,1)S(1)} %get-tuple-element.27.refs_2_), channel_id=1, source_target_pairs={{16,0},{0,16},{17,1},{1,17},{18,2},{2,18},{19,3},{3,19},{20,4},{4,... | collective-permute-start | bytes 1118216 | tf_op jit(solution)/shard_map/ppermute | solution.py:26
  21.5 0.0 collective-permute-start.7
  21.5 0.0 collective-permute-done.9.refs_0_.refs_10_
  21.5 0.5 collective-permute-start.8
  22.0 0.3 collective-permute-done.10.refs_1_.refs_11_
  22.3 0.1 collective-permute-start.11
  22.4 0.0 copy-done.2
  22.4 0.0 copy-done.4
  22.4 4.2 %prepare.1 = (s32[83]{0:T(128)S(1)}, s32[83]{0:T(128)S(1)}, s32[83]{0:T(128)S(1)}, s32[14]{0:T(128)S(1)}) custom-call(s32[12,32]{1,0:T(8,128)S(1)} %bitcast.20, s32[32]{0:T(128)S(1)} %copy-done.4, bf16[1456,128]{1,0:T(8,128)(2,1)S(1)} %get-tuple-element.27.refs_2_), custom_call_target="tpu_custom_call" | custom-call | flops 1000 | bytes 1000 | tf_op jit(solution)/shard_map/prepare/pallas_call | solution.py:599
  26.7 4.3 %collective-permute-done.5.refs_0_.refs_13_ = bf16[1456,128]{1,0:T(8,128)(2,1)S(1)} collective-permute-done((bf16[1456,128]{1,0:T(8,128)(2,1)S(1)}, bf16[1456,128]{1,0:T(8,128)(2,1)S(1)}, u32[]{:S(2)}, u32[]{:S(2)}) %collective-permute-start.5) | collective-permute-done | bytes 372768 | tf_op jit(solution)/shard_map/ppermute | solution.py:37
  31.0 0.3 collective-permute-done.6.refs_2_.refs_12_
  31.3 0.0 collective-permute-done.7.refs_3_.refs_9_
  31.3 0.0 collective-permute-done.8.refs_4_.refs_8_
  31.3 0.1 pack_three.1
  31.4 0.1 collective-permute-start.14
  31.5 0.6 %collective-permute-start.12 = (bf16[640,128]{1,0:T(8,128)(2,1)S(1)}, bf16[640,128]{1,0:T(8,128)(2,1)S(1)}, u32[]{:S(2)}, u32[]{:S(2)}) collective-permute-start(bf16[640,128]{1,0:T(8,128)(2,1)S(1)} %get-tuple-element.34.refs_2_.refs_15_), channel_id=1, source_target_pairs={{16,0},{0,16},{17,1},{1,17},{18,2},{2,18},{19,3},{3,19},{20,4},{4,... | collective-permute-start | bytes 491528 | tf_op jit(solution)/shard_map/ppermute | solution.py:26
  32.1 1.6 %collective-permute-start.13 = (bf16[640,128]{1,0:T(8,128)(2,1)S(1)}, bf16[640,128]{1,0:T(8,128)(2,1)S(1)}, u32[]{:S(2)}, u32[]{:S(2)}) collective-permute-start(bf16[640,128]{1,0:T(8,128)(2,1)S(1)} %get-tuple-element.39), channel_id=1, source_target_pairs={{2,0},{3,1},{0,2},{1,3},{6,4},{7,5},{4,6},{5,7},{10,8},{11,9},{8,1... | collective-permute-start | bytes 491528 | tf_op jit(solution)/shard_map/ppermute | solution.py:37
  33.6 0.0 collective-permute-start.15
  33.6 0.0 copy-done.3
  33.6 1.0 %spread_basis.1 = (bf16[128,1536]{1,0:T(8,128)(2,1)S(1)}, bf16[16,128]{1,0:T(8,128)(2,1)S(1)}) custom-call(s32[12,32]{1,0:T(8,128)S(1)} %bitcast.21, bf16[192,128]{1,0:T(8,128)(2,1)S(1)} %bitcast.22, bf16[640,128]{1,0:T(8,128)(2,1)S(1)} %get-tuple-element.34.refs_2_.refs_15_), custom_call_target="tpu_custom_call" | custom-call | flops 1000 | bytes 1000 | tf_op jit(solution)/shard_map/spread_basis/pallas_call | solution.py:648
  34.7 0.0 collective-permute-done.11.refs_14_
  34.7 0.0 copy-done
  34.7 1.9 %gram_early.1.refs_2_.refs_3_ = bf16[1536,1536]{1,0:T(8,128)(2,1)S(1)} custom-call(s32[83]{0:T(128)S(1)} %get-tuple-element.38.refs_0_, bf16[1536,128]{1,0:T(8,128)(2,1)S(1)} %bitcast.15, bf16[1536,128]{1,0:T(8,128)(2,1)S(1)} %collective-permute-done.4.refs_5_.refs_2_, bf16[1536,128]{1,0:T(8,128)(2,1)S(1)} %collective-permute-done.2.refs_0_.refs_3_, ...), custom_call_target="tpu_custom_call" | custom-call | flops 1000 | bytes 1000 | tf_op jit(solution)/shard_map/gram_early/pallas_call | solution.py:663
  36.6 1.5 %collective-permute-done.15.refs_3_.refs_2_ = bf16[96,128]{1,0:T(8,128)(2,1)S(1)} collective-permute-done((bf16[96,128]{1,0:T(8,128)(2,1)S(1)}, bf16[96,128]{1,0:T(8,128)(2,1)S(1)}, u32[]{:S(2)}, u32[]{:S(2)}) %collective-permute-start.15) | collective-permute-done | bytes 24608 | tf_op jit(solution)/shard_map/ppermute | solution.py:37
  38.1 0.0 collective-permute-done.12.refs_0_.refs_4_
  38.1 0.5 collective-permute-done.13.refs_1_.refs_5_
  38.6 0.2 collective-permute-start.16
  38.8 0.0 collective-permute-done.14.refs_6_.refs_1_
  38.8 1.2 %gram_middle.1 = (bf16[1536,1536]{1,0:T(8,128)(2,1)S(1)}, bf16[128,1536]{1,0:T(8,128)(2,1)S(1)}) custom-call(s32[83]{0:T(128)S(1)} %get-tuple-element.37.refs_0_, s32[14]{0:T(128)S(1)} %get-tuple-element.29.refs_6_.refs_1_, bf16[12,128,128]{2,1,0:T(8,128)(2,1)S(1)} %bitcast.16, bf16[1536,1536]{1,0:T(8,128)(2,1)S(1)} %gram_early.1.refs_2_.refs_3_, ...), custom_call_target="tpu_custom_call" | custom-call | flops 1000 | bytes 1000 | tf_op jit(solution)/shard_map/gram_middle/pallas_call | solution.py:700
  40.1 0.3 collective-permute-done.16.refs_6_
  40.3 4.1 %square_cube_coefficients.1 = (bf16[12,128,128]{2,1,0:T(8,128)(2,1)S(1)}, f32[8,128]{1,0:T(8,128)S(1)}) custom-call(s32[83]{0:T(128)S(1)} %get-tuple-element.28.refs_0_, s32[14]{0:T(128)S(1)} %get-tuple-element.29.refs_6_.refs_1_, bf16[16,128]{1,0:T(8,128)(2,1)S(1)} %get-tuple-element.35.refs_4_.refs_2_, bf16[128,1536]{1,0:T(8,128)(2,1)S(1)} %get-tuple-element.36.refs_3_, ...), custom_call_target="tpu_custom_call" | custom-call | flops 1300000000 | bytes 8000000 | tf_op jit(solution)/shard_map/square_cube_coefficients/pallas_call | solution.py:717
  44.4 0.2 collective-permute-start.17
  44.5 1.5 %collective-permute-start.18 = (f32[8,128]{1,0:T(8,128)S(1)}, f32[8,128]{1,0:T(8,128)S(1)}, u32[]{:S(2)}, u32[]{:S(2)}) collective-permute-start(f32[8,128]{1,0:T(8,128)S(1)} %get-tuple-element.46), channel_id=1, source_target_pairs={{3,0},{2,1},{1,2},{0,3},{7,4},{6,5},{5,6},{4,7},{11,8},{10,9},{9,1... | collective-permute-start | bytes 12296 | tf_op jit(solution)/shard_map/ppermute | solution.py:37
  46.0 0.1 pad.3.clone
  46.1 0.0 collective-permute-done.17
  46.1 1.5 %collective-permute-done.18 = f32[8,128]{1,0:T(8,128)S(1)} collective-permute-done((f32[8,128]{1,0:T(8,128)S(1)}, f32[8,128]{1,0:T(8,128)S(1)}, u32[]{:S(2)}, u32[]{:S(2)}) %collective-permute-start.18) | collective-permute-done | bytes 4128 | tf_op jit(solution)/shard_map/ppermute | solution.py:37
  47.6 0.1 slice.11
  47.7 0.1 slice.10
  47.7 0.1 maximum_maximum_fusion.refs_0_
  47.8 1.5 %collective-permute-start.19 = (f32[8,128]{1,0:T(8,128)S(1)}, f32[8,128]{1,0:T(8,128)S(1)}, u32[]{:S(2)}, u32[]{:S(2)}) collective-permute-start(f32[8,128]{1,0:T(8,128)S(1)} %maximum_maximum_fusion.refs_0_), channel_id=1, source_target_pairs={{16,0},{0,16},{17,1},{1,17},{18,2},{2,18},{19,3},{3,19},{20,4},{4,... | collective-permute-start | bytes 12296 | tf_op jit(solution)/shard_map/ppermute | solution.py:26
  49.3 0.8 %give_sign.1 = (bf16[1536,128]{1,0:T(8,128)(2,1)}, bf16[16,128]{1,0:T(8,128)(2,1)S(1)}) custom-call(bf16[1536,128]{1,0:T(8,128)(2,1)S(1)} %bitcast.18), custom_call_target="tpu_custom_call" | custom-call | bytes 1000 | tf_op jit(solution)/shard_map/give_sign/pallas_call | solution.py:246
  50.1 1.4 %collective-permute-done.19.refs_1_ = f32[8,128]{1,0:T(8,128)S(1)} collective-permute-done((f32[8,128]{1,0:T(8,128)S(1)}, f32[8,128]{1,0:T(8,128)S(1)}, u32[]{:S(2)}, u32[]{:S(2)}) %collective-permute-start.19) | collective-permute-done | bytes 4128 | tf_op jit(solution)/shard_map/ppermute | solution.py:26
  51.5 2.6 %collective-permute-start.20 = (f32[16,128]{1,0:T(8,128)S(1)}, f32[16,128]{1,0:T(8,128)S(1)}, u32[]{:S(2)}, u32[]{:S(2)}) collective-permute-start(f32[16,128]{1,0:T(8,128)S(1)} %stack_tiles.1.refs_0_), channel_id=1, source_target_pairs={{12,0},{8,4},{4,8},{0,12},{13,1},{9,5},{5,9},{1,13},{14,2},{10,6},... | collective-permute-start | bytes 24584 | tf_op jit(solution)/shard_map/ppermute | solution.py:32
  54.0 0.0 collective-permute-start.21
  54.0 2.8 %profiles.1 = (bf16[6,6,256,128]{3,2,1,0:T(8,128)(2,1)S(1)}, bf16[6,6,128,128]{3,2,1,0:T(8,128)(2,1)S(1)}) custom-call(bf16[96,128]{1,0:T(8,128)(2,1)S(1)} %get-tuple-element.41.refs_0_, bf16[2960,128]{1,0:T(8,128)(2,1)S(1)} %collective-permute-done.14.refs_6_.refs_1_, bf16[96,128]{1,0:T(8,128)(2,1)S(1)} %collective-permute-done.15.refs_3_.refs_2_), custom_call_target="tpu_custom_call" | custom-call | flops 1000 | bytes 1000 | tf_op jit(solution)/shard_map/profiles/pallas_call | solution.py:682
  56.9 0.0 collective-permute-done.20.refs_1_
  56.9 0.8 %collective-permute-done.21.refs_2_ = f32[16,128]{1,0:T(8,128)S(1)} collective-permute-done((f32[16,128]{1,0:T(8,128)S(1)}, f32[16,128]{1,0:T(8,128)S(1)}, u32[]{:S(2)}, u32[]{:S(2)}) %collective-permute-start.21) | collective-permute-done | bytes 8224 | tf_op jit(solution)/shard_map/ppermute | solution.py:32
  57.7 1.4 %density.1 = f32[256,128]{1,0:T(8,128)} custom-call(f32[16,128]{1,0:T(8,128)S(1)} %stack_tiles.1.refs_0_, f32[16,128]{1,0:T(8,128)S(1)} %collective-permute-done.20.refs_1_, f32[16,128]{1,0:T(8,128)S(1)} %collective-permute-done.21.refs_2_, bf16[6,6,256,128]{3,2,1,0:T(8,128)(2,1)S(1)} %get-tuple-element.48.refs_3_, bf16[4608,128]{1,0:T(8,128)(2,1)S(1)} %bitcast.17), custom_call_target="tpu_custom_call" | custom-call | flops 310000000 | bytes 4000000 | tf_op jit(solution)/shard_map/density/pallas_call | solution.py:755
  (11 shorter events, 0.1 us)
Async XLA Ops:
  0.6 12.4 %collective-permute-start.2 = (bf16[1536,128]{1,0:T(8,128)(2,1)}, bf16[1536,128]{1,0:T(8,128)(2,1)S(1)}, u32[]{:S(2)}, u32[]{:S(2)}) collective-permute-start(bf16[1536,128]{1,0:T(8,128)(2,1)} %bitcast.11), channel_id=1, source_target_pairs={{2,0},{3,1},{0,2},{1,3},{6,4},{7,5},{4,6},{5,7},{10,8},{11,9},{8,1... | collective-permute-start | bytes 1179656 | tf_op jit(solution)/shard_map/ppermute | solution.py:37
  3.7 10.8 %collective-permute-start.3 = (bf16[1536,128]{1,0:T(8,128)(2,1)}, bf16[1536,128]{1,0:T(8,128)(2,1)S(1)}, u32[]{:S(2)}, u32[]{:S(2)}) collective-permute-start(bf16[1536,128]{1,0:T(8,128)(2,1)} %bitcast.12), channel_id=1, source_target_pairs={{16,0},{0,16},{17,1},{1,17},{18,2},{2,18},{19,3},{3,19},{20,4},{4,... | collective-permute-start | bytes 1179656 | tf_op jit(solution)/shard_map/ppermute | solution.py:26
  5.2 15.0 %collective-permute-start.4 = (bf16[1536,128]{1,0:T(8,128)(2,1)}, bf16[1536,128]{1,0:T(8,128)(2,1)S(1)}, u32[]{:S(2)}, u32[]{:S(2)}) collective-permute-start(bf16[1536,128]{1,0:T(8,128)(2,1)} %bitcast.13), channel_id=1, source_target_pairs={{1,0},{0,1},{3,2},{2,3},{5,4},{4,5},{7,6},{6,7},{9,8},{8,9},{11,10... | collective-permute-start | bytes 1179656 | tf_op jit(solution)/shard_map/ppermute | solution.py:37
  7.6 9.8 %collective-permute-start = (bf16[656,128]{1,0:T(8,128)(2,1)}, bf16[656,128]{1,0:T(8,128)(2,1)S(1)}, u32[]{:S(2)}, u32[]{:S(2)}) collective-permute-start(bf16[656,128]{1,0:T(8,128)(2,1)} %pick_column_blocks.1.refs_2_), channel_id=1, source_target_pairs={{12,0},{8,4},{4,8},{0,12},{13,1},{9,5},{5,9},{1,13},{14,2},{10,6},... | collective-permute-start | bytes 503816 | tf_op jit(solution)/shard_map/ppermute | solution.py:32
  11.3 8.9 %collective-permute-start.1 = (bf16[656,128]{1,0:T(8,128)(2,1)}, bf16[656,128]{1,0:T(8,128)(2,1)S(1)}, u32[]{:S(2)}, u32[]{:S(2)}) collective-permute-start(bf16[656,128]{1,0:T(8,128)(2,1)} %pick_column_blocks.1.refs_2_), channel_id=1, source_target_pairs={{4,0},{0,4},{12,8},{8,12},{5,1},{1,5},{13,9},{9,13},{6,2},{2,6},{1... | collective-permute-start | bytes 503816 | tf_op jit(solution)/shard_map/ppermute | solution.py:32
  14.4 0.9 %copy-start.1 = (bf16[656,128]{1,0:T(8,128)(2,1)S(1)}, bf16[656,128]{1,0:T(8,128)(2,1)}, u32[]{:S(2)}) copy-start(bf16[656,128]{1,0:T(8,128)(2,1)} %pick_column_blocks.1.refs_2_) | copy-start | bytes 503812
  15.4 6.1 %collective-permute-start.9 = (bf16[640,128]{1,0:T(8,128)(2,1)S(1)}, bf16[640,128]{1,0:T(8,128)(2,1)S(1)}, u32[]{:S(2)}, u32[]{:S(2)}) collective-permute-start(bf16[640,128]{1,0:T(8,128)(2,1)S(1)} %get-tuple-element.32), channel_id=1, source_target_pairs={{16,0},{0,16},{17,1},{1,17},{18,2},{2,18},{19,3},{3,19},{20,4},{4,... | collective-permute-start | bytes 491528 | tf_op jit(solution)/shard_map/ppermute | solution.py:26
  16.9 5.3 %collective-permute-start.10 = (bf16[640,128]{1,0:T(8,128)(2,1)S(1)}, bf16[640,128]{1,0:T(8,128)(2,1)S(1)}, u32[]{:S(2)}, u32[]{:S(2)}) collective-permute-start(bf16[640,128]{1,0:T(8,128)(2,1)S(1)} %get-tuple-element.33), channel_id=1, source_target_pairs={{2,0},{3,1},{0,2},{1,3},{6,4},{7,5},{4,6},{5,7},{10,8},{11,9},{8,1... | collective-permute-start | bytes 491528 | tf_op jit(solution)/shard_map/ppermute | solution.py:37
  20.3 10.7 %collective-permute-start.5 = (bf16[1456,128]{1,0:T(8,128)(2,1)S(1)}, bf16[1456,128]{1,0:T(8,128)(2,1)S(1)}, u32[]{:S(2)}, u32[]{:S(2)}) collective-permute-start(bf16[1456,128]{1,0:T(8,128)(2,1)S(1)} %get-tuple-element.30), channel_id=1, source_target_pairs={{2,0},{3,1},{0,2},{1,3},{6,4},{7,5},{4,6},{5,7},{10,8},{11,9},{8,1... | collective-permute-start | bytes 1118216 | tf_op jit(solution)/shard_map/ppermute | solution.py:37
  20.8 1.5 %copy-start.2 = (s32[32,12]{0,1:T(8,128)S(1)}, s32[32,12]{0,1:T(8,128)}, u32[]{:S(2)}) copy-start(s32[32,12]{0,1:T(8,128)} %param.9) | copy-start | bytes 4612
  20.9 1.6 %copy-start.4 = (s32[32]{0:T(128)S(1)}, s32[32]{0:T(128)}, u32[]{:S(2)}) copy-start(s32[32]{0:T(128)} %refs_1_.3) | copy-start | bytes 388
  20.9 12.8 %copy-start.3 = (bf16[32,6,128]{2,0,1:T(8,128)(2,1)S(1)}, bf16[32,6,128]{2,0,1:T(8,128)(2,1)}, u32[]{:S(2)}) copy-start(bf16[32,6,128]{2,0,1:T(8,128)(2,1)} %param.11) | copy-start | bytes 147460
  20.9 13.8 %copy-start = (bf16[1,12,128,128]{3,2,1,0:T(8,128)(2,1)S(1)}, bf16[1,12,128,128]{3,2,1,0:T(8,128)(2,1)}, u32[]{:S(2)}) copy-start(bf16[1,12,128,128]{3,2,1,0:T(8,128)(2,1)} %param.8) | copy-start | bytes 1179652
  20.9 10.4 %collective-permute-start.6 = (bf16[1456,128]{1,0:T(8,128)(2,1)S(1)}, bf16[1456,128]{1,0:T(8,128)(2,1)S(1)}, u32[]{:S(2)}, u32[]{:S(2)}) collective-permute-start(bf16[1456,128]{1,0:T(8,128)(2,1)S(1)} %get-tuple-element.27.refs_2_), channel_id=1, source_target_pairs={{16,0},{0,16},{17,1},{1,17},{18,2},{2,18},{19,3},{3,19},{20,4},{4,... | collective-permute-start | bytes 1118216 | tf_op jit(solution)/shard_map/ppermute | solution.py:26
  21.5 9.8 %collective-permute-start.7 = (bf16[1536,128]{1,0:T(8,128)(2,1)S(1)}, bf16[1536,128]{1,0:T(8,128)(2,1)S(1)}, u32[]{:S(2)}, u32[]{:S(2)}) collective-permute-start(bf16[1536,128]{1,0:T(8,128)(2,1)S(1)} %collective-permute-done.2.refs_0_.refs_3_), channel_id=1, source_target_pairs={{1,0},{0,1},{3,2},{2,3},{5,4},{4,5},{7,6},{6,7},{9,8},{8,9},{11,10... | collective-permute-start | bytes 1179656 | tf_op jit(solution)/shard_map/ppermute | solution.py:37
  21.5 9.8 %collective-permute-start.8 = (bf16[1536,128]{1,0:T(8,128)(2,1)S(1)}, bf16[1536,128]{1,0:T(8,128)(2,1)S(1)}, u32[]{:S(2)}, u32[]{:S(2)}) collective-permute-start(bf16[1536,128]{1,0:T(8,128)(2,1)S(1)} %collective-permute-done.3.refs_1_.refs_4_.refs_7_), channel_id=1, source_target_pairs={{1,0},{0,1},{3,2},{2,3},{5,4},{4,5},{7,6},{6,7},{9,8},{8,9},{11,10... | collective-permute-start | bytes 1179656 | tf_op jit(solution)/shard_map/ppermute | solution.py:37
  22.3 12.3 %collective-permute-start.11 = (bf16[2560,128]{1,0:T(8,128)(2,1)S(1)}, bf16[2560,128]{1,0:T(8,128)(2,1)S(1)}, u32[]{:S(2)}, u32[]{:S(2)}) collective-permute-start(bf16[2560,128]{1,0:T(8,128)(2,1)S(1)} %pack_two_mate.1.refs_5_), channel_id=1, source_target_pairs={{1,0},{0,1},{3,2},{2,3},{5,4},{4,5},{7,6},{6,7},{9,8},{8,9},{11,10... | collective-permute-start | bytes 1966088 | tf_op jit(solution)/shard_map/ppermute | solution.py:37
  31.4 7.4 %collective-permute-start.14 = (bf16[2960,128]{1,0:T(8,128)(2,1)S(1)}, bf16[2960,128]{1,0:T(8,128)(2,1)S(1)}, u32[]{:S(2)}, u32[]{:S(2)}) collective-permute-start(bf16[2960,128]{1,0:T(8,128)(2,1)S(1)} %get-tuple-element.40), channel_id=1, source_target_pairs={{1,0},{0,1},{3,2},{2,3},{5,4},{4,5},{7,6},{6,7},{9,8},{8,9},{11,10... | collective-permute-start | bytes 2273288 | tf_op jit(solution)/shard_map/ppermute | solution.py:37
  31.5 6.6 %collective-permute-start.12 = (bf16[640,128]{1,0:T(8,128)(2,1)S(1)}, bf16[640,128]{1,0:T(8,128)(2,1)S(1)}, u32[]{:S(2)}, u32[]{:S(2)}) collective-permute-start(bf16[640,128]{1,0:T(8,128)(2,1)S(1)} %get-tuple-element.34.refs_2_.refs_15_), channel_id=1, source_target_pairs={{16,0},{0,16},{17,1},{1,17},{18,2},{2,18},{19,3},{3,19},{20,4},{4,... | collective-permute-start | bytes 491528 | tf_op jit(solution)/shard_map/ppermute | solution.py:26
  32.1 6.5 %collective-permute-start.13 = (bf16[640,128]{1,0:T(8,128)(2,1)S(1)}, bf16[640,128]{1,0:T(8,128)(2,1)S(1)}, u32[]{:S(2)}, u32[]{:S(2)}) collective-permute-start(bf16[640,128]{1,0:T(8,128)(2,1)S(1)} %get-tuple-element.39), channel_id=1, source_target_pairs={{2,0},{3,1},{0,2},{1,3},{6,4},{7,5},{4,6},{5,7},{10,8},{11,9},{8,1... | collective-permute-start | bytes 491528 | tf_op jit(solution)/shard_map/ppermute | solution.py:37
  33.6 4.5 %collective-permute-start.15 = (bf16[96,128]{1,0:T(8,128)(2,1)S(1)}, bf16[96,128]{1,0:T(8,128)(2,1)S(1)}, u32[]{:S(2)}, u32[]{:S(2)}) collective-permute-start(bf16[96,128]{1,0:T(8,128)(2,1)S(1)} %get-tuple-element.41.refs_0_), channel_id=1, source_target_pairs={{3,0},{2,1},{1,2},{0,3},{7,4},{6,5},{5,6},{4,7},{11,8},{10,9},{9,1... | collective-permute-start | bytes 73736 | tf_op jit(solution)/shard_map/ppermute | solution.py:37
  38.6 1.7 %collective-permute-start.16 = (bf16[1280,128]{1,0:T(8,128)(2,1)S(1)}, bf16[1280,128]{1,0:T(8,128)(2,1)S(1)}, u32[]{:S(2)}, u32[]{:S(2)}) collective-permute-start(bf16[1280,128]{1,0:T(8,128)(2,1)S(1)} %pack_four.1.refs_7_), channel_id=1, source_target_pairs={{1,0},{0,1},{3,2},{2,3},{5,4},{4,5},{7,6},{6,7},{9,8},{8,9},{11,10... | collective-permute-start | bytes 983048 | tf_op jit(solution)/shard_map/ppermute | solution.py:37
  44.4 1.7 %collective-permute-start.17 = (f32[8,128]{1,0:T(8,128)S(1)}, f32[8,128]{1,0:T(8,128)S(1)}, u32[]{:S(2)}, u32[]{:S(2)}) collective-permute-start(f32[8,128]{1,0:T(8,128)S(1)} %get-tuple-element.46), channel_id=1, source_target_pairs={{1,0},{0,1},{3,2},{2,3},{5,4},{4,5},{7,6},{6,7},{9,8},{8,9},{11,10... | collective-permute-start | bytes 12296 | tf_op jit(solution)/shard_map/ppermute | solution.py:37
  44.5 3.0 %collective-permute-start.18 = (f32[8,128]{1,0:T(8,128)S(1)}, f32[8,128]{1,0:T(8,128)S(1)}, u32[]{:S(2)}, u32[]{:S(2)}) collective-permute-start(f32[8,128]{1,0:T(8,128)S(1)} %get-tuple-element.46), channel_id=1, source_target_pairs={{3,0},{2,1},{1,2},{0,3},{7,4},{6,5},{5,6},{4,7},{11,8},{10,9},{9,1... | collective-permute-start | bytes 12296 | tf_op jit(solution)/shard_map/ppermute | solution.py:37
  47.8 3.6 %collective-permute-start.19 = (f32[8,128]{1,0:T(8,128)S(1)}, f32[8,128]{1,0:T(8,128)S(1)}, u32[]{:S(2)}, u32[]{:S(2)}) collective-permute-start(f32[8,128]{1,0:T(8,128)S(1)} %maximum_maximum_fusion.refs_0_), channel_id=1, source_target_pairs={{16,0},{0,16},{17,1},{1,17},{18,2},{2,18},{19,3},{3,19},{20,4},{4,... | collective-permute-start | bytes 12296 | tf_op jit(solution)/shard_map/ppermute | solution.py:26
  51.5 5.4 %collective-permute-start.20 = (f32[16,128]{1,0:T(8,128)S(1)}, f32[16,128]{1,0:T(8,128)S(1)}, u32[]{:S(2)}, u32[]{:S(2)}) collective-permute-start(f32[16,128]{1,0:T(8,128)S(1)} %stack_tiles.1.refs_0_), channel_id=1, source_target_pairs={{12,0},{8,4},{4,8},{0,12},{13,1},{9,5},{5,9},{1,13},{14,2},{10,6},... | collective-permute-start | bytes 24584 | tf_op jit(solution)/shard_map/ppermute | solution.py:32
  54.0 3.7 %collective-permute-start.21 = (f32[16,128]{1,0:T(8,128)S(1)}, f32[16,128]{1,0:T(8,128)S(1)}, u32[]{:S(2)}, u32[]{:S(2)}) collective-permute-start(f32[16,128]{1,0:T(8,128)S(1)} %stack_tiles.1.refs_0_), channel_id=1, source_target_pairs={{4,0},{0,4},{12,8},{8,12},{5,1},{1,5},{13,9},{9,13},{6,2},{2,6},{1... | collective-permute-start | bytes 24584 | tf_op jit(solution)/shard_map/ppermute | solution.py:32

commit v21 on v20

--- a/solution.py
+++ b/solution.py
@@ -92,7 +92,7 @@
 
 
 def pick_kernel(axes, *refs):
-    sign_ref, out_ref, neighbors_ref, extent_ref, x_ref, y_ref, z_ref, place_ref, loads, sems = refs[5:]
+    sign_ref, out_ref, geo_ref, neighbors_ref, extent_ref, x_ref, y_ref, z_ref, place_ref, loads, sems = refs[5:]
     at = Places(*axes)
     slots = sign_ref.shape[0]
     n_pick = place_ref.shape[0] - 1
@@ -124,7 +124,9 @@
         extent = extent_ref[0, w]
         values = jnp.where(sub == 0, twice_x, jnp.where(sub == 1, twice_y, jnp.where(sub == 2, twice_z, extent)))
         geo = jnp.where(lane_pair == rank, values, geo)
-    out_ref[n_pick * size :] = geo.astype(jnp.float32).astype(out_ref.dtype)
+    geo = geo.astype(jnp.float32).astype(out_ref.dtype)
+    geo_ref[...] = geo
+    out_ref[n_pick * size :] = geo
     for copy in copies:
         copy.wait()
 
@@ -417,6 +419,15 @@
             line_ref[o, s] = jnp.where(inside_z, jnp.exp(-rate_z * squared_z), 0.0).astype(line_ref.dtype)
 
 
+def merge_kernel(own_ref, mate_ref, third_ref, out_ref):
+    odd = (lax.axis_index("layer") & 1) == 1
+    lane = lax.broadcasted_iota(jnp.int32, out_ref.shape, 1)
+    below = jnp.where(odd, mate_ref[...], third_ref[...])
+    above = jnp.where(odd, third_ref[...], mate_ref[...])
+    moved = jnp.where(lane < 6 * SPAN, pltpu.roll(below, 3 * SPAN, axis=1), pltpu.roll(above, 3 * SPAN, axis=1))
+    out_ref[...] = jnp.where(lane < 4 * SPAN, own_ref[...], jnp.where(lane < 7 * SPAN, moved, 0.0))
+
+
 def density_kernel(column_steps, *refs):
     coef_refs = refs[:column_steps]
     plane_ref, line_ref, out_ref = refs[column_steps:]
@@ -465,11 +476,14 @@
     x_row = {di: on_row(flat, di) for di in others}
     y_row = from_layer(flat, 2)
     m_row = from_layer(flat, 1)
-    picked = pl.pallas_call(
+    picked, geo = pl.pallas_call(
         functools.partial(pick_kernel, axes),
-        out_shape=jax.ShapeDtypeStruct((part, size), own.dtype),
+        out_shape=(
+            jax.ShapeDtypeStruct((part, size), own.dtype),
+            jax.ShapeDtypeStruct((GEO, LANES), own.dtype),
+        ),
         in_specs=[HBM] * 6,
-        out_specs=VMEM,
+        out_specs=(VMEM, VMEM),
         scratch_shapes=[
             pltpu.SMEM((slots, atoms), jnp.int32),
             pltpu.SMEM((1, slots), jnp.int32),
@@ -487,8 +501,8 @@
     up = from_column(picked, 0)
 
     halves = pack(
-        [y_row] + [x_row[di] for di in others] + [picked],
-        [[(0, half, most)]] + [[(di, 0, most)] for di in others] + [[(count, picks, GEO)]],
+        [y_row] + [x_row[di] for di in others] + [geo],
+        [[(0, half, most)]] + [[(di, 0, most)] for di in others] + [[(count, 0, GEO)]],
         [],
         "pack_halves",
     )
@@ -734,18 +748,15 @@
 
     mate_coef = from_layer(coef, 1)
     third_coef = from_layer(coef, 3)
-    odd = lax.axis_index("layer") % 2 == 1
-    below = jnp.where(odd, mate_coef, third_coef)
-    above = jnp.where(odd, third_coef, mate_coef)
-    merged = jnp.concatenate(
-        [
-            coef[:, : 4 * SPAN],
-            below[:, SPAN : 3 * SPAN],
-            above[:, 3 * SPAN : 4 * SPAN],
-            jnp.zeros((8, LANES - 7 * SPAN), jnp.float32),
-        ],
-        axis=1,
-    )
+    merged = pl.pallas_call(
+        merge_kernel,
+        out_shape=jax.ShapeDtypeStruct((8, LANES), jnp.float32),
+        in_specs=[VMEM] * 3,
+        out_specs=VMEM,
+        compiler_params=pltpu.CompilerParams(vmem_limit_bytes=1 << 20),
+        cost_estimate=pl.CostEstimate(flops=1000, bytes_accessed=1000, transcendentals=0),
+        name="merge_layers",
+    )(coef, mate_coef, third_coef)
     given, token = pack([sign_next.reshape(full, size)], [[(0, 0, full)], [(0, 0, GEO)]], [], "give_sign")
     parts = [merged] + [on_row(merged, di) for di in others]
     stacked = pack(parts, [[(i, 0, 8) for i in range(count)]], [token], "stack_tiles")[0]

time: 59.4 us -> 59.1 us (level)
    pallas_call x1 -> x2, Pallas kernels: 2.47 us -> 2.55 us  [the longest x1 2.48 us: local(): pl.pallas_call(functools.partial(pick_kernel, axes), out_shape=(jax.Shape...]
  transfers between devices with their start and end apart: 22 -> 22, of which waited for: 12 -> 13; matrix products, arithmetic and copies ran while one was open for 0% -> 0% of each run, Pallas kernels for 25% -> 25%
where the time goes in v21:
time: 59.1 us; the launch traced here: 58.8 us
  Pallas kernels  20.3 us (34%)
  starting transfers between devices  19.9 us (34%)
  waiting for transfers between devices  17 us (29%)
  between operations  0.78 us (1%)
  local copies, waits for them, and re-layouts  0.7 us (1%)
    ppermute x13, waiting for transfers between devices, from_layer(): return lax.ppermute(x, 'layer', [(i ^ flip, i) for i in range(count)])  10.2 us
    ppermute x13, starting transfers between devices, from_layer(): return lax.ppermute(x, 'layer', [(i ^ flip, i) for i in range(count)])  8.15 us
    ppermute x4, starting transfers between devices, from_column(): lax.ppermute(x, 'col', [((i + step[i]) % count, i) for i in range(count)])  6.04 us
    ppermute x5, starting transfers between devices, from_offset(): lax.ppermute(x, axis, [((i + step) % count, i) for i in range(count)])  5.75 us
    pallas_call x1, Pallas kernels, local(): pl.pallas_call(functools.partial(prepare_kernel, axes, count, tuple(layou...  4.24 us
    pallas_call x1, Pallas kernels, local(): pl.pallas_call(functools.partial(step_kernel, len(late_values)), out_shap...  4.06 us
    ppermute x4, waiting for transfers between devices, from_column(): lax.ppermute(x, 'col', [((i + step[i]) % count, i) for i in range(count)])  3.74 us
    ppermute x5, waiting for transfers between devices, from_offset(): lax.ppermute(x, axis, [((i + step) % count, i) for i in range(count)])  3.11 us
  transfers between devices with their start and end apart: 22, of which 13 were waited for; matrix products, arithmetic and copies ran while one was open for 0% of the time, Pallas kernels for 25%

profile of v21, /device:TPU:0, one launch (start us, length us, event | category | flops | bytes accessed | tf_op | source)
XLA Modules:
  0.0 58.8 jit_solution(16211861954418019081)
XLA Ops:
  0.6 3.0 %collective-permute-start.2 = (bf16[1536,128]{1,0:T(8,128)(2,1)}, bf16[1536,128]{1,0:T(8,128)(2,1)S(1)}, u32[]{:S(2)}, u32[]{:S(2)}) collective-permute-start(bf16[1536,128]{1,0:T(8,128)(2,1)} %bitcast.10), channel_id=1, source_target_pairs={{2,0},{3,1},{0,2},{1,3},{6,4},{7,5},{4,6},{5,7},{10,8},{11,9},{8,1... | collective-permute-start | bytes 1179656 | tf_op jit(solution)/shard_map/ppermute | solution.py:37
  3.7 1.5 %collective-permute-start.3 = (bf16[1536,128]{1,0:T(8,128)(2,1)}, bf16[1536,128]{1,0:T(8,128)(2,1)S(1)}, u32[]{:S(2)}, u32[]{:S(2)}) collective-permute-start(bf16[1536,128]{1,0:T(8,128)(2,1)} %bitcast.11), channel_id=1, source_target_pairs={{16,0},{0,16},{17,1},{1,17},{18,2},{2,18},{19,3},{3,19},{20,4},{4,... | collective-permute-start | bytes 1179656 | tf_op jit(solution)/shard_map/ppermute | solution.py:26
  5.2 0.0 collective-permute-start.4
  5.2 2.5 %pick_column_blocks.1 = (bf16[656,128]{1,0:T(8,128)(2,1)}, bf16[16,128]{1,0:T(8,128)(2,1)}) custom-call(s32[12,32]{1,0:T(8,128)} %bitcast.18, s32[1,12]{1,0:T(1,128)} %refs_1_.2, s32[32]{0:T(128)} %refs_2_.1, s32[32]{0:T(128)} %refs_3_.1, s32[32]{0:T(128)} %refs_4_.1, bf16[12,128,128]{2,1,0:T(8,128)(2,1)} %bitcast.13), custom_call_target="tpu_custom_call" | custom-call | tf_op jit(solution)/shard_map/pick_column_blocks/pallas_call | solution.py:479
  7.6 3.7 %collective-permute-start = (bf16[656,128]{1,0:T(8,128)(2,1)}, bf16[656,128]{1,0:T(8,128)(2,1)S(1)}, u32[]{:S(2)}, u32[]{:S(2)}) collective-permute-start(bf16[656,128]{1,0:T(8,128)(2,1)} %get-tuple-element.28), channel_id=1, source_target_pairs={{12,0},{8,4},{4,8},{0,12},{13,1},{9,5},{5,9},{1,13},{14,2},{10,6},... | collective-permute-start | bytes 503816 | tf_op jit(solution)/shard_map/ppermute | solution.py:32
  11.3 0.0 collective-permute-start.1
  11.3 1.7 %collective-permute-done.2.refs_0_.refs_3_ = bf16[1536,128]{1,0:T(8,128)(2,1)S(1)} collective-permute-done((bf16[1536,128]{1,0:T(8,128)(2,1)}, bf16[1536,128]{1,0:T(8,128)(2,1)S(1)}, u32[]{:S(2)}, u32[]{:S(2)}) %collective-permute-start.2) | collective-permute-done | bytes 393248 | tf_op jit(solution)/shard_map/ppermute | solution.py:37
  13.0 1.5 %collective-permute-done.3.refs_1_.refs_4_.refs_7_ = bf16[1536,128]{1,0:T(8,128)(2,1)S(1)} collective-permute-done((bf16[1536,128]{1,0:T(8,128)(2,1)}, bf16[1536,128]{1,0:T(8,128)(2,1)S(1)}, u32[]{:S(2)}, u32[]{:S(2)}) %collective-permute-start.3) | collective-permute-done | bytes 393248 | tf_op jit(solution)/shard_map/ppermute | solution.py:26
  14.4 0.0 copy-start.3
  14.5 0.7 %copy-done.3 = bf16[16,128]{1,0:T(8,128)(2,1)S(1)} copy-done((bf16[16,128]{1,0:T(8,128)(2,1)S(1)}, bf16[16,128]{1,0:T(8,128)(2,1)}, u32[]{:S(2)}) %copy-start.3) | copy-done | bytes 4120
  15.2 1.6 %collective-permute-start.9 = (bf16[640,128]{1,0:T(8,128)(2,1)S(1)}, bf16[640,128]{1,0:T(8,128)(2,1)S(1)}, u32[]{:S(2)}, u32[]{:S(2)}) collective-permute-start(bf16[640,128]{1,0:T(8,128)(2,1)S(1)} %get-tuple-element.36), channel_id=1, source_target_pairs={{16,0},{0,16},{17,1},{1,17},{18,2},{2,18},{19,3},{3,19},{20,4},{4,... | collective-permute-start | bytes 491528 | tf_op jit(solution)/shard_map/ppermute | solution.py:26
  16.7 0.5 collective-permute-start.10
  17.2 0.0 collective-permute-done.refs_0_.refs_3_.refs_5_
  17.2 2.9 %collective-permute-done.1.refs_1_.refs_2_.refs_4_ = bf16[656,128]{1,0:T(8,128)(2,1)S(1)} collective-permute-done((bf16[656,128]{1,0:T(8,128)(2,1)}, bf16[656,128]{1,0:T(8,128)(2,1)S(1)}, u32[]{:S(2)}, u32[]{:S(2)}) %collective-permute-start.1) | collective-permute-done | bytes 167968 | tf_op jit(solution)/shard_map/ppermute | solution.py:32
  20.2 0.0 collective-permute-done.4.refs_5_.refs_2_
  20.2 0.1 pack_two.1
  20.3 0.6 collective-permute-start.5
  20.9 0.0 copy-start.1
  20.9 0.0 copy-start.4
  20.9 0.6 %collective-permute-start.6 = (bf16[1456,128]{1,0:T(8,128)(2,1)S(1)}, bf16[1456,128]{1,0:T(8,128)(2,1)S(1)}, u32[]{:S(2)}, u32[]{:S(2)}) collective-permute-start(bf16[1456,128]{1,0:T(8,128)(2,1)S(1)} %get-tuple-element.31.refs_2_), channel_id=1, source_target_pairs={{16,0},{0,16},{17,1},{1,17},{18,2},{2,18},{19,3},{3,19},{20,4},{4,... | collective-permute-start | bytes 1118216 | tf_op jit(solution)/shard_map/ppermute | solution.py:26
  21.5 0.0 collective-permute-start.7
  21.5 0.0 collective-permute-done.9.refs_0_.refs_10_
  21.5 0.5 collective-permute-start.8
  22.0 0.1 collective-permute-done.10.refs_1_.refs_11_
  22.1 0.1 collective-permute-start.11
  22.2 0.0 copy-done.1
  22.2 0.0 copy-done.4
  22.2 4.2 %prepare.1 = (s32[83]{0:T(128)S(1)}, s32[83]{0:T(128)S(1)}, s32[83]{0:T(128)S(1)}, s32[14]{0:T(128)S(1)}) custom-call(s32[12,32]{1,0:T(8,128)S(1)} %bitcast.19, s32[32]{0:T(128)S(1)} %copy-done.4, bf16[1456,128]{1,0:T(8,128)(2,1)S(1)} %get-tuple-element.31.refs_2_), custom_call_target="tpu_custom_call" | custom-call | flops 1000 | bytes 1000 | tf_op jit(solution)/shard_map/prepare/pallas_call | solution.py:613
  26.4 4.5 %collective-permute-done.5.refs_0_.refs_13_ = bf16[1456,128]{1,0:T(8,128)(2,1)S(1)} collective-permute-done((bf16[1456,128]{1,0:T(8,128)(2,1)S(1)}, bf16[1456,128]{1,0:T(8,128)(2,1)S(1)}, u32[]{:S(2)}, u32[]{:S(2)}) %collective-permute-start.5) | collective-permute-done | bytes 372768 | tf_op jit(solution)/shard_map/ppermute | solution.py:37
  31.0 0.3 collective-permute-done.6.refs_2_.refs_12_
  31.3 0.0 collective-permute-done.7.refs_3_.refs_9_
  31.3 0.0 collective-permute-done.8.refs_4_.refs_8_
  31.3 0.1 pack_three.1
  31.4 0.1 collective-permute-start.14
  31.5 0.6 %collective-permute-start.12 = (bf16[640,128]{1,0:T(8,128)(2,1)S(1)}, bf16[640,128]{1,0:T(8,128)(2,1)S(1)}, u32[]{:S(2)}, u32[]{:S(2)}) collective-permute-start(bf16[640,128]{1,0:T(8,128)(2,1)S(1)} %get-tuple-element.38.refs_2_.refs_15_), channel_id=1, source_target_pairs={{16,0},{0,16},{17,1},{1,17},{18,2},{2,18},{19,3},{3,19},{20,4},{4,... | collective-permute-start | bytes 491528 | tf_op jit(solution)/shard_map/ppermute | solution.py:26
  32.1 1.5 %collective-permute-start.13 = (bf16[640,128]{1,0:T(8,128)(2,1)S(1)}, bf16[640,128]{1,0:T(8,128)(2,1)S(1)}, u32[]{:S(2)}, u32[]{:S(2)}) collective-permute-start(bf16[640,128]{1,0:T(8,128)(2,1)S(1)} %get-tuple-element.43), channel_id=1, source_target_pairs={{2,0},{3,1},{0,2},{1,3},{6,4},{7,5},{4,6},{5,7},{10,8},{11,9},{8,1... | collective-permute-start | bytes 491528 | tf_op jit(solution)/shard_map/ppermute | solution.py:37
  33.6 0.0 collective-permute-start.15
  33.6 0.0 copy-done.2
  33.6 1.0 %spread_basis.1 = (bf16[128,1536]{1,0:T(8,128)(2,1)S(1)}, bf16[16,128]{1,0:T(8,128)(2,1)S(1)}) custom-call(s32[12,32]{1,0:T(8,128)S(1)} %bitcast.20, bf16[192,128]{1,0:T(8,128)(2,1)S(1)} %bitcast.21, bf16[640,128]{1,0:T(8,128)(2,1)S(1)} %get-tuple-element.38.refs_2_.refs_15_), custom_call_target="tpu_custom_call" | custom-call | flops 1000 | bytes 1000 | tf_op jit(solution)/shard_map/spread_basis/pallas_call | solution.py:662
  34.6 0.0 collective-permute-done.11.refs_14_
  34.6 0.0 copy-done
  34.7 1.9 %gram_early.1.refs_2_.refs_3_ = bf16[1536,1536]{1,0:T(8,128)(2,1)S(1)} custom-call(s32[83]{0:T(128)S(1)} %get-tuple-element.42.refs_0_, bf16[1536,128]{1,0:T(8,128)(2,1)S(1)} %bitcast.14, bf16[1536,128]{1,0:T(8,128)(2,1)S(1)} %collective-permute-done.4.refs_5_.refs_2_, bf16[1536,128]{1,0:T(8,128)(2,1)S(1)} %collective-permute-done.2.refs_0_.refs_3_, ...), custom_call_target="tpu_custom_call" | custom-call | flops 1000 | bytes 1000 | tf_op jit(solution)/shard_map/gram_early/pallas_call | solution.py:677
  36.6 1.5 %collective-permute-done.15.refs_3_.refs_2_ = bf16[96,128]{1,0:T(8,128)(2,1)S(1)} collective-permute-done((bf16[96,128]{1,0:T(8,128)(2,1)S(1)}, bf16[96,128]{1,0:T(8,128)(2,1)S(1)}, u32[]{:S(2)}, u32[]{:S(2)}) %collective-permute-start.15) | collective-permute-done | bytes 24608 | tf_op jit(solution)/shard_map/ppermute | solution.py:37
  38.1 0.0 collective-permute-done.12.refs_0_.refs_4_
  38.1 0.5 collective-permute-done.13.refs_1_.refs_5_
  38.6 0.2 collective-permute-start.16
  38.8 0.0 collective-permute-done.14.refs_6_.refs_1_
  38.8 1.1 %gram_middle.1 = (bf16[1536,1536]{1,0:T(8,128)(2,1)S(1)}, bf16[128,1536]{1,0:T(8,128)(2,1)S(1)}) custom-call(s32[83]{0:T(128)S(1)} %get-tuple-element.41.refs_0_, s32[14]{0:T(128)S(1)} %get-tuple-element.33.refs_6_.refs_1_, bf16[12,128,128]{2,1,0:T(8,128)(2,1)S(1)} %bitcast.15, bf16[1536,1536]{1,0:T(8,128)(2,1)S(1)} %gram_early.1.refs_2_.refs_3_, ...), custom_call_target="tpu_custom_call" | custom-call | flops 1000 | bytes 1000 | tf_op jit(solution)/shard_map/gram_middle/pallas_call | solution.py:714
  40.0 0.4 collective-permute-done.16.refs_6_
  40.3 4.1 %square_cube_coefficients.1 = (bf16[12,128,128]{2,1,0:T(8,128)(2,1)S(1)}, f32[8,128]{1,0:T(8,128)S(1)}) custom-call(s32[83]{0:T(128)S(1)} %get-tuple-element.32.refs_0_, s32[14]{0:T(128)S(1)} %get-tuple-element.33.refs_6_.refs_1_, bf16[16,128]{1,0:T(8,128)(2,1)S(1)} %get-tuple-element.39.refs_4_.refs_2_, bf16[128,1536]{1,0:T(8,128)(2,1)S(1)} %get-tuple-element.40.refs_3_, ...), custom_call_target="tpu_custom_call" | custom-call | flops 1300000000 | bytes 8000000 | tf_op jit(solution)/shard_map/square_cube_coefficients/pallas_call | solution.py:731
  44.4 0.2 collective-permute-start.17
  44.5 1.5 %collective-permute-start.18 = (f32[8,128]{1,0:T(8,128)S(1)}, f32[8,128]{1,0:T(8,128)S(1)}, u32[]{:S(2)}, u32[]{:S(2)}) collective-permute-start(f32[8,128]{1,0:T(8,128)S(1)} %get-tuple-element.50.own_ref), channel_id=1, source_target_pairs={{3,0},{2,1},{1,2},{0,3},{7,4},{6,5},{5,6},{4,7},{11,8},{10,9},{9,1... | collective-permute-start | bytes 12296 | tf_op jit(solution)/shard_map/ppermute | solution.py:37
  46.0 0.0 collective-permute-done.17.mate_ref
  46.0 1.6 %collective-permute-done.18.third_ref = f32[8,128]{1,0:T(8,128)S(1)} collective-permute-done((f32[8,128]{1,0:T(8,128)S(1)}, f32[8,128]{1,0:T(8,128)S(1)}, u32[]{:S(2)}, u32[]{:S(2)}) %collective-permute-start.18) | collective-permute-done | bytes 4128 | tf_op jit(solution)/shard_map/ppermute | solution.py:37
  47.6 0.1 merge_layers.1.refs_0_
  47.7 1.5 %collective-permute-start.19 = (f32[8,128]{1,0:T(8,128)S(1)}, f32[8,128]{1,0:T(8,128)S(1)}, u32[]{:S(2)}, u32[]{:S(2)}) collective-permute-start(f32[8,128]{1,0:T(8,128)S(1)} %merge_layers.1.refs_0_), channel_id=1, source_target_pairs={{16,0},{0,16},{17,1},{1,17},{18,2},{2,18},{19,3},{3,19},{20,4},{4,... | collective-permute-start | bytes 12296 | tf_op jit(solution)/shard_map/ppermute | solution.py:26
  49.2 0.8 %give_sign.1 = (bf16[1536,128]{1,0:T(8,128)(2,1)}, bf16[16,128]{1,0:T(8,128)(2,1)S(1)}) custom-call(bf16[1536,128]{1,0:T(8,128)(2,1)S(1)} %bitcast.17), custom_call_target="tpu_custom_call" | custom-call | bytes 1000 | tf_op jit(solution)/shard_map/give_sign/pallas_call | solution.py:248
  49.9 1.3 %collective-permute-done.19.refs_1_ = f32[8,128]{1,0:T(8,128)S(1)} collective-permute-done((f32[8,128]{1,0:T(8,128)S(1)}, f32[8,128]{1,0:T(8,128)S(1)}, u32[]{:S(2)}, u32[]{:S(2)}) %collective-permute-start.19) | collective-permute-done | bytes 4128 | tf_op jit(solution)/shard_map/ppermute | solution.py:26
  51.3 2.4 %collective-permute-start.20 = (f32[16,128]{1,0:T(8,128)S(1)}, f32[16,128]{1,0:T(8,128)S(1)}, u32[]{:S(2)}, u32[]{:S(2)}) collective-permute-start(f32[16,128]{1,0:T(8,128)S(1)} %stack_tiles.1.refs_0_), channel_id=1, source_target_pairs={{12,0},{8,4},{4,8},{0,12},{13,1},{9,5},{5,9},{1,13},{14,2},{10,6},... | collective-permute-start | bytes 24584 | tf_op jit(solution)/shard_map/ppermute | solution.py:32
  53.6 0.0 collective-permute-start.21
  53.7 2.8 %profiles.1 = (bf16[6,6,256,128]{3,2,1,0:T(8,128)(2,1)S(1)}, bf16[6,6,128,128]{3,2,1,0:T(8,128)(2,1)S(1)}) custom-call(bf16[96,128]{1,0:T(8,128)(2,1)S(1)} %get-tuple-element.45.refs_0_, bf16[2960,128]{1,0:T(8,128)(2,1)S(1)} %collective-permute-done.14.refs_6_.refs_1_, bf16[96,128]{1,0:T(8,128)(2,1)S(1)} %collective-permute-done.15.refs_3_.refs_2_), custom_call_target="tpu_custom_call" | custom-call | flops 1000 | bytes 1000 | tf_op jit(solution)/shard_map/profiles/pallas_call | solution.py:696
  56.5 0.2 collective-permute-done.20.refs_1_
  56.7 0.6 collective-permute-done.21.refs_2_
  57.3 1.5 %density.1 = f32[256,128]{1,0:T(8,128)} custom-call(f32[16,128]{1,0:T(8,128)S(1)} %stack_tiles.1.refs_0_, f32[16,128]{1,0:T(8,128)S(1)} %collective-permute-done.20.refs_1_, f32[16,128]{1,0:T(8,128)S(1)} %collective-permute-done.21.refs_2_, bf16[6,6,256,128]{3,2,1,0:T(8,128)(2,1)S(1)} %get-tuple-element.52.refs_3_, bf16[4608,128]{1,0:T(8,128)(2,1)S(1)} %bitcast.16), custom_call_target="tpu_custom_call" | custom-call | flops 310000000 | bytes 4000000 | tf_op jit(solution)/shard_map/density/pallas_call | solution.py:766
  (6 shorter events, 0.1 us)
Async XLA Ops:
  0.6 12.4 %collective-permute-start.2 = (bf16[1536,128]{1,0:T(8,128)(2,1)}, bf16[1536,128]{1,0:T(8,128)(2,1)S(1)}, u32[]{:S(2)}, u32[]{:S(2)}) collective-permute-start(bf16[1536,128]{1,0:T(8,128)(2,1)} %bitcast.10), channel_id=1, source_target_pairs={{2,0},{3,1},{0,2},{1,3},{6,4},{7,5},{4,6},{5,7},{10,8},{11,9},{8,1... | collective-permute-start | bytes 1179656 | tf_op jit(solution)/shard_map/ppermute | solution.py:37
  3.7 10.8 %collective-permute-start.3 = (bf16[1536,128]{1,0:T(8,128)(2,1)}, bf16[1536,128]{1,0:T(8,128)(2,1)S(1)}, u32[]{:S(2)}, u32[]{:S(2)}) collective-permute-start(bf16[1536,128]{1,0:T(8,128)(2,1)} %bitcast.11), channel_id=1, source_target_pairs={{16,0},{0,16},{17,1},{1,17},{18,2},{2,18},{19,3},{3,19},{20,4},{4,... | collective-permute-start | bytes 1179656 | tf_op jit(solution)/shard_map/ppermute | solution.py:26
  5.2 15.0 %collective-permute-start.4 = (bf16[1536,128]{1,0:T(8,128)(2,1)}, bf16[1536,128]{1,0:T(8,128)(2,1)S(1)}, u32[]{:S(2)}, u32[]{:S(2)}) collective-permute-start(bf16[1536,128]{1,0:T(8,128)(2,1)} %bitcast.12), channel_id=1, source_target_pairs={{1,0},{0,1},{3,2},{2,3},{5,4},{4,5},{7,6},{6,7},{9,8},{8,9},{11,10... | collective-permute-start | bytes 1179656 | tf_op jit(solution)/shard_map/ppermute | solution.py:37
  7.6 9.6 %collective-permute-start = (bf16[656,128]{1,0:T(8,128)(2,1)}, bf16[656,128]{1,0:T(8,128)(2,1)S(1)}, u32[]{:S(2)}, u32[]{:S(2)}) collective-permute-start(bf16[656,128]{1,0:T(8,128)(2,1)} %get-tuple-element.28), channel_id=1, source_target_pairs={{12,0},{8,4},{4,8},{0,12},{13,1},{9,5},{5,9},{1,13},{14,2},{10,6},... | collective-permute-start | bytes 503816 | tf_op jit(solution)/shard_map/ppermute | solution.py:32
  11.3 8.9 %collective-permute-start.1 = (bf16[656,128]{1,0:T(8,128)(2,1)}, bf16[656,128]{1,0:T(8,128)(2,1)S(1)}, u32[]{:S(2)}, u32[]{:S(2)}) collective-permute-start(bf16[656,128]{1,0:T(8,128)(2,1)} %get-tuple-element.28), channel_id=1, source_target_pairs={{4,0},{0,4},{12,8},{8,12},{5,1},{1,5},{13,9},{9,13},{6,2},{2,6},{1... | collective-permute-start | bytes 503816 | tf_op jit(solution)/shard_map/ppermute | solution.py:32
  14.4 0.7 %copy-start.3 = (bf16[16,128]{1,0:T(8,128)(2,1)S(1)}, bf16[16,128]{1,0:T(8,128)(2,1)}, u32[]{:S(2)}) copy-start(bf16[16,128]{1,0:T(8,128)(2,1)} %get-tuple-element.29.refs_2_) | copy-start | bytes 12292
  15.2 6.3 %collective-permute-start.9 = (bf16[640,128]{1,0:T(8,128)(2,1)S(1)}, bf16[640,128]{1,0:T(8,128)(2,1)S(1)}, u32[]{:S(2)}, u32[]{:S(2)}) collective-permute-start(bf16[640,128]{1,0:T(8,128)(2,1)S(1)} %get-tuple-element.36), channel_id=1, source_target_pairs={{16,0},{0,16},{17,1},{1,17},{18,2},{2,18},{19,3},{3,19},{20,4},{4,... | collective-permute-start | bytes 491528 | tf_op jit(solution)/shard_map/ppermute | solution.py:26
  16.7 5.3 %collective-permute-start.10 = (bf16[640,128]{1,0:T(8,128)(2,1)S(1)}, bf16[640,128]{1,0:T(8,128)(2,1)S(1)}, u32[]{:S(2)}, u32[]{:S(2)}) collective-permute-start(bf16[640,128]{1,0:T(8,128)(2,1)S(1)} %get-tuple-element.37), channel_id=1, source_target_pairs={{2,0},{3,1},{0,2},{1,3},{6,4},{7,5},{4,6},{5,7},{10,8},{11,9},{8,1... | collective-permute-start | bytes 491528 | tf_op jit(solution)/shard_map/ppermute | solution.py:37
  20.3 10.7 %collective-permute-start.5 = (bf16[1456,128]{1,0:T(8,128)(2,1)S(1)}, bf16[1456,128]{1,0:T(8,128)(2,1)S(1)}, u32[]{:S(2)}, u32[]{:S(2)}) collective-permute-start(bf16[1456,128]{1,0:T(8,128)(2,1)S(1)} %get-tuple-element.34), channel_id=1, source_target_pairs={{2,0},{3,1},{0,2},{1,3},{6,4},{7,5},{4,6},{5,7},{10,8},{11,9},{8,1... | collective-permute-start | bytes 1118216 | tf_op jit(solution)/shard_map/ppermute | solution.py:37
  20.9 1.3 %copy-start.1 = (s32[32,12]{0,1:T(8,128)S(1)}, s32[32,12]{0,1:T(8,128)}, u32[]{:S(2)}) copy-start(s32[32,12]{0,1:T(8,128)} %param.9) | copy-start | bytes 4612
  20.9 1.3 %copy-start.4 = (s32[32]{0:T(128)S(1)}, s32[32]{0:T(128)}, u32[]{:S(2)}) copy-start(s32[32]{0:T(128)} %refs_1_.3) | copy-start | bytes 388
  20.9 12.8 %copy-start.2 = (bf16[32,6,128]{2,0,1:T(8,128)(2,1)S(1)}, bf16[32,6,128]{2,0,1:T(8,128)(2,1)}, u32[]{:S(2)}) copy-start(bf16[32,6,128]{2,0,1:T(8,128)(2,1)} %param.11) | copy-start | bytes 147460
  20.9 13.8 %copy-start = (bf16[1,12,128,128]{3,2,1,0:T(8,128)(2,1)S(1)}, bf16[1,12,128,128]{3,2,1,0:T(8,128)(2,1)}, u32[]{:S(2)}) copy-start(bf16[1,12,128,128]{3,2,1,0:T(8,128)(2,1)} %param.8) | copy-start | bytes 1179652
  20.9 10.4 %collective-permute-start.6 = (bf16[1456,128]{1,0:T(8,128)(2,1)S(1)}, bf16[1456,128]{1,0:T(8,128)(2,1)S(1)}, u32[]{:S(2)}, u32[]{:S(2)}) collective-permute-start(bf16[1456,128]{1,0:T(8,128)(2,1)S(1)} %get-tuple-element.31.refs_2_), channel_id=1, source_target_pairs={{16,0},{0,16},{17,1},{1,17},{18,2},{2,18},{19,3},{3,19},{20,4},{4,... | collective-permute-start | bytes 1118216 | tf_op jit(solution)/shard_map/ppermute | solution.py:26
  21.5 9.8 %collective-permute-start.7 = (bf16[1536,128]{1,0:T(8,128)(2,1)S(1)}, bf16[1536,128]{1,0:T(8,128)(2,1)S(1)}, u32[]{:S(2)}, u32[]{:S(2)}) collective-permute-start(bf16[1536,128]{1,0:T(8,128)(2,1)S(1)} %collective-permute-done.2.refs_0_.refs_3_), channel_id=1, source_target_pairs={{1,0},{0,1},{3,2},{2,3},{5,4},{4,5},{7,6},{6,7},{9,8},{8,9},{11,10... | collective-permute-start | bytes 1179656 | tf_op jit(solution)/shard_map/ppermute | solution.py:37
  21.5 9.8 %collective-permute-start.8 = (bf16[1536,128]{1,0:T(8,128)(2,1)S(1)}, bf16[1536,128]{1,0:T(8,128)(2,1)S(1)}, u32[]{:S(2)}, u32[]{:S(2)}) collective-permute-start(bf16[1536,128]{1,0:T(8,128)(2,1)S(1)} %collective-permute-done.3.refs_1_.refs_4_.refs_7_), channel_id=1, source_target_pairs={{1,0},{0,1},{3,2},{2,3},{5,4},{4,5},{7,6},{6,7},{9,8},{8,9},{11,10... | collective-permute-start | bytes 1179656 | tf_op jit(solution)/shard_map/ppermute | solution.py:37
  22.1 12.6 %collective-permute-start.11 = (bf16[2560,128]{1,0:T(8,128)(2,1)S(1)}, bf16[2560,128]{1,0:T(8,128)(2,1)S(1)}, u32[]{:S(2)}, u32[]{:S(2)}) collective-permute-start(bf16[2560,128]{1,0:T(8,128)(2,1)S(1)} %pack_two_mate.1.refs_5_), channel_id=1, source_target_pairs={{1,0},{0,1},{3,2},{2,3},{5,4},{4,5},{7,6},{6,7},{9,8},{8,9},{11,10... | collective-permute-start | bytes 1966088 | tf_op jit(solution)/shard_map/ppermute | solution.py:37
  31.4 7.4 %collective-permute-start.14 = (bf16[2960,128]{1,0:T(8,128)(2,1)S(1)}, bf16[2960,128]{1,0:T(8,128)(2,1)S(1)}, u32[]{:S(2)}, u32[]{:S(2)}) collective-permute-start(bf16[2960,128]{1,0:T(8,128)(2,1)S(1)} %get-tuple-element.44), channel_id=1, source_target_pairs={{1,0},{0,1},{3,2},{2,3},{5,4},{4,5},{7,6},{6,7},{9,8},{8,9},{11,10... | collective-permute-start | bytes 2273288 | tf_op jit(solution)/shard_map/ppermute | solution.py:37
  31.5 6.6 %collective-permute-start.12 = (bf16[640,128]{1,0:T(8,128)(2,1)S(1)}, bf16[640,128]{1,0:T(8,128)(2,1)S(1)}, u32[]{:S(2)}, u32[]{:S(2)}) collective-permute-start(bf16[640,128]{1,0:T(8,128)(2,1)S(1)} %get-tuple-element.38.refs_2_.refs_15_), channel_id=1, source_target_pairs={{16,0},{0,16},{17,1},{1,17},{18,2},{2,18},{19,3},{3,19},{20,4},{4,... | collective-permute-start | bytes 491528 | tf_op jit(solution)/shard_map/ppermute | solution.py:26
  32.1 6.5 %collective-permute-start.13 = (bf16[640,128]{1,0:T(8,128)(2,1)S(1)}, bf16[640,128]{1,0:T(8,128)(2,1)S(1)}, u32[]{:S(2)}, u32[]{:S(2)}) collective-permute-start(bf16[640,128]{1,0:T(8,128)(2,1)S(1)} %get-tuple-element.43), channel_id=1, source_target_pairs={{2,0},{3,1},{0,2},{1,3},{6,4},{7,5},{4,6},{5,7},{10,8},{11,9},{8,1... | collective-permute-start | bytes 491528 | tf_op jit(solution)/shard_map/ppermute | solution.py:37
  33.6 4.5 %collective-permute-start.15 = (bf16[96,128]{1,0:T(8,128)(2,1)S(1)}, bf16[96,128]{1,0:T(8,128)(2,1)S(1)}, u32[]{:S(2)}, u32[]{:S(2)}) collective-permute-start(bf16[96,128]{1,0:T(8,128)(2,1)S(1)} %get-tuple-element.45.refs_0_), channel_id=1, source_target_pairs={{3,0},{2,1},{1,2},{0,3},{7,4},{6,5},{5,6},{4,7},{11,8},{10,9},{9,1... | collective-permute-start | bytes 73736 | tf_op jit(solution)/shard_map/ppermute | solution.py:37
  38.6 1.7 %collective-permute-start.16 = (bf16[1280,128]{1,0:T(8,128)(2,1)S(1)}, bf16[1280,128]{1,0:T(8,128)(2,1)S(1)}, u32[]{:S(2)}, u32[]{:S(2)}) collective-permute-start(bf16[1280,128]{1,0:T(8,128)(2,1)S(1)} %pack_four.1.refs_7_), channel_id=1, source_target_pairs={{1,0},{0,1},{3,2},{2,3},{5,4},{4,5},{7,6},{6,7},{9,8},{8,9},{11,10... | collective-permute-start | bytes 983048 | tf_op jit(solution)/shard_map/ppermute | solution.py:37
  44.4 1.7 %collective-permute-start.17 = (f32[8,128]{1,0:T(8,128)S(1)}, f32[8,128]{1,0:T(8,128)S(1)}, u32[]{:S(2)}, u32[]{:S(2)}) collective-permute-start(f32[8,128]{1,0:T(8,128)S(1)} %get-tuple-element.50.own_ref), channel_id=1, source_target_pairs={{1,0},{0,1},{3,2},{2,3},{5,4},{4,5},{7,6},{6,7},{9,8},{8,9},{11,10... | collective-permute-start | bytes 12296 | tf_op jit(solution)/shard_map/ppermute | solution.py:37
  44.5 3.0 %collective-permute-start.18 = (f32[8,128]{1,0:T(8,128)S(1)}, f32[8,128]{1,0:T(8,128)S(1)}, u32[]{:S(2)}, u32[]{:S(2)}) collective-permute-start(f32[8,128]{1,0:T(8,128)S(1)} %get-tuple-element.50.own_ref), channel_id=1, source_target_pairs={{3,0},{2,1},{1,2},{0,3},{7,4},{6,5},{5,6},{4,7},{11,8},{10,9},{9,1... | collective-permute-start | bytes 12296 | tf_op jit(solution)/shard_map/ppermute | solution.py:37
  47.7 3.6 %collective-permute-start.19 = (f32[8,128]{1,0:T(8,128)S(1)}, f32[8,128]{1,0:T(8,128)S(1)}, u32[]{:S(2)}, u32[]{:S(2)}) collective-permute-start(f32[8,128]{1,0:T(8,128)S(1)} %merge_layers.1.refs_0_), channel_id=1, source_target_pairs={{16,0},{0,16},{17,1},{1,17},{18,2},{2,18},{19,3},{3,19},{20,4},{4,... | collective-permute-start | bytes 12296 | tf_op jit(solution)/shard_map/ppermute | solution.py:26
  51.3 5.4 %collective-permute-start.20 = (f32[16,128]{1,0:T(8,128)S(1)}, f32[16,128]{1,0:T(8,128)S(1)}, u32[]{:S(2)}, u32[]{:S(2)}) collective-permute-start(f32[16,128]{1,0:T(8,128)S(1)} %stack_tiles.1.refs_0_), channel_id=1, source_target_pairs={{12,0},{8,4},{4,8},{0,12},{13,1},{9,5},{5,9},{1,13},{14,2},{10,6},... | collective-permute-start | bytes 24584 | tf_op jit(solution)/shard_map/ppermute | solution.py:32
  53.6 3.7 %collective-permute-start.21 = (f32[16,128]{1,0:T(8,128)S(1)}, f32[16,128]{1,0:T(8,128)S(1)}, u32[]{:S(2)}, u32[]{:S(2)}) collective-permute-start(f32[16,128]{1,0:T(8,128)S(1)} %stack_tiles.1.refs_0_), channel_id=1, source_target_pairs={{4,0},{0,4},{12,8},{8,12},{5,1},{1,5},{13,9},{9,13},{6,2},{2,6},{1... | collective-permute-start | bytes 24584 | tf_op jit(solution)/shard_map/ppermute | solution.py:32

commit v22 on v21

--- a/solution.py
+++ b/solution.py
@@ -99,7 +99,11 @@
     size = sign_ref.shape[1]
     for i in range(n_pick + 1):
         place_ref[i] = 0
-    load(refs[:5], (neighbors_ref, extent_ref, x_ref, y_ref, z_ref), loads)
+    scalars = (neighbors_ref, extent_ref, x_ref, y_ref, z_ref)
+    loading = [pltpu.make_async_copy(refs[i], target, loads.at[i]) for i, target in enumerate(scalars)]
+    for copy in loading:
+        copy.start()
+    loading[0].wait()
     for w in range(slots):
         row, col, lay = at.split(neighbors_ref[w, at.me])
         place = target_place(at.n_row, (row - at.row) & (at.n_row - 1), (lay - at.lay) & (at.n_lay - 1), at.row)
@@ -110,6 +114,8 @@
         copy.start()
         copies.append(copy)
     ranks = own_ranks(at, neighbors_ref)
+    for copy in loading[1:]:
+        copy.wait()
     sub = lax.broadcasted_iota(jnp.int32, (GEO, LANES), 0)
     lane_pair = lax.broadcasted_iota(jnp.int32, (GEO, LANES), 1) // SHELLS
     geo = jnp.zeros((GEO, LANES), jnp.int32)

time: 59.1 us -> 59.1 us (level)
  transfers between devices with their start and end apart: 22 -> 22, of which waited for: 13 -> 12; matrix products, arithmetic and copies ran while one was open for 0% -> 0% of each run, Pallas kernels for 25% -> 26%
where the time goes in v22:
time: 59.1 us; the launch traced here: 58.9 us
  Pallas kernels  20.7 us (35%)
  starting transfers between devices  19.8 us (34%)
  waiting for transfers between devices  16.8 us (28%)
  between operations  0.77 us (1%)
  local copies, waits for them, and re-layouts  0.7 us (1%)
    ppermute x13, waiting for transfers between devices, from_layer(): return lax.ppermute(x, 'layer', [(i ^ flip, i) for i in range(count)])  9.92 us
    ppermute x13, starting transfers between devices, from_layer(): return lax.ppermute(x, 'layer', [(i ^ flip, i) for i in range(count)])  8.11 us
    ppermute x4, starting transfers between devices, from_column(): lax.ppermute(x, 'col', [((i + step[i]) % count, i) for i in range(count)])  5.97 us
    ppermute x5, starting transfers between devices, from_offset(): lax.ppermute(x, axis, [((i + step) % count, i) for i in range(count)])  5.74 us
    pallas_call x1, Pallas kernels, local(): pl.pallas_call(functools.partial(prepare_kernel, axes, count, tuple(layou...  4.24 us
    pallas_call x1, Pallas kernels, local(): pl.pallas_call(functools.partial(step_kernel, len(late_values)), out_shap...  4.16 us
    ppermute x4, waiting for transfers between devices, from_column(): lax.ppermute(x, 'col', [((i + step[i]) % count, i) for i in range(count)])  3.8 us
    ppermute x5, waiting for transfers between devices, from_offset(): lax.ppermute(x, axis, [((i + step) % count, i) for i in range(count)])  3.11 us
  transfers between devices with their start and end apart: 22, of which 12 were waited for; matrix products, arithmetic and copies ran while one was open for 0% of the time, Pallas kernels for 26%

profile of v22, /device:TPU:0, one launch (start us, length us, event | category | flops | bytes accessed | tf_op | source)
XLA Modules:
  0.0 58.9 jit_solution(3841840667549717831)
XLA Ops:
  0.6 3.0 %collective-permute-start.2 = (bf16[1536,128]{1,0:T(8,128)(2,1)}, bf16[1536,128]{1,0:T(8,128)(2,1)S(1)}, u32[]{:S(2)}, u32[]{:S(2)}) collective-permute-start(bf16[1536,128]{1,0:T(8,128)(2,1)} %bitcast.10), channel_id=1, source_target_pairs={{2,0},{3,1},{0,2},{1,3},{6,4},{7,5},{4,6},{5,7},{10,8},{11,9},{8,1... | collective-permute-start | bytes 1179656 | tf_op jit(solution)/shard_map/ppermute | solution.py:37
  3.7 1.5 %collective-permute-start.3 = (bf16[1536,128]{1,0:T(8,128)(2,1)}, bf16[1536,128]{1,0:T(8,128)(2,1)S(1)}, u32[]{:S(2)}, u32[]{:S(2)}) collective-permute-start(bf16[1536,128]{1,0:T(8,128)(2,1)} %bitcast.11), channel_id=1, source_target_pairs={{16,0},{0,16},{17,1},{1,17},{18,2},{2,18},{19,3},{3,19},{20,4},{4,... | collective-permute-start | bytes 1179656 | tf_op jit(solution)/shard_map/ppermute | solution.py:26
  5.2 0.0 collective-permute-start.4
  5.2 2.5 %pick_column_blocks.1 = (bf16[656,128]{1,0:T(8,128)(2,1)}, bf16[16,128]{1,0:T(8,128)(2,1)}) custom-call(s32[12,32]{1,0:T(8,128)} %bitcast.18, s32[1,12]{1,0:T(1,128)} %refs_1_.2, s32[32]{0:T(128)} %refs_2_.1, s32[32]{0:T(128)} %refs_3_.1, s32[32]{0:T(128)} %refs_4_.1, bf16[12,128,128]{2,1,0:T(8,128)(2,1)} %bitcast.13), custom_call_target="tpu_custom_call" | custom-call | tf_op jit(solution)/shard_map/pick_column_blocks/pallas_call | solution.py:485
  7.7 3.7 %collective-permute-start = (bf16[656,128]{1,0:T(8,128)(2,1)}, bf16[656,128]{1,0:T(8,128)(2,1)S(1)}, u32[]{:S(2)}, u32[]{:S(2)}) collective-permute-start(bf16[656,128]{1,0:T(8,128)(2,1)} %get-tuple-element.28), channel_id=1, source_target_pairs={{12,0},{8,4},{4,8},{0,12},{13,1},{9,5},{5,9},{1,13},{14,2},{10,6},... | collective-permute-start | bytes 503816 | tf_op jit(solution)/shard_map/ppermute | solution.py:32
  11.3 0.0 collective-permute-start.1
  11.3 1.6 %collective-permute-done.2.refs_0_.refs_3_ = bf16[1536,128]{1,0:T(8,128)(2,1)S(1)} collective-permute-done((bf16[1536,128]{1,0:T(8,128)(2,1)}, bf16[1536,128]{1,0:T(8,128)(2,1)S(1)}, u32[]{:S(2)}, u32[]{:S(2)}) %collective-permute-start.2) | collective-permute-done | bytes 393248 | tf_op jit(solution)/shard_map/ppermute | solution.py:37
  13.0 1.5 %collective-permute-done.3.refs_1_.refs_4_.refs_7_ = bf16[1536,128]{1,0:T(8,128)(2,1)S(1)} collective-permute-done((bf16[1536,128]{1,0:T(8,128)(2,1)}, bf16[1536,128]{1,0:T(8,128)(2,1)S(1)}, u32[]{:S(2)}, u32[]{:S(2)}) %collective-permute-start.3) | collective-permute-done | bytes 393248 | tf_op jit(solution)/shard_map/ppermute | solution.py:26
  14.4 0.0 copy-start.3
  14.5 0.7 %copy-done.3 = bf16[16,128]{1,0:T(8,128)(2,1)S(1)} copy-done((bf16[16,128]{1,0:T(8,128)(2,1)S(1)}, bf16[16,128]{1,0:T(8,128)(2,1)}, u32[]{:S(2)}) %copy-start.3) | copy-done | bytes 4120
  15.2 1.6 %collective-permute-start.9 = (bf16[640,128]{1,0:T(8,128)(2,1)S(1)}, bf16[640,128]{1,0:T(8,128)(2,1)S(1)}, u32[]{:S(2)}, u32[]{:S(2)}) collective-permute-start(bf16[640,128]{1,0:T(8,128)(2,1)S(1)} %get-tuple-element.36), channel_id=1, source_target_pairs={{16,0},{0,16},{17,1},{1,17},{18,2},{2,18},{19,3},{3,19},{20,4},{4,... | collective-permute-start | bytes 491528 | tf_op jit(solution)/shard_map/ppermute | solution.py:26
  16.7 0.5 collective-permute-start.10
  17.2 0.0 collective-permute-done.refs_0_.refs_3_.refs_5_
  17.2 3.0 %collective-permute-done.1.refs_1_.refs_2_.refs_4_ = bf16[656,128]{1,0:T(8,128)(2,1)S(1)} collective-permute-done((bf16[656,128]{1,0:T(8,128)(2,1)}, bf16[656,128]{1,0:T(8,128)(2,1)S(1)}, u32[]{:S(2)}, u32[]{:S(2)}) %collective-permute-start.1) | collective-permute-done | bytes 167968 | tf_op jit(solution)/shard_map/ppermute | solution.py:32
  20.2 0.0 collective-permute-done.4.refs_5_.refs_2_
  20.2 0.1 pack_two.1
  20.3 0.6 collective-permute-start.5
  20.9 0.0 copy-start.1
  20.9 0.0 copy-start.4
  20.9 0.6 %collective-permute-start.6 = (bf16[1456,128]{1,0:T(8,128)(2,1)S(1)}, bf16[1456,128]{1,0:T(8,128)(2,1)S(1)}, u32[]{:S(2)}, u32[]{:S(2)}) collective-permute-start(bf16[1456,128]{1,0:T(8,128)(2,1)S(1)} %get-tuple-element.31.refs_2_), channel_id=1, source_target_pairs={{16,0},{0,16},{17,1},{1,17},{18,2},{2,18},{19,3},{3,19},{20,4},{4,... | collective-permute-start | bytes 1118216 | tf_op jit(solution)/shard_map/ppermute | solution.py:26
  21.5 0.0 collective-permute-start.7
  21.5 0.0 collective-permute-done.9.refs_0_.refs_10_
  21.5 0.5 collective-permute-start.8
  22.0 0.0 collective-permute-done.10.refs_1_.refs_11_
  22.1 0.1 collective-permute-start.11
  22.2 0.0 copy-done.1
  22.2 0.0 copy-done.4
  22.2 4.2 %prepare.1 = (s32[83]{0:T(128)S(1)}, s32[83]{0:T(128)S(1)}, s32[83]{0:T(128)S(1)}, s32[14]{0:T(128)S(1)}) custom-call(s32[12,32]{1,0:T(8,128)S(1)} %bitcast.19, s32[32]{0:T(128)S(1)} %copy-done.4, bf16[1456,128]{1,0:T(8,128)(2,1)S(1)} %get-tuple-element.31.refs_2_), custom_call_target="tpu_custom_call" | custom-call | flops 1000 | bytes 1000 | tf_op jit(solution)/shard_map/prepare/pallas_call | solution.py:619
  26.4 4.6 %collective-permute-done.5.refs_0_.refs_13_ = bf16[1456,128]{1,0:T(8,128)(2,1)S(1)} collective-permute-done((bf16[1456,128]{1,0:T(8,128)(2,1)S(1)}, bf16[1456,128]{1,0:T(8,128)(2,1)S(1)}, u32[]{:S(2)}, u32[]{:S(2)}) %collective-permute-start.5) | collective-permute-done | bytes 372768 | tf_op jit(solution)/shard_map/ppermute | solution.py:37
  31.0 0.3 collective-permute-done.6.refs_2_.refs_12_
  31.3 0.0 collective-permute-done.7.refs_3_.refs_9_
  31.3 0.0 collective-permute-done.8.refs_4_.refs_8_
  31.3 0.1 pack_three.1
  31.4 0.1 collective-permute-start.14
  31.5 0.6 %collective-permute-start.12 = (bf16[640,128]{1,0:T(8,128)(2,1)S(1)}, bf16[640,128]{1,0:T(8,128)(2,1)S(1)}, u32[]{:S(2)}, u32[]{:S(2)}) collective-permute-start(bf16[640,128]{1,0:T(8,128)(2,1)S(1)} %get-tuple-element.38.refs_2_.refs_15_), channel_id=1, source_target_pairs={{16,0},{0,16},{17,1},{1,17},{18,2},{2,18},{19,3},{3,19},{20,4},{4,... | collective-permute-start | bytes 491528 | tf_op jit(solution)/shard_map/ppermute | solution.py:26
  32.1 1.5 %collective-permute-start.13 = (bf16[640,128]{1,0:T(8,128)(2,1)S(1)}, bf16[640,128]{1,0:T(8,128)(2,1)S(1)}, u32[]{:S(2)}, u32[]{:S(2)}) collective-permute-start(bf16[640,128]{1,0:T(8,128)(2,1)S(1)} %get-tuple-element.43), channel_id=1, source_target_pairs={{2,0},{3,1},{0,2},{1,3},{6,4},{7,5},{4,6},{5,7},{10,8},{11,9},{8,1... | collective-permute-start | bytes 491528 | tf_op jit(solution)/shard_map/ppermute | solution.py:37
  33.6 0.0 collective-permute-start.15
  33.7 0.0 copy-done.2
  33.7 1.0 %spread_basis.1 = (bf16[128,1536]{1,0:T(8,128)(2,1)S(1)}, bf16[16,128]{1,0:T(8,128)(2,1)S(1)}) custom-call(s32[12,32]{1,0:T(8,128)S(1)} %bitcast.20, bf16[192,128]{1,0:T(8,128)(2,1)S(1)} %bitcast.21, bf16[640,128]{1,0:T(8,128)(2,1)S(1)} %get-tuple-element.38.refs_2_.refs_15_), custom_call_target="tpu_custom_call" | custom-call | flops 1000 | bytes 1000 | tf_op jit(solution)/shard_map/spread_basis/pallas_call | solution.py:668
  34.7 0.0 collective-permute-done.11.refs_14_
  34.7 0.0 copy-done
  34.7 2.1 %gram_early.1.refs_2_.refs_3_ = bf16[1536,1536]{1,0:T(8,128)(2,1)S(1)} custom-call(s32[83]{0:T(128)S(1)} %get-tuple-element.42.refs_0_, bf16[1536,128]{1,0:T(8,128)(2,1)S(1)} %bitcast.14, bf16[1536,128]{1,0:T(8,128)(2,1)S(1)} %collective-permute-done.4.refs_5_.refs_2_, bf16[1536,128]{1,0:T(8,128)(2,1)S(1)} %collective-permute-done.2.refs_0_.refs_3_, ...), custom_call_target="tpu_custom_call" | custom-call | flops 1000 | bytes 1000 | tf_op jit(solution)/shard_map/gram_early/pallas_call | solution.py:683
  36.9 1.3 %collective-permute-done.15.refs_3_.refs_2_ = bf16[96,128]{1,0:T(8,128)(2,1)S(1)} collective-permute-done((bf16[96,128]{1,0:T(8,128)(2,1)S(1)}, bf16[96,128]{1,0:T(8,128)(2,1)S(1)}, u32[]{:S(2)}, u32[]{:S(2)}) %collective-permute-start.15) | collective-permute-done | bytes 24608 | tf_op jit(solution)/shard_map/ppermute | solution.py:37
  38.1 0.0 collective-permute-done.12.refs_0_.refs_4_
  38.2 0.5 collective-permute-done.13.refs_1_.refs_5_
  38.7 0.2 collective-permute-start.16
  38.9 0.0 collective-permute-done.14.refs_6_.refs_1_
  38.9 1.2 %gram_middle.1 = (bf16[1536,1536]{1,0:T(8,128)(2,1)S(1)}, bf16[128,1536]{1,0:T(8,128)(2,1)S(1)}) custom-call(s32[83]{0:T(128)S(1)} %get-tuple-element.41.refs_0_, s32[14]{0:T(128)S(1)} %get-tuple-element.33.refs_6_.refs_1_, bf16[12,128,128]{2,1,0:T(8,128)(2,1)S(1)} %bitcast.15, bf16[1536,1536]{1,0:T(8,128)(2,1)S(1)} %gram_early.1.refs_2_.refs_3_, ...), custom_call_target="tpu_custom_call" | custom-call | flops 1000 | bytes 1000 | tf_op jit(solution)/shard_map/gram_middle/pallas_call | solution.py:720
  40.1 0.3 collective-permute-done.16.refs_6_
  40.4 4.2 %square_cube_coefficients.1 = (bf16[12,128,128]{2,1,0:T(8,128)(2,1)S(1)}, f32[8,128]{1,0:T(8,128)S(1)}) custom-call(s32[83]{0:T(128)S(1)} %get-tuple-element.32.refs_0_, s32[14]{0:T(128)S(1)} %get-tuple-element.33.refs_6_.refs_1_, bf16[16,128]{1,0:T(8,128)(2,1)S(1)} %get-tuple-element.39.refs_4_.refs_2_, bf16[128,1536]{1,0:T(8,128)(2,1)S(1)} %get-tuple-element.40.refs_3_, ...), custom_call_target="tpu_custom_call" | custom-call | flops 1300000000 | bytes 8000000 | tf_op jit(solution)/shard_map/square_cube_coefficients/pallas_call | solution.py:737
  44.5 0.2 collective-permute-start.17
  44.7 1.4 %collective-permute-start.18 = (f32[8,128]{1,0:T(8,128)S(1)}, f32[8,128]{1,0:T(8,128)S(1)}, u32[]{:S(2)}, u32[]{:S(2)}) collective-permute-start(f32[8,128]{1,0:T(8,128)S(1)} %get-tuple-element.50.own_ref), channel_id=1, source_target_pairs={{3,0},{2,1},{1,2},{0,3},{7,4},{6,5},{5,6},{4,7},{11,8},{10,9},{9,1... | collective-permute-start | bytes 12296 | tf_op jit(solution)/shard_map/ppermute | solution.py:37
  46.2 0.0 collective-permute-done.17.mate_ref
  46.2 1.6 %collective-permute-done.18.third_ref = f32[8,128]{1,0:T(8,128)S(1)} collective-permute-done((f32[8,128]{1,0:T(8,128)S(1)}, f32[8,128]{1,0:T(8,128)S(1)}, u32[]{:S(2)}, u32[]{:S(2)}) %collective-permute-start.18) | collective-permute-done | bytes 4128 | tf_op jit(solution)/shard_map/ppermute | solution.py:37
  47.8 0.1 merge_layers.1.refs_0_
  47.8 1.5 %collective-permute-start.19 = (f32[8,128]{1,0:T(8,128)S(1)}, f32[8,128]{1,0:T(8,128)S(1)}, u32[]{:S(2)}, u32[]{:S(2)}) collective-permute-start(f32[8,128]{1,0:T(8,128)S(1)} %merge_layers.1.refs_0_), channel_id=1, source_target_pairs={{16,0},{0,16},{17,1},{1,17},{18,2},{2,18},{19,3},{3,19},{20,4},{4,... | collective-permute-start | bytes 12296 | tf_op jit(solution)/shard_map/ppermute | solution.py:26
  49.3 0.8 %give_sign.1 = (bf16[1536,128]{1,0:T(8,128)(2,1)}, bf16[16,128]{1,0:T(8,128)(2,1)S(1)}) custom-call(bf16[1536,128]{1,0:T(8,128)(2,1)S(1)} %bitcast.17), custom_call_target="tpu_custom_call" | custom-call | bytes 1000 | tf_op jit(solution)/shard_map/give_sign/pallas_call | solution.py:254
  50.1 1.3 %collective-permute-done.19.refs_1_ = f32[8,128]{1,0:T(8,128)S(1)} collective-permute-done((f32[8,128]{1,0:T(8,128)S(1)}, f32[8,128]{1,0:T(8,128)S(1)}, u32[]{:S(2)}, u32[]{:S(2)}) %collective-permute-start.19) | collective-permute-done | bytes 4128 | tf_op jit(solution)/shard_map/ppermute | solution.py:26
  51.5 2.3 %collective-permute-start.20 = (f32[16,128]{1,0:T(8,128)S(1)}, f32[16,128]{1,0:T(8,128)S(1)}, u32[]{:S(2)}, u32[]{:S(2)}) collective-permute-start(f32[16,128]{1,0:T(8,128)S(1)} %stack_tiles.1.refs_0_), channel_id=1, source_target_pairs={{12,0},{8,4},{4,8},{0,12},{13,1},{9,5},{5,9},{1,13},{14,2},{10,6},... | collective-permute-start | bytes 24584 | tf_op jit(solution)/shard_map/ppermute | solution.py:32
  53.8 0.0 collective-permute-start.21
  53.8 2.8 %profiles.1 = (bf16[6,6,256,128]{3,2,1,0:T(8,128)(2,1)S(1)}, bf16[6,6,128,128]{3,2,1,0:T(8,128)(2,1)S(1)}) custom-call(bf16[96,128]{1,0:T(8,128)(2,1)S(1)} %get-tuple-element.45.refs_0_, bf16[2960,128]{1,0:T(8,128)(2,1)S(1)} %collective-permute-done.14.refs_6_.refs_1_, bf16[96,128]{1,0:T(8,128)(2,1)S(1)} %collective-permute-done.15.refs_3_.refs_2_), custom_call_target="tpu_custom_call" | custom-call | flops 1000 | bytes 1000 | tf_op jit(solution)/shard_map/profiles/pallas_call | solution.py:702
  56.6 0.3 collective-permute-done.20.refs_1_
  56.9 0.5 collective-permute-done.21.refs_2_
  57.4 1.5 %density.1 = f32[256,128]{1,0:T(8,128)} custom-call(f32[16,128]{1,0:T(8,128)S(1)} %stack_tiles.1.refs_0_, f32[16,128]{1,0:T(8,128)S(1)} %collective-permute-done.20.refs_1_, f32[16,128]{1,0:T(8,128)S(1)} %collective-permute-done.21.refs_2_, bf16[6,6,256,128]{3,2,1,0:T(8,128)(2,1)S(1)} %get-tuple-element.52.refs_3_, bf16[4608,128]{1,0:T(8,128)(2,1)S(1)} %bitcast.16), custom_call_target="tpu_custom_call" | custom-call | flops 310000000 | bytes 4000000 | tf_op jit(solution)/shard_map/density/pallas_call | solution.py:772
  (6 shorter events, 0.1 us)
Async XLA Ops:
  0.6 12.4 %collective-permute-start.2 = (bf16[1536,128]{1,0:T(8,128)(2,1)}, bf16[1536,128]{1,0:T(8,128)(2,1)S(1)}, u32[]{:S(2)}, u32[]{:S(2)}) collective-permute-start(bf16[1536,128]{1,0:T(8,128)(2,1)} %bitcast.10), channel_id=1, source_target_pairs={{2,0},{3,1},{0,2},{1,3},{6,4},{7,5},{4,6},{5,7},{10,8},{11,9},{8,1... | collective-permute-start | bytes 1179656 | tf_op jit(solution)/shard_map/ppermute | solution.py:37
  3.7 10.8 %collective-permute-start.3 = (bf16[1536,128]{1,0:T(8,128)(2,1)}, bf16[1536,128]{1,0:T(8,128)(2,1)S(1)}, u32[]{:S(2)}, u32[]{:S(2)}) collective-permute-start(bf16[1536,128]{1,0:T(8,128)(2,1)} %bitcast.11), channel_id=1, source_target_pairs={{16,0},{0,16},{17,1},{1,17},{18,2},{2,18},{19,3},{3,19},{20,4},{4,... | collective-permute-start | bytes 1179656 | tf_op jit(solution)/shard_map/ppermute | solution.py:26
  5.2 15.1 %collective-permute-start.4 = (bf16[1536,128]{1,0:T(8,128)(2,1)}, bf16[1536,128]{1,0:T(8,128)(2,1)S(1)}, u32[]{:S(2)}, u32[]{:S(2)}) collective-permute-start(bf16[1536,128]{1,0:T(8,128)(2,1)} %bitcast.12), channel_id=1, source_target_pairs={{1,0},{0,1},{3,2},{2,3},{5,4},{4,5},{7,6},{6,7},{9,8},{8,9},{11,10... | collective-permute-start | bytes 1179656 | tf_op jit(solution)/shard_map/ppermute | solution.py:37
  7.7 9.6 %collective-permute-start = (bf16[656,128]{1,0:T(8,128)(2,1)}, bf16[656,128]{1,0:T(8,128)(2,1)S(1)}, u32[]{:S(2)}, u32[]{:S(2)}) collective-permute-start(bf16[656,128]{1,0:T(8,128)(2,1)} %get-tuple-element.28), channel_id=1, source_target_pairs={{12,0},{8,4},{4,8},{0,12},{13,1},{9,5},{5,9},{1,13},{14,2},{10,6},... | collective-permute-start | bytes 503816 | tf_op jit(solution)/shard_map/ppermute | solution.py:32
  11.3 8.9 %collective-permute-start.1 = (bf16[656,128]{1,0:T(8,128)(2,1)}, bf16[656,128]{1,0:T(8,128)(2,1)S(1)}, u32[]{:S(2)}, u32[]{:S(2)}) collective-permute-start(bf16[656,128]{1,0:T(8,128)(2,1)} %get-tuple-element.28), channel_id=1, source_target_pairs={{4,0},{0,4},{12,8},{8,12},{5,1},{1,5},{13,9},{9,13},{6,2},{2,6},{1... | collective-permute-start | bytes 503816 | tf_op jit(solution)/shard_map/ppermute | solution.py:32
  14.4 0.7 %copy-start.3 = (bf16[16,128]{1,0:T(8,128)(2,1)S(1)}, bf16[16,128]{1,0:T(8,128)(2,1)}, u32[]{:S(2)}) copy-start(bf16[16,128]{1,0:T(8,128)(2,1)} %get-tuple-element.29.refs_2_) | copy-start | bytes 12292
  15.2 6.4 %collective-permute-start.9 = (bf16[640,128]{1,0:T(8,128)(2,1)S(1)}, bf16[640,128]{1,0:T(8,128)(2,1)S(1)}, u32[]{:S(2)}, u32[]{:S(2)}) collective-permute-start(bf16[640,128]{1,0:T(8,128)(2,1)S(1)} %get-tuple-element.36), channel_id=1, source_target_pairs={{16,0},{0,16},{17,1},{1,17},{18,2},{2,18},{19,3},{3,19},{20,4},{4,... | collective-permute-start | bytes 491528 | tf_op jit(solution)/shard_map/ppermute | solution.py:26
  16.7 5.3 %collective-permute-start.10 = (bf16[640,128]{1,0:T(8,128)(2,1)S(1)}, bf16[640,128]{1,0:T(8,128)(2,1)S(1)}, u32[]{:S(2)}, u32[]{:S(2)}) collective-permute-start(bf16[640,128]{1,0:T(8,128)(2,1)S(1)} %get-tuple-element.37), channel_id=1, source_target_pairs={{2,0},{3,1},{0,2},{1,3},{6,4},{7,5},{4,6},{5,7},{10,8},{11,9},{8,1... | collective-permute-start | bytes 491528 | tf_op jit(solution)/shard_map/ppermute | solution.py:37
  20.3 10.7 %collective-permute-start.5 = (bf16[1456,128]{1,0:T(8,128)(2,1)S(1)}, bf16[1456,128]{1,0:T(8,128)(2,1)S(1)}, u32[]{:S(2)}, u32[]{:S(2)}) collective-permute-start(bf16[1456,128]{1,0:T(8,128)(2,1)S(1)} %get-tuple-element.34), channel_id=1, source_target_pairs={{2,0},{3,1},{0,2},{1,3},{6,4},{7,5},{4,6},{5,7},{10,8},{11,9},{8,1... | collective-permute-start | bytes 1118216 | tf_op jit(solution)/shard_map/ppermute | solution.py:37
  20.9 1.3 %copy-start.1 = (s32[32,12]{0,1:T(8,128)S(1)}, s32[32,12]{0,1:T(8,128)}, u32[]{:S(2)}) copy-start(s32[32,12]{0,1:T(8,128)} %param.9) | copy-start | bytes 4612
  20.9 1.3 %copy-start.4 = (s32[32]{0:T(128)S(1)}, s32[32]{0:T(128)}, u32[]{:S(2)}) copy-start(s32[32]{0:T(128)} %refs_1_.3) | copy-start | bytes 388
  20.9 12.7 %copy-start.2 = (bf16[32,6,128]{2,0,1:T(8,128)(2,1)S(1)}, bf16[32,6,128]{2,0,1:T(8,128)(2,1)}, u32[]{:S(2)}) copy-start(bf16[32,6,128]{2,0,1:T(8,128)(2,1)} %param.11) | copy-start | bytes 147460
  20.9 13.8 %copy-start = (bf16[1,12,128,128]{3,2,1,0:T(8,128)(2,1)S(1)}, bf16[1,12,128,128]{3,2,1,0:T(8,128)(2,1)}, u32[]{:S(2)}) copy-start(bf16[1,12,128,128]{3,2,1,0:T(8,128)(2,1)} %param.8) | copy-start | bytes 1179652
  20.9 10.4 %collective-permute-start.6 = (bf16[1456,128]{1,0:T(8,128)(2,1)S(1)}, bf16[1456,128]{1,0:T(8,128)(2,1)S(1)}, u32[]{:S(2)}, u32[]{:S(2)}) collective-permute-start(bf16[1456,128]{1,0:T(8,128)(2,1)S(1)} %get-tuple-element.31.refs_2_), channel_id=1, source_target_pairs={{16,0},{0,16},{17,1},{1,17},{18,2},{2,18},{19,3},{3,19},{20,4},{4,... | collective-permute-start | bytes 1118216 | tf_op jit(solution)/shard_map/ppermute | solution.py:26
  21.5 9.8 %collective-permute-start.7 = (bf16[1536,128]{1,0:T(8,128)(2,1)S(1)}, bf16[1536,128]{1,0:T(8,128)(2,1)S(1)}, u32[]{:S(2)}, u32[]{:S(2)}) collective-permute-start(bf16[1536,128]{1,0:T(8,128)(2,1)S(1)} %collective-permute-done.2.refs_0_.refs_3_), channel_id=1, source_target_pairs={{1,0},{0,1},{3,2},{2,3},{5,4},{4,5},{7,6},{6,7},{9,8},{8,9},{11,10... | collective-permute-start | bytes 1179656 | tf_op jit(solution)/shard_map/ppermute | solution.py:37
  21.5 9.8 %collective-permute-start.8 = (bf16[1536,128]{1,0:T(8,128)(2,1)S(1)}, bf16[1536,128]{1,0:T(8,128)(2,1)S(1)}, u32[]{:S(2)}, u32[]{:S(2)}) collective-permute-start(bf16[1536,128]{1,0:T(8,128)(2,1)S(1)} %collective-permute-done.3.refs_1_.refs_4_.refs_7_), channel_id=1, source_target_pairs={{1,0},{0,1},{3,2},{2,3},{5,4},{4,5},{7,6},{6,7},{9,8},{8,9},{11,10... | collective-permute-start | bytes 1179656 | tf_op jit(solution)/shard_map/ppermute | solution.py:37
  22.1 12.6 %collective-permute-start.11 = (bf16[2560,128]{1,0:T(8,128)(2,1)S(1)}, bf16[2560,128]{1,0:T(8,128)(2,1)S(1)}, u32[]{:S(2)}, u32[]{:S(2)}) collective-permute-start(bf16[2560,128]{1,0:T(8,128)(2,1)S(1)} %pack_two_mate.1.refs_5_), channel_id=1, source_target_pairs={{1,0},{0,1},{3,2},{2,3},{5,4},{4,5},{7,6},{6,7},{9,8},{8,9},{11,10... | collective-permute-start | bytes 1966088 | tf_op jit(solution)/shard_map/ppermute | solution.py:37
  31.4 7.4 %collective-permute-start.14 = (bf16[2960,128]{1,0:T(8,128)(2,1)S(1)}, bf16[2960,128]{1,0:T(8,128)(2,1)S(1)}, u32[]{:S(2)}, u32[]{:S(2)}) collective-permute-start(bf16[2960,128]{1,0:T(8,128)(2,1)S(1)} %get-tuple-element.44), channel_id=1, source_target_pairs={{1,0},{0,1},{3,2},{2,3},{5,4},{4,5},{7,6},{6,7},{9,8},{8,9},{11,10... | collective-permute-start | bytes 2273288 | tf_op jit(solution)/shard_map/ppermute | solution.py:37
  31.5 6.6 %collective-permute-start.12 = (bf16[640,128]{1,0:T(8,128)(2,1)S(1)}, bf16[640,128]{1,0:T(8,128)(2,1)S(1)}, u32[]{:S(2)}, u32[]{:S(2)}) collective-permute-start(bf16[640,128]{1,0:T(8,128)(2,1)S(1)} %get-tuple-element.38.refs_2_.refs_15_), channel_id=1, source_target_pairs={{16,0},{0,16},{17,1},{1,17},{18,2},{2,18},{19,3},{3,19},{20,4},{4,... | collective-permute-start | bytes 491528 | tf_op jit(solution)/shard_map/ppermute | solution.py:26
  32.1 6.5 %collective-permute-start.13 = (bf16[640,128]{1,0:T(8,128)(2,1)S(1)}, bf16[640,128]{1,0:T(8,128)(2,1)S(1)}, u32[]{:S(2)}, u32[]{:S(2)}) collective-permute-start(bf16[640,128]{1,0:T(8,128)(2,1)S(1)} %get-tuple-element.43), channel_id=1, source_target_pairs={{2,0},{3,1},{0,2},{1,3},{6,4},{7,5},{4,6},{5,7},{10,8},{11,9},{8,1... | collective-permute-start | bytes 491528 | tf_op jit(solution)/shard_map/ppermute | solution.py:37
  33.6 4.5 %collective-permute-start.15 = (bf16[96,128]{1,0:T(8,128)(2,1)S(1)}, bf16[96,128]{1,0:T(8,128)(2,1)S(1)}, u32[]{:S(2)}, u32[]{:S(2)}) collective-permute-start(bf16[96,128]{1,0:T(8,128)(2,1)S(1)} %get-tuple-element.45.refs_0_), channel_id=1, source_target_pairs={{3,0},{2,1},{1,2},{0,3},{7,4},{6,5},{5,6},{4,7},{11,8},{10,9},{9,1... | collective-permute-start | bytes 73736 | tf_op jit(solution)/shard_map/ppermute | solution.py:37
  38.7 1.7 %collective-permute-start.16 = (bf16[1280,128]{1,0:T(8,128)(2,1)S(1)}, bf16[1280,128]{1,0:T(8,128)(2,1)S(1)}, u32[]{:S(2)}, u32[]{:S(2)}) collective-permute-start(bf16[1280,128]{1,0:T(8,128)(2,1)S(1)} %pack_four.1.refs_7_), channel_id=1, source_target_pairs={{1,0},{0,1},{3,2},{2,3},{5,4},{4,5},{7,6},{6,7},{9,8},{8,9},{11,10... | collective-permute-start | bytes 983048 | tf_op jit(solution)/shard_map/ppermute | solution.py:37
  44.5 1.6 %collective-permute-start.17 = (f32[8,128]{1,0:T(8,128)S(1)}, f32[8,128]{1,0:T(8,128)S(1)}, u32[]{:S(2)}, u32[]{:S(2)}) collective-permute-start(f32[8,128]{1,0:T(8,128)S(1)} %get-tuple-element.50.own_ref), channel_id=1, source_target_pairs={{1,0},{0,1},{3,2},{2,3},{5,4},{4,5},{7,6},{6,7},{9,8},{8,9},{11,10... | collective-permute-start | bytes 12296 | tf_op jit(solution)/shard_map/ppermute | solution.py:37
  44.7 3.0 %collective-permute-start.18 = (f32[8,128]{1,0:T(8,128)S(1)}, f32[8,128]{1,0:T(8,128)S(1)}, u32[]{:S(2)}, u32[]{:S(2)}) collective-permute-start(f32[8,128]{1,0:T(8,128)S(1)} %get-tuple-element.50.own_ref), channel_id=1, source_target_pairs={{3,0},{2,1},{1,2},{0,3},{7,4},{6,5},{5,6},{4,7},{11,8},{10,9},{9,1... | collective-permute-start | bytes 12296 | tf_op jit(solution)/shard_map/ppermute | solution.py:37
  47.8 3.6 %collective-permute-start.19 = (f32[8,128]{1,0:T(8,128)S(1)}, f32[8,128]{1,0:T(8,128)S(1)}, u32[]{:S(2)}, u32[]{:S(2)}) collective-permute-start(f32[8,128]{1,0:T(8,128)S(1)} %merge_layers.1.refs_0_), channel_id=1, source_target_pairs={{16,0},{0,16},{17,1},{1,17},{18,2},{2,18},{19,3},{3,19},{20,4},{4,... | collective-permute-start | bytes 12296 | tf_op jit(solution)/shard_map/ppermute | solution.py:26
  51.5 5.4 %collective-permute-start.20 = (f32[16,128]{1,0:T(8,128)S(1)}, f32[16,128]{1,0:T(8,128)S(1)}, u32[]{:S(2)}, u32[]{:S(2)}) collective-permute-start(f32[16,128]{1,0:T(8,128)S(1)} %stack_tiles.1.refs_0_), channel_id=1, source_target_pairs={{12,0},{8,4},{4,8},{0,12},{13,1},{9,5},{5,9},{1,13},{14,2},{10,6},... | collective-permute-start | bytes 24584 | tf_op jit(solution)/shard_map/ppermute | solution.py:32
  53.8 3.7 %collective-permute-start.21 = (f32[16,128]{1,0:T(8,128)S(1)}, f32[16,128]{1,0:T(8,128)S(1)}, u32[]{:S(2)}, u32[]{:S(2)}) collective-permute-start(f32[16,128]{1,0:T(8,128)S(1)} %stack_tiles.1.refs_0_), channel_id=1, source_target_pairs={{4,0},{0,4},{12,8},{8,12},{5,1},{1,5},{13,9},{9,13},{6,2},{2,6},{1... | collective-permute-start | bytes 24584 | tf_op jit(solution)/shard_map/ppermute | solution.py:32

commit v23 on v22

--- a/solution.py
+++ b/solution.py
@@ -440,7 +440,7 @@
     total = jnp.zeros(out_ref.shape, jnp.float32)
     wide = SHELLS * LANES
     for o in range(plane_ref.shape[0]):
-        coef = coef_refs[-o % column_steps]
+        coef = coef_refs[o % column_steps]
         first = 8 * (o // column_steps)
         terms = [
             (plane_ref[o, s].astype(jnp.float32) * coef[first + s : first + s + 1, :]).astype(line_ref.dtype)
@@ -767,7 +767,7 @@
     parts = [merged] + [on_row(merged, di) for di in others]
     stacked = pack(parts, [[(i, 0, 8) for i in range(count)]], [token], "stack_tiles")[0]
     far_side = from_column(stacked, 1)
-    received = [stacked, far_side, from_column(stacked, 0)]
+    received = [stacked, from_column(stacked, 0), far_side]
 
     density = pl.pallas_call(
         functools.partial(density_kernel, len(column_steps)),

time: 59.1 us -> 59.9 us (1.014)
  starting transfers between devices: 19.8 us -> 20.4 us
  transfers between devices with their start and end apart: 22 -> 22, of which waited for: 12 -> 11; matrix products, arithmetic and copies ran while one was open for 0% -> 0% of each run, Pallas kernels for 26% -> 25%
where the time goes in v23:
time: 59.9 us; the launch traced here: 59.7 us
  Pallas kernels  20.7 us (35%)
  starting transfers between devices  20.4 us (34%)
  waiting for transfers between devices  17.1 us (29%)
  between operations  0.78 us (1%)
  local copies, waits for them, and re-layouts  0.7 us (1%)
    ppermute x13, waiting for transfers between devices, from_layer(): return lax.ppermute(x, 'layer', [(i ^ flip, i) for i in range(count)])  9.79 us
    ppermute x13, starting transfers between devices, from_layer(): return lax.ppermute(x, 'layer', [(i ^ flip, i) for i in range(count)])  8.21 us
    ppermute x4, starting transfers between devices, from_column(): lax.ppermute(x, 'col', [((i + step[i]) % count, i) for i in range(count)])  6.45 us
    ppermute x5, starting transfers between devices, from_offset(): lax.ppermute(x, axis, [((i + step) % count, i) for i in range(count)])  5.76 us
    pallas_call x1, Pallas kernels, local(): pl.pallas_call(functools.partial(prepare_kernel, axes, count, tuple(layou...  4.24 us
    ppermute x4, waiting for transfers between devices, from_column(): lax.ppermute(x, 'col', [((i + step[i]) % count, i) for i in range(count)])  4.16 us
    pallas_call x1, Pallas kernels, local(): pl.pallas_call(functools.partial(step_kernel, len(late_values)), out_shap...  4.16 us
    ppermute x5, waiting for transfers between devices, from_offset(): lax.ppermute(x, axis, [((i + step) % count, i) for i in range(count)])  3.11 us
  transfers between devices with their start and end apart: 22, of which 11 were waited for; matrix products, arithmetic and copies ran while one was open for 0% of the time, Pallas kernels for 25%

profile of v23, /device:TPU:0, one launch (start us, length us, event | category | flops | bytes accessed | tf_op | source)
XLA Modules:
  0.0 59.7 jit_solution(10829637019832333866)
XLA Ops:
  0.6 3.0 %collective-permute-start.2 = (bf16[1536,128]{1,0:T(8,128)(2,1)}, bf16[1536,128]{1,0:T(8,128)(2,1)S(1)}, u32[]{:S(2)}, u32[]{:S(2)}) collective-permute-start(bf16[1536,128]{1,0:T(8,128)(2,1)} %bitcast.10), channel_id=1, source_target_pairs={{2,0},{3,1},{0,2},{1,3},{6,4},{7,5},{4,6},{5,7},{10,8},{11,9},{8,1... | collective-permute-start | bytes 1179656 | tf_op jit(solution)/shard_map/ppermute | solution.py:37
  3.7 1.5 %collective-permute-start.3 = (bf16[1536,128]{1,0:T(8,128)(2,1)}, bf16[1536,128]{1,0:T(8,128)(2,1)S(1)}, u32[]{:S(2)}, u32[]{:S(2)}) collective-permute-start(bf16[1536,128]{1,0:T(8,128)(2,1)} %bitcast.11), channel_id=1, source_target_pairs={{16,0},{0,16},{17,1},{1,17},{18,2},{2,18},{19,3},{3,19},{20,4},{4,... | collective-permute-start | bytes 1179656 | tf_op jit(solution)/shard_map/ppermute | solution.py:26
  5.2 0.0 collective-permute-start.4
  5.2 2.5 %pick_column_blocks.1 = (bf16[656,128]{1,0:T(8,128)(2,1)}, bf16[16,128]{1,0:T(8,128)(2,1)}) custom-call(s32[12,32]{1,0:T(8,128)} %bitcast.18, s32[1,12]{1,0:T(1,128)} %refs_1_.2, s32[32]{0:T(128)} %refs_2_.1, s32[32]{0:T(128)} %refs_3_.1, s32[32]{0:T(128)} %refs_4_.1, bf16[12,128,128]{2,1,0:T(8,128)(2,1)} %bitcast.13), custom_call_target="tpu_custom_call" | custom-call | tf_op jit(solution)/shard_map/pick_column_blocks/pallas_call | solution.py:485
  7.7 3.7 %collective-permute-start = (bf16[656,128]{1,0:T(8,128)(2,1)}, bf16[656,128]{1,0:T(8,128)(2,1)S(1)}, u32[]{:S(2)}, u32[]{:S(2)}) collective-permute-start(bf16[656,128]{1,0:T(8,128)(2,1)} %get-tuple-element.28), channel_id=1, source_target_pairs={{12,0},{8,4},{4,8},{0,12},{13,1},{9,5},{5,9},{1,13},{14,2},{10,6},... | collective-permute-start | bytes 503816 | tf_op jit(solution)/shard_map/ppermute | solution.py:32
  11.3 0.0 collective-permute-start.1
  11.3 1.6 %collective-permute-done.2.refs_0_.refs_3_ = bf16[1536,128]{1,0:T(8,128)(2,1)S(1)} collective-permute-done((bf16[1536,128]{1,0:T(8,128)(2,1)}, bf16[1536,128]{1,0:T(8,128)(2,1)S(1)}, u32[]{:S(2)}, u32[]{:S(2)}) %collective-permute-start.2) | collective-permute-done | bytes 393248 | tf_op jit(solution)/shard_map/ppermute | solution.py:37
  13.0 1.5 %collective-permute-done.3.refs_1_.refs_4_.refs_7_ = bf16[1536,128]{1,0:T(8,128)(2,1)S(1)} collective-permute-done((bf16[1536,128]{1,0:T(8,128)(2,1)}, bf16[1536,128]{1,0:T(8,128)(2,1)S(1)}, u32[]{:S(2)}, u32[]{:S(2)}) %collective-permute-start.3) | collective-permute-done | bytes 393248 | tf_op jit(solution)/shard_map/ppermute | solution.py:26
  14.4 0.0 copy-start.3
  14.5 0.7 %copy-done.3 = bf16[16,128]{1,0:T(8,128)(2,1)S(1)} copy-done((bf16[16,128]{1,0:T(8,128)(2,1)S(1)}, bf16[16,128]{1,0:T(8,128)(2,1)}, u32[]{:S(2)}) %copy-start.3) | copy-done | bytes 4120
  15.2 1.6 %collective-permute-start.9 = (bf16[640,128]{1,0:T(8,128)(2,1)S(1)}, bf16[640,128]{1,0:T(8,128)(2,1)S(1)}, u32[]{:S(2)}, u32[]{:S(2)}) collective-permute-start(bf16[640,128]{1,0:T(8,128)(2,1)S(1)} %get-tuple-element.36), channel_id=1, source_target_pairs={{16,0},{0,16},{17,1},{1,17},{18,2},{2,18},{19,3},{3,19},{20,4},{4,... | collective-permute-start | bytes 491528 | tf_op jit(solution)/shard_map/ppermute | solution.py:26
  16.7 0.5 collective-permute-start.10
  17.2 0.0 collective-permute-done.refs_0_.refs_3_.refs_5_
  17.2 3.0 %collective-permute-done.1.refs_1_.refs_2_.refs_4_ = bf16[656,128]{1,0:T(8,128)(2,1)S(1)} collective-permute-done((bf16[656,128]{1,0:T(8,128)(2,1)}, bf16[656,128]{1,0:T(8,128)(2,1)S(1)}, u32[]{:S(2)}, u32[]{:S(2)}) %collective-permute-start.1) | collective-permute-done | bytes 167968 | tf_op jit(solution)/shard_map/ppermute | solution.py:32
  20.2 0.0 collective-permute-done.4.refs_5_.refs_2_
  20.2 0.1 pack_two.1
  20.3 0.6 collective-permute-start.5
  20.9 0.0 copy-start.1
  20.9 0.0 copy-start.4
  20.9 0.6 %collective-permute-start.6 = (bf16[1456,128]{1,0:T(8,128)(2,1)S(1)}, bf16[1456,128]{1,0:T(8,128)(2,1)S(1)}, u32[]{:S(2)}, u32[]{:S(2)}) collective-permute-start(bf16[1456,128]{1,0:T(8,128)(2,1)S(1)} %get-tuple-element.31.refs_2_), channel_id=1, source_target_pairs={{16,0},{0,16},{17,1},{1,17},{18,2},{2,18},{19,3},{3,19},{20,4},{4,... | collective-permute-start | bytes 1118216 | tf_op jit(solution)/shard_map/ppermute | solution.py:26
  21.5 0.0 collective-permute-start.7
  21.5 0.0 collective-permute-done.9.refs_0_.refs_10_
  21.5 0.5 collective-permute-start.8
  22.0 0.0 collective-permute-done.10.refs_1_.refs_11_
  22.1 0.1 collective-permute-start.11
  22.2 0.0 copy-done.1
  22.2 0.0 copy-done.4
  22.2 4.2 %prepare.1 = (s32[83]{0:T(128)S(1)}, s32[83]{0:T(128)S(1)}, s32[83]{0:T(128)S(1)}, s32[14]{0:T(128)S(1)}) custom-call(s32[12,32]{1,0:T(8,128)S(1)} %bitcast.19, s32[32]{0:T(128)S(1)} %copy-done.4, bf16[1456,128]{1,0:T(8,128)(2,1)S(1)} %get-tuple-element.31.refs_2_), custom_call_target="tpu_custom_call" | custom-call | flops 1000 | bytes 1000 | tf_op jit(solution)/shard_map/prepare/pallas_call | solution.py:619
  26.4 4.6 %collective-permute-done.5.refs_0_.refs_13_ = bf16[1456,128]{1,0:T(8,128)(2,1)S(1)} collective-permute-done((bf16[1456,128]{1,0:T(8,128)(2,1)S(1)}, bf16[1456,128]{1,0:T(8,128)(2,1)S(1)}, u32[]{:S(2)}, u32[]{:S(2)}) %collective-permute-start.5) | collective-permute-done | bytes 372768 | tf_op jit(solution)/shard_map/ppermute | solution.py:37
  31.0 0.3 collective-permute-done.6.refs_2_.refs_12_
  31.3 0.0 collective-permute-done.7.refs_3_.refs_9_
  31.3 0.0 collective-permute-done.8.refs_4_.refs_8_
  31.3 0.1 pack_three.1
  31.4 0.1 collective-permute-start.14
  31.5 0.6 %collective-permute-start.12 = (bf16[640,128]{1,0:T(8,128)(2,1)S(1)}, bf16[640,128]{1,0:T(8,128)(2,1)S(1)}, u32[]{:S(2)}, u32[]{:S(2)}) collective-permute-start(bf16[640,128]{1,0:T(8,128)(2,1)S(1)} %get-tuple-element.38.refs_2_.refs_15_), channel_id=1, source_target_pairs={{16,0},{0,16},{17,1},{1,17},{18,2},{2,18},{19,3},{3,19},{20,4},{4,... | collective-permute-start | bytes 491528 | tf_op jit(solution)/shard_map/ppermute | solution.py:26
  32.1 1.6 %collective-permute-start.13 = (bf16[640,128]{1,0:T(8,128)(2,1)S(1)}, bf16[640,128]{1,0:T(8,128)(2,1)S(1)}, u32[]{:S(2)}, u32[]{:S(2)}) collective-permute-start(bf16[640,128]{1,0:T(8,128)(2,1)S(1)} %get-tuple-element.43), channel_id=1, source_target_pairs={{2,0},{3,1},{0,2},{1,3},{6,4},{7,5},{4,6},{5,7},{10,8},{11,9},{8,1... | collective-permute-start | bytes 491528 | tf_op jit(solution)/shard_map/ppermute | solution.py:37
  33.7 0.0 collective-permute-start.15
  33.7 0.0 copy-done.2
  33.7 1.0 %spread_basis.1 = (bf16[128,1536]{1,0:T(8,128)(2,1)S(1)}, bf16[16,128]{1,0:T(8,128)(2,1)S(1)}) custom-call(s32[12,32]{1,0:T(8,128)S(1)} %bitcast.20, bf16[192,128]{1,0:T(8,128)(2,1)S(1)} %bitcast.21, bf16[640,128]{1,0:T(8,128)(2,1)S(1)} %get-tuple-element.38.refs_2_.refs_15_), custom_call_target="tpu_custom_call" | custom-call | flops 1000 | bytes 1000 | tf_op jit(solution)/shard_map/spread_basis/pallas_call | solution.py:668
  34.7 0.0 collective-permute-done.11.refs_14_
  34.7 0.0 copy-done
  34.7 2.1 %gram_early.1.refs_2_.refs_3_ = bf16[1536,1536]{1,0:T(8,128)(2,1)S(1)} custom-call(s32[83]{0:T(128)S(1)} %get-tuple-element.42.refs_0_, bf16[1536,128]{1,0:T(8,128)(2,1)S(1)} %bitcast.14, bf16[1536,128]{1,0:T(8,128)(2,1)S(1)} %collective-permute-done.4.refs_5_.refs_2_, bf16[1536,128]{1,0:T(8,128)(2,1)S(1)} %collective-permute-done.2.refs_0_.refs_3_, ...), custom_call_target="tpu_custom_call" | custom-call | flops 1000 | bytes 1000 | tf_op jit(solution)/shard_map/gram_early/pallas_call | solution.py:683
  36.9 1.2 %collective-permute-done.15.refs_3_.refs_2_ = bf16[96,128]{1,0:T(8,128)(2,1)S(1)} collective-permute-done((bf16[96,128]{1,0:T(8,128)(2,1)S(1)}, bf16[96,128]{1,0:T(8,128)(2,1)S(1)}, u32[]{:S(2)}, u32[]{:S(2)}) %collective-permute-start.15) | collective-permute-done | bytes 24608 | tf_op jit(solution)/shard_map/ppermute | solution.py:37
  38.1 0.0 collective-permute-done.12.refs_0_.refs_4_
  38.1 0.5 collective-permute-done.13.refs_1_.refs_5_
  38.7 0.2 collective-permute-start.16
  38.8 0.0 collective-permute-done.14.refs_6_.refs_1_
  38.8 1.2 %gram_middle.1 = (bf16[1536,1536]{1,0:T(8,128)(2,1)S(1)}, bf16[128,1536]{1,0:T(8,128)(2,1)S(1)}) custom-call(s32[83]{0:T(128)S(1)} %get-tuple-element.41.refs_0_, s32[14]{0:T(128)S(1)} %get-tuple-element.33.refs_6_.refs_1_, bf16[12,128,128]{2,1,0:T(8,128)(2,1)S(1)} %bitcast.15, bf16[1536,1536]{1,0:T(8,128)(2,1)S(1)} %gram_early.1.refs_2_.refs_3_, ...), custom_call_target="tpu_custom_call" | custom-call | flops 1000 | bytes 1000 | tf_op jit(solution)/shard_map/gram_middle/pallas_call | solution.py:720
  40.1 0.3 collective-permute-done.16.refs_6_
  40.4 4.2 %square_cube_coefficients.1 = (bf16[12,128,128]{2,1,0:T(8,128)(2,1)S(1)}, f32[8,128]{1,0:T(8,128)S(1)}) custom-call(s32[83]{0:T(128)S(1)} %get-tuple-element.32.refs_0_, s32[14]{0:T(128)S(1)} %get-tuple-element.33.refs_6_.refs_1_, bf16[16,128]{1,0:T(8,128)(2,1)S(1)} %get-tuple-element.39.refs_4_.refs_2_, bf16[128,1536]{1,0:T(8,128)(2,1)S(1)} %get-tuple-element.40.refs_3_, ...), custom_call_target="tpu_custom_call" | custom-call | flops 1300000000 | bytes 8000000 | tf_op jit(solution)/shard_map/square_cube_coefficients/pallas_call | solution.py:737
  44.5 0.2 collective-permute-start.17
  44.7 1.5 %collective-permute-start.18 = (f32[8,128]{1,0:T(8,128)S(1)}, f32[8,128]{1,0:T(8,128)S(1)}, u32[]{:S(2)}, u32[]{:S(2)}) collective-permute-start(f32[8,128]{1,0:T(8,128)S(1)} %get-tuple-element.50.own_ref), channel_id=1, source_target_pairs={{3,0},{2,1},{1,2},{0,3},{7,4},{6,5},{5,6},{4,7},{11,8},{10,9},{9,1... | collective-permute-start | bytes 12296 | tf_op jit(solution)/shard_map/ppermute | solution.py:37
  46.2 0.0 collective-permute-done.17.mate_ref
  46.2 1.5 %collective-permute-done.18.third_ref = f32[8,128]{1,0:T(8,128)S(1)} collective-permute-done((f32[8,128]{1,0:T(8,128)S(1)}, f32[8,128]{1,0:T(8,128)S(1)}, u32[]{:S(2)}, u32[]{:S(2)}) %collective-permute-start.18) | collective-permute-done | bytes 4128 | tf_op jit(solution)/shard_map/ppermute | solution.py:37
  47.7 0.1 merge_layers.1.refs_0_
  47.8 1.5 %collective-permute-start.19 = (f32[8,128]{1,0:T(8,128)S(1)}, f32[8,128]{1,0:T(8,128)S(1)}, u32[]{:S(2)}, u32[]{:S(2)}) collective-permute-start(f32[8,128]{1,0:T(8,128)S(1)} %merge_layers.1.refs_0_), channel_id=1, source_target_pairs={{16,0},{0,16},{17,1},{1,17},{18,2},{2,18},{19,3},{3,19},{20,4},{4,... | collective-permute-start | bytes 12296 | tf_op jit(solution)/shard_map/ppermute | solution.py:26
  49.3 0.8 %give_sign.1 = (bf16[1536,128]{1,0:T(8,128)(2,1)}, bf16[16,128]{1,0:T(8,128)(2,1)S(1)}) custom-call(bf16[1536,128]{1,0:T(8,128)(2,1)S(1)} %bitcast.17), custom_call_target="tpu_custom_call" | custom-call | bytes 1000 | tf_op jit(solution)/shard_map/give_sign/pallas_call | solution.py:254
  50.1 1.4 %collective-permute-done.19.refs_1_ = f32[8,128]{1,0:T(8,128)S(1)} collective-permute-done((f32[8,128]{1,0:T(8,128)S(1)}, f32[8,128]{1,0:T(8,128)S(1)}, u32[]{:S(2)}, u32[]{:S(2)}) %collective-permute-start.19) | collective-permute-done | bytes 4128 | tf_op jit(solution)/shard_map/ppermute | solution.py:26
  51.4 1.4 %collective-permute-start.20 = (f32[16,128]{1,0:T(8,128)S(1)}, f32[16,128]{1,0:T(8,128)S(1)}, u32[]{:S(2)}, u32[]{:S(2)}) collective-permute-start(f32[16,128]{1,0:T(8,128)S(1)} %stack_tiles.1.refs_0_), channel_id=1, source_target_pairs={{4,0},{0,4},{12,8},{8,12},{5,1},{1,5},{13,9},{9,13},{6,2},{2,6},{1... | collective-permute-start | bytes 24584 | tf_op jit(solution)/shard_map/ppermute | solution.py:32
  52.8 1.4 %collective-permute-start.21 = (f32[16,128]{1,0:T(8,128)S(1)}, f32[16,128]{1,0:T(8,128)S(1)}, u32[]{:S(2)}, u32[]{:S(2)}) collective-permute-start(f32[16,128]{1,0:T(8,128)S(1)} %stack_tiles.1.refs_0_), channel_id=1, source_target_pairs={{12,0},{8,4},{4,8},{0,12},{13,1},{9,5},{5,9},{1,13},{14,2},{10,6},... | collective-permute-start | bytes 24584 | tf_op jit(solution)/shard_map/ppermute | solution.py:32
  54.2 2.8 %profiles.1 = (bf16[6,6,256,128]{3,2,1,0:T(8,128)(2,1)S(1)}, bf16[6,6,128,128]{3,2,1,0:T(8,128)(2,1)S(1)}) custom-call(bf16[96,128]{1,0:T(8,128)(2,1)S(1)} %get-tuple-element.45.refs_0_, bf16[2960,128]{1,0:T(8,128)(2,1)S(1)} %collective-permute-done.14.refs_6_.refs_1_, bf16[96,128]{1,0:T(8,128)(2,1)S(1)} %collective-permute-done.15.refs_3_.refs_2_), custom_call_target="tpu_custom_call" | custom-call | flops 1000 | bytes 1000 | tf_op jit(solution)/shard_map/profiles/pallas_call | solution.py:702
  57.0 0.0 collective-permute-done.20.refs_1_
  57.1 1.2 %collective-permute-done.21.refs_2_ = f32[16,128]{1,0:T(8,128)S(1)} collective-permute-done((f32[16,128]{1,0:T(8,128)S(1)}, f32[16,128]{1,0:T(8,128)S(1)}, u32[]{:S(2)}, u32[]{:S(2)}) %collective-permute-start.21) | collective-permute-done | bytes 8224 | tf_op jit(solution)/shard_map/ppermute | solution.py:32
  58.2 1.4 %density.1 = f32[256,128]{1,0:T(8,128)} custom-call(f32[16,128]{1,0:T(8,128)S(1)} %stack_tiles.1.refs_0_, f32[16,128]{1,0:T(8,128)S(1)} %collective-permute-done.20.refs_1_, f32[16,128]{1,0:T(8,128)S(1)} %collective-permute-done.21.refs_2_, bf16[6,6,256,128]{3,2,1,0:T(8,128)(2,1)S(1)} %get-tuple-element.52.refs_3_, bf16[4608,128]{1,0:T(8,128)(2,1)S(1)} %bitcast.16), custom_call_target="tpu_custom_call" | custom-call | flops 310000000 | bytes 4000000 | tf_op jit(solution)/shard_map/density/pallas_call | solution.py:772
  (6 shorter events, 0.1 us)
Async XLA Ops:
  0.6 12.4 %collective-permute-start.2 = (bf16[1536,128]{1,0:T(8,128)(2,1)}, bf16[1536,128]{1,0:T(8,128)(2,1)S(1)}, u32[]{:S(2)}, u32[]{:S(2)}) collective-permute-start(bf16[1536,128]{1,0:T(8,128)(2,1)} %bitcast.10), channel_id=1, source_target_pairs={{2,0},{3,1},{0,2},{1,3},{6,4},{7,5},{4,6},{5,7},{10,8},{11,9},{8,1... | collective-permute-start | bytes 1179656 | tf_op jit(solution)/shard_map/ppermute | solution.py:37
  3.7 10.8 %collective-permute-start.3 = (bf16[1536,128]{1,0:T(8,128)(2,1)}, bf16[1536,128]{1,0:T(8,128)(2,1)S(1)}, u32[]{:S(2)}, u32[]{:S(2)}) collective-permute-start(bf16[1536,128]{1,0:T(8,128)(2,1)} %bitcast.11), channel_id=1, source_target_pairs={{16,0},{0,16},{17,1},{1,17},{18,2},{2,18},{19,3},{3,19},{20,4},{4,... | collective-permute-start | bytes 1179656 | tf_op jit(solution)/shard_map/ppermute | solution.py:26
  5.2 15.1 %collective-permute-start.4 = (bf16[1536,128]{1,0:T(8,128)(2,1)}, bf16[1536,128]{1,0:T(8,128)(2,1)S(1)}, u32[]{:S(2)}, u32[]{:S(2)}) collective-permute-start(bf16[1536,128]{1,0:T(8,128)(2,1)} %bitcast.12), channel_id=1, source_target_pairs={{1,0},{0,1},{3,2},{2,3},{5,4},{4,5},{7,6},{6,7},{9,8},{8,9},{11,10... | collective-permute-start | bytes 1179656 | tf_op jit(solution)/shard_map/ppermute | solution.py:37
  7.7 9.6 %collective-permute-start = (bf16[656,128]{1,0:T(8,128)(2,1)}, bf16[656,128]{1,0:T(8,128)(2,1)S(1)}, u32[]{:S(2)}, u32[]{:S(2)}) collective-permute-start(bf16[656,128]{1,0:T(8,128)(2,1)} %get-tuple-element.28), channel_id=1, source_target_pairs={{12,0},{8,4},{4,8},{0,12},{13,1},{9,5},{5,9},{1,13},{14,2},{10,6},... | collective-permute-start | bytes 503816 | tf_op jit(solution)/shard_map/ppermute | solution.py:32
  11.3 8.9 %collective-permute-start.1 = (bf16[656,128]{1,0:T(8,128)(2,1)}, bf16[656,128]{1,0:T(8,128)(2,1)S(1)}, u32[]{:S(2)}, u32[]{:S(2)}) collective-permute-start(bf16[656,128]{1,0:T(8,128)(2,1)} %get-tuple-element.28), channel_id=1, source_target_pairs={{4,0},{0,4},{12,8},{8,12},{5,1},{1,5},{13,9},{9,13},{6,2},{2,6},{1... | collective-permute-start | bytes 503816 | tf_op jit(solution)/shard_map/ppermute | solution.py:32
  14.4 0.7 %copy-start.3 = (bf16[16,128]{1,0:T(8,128)(2,1)S(1)}, bf16[16,128]{1,0:T(8,128)(2,1)}, u32[]{:S(2)}) copy-start(bf16[16,128]{1,0:T(8,128)(2,1)} %get-tuple-element.29.refs_2_) | copy-start | bytes 12292
  15.2 6.3 %collective-permute-start.9 = (bf16[640,128]{1,0:T(8,128)(2,1)S(1)}, bf16[640,128]{1,0:T(8,128)(2,1)S(1)}, u32[]{:S(2)}, u32[]{:S(2)}) collective-permute-start(bf16[640,128]{1,0:T(8,128)(2,1)S(1)} %get-tuple-element.36), channel_id=1, source_target_pairs={{16,0},{0,16},{17,1},{1,17},{18,2},{2,18},{19,3},{3,19},{20,4},{4,... | collective-permute-start | bytes 491528 | tf_op jit(solution)/shard_map/ppermute | solution.py:26
  16.7 5.3 %collective-permute-start.10 = (bf16[640,128]{1,0:T(8,128)(2,1)S(1)}, bf16[640,128]{1,0:T(8,128)(2,1)S(1)}, u32[]{:S(2)}, u32[]{:S(2)}) collective-permute-start(bf16[640,128]{1,0:T(8,128)(2,1)S(1)} %get-tuple-element.37), channel_id=1, source_target_pairs={{2,0},{3,1},{0,2},{1,3},{6,4},{7,5},{4,6},{5,7},{10,8},{11,9},{8,1... | collective-permute-start | bytes 491528 | tf_op jit(solution)/shard_map/ppermute | solution.py:37
  20.3 10.7 %collective-permute-start.5 = (bf16[1456,128]{1,0:T(8,128)(2,1)S(1)}, bf16[1456,128]{1,0:T(8,128)(2,1)S(1)}, u32[]{:S(2)}, u32[]{:S(2)}) collective-permute-start(bf16[1456,128]{1,0:T(8,128)(2,1)S(1)} %get-tuple-element.34), channel_id=1, source_target_pairs={{2,0},{3,1},{0,2},{1,3},{6,4},{7,5},{4,6},{5,7},{10,8},{11,9},{8,1... | collective-permute-start | bytes 1118216 | tf_op jit(solution)/shard_map/ppermute | solution.py:37
  20.9 1.3 %copy-start.1 = (s32[32,12]{0,1:T(8,128)S(1)}, s32[32,12]{0,1:T(8,128)}, u32[]{:S(2)}) copy-start(s32[32,12]{0,1:T(8,128)} %param.9) | copy-start | bytes 4612
  20.9 1.3 %copy-start.4 = (s32[32]{0:T(128)S(1)}, s32[32]{0:T(128)}, u32[]{:S(2)}) copy-start(s32[32]{0:T(128)} %refs_1_.3) | copy-start | bytes 388
  20.9 12.8 %copy-start.2 = (bf16[32,6,128]{2,0,1:T(8,128)(2,1)S(1)}, bf16[32,6,128]{2,0,1:T(8,128)(2,1)}, u32[]{:S(2)}) copy-start(bf16[32,6,128]{2,0,1:T(8,128)(2,1)} %param.11) | copy-start | bytes 147460
  20.9 13.8 %copy-start = (bf16[1,12,128,128]{3,2,1,0:T(8,128)(2,1)S(1)}, bf16[1,12,128,128]{3,2,1,0:T(8,128)(2,1)}, u32[]{:S(2)}) copy-start(bf16[1,12,128,128]{3,2,1,0:T(8,128)(2,1)} %param.8) | copy-start | bytes 1179652
  20.9 10.4 %collective-permute-start.6 = (bf16[1456,128]{1,0:T(8,128)(2,1)S(1)}, bf16[1456,128]{1,0:T(8,128)(2,1)S(1)}, u32[]{:S(2)}, u32[]{:S(2)}) collective-permute-start(bf16[1456,128]{1,0:T(8,128)(2,1)S(1)} %get-tuple-element.31.refs_2_), channel_id=1, source_target_pairs={{16,0},{0,16},{17,1},{1,17},{18,2},{2,18},{19,3},{3,19},{20,4},{4,... | collective-permute-start | bytes 1118216 | tf_op jit(solution)/shard_map/ppermute | solution.py:26
  21.5 9.8 %collective-permute-start.7 = (bf16[1536,128]{1,0:T(8,128)(2,1)S(1)}, bf16[1536,128]{1,0:T(8,128)(2,1)S(1)}, u32[]{:S(2)}, u32[]{:S(2)}) collective-permute-start(bf16[1536,128]{1,0:T(8,128)(2,1)S(1)} %collective-permute-done.2.refs_0_.refs_3_), channel_id=1, source_target_pairs={{1,0},{0,1},{3,2},{2,3},{5,4},{4,5},{7,6},{6,7},{9,8},{8,9},{11,10... | collective-permute-start | bytes 1179656 | tf_op jit(solution)/shard_map/ppermute | solution.py:37
  21.5 9.8 %collective-permute-start.8 = (bf16[1536,128]{1,0:T(8,128)(2,1)S(1)}, bf16[1536,128]{1,0:T(8,128)(2,1)S(1)}, u32[]{:S(2)}, u32[]{:S(2)}) collective-permute-start(bf16[1536,128]{1,0:T(8,128)(2,1)S(1)} %collective-permute-done.3.refs_1_.refs_4_.refs_7_), channel_id=1, source_target_pairs={{1,0},{0,1},{3,2},{2,3},{5,4},{4,5},{7,6},{6,7},{9,8},{8,9},{11,10... | collective-permute-start | bytes 1179656 | tf_op jit(solution)/shard_map/ppermute | solution.py:37
  22.1 12.6 %collective-permute-start.11 = (bf16[2560,128]{1,0:T(8,128)(2,1)S(1)}, bf16[2560,128]{1,0:T(8,128)(2,1)S(1)}, u32[]{:S(2)}, u32[]{:S(2)}) collective-permute-start(bf16[2560,128]{1,0:T(8,128)(2,1)S(1)} %pack_two_mate.1.refs_5_), channel_id=1, source_target_pairs={{1,0},{0,1},{3,2},{2,3},{5,4},{4,5},{7,6},{6,7},{9,8},{8,9},{11,10... | collective-permute-start | bytes 1966088 | tf_op jit(solution)/shard_map/ppermute | solution.py:37
  31.4 7.4 %collective-permute-start.14 = (bf16[2960,128]{1,0:T(8,128)(2,1)S(1)}, bf16[2960,128]{1,0:T(8,128)(2,1)S(1)}, u32[]{:S(2)}, u32[]{:S(2)}) collective-permute-start(bf16[2960,128]{1,0:T(8,128)(2,1)S(1)} %get-tuple-element.44), channel_id=1, source_target_pairs={{1,0},{0,1},{3,2},{2,3},{5,4},{4,5},{7,6},{6,7},{9,8},{8,9},{11,10... | collective-permute-start | bytes 2273288 | tf_op jit(solution)/shard_map/ppermute | solution.py:37
  31.5 6.6 %collective-permute-start.12 = (bf16[640,128]{1,0:T(8,128)(2,1)S(1)}, bf16[640,128]{1,0:T(8,128)(2,1)S(1)}, u32[]{:S(2)}, u32[]{:S(2)}) collective-permute-start(bf16[640,128]{1,0:T(8,128)(2,1)S(1)} %get-tuple-element.38.refs_2_.refs_15_), channel_id=1, source_target_pairs={{16,0},{0,16},{17,1},{1,17},{18,2},{2,18},{19,3},{3,19},{20,4},{4,... | collective-permute-start | bytes 491528 | tf_op jit(solution)/shard_map/ppermute | solution.py:26
  32.1 6.5 %collective-permute-start.13 = (bf16[640,128]{1,0:T(8,128)(2,1)S(1)}, bf16[640,128]{1,0:T(8,128)(2,1)S(1)}, u32[]{:S(2)}, u32[]{:S(2)}) collective-permute-start(bf16[640,128]{1,0:T(8,128)(2,1)S(1)} %get-tuple-element.43), channel_id=1, source_target_pairs={{2,0},{3,1},{0,2},{1,3},{6,4},{7,5},{4,6},{5,7},{10,8},{11,9},{8,1... | collective-permute-start | bytes 491528 | tf_op jit(solution)/shard_map/ppermute | solution.py:37
  33.7 4.5 %collective-permute-start.15 = (bf16[96,128]{1,0:T(8,128)(2,1)S(1)}, bf16[96,128]{1,0:T(8,128)(2,1)S(1)}, u32[]{:S(2)}, u32[]{:S(2)}) collective-permute-start(bf16[96,128]{1,0:T(8,128)(2,1)S(1)} %get-tuple-element.45.refs_0_), channel_id=1, source_target_pairs={{3,0},{2,1},{1,2},{0,3},{7,4},{6,5},{5,6},{4,7},{11,8},{10,9},{9,1... | collective-permute-start | bytes 73736 | tf_op jit(solution)/shard_map/ppermute | solution.py:37
  38.7 1.7 %collective-permute-start.16 = (bf16[1280,128]{1,0:T(8,128)(2,1)S(1)}, bf16[1280,128]{1,0:T(8,128)(2,1)S(1)}, u32[]{:S(2)}, u32[]{:S(2)}) collective-permute-start(bf16[1280,128]{1,0:T(8,128)(2,1)S(1)} %pack_four.1.refs_7_), channel_id=1, source_target_pairs={{1,0},{0,1},{3,2},{2,3},{5,4},{4,5},{7,6},{6,7},{9,8},{8,9},{11,10... | collective-permute-start | bytes 983048 | tf_op jit(solution)/shard_map/ppermute | solution.py:37
  44.5 1.7 %collective-permute-start.17 = (f32[8,128]{1,0:T(8,128)S(1)}, f32[8,128]{1,0:T(8,128)S(1)}, u32[]{:S(2)}, u32[]{:S(2)}) collective-permute-start(f32[8,128]{1,0:T(8,128)S(1)} %get-tuple-element.50.own_ref), channel_id=1, source_target_pairs={{1,0},{0,1},{3,2},{2,3},{5,4},{4,5},{7,6},{6,7},{9,8},{8,9},{11,10... | collective-permute-start | bytes 12296 | tf_op jit(solution)/shard_map/ppermute | solution.py:37
  44.7 3.0 %collective-permute-start.18 = (f32[8,128]{1,0:T(8,128)S(1)}, f32[8,128]{1,0:T(8,128)S(1)}, u32[]{:S(2)}, u32[]{:S(2)}) collective-permute-start(f32[8,128]{1,0:T(8,128)S(1)} %get-tuple-element.50.own_ref), channel_id=1, source_target_pairs={{3,0},{2,1},{1,2},{0,3},{7,4},{6,5},{5,6},{4,7},{11,8},{10,9},{9,1... | collective-permute-start | bytes 12296 | tf_op jit(solution)/shard_map/ppermute | solution.py:37
  47.8 3.6 %collective-permute-start.19 = (f32[8,128]{1,0:T(8,128)S(1)}, f32[8,128]{1,0:T(8,128)S(1)}, u32[]{:S(2)}, u32[]{:S(2)}) collective-permute-start(f32[8,128]{1,0:T(8,128)S(1)} %merge_layers.1.refs_0_), channel_id=1, source_target_pairs={{16,0},{0,16},{17,1},{1,17},{18,2},{2,18},{19,3},{3,19},{20,4},{4,... | collective-permute-start | bytes 12296 | tf_op jit(solution)/shard_map/ppermute | solution.py:26
  51.4 5.6 %collective-permute-start.20 = (f32[16,128]{1,0:T(8,128)S(1)}, f32[16,128]{1,0:T(8,128)S(1)}, u32[]{:S(2)}, u32[]{:S(2)}) collective-permute-start(f32[16,128]{1,0:T(8,128)S(1)} %stack_tiles.1.refs_0_), channel_id=1, source_target_pairs={{4,0},{0,4},{12,8},{8,12},{5,1},{1,5},{13,9},{9,13},{6,2},{2,6},{1... | collective-permute-start | bytes 24584 | tf_op jit(solution)/shard_map/ppermute | solution.py:32
  52.8 5.4 %collective-permute-start.21 = (f32[16,128]{1,0:T(8,128)S(1)}, f32[16,128]{1,0:T(8,128)S(1)}, u32[]{:S(2)}, u32[]{:S(2)}) collective-permute-start(f32[16,128]{1,0:T(8,128)S(1)} %stack_tiles.1.refs_0_), channel_id=1, source_target_pairs={{12,0},{8,4},{4,8},{0,12},{13,1},{9,5},{5,9},{1,13},{14,2},{10,6},... | collective-permute-start | bytes 24584 | tf_op jit(solution)/shard_map/ppermute | solution.py:32
